TPU v7x, 32 devices: a whole 2x2x4 slice. The times are simulated.
32 devices in a mesh: pair: 8 (over z, x), mo: 4 (over y, core).
Axes of the slice: x: 2, y: 2, z: 4, core: 2. Of those that a mesh axis runs over, the one named last changes fastest.
Arguments:
- integrals: bfloat16 [128, 1000, 1000], P('pair', 'mo'), may hold values from -6 to 6
- coeffs: bfloat16 [1000, 512], replicated, may hold values from -0.1875 to 0.1875
- mirror: int32 [128], replicated, may hold values from 0 to 127, as said below
Outputs:
- combined: float32 [128, 512, 512], P(None, 'pair', 'mo')
Inputs may be any that keep to these rules, and one draw needn't show every extreme that they name: mirror pairs the rows: mirror[mirror[k]] = k and mirror[k] != k for every row k; a row and its mirror may lie on any devices.
All inputs are finite; a program needn't handle non-finite values.
Results may differ from a plain program's by a relative error of at most 0.0029.
Values may be sent and summed in bfloat16 or wider, within the bound.
No kernel may reach another device: no remote copies, remote signals or barrier semaphores. Data moves between devices by JAX's collectives and lax.ppermute only.
A program may use at most 128 MiB of HBM per device.

v0:
```python
import jax
import jax.numpy as jnp
from jax import lax
from jax.sharding import PartitionSpec as P


def on_device(integrals, coeffs, mirror):
    quarter = jnp.einsum(
        "krs,sj->krj", integrals, coeffs, preferred_element_type=jnp.float32
    ).astype(jnp.bfloat16)
    arrived = lax.all_to_all(quarter, "mo", split_axis=2, concat_axis=1, tiled=True)
    half = jnp.einsum("ri,krj->kij", coeffs, arrived, preferred_element_type=jnp.float32)
    pieces = lax.all_to_all(half, "pair", split_axis=1, concat_axis=0, tiled=True)
    partner = jnp.take(pieces, mirror, axis=0)
    return 0.5 * (pieces + partner)


def solution(mesh):
    return jax.shard_map(
        on_device,
        mesh=mesh,
        in_specs=(P("pair", "mo", None), P(), P()),
        out_specs=P(None, "pair", "mo"),
        check_vma=False,
    )
```

profile of v0, /device:TPU:0, one launch (start us, length us, event | category | flops | bytes accessed | tf_op | source)
XLA Modules:
  0.0 223.8 jit_solution(14576684764834407569)
XLA Ops:
  0.0 0.0 copy-start
  0.0 1.2 copy-done
  1.2 23.2 %fusion.4 = bf16[16,250,512]{2,1,0:T(8,128)(2,1)} fusion(bf16[16,250,1000]{2,0,1:T(8,128)(2,1)} %param.3, bf16[1000,512]{1,0:T(8,128)(2,1)S(1)} %copy-done), kind=kOutput, calls=%fused_computation.6 | convolution fusion | flops 4098048000 | bytes 13120000 | tf_op jit(solution)/shard_map/krs,sj->krj/dot_general | solution.py:8
  24.4 7.9 %copy.14 = bf16[16,250,512]{1,0,2:T(8,128)(2,1)} copy(bf16[16,250,512]{2,1,0:T(8,128)(2,1)} %fusion.4) | data formatting | bytes 8192000 | tf_op jit(solution)/shard_map/convert_element_type | solution.py:10
  32.3 54.7 %all_to_all.36 = bf16[16,250,512]{1,0,2:T(8,128)(2,1)} all-to-all(bf16[16,250,512]{1,0,2:T(8,128)(2,1)} %copy.14), channel_id=1, replica_groups=mesh['pair'=8,'mo'=4] {'mo'}, dimensions={2} | all-to-all | bytes 8192000 | tf_op jit(solution)/shard_map/all_to_all | solution.py:11
  87.0 8.5 %copy.16 = bf16[16,4,250,128]{3,0,2,1:T(8,128)(2,1)} copy(bf16[16,4,250,128]{2,0,3,1:T(8,128)(2,1)} %bitcast.18) | data formatting | bytes 8192000 | tf_op jit(solution)/shard_map/all_to_all | solution.py:11
  95.5 6.8 %fusion.7 = f32[16,512,128]{1,2,0:T(8,128)} fusion(bf16[16,1000,128]{2,0,1:T(8,128)(2,1)} %bitcast.17, bf16[1000,512]{1,0:T(8,128)(2,1)S(1)} %copy-done), kind=kOutput, calls=%fused_computation.7 | convolution fusion | flops 2097152000 | bytes 9314304 | tf_op jit(solution)/shard_map/ri,krj->kij/dot_general | solution.py:12
  102.4 5.5 %copy.18 = f32[16,512,128]{2,0,1:T(8,128)} copy(f32[16,512,128]{1,2,0:T(8,128)} %fusion.7) | data formatting | bytes 8388608 | tf_op jit(solution)/shard_map/ri,krj->kij/transpose | solution.py:12
  107.8 0.0 copy-start.1
  107.8 6.6 %all-to-all-start.1 = ((f32[16,512,128]{2,0,1:T(8,128)}), f32[16,512,128]{2,0,1:T(8,128)}, u32[]{:S(2)}, u32[]{:S(2)}) async-start(f32[16,512,128]{2,0,1:T(8,128)} %copy.18), calls=%async_computation.1 | async-start | bytes 8388608 | tf_op jit(solution)/shard_map/all_to_all | solution.py:13
  114.4 0.0 copy-done.1
  114.4 92.9 %all-to-all-done.1 = f32[16,512,128]{2,0,1:T(8,128)} async-done(((f32[16,512,128]{2,0,1:T(8,128)}), f32[16,512,128]{2,0,1:T(8,128)}, u32[]{:S(2)}, u32[]{:S(2)}) %all-to-all-start.1) | async-done | bytes 4194336 | tf_op jit(solution)/shard_map/all_to_all | solution.py:13
  207.3 5.4 %copy.20 = f32[8,16,64,128]{3,2,1,0:T(8,128)} copy(f32[8,16,64,128]{3,1,2,0:T(8,128)} %bitcast.8) | data formatting | bytes 8388608 | tf_op jit(solution)/shard_map/all_to_all | solution.py:13
  212.7 5.0 %gather_fusion = f32[128,64,128]{2,1,0:T(8,128)} fusion(f32[128,64,128]{2,1,0:T(8,128)} %bitcast.16, s32[1024]{0:T(1024)S(1)} %pad_clamp_fusion), kind=kCustom, calls=%fused_computation | custom fusion | bytes 8389120 | tf_op jit(solution)/shard_map/jit(_take)/gather | solution.py:14
  217.7 6.0 %add_multiply_fusion = f32[128,64,128]{2,1,0:T(8,128)} fusion(f32[128,64,128]{2,1,0:T(8,128)} %gather_fusion, pred[128]{0:T(512)(128)(4,1)S(1)} %compare_and_fusion, f32[8,16,64,128]{3,2,1,0:T(8,128)} %copy.20), kind=kLoop, calls=%fused_computation.3 | loop fusion | flops 3145728 | bytes 12583040 | tf_op jit(solution)/shard_map/mul | solution.py:15
  (3 shorter events, 0.0 us)
Async XLA Ops:
  0.0 1.2 copy-start
  107.8 6.6 %copy-start.1 = (s32[128]{0:T(128)S(1)}, s32[128]{0:T(128)}, u32[]{:S(2)}) copy-start(s32[128]{0:T(128)} %param.5) | copy-start | bytes 1540
  107.8 99.5 %all-to-all-start.1 = ((f32[16,512,128]{2,0,1:T(8,128)}), f32[16,512,128]{2,0,1:T(8,128)}, u32[]{:S(2)}, u32[]{:S(2)}) async-start(f32[16,512,128]{2,0,1:T(8,128)} %copy.18), calls=%async_computation.1 | async-start | bytes 8388608 | tf_op jit(solution)/shard_map/all_to_all | solution.py:13
where the time goes:
time: 225 us; the launch traced here: 224 us
  waiting for transfers between devices  92.9 us (41%)
  blocking collectives  54.7 us (24%)
  local copies, waits for them, and re-layouts  33.5 us (15%)
  matrix products  30.1 us (13%)
  starting transfers between devices  6.55 us (3%)
  other arithmetic  6.04 us (3%)
    all_to_all x1, waiting for transfers between devices, on_device(): lax.all_to_all(half, 'pair', split_axis=1, concat_axis=0, tiled=True)  92.9 us
    all_to_all x1, blocking collectives, on_device(): lax.all_to_all(quarter, 'mo', split_axis=2, concat_axis=1, tiled=True)  54.7 us
    dot_general x1, matrix products, on_device(): jnp.einsum('krs,sj->krj', integrals, coeffs, preferred_element_type=jnp.f...  23.2 us
    all_to_all x1, local copies, waits for them, and re-layouts, on_device(): lax.all_to_all(quarter, 'mo', split_axis=2, concat_axis=1, tiled=True)  8.54 us
    convert_element_type x1, local copies, waits for them, and re-layouts, on_device(): quarter = jnp.einsum('krs,sj->krj', integrals, coeffs, preferred_element_...  7.91 us
    dot_general x1, matrix products, on_device(): jnp.einsum('ri,krj->kij', coeffs, arrived, preferred_element_type=jnp.flo...  6.85 us
    all_to_all x1, starting transfers between devices, on_device(): lax.all_to_all(half, 'pair', split_axis=1, concat_axis=0, tiled=True)  6.55 us
    mul x1, other arithmetic, on_device(): return 0.5 * (pieces + partner)  6.03 us
  transfers between devices with their start and end apart: 1, of which 1 were waited for; matrix products, arithmetic and copies ran while one was open for 0% of the time, Pallas kernels for 0%

commit v1 on v0

v1 whole, which is shorter than its diff:
```python
import functools

import jax
import jax.numpy as jnp
from jax import lax
from jax.experimental import pallas as pl
from jax.experimental.pallas import tpu as pltpu
from jax.sharding import PartitionSpec as P

LANES = 128
STEP = 64
CHUNKS = (4, 4, 4, 4)
VMEM = 48 * 1024 * 1024


def quarter_kernel(rows, starts, x_ref, c_ref, *refs):
    outs, acc = refs[:-1], refs[-1]
    step, k_all, depth = x_ref.shape
    x = x_ref[...].reshape(step * k_all, depth)
    for d in range(acc.shape[0]):
        columns = c_ref[:, d * LANES : (d + 1) * LANES]
        acc[d] = jnp.dot(x, columns, preferred_element_type=jnp.float32)
    left = rows - pl.program_id(0) * step
    keep = lax.broadcasted_iota(jnp.int32, (step, LANES), 0) < left
    for out, first in zip(outs, starts):
        for d in range(out.shape[0]):
            for k in range(out.shape[1]):
                block = acc[d, pl.ds(first + k, step, stride=k_all), :]
                out[d, k] = jnp.where(keep, block, 0.0).astype(jnp.bfloat16)


def quarter_of(by_r, coeffs, n_mo, padded):
    rows, k_all, depth = by_r.shape
    orbitals = coeffs.shape[1]
    starts = [sum(CHUNKS[:c]) for c in range(len(CHUNKS))]
    return pl.pallas_call(
        functools.partial(quarter_kernel, rows, starts),
        grid=(padded // STEP,),
        out_shape=[jax.ShapeDtypeStruct((n_mo, kc, padded, LANES), jnp.bfloat16) for kc in CHUNKS],
        in_specs=[
            pl.BlockSpec((STEP, k_all, depth), lambda r: (r, 0, 0)),
            pl.BlockSpec((depth, orbitals), lambda r: (0, 0)),
        ],
        out_specs=[pl.BlockSpec((n_mo, kc, STEP, LANES), lambda r: (0, 0, r, 0)) for kc in CHUNKS],
        scratch_shapes=[pltpu.VMEM((n_mo, STEP * k_all, LANES), jnp.float32)],
        compiler_params=pltpu.CompilerParams(vmem_limit_bytes=VMEM),
        cost_estimate=pl.CostEstimate(
            flops=2 * rows * k_all * depth * orbitals,
            bytes_accessed=2 * (by_r.size + coeffs.size + rows * k_all * orbitals),
            transcendentals=0,
        ),
        name="quarter",
    )(by_r, coeffs)


def half_kernel(a_ref, t_ref, out_ref):
    n_mo, pair, padded, lanes = a_ref.shape
    columns = [a_ref[:, k].reshape(n_mo * padded, lanes) for k in range(pair)]
    half = jnp.dot(
        t_ref[...], jnp.concatenate(columns, axis=1), preferred_element_type=jnp.float32
    ).astype(jnp.bfloat16)
    n_pair, _, block, _ = out_ref.shape
    for k in range(pair):
        out_ref[:, k] = half[:, k * lanes : (k + 1) * lanes].reshape(n_pair, block, lanes)


def half_of(arrived, turned, n_pair):
    n_mo, kc, padded, lanes = arrived.shape
    orbitals = turned.shape[0]
    block = orbitals // n_pair
    return pl.pallas_call(
        half_kernel,
        grid=(kc // 2,),
        out_shape=jax.ShapeDtypeStruct((n_pair, kc, block, lanes), jnp.bfloat16),
        in_specs=[
            pl.BlockSpec((n_mo, 2, padded, lanes), lambda k: (0, k, 0, 0)),
            pl.BlockSpec(turned.shape, lambda k: (0, 0)),
        ],
        out_specs=pl.BlockSpec((n_pair, 2, block, lanes), lambda k: (0, k, 0, 0)),
        compiler_params=pltpu.CompilerParams(vmem_limit_bytes=VMEM),
        cost_estimate=pl.CostEstimate(
            flops=2 * orbitals * n_mo * padded * kc * lanes,
            bytes_accessed=2 * (arrived.size + turned.size + orbitals * kc * lanes),
            transcendentals=0,
        ),
        name="half",
    )(arrived, turned)


def combine_kernel(per_step, mirror_ref, *refs):
    pieces, out_ref, held, sems = refs[:-3], refs[-3], refs[-2], refs[-1]
    step = pl.program_id(0)

    @pl.when(step == 0)
    def _():
        first = 0
        copies = []
        for c, piece in enumerate(pieces):
            kc = piece.shape[1]
            copies.append(pltpu.make_async_copy(piece, held.at[:, first : first + kc], sems.at[c]))
            first += kc
        for copy in copies:
            copy.start()
        for copy in copies:
            copy.wait()

    k_all = held.shape[1]
    for n in range(per_step):
        k = step * per_step + n
        m = mirror_ref[k]
        own = held[k // k_all, lax.rem(k, k_all)].astype(jnp.float32)
        partner = held[m // k_all, lax.rem(m, k_all)].astype(jnp.float32)
        out_ref[n] = 0.5 * (own + partner)


def combine(pieces, mirror):
    n_pair, _, block, lanes = pieces[0].shape
    k_all = sum(p.shape[1] for p in pieces)
    rows = n_pair * k_all
    per_step = max(1, 16 * 64 // block)
    return pl.pallas_call(
        functools.partial(combine_kernel, per_step),
        grid_spec=pltpu.PrefetchScalarGridSpec(
            num_scalar_prefetch=1,
            grid=(rows // per_step,),
            in_specs=[pl.BlockSpec(memory_space=pl.ANY)] * len(pieces),
            out_specs=pl.BlockSpec((per_step, block, lanes), lambda k, m: (k, 0, 0)),
            scratch_shapes=[
                pltpu.VMEM((n_pair, k_all, block, lanes), jnp.bfloat16),
                pltpu.SemaphoreType.DMA((len(pieces),)),
            ],
        ),
        out_shape=jax.ShapeDtypeStruct((rows, block, lanes), jnp.float32),
        compiler_params=pltpu.CompilerParams(vmem_limit_bytes=VMEM),
        cost_estimate=pl.CostEstimate(
            flops=2 * rows * block * lanes,
            bytes_accessed=6 * rows * block * lanes,
            transcendentals=0,
        ),
        name="combine",
    )(mirror, *pieces)


def on_device(n_pair, n_mo, integrals, coeffs, mirror):
    k_all, rows, depth = integrals.shape
    orbitals = coeffs.shape[1]
    padded = -(-rows // STEP) * STEP
    by_r = jnp.transpose(integrals, (1, 0, 2))
    turned = jnp.pad(coeffs.T.reshape(orbitals, n_mo, rows), ((0, 0), (0, 0), (0, padded - rows)))
    turned = turned.reshape(orbitals, n_mo * padded)
    pieces = []
    for quarter in quarter_of(by_r, coeffs, n_mo, padded):
        arrived = lax.all_to_all(quarter, "mo", split_axis=0, concat_axis=0, tiled=True)
        half = half_of(arrived, turned, n_pair)
        pieces.append(lax.all_to_all(half, "pair", split_axis=0, concat_axis=0, tiled=True))
    return combine(pieces, mirror)


def solution(mesh):
    return jax.shard_map(
        functools.partial(on_device, mesh.shape["pair"], mesh.shape["mo"]),
        mesh=mesh,
        in_specs=(P("pair", "mo", None), P(), P()),
        out_specs=P(None, "pair", "mo"),
        check_vma=False,
    )
```

time: 225 us -> 168 us (0.75)
  waiting for transfers between devices: 92.9 us -> 43.4 us
  matrix products: 30.1 us -> 0 us
  Pallas kernels: 0 us -> 23.5 us
  local copies, waits for them, and re-layouts: 33.5 us -> 11.1 us
  blocking collectives: 54.7 us -> 71.1 us
  starting transfers between devices: 6.55 us -> 17.6 us
  other arithmetic: 6.04 us -> 0 us
    all_to_all x1 -> x4, waiting for transfers between devices: 92.9 us -> 43.4 us  [the longest x3 37.1 us: on_device(): lax.all_to_all(half, 'pair', split_axis=0, concat_axis=0, tiled=True)]
    dot_general x2 -> x0, matrix products: 30.1 us -> none  [the longest x1 23.2 us: on_device(): jnp.einsum('krs,sj->krj', integrals, coeffs, preferred_element_type=jnp.f...]
    pallas_call x0 -> x6, Pallas kernels: none -> 23.5 us  [the longest x1 13.6 us: quarter_of(): pl.pallas_call(functools.partial(quarter_kernel, rows, starts), grid=(pad...]
    all_to_all x1 -> x4, blocking collectives: 54.7 us -> 71.1 us  [the longest x3 53.1 us: on_device(): lax.all_to_all(quarter, 'mo', split_axis=0, concat_axis=0, tiled=True)]
    all_to_all x2 -> x0, local copies, waits for them, and re-layouts: 14 us -> none  [the longest x1 8.54 us: on_device(): lax.all_to_all(quarter, 'mo', split_axis=2, concat_axis=1, tiled=True)]
    all_to_all x1 -> x4, starting transfers between devices: 6.55 us -> 17.6 us  [the longest x3 14.1 us: on_device(): lax.all_to_all(half, 'pair', split_axis=0, concat_axis=0, tiled=True)]
    convert_element_type x1 -> x0, local copies, waits for them, and re-layouts: 7.91 us -> none  [on_device(): quarter = jnp.einsum('krs,sj->krj', integrals, coeffs, preferred_element_...]
    mul x1 -> x0, other arithmetic: 6.03 us -> none  [on_device(): return 0.5 * (pieces + partner)]
  transfers between devices with their start and end apart: 1 -> 4, of which waited for: 1 -> 4; matrix products, arithmetic and copies ran while one was open for 0% -> 3% of each run, Pallas kernels for 0% -> 2%
where the time goes in v1:
time: 168 us; the launch traced here: 167 us
  blocking collectives  71.1 us (42%)
  waiting for transfers between devices  43.4 us (26%)
  Pallas kernels  23.5 us (14%)
  starting transfers between devices  17.6 us (10%)
  local copies, waits for them, and re-layouts  11.1 us (7%)
    all_to_all x3, blocking collectives, on_device(): lax.all_to_all(quarter, 'mo', split_axis=0, concat_axis=0, tiled=True)  53.1 us
    all_to_all x3, waiting for transfers between devices, on_device(): lax.all_to_all(half, 'pair', split_axis=0, concat_axis=0, tiled=True)  37.1 us
    all_to_all x1, blocking collectives, on_device(): lax.all_to_all(half, 'pair', split_axis=0, concat_axis=0, tiled=True)  18.1 us
    all_to_all x3, starting transfers between devices, on_device(): lax.all_to_all(half, 'pair', split_axis=0, concat_axis=0, tiled=True)  14.1 us
    pallas_call x1, Pallas kernels, quarter_of(): pl.pallas_call(functools.partial(quarter_kernel, rows, starts), grid=(pad...  13.6 us
    all_to_all x1, waiting for transfers between devices, on_device(): lax.all_to_all(quarter, 'mo', split_axis=0, concat_axis=0, tiled=True)  6.27 us
    unnamed x16, local copies, waits for them, and re-layouts  6.06 us
    pallas_call x1, Pallas kernels, combine(): pl.pallas_call(functools.partial(combine_kernel, per_step), grid_spec=plt...  5.85 us
  transfers between devices with their start and end apart: 4, of which 4 were waited for; matrix products, arithmetic and copies ran while one was open for 3% of the time, Pallas kernels for 2%

profile of v1, /device:TPU:0, one launch (start us, length us, event | category | flops | bytes accessed | tf_op | source)
XLA Modules:
  0.0 166.9 jit_solution(732069186755931706)
XLA Ops:
  0.0 0.0 copy-start.5
  0.0 1.2 copy-done.5
  1.2 0.0 copy-start.6
  1.2 13.6 %quarter.1 = (bf16[4,4,256,128]{3,2,1,0:T(8,128)(2,1)S(1)}, bf16[4,4,256,128]{3,2,1,0:T(8,128)(2,1)S(1)}, bf16[4,4,256,128]{3,2,1,0:T(8,128)(2,1)S(1)}, bf16[4,4,256,128]{3,2,1,0:T(8,128)(2,1)}) custom-call(bf16[250,16,1000]{2,1,0:T(8,128)(2,1)} %bitcast.7, bf16[1000,512]{1,0:T(8,128)(2,1)S(1)} %copy-done.5), custom_call_target="tpu_custom_call" | custom-call | flops 4096000000 | bytes 13120000 | tf_op jit(solution)/shard_map/quarter/pallas_call | solution.py:36
  14.8 18.6 %all_to_all.40.a_ref = bf16[4,4,256,128]{3,2,1,0:T(8,128)(2,1)} all-to-all(bf16[4,4,256,128]{3,2,1,0:T(8,128)(2,1)S(1)} %get-tuple-element.9), channel_id=1, replica_groups=mesh['pair'=8,'mo'=4] {'mo'}, dimensions={0} | all-to-all | bytes 2097152 | tf_op jit(solution)/shard_map/all_to_all | solution.py:153
  33.4 17.6 %all_to_all.41.a_ref = bf16[4,4,256,128]{3,2,1,0:T(8,128)(2,1)} all-to-all(bf16[4,4,256,128]{3,2,1,0:T(8,128)(2,1)S(1)} %get-tuple-element.10), channel_id=1, replica_groups=mesh['pair'=8,'mo'=4] {'mo'}, dimensions={0} | all-to-all | bytes 2097152 | tf_op jit(solution)/shard_map/all_to_all | solution.py:153
  51.0 16.9 %all_to_all.42.a_ref = bf16[4,4,256,128]{3,2,1,0:T(8,128)(2,1)S(1)} all-to-all(bf16[4,4,256,128]{3,2,1,0:T(8,128)(2,1)S(1)} %get-tuple-element.11), channel_id=1, replica_groups=mesh['pair'=8,'mo'=4] {'mo'}, dimensions={0} | all-to-all | bytes 2097152 | tf_op jit(solution)/shard_map/all_to_all | solution.py:153
  67.9 3.5 %all-to-all-start.6 = ((bf16[4,4,256,128]{3,2,1,0:T(8,128)(2,1)}), bf16[4,4,256,128]{3,2,1,0:T(8,128)(2,1)S(1)}, u32[]{:S(2)}, u32[]{:S(2)}) async-start(bf16[4,4,256,128]{3,2,1,0:T(8,128)(2,1)} %get-tuple-element.12), calls=%async_computation.6 | async-start | bytes 2097152 | tf_op jit(solution)/shard_map/all_to_all | solution.py:153
  71.4 0.0 copy-done.6
  71.4 1.2 reshape.6
  72.7 2.3 %pad.4 = bf16[512,4,256]{0,2,1:T(8,128)(2,1)} pad(bf16[512,4,250]{0,2,1:T(8,128)(2,1)} %reshape.6, bf16[]{:T(256)} %constant.2.clone.1), padding=0_0x0_0x0_6 | pad | bytes 2072578 | tf_op jit(solution)/shard_map/jit(_pad)/pad | solution.py:149
  75.0 0.0 copy-start.7
  75.0 1.5 copy.6.t_ref
  76.5 0.0 copy-start.1
  76.5 1.2 copy-done.1
  77.7 1.0 half.4
  78.7 0.0 copy-start.3
  78.8 0.8 copy-done.3
  79.6 6.3 %all-to-all-done.6.a_ref = bf16[4,4,256,128]{3,2,1,0:T(8,128)(2,1)S(1)} async-done(((bf16[4,4,256,128]{3,2,1,0:T(8,128)(2,1)}), bf16[4,4,256,128]{3,2,1,0:T(8,128)(2,1)S(1)}, u32[]{:S(2)}, u32[]{:S(2)}) %all-to-all-start.6) | async-done | bytes 1048608 | tf_op jit(solution)/shard_map/all_to_all | solution.py:153
  85.8 6.3 %all-to-all-start.1 = ((bf16[8,4,64,128]{3,2,1,0:T(8,128)(2,1)}), bf16[8,4,64,128]{3,2,1,0:T(8,128)(2,1)}, u32[]{:S(2)}, u32[]{:S(2)}) async-start(bf16[8,4,64,128]{3,2,1,0:T(8,128)(2,1)} %copy-done.3), calls=%async_computation.1 | async-start | bytes 1048576 | tf_op jit(solution)/shard_map/all_to_all | solution.py:155
  92.1 0.0 copy-start
  92.1 1.2 copy-done
  93.3 1.0 half.5
  94.4 0.0 copy-start.4
  94.4 0.8 copy-done.4
  95.2 11.4 %all-to-all-done.1.refs_0_ = bf16[8,4,64,128]{3,2,1,0:T(8,128)(2,1)} async-done(((bf16[8,4,64,128]{3,2,1,0:T(8,128)(2,1)}), bf16[8,4,64,128]{3,2,1,0:T(8,128)(2,1)}, u32[]{:S(2)}, u32[]{:S(2)}) %all-to-all-start.1) | async-done | bytes 524320 | tf_op jit(solution)/shard_map/all_to_all | solution.py:155
  106.5 4.1 %all-to-all-start.3 = ((bf16[8,4,64,128]{3,2,1,0:T(8,128)(2,1)}), bf16[8,4,64,128]{3,2,1,0:T(8,128)(2,1)}, u32[]{:S(2)}, u32[]{:S(2)}) async-start(bf16[8,4,64,128]{3,2,1,0:T(8,128)(2,1)} %copy-done.4), calls=%async_computation.3 | async-start | bytes 1048576 | tf_op jit(solution)/shard_map/all_to_all | solution.py:155
  110.7 1.0 half.6
  111.7 0.0 copy-start.2
  111.7 0.8 copy-done.2
  112.5 12.3 %all-to-all-done.3.refs_1_ = bf16[8,4,64,128]{3,2,1,0:T(8,128)(2,1)} async-done(((bf16[8,4,64,128]{3,2,1,0:T(8,128)(2,1)}), bf16[8,4,64,128]{3,2,1,0:T(8,128)(2,1)}, u32[]{:S(2)}, u32[]{:S(2)}) %all-to-all-start.3) | async-done | bytes 524320 | tf_op jit(solution)/shard_map/all_to_all | solution.py:155
  124.9 3.6 %all-to-all-start.5 = ((bf16[8,4,64,128]{3,2,1,0:T(8,128)(2,1)}), bf16[8,4,64,128]{3,2,1,0:T(8,128)(2,1)S(1)}, u32[]{:S(2)}, u32[]{:S(2)}) async-start(bf16[8,4,64,128]{3,2,1,0:T(8,128)(2,1)} %copy-done.2), calls=%async_computation.5 | async-start | bytes 1048576 | tf_op jit(solution)/shard_map/all_to_all | solution.py:155
  128.5 1.0 half.7
  129.5 13.4 %all-to-all-done.5.refs_2_ = bf16[8,4,64,128]{3,2,1,0:T(8,128)(2,1)S(1)} async-done(((bf16[8,4,64,128]{3,2,1,0:T(8,128)(2,1)}), bf16[8,4,64,128]{3,2,1,0:T(8,128)(2,1)S(1)}, u32[]{:S(2)}, u32[]{:S(2)}) %all-to-all-start.5) | async-done | bytes 524320 | tf_op jit(solution)/shard_map/all_to_all | solution.py:155
  142.9 18.1 %all_to_all.43.refs_3_ = bf16[8,4,64,128]{3,2,1,0:T(8,128)(2,1)S(1)} all-to-all(bf16[8,4,64,128]{3,2,1,0:T(8,128)(2,1)S(1)} %half.7), channel_id=1, replica_groups=mesh['pair'=8,'mo'=4] {'pair'}, dimensions={0} | all-to-all | bytes 1048576 | tf_op jit(solution)/shard_map/all_to_all | solution.py:155
  161.0 0.0 copy-done.7
  161.0 5.9 %combine.1 = f32[128,64,128]{2,1,0:T(8,128)} custom-call(s32[128]{0:T(128)S(1)} %copy-done.7, bf16[8,4,64,128]{3,2,1,0:T(8,128)(2,1)} %all-to-all-done.1.refs_0_, bf16[8,4,64,128]{3,2,1,0:T(8,128)(2,1)} %all-to-all-done.3.refs_1_, bf16[8,4,64,128]{3,2,1,0:T(8,128)(2,1)S(1)} %all-to-all-done.5.refs_2_, bf16[8,4,64,128]{3,2,1,0:T(8,128)(2,1)S(1)} %all_to_all.43.refs_3_), custom_call_target="tpu_custom_call" | custom-call | flops 2097152 | bytes 6291456 | tf_op jit(solution)/shard_map/combine/pallas_call | solution.py:121
Async XLA Ops:
  0.0 1.2 copy-start.5
  1.2 70.2 %copy-start.6 = (bf16[1000,512]{1,0:T(8,128)(2,1)S(1)}, bf16[1000,512]{1,0:T(8,128)(2,1)}, u32[]{:S(2)}) copy-start(bf16[1000,512]{1,0:T(8,128)(2,1)} %c_ref.1) | copy-start | bytes 3072004
  67.9 18.0 %all-to-all-start.6 = ((bf16[4,4,256,128]{3,2,1,0:T(8,128)(2,1)}), bf16[4,4,256,128]{3,2,1,0:T(8,128)(2,1)S(1)}, u32[]{:S(2)}, u32[]{:S(2)}) async-start(bf16[4,4,256,128]{3,2,1,0:T(8,128)(2,1)} %get-tuple-element.12), calls=%async_computation.6 | async-start | bytes 2097152 | tf_op jit(solution)/shard_map/all_to_all | solution.py:153
  75.0 86.0 %copy-start.7 = (s32[128]{0:T(128)S(1)}, s32[128]{0:T(128)}, u32[]{:S(2)}) copy-start(s32[128]{0:T(128)} %mirror_ref.1) | copy-start | bytes 1540
  76.5 1.2 copy-start.1
  78.7 0.8 copy-start.3
  85.8 20.7 %all-to-all-start.1 = ((bf16[8,4,64,128]{3,2,1,0:T(8,128)(2,1)}), bf16[8,4,64,128]{3,2,1,0:T(8,128)(2,1)}, u32[]{:S(2)}, u32[]{:S(2)}) async-start(bf16[8,4,64,128]{3,2,1,0:T(8,128)(2,1)} %copy-done.3), calls=%async_computation.1 | async-start | bytes 1048576 | tf_op jit(solution)/shard_map/all_to_all | solution.py:155
  92.1 1.2 copy-start
  94.4 0.8 copy-start.4
  106.5 18.3 %all-to-all-start.3 = ((bf16[8,4,64,128]{3,2,1,0:T(8,128)(2,1)}), bf16[8,4,64,128]{3,2,1,0:T(8,128)(2,1)}, u32[]{:S(2)}, u32[]{:S(2)}) async-start(bf16[8,4,64,128]{3,2,1,0:T(8,128)(2,1)} %copy-done.4), calls=%async_computation.3 | async-start | bytes 1048576 | tf_op jit(solution)/shard_map/all_to_all | solution.py:155
  111.7 0.8 copy-start.2
  124.9 18.1 %all-to-all-start.5 = ((bf16[8,4,64,128]{3,2,1,0:T(8,128)(2,1)}), bf16[8,4,64,128]{3,2,1,0:T(8,128)(2,1)S(1)}, u32[]{:S(2)}, u32[]{:S(2)}) async-start(bf16[8,4,64,128]{3,2,1,0:T(8,128)(2,1)} %copy-done.2), calls=%async_computation.5 | async-start | bytes 1048576 | tf_op jit(solution)/shard_map/all_to_all | solution.py:155

commit v2 on v1

v2 whole, which is shorter than its diff:
```python
import functools

import jax
import jax.numpy as jnp
from jax import lax
from jax.experimental import pallas as pl
from jax.experimental.pallas import tpu as pltpu
from jax.sharding import PartitionSpec as P

LANES = 128
STEP = 64
CHUNKS = (4, 4, 4, 4)
VMEM = 48 * 1024 * 1024


def quarter_kernel(rows, me_ref, x_ref, c_ref, *refs):
    outs, acc = refs[:-1], refs[-1]
    step, k_all, depth = x_ref.shape
    x = x_ref[...].reshape(step * k_all, depth)
    product = jnp.dot(x, c_ref[...], preferred_element_type=jnp.float32)
    for d in range(2):
        acc[d] = product[:, d * LANES : (d + 1) * LANES]
    left = rows - pl.program_id(0) * step
    keep = lax.broadcasted_iota(jnp.int32, (step, LANES), 0) < left
    first = 0
    for c in range(len(CHUNKS)):
        for flip in range(2):
            out = outs[2 * c + flip]
            d = (me_ref[0] & 1) ^ flip
            for k in range(out.shape[0]):
                block = acc[d, pl.ds(first + k, step, stride=k_all), :]
                out[k] = jnp.where(keep, block, 0.0).astype(jnp.bfloat16)
        first += CHUNKS[c]


def quarter_of(me, by_r, coeffs, far, padded):
    rows, k_all, depth = by_r.shape
    outs = [jax.ShapeDtypeStruct((kc, padded, LANES), jnp.bfloat16) for kc in CHUNKS for _ in range(2)]
    out = pl.pallas_call(
        functools.partial(quarter_kernel, rows),
        grid_spec=pltpu.PrefetchScalarGridSpec(
            num_scalar_prefetch=1,
            grid=(padded // STEP,),
            in_specs=[
                pl.BlockSpec((STEP, k_all, depth), lambda r, me: (r, 0, 0)),
                pl.BlockSpec((depth, 2 * LANES), lambda r, me: (0, (me[0] >> 1) ^ far)),
            ],
            out_specs=[pl.BlockSpec((o.shape[0], STEP, LANES), lambda r, me: (0, r, 0)) for o in outs],
            scratch_shapes=[pltpu.VMEM((2, STEP * k_all, LANES), jnp.float32)],
        ),
        out_shape=outs,
        compiler_params=pltpu.CompilerParams(vmem_limit_bytes=VMEM),
        cost_estimate=pl.CostEstimate(
            flops=2 * rows * k_all * depth * 2 * LANES,
            bytes_accessed=2 * (by_r.size + (depth + padded * k_all) * 2 * LANES),
            transcendentals=0,
        ),
        name=f"quarter{far}",
    )(me, by_r, coeffs)
    return [out[2 * c : 2 * c + 2] for c in range(len(CHUNKS))]


def half_kernel(me_ref, *refs):
    arrived, t_ref, out_ref = refs[:-2], refs[-2], refs[-1]
    n_pair, pair, block, lanes = out_ref.shape
    half = None
    for o, a_ref in enumerate(arrived):
        columns = jnp.concatenate([a_ref[k] for k in range(pair)], axis=1)
        part = jnp.dot(t_ref[me_ref[0] ^ o], columns, preferred_element_type=jnp.float32)
        half = part if half is None else half + part
    half = half.astype(jnp.bfloat16)
    for k in range(pair):
        out_ref[:, k] = half[:, k * lanes : (k + 1) * lanes].reshape(n_pair, block, lanes)


def half_of(me, arrived, turned, n_pair):
    kc, padded, lanes = arrived[0].shape
    n_mo, orbitals, _ = turned.shape
    block = orbitals // n_pair
    return pl.pallas_call(
        half_kernel,
        grid_spec=pltpu.PrefetchScalarGridSpec(
            num_scalar_prefetch=1,
            grid=(kc // 2,),
            in_specs=[pl.BlockSpec((2, padded, lanes), lambda k, me: (k, 0, 0))] * n_mo
            + [pl.BlockSpec(turned.shape, lambda k, me: (0, 0, 0))],
            out_specs=pl.BlockSpec((n_pair, 2, block, lanes), lambda k, me: (0, k, 0, 0)),
        ),
        out_shape=jax.ShapeDtypeStruct((n_pair, kc, block, lanes), jnp.bfloat16),
        compiler_params=pltpu.CompilerParams(vmem_limit_bytes=VMEM),
        cost_estimate=pl.CostEstimate(
            flops=2 * orbitals * n_mo * padded * kc * lanes,
            bytes_accessed=2 * (n_mo * arrived[0].size + turned.size + orbitals * kc * lanes),
            transcendentals=0,
        ),
        name="half",
    )(me, *arrived, turned)


def combine_kernel(per_step, mirror_ref, *refs):
    pieces, out_ref, held, sems = refs[:-3], refs[-3], refs[-2], refs[-1]
    step = pl.program_id(0)

    @pl.when(step == 0)
    def _():
        first = 0
        copies = []
        for c, piece in enumerate(pieces):
            kc = piece.shape[1]
            copies.append(pltpu.make_async_copy(piece, held.at[:, first : first + kc], sems.at[c]))
            first += kc
        for copy in copies:
            copy.start()
        for copy in copies:
            copy.wait()

    k_all = held.shape[1]
    for n in range(per_step):
        k = step * per_step + n
        m = mirror_ref[k]
        own = held[k // k_all, lax.rem(k, k_all)].astype(jnp.float32)
        partner = held[m // k_all, lax.rem(m, k_all)].astype(jnp.float32)
        out_ref[n] = 0.5 * (own + partner)


def combine(pieces, mirror):
    n_pair, _, block, lanes = pieces[0].shape
    k_all = sum(p.shape[1] for p in pieces)
    rows = n_pair * k_all
    per_step = max(1, 32 * 64 // block)
    return pl.pallas_call(
        functools.partial(combine_kernel, per_step),
        grid_spec=pltpu.PrefetchScalarGridSpec(
            num_scalar_prefetch=1,
            grid=(rows // per_step,),
            in_specs=[pl.BlockSpec(memory_space=pl.ANY)] * len(pieces),
            out_specs=pl.BlockSpec((per_step, block, lanes), lambda k, m: (k, 0, 0)),
            scratch_shapes=[
                pltpu.VMEM((n_pair, k_all, block, lanes), jnp.bfloat16),
                pltpu.SemaphoreType.DMA((len(pieces),)),
            ],
        ),
        out_shape=jax.ShapeDtypeStruct((rows, block, lanes), jnp.float32),
        compiler_params=pltpu.CompilerParams(vmem_limit_bytes=VMEM),
        cost_estimate=pl.CostEstimate(
            flops=2 * rows * block * lanes,
            bytes_accessed=6 * rows * block * lanes,
            transcendentals=0,
        ),
        name="combine",
    )(mirror, *pieces)


def flipped(x, axis, size, offset):
    if offset == 0:
        return x
    return lax.ppermute(x, axis, [(i, i ^ offset) for i in range(size)])


def on_device(n_pair, n_mo, integrals, coeffs, mirror):
    k_all, rows, depth = integrals.shape
    orbitals = coeffs.shape[1]
    padded = -(-rows // STEP) * STEP
    by_r = jnp.transpose(integrals, (1, 0, 2))
    me = lax.axis_index("mo").astype(jnp.int32).reshape(1)
    turned = jnp.pad(coeffs.reshape(n_mo, rows, orbitals), ((0, 0), (0, padded - rows), (0, 0)))
    turned = jnp.transpose(turned, (0, 2, 1))
    quarters = [[None] * n_mo for _ in CHUNKS]
    for far in reversed(range(n_mo // 2)):
        for c, blocks in enumerate(quarter_of(me, by_r, coeffs, far, padded)):
            quarters[c][2 * far : 2 * far + 2] = blocks
    pieces = []
    for blocks in quarters:
        arrived = [flipped(b, "mo", n_mo, o) for o, b in enumerate(blocks)]
        half = half_of(me, arrived, turned, n_pair)
        pieces.append(lax.all_to_all(half, "pair", split_axis=0, concat_axis=0, tiled=True))
    return combine(pieces, mirror)


def solution(mesh):
    return jax.shard_map(
        functools.partial(on_device, mesh.shape["pair"], mesh.shape["mo"]),
        mesh=mesh,
        in_specs=(P("pair", "mo", None), P(), P()),
        out_specs=P(None, "pair", "mo"),
        check_vma=False,
    )
```

time: 168 us -> 116 us (0.69)
  blocking collectives: 71.1 us -> 19.8 us
  starting transfers between devices: 17.6 us -> 26.9 us
  waiting for transfers between devices: 43.4 us -> 35.1 us
    all_to_all x3 -> x0, blocking collectives: 53.1 us -> none  [on_device(): lax.all_to_all(quarter, 'mo', split_axis=0, concat_axis=0, tiled=True)]
    all_to_all x3, waiting for transfers between devices: 37.1 us -> 1.46 us  [on_device(): lax.all_to_all(half, 'pair', split_axis=0, concat_axis=0, tiled=True)]
    ppermute x0 -> x12, waiting for transfers between devices: none -> 33.6 us  [flipped(): return lax.ppermute(x, axis, [(i, i ^ offset) for i in range(size)])]
    ppermute x0 -> x12, starting transfers between devices: none -> 10.3 us  [flipped(): return lax.ppermute(x, axis, [(i, i ^ offset) for i in range(size)])]
    all_to_all x1 -> x0, waiting for transfers between devices: 6.27 us -> none  [on_device(): lax.all_to_all(quarter, 'mo', split_axis=0, concat_axis=0, tiled=True)]
    all_to_all x1 -> x0, starting transfers between devices: 3.52 us -> none  [on_device(): lax.all_to_all(quarter, 'mo', split_axis=0, concat_axis=0, tiled=True)]
    all_to_all x3, starting transfers between devices: 14.1 us -> 16.6 us  [on_device(): lax.all_to_all(half, 'pair', split_axis=0, concat_axis=0, tiled=True)]
    pallas_call x5 -> x6, Pallas kernels: 17.7 us -> 20.1 us  [the longest x2 14.4 us: quarter_of(): pl.pallas_call(functools.partial(quarter_kernel, rows), grid_spec=pltpu.P...]
  transfers between devices with their start and end apart: 4 -> 15, of which waited for: 4 -> 8; matrix products, arithmetic and copies ran while one was open for 3% -> 4% of each run, Pallas kernels for 2% -> 10%
where the time goes in v2:
time: 116 us
  waiting for transfers between devices  35.1 us (30%)
  starting transfers between devices  26.9 us (23%)
  Pallas kernels  23.9 us (21%)
  blocking collectives  19.8 us (17%)
  local copies, waits for them, and re-layouts  9.71 us (8%)
    ppermute x12, waiting for transfers between devices, flipped(): return lax.ppermute(x, axis, [(i, i ^ offset) for i in range(size)])  33.6 us
    all_to_all x1, blocking collectives, on_device(): lax.all_to_all(half, 'pair', split_axis=0, concat_axis=0, tiled=True)  19.8 us
    all_to_all x3, starting transfers between devices, on_device(): lax.all_to_all(half, 'pair', split_axis=0, concat_axis=0, tiled=True)  16.6 us
    pallas_call x2, Pallas kernels, quarter_of(): pl.pallas_call(functools.partial(quarter_kernel, rows), grid_spec=pltpu.P...  14.4 us
    ppermute x12, starting transfers between devices, flipped(): return lax.ppermute(x, axis, [(i, i ^ offset) for i in range(size)])  10.3 us
    pallas_call x4, Pallas kernels, half_of(): pl.pallas_call(half_kernel, grid_spec=pltpu.PrefetchScalarGridSpec(num_sc...  5.77 us
    unnamed x20, local copies, waits for them, and re-layouts  4.78 us
    pallas_call x1, Pallas kernels, combine(): pl.pallas_call(functools.partial(combine_kernel, per_step), grid_spec=plt...  3.8 us
  transfers between devices with their start and end apart: 15, of which 8 were waited for; matrix products, arithmetic and copies ran while one was open for 4% of the time, Pallas kernels for 10%

profile of v2, /device:TPU:0, one launch (start us, length us, event | category | flops | bytes accessed | tf_op | source)
XLA Modules:
  0.0 115.5 jit_solution(10199414554487774334)
XLA Ops:
  0.0 1.2 %copy-done = bf16[1000,512]{1,0:T(8,128)(2,1)S(1)} copy-done((bf16[1000,512]{1,0:T(8,128)(2,1)S(1)}, bf16[1000,512]{1,0:T(8,128)(2,1)}, u32[]{:S(2)}) %copy-start) | copy-done | bytes 1024024
  1.2 7.3 %quarter1.1 = (bf16[4,256,128]{2,1,0:T(8,128)(2,1)}, bf16[4,256,128]{2,1,0:T(8,128)(2,1)}, bf16[4,256,128]{2,1,0:T(8,128)(2,1)S(1)}, bf16[4,256,128]{2,1,0:T(8,1...) custom-call(s32[1]{0:T(128)} %bitcast.me_ref, ...), custom_call_target="tpu_custom_call" | custom-call | flops 2048000000 | bytes 10609152 | tf_op jit(solution)/shard_map/quarter1/pallas_call | solution.py:39
  8.5 0.7 copy-done.7
  9.2 0.7 copy-done.8
  9.9 3.0 %collective-permute-start.1 = (bf16[4,256,128]{2,1,0:T(8,128)(2,1)}, bf16[4,256,128]{2,1,0:T(8,128)(2,1)S(1)}, u32[]{:S(2)}, u32[]{:S(2)}) collective-permute-start(bf16[4,256,128]{2,1,0:T(8,128)(2,1)} %get-tuple-element.23), channel_id=1, source_target_pairs={{0,2},{1,3},{2,0},{3,1},{4,6},{5,7},{6,4},{7,5},{8,10},{9,11},{10,... | collective-permute-start | bytes 786440 | tf_op jit(solution)/shard_map/ppermute | solution.py:157
  12.9 0.0 copy-done.4
  12.9 0.2 collective-permute-start.2
  13.1 7.1 %quarter0.1 = (bf16[4,256,128]{2,1,0:T(8,128)(2,1)S(1)}, bf16[4,256,128]{2,1,0:T(8,128)(2,1)}, bf16[4,256,128]{2,1,0:T(8,128)(2,1)S(1)}, bf16[4,256,128]{2,1,0:T...) custom-call(s32[1]{0:T(128)} %bitcast.me_ref, ...), custom_call_target="tpu_custom_call" | custom-call | flops 2048000000 | bytes 10609152 | tf_op jit(solution)/shard_map/quarter0/pallas_call | solution.py:39
  20.2 0.7 copy-done.3
  20.9 0.7 copy-done.9
  21.6 0.7 copy-done.6
  22.3 0.7 collective-permute-start
  23.0 1.2 %reshape.7 = bf16[4,250,512]{2,1,0:T(8,128)(2,1)} reshape(bf16[1000,512]{1,0:T(8,128)(2,1)S(1)} %copy-done.1) | data formatting | bytes 2048000 | tf_op jit(solution)/shard_map/reshape | solution.py:166
  24.2 2.3 %copy.4 = bf16[4,250,512]{1,2,0:T(8,128)(2,1)} copy(bf16[4,250,512]{2,1,0:T(8,128)(2,1)} %reshape.7) | data formatting | bytes 2048000 | tf_op jit(solution)/shard_map/reshape | solution.py:166
  26.5 1.4 %pad_bitcast_fusion.refs_4_ = bf16[4,512,256]{2,1,0:T(8,128)(2,1)S(1)} fusion(bf16[4,250,512]{1,2,0:T(8,128)(2,1)} %copy.4), kind=kLoop, calls=%fused_computation | loop fusion | bytes 2072576 | tf_op jit(solution)/shard_map/transpose | solution.py:167
  27.9 0.0 collective-permute-done.1.refs_2_
  27.9 0.0 collective-permute-done.2.refs_3_
  28.0 0.0 collective-permute-done.refs_1_
  28.0 1.6 %half.4 = bf16[8,4,64,128]{3,2,1,0:T(8,128)(2,1)} custom-call(s32[1]{0:T(128)} %bitcast.me_ref, bf16[4,256,128]{2,1,0:T(8,128)(2,1)S(1)} %get-tuple-element.21.refs_0_, bf16[4,256,128]{2,1,0:T(8,128)(2,1)S(1)} %collective-permute-done.refs_1_, bf16[4,256,128]{2,1,0:T(8,128)(2,1)S(1)} %collective-permute-done.1.refs_2_, ...), custom_call_target="tpu_custom_call" | custom-call | flops 536870912 | bytes 2621440 | tf_op jit(solution)/shard_map/half/pallas_call | solution.py:80
  29.6 5.8 %all-to-all-start = ((bf16[8,4,64,128]{3,2,1,0:T(8,128)(2,1)}), bf16[8,4,64,128]{3,2,1,0:T(8,128)(2,1)S(1)}, u32[]{:S(2)}, u32[]{:S(2)}) async-start(bf16[8,4,64,128]{3,2,1,0:T(8,128)(2,1)} %half.4), calls=%async_computation | async-start | bytes 1048576 | tf_op jit(solution)/shard_map/all_to_all | solution.py:176
  35.4 1.2 %collective-permute-start.4 = (bf16[4,256,128]{2,1,0:T(8,128)(2,1)}, bf16[4,256,128]{2,1,0:T(8,128)(2,1)S(1)}, u32[]{:S(2)}, u32[]{:S(2)}) collective-permute-start(bf16[4,256,128]{2,1,0:T(8,128)(2,1)} %copy-done.8), channel_id=1, source_target_pairs={{0,2},{1,3},{2,0},{3,1},{4,6},{5,7},{6,4},{7,5},{8,10},{9,11},{10,... | collective-permute-start | bytes 786440 | tf_op jit(solution)/shard_map/ppermute | solution.py:157
  36.7 0.0 collective-permute-start.5
  36.7 0.9 collective-permute-start.3
  37.5 7.3 %collective-permute-done.4.refs_2_ = bf16[4,256,128]{2,1,0:T(8,128)(2,1)S(1)} collective-permute-done((bf16[4,256,128]{2,1,0:T(8,128)(2,1)}, bf16[4,256,128]{2,1,0:T(8,128)(2,1)S(1)}, u32[]{:S(2)}, u32[]{:S(2)}) %collective-permute-start.4) | collective-permute-done | bytes 262176 | tf_op jit(solution)/shard_map/ppermute | solution.py:157
  44.8 3.2 %collective-permute-done.5.refs_3_ = bf16[4,256,128]{2,1,0:T(8,128)(2,1)S(1)} collective-permute-done((bf16[4,256,128]{2,1,0:T(8,128)(2,1)}, bf16[4,256,128]{2,1,0:T(8,128)(2,1)S(1)}, u32[]{:S(2)}, u32[]{:S(2)}) %collective-permute-start.5) | collective-permute-done | bytes 262176 | tf_op jit(solution)/shard_map/ppermute | solution.py:157
  48.0 0.0 collective-permute-done.3.refs_1_
  48.0 1.6 %half.5 = bf16[8,4,64,128]{3,2,1,0:T(8,128)(2,1)} custom-call(s32[1]{0:T(128)} %bitcast.me_ref, bf16[4,256,128]{2,1,0:T(8,128)(2,1)S(1)} %get-tuple-element.25.refs_0_, bf16[4,256,128]{2,1,0:T(8,128)(2,1)S(1)} %collective-permute-done.3.refs_1_, bf16[4,256,128]{2,1,0:T(8,128)(2,1)S(1)} %collective-permute-done.4.refs_2_, ...), custom_call_target="tpu_custom_call" | custom-call | flops 536870912 | bytes 2621440 | tf_op jit(solution)/shard_map/half/pallas_call | solution.py:80
  49.7 0.4 all-to-all-done.refs_0_
  50.1 5.3 %all-to-all-start.1 = ((bf16[8,4,64,128]{3,2,1,0:T(8,128)(2,1)}), bf16[8,4,64,128]{3,2,1,0:T(8,128)(2,1)S(1)}, u32[]{:S(2)}, u32[]{:S(2)}) async-start(bf16[8,4,64,128]{3,2,1,0:T(8,128)(2,1)} %half.5), calls=%async_computation.1 | async-start | bytes 1048576 | tf_op jit(solution)/shard_map/all_to_all | solution.py:176
  55.4 0.8 collective-permute-start.7
  56.2 1.2 %collective-permute-start.8 = (bf16[4,256,128]{2,1,0:T(8,128)(2,1)}, bf16[4,256,128]{2,1,0:T(8,128)(2,1)S(1)}, u32[]{:S(2)}, u32[]{:S(2)}) collective-permute-start(bf16[4,256,128]{2,1,0:T(8,128)(2,1)} %copy-done.4), channel_id=1, source_target_pairs={{0,3},{1,2},{2,1},{3,0},{4,7},{5,6},{6,5},{7,4},{8,11},{9,10},{10,... | collective-permute-start | bytes 786440 | tf_op jit(solution)/shard_map/ppermute | solution.py:157
  57.4 0.1 collective-permute-start.6
  57.5 7.2 %collective-permute-done.7.refs_2_ = bf16[4,256,128]{2,1,0:T(8,128)(2,1)S(1)} collective-permute-done((bf16[4,256,128]{2,1,0:T(8,128)(2,1)}, bf16[4,256,128]{2,1,0:T(8,128)(2,1)S(1)}, u32[]{:S(2)}, u32[]{:S(2)}) %collective-permute-start.7) | collective-permute-done | bytes 262176 | tf_op jit(solution)/shard_map/ppermute | solution.py:157
  64.8 5.0 %collective-permute-done.8.refs_3_ = bf16[4,256,128]{2,1,0:T(8,128)(2,1)S(1)} collective-permute-done((bf16[4,256,128]{2,1,0:T(8,128)(2,1)}, bf16[4,256,128]{2,1,0:T(8,128)(2,1)S(1)}, u32[]{:S(2)}, u32[]{:S(2)}) %collective-permute-start.8) | collective-permute-done | bytes 262176 | tf_op jit(solution)/shard_map/ppermute | solution.py:157
  69.8 0.0 collective-permute-done.6.refs_1_
  69.8 1.6 %half.6 = bf16[8,4,64,128]{3,2,1,0:T(8,128)(2,1)} custom-call(s32[1]{0:T(128)} %bitcast.me_ref, bf16[4,256,128]{2,1,0:T(8,128)(2,1)S(1)} %get-tuple-element.29.refs_0_, bf16[4,256,128]{2,1,0:T(8,128)(2,1)S(1)} %collective-permute-done.6.refs_1_, bf16[4,256,128]{2,1,0:T(8,128)(2,1)S(1)} %collective-permute-done.7.refs_2_, ...), custom_call_target="tpu_custom_call" | custom-call | flops 536870912 | bytes 2621440 | tf_op jit(solution)/shard_map/half/pallas_call | solution.py:80
  71.4 0.0 all-to-all-done.1.refs_1_
  71.4 5.5 %all-to-all-start.2 = ((bf16[8,4,64,128]{3,2,1,0:T(8,128)(2,1)}), bf16[8,4,64,128]{3,2,1,0:T(8,128)(2,1)S(1)}, u32[]{:S(2)}, u32[]{:S(2)}) async-start(bf16[8,4,64,128]{3,2,1,0:T(8,128)(2,1)} %half.6), calls=%async_computation.2 | async-start | bytes 1048576 | tf_op jit(solution)/shard_map/all_to_all | solution.py:176
  76.9 1.7 %collective-permute-start.10 = (bf16[4,256,128]{2,1,0:T(8,128)(2,1)S(1)}, bf16[4,256,128]{2,1,0:T(8,128)(2,1)S(1)}, u32[]{:S(2)}, u32[]{:S(2)}) collective-permute-start(bf16[4,256,128]{2,1,0:T(8,128)(2,1)S(1)} %get-tuple-element.35), channel_id=1, source_target_pairs={{0,2},{1,3},{2,0},{3,1},{4,6},{5,7},{6,4},{7,5},{8,10},{9,11},{10,... | collective-permute-start | bytes 786440 | tf_op jit(solution)/shard_map/ppermute | solution.py:157
  78.5 0.0 collective-permute-start.11
  78.5 0.5 collective-permute-start.9
  79.0 7.0 %collective-permute-done.10.refs_2_ = bf16[4,256,128]{2,1,0:T(8,128)(2,1)S(1)} collective-permute-done((bf16[4,256,128]{2,1,0:T(8,128)(2,1)S(1)}, bf16[4,256,128]{2,1,0:T(8,128)(2,1)S(1)}, u32[]{:S(2)}, u32[]{:S(2)}) %collective-permute-start.10) | collective-permute-done | bytes 262176 | tf_op jit(solution)/shard_map/ppermute | solution.py:157
  86.0 3.9 %collective-permute-done.11.refs_3_ = bf16[4,256,128]{2,1,0:T(8,128)(2,1)S(1)} collective-permute-done((bf16[4,256,128]{2,1,0:T(8,128)(2,1)S(1)}, bf16[4,256,128]{2,1,0:T(8,128)(2,1)S(1)}, u32[]{:S(2)}, u32[]{:S(2)}) %collective-permute-start.11) | collective-permute-done | bytes 262176 | tf_op jit(solution)/shard_map/ppermute | solution.py:157
  89.9 0.0 collective-permute-done.9.refs_1_
  89.9 0.9 half.7
  90.8 1.1 all-to-all-done.2.refs_2_
  91.9 19.8 %all_to_all.20.refs_3_ = bf16[8,4,64,128]{3,2,1,0:T(8,128)(2,1)S(1)} all-to-all(bf16[8,4,64,128]{3,2,1,0:T(8,128)(2,1)S(1)} %half.7), channel_id=1, replica_groups=mesh['pair'=8,'mo'=4] {'pair'}, dimensions={0} | all-to-all | bytes 1048576 | tf_op jit(solution)/shard_map/all_to_all | solution.py:176
  111.7 3.8 %combine.1 = f32[128,64,128]{2,1,0:T(8,128)} custom-call(s32[128]{0:T(128)S(1)} %copy-done.2, bf16[8,4,64,128]{3,2,1,0:T(8,128)(2,1)S(1)} %all-to-all-done.refs_0_, bf16[8,4,64,128]{3,2,1,0:T(8,128)(2,1)S(1)} %all-to-all-done.1.refs_1_, bf16[8,4,64,128]{3,2,1,0:T(8,128)(2,1)S(1)} %all-to-all-done.2.refs_2_, bf16[8,4,64,128]{3,2,1,0:T(8,128)(2,1)S(1)} %all_to_all.20.refs_3_), custom_call_target="tpu_custom_call" | custom-call | flops 2097152 | bytes 6291456 | tf_op jit(solution)/shard_map/combine/pallas_call | solution.py:131
  (13 shorter events, 0.0 us)
Async XLA Ops:
  0.0 1.2 %copy-start = (bf16[1000,512]{1,0:T(8,128)(2,1)S(1)}, bf16[1000,512]{1,0:T(8,128)(2,1)}, u32[]{:S(2)}) copy-start(bf16[1000,512]{1,0:T(8,128)(2,1)} %c_ref.3) | copy-start | bytes 3072004
  1.2 21.8 %copy-start.1 = (bf16[1000,512]{1,0:T(8,128)(2,1)S(1)}, bf16[1000,512]{1,0:T(8,128)(2,1)}, u32[]{:S(2)}) copy-start(bf16[1000,512]{1,0:T(8,128)(2,1)} %c_ref.3) | copy-start | bytes 3072004
  8.5 0.7 copy-start.7
  9.2 0.7 copy-start.8
  9.9 3.0 %copy-start.4 = (bf16[4,256,128]{2,1,0:T(8,128)(2,1)}, bf16[4,256,128]{2,1,0:T(8,128)(2,1)S(1)}, u32[]{:S(2)}) copy-start(bf16[4,256,128]{2,1,0:T(8,128)(2,1)S(1)} %get-tuple-element.32) | copy-start | bytes 786436
  9.9 3.0 %copy-start.5 = (bf16[4,256,128]{2,1,0:T(8,128)(2,1)}, bf16[4,256,128]{2,1,0:T(8,128)(2,1)S(1)}, u32[]{:S(2)}) copy-start(bf16[4,256,128]{2,1,0:T(8,128)(2,1)S(1)} %get-tuple-element.31) | copy-start | bytes 786436
  9.9 18.0 %collective-permute-start.1 = (bf16[4,256,128]{2,1,0:T(8,128)(2,1)}, bf16[4,256,128]{2,1,0:T(8,128)(2,1)S(1)}, u32[]{:S(2)}, u32[]{:S(2)}) collective-permute-start(bf16[4,256,128]{2,1,0:T(8,128)(2,1)} %get-tuple-element.23), channel_id=1, source_target_pairs={{0,2},{1,3},{2,0},{3,1},{4,6},{5,7},{6,4},{7,5},{8,10},{9,11},{10,... | collective-permute-start | bytes 786440 | tf_op jit(solution)/shard_map/ppermute | solution.py:157
  12.9 15.1 %collective-permute-start.2 = (bf16[4,256,128]{2,1,0:T(8,128)(2,1)}, bf16[4,256,128]{2,1,0:T(8,128)(2,1)S(1)}, u32[]{:S(2)}, u32[]{:S(2)}) collective-permute-start(bf16[4,256,128]{2,1,0:T(8,128)(2,1)} %get-tuple-element.24), channel_id=1, source_target_pairs={{0,3},{1,2},{2,1},{3,0},{4,7},{5,6},{6,5},{7,4},{8,11},{9,10},{10,... | collective-permute-start | bytes 786440 | tf_op jit(solution)/shard_map/ppermute | solution.py:157
  20.2 0.7 copy-start.3
  20.9 0.7 copy-start.9
  21.6 0.7 copy-start.6
  22.3 5.6 %collective-permute-start = (bf16[4,256,128]{2,1,0:T(8,128)(2,1)}, bf16[4,256,128]{2,1,0:T(8,128)(2,1)S(1)}, u32[]{:S(2)}, u32[]{:S(2)}) collective-permute-start(bf16[4,256,128]{2,1,0:T(8,128)(2,1)} %get-tuple-element.22), channel_id=1, source_target_pairs={{0,1},{1,0},{2,3},{3,2},{4,5},{5,4},{6,7},{7,6},{8,9},{9,8},{10,11... | collective-permute-start | bytes 786440 | tf_op jit(solution)/shard_map/ppermute | solution.py:157
  26.5 85.2 %copy-start.2 = (s32[128]{0:T(128)S(1)}, s32[128]{0:T(128)}, u32[]{:S(2)}) copy-start(s32[128]{0:T(128)} %mirror_ref.1) | copy-start | bytes 1540
  29.6 20.5 %all-to-all-start = ((bf16[8,4,64,128]{3,2,1,0:T(8,128)(2,1)}), bf16[8,4,64,128]{3,2,1,0:T(8,128)(2,1)S(1)}, u32[]{:S(2)}, u32[]{:S(2)}) async-start(bf16[8,4,64,128]{3,2,1,0:T(8,128)(2,1)} %half.4), calls=%async_computation | async-start | bytes 1048576 | tf_op jit(solution)/shard_map/all_to_all | solution.py:176
  35.4 9.4 %collective-permute-start.4 = (bf16[4,256,128]{2,1,0:T(8,128)(2,1)}, bf16[4,256,128]{2,1,0:T(8,128)(2,1)S(1)}, u32[]{:S(2)}, u32[]{:S(2)}) collective-permute-start(bf16[4,256,128]{2,1,0:T(8,128)(2,1)} %copy-done.8), channel_id=1, source_target_pairs={{0,2},{1,3},{2,0},{3,1},{4,6},{5,7},{6,4},{7,5},{8,10},{9,11},{10,... | collective-permute-start | bytes 786440 | tf_op jit(solution)/shard_map/ppermute | solution.py:157
  36.7 11.4 %collective-permute-start.5 = (bf16[4,256,128]{2,1,0:T(8,128)(2,1)}, bf16[4,256,128]{2,1,0:T(8,128)(2,1)S(1)}, u32[]{:S(2)}, u32[]{:S(2)}) collective-permute-start(bf16[4,256,128]{2,1,0:T(8,128)(2,1)} %copy-done.7), channel_id=1, source_target_pairs={{0,3},{1,2},{2,1},{3,0},{4,7},{5,6},{6,5},{7,4},{8,11},{9,10},{10,... | collective-permute-start | bytes 786440 | tf_op jit(solution)/shard_map/ppermute | solution.py:157
  36.7 11.4 %collective-permute-start.3 = (bf16[4,256,128]{2,1,0:T(8,128)(2,1)}, bf16[4,256,128]{2,1,0:T(8,128)(2,1)S(1)}, u32[]{:S(2)}, u32[]{:S(2)}) collective-permute-start(bf16[4,256,128]{2,1,0:T(8,128)(2,1)} %copy-done.9), channel_id=1, source_target_pairs={{0,1},{1,0},{2,3},{3,2},{4,5},{5,4},{6,7},{7,6},{8,9},{9,8},{10,11... | collective-permute-start | bytes 786440 | tf_op jit(solution)/shard_map/ppermute | solution.py:157
  50.1 21.3 %all-to-all-start.1 = ((bf16[8,4,64,128]{3,2,1,0:T(8,128)(2,1)}), bf16[8,4,64,128]{3,2,1,0:T(8,128)(2,1)S(1)}, u32[]{:S(2)}, u32[]{:S(2)}) async-start(bf16[8,4,64,128]{3,2,1,0:T(8,128)(2,1)} %half.5), calls=%async_computation.1 | async-start | bytes 1048576 | tf_op jit(solution)/shard_map/all_to_all | solution.py:176
  55.4 9.4 %collective-permute-start.7 = (bf16[4,256,128]{2,1,0:T(8,128)(2,1)}, bf16[4,256,128]{2,1,0:T(8,128)(2,1)S(1)}, u32[]{:S(2)}, u32[]{:S(2)}) collective-permute-start(bf16[4,256,128]{2,1,0:T(8,128)(2,1)} %copy-done.5), channel_id=1, source_target_pairs={{0,2},{1,3},{2,0},{3,1},{4,6},{5,7},{6,4},{7,5},{8,10},{9,11},{10,... | collective-permute-start | bytes 786440 | tf_op jit(solution)/shard_map/ppermute | solution.py:157
  56.2 13.6 %collective-permute-start.8 = (bf16[4,256,128]{2,1,0:T(8,128)(2,1)}, bf16[4,256,128]{2,1,0:T(8,128)(2,1)S(1)}, u32[]{:S(2)}, u32[]{:S(2)}) collective-permute-start(bf16[4,256,128]{2,1,0:T(8,128)(2,1)} %copy-done.4), channel_id=1, source_target_pairs={{0,3},{1,2},{2,1},{3,0},{4,7},{5,6},{6,5},{7,4},{8,11},{9,10},{10,... | collective-permute-start | bytes 786440 | tf_op jit(solution)/shard_map/ppermute | solution.py:157
  57.4 12.4 %collective-permute-start.6 = (bf16[4,256,128]{2,1,0:T(8,128)(2,1)}, bf16[4,256,128]{2,1,0:T(8,128)(2,1)S(1)}, u32[]{:S(2)}, u32[]{:S(2)}) collective-permute-start(bf16[4,256,128]{2,1,0:T(8,128)(2,1)} %copy-done.6), channel_id=1, source_target_pairs={{0,1},{1,0},{2,3},{3,2},{4,5},{5,4},{6,7},{7,6},{8,9},{9,8},{10,11... | collective-permute-start | bytes 786440 | tf_op jit(solution)/shard_map/ppermute | solution.py:157
  71.4 20.5 %all-to-all-start.2 = ((bf16[8,4,64,128]{3,2,1,0:T(8,128)(2,1)}), bf16[8,4,64,128]{3,2,1,0:T(8,128)(2,1)S(1)}, u32[]{:S(2)}, u32[]{:S(2)}) async-start(bf16[8,4,64,128]{3,2,1,0:T(8,128)(2,1)} %half.6), calls=%async_computation.2 | async-start | bytes 1048576 | tf_op jit(solution)/shard_map/all_to_all | solution.py:176
  76.9 9.2 %collective-permute-start.10 = (bf16[4,256,128]{2,1,0:T(8,128)(2,1)S(1)}, bf16[4,256,128]{2,1,0:T(8,128)(2,1)S(1)}, u32[]{:S(2)}, u32[]{:S(2)}) collective-permute-start(bf16[4,256,128]{2,1,0:T(8,128)(2,1)S(1)} %get-tuple-element.35), channel_id=1, source_target_pairs={{0,2},{1,3},{2,0},{3,1},{4,6},{5,7},{6,4},{7,5},{8,10},{9,11},{10,... | collective-permute-start | bytes 786440 | tf_op jit(solution)/shard_map/ppermute | solution.py:157
  78.5 11.4 %collective-permute-start.11 = (bf16[4,256,128]{2,1,0:T(8,128)(2,1)S(1)}, bf16[4,256,128]{2,1,0:T(8,128)(2,1)S(1)}, u32[]{:S(2)}, u32[]{:S(2)}) collective-permute-start(bf16[4,256,128]{2,1,0:T(8,128)(2,1)S(1)} %get-tuple-element.36), channel_id=1, source_target_pairs={{0,3},{1,2},{2,1},{3,0},{4,7},{5,6},{6,5},{7,4},{8,11},{9,10},{10,... | collective-permute-start | bytes 786440 | tf_op jit(solution)/shard_map/ppermute | solution.py:157
  78.5 11.4 %collective-permute-start.9 = (bf16[4,256,128]{2,1,0:T(8,128)(2,1)}, bf16[4,256,128]{2,1,0:T(8,128)(2,1)S(1)}, u32[]{:S(2)}, u32[]{:S(2)}) collective-permute-start(bf16[4,256,128]{2,1,0:T(8,128)(2,1)} %copy-done.3), channel_id=1, source_target_pairs={{0,1},{1,0},{2,3},{3,2},{4,5},{5,4},{6,7},{7,6},{8,9},{9,8},{10,11... | collective-permute-start | bytes 786440 | tf_op jit(solution)/shard_map/ppermute | solution.py:157

commit v3 on v2

v3 whole, which is shorter than its diff:
```python
import functools

import jax
import jax.numpy as jnp
from jax import lax
from jax.experimental import pallas as pl
from jax.experimental.pallas import tpu as pltpu
from jax.sharding import PartitionSpec as P

LANES = 128
STEP = 64
CHUNKS = (4, 4, 4, 4)
VMEM = 24 * 1024 * 1024


def quarter_kernel(rows, place_ref, x_ref, c_ref, *refs):
    outs, acc = refs[:-1], refs[-1]
    step, k_all, depth = x_ref.shape
    x = x_ref[...].reshape(step * k_all, depth)
    product = jnp.dot(x, c_ref[...], preferred_element_type=jnp.float32)
    for d in range(2):
        acc[d] = product[:, d * LANES : (d + 1) * LANES]
    left = rows - pl.program_id(0) * step
    keep = lax.broadcasted_iota(jnp.int32, (step, LANES), 0) < left
    first = 0
    for c in range(len(CHUNKS)):
        for flip in range(2):
            out = outs[2 * c + flip]
            d = (place_ref[0] & 1) ^ flip
            for k in range(out.shape[0]):
                block = acc[d, pl.ds(first + k, step, stride=k_all), :]
                out[k] = jnp.where(keep, block, 0.0).astype(jnp.bfloat16)
        first += CHUNKS[c]


def quarter_of(place, by_r, coeffs, far, padded):
    rows, k_all, depth = by_r.shape
    outs = [jax.ShapeDtypeStruct((kc, padded, LANES), jnp.bfloat16) for kc in CHUNKS for _ in range(2)]
    out = pl.pallas_call(
        functools.partial(quarter_kernel, rows),
        grid_spec=pltpu.PrefetchScalarGridSpec(
            num_scalar_prefetch=1,
            grid=(padded // STEP,),
            in_specs=[
                pl.BlockSpec((STEP, k_all, depth), lambda r, place: (r, 0, 0)),
                pl.BlockSpec((depth, 2 * LANES), lambda r, place: (0, (place[0] >> 1) ^ far)),
            ],
            out_specs=[pl.BlockSpec((o.shape[0], STEP, LANES), lambda r, place: (0, r, 0)) for o in outs],
            scratch_shapes=[pltpu.VMEM((2, STEP * k_all, LANES), jnp.float32)],
        ),
        out_shape=outs,
        compiler_params=pltpu.CompilerParams(vmem_limit_bytes=VMEM),
        cost_estimate=pl.CostEstimate(
            flops=2 * rows * k_all * depth * 2 * LANES,
            bytes_accessed=2 * (by_r.size + (depth + padded * k_all) * 2 * LANES),
            transcendentals=0,
        ),
        name=f"quarter{far}",
    )(place, by_r, coeffs)
    return [out[2 * c : 2 * c + 2] for c in range(len(CHUNKS))]


def half_kernel(n_mo, place_ref, *refs):
    arrived, t_ref, outs, held = refs[:n_mo], refs[n_mo], refs[n_mo + 1 : -1], refs[-1]
    pair, block, lanes = outs[0].shape
    half = None
    for o, a_ref in enumerate(arrived):
        columns = jnp.concatenate([a_ref[k] for k in range(pair)], axis=1)
        part = jnp.dot(t_ref[place_ref[0] ^ o], columns, preferred_element_type=jnp.float32)
        half = part if half is None else half + part
    held[...] = half
    for o, out in enumerate(outs):
        start = pl.multiple_of((place_ref[1] ^ o) * block, block)
        for k in range(pair):
            out[k] = held[pl.ds(start, block), k * lanes : (k + 1) * lanes].astype(jnp.bfloat16)


def half_of(place, arrived, turned, n_pair):
    kc, padded, lanes = arrived[0].shape
    n_mo, orbitals, _ = turned.shape
    block = orbitals // n_pair
    return pl.pallas_call(
        functools.partial(half_kernel, n_mo),
        grid_spec=pltpu.PrefetchScalarGridSpec(
            num_scalar_prefetch=1,
            grid=(kc // 2,),
            in_specs=[pl.BlockSpec((2, padded, lanes), lambda k, place: (k, 0, 0))] * n_mo
            + [pl.BlockSpec(turned.shape, lambda k, place: (0, 0, 0))],
            out_specs=[pl.BlockSpec((2, block, lanes), lambda k, place: (k, 0, 0))] * n_pair,
            scratch_shapes=[pltpu.VMEM((orbitals, 2 * lanes), jnp.float32)],
        ),
        out_shape=[jax.ShapeDtypeStruct((kc, block, lanes), jnp.bfloat16)] * n_pair,
        compiler_params=pltpu.CompilerParams(vmem_limit_bytes=VMEM),
        cost_estimate=pl.CostEstimate(
            flops=2 * orbitals * n_mo * padded * kc * lanes,
            bytes_accessed=2 * (n_mo * arrived[0].size + turned.size + orbitals * kc * lanes),
            transcendentals=0,
        ),
        name="half",
    )(place, *arrived, turned)


def combine_kernel(n_pair, per_step, mirror_ref, place_ref, *refs):
    pieces, out_ref, held, sems = refs[:-3], refs[-3], refs[-2], refs[-1]
    step = pl.program_id(0)

    @pl.when(step == 0)
    def _():
        copies = []
        first = 0
        for n, piece in enumerate(pieces):
            source, kc = place_ref[1] ^ (n % n_pair), piece.shape[0]
            copies.append(pltpu.make_async_copy(piece, held.at[source, first : first + kc], sems.at[n]))
            if n % n_pair == n_pair - 1:
                first += kc
        for copy in copies:
            copy.start()
        for copy in copies:
            copy.wait()

    k_all = held.shape[1]
    for n in range(per_step):
        k = step * per_step + n
        m = mirror_ref[k]
        own = held[k // k_all, lax.rem(k, k_all)].astype(jnp.float32)
        partner = held[m // k_all, lax.rem(m, k_all)].astype(jnp.float32)
        out_ref[n] = 0.5 * (own + partner)


def combine(pieces, mirror, place, n_pair):
    _, block, lanes = pieces[0].shape
    k_all = sum(p.shape[0] for p in pieces) // n_pair
    rows = n_pair * k_all
    per_step = max(1, 32 * 64 // block)
    return pl.pallas_call(
        functools.partial(combine_kernel, n_pair, per_step),
        grid_spec=pltpu.PrefetchScalarGridSpec(
            num_scalar_prefetch=2,
            grid=(rows // per_step,),
            in_specs=[pl.BlockSpec(memory_space=pl.ANY)] * len(pieces),
            out_specs=pl.BlockSpec((per_step, block, lanes), lambda k, m, place: (k, 0, 0)),
            scratch_shapes=[
                pltpu.VMEM((n_pair, k_all, block, lanes), jnp.bfloat16),
                pltpu.SemaphoreType.DMA((len(pieces),)),
            ],
        ),
        out_shape=jax.ShapeDtypeStruct((rows, block, lanes), jnp.float32),
        compiler_params=pltpu.CompilerParams(vmem_limit_bytes=VMEM),
        cost_estimate=pl.CostEstimate(
            flops=2 * rows * block * lanes,
            bytes_accessed=6 * rows * block * lanes,
            transcendentals=0,
        ),
        name="combine",
    )(mirror, place, *pieces)


def flipped(x, axis, size, offset):
    if offset == 0:
        return x
    return lax.ppermute(x, axis, [(i, i ^ offset) for i in range(size)])


def on_device(n_pair, n_mo, integrals, coeffs, mirror):
    k_all, rows, depth = integrals.shape
    orbitals = coeffs.shape[1]
    padded = -(-rows // STEP) * STEP
    by_r = jnp.transpose(integrals, (1, 0, 2))
    place = jnp.stack([lax.axis_index("mo"), lax.axis_index("pair")]).astype(jnp.int32)
    turned = jnp.pad(coeffs.reshape(n_mo, rows, orbitals), ((0, 0), (0, padded - rows), (0, 0)))
    turned = jnp.transpose(turned, (0, 2, 1))
    quarters = [[None] * n_mo for _ in CHUNKS]
    for far in reversed(range(n_mo // 2)):
        for c, blocks in enumerate(quarter_of(place, by_r, coeffs, far, padded)):
            quarters[c][2 * far : 2 * far + 2] = blocks
    pieces = []
    for blocks in quarters:
        arrived = [flipped(b, "mo", n_mo, o) for o, b in enumerate(blocks)]
        half = half_of(place, arrived, turned, n_pair)
        pieces += [flipped(h, "pair", n_pair, o) for o, h in enumerate(half)]
    return combine(pieces, mirror, place, n_pair)


def solution(mesh):
    return jax.shard_map(
        functools.partial(on_device, mesh.shape["pair"], mesh.shape["mo"]),
        mesh=mesh,
        in_specs=(P("pair", "mo", None), P(), P()),
        out_specs=P(None, "pair", "mo"),
        check_vma=False,
    )
```

time: 116 us -> 129 us (1.11)
  starting transfers between devices: 26.9 us -> 57.7 us
  blocking collectives: 19.8 us -> 0 us
  local copies, waits for them, and re-layouts: 9.71 us -> 19.4 us
  waiting for transfers between devices: 35.1 us -> 26 us
  Pallas kernels: 23.9 us -> 25.3 us
    ppermute x12 -> x40, starting transfers between devices: 10.3 us -> 57.7 us  [flipped(): return lax.ppermute(x, axis, [(i, i ^ offset) for i in range(size)])]
    all_to_all x1 -> x0, blocking collectives: 19.8 us -> none  [on_device(): lax.all_to_all(half, 'pair', split_axis=0, concat_axis=0, tiled=True)]
    all_to_all x3 -> x0, starting transfers between devices: 16.6 us -> none  [on_device(): lax.all_to_all(half, 'pair', split_axis=0, concat_axis=0, tiled=True)]
    unnamed x20 -> x32, local copies, waits for them, and re-layouts: 4.78 us -> 14.4 us
    ppermute x12 -> x40, waiting for transfers between devices: 33.6 us -> 26 us  [flipped(): return lax.ppermute(x, axis, [(i, i ^ offset) for i in range(size)])]
    pallas_call x5, Pallas kernels: 9.57 us -> 14 us  [the longest x1 7.03 us: combine(): pl.pallas_call(functools.partial(combine_kernel, n_pair, per_step), grid_...]
    pallas_call x2, Pallas kernels: 14.4 us -> 11.3 us  [quarter_of(): pl.pallas_call(functools.partial(quarter_kernel, rows), grid_spec=pltpu.P...]
    all_to_all x3 -> x0, waiting for transfers between devices: 1.46 us -> none  [on_device(): lax.all_to_all(half, 'pair', split_axis=0, concat_axis=0, tiled=True)]
  transfers between devices with their start and end apart: 15 -> 40, of which waited for: 8 -> 10; matrix products, arithmetic and copies ran while one was open for 4% -> 4% of each run, Pallas kernels for 10% -> 10%
where the time goes in v3:
time: 129 us
  starting transfers between devices  57.7 us (45%)
  waiting for transfers between devices  26 us (20%)
  Pallas kernels  25.3 us (20%)
  local copies, waits for them, and re-layouts  19.4 us (15%)
    ppermute x40, starting transfers between devices, flipped(): return lax.ppermute(x, axis, [(i, i ^ offset) for i in range(size)])  57.7 us
    ppermute x40, waiting for transfers between devices, flipped(): return lax.ppermute(x, axis, [(i, i ^ offset) for i in range(size)])  26 us
    unnamed x32, local copies, waits for them, and re-layouts  14.4 us
    pallas_call x2, Pallas kernels, quarter_of(): pl.pallas_call(functools.partial(quarter_kernel, rows), grid_spec=pltpu.P...  11.3 us
    pallas_call x1, Pallas kernels, combine(): pl.pallas_call(functools.partial(combine_kernel, n_pair, per_step), grid_...  7.03 us
    pallas_call x4, Pallas kernels, half_of(): pl.pallas_call(functools.partial(half_kernel, n_mo), grid_spec=pltpu.Pref...  6.99 us
    reshape x2, local copies, waits for them, and re-layouts, on_device(): coeffs.reshape(n_mo, rows, orbitals)  3.52 us
  transfers between devices with their start and end apart: 40, of which 10 were waited for; matrix products, arithmetic and copies ran while one was open for 4% of the time, Pallas kernels for 10%

profile of v3, /device:TPU:0, one launch (start us, length us, event | category | flops | bytes accessed | tf_op | source)
XLA Modules:
  0.0 128.6 jit_solution(7326600497084386524)
XLA Ops:
  0.1 3.3 %copy-done = bf16[16,250,1000]{2,0,1:T(8,128)(2,1)S(1)} copy-done((bf16[16,250,1000]{2,0,1:T(8,128)(2,1)S(1)}, bf16[16,250,1000]{2,0,1:T(8,128)(2,1)}, u32[]{:S(2)}) %copy-start) | copy-done | bytes 8000024
  3.4 1.2 copy-done.1
  4.6 5.6 %quarter1.1 = (bf16[4,256,128]{2,1,0:T(8,128)(2,1)S(1)}, bf16[4,256,128]{2,1,0:T(8,128)(2,1)S(1)}, bf16[4,256,128]{2,1,0:T(8,128)(2,1)S(1)}, bf16[4,256,128]{2,1...) custom-call(s32[2]{0:T(128)S(1)} %pad_add_fusion.place_ref, ...), custom_call_target="tpu_custom_call" | custom-call | flops 2048000000 | bytes 10609152 | tf_op jit(solution)/shard_map/quarter1/pallas_call | solution.py:39
  10.3 3.0 %collective-permute-start.1 = (bf16[4,256,128]{2,1,0:T(8,128)(2,1)S(1)}, bf16[4,256,128]{2,1,0:T(8,128)(2,1)S(1)}, u32[]{:S(2)}, u32[]{:S(2)}) collective-permute-start(bf16[4,256,128]{2,1,0:T(8,128)(2,1)S(1)} %get-tuple-element.55), channel_id=1, source_target_pairs={{0,2},{1,3},{2,0},{3,1},{4,6},{5,7},{6,4},{7,5},{8,10},{9,11},{10,... | collective-permute-start | bytes 786440 | tf_op jit(solution)/shard_map/ppermute | solution.py:161
  13.2 1.2 collective-permute-start.11
  15.0 1.7 %collective-permute-start.21 = (bf16[4,256,128]{2,1,0:T(8,128)(2,1)S(1)}, bf16[4,256,128]{2,1,0:T(8,128)(2,1)S(1)}, u32[]{:S(2)}, u32[]{:S(2)}) collective-permute-start(bf16[4,256,128]{2,1,0:T(8,128)(2,1)S(1)} %get-tuple-element.79), channel_id=1, source_target_pairs={{0,2},{1,3},{2,0},{3,1},{4,6},{5,7},{6,4},{7,5},{8,10},{9,11},{10,... | collective-permute-start | bytes 786440 | tf_op jit(solution)/shard_map/ppermute | solution.py:161
  16.7 5.7 %quarter0.1 = (bf16[4,256,128]{2,1,0:T(8,128)(2,1)S(1)}, bf16[4,256,128]{2,1,0:T(8,128)(2,1)S(1)}, bf16[4,256,128]{2,1,0:T(8,128)(2,1)S(1)}, bf16[4,256,128]{2,1...) custom-call(s32[2]{0:T(128)S(1)} %pad_add_fusion.place_ref, ...), custom_call_target="tpu_custom_call" | custom-call | flops 2048000000 | bytes 10609152 | tf_op jit(solution)/shard_map/quarter0/pallas_call | solution.py:39
  24.5 1.0 collective-permute-done.2.refs_3_
  26.5 5.1 %collective-permute-done.11.refs_2_ = bf16[4,256,128]{2,1,0:T(8,128)(2,1)S(1)} collective-permute-done((bf16[4,256,128]{2,1,0:T(8,128)(2,1)S(1)}, bf16[4,256,128]{2,1,0:T(8,128)(2,1)S(1)}, u32[]{:S(2)}, u32[]{:S(2)}) %collective-permute-start.11) | collective-permute-done | bytes 262176 | tf_op jit(solution)/shard_map/ppermute | solution.py:161
  31.6 2.1 %collective-permute-start.31 = (bf16[4,256,128]{2,1,0:T(8,128)(2,1)}, bf16[4,256,128]{2,1,0:T(8,128)(2,1)S(1)}, u32[]{:S(2)}, u32[]{:S(2)}) collective-permute-start(bf16[4,256,128]{2,1,0:T(8,128)(2,1)} %get-tuple-element.91), channel_id=1, source_target_pairs={{0,2},{1,3},{2,0},{3,1},{4,6},{5,7},{6,4},{7,5},{8,10},{9,11},{10,... | collective-permute-start | bytes 786440 | tf_op jit(solution)/shard_map/ppermute | solution.py:161
  33.7 3.1 %collective-permute-done.12.refs_3_ = bf16[4,256,128]{2,1,0:T(8,128)(2,1)S(1)} collective-permute-done((bf16[4,256,128]{2,1,0:T(8,128)(2,1)S(1)}, bf16[4,256,128]{2,1,0:T(8,128)(2,1)S(1)}, u32[]{:S(2)}, u32[]{:S(2)}) %collective-permute-start.12) | collective-permute-done | bytes 262176 | tf_op jit(solution)/shard_map/ppermute | solution.py:161
  37.5 1.9 %collective-permute-start.32 = (bf16[4,256,128]{2,1,0:T(8,128)(2,1)}, bf16[4,256,128]{2,1,0:T(8,128)(2,1)S(1)}, u32[]{:S(2)}, u32[]{:S(2)}) collective-permute-start(bf16[4,256,128]{2,1,0:T(8,128)(2,1)} %get-tuple-element.92), channel_id=1, source_target_pairs={{0,3},{1,2},{2,1},{3,0},{4,7},{5,6},{6,5},{7,4},{8,11},{9,10},{10,... | collective-permute-start | bytes 786440 | tf_op jit(solution)/shard_map/ppermute | solution.py:161
  39.4 3.4 %collective-permute-done.21.refs_2_ = bf16[4,256,128]{2,1,0:T(8,128)(2,1)S(1)} collective-permute-done((bf16[4,256,128]{2,1,0:T(8,128)(2,1)S(1)}, bf16[4,256,128]{2,1,0:T(8,128)(2,1)S(1)}, u32[]{:S(2)}, u32[]{:S(2)}) %collective-permute-start.21) | collective-permute-done | bytes 262176 | tf_op jit(solution)/shard_map/ppermute | solution.py:161
  42.8 5.2 %collective-permute-done.22.refs_3_ = bf16[4,256,128]{2,1,0:T(8,128)(2,1)S(1)} collective-permute-done((bf16[4,256,128]{2,1,0:T(8,128)(2,1)S(1)}, bf16[4,256,128]{2,1,0:T(8,128)(2,1)S(1)}, u32[]{:S(2)}, u32[]{:S(2)}) %collective-permute-start.22) | collective-permute-done | bytes 262176 | tf_op jit(solution)/shard_map/ppermute | solution.py:161
  49.3 1.2 reshape.3
  50.5 2.3 %copy.4 = bf16[4,250,512]{1,2,0:T(8,128)(2,1)} copy(bf16[4,250,512]{2,1,0:T(8,128)(2,1)} %reshape.3) | data formatting | bytes 2048000 | tf_op jit(solution)/shard_map/reshape | solution.py:170
  52.8 1.4 %pad_bitcast_fusion.refs_4_ = bf16[4,512,256]{2,1,0:T(8,128)(2,1)S(1)} fusion(bf16[4,250,512]{1,2,0:T(8,128)(2,1)} %copy.4), kind=kLoop, calls=%fused_computation | loop fusion | bytes 2072576 | tf_op jit(solution)/shard_map/transpose | solution.py:171
  55.1 0.9 copy-done.10
  56.1 0.9 copy-done.12
  57.0 0.9 copy-done.14
  58.0 1.5 %half.4 = (bf16[4,64,128]{2,1,0:T(8,128)(2,1)S(1)}, bf16[4,64,128]{2,1,0:T(8,128)(2,1)S(1)}, bf16[4,64,128]{2,1,0:T(8,128)(2,1)S(1)}, bf16[4,64,128]{2,1,0:T(8,1...) custom-call(s32[2]{0:T(128)S(1)} %pad_add_fusion.place_ref, ...), custom_call_target="tpu_custom_call" | custom-call | flops 536870912 | bytes 2621440 | tf_op jit(solution)/shard_map/half/pallas_call | solution.py:82
  59.5 1.8 %collective-permute-start.3 = (bf16[4,64,128]{2,1,0:T(8,128)(2,1)S(1)}, bf16[4,64,128]{2,1,0:T(8,128)(2,1)S(1)}, u32[]{:S(2)}, u32[]{:S(2)}) collective-permute-start(bf16[4,64,128]{2,1,0:T(8,128)(2,1)S(1)} %get-tuple-element.58), channel_id=1, source_target_pairs={{0,4},{4,0},{8,12},{12,8},{16,20},{20,16},{24,28},{28,24},{1,5},{5... | collective-permute-start | bytes 196616 | tf_op jit(solution)/shard_map/ppermute | solution.py:161
  61.3 1.6 %collective-permute-start.4 = (bf16[4,64,128]{2,1,0:T(8,128)(2,1)S(1)}, bf16[4,64,128]{2,1,0:T(8,128)(2,1)S(1)}, u32[]{:S(2)}, u32[]{:S(2)}) collective-permute-start(bf16[4,64,128]{2,1,0:T(8,128)(2,1)S(1)} %get-tuple-element.59), channel_id=1, source_target_pairs={{0,8},{4,12},{8,0},{12,4},{16,24},{20,28},{24,16},{28,20},{1,9},{5... | collective-permute-start | bytes 196616 | tf_op jit(solution)/shard_map/ppermute | solution.py:161
  63.1 0.9 copy-done.4
  65.0 2.4 %half.5 = (bf16[4,64,128]{2,1,0:T(8,128)(2,1)S(1)}, bf16[4,64,128]{2,1,0:T(8,128)(2,1)S(1)}, bf16[4,64,128]{2,1,0:T(8,128)(2,1)S(1)}, bf16[4,64,128]{2,1,0:T(8,1...) custom-call(s32[2]{0:T(128)S(1)} %pad_add_fusion.place_ref, ...), custom_call_target="tpu_custom_call" | custom-call | flops 536870912 | bytes 2621440 | tf_op jit(solution)/shard_map/half/pallas_call | solution.py:82
  67.4 2.9 %collective-permute-start.6 = (bf16[4,64,128]{2,1,0:T(8,128)(2,1)S(1)}, bf16[4,64,128]{2,1,0:T(8,128)(2,1)S(1)}, u32[]{:S(2)}, u32[]{:S(2)}) collective-permute-start(bf16[4,64,128]{2,1,0:T(8,128)(2,1)S(1)} %get-tuple-element.61), channel_id=1, source_target_pairs={{0,16},{4,20},{8,24},{12,28},{16,0},{20,4},{24,8},{28,12},{1,17},{... | collective-permute-start | bytes 196616 | tf_op jit(solution)/shard_map/ppermute | solution.py:161
  70.4 1.3 collective-permute-start.7
  71.6 3.6 %collective-permute-start.8 = (bf16[4,64,128]{2,1,0:T(8,128)(2,1)S(1)}, bf16[4,64,128]{2,1,0:T(8,128)(2,1)S(1)}, u32[]{:S(2)}, u32[]{:S(2)}) collective-permute-start(bf16[4,64,128]{2,1,0:T(8,128)(2,1)S(1)} %get-tuple-element.63), channel_id=1, source_target_pairs={{0,24},{4,28},{8,16},{12,20},{16,8},{20,12},{24,0},{28,4},{1,25},{... | collective-permute-start | bytes 196616 | tf_op jit(solution)/shard_map/ppermute | solution.py:161
  75.3 1.6 %collective-permute-start.13 = (bf16[4,64,128]{2,1,0:T(8,128)(2,1)S(1)}, bf16[4,64,128]{2,1,0:T(8,128)(2,1)S(1)}, u32[]{:S(2)}, u32[]{:S(2)}) collective-permute-start(bf16[4,64,128]{2,1,0:T(8,128)(2,1)S(1)} %get-tuple-element.70), channel_id=1, source_target_pairs={{0,4},{4,0},{8,12},{12,8},{16,20},{20,16},{24,28},{28,24},{1,5},{5... | collective-permute-start | bytes 196616 | tf_op jit(solution)/shard_map/ppermute | solution.py:161
  76.9 2.4 %collective-permute-done.7.refs_5_ = bf16[4,64,128]{2,1,0:T(8,128)(2,1)S(1)} collective-permute-done((bf16[4,64,128]{2,1,0:T(8,128)(2,1)S(1)}, bf16[4,64,128]{2,1,0:T(8,128)(2,1)S(1)}, u32[]{:S(2)}, u32[]{:S(2)}) %collective-permute-start.7) | collective-permute-done | bytes 65568 | tf_op jit(solution)/shard_map/ppermute | solution.py:161
  79.4 1.7 %collective-permute-start.15 = (bf16[4,64,128]{2,1,0:T(8,128)(2,1)S(1)}, bf16[4,64,128]{2,1,0:T(8,128)(2,1)S(1)}, u32[]{:S(2)}, u32[]{:S(2)}) collective-permute-start(bf16[4,64,128]{2,1,0:T(8,128)(2,1)S(1)} %get-tuple-element.72), channel_id=1, source_target_pairs={{0,12},{4,8},{8,4},{12,0},{16,28},{20,24},{24,20},{28,16},{1,13},{... | collective-permute-start | bytes 196616 | tf_op jit(solution)/shard_map/ppermute | solution.py:161
  81.1 3.6 %collective-permute-start.16 = (bf16[4,64,128]{2,1,0:T(8,128)(2,1)S(1)}, bf16[4,64,128]{2,1,0:T(8,128)(2,1)S(1)}, u32[]{:S(2)}, u32[]{:S(2)}) collective-permute-start(bf16[4,64,128]{2,1,0:T(8,128)(2,1)S(1)} %get-tuple-element.73), channel_id=1, source_target_pairs={{0,16},{4,20},{8,24},{12,28},{16,0},{20,4},{24,8},{28,12},{1,17},{... | collective-permute-start | bytes 196616 | tf_op jit(solution)/shard_map/ppermute | solution.py:161
  84.6 1.0 collective-permute-start.17
  85.7 1.3 %collective-permute-start.18 = (bf16[4,64,128]{2,1,0:T(8,128)(2,1)S(1)}, bf16[4,64,128]{2,1,0:T(8,128)(2,1)S(1)}, u32[]{:S(2)}, u32[]{:S(2)}) collective-permute-start(bf16[4,64,128]{2,1,0:T(8,128)(2,1)S(1)} %get-tuple-element.75), channel_id=1, source_target_pairs={{0,24},{4,28},{8,16},{12,20},{16,8},{20,12},{24,0},{28,4},{1,25},{... | collective-permute-start | bytes 196616 | tf_op jit(solution)/shard_map/ppermute | solution.py:161
  87.0 1.5 %half.6 = (bf16[4,64,128]{2,1,0:T(8,128)(2,1)S(1)}, bf16[4,64,128]{2,1,0:T(8,128)(2,1)S(1)}, bf16[4,64,128]{2,1,0:T(8,128)(2,1)S(1)}, bf16[4,64,128]{2,1,0:T(8,1...) custom-call(s32[2]{0:T(128)S(1)} %pad_add_fusion.place_ref, ...), custom_call_target="tpu_custom_call" | custom-call | flops 536870912 | bytes 2621440 | tf_op jit(solution)/shard_map/half/pallas_call | solution.py:82
  88.5 4.2 %collective-permute-start.19 = (bf16[4,64,128]{2,1,0:T(8,128)(2,1)S(1)}, bf16[4,64,128]{2,1,0:T(8,128)(2,1)S(1)}, u32[]{:S(2)}, u32[]{:S(2)}) collective-permute-start(bf16[4,64,128]{2,1,0:T(8,128)(2,1)S(1)} %get-tuple-element.76), channel_id=1, source_target_pairs={{0,28},{4,24},{8,20},{12,16},{16,12},{20,8},{24,4},{28,0},{1,29},{... | collective-permute-start | bytes 196616 | tf_op jit(solution)/shard_map/ppermute | solution.py:161
  92.8 3.4 %collective-permute-start.25 = (bf16[4,64,128]{2,1,0:T(8,128)(2,1)S(1)}, bf16[4,64,128]{2,1,0:T(8,128)(2,1)S(1)}, u32[]{:S(2)}, u32[]{:S(2)}) collective-permute-start(bf16[4,64,128]{2,1,0:T(8,128)(2,1)S(1)} %get-tuple-element.84), channel_id=1, source_target_pairs={{0,12},{4,8},{8,4},{12,0},{16,28},{20,24},{24,20},{28,16},{1,13},{... | collective-permute-start | bytes 196616 | tf_op jit(solution)/shard_map/ppermute | solution.py:161
  96.6 1.5 %half.7 = (bf16[4,64,128]{2,1,0:T(8,128)(2,1)S(1)}, bf16[4,64,128]{2,1,0:T(8,128)(2,1)S(1)}, bf16[4,64,128]{2,1,0:T(8,128)(2,1)S(1)}, bf16[4,64,128]{2,1,0:T(8,1...) custom-call(s32[2]{0:T(128)S(1)} %pad_add_fusion.place_ref, ...), custom_call_target="tpu_custom_call" | custom-call | flops 536870912 | bytes 2621440 | tf_op jit(solution)/shard_map/half/pallas_call | solution.py:82
  98.1 2.2 %collective-permute-start.27 = (bf16[4,64,128]{2,1,0:T(8,128)(2,1)S(1)}, bf16[4,64,128]{2,1,0:T(8,128)(2,1)S(1)}, u32[]{:S(2)}, u32[]{:S(2)}) collective-permute-start(bf16[4,64,128]{2,1,0:T(8,128)(2,1)S(1)} %get-tuple-element.86), channel_id=1, source_target_pairs={{0,20},{4,16},{8,28},{12,24},{16,4},{20,0},{24,12},{28,8},{1,21},{... | collective-permute-start | bytes 196616 | tf_op jit(solution)/shard_map/ppermute | solution.py:161
  100.3 1.1 collective-permute-start.28
  101.4 4.1 %collective-permute-start.29 = (bf16[4,64,128]{2,1,0:T(8,128)(2,1)S(1)}, bf16[4,64,128]{2,1,0:T(8,128)(2,1)S(1)}, u32[]{:S(2)}, u32[]{:S(2)}) collective-permute-start(bf16[4,64,128]{2,1,0:T(8,128)(2,1)S(1)} %get-tuple-element.88), channel_id=1, source_target_pairs={{0,28},{4,24},{8,20},{12,16},{16,12},{20,8},{24,4},{28,0},{1,29},{... | collective-permute-start | bytes 196616 | tf_op jit(solution)/shard_map/ppermute | solution.py:161
  105.6 1.6 %collective-permute-done.27.refs_21_ = bf16[4,64,128]{2,1,0:T(8,128)(2,1)S(1)} collective-permute-done((bf16[4,64,128]{2,1,0:T(8,128)(2,1)S(1)}, bf16[4,64,128]{2,1,0:T(8,128)(2,1)S(1)}, u32[]{:S(2)}, u32[]{:S(2)}) %collective-permute-start.27) | collective-permute-done | bytes 65568 | tf_op jit(solution)/shard_map/ppermute | solution.py:161
  107.2 1.8 %collective-permute-start.35 = (bf16[4,64,128]{2,1,0:T(8,128)(2,1)S(1)}, bf16[4,64,128]{2,1,0:T(8,128)(2,1)S(1)}, u32[]{:S(2)}, u32[]{:S(2)}) collective-permute-start(bf16[4,64,128]{2,1,0:T(8,128)(2,1)S(1)} %get-tuple-element.96), channel_id=1, source_target_pairs={{0,12},{4,8},{8,4},{12,0},{16,28},{20,24},{24,20},{28,16},{1,13},{... | collective-permute-start | bytes 196616 | tf_op jit(solution)/shard_map/ppermute | solution.py:161
  109.8 2.6 %collective-permute-start.37 = (bf16[4,64,128]{2,1,0:T(8,128)(2,1)S(1)}, bf16[4,64,128]{2,1,0:T(8,128)(2,1)S(1)}, u32[]{:S(2)}, u32[]{:S(2)}) collective-permute-start(bf16[4,64,128]{2,1,0:T(8,128)(2,1)S(1)} %get-tuple-element.98), channel_id=1, source_target_pairs={{0,20},{4,16},{8,28},{12,24},{16,4},{20,0},{24,12},{28,8},{1,21},{... | collective-permute-start | bytes 196616 | tf_op jit(solution)/shard_map/ppermute | solution.py:161
  112.4 2.2 %collective-permute-start.38 = (bf16[4,64,128]{2,1,0:T(8,128)(2,1)S(1)}, bf16[4,64,128]{2,1,0:T(8,128)(2,1)S(1)}, u32[]{:S(2)}, u32[]{:S(2)}) collective-permute-start(bf16[4,64,128]{2,1,0:T(8,128)(2,1)S(1)} %get-tuple-element.99), channel_id=1, source_target_pairs={{0,24},{4,28},{8,16},{12,20},{16,8},{20,12},{24,0},{28,4},{1,25},{... | collective-permute-start | bytes 196616 | tf_op jit(solution)/shard_map/ppermute | solution.py:161
  114.6 2.9 %collective-permute-start.39 = (bf16[4,64,128]{2,1,0:T(8,128)(2,1)S(1)}, bf16[4,64,128]{2,1,0:T(8,128)(2,1)S(1)}, u32[]{:S(2)}, u32[]{:S(2)}) collective-permute-start(bf16[4,64,128]{2,1,0:T(8,128)(2,1)S(1)} %get-tuple-element.100), channel_id=1, source_target_pairs={{0,28},{4,24},{8,20},{12,16},{16,12},{20,8},{24,4},{28,0},{1,29},{... | collective-permute-start | bytes 196616 | tf_op jit(solution)/shard_map/ppermute | solution.py:161
  118.6 3.0 %collective-permute-done.39.refs_31_ = bf16[4,64,128]{2,1,0:T(8,128)(2,1)S(1)} collective-permute-done((bf16[4,64,128]{2,1,0:T(8,128)(2,1)S(1)}, bf16[4,64,128]{2,1,0:T(8,128)(2,1)S(1)}, u32[]{:S(2)}, u32[]{:S(2)}) %collective-permute-start.39) | collective-permute-done | bytes 65568 | tf_op jit(solution)/shard_map/ppermute | solution.py:161
  121.6 7.0 %combine.1 = f32[128,64,128]{2,1,0:T(8,128)} custom-call(s32[128]{0:T(128)S(1)} %copy-done.15, s32[2]{0:T(128)S(1)} %pad_add_fusion.place_ref, bf16[4,64,128]{2,1,0:T(8,128)(2,1)S(1)} %get-tuple-element.57.refs_0_, bf16[4,64,128]{2,1,0:T(8,128)(2,1)S(1)} %collective-permute-done.3.refs_1_, bf16[4,64,128]{2,1,0:T(8,128)(2,1)S(1)} %collective-permute-done.4.refs_2_, ...), custom_call_target="tpu_custom_call" | custom-call | flops 2097152 | bytes 6291456 | tf_op jit(solution)/shard_map/combine/pallas_call | solution.py:135
  (75 shorter events, 10.2 us)
Async XLA Ops:
  0.1 3.3 %copy-start = (bf16[16,250,1000]{2,0,1:T(8,128)(2,1)S(1)}, bf16[16,250,1000]{2,0,1:T(8,128)(2,1)}, u32[]{:S(2)}) copy-start(bf16[16,250,1000]{2,0,1:T(8,128)(2,1)} %param.3) | copy-start | bytes 24000004
  3.4 1.2 copy-start.1
  4.6 44.6 %copy-start.2 = (bf16[1000,512]{1,0:T(8,128)(2,1)S(1)}, bf16[1000,512]{1,0:T(8,128)(2,1)}, u32[]{:S(2)}) copy-start(bf16[1000,512]{1,0:T(8,128)(2,1)} %c_ref.3) | copy-start | bytes 3072004
  10.3 13.5 %collective-permute-start.1 = (bf16[4,256,128]{2,1,0:T(8,128)(2,1)S(1)}, bf16[4,256,128]{2,1,0:T(8,128)(2,1)S(1)}, u32[]{:S(2)}, u32[]{:S(2)}) collective-permute-start(bf16[4,256,128]{2,1,0:T(8,128)(2,1)S(1)} %get-tuple-element.55), channel_id=1, source_target_pairs={{0,2},{1,3},{2,0},{3,1},{4,6},{5,7},{6,4},{7,5},{8,10},{9,11},{10,... | collective-permute-start | bytes 786440 | tf_op jit(solution)/shard_map/ppermute | solution.py:161
  13.2 12.3 %collective-permute-start.2 = (bf16[4,256,128]{2,1,0:T(8,128)(2,1)S(1)}, bf16[4,256,128]{2,1,0:T(8,128)(2,1)S(1)}, u32[]{:S(2)}, u32[]{:S(2)}) collective-permute-start(bf16[4,256,128]{2,1,0:T(8,128)(2,1)S(1)} %get-tuple-element.56), channel_id=1, source_target_pairs={{0,3},{1,2},{2,1},{3,0},{4,7},{5,6},{6,5},{7,4},{8,11},{9,10},{10,... | collective-permute-start | bytes 786440 | tf_op jit(solution)/shard_map/ppermute | solution.py:161
  13.2 18.4 %collective-permute-start.11 = (bf16[4,256,128]{2,1,0:T(8,128)(2,1)S(1)}, bf16[4,256,128]{2,1,0:T(8,128)(2,1)S(1)}, u32[]{:S(2)}, u32[]{:S(2)}) collective-permute-start(bf16[4,256,128]{2,1,0:T(8,128)(2,1)S(1)} %get-tuple-element.67), channel_id=1, source_target_pairs={{0,2},{1,3},{2,0},{3,1},{4,6},{5,7},{6,4},{7,5},{8,10},{9,11},{10,... | collective-permute-start | bytes 786440 | tf_op jit(solution)/shard_map/ppermute | solution.py:161
  14.4 22.4 %collective-permute-start.12 = (bf16[4,256,128]{2,1,0:T(8,128)(2,1)S(1)}, bf16[4,256,128]{2,1,0:T(8,128)(2,1)S(1)}, u32[]{:S(2)}, u32[]{:S(2)}) collective-permute-start(bf16[4,256,128]{2,1,0:T(8,128)(2,1)S(1)} %get-tuple-element.68), channel_id=1, source_target_pairs={{0,3},{1,2},{2,1},{3,0},{4,7},{5,6},{6,5},{7,4},{8,11},{9,10},{10,... | collective-permute-start | bytes 786440 | tf_op jit(solution)/shard_map/ppermute | solution.py:161
  15.0 27.8 %collective-permute-start.21 = (bf16[4,256,128]{2,1,0:T(8,128)(2,1)S(1)}, bf16[4,256,128]{2,1,0:T(8,128)(2,1)S(1)}, u32[]{:S(2)}, u32[]{:S(2)}) collective-permute-start(bf16[4,256,128]{2,1,0:T(8,128)(2,1)S(1)} %get-tuple-element.79), channel_id=1, source_target_pairs={{0,2},{1,3},{2,0},{3,1},{4,6},{5,7},{6,4},{7,5},{8,10},{9,11},{10,... | collective-permute-start | bytes 786440 | tf_op jit(solution)/shard_map/ppermute | solution.py:161
  23.8 97.8 %copy-start.15 = (s32[128]{0:T(128)S(1)}, s32[128]{0:T(128)}, u32[]{:S(2)}) copy-start(s32[128]{0:T(128)} %mirror_ref.1) | copy-start | bytes 1540
  24.5 23.6 %collective-permute-start.22 = (bf16[4,256,128]{2,1,0:T(8,128)(2,1)S(1)}, bf16[4,256,128]{2,1,0:T(8,128)(2,1)S(1)}, u32[]{:S(2)}, u32[]{:S(2)}) collective-permute-start(bf16[4,256,128]{2,1,0:T(8,128)(2,1)S(1)} %get-tuple-element.80), channel_id=1, source_target_pairs={{0,3},{1,2},{2,1},{3,0},{4,7},{5,6},{6,5},{7,4},{8,11},{9,10},{10,... | collective-permute-start | bytes 786440 | tf_op jit(solution)/shard_map/ppermute | solution.py:161
  26.3 22.0 %collective-permute-start = (bf16[4,256,128]{2,1,0:T(8,128)(2,1)S(1)}, bf16[4,256,128]{2,1,0:T(8,128)(2,1)S(1)}, u32[]{:S(2)}, u32[]{:S(2)}) collective-permute-start(bf16[4,256,128]{2,1,0:T(8,128)(2,1)S(1)} %get-tuple-element.54), channel_id=1, source_target_pairs={{0,1},{1,0},{2,3},{3,2},{4,5},{5,4},{6,7},{7,6},{8,9},{9,8},{10,11... | collective-permute-start | bytes 786440 | tf_op jit(solution)/shard_map/ppermute | solution.py:161
  31.6 27.9 %collective-permute-start.31 = (bf16[4,256,128]{2,1,0:T(8,128)(2,1)}, bf16[4,256,128]{2,1,0:T(8,128)(2,1)S(1)}, u32[]{:S(2)}, u32[]{:S(2)}) collective-permute-start(bf16[4,256,128]{2,1,0:T(8,128)(2,1)} %get-tuple-element.91), channel_id=1, source_target_pairs={{0,2},{1,3},{2,0},{3,1},{4,6},{5,7},{6,4},{7,5},{8,10},{9,11},{10,... | collective-permute-start | bytes 786440 | tf_op jit(solution)/shard_map/ppermute | solution.py:161
  37.5 23.8 %collective-permute-start.32 = (bf16[4,256,128]{2,1,0:T(8,128)(2,1)}, bf16[4,256,128]{2,1,0:T(8,128)(2,1)S(1)}, u32[]{:S(2)}, u32[]{:S(2)}) collective-permute-start(bf16[4,256,128]{2,1,0:T(8,128)(2,1)} %get-tuple-element.92), channel_id=1, source_target_pairs={{0,3},{1,2},{2,1},{3,0},{4,7},{5,6},{6,5},{7,4},{8,11},{9,10},{10,... | collective-permute-start | bytes 786440 | tf_op jit(solution)/shard_map/ppermute | solution.py:161
  42.8 20.1 %collective-permute-start.10 = (bf16[4,256,128]{2,1,0:T(8,128)(2,1)}, bf16[4,256,128]{2,1,0:T(8,128)(2,1)}, u32[]{:S(2)}, u32[]{:S(2)}) collective-permute-start(bf16[4,256,128]{2,1,0:T(8,128)(2,1)} %get-tuple-element.66), channel_id=1, source_target_pairs={{0,1},{1,0},{2,3},{3,2},{4,5},{5,4},{6,7},{7,6},{8,9},{9,8},{10,11... | collective-permute-start | bytes 786440 | tf_op jit(solution)/shard_map/ppermute | solution.py:161
  48.0 19.4 %collective-permute-start.20 = (bf16[4,256,128]{2,1,0:T(8,128)(2,1)}, bf16[4,256,128]{2,1,0:T(8,128)(2,1)S(1)}, u32[]{:S(2)}, u32[]{:S(2)}) collective-permute-start(bf16[4,256,128]{2,1,0:T(8,128)(2,1)} %get-tuple-element.78), channel_id=1, source_target_pairs={{0,1},{1,0},{2,3},{3,2},{4,5},{5,4},{6,7},{7,6},{8,9},{9,8},{10,11... | collective-permute-start | bytes 786440 | tf_op jit(solution)/shard_map/ppermute | solution.py:161
  49.0 21.4 %collective-permute-start.30 = (bf16[4,256,128]{2,1,0:T(8,128)(2,1)}, bf16[4,256,128]{2,1,0:T(8,128)(2,1)S(1)}, u32[]{:S(2)}, u32[]{:S(2)}) collective-permute-start(bf16[4,256,128]{2,1,0:T(8,128)(2,1)} %get-tuple-element.90), channel_id=1, source_target_pairs={{0,1},{1,0},{2,3},{3,2},{4,5},{5,4},{6,7},{7,6},{8,9},{9,8},{10,11... | collective-permute-start | bytes 786440 | tf_op jit(solution)/shard_map/ppermute | solution.py:161
  54.2 1.0 copy-start.8
  55.1 0.9 copy-start.10
  56.1 0.9 copy-start.12
  57.0 0.9 copy-start.14
  59.5 12.1 %collective-permute-start.3 = (bf16[4,64,128]{2,1,0:T(8,128)(2,1)S(1)}, bf16[4,64,128]{2,1,0:T(8,128)(2,1)S(1)}, u32[]{:S(2)}, u32[]{:S(2)}) collective-permute-start(bf16[4,64,128]{2,1,0:T(8,128)(2,1)S(1)} %get-tuple-element.58), channel_id=1, source_target_pairs={{0,4},{4,0},{8,12},{12,8},{16,20},{20,16},{24,28},{28,24},{1,5},{5... | collective-permute-start | bytes 196616 | tf_op jit(solution)/shard_map/ppermute | solution.py:161
  61.3 13.9 %collective-permute-start.4 = (bf16[4,64,128]{2,1,0:T(8,128)(2,1)S(1)}, bf16[4,64,128]{2,1,0:T(8,128)(2,1)S(1)}, u32[]{:S(2)}, u32[]{:S(2)}) collective-permute-start(bf16[4,64,128]{2,1,0:T(8,128)(2,1)S(1)} %get-tuple-element.59), channel_id=1, source_target_pairs={{0,8},{4,12},{8,0},{12,4},{16,24},{20,28},{24,16},{28,20},{1,9},{5... | collective-permute-start | bytes 196616 | tf_op jit(solution)/shard_map/ppermute | solution.py:161
  62.9 12.4 %collective-permute-start.5 = (bf16[4,64,128]{2,1,0:T(8,128)(2,1)S(1)}, bf16[4,64,128]{2,1,0:T(8,128)(2,1)S(1)}, u32[]{:S(2)}, u32[]{:S(2)}) collective-permute-start(bf16[4,64,128]{2,1,0:T(8,128)(2,1)S(1)} %get-tuple-element.60), channel_id=1, source_target_pairs={{0,12},{4,8},{8,4},{12,0},{16,28},{20,24},{24,20},{28,16},{1,13},{... | collective-permute-start | bytes 196616 | tf_op jit(solution)/shard_map/ppermute | solution.py:161
  67.4 9.5 %collective-permute-start.6 = (bf16[4,64,128]{2,1,0:T(8,128)(2,1)S(1)}, bf16[4,64,128]{2,1,0:T(8,128)(2,1)S(1)}, u32[]{:S(2)}, u32[]{:S(2)}) collective-permute-start(bf16[4,64,128]{2,1,0:T(8,128)(2,1)S(1)} %get-tuple-element.61), channel_id=1, source_target_pairs={{0,16},{4,20},{8,24},{12,28},{16,0},{20,4},{24,8},{28,12},{1,17},{... | collective-permute-start | bytes 196616 | tf_op jit(solution)/shard_map/ppermute | solution.py:161
  70.4 9.0 %collective-permute-start.7 = (bf16[4,64,128]{2,1,0:T(8,128)(2,1)S(1)}, bf16[4,64,128]{2,1,0:T(8,128)(2,1)S(1)}, u32[]{:S(2)}, u32[]{:S(2)}) collective-permute-start(bf16[4,64,128]{2,1,0:T(8,128)(2,1)S(1)} %get-tuple-element.62), channel_id=1, source_target_pairs={{0,20},{4,16},{8,28},{12,24},{16,4},{20,0},{24,12},{28,8},{1,21},{... | collective-permute-start | bytes 196616 | tf_op jit(solution)/shard_map/ppermute | solution.py:161
  71.6 9.4 %collective-permute-start.8 = (bf16[4,64,128]{2,1,0:T(8,128)(2,1)S(1)}, bf16[4,64,128]{2,1,0:T(8,128)(2,1)S(1)}, u32[]{:S(2)}, u32[]{:S(2)}) collective-permute-start(bf16[4,64,128]{2,1,0:T(8,128)(2,1)S(1)} %get-tuple-element.63), channel_id=1, source_target_pairs={{0,24},{4,28},{8,16},{12,20},{16,8},{20,12},{24,0},{28,4},{1,25},{... | collective-permute-start | bytes 196616 | tf_op jit(solution)/shard_map/ppermute | solution.py:161
  75.2 9.4 %collective-permute-start.9 = (bf16[4,64,128]{2,1,0:T(8,128)(2,1)S(1)}, bf16[4,64,128]{2,1,0:T(8,128)(2,1)S(1)}, u32[]{:S(2)}, u32[]{:S(2)}) collective-permute-start(bf16[4,64,128]{2,1,0:T(8,128)(2,1)S(1)} %get-tuple-element.64), channel_id=1, source_target_pairs={{0,28},{4,24},{8,20},{12,16},{16,12},{20,8},{24,4},{28,0},{1,29},{... | collective-permute-start | bytes 196616 | tf_op jit(solution)/shard_map/ppermute | solution.py:161
  75.3 10.4 %collective-permute-start.13 = (bf16[4,64,128]{2,1,0:T(8,128)(2,1)S(1)}, bf16[4,64,128]{2,1,0:T(8,128)(2,1)S(1)}, u32[]{:S(2)}, u32[]{:S(2)}) collective-permute-start(bf16[4,64,128]{2,1,0:T(8,128)(2,1)S(1)} %get-tuple-element.70), channel_id=1, source_target_pairs={{0,4},{4,0},{8,12},{12,8},{16,20},{20,16},{24,28},{28,24},{1,5},{5... | collective-permute-start | bytes 196616 | tf_op jit(solution)/shard_map/ppermute | solution.py:161
  76.9 11.6 %collective-permute-start.14 = (bf16[4,64,128]{2,1,0:T(8,128)(2,1)S(1)}, bf16[4,64,128]{2,1,0:T(8,128)(2,1)S(1)}, u32[]{:S(2)}, u32[]{:S(2)}) collective-permute-start(bf16[4,64,128]{2,1,0:T(8,128)(2,1)S(1)} %get-tuple-element.71), channel_id=1, source_target_pairs={{0,8},{4,12},{8,0},{12,4},{16,24},{20,28},{24,16},{28,20},{1,9},{5... | collective-permute-start | bytes 196616 | tf_op jit(solution)/shard_map/ppermute | solution.py:161
  79.4 13.4 %collective-permute-start.15 = (bf16[4,64,128]{2,1,0:T(8,128)(2,1)S(1)}, bf16[4,64,128]{2,1,0:T(8,128)(2,1)S(1)}, u32[]{:S(2)}, u32[]{:S(2)}) collective-permute-start(bf16[4,64,128]{2,1,0:T(8,128)(2,1)S(1)} %get-tuple-element.72), channel_id=1, source_target_pairs={{0,12},{4,8},{8,4},{12,0},{16,28},{20,24},{24,20},{28,16},{1,13},{... | collective-permute-start | bytes 196616 | tf_op jit(solution)/shard_map/ppermute | solution.py:161
  81.1 11.7 %collective-permute-start.16 = (bf16[4,64,128]{2,1,0:T(8,128)(2,1)S(1)}, bf16[4,64,128]{2,1,0:T(8,128)(2,1)S(1)}, u32[]{:S(2)}, u32[]{:S(2)}) collective-permute-start(bf16[4,64,128]{2,1,0:T(8,128)(2,1)S(1)} %get-tuple-element.73), channel_id=1, source_target_pairs={{0,16},{4,20},{8,24},{12,28},{16,0},{20,4},{24,8},{28,12},{1,17},{... | collective-permute-start | bytes 196616 | tf_op jit(solution)/shard_map/ppermute | solution.py:161
  84.6 8.2 %collective-permute-start.17 = (bf16[4,64,128]{2,1,0:T(8,128)(2,1)S(1)}, bf16[4,64,128]{2,1,0:T(8,128)(2,1)S(1)}, u32[]{:S(2)}, u32[]{:S(2)}) collective-permute-start(bf16[4,64,128]{2,1,0:T(8,128)(2,1)S(1)} %get-tuple-element.74), channel_id=1, source_target_pairs={{0,20},{4,16},{8,28},{12,24},{16,4},{20,0},{24,12},{28,8},{1,21},{... | collective-permute-start | bytes 196616 | tf_op jit(solution)/shard_map/ppermute | solution.py:161
  85.7 10.6 %collective-permute-start.18 = (bf16[4,64,128]{2,1,0:T(8,128)(2,1)S(1)}, bf16[4,64,128]{2,1,0:T(8,128)(2,1)S(1)}, u32[]{:S(2)}, u32[]{:S(2)}) collective-permute-start(bf16[4,64,128]{2,1,0:T(8,128)(2,1)S(1)} %get-tuple-element.75), channel_id=1, source_target_pairs={{0,24},{4,28},{8,16},{12,20},{16,8},{20,12},{24,0},{28,4},{1,25},{... | collective-permute-start | bytes 196616 | tf_op jit(solution)/shard_map/ppermute | solution.py:161
  88.5 9.6 %collective-permute-start.19 = (bf16[4,64,128]{2,1,0:T(8,128)(2,1)S(1)}, bf16[4,64,128]{2,1,0:T(8,128)(2,1)S(1)}, u32[]{:S(2)}, u32[]{:S(2)}) collective-permute-start(bf16[4,64,128]{2,1,0:T(8,128)(2,1)S(1)} %get-tuple-element.76), channel_id=1, source_target_pairs={{0,28},{4,24},{8,20},{12,16},{16,12},{20,8},{24,4},{28,0},{1,29},{... | collective-permute-start | bytes 196616 | tf_op jit(solution)/shard_map/ppermute | solution.py:161
  92.7 7.5 %collective-permute-start.23 = (bf16[4,64,128]{2,1,0:T(8,128)(2,1)S(1)}, bf16[4,64,128]{2,1,0:T(8,128)(2,1)S(1)}, u32[]{:S(2)}, u32[]{:S(2)}) collective-permute-start(bf16[4,64,128]{2,1,0:T(8,128)(2,1)S(1)} %get-tuple-element.82), channel_id=1, source_target_pairs={{0,4},{4,0},{8,12},{12,8},{16,20},{20,16},{24,28},{28,24},{1,5},{5... | collective-permute-start | bytes 196616 | tf_op jit(solution)/shard_map/ppermute | solution.py:161
  92.7 8.6 %collective-permute-start.24 = (bf16[4,64,128]{2,1,0:T(8,128)(2,1)S(1)}, bf16[4,64,128]{2,1,0:T(8,128)(2,1)S(1)}, u32[]{:S(2)}, u32[]{:S(2)}) collective-permute-start(bf16[4,64,128]{2,1,0:T(8,128)(2,1)S(1)} %get-tuple-element.83), channel_id=1, source_target_pairs={{0,8},{4,12},{8,0},{12,4},{16,24},{20,28},{24,16},{28,20},{1,9},{5... | collective-permute-start | bytes 196616 | tf_op jit(solution)/shard_map/ppermute | solution.py:161
  92.8 12.7 %collective-permute-start.25 = (bf16[4,64,128]{2,1,0:T(8,128)(2,1)S(1)}, bf16[4,64,128]{2,1,0:T(8,128)(2,1)S(1)}, u32[]{:S(2)}, u32[]{:S(2)}) collective-permute-start(bf16[4,64,128]{2,1,0:T(8,128)(2,1)S(1)} %get-tuple-element.84), channel_id=1, source_target_pairs={{0,12},{4,8},{8,4},{12,0},{16,28},{20,24},{24,20},{28,16},{1,13},{... | collective-permute-start | bytes 196616 | tf_op jit(solution)/shard_map/ppermute | solution.py:161
  96.2 9.3 %collective-permute-start.26 = (bf16[4,64,128]{2,1,0:T(8,128)(2,1)S(1)}, bf16[4,64,128]{2,1,0:T(8,128)(2,1)S(1)}, u32[]{:S(2)}, u32[]{:S(2)}) collective-permute-start(bf16[4,64,128]{2,1,0:T(8,128)(2,1)S(1)} %get-tuple-element.85), channel_id=1, source_target_pairs={{0,16},{4,20},{8,24},{12,28},{16,0},{20,4},{24,8},{28,12},{1,17},{... | collective-permute-start | bytes 196616 | tf_op jit(solution)/shard_map/ppermute | solution.py:161
  98.1 9.1 %collective-permute-start.27 = (bf16[4,64,128]{2,1,0:T(8,128)(2,1)S(1)}, bf16[4,64,128]{2,1,0:T(8,128)(2,1)S(1)}, u32[]{:S(2)}, u32[]{:S(2)}) collective-permute-start(bf16[4,64,128]{2,1,0:T(8,128)(2,1)S(1)} %get-tuple-element.86), channel_id=1, source_target_pairs={{0,20},{4,16},{8,28},{12,24},{16,4},{20,0},{24,12},{28,8},{1,21},{... | collective-permute-start | bytes 196616 | tf_op jit(solution)/shard_map/ppermute | solution.py:161
  100.3 8.7 %collective-permute-start.28 = (bf16[4,64,128]{2,1,0:T(8,128)(2,1)S(1)}, bf16[4,64,128]{2,1,0:T(8,128)(2,1)S(1)}, u32[]{:S(2)}, u32[]{:S(2)}) collective-permute-start(bf16[4,64,128]{2,1,0:T(8,128)(2,1)S(1)} %get-tuple-element.87), channel_id=1, source_target_pairs={{0,24},{4,28},{8,16},{12,20},{16,8},{20,12},{24,0},{28,4},{1,25},{... | collective-permute-start | bytes 196616 | tf_op jit(solution)/shard_map/ppermute | solution.py:161
  101.4 8.5 %collective-permute-start.29 = (bf16[4,64,128]{2,1,0:T(8,128)(2,1)S(1)}, bf16[4,64,128]{2,1,0:T(8,128)(2,1)S(1)}, u32[]{:S(2)}, u32[]{:S(2)}) collective-permute-start(bf16[4,64,128]{2,1,0:T(8,128)(2,1)S(1)} %get-tuple-element.88), channel_id=1, source_target_pairs={{0,28},{4,24},{8,20},{12,16},{16,12},{20,8},{24,4},{28,0},{1,29},{... | collective-permute-start | bytes 196616 | tf_op jit(solution)/shard_map/ppermute | solution.py:161
  105.5 6.9 %collective-permute-start.33 = (bf16[4,64,128]{2,1,0:T(8,128)(2,1)S(1)}, bf16[4,64,128]{2,1,0:T(8,128)(2,1)S(1)}, u32[]{:S(2)}, u32[]{:S(2)}) collective-permute-start(bf16[4,64,128]{2,1,0:T(8,128)(2,1)S(1)} %get-tuple-element.94), channel_id=1, source_target_pairs={{0,4},{4,0},{8,12},{12,8},{16,20},{20,16},{24,28},{28,24},{1,5},{5... | collective-permute-start | bytes 196616 | tf_op jit(solution)/shard_map/ppermute | solution.py:161
  105.6 9.1 %collective-permute-start.34 = (bf16[4,64,128]{2,1,0:T(8,128)(2,1)S(1)}, bf16[4,64,128]{2,1,0:T(8,128)(2,1)S(1)}, u32[]{:S(2)}, u32[]{:S(2)}) collective-permute-start(bf16[4,64,128]{2,1,0:T(8,128)(2,1)S(1)} %get-tuple-element.95), channel_id=1, source_target_pairs={{0,8},{4,12},{8,0},{12,4},{16,24},{20,28},{24,16},{28,20},{1,9},{5... | collective-permute-start | bytes 196616 | tf_op jit(solution)/shard_map/ppermute | solution.py:161
  107.2 10.4 %collective-permute-start.35 = (bf16[4,64,128]{2,1,0:T(8,128)(2,1)S(1)}, bf16[4,64,128]{2,1,0:T(8,128)(2,1)S(1)}, u32[]{:S(2)}, u32[]{:S(2)}) collective-permute-start(bf16[4,64,128]{2,1,0:T(8,128)(2,1)S(1)} %get-tuple-element.96), channel_id=1, source_target_pairs={{0,12},{4,8},{8,4},{12,0},{16,28},{20,24},{24,20},{28,16},{1,13},{... | collective-permute-start | bytes 196616 | tf_op jit(solution)/shard_map/ppermute | solution.py:161
  109.0 8.6 %collective-permute-start.36 = (bf16[4,64,128]{2,1,0:T(8,128)(2,1)S(1)}, bf16[4,64,128]{2,1,0:T(8,128)(2,1)S(1)}, u32[]{:S(2)}, u32[]{:S(2)}) collective-permute-start(bf16[4,64,128]{2,1,0:T(8,128)(2,1)S(1)} %get-tuple-element.97), channel_id=1, source_target_pairs={{0,16},{4,20},{8,24},{12,28},{16,0},{20,4},{24,8},{28,12},{1,17},{... | collective-permute-start | bytes 196616 | tf_op jit(solution)/shard_map/ppermute | solution.py:161
  109.8 8.6 %collective-permute-start.37 = (bf16[4,64,128]{2,1,0:T(8,128)(2,1)S(1)}, bf16[4,64,128]{2,1,0:T(8,128)(2,1)S(1)}, u32[]{:S(2)}, u32[]{:S(2)}) collective-permute-start(bf16[4,64,128]{2,1,0:T(8,128)(2,1)S(1)} %get-tuple-element.98), channel_id=1, source_target_pairs={{0,20},{4,16},{8,28},{12,24},{16,4},{20,0},{24,12},{28,8},{1,21},{... | collective-permute-start | bytes 196616 | tf_op jit(solution)/shard_map/ppermute | solution.py:161
  112.4 6.2 %collective-permute-start.38 = (bf16[4,64,128]{2,1,0:T(8,128)(2,1)S(1)}, bf16[4,64,128]{2,1,0:T(8,128)(2,1)S(1)}, u32[]{:S(2)}, u32[]{:S(2)}) collective-permute-start(bf16[4,64,128]{2,1,0:T(8,128)(2,1)S(1)} %get-tuple-element.99), channel_id=1, source_target_pairs={{0,24},{4,28},{8,16},{12,20},{16,8},{20,12},{24,0},{28,4},{1,25},{... | collective-permute-start | bytes 196616 | tf_op jit(solution)/shard_map/ppermute | solution.py:161
  114.6 7.0 %collective-permute-start.39 = (bf16[4,64,128]{2,1,0:T(8,128)(2,1)S(1)}, bf16[4,64,128]{2,1,0:T(8,128)(2,1)S(1)}, u32[]{:S(2)}, u32[]{:S(2)}) collective-permute-start(bf16[4,64,128]{2,1,0:T(8,128)(2,1)S(1)} %get-tuple-element.100), channel_id=1, source_target_pairs={{0,28},{4,24},{8,20},{12,16},{16,12},{20,8},{24,4},{28,0},{1,29},{... | collective-permute-start | bytes 196616 | tf_op jit(solution)/shard_map/ppermute | solution.py:161
  (8 other events, 6.1 us)

commit v4 on v0

v4 whole, which is shorter than its diff:
```python
import functools

import jax
import jax.numpy as jnp
from jax import lax
from jax.experimental import pallas as pl
from jax.experimental.pallas import tpu as pltpu
from jax.sharding import PartitionSpec as P

LANES = 128
STEP = 64
CHUNKS = (4, 4, 4, 4)
GROUPS = ((0, 1), (2,), (3,))
MIB = 1024 * 1024
CHEAP = pl.CostEstimate(flops=1024, bytes_accessed=1024, transcendentals=0)
IN_VMEM = pl.BlockSpec(memory_space=pltpu.VMEM)
IN_SMEM = pl.BlockSpec(memory_space=pltpu.SMEM)
ANYWHERE = pl.BlockSpec(memory_space=pl.ANY)
IN_HBM = pl.BlockSpec(memory_space=pltpu.MemorySpace.HBM)


def quarter_kernel(rows, far, n_later, place_ref, x_ref, c_hbm, *refs):
    refs = refs[2 * n_later :]
    outs, (acc, c_ref, held, c_sem, sems) = refs[:-5], refs[-5:]
    at = pl.program_id(0)
    step, k_all, depth = x_ref.shape
    padded = held.shape[2]

    @pl.when(at == 0)
    def _():
        first = pl.multiple_of(((place_ref[0] >> 1) ^ far) * 2 * LANES, 2 * LANES)
        copy = pltpu.make_async_copy(c_hbm.at[:, pl.ds(first, 2 * LANES)], c_ref, c_sem)
        copy.start()
        copy.wait()

    x = x_ref[...].reshape(step * k_all, depth)
    product = jnp.dot(x, c_ref[...], preferred_element_type=jnp.float32)
    for d in range(2):
        acc[d] = product[:, d * LANES : (d + 1) * LANES]
    here = pl.ds(pl.multiple_of(at * step, step), step)
    keep = lax.broadcasted_iota(jnp.int32, (step, LANES), 0) < rows - at * step
    first = 0
    for n, out in enumerate(outs):
        d = (place_ref[0] & 1) ^ (n & 1)
        kc = out.shape[0]
        for k in range(first, first + kc):
            block = acc[d, pl.ds(k, step, stride=k_all), :]
            held[n & 1, k, here] = jnp.where(keep, block, 0.0).astype(jnp.bfloat16)
        mine = held.at[n & 1, pl.ds(first, kc)]
        pltpu.make_async_copy(mine.at[:, here], out.at[:, here], sems.at[n]).start()
        if n & 1:
            first += kc

    @pl.when(at == padded // step - 1)
    def _():
        first = 0
        for n, out in enumerate(outs):
            kc = out.shape[0]
            pltpu.make_async_copy(held.at[n & 1, pl.ds(first, kc)], out, sems.at[n]).wait()
            if n & 1:
                first += kc


def quarter_of(place, by_r, coeffs, far, padded, chunks, later=()):
    rows, k_all, depth = by_r.shape
    outs = [jax.ShapeDtypeStruct((kc, padded, LANES), jnp.bfloat16) for kc in chunks for _ in range(2)]
    out = pl.pallas_call(
        functools.partial(quarter_kernel, rows, far, len(later)),
        grid_spec=pltpu.PrefetchScalarGridSpec(
            num_scalar_prefetch=1,
            grid=(padded // STEP,),
            in_specs=[pl.BlockSpec((STEP, k_all, depth), lambda r, place: (r, 0, 0))]
            + [IN_HBM] * (1 + len(later)),
            out_specs=[IN_HBM] * (len(later) + len(outs)),
            scratch_shapes=[
                pltpu.VMEM((2, STEP * k_all, LANES), jnp.float32),
                pltpu.VMEM((depth, 2 * LANES), jnp.bfloat16),
                pltpu.VMEM((2, k_all, padded, LANES), jnp.bfloat16),
                pltpu.SemaphoreType.DMA,
                pltpu.SemaphoreType.DMA((len(outs),)),
            ],
        ),
        out_shape=[jax.ShapeDtypeStruct(x.shape, x.dtype) for x in later] + outs,
        input_output_aliases={3 + n: n for n in range(len(later))},
        compiler_params=pltpu.CompilerParams(vmem_limit_bytes=50 * MIB),
        cost_estimate=CHEAP,
        name=f"quarter{far}",
    )(place, by_r, coeffs, *later)
    n = len(later)
    return list(out[:n]), list(out[n:])


def turn_kernel(rows, c_ref, out_ref):
    n_mo, orbitals, padded = out_ref.shape
    none = jnp.zeros((padded - rows, orbitals), jnp.float32)
    for n in range(n_mo):
        part = c_ref[n * rows : (n + 1) * rows, :].astype(jnp.float32)
        out_ref[n] = jnp.concatenate([part, none], axis=0).T.astype(jnp.bfloat16)


def turn(coeffs, n_mo, padded):
    depth, orbitals = coeffs.shape
    return pl.pallas_call(
        functools.partial(turn_kernel, depth // n_mo),
        in_specs=[IN_VMEM],
        out_specs=IN_VMEM,
        out_shape=jax.ShapeDtypeStruct((n_mo, orbitals, padded), jnp.bfloat16),
        compiler_params=pltpu.CompilerParams(vmem_limit_bytes=24 * MIB),
        cost_estimate=CHEAP,
        name="turn",
    )(coeffs)


def half_kernel(first, n_mo, n_near, place_ref, *refs):
    blocks, t_ref, refs = refs[:n_mo], refs[n_mo], refs[n_mo + 1 :]
    far, near, held = refs[-n_near - 2], refs[-n_near - 1 : -1], refs[-1]
    kc, block, lanes = near[0].shape
    for k in range(0, kc, 2):
        half = None
        for o, a_ref in enumerate(blocks):
            at = k if a_ref.shape[0] == kc else first + k
            columns = jnp.concatenate([a_ref[at], a_ref[at + 1]], axis=1)
            part = jnp.dot(t_ref[place_ref[0] ^ o], columns, preferred_element_type=jnp.float32)
            half = part if half is None else half + part
        held[...] = half
        for o in range(2 * n_near):
            start = pl.multiple_of((place_ref[1] ^ o) * block, block)
            for n in range(2):
                piece = held[pl.ds(start, block), n * lanes : (n + 1) * lanes].astype(jnp.bfloat16)
                if o < n_near:
                    near[o][k + n] = piece
                else:
                    far[o - n_near, k + n] = piece


def half_of(place, blocks, turned, n_pair, first, kc, later, after):
    n_mo, orbitals, padded = turned.shape
    lanes = blocks[0].shape[-1]
    block, n_near = orbitals // n_pair, n_pair // 2
    piece = jax.ShapeDtypeStruct((kc, block, lanes), jnp.bfloat16)
    far = jax.ShapeDtypeStruct((n_near, *piece.shape), jnp.bfloat16)
    out = pl.pallas_call(
        functools.partial(half_kernel, first, n_mo, n_near),
        in_specs=[IN_SMEM]
        + [IN_VMEM] * (n_mo + 1)
        + [IN_HBM] * len(later)
        + [ANYWHERE] * len(after),
        out_specs=[IN_HBM] * len(later) + [IN_VMEM] * (1 + n_near),
        out_shape=[jax.ShapeDtypeStruct(x.shape, x.dtype) for x in later] + [far] + [piece] * n_near,
        scratch_shapes=[pltpu.VMEM((orbitals, 2 * lanes), jnp.float32)],
        input_output_aliases={n_mo + 2 + n: n for n in range(len(later))},
        compiler_params=pltpu.CompilerParams(vmem_limit_bytes=24 * MIB),
        cost_estimate=CHEAP,
        name="half",
    )(place, *blocks, turned, *later, *after)
    n = len(later)
    return out[:n], out[n], out[n + 1 :]


def merge_kernel(n_near, n_chunks, *refs):
    near, far, outs = refs[: n_chunks * (n_near - 1)], refs[n_chunks * (n_near - 1) :], refs[1 - n_near :]
    for o, out in enumerate(outs, 1):
        at = 0
        for c in range(n_chunks):
            x = near[c * (n_near - 1) + o - 1]
            out[at : at + x.shape[0]] = x[...]
            at += x.shape[0]
        for c in range(n_chunks):
            kc = far[c].shape[1]
            out[at : at + kc] = far[c][o]
            at += kc


def merge(near, far, after):
    n_near, _, block, lanes = far[0].shape
    size = 2 * sum(x.shape[1] for x in far)
    parts = [x for chunk in near for x in chunk[1:]]
    return pl.pallas_call(
        functools.partial(merge_kernel, n_near, len(far)),
        in_specs=[IN_VMEM] * (len(parts) + len(far)) + [ANYWHERE] * len(after),
        out_specs=[IN_VMEM] * (n_near - 1),
        out_shape=[jax.ShapeDtypeStruct((size, block, lanes), jnp.bfloat16)] * (n_near - 1),
        compiler_params=pltpu.CompilerParams(vmem_limit_bytes=24 * MIB),
        cost_estimate=CHEAP,
        name="merge",
    )(*parts, *far, *after)


def combine_kernel(sources, per_step, mirror_ref, place_ref, *refs):
    pieces, out_ref, held = refs[:-2], refs[-2], refs[-1]
    step = pl.program_id(0)

    @pl.when(step == 0)
    def _():
        for piece, parts in zip(pieces, sources):
            for offset, at, first, kc in parts:
                held[place_ref[1] ^ offset, first : first + kc] = piece[...] if at is None else piece[at]

    k_all = held.shape[1]
    for n in range(per_step):
        k = step * per_step + n
        m = mirror_ref[k]
        own = held[k // k_all, lax.rem(k, k_all)].astype(jnp.float32)
        partner = held[m // k_all, lax.rem(m, k_all)].astype(jnp.float32)
        out_ref[n] = 0.5 * (own + partner)


def combine(pieces, sources, mirror, place, n_pair):
    _, block, lanes = pieces[0].shape
    k_all = sum(CHUNKS)
    rows = n_pair * k_all
    per_step = max(1, 32 * 64 // block)
    return pl.pallas_call(
        functools.partial(combine_kernel, sources, per_step),
        grid_spec=pltpu.PrefetchScalarGridSpec(
            num_scalar_prefetch=2,
            grid=(rows // per_step,),
            in_specs=[IN_VMEM] * len(pieces),
            out_specs=pl.BlockSpec((per_step, block, lanes), lambda k, m, place: (k, 0, 0)),
            scratch_shapes=[pltpu.VMEM((n_pair, k_all, block, lanes), jnp.bfloat16)],
        ),
        out_shape=jax.ShapeDtypeStruct((rows, block, lanes), jnp.float32),
        compiler_params=pltpu.CompilerParams(vmem_limit_bytes=24 * MIB),
        cost_estimate=CHEAP,
        name="combine",
    )(mirror, place, *pieces)


def flipped(x, axis, size, offset):
    return lax.ppermute(x, axis, [(i, i ^ offset) for i in range(size)])


def on_device(n_pair, n_mo, integrals, coeffs, mirror):
    k_all, rows, depth = integrals.shape
    orbitals = coeffs.shape[1]
    padded = -(-rows // STEP) * STEP
    n_near = n_pair // 2
    by_r = jnp.transpose(integrals, (1, 0, 2))
    place = jnp.stack([lax.axis_index("mo"), lax.axis_index("pair")]).astype(jnp.int32)
    turned = turn(coeffs, n_mo, padded)
    _, queue = quarter_of(place, by_r, coeffs, 1, padded, CHUNKS)
    queue[2:3], (own, beside) = quarter_of(place, by_r, coeffs, 0, padded, (k_all,), queue[2:3])
    beside = flipped(beside, "mo", n_mo, 1)

    firsts = [sum(CHUNKS[:c]) for c in range(len(CHUNKS))]
    pieces, sources, near, far = [], [], {}, {}
    for c, kc in enumerate(CHUNKS):
        across = [flipped(x, "mo", n_mo, 2 + n) for n, x in enumerate(queue[2 * c : 2 * c + 2])]
        coming = slice(2 * c + 3, 2 * c + 5)
        after = [far[c - 2]] if c >= 2 else []
        queue[coming], out, near[c] = half_of(
            place, [own, beside, *across], turned, n_pair, firsts[c], kc, queue[coming], after
        )
        far[c] = flipped(out, "pair", n_pair, n_near)
        pieces += [near[c][0], far[c]]
        sources += [((0, None, firsts[c], kc),), ((n_near, 0, firsts[c], kc),)]
    after = []
    for group in GROUPS:
        start, size = firsts[group[0]], sum(CHUNKS[c] for c in group)
        messages = merge([near[c] for c in group], [far[c] for c in group], after)
        after = [flipped(x, "pair", n_pair, o) for o, x in enumerate(messages, 1)]
        pieces += after
        for o in range(1, n_near):
            sources.append(((o, slice(0, size), start, size), (o ^ n_near, slice(size, 2 * size), start, size)))
    return combine(pieces, sources, mirror, place, n_pair)


def solution(mesh):
    return jax.shard_map(
        functools.partial(on_device, mesh.shape["pair"], mesh.shape["mo"]),
        mesh=mesh,
        in_specs=(P("pair", "mo", None), P(), P()),
        out_specs=P(None, "pair", "mo"),
        check_vma=False,
    )
```

time: 225 us -> 107 us (0.48)
  the two profiles are of different devices: /device:TPU:0 before, /device:TPU:16 now
where the time goes in v4:
time: 107 us
  waiting for transfers between devices  56.2 us (53%)
  starting transfers between devices  24.8 us (23%)
  Pallas kernels  24.7 us (23%)
  local copies, waits for them, and re-layouts  1.22 us (1%)
    ppermute x22, waiting for transfers between devices, flipped(): return lax.ppermute(x, axis, [(i, i ^ offset) for i in range(size)])  56.2 us
    ppermute x22, starting transfers between devices, flipped(): return lax.ppermute(x, axis, [(i, i ^ offset) for i in range(size)])  24.8 us
    pallas_call x2, Pallas kernels, quarter_of(): pl.pallas_call(functools.partial(quarter_kernel, rows, far, len(later)),...  15.1 us
    pallas_call x4, Pallas kernels, half_of(): pl.pallas_call(functools.partial(half_kernel, first, n_mo, n_near), in_sp...  5.38 us
    pallas_call x1, Pallas kernels, combine(): pl.pallas_call(functools.partial(combine_kernel, sources, per_step), grid...  3.79 us
  transfers between devices with their start and end apart: 22, of which 15 were waited for; matrix products, arithmetic and copies ran while one was open for 0% of the time, Pallas kernels for 5%

profile of v4, /device:TPU:16, one launch (start us, length us, event | category | flops | bytes accessed | tf_op | source)
XLA Modules:
  0.0 107.1 jit_solution(14707675985153183287)
XLA Ops:
  0.0 0.1 pad_add_fusion.place_ref
  0.1 1.2 %copy-done = bf16[1000,512]{1,0:T(8,128)(2,1)S(1)} copy-done((bf16[1000,512]{1,0:T(8,128)(2,1)S(1)}, bf16[1000,512]{1,0:T(8,128)(2,1)}, u32[]{:S(2)}) %copy-start) | copy-done | bytes 1024024
  1.3 7.9 %quarter1.1 = (bf16[4,256,128]{2,1,0:T(8,128)(2,1)S(1)}, bf16[4,256,128]{2,1,0:T(8,128)(2,1)S(1)}, bf16[4,256,128]{2,1,0:T(8,128)(2,1)S(1)}, bf16[4,256,128]{2,1...) custom-call(s32[2]{0:T(128)S(1)} %pad_add_fusion.place_ref, ...), custom_call_target="tpu_custom_call" | custom-call | flops 1024 | bytes 1024 | tf_op jit(solution)/shard_map/quarter1/pallas_call | solution.py:67
  9.2 7.1 %quarter0.1 = (bf16[4,256,128]{2,1,0:T(8,128)(2,1)S(1)}, bf16[16,256,128]{2,1,0:T(8,128)(2,1)S(1)}, bf16[16,256,128]{2,1,0:T(8,128)(2,1)S(1)}) custom-call(s32[2]{0:T(128)S(1)} %pad_add_fusion.place_ref, bf16[250,16,1000]{2,1,0:T(8,128)(2,1)} %bitcast.4, bf16[1000,512]{1,0:T(8,128)(2,1)S(1)} %copy-done, ...), custom_call_target="tpu_custom_call", output_to_operand_aliasing={{0}: (3, {})} | custom-call | flops 1024 | bytes 1024 | tf_op jit(solution)/shard_map/quarter0/pallas_call | solution.py:67
  16.4 0.1 collective-permute-start
  16.4 1.6 %collective-permute-start.1 = (bf16[4,256,128]{2,1,0:T(8,128)(2,1)S(1)}, bf16[4,256,128]{2,1,0:T(8,128)(2,1)S(1)}, u32[]{:S(2)}, u32[]{:S(2)}) collective-permute-start(bf16[4,256,128]{2,1,0:T(8,128)(2,1)S(1)} %get-tuple-element.53), channel_id=1, source_target_pairs={{0,2},{1,3},{2,0},{3,1},{4,6},{5,7},{6,4},{7,5},{8,10},{9,11},{10,... | collective-permute-start | bytes 786440 | tf_op jit(solution)/shard_map/ppermute | solution.py:230
  18.0 0.3 collective-permute-start.2
  18.3 1.5 %collective-permute-start.4 = (bf16[4,256,128]{2,1,0:T(8,128)(2,1)S(1)}, bf16[4,256,128]{2,1,0:T(8,128)(2,1)S(1)}, u32[]{:S(2)}, u32[]{:S(2)}) collective-permute-start(bf16[4,256,128]{2,1,0:T(8,128)(2,1)S(1)} %get-tuple-element.59), channel_id=1, source_target_pairs={{0,2},{1,3},{2,0},{3,1},{4,6},{5,7},{6,4},{7,5},{8,10},{9,11},{10,... | collective-permute-start | bytes 786440 | tf_op jit(solution)/shard_map/ppermute | solution.py:230
  19.8 0.4 turn.1.refs_4_
  20.2 5.4 %collective-permute-done.1.refs_2_ = bf16[4,256,128]{2,1,0:T(8,128)(2,1)S(1)} collective-permute-done((bf16[4,256,128]{2,1,0:T(8,128)(2,1)S(1)}, bf16[4,256,128]{2,1,0:T(8,128)(2,1)S(1)}, u32[]{:S(2)}, u32[]{:S(2)}) %collective-permute-start.1) | collective-permute-done | bytes 262176 | tf_op jit(solution)/shard_map/ppermute | solution.py:230
  25.6 4.7 %collective-permute-done.2.refs_3_ = bf16[4,256,128]{2,1,0:T(8,128)(2,1)S(1)} collective-permute-done((bf16[4,256,128]{2,1,0:T(8,128)(2,1)S(1)}, bf16[4,256,128]{2,1,0:T(8,128)(2,1)S(1)}, u32[]{:S(2)}, u32[]{:S(2)}) %collective-permute-start.2) | collective-permute-done | bytes 262176 | tf_op jit(solution)/shard_map/ppermute | solution.py:230
  30.3 0.0 collective-permute-done.refs_1_
  30.3 1.4 %half.4 = (bf16[4,256,128]{2,1,0:T(8,128)(2,1)S(1)}, bf16[4,256,128]{2,1,0:T(8,128)(2,1)S(1)}, bf16[4,4,64,128]{3,2,1,0:T(8,128)(2,1)S(1)}, bf16[4,64,128]{2,1,0...) custom-call(s32[2]{0:T(128)S(1)} %pad_add_fusion.place_ref, ...), custom_call_target="tpu_custom_call", output_to_operand_aliasing={{0}: (6, {}), {1}: (7, {})} | custom-call | flops 1024 | bytes 1024 | tf_op jit(solution)/shard_map/half/pallas_call | solution.py:142
  31.7 0.0 copy-start.1
  31.7 1.9 %collective-permute-start.5 = (bf16[4,256,128]{2,1,0:T(8,128)(2,1)S(1)}, bf16[4,256,128]{2,1,0:T(8,128)(2,1)S(1)}, u32[]{:S(2)}, u32[]{:S(2)}) collective-permute-start(bf16[4,256,128]{2,1,0:T(8,128)(2,1)S(1)} %get-tuple-element.60), channel_id=1, source_target_pairs={{0,3},{1,2},{2,1},{3,0},{4,7},{5,6},{6,5},{7,4},{8,11},{9,10},{10,... | collective-permute-start | bytes 786440 | tf_op jit(solution)/shard_map/ppermute | solution.py:230
  33.6 0.3 collective-permute-start.3
  34.0 0.2 collective-permute-start.7
  34.1 2.7 %collective-permute-done.4.refs_2_ = bf16[4,256,128]{2,1,0:T(8,128)(2,1)S(1)} collective-permute-done((bf16[4,256,128]{2,1,0:T(8,128)(2,1)S(1)}, bf16[4,256,128]{2,1,0:T(8,128)(2,1)S(1)}, u32[]{:S(2)}, u32[]{:S(2)}) %collective-permute-start.4) | collective-permute-done | bytes 262176 | tf_op jit(solution)/shard_map/ppermute | solution.py:230
  36.9 4.7 %collective-permute-done.5.refs_3_ = bf16[4,256,128]{2,1,0:T(8,128)(2,1)S(1)} collective-permute-done((bf16[4,256,128]{2,1,0:T(8,128)(2,1)S(1)}, bf16[4,256,128]{2,1,0:T(8,128)(2,1)S(1)}, u32[]{:S(2)}, u32[]{:S(2)}) %collective-permute-start.5) | collective-permute-done | bytes 262176 | tf_op jit(solution)/shard_map/ppermute | solution.py:230
  41.6 1.3 %half.5 = (bf16[4,256,128]{2,1,0:T(8,128)(2,1)S(1)}, bf16[4,256,128]{2,1,0:T(8,128)(2,1)S(1)}, bf16[4,4,64,128]{3,2,1,0:T(8,128)(2,1)S(1)}, bf16[4,64,128]{2,1,0...) custom-call(s32[2]{0:T(128)S(1)} %pad_add_fusion.place_ref, ...), custom_call_target="tpu_custom_call", output_to_operand_aliasing={{0}: (6, {}), {1}: (7, {})} | custom-call | flops 1024 | bytes 1024 | tf_op jit(solution)/shard_map/half/pallas_call | solution.py:142
  42.9 1.9 %collective-permute-start.8 = (bf16[4,256,128]{2,1,0:T(8,128)(2,1)S(1)}, bf16[4,256,128]{2,1,0:T(8,128)(2,1)S(1)}, u32[]{:S(2)}, u32[]{:S(2)}) collective-permute-start(bf16[4,256,128]{2,1,0:T(8,128)(2,1)S(1)} %get-tuple-element.66), channel_id=1, source_target_pairs={{0,3},{1,2},{2,1},{3,0},{4,7},{5,6},{6,5},{7,4},{8,11},{9,10},{10,... | collective-permute-start | bytes 786440 | tf_op jit(solution)/shard_map/ppermute | solution.py:230
  44.8 0.6 collective-permute-start.6
  45.5 0.2 collective-permute-start.10
  45.6 2.4 %collective-permute-done.7.refs_2_ = bf16[4,256,128]{2,1,0:T(8,128)(2,1)S(1)} collective-permute-done((bf16[4,256,128]{2,1,0:T(8,128)(2,1)S(1)}, bf16[4,256,128]{2,1,0:T(8,128)(2,1)S(1)}, u32[]{:S(2)}, u32[]{:S(2)}) %collective-permute-start.7) | collective-permute-done | bytes 262176 | tf_op jit(solution)/shard_map/ppermute | solution.py:230
  48.1 4.7 %collective-permute-done.8.refs_3_ = bf16[4,256,128]{2,1,0:T(8,128)(2,1)S(1)} collective-permute-done((bf16[4,256,128]{2,1,0:T(8,128)(2,1)S(1)}, bf16[4,256,128]{2,1,0:T(8,128)(2,1)S(1)}, u32[]{:S(2)}, u32[]{:S(2)}) %collective-permute-start.8) | collective-permute-done | bytes 262176 | tf_op jit(solution)/shard_map/ppermute | solution.py:230
  52.8 1.3 %half.6 = (bf16[4,256,128]{2,1,0:T(8,128)(2,1)S(1)}, bf16[4,4,64,128]{3,2,1,0:T(8,128)(2,1)S(1)}, bf16[4,64,128]{2,1,0:T(8,128)(2,1)S(1)}, bf16[4,64,128]{2,1,0:...) custom-call(s32[2]{0:T(128)S(1)} %pad_add_fusion.place_ref, ...), custom_call_target="tpu_custom_call", output_to_operand_aliasing={{0}: (6, {})} | custom-call | flops 1024 | bytes 1024 | tf_op jit(solution)/shard_map/half/pallas_call | solution.py:142
  54.1 1.9 %collective-permute-start.11 = (bf16[4,256,128]{2,1,0:T(8,128)(2,1)S(1)}, bf16[4,256,128]{2,1,0:T(8,128)(2,1)S(1)}, u32[]{:S(2)}, u32[]{:S(2)}) collective-permute-start(bf16[4,256,128]{2,1,0:T(8,128)(2,1)S(1)} %get-tuple-element.71), channel_id=1, source_target_pairs={{0,3},{1,2},{2,1},{3,0},{4,7},{5,6},{6,5},{7,4},{8,11},{9,10},{10,... | collective-permute-start | bytes 786440 | tf_op jit(solution)/shard_map/ppermute | solution.py:230
  56.1 0.6 collective-permute-start.9
  56.7 0.1 merge.3
  56.7 1.6 %collective-permute-start.13 = (bf16[16,64,128]{2,1,0:T(8,128)(2,1)S(1)}, bf16[16,64,128]{2,1,0:T(8,128)(2,1)S(1)}, u32[]{:S(2)}, u32[]{:S(2)}) collective-permute-start(bf16[16,64,128]{2,1,0:T(8,128)(2,1)S(1)} %get-tuple-element.80), channel_id=1, source_target_pairs={{0,4},{4,0},{8,12},{12,8},{16,20},{20,16},{24,28},{28,24},{1,5},{5... | collective-permute-start | bytes 786440 | tf_op jit(solution)/shard_map/ppermute | solution.py:230
  58.3 4.1 %collective-permute-start.14 = (bf16[16,64,128]{2,1,0:T(8,128)(2,1)S(1)}, bf16[16,64,128]{2,1,0:T(8,128)(2,1)S(1)}, u32[]{:S(2)}, u32[]{:S(2)}) collective-permute-start(bf16[16,64,128]{2,1,0:T(8,128)(2,1)S(1)} %get-tuple-element.81), channel_id=1, source_target_pairs={{0,8},{4,12},{8,0},{12,4},{16,24},{20,28},{24,16},{28,20},{1,9},{5... | collective-permute-start | bytes 786440 | tf_op jit(solution)/shard_map/ppermute | solution.py:230
  62.5 1.6 %collective-permute-done.11.refs_3_ = bf16[4,256,128]{2,1,0:T(8,128)(2,1)S(1)} collective-permute-done((bf16[4,256,128]{2,1,0:T(8,128)(2,1)S(1)}, bf16[4,256,128]{2,1,0:T(8,128)(2,1)S(1)}, u32[]{:S(2)}, u32[]{:S(2)}) %collective-permute-start.11) | collective-permute-done | bytes 262176 | tf_op jit(solution)/shard_map/ppermute | solution.py:230
  64.0 1.3 %half.7 = (bf16[4,4,64,128]{3,2,1,0:T(8,128)(2,1)S(1)}, bf16[4,64,128]{2,1,0:T(8,128)(2,1)S(1)}, bf16[4,64,128]{2,1,0:T(8,128)(2,1)S(1)}, bf16[4,64,128]{2,1,0:T(8,128)(2,1)S(1)}, bf16[4,64,128]{2,1,0:T(8,128)(2,1)S(1)}) custom-call(s32[2]{0:T(128)S(1)} %pad_add_fusion.place_ref, bf16[16,256,128]{2,1,0:T(8,128)(2,1)S(1)} %get-tuple-element.51.refs_0_, ...), custom_call_target="tpu_custom_call" | custom-call | flops 1024 | bytes 1024 | tf_op jit(solution)/shard_map/half/pallas_call | solution.py:142
  65.4 0.4 collective-permute-start.12
  65.8 3.0 %collective-permute-done.9.refs_3_.refs_5_ = bf16[4,4,64,128]{3,2,1,0:T(8,128)(2,1)S(1)} collective-permute-done((bf16[4,4,64,128]{3,2,1,0:T(8,128)(2,1)S(1)}, bf16[4,4,64,128]{3,2,1,0:T(8,128)(2,1)S(1)}, u32[]{:S(2)}, u32[]{:S(2)}) %collective-permute-start.9) | collective-permute-done | bytes 262176 | tf_op jit(solution)/shard_map/ppermute | solution.py:230
  68.8 11.3 %collective-permute-done.14.refs_5_.refs_9_ = bf16[16,64,128]{2,1,0:T(8,128)(2,1)S(1)} collective-permute-done((bf16[16,64,128]{2,1,0:T(8,128)(2,1)S(1)}, bf16[16,64,128]{2,1,0:T(8,128)(2,1)S(1)}, u32[]{:S(2)}, u32[]{:S(2)}) %collective-permute-start.14) | collective-permute-done | bytes 262176 | tf_op jit(solution)/shard_map/ppermute | solution.py:230
  80.0 4.7 %collective-permute-done.15.refs_6_.refs_10_ = bf16[16,64,128]{2,1,0:T(8,128)(2,1)S(1)} collective-permute-done((bf16[16,64,128]{2,1,0:T(8,128)(2,1)S(1)}, bf16[16,64,128]{2,1,0:T(8,128)(2,1)S(1)}, u32[]{:S(2)}, u32[]{:S(2)}) %collective-permute-start.15) | collective-permute-done | bytes 262176 | tf_op jit(solution)/shard_map/ppermute | solution.py:230
  84.7 0.6 collective-permute-start.16
  85.3 3.4 %collective-permute-start.17 = (bf16[8,64,128]{2,1,0:T(8,128)(2,1)S(1)}, bf16[8,64,128]{2,1,0:T(8,128)(2,1)S(1)}, u32[]{:S(2)}, u32[]{:S(2)}) collective-permute-start(bf16[8,64,128]{2,1,0:T(8,128)(2,1)S(1)} %get-tuple-element.87), channel_id=1, source_target_pairs={{0,8},{4,12},{8,0},{12,4},{16,24},{20,28},{24,16},{28,20},{1,9},{5... | collective-permute-start | bytes 393224 | tf_op jit(solution)/shard_map/ppermute | solution.py:230
  88.7 1.0 collective-permute-done.16.refs_4_.refs_11_
  89.8 2.9 %collective-permute-done.17.refs_5_.refs_12_ = bf16[8,64,128]{2,1,0:T(8,128)(2,1)S(1)} collective-permute-done((bf16[8,64,128]{2,1,0:T(8,128)(2,1)S(1)}, bf16[8,64,128]{2,1,0:T(8,128)(2,1)S(1)}, u32[]{:S(2)}, u32[]{:S(2)}) %collective-permute-start.17) | collective-permute-done | bytes 131104 | tf_op jit(solution)/shard_map/ppermute | solution.py:230
  92.7 1.9 %collective-permute-done.18.refs_6_.refs_13_ = bf16[8,64,128]{2,1,0:T(8,128)(2,1)S(1)} collective-permute-done((bf16[8,64,128]{2,1,0:T(8,128)(2,1)S(1)}, bf16[8,64,128]{2,1,0:T(8,128)(2,1)S(1)}, u32[]{:S(2)}, u32[]{:S(2)}) %collective-permute-start.18) | collective-permute-done | bytes 131104 | tf_op jit(solution)/shard_map/ppermute | solution.py:230
  94.6 1.0 collective-permute-start.19
  95.7 1.7 %collective-permute-start.20 = (bf16[8,64,128]{2,1,0:T(8,128)(2,1)S(1)}, bf16[8,64,128]{2,1,0:T(8,128)(2,1)S(1)}, u32[]{:S(2)}, u32[]{:S(2)}) collective-permute-start(bf16[8,64,128]{2,1,0:T(8,128)(2,1)S(1)} %get-tuple-element.93), channel_id=1, source_target_pairs={{0,8},{4,12},{8,0},{12,4},{16,24},{20,28},{24,16},{28,20},{1,9},{5... | collective-permute-start | bytes 393224 | tf_op jit(solution)/shard_map/ppermute | solution.py:230
  97.4 0.8 collective-permute-start.21
  98.2 2.8 %collective-permute-done.19.refs_14_ = bf16[8,64,128]{2,1,0:T(8,128)(2,1)S(1)} collective-permute-done((bf16[8,64,128]{2,1,0:T(8,128)(2,1)S(1)}, bf16[8,64,128]{2,1,0:T(8,128)(2,1)S(1)}, u32[]{:S(2)}, u32[]{:S(2)}) %collective-permute-start.19) | collective-permute-done | bytes 131104 | tf_op jit(solution)/shard_map/ppermute | solution.py:230
  101.0 2.3 %collective-permute-done.21.refs_16_ = bf16[8,64,128]{2,1,0:T(8,128)(2,1)S(1)} collective-permute-done((bf16[8,64,128]{2,1,0:T(8,128)(2,1)S(1)}, bf16[8,64,128]{2,1,0:T(8,128)(2,1)S(1)}, u32[]{:S(2)}, u32[]{:S(2)}) %collective-permute-start.21) | collective-permute-done | bytes 131104 | tf_op jit(solution)/shard_map/ppermute | solution.py:230
  103.3 3.8 %combine.1 = f32[128,64,128]{2,1,0:T(8,128)} custom-call(s32[128]{0:T(128)S(1)} %copy-done.1, s32[2]{0:T(128)S(1)} %pad_add_fusion.place_ref, bf16[4,64,128]{2,1,0:T(8,128)(2,1)S(1)} %get-tuple-element.57.refs_0_, bf16[4,4,64,128]{3,2,1,0:T(8,128)(2,1)S(1)} %collective-permute-done.3.refs_6_.refs_1_, bf16[4,64,128]{2,1,0:T(8,128)(2,1)S(1)} %get-tuple-element.63.refs_2_, ...), custom_call_target="tpu_custom_call" | custom-call | flops 1024 | bytes 1024 | tf_op jit(solution)/shard_map/combine/pallas_call | solution.py:213
  (12 shorter events, 0.1 us)
Async XLA Ops:
  0.1 1.2 %copy-start = (bf16[1000,512]{1,0:T(8,128)(2,1)S(1)}, bf16[1000,512]{1,0:T(8,128)(2,1)}, u32[]{:S(2)}) copy-start(bf16[1000,512]{1,0:T(8,128)(2,1)} %c_ref.1) | copy-start | bytes 3072004
  16.4 14.0 %collective-permute-start = (bf16[16,256,128]{2,1,0:T(8,128)(2,1)S(1)}, bf16[16,256,128]{2,1,0:T(8,128)(2,1)S(1)}, u32[]{:S(2)}, u32[]{:S(2)}) collective-permute-start(bf16[16,256,128]{2,1,0:T(8,128)(2,1)S(1)} %get-tuple-element.52), channel_id=1, source_target_pairs={{0,1},{1,0},{2,3},{3,2},{4,5},{5,4},{6,7},{7,6},{8,9},{9,8},{10,11... | collective-permute-start | bytes 3145736 | tf_op jit(solution)/shard_map/ppermute | solution.py:230
  16.4 9.2 %collective-permute-start.1 = (bf16[4,256,128]{2,1,0:T(8,128)(2,1)S(1)}, bf16[4,256,128]{2,1,0:T(8,128)(2,1)S(1)}, u32[]{:S(2)}, u32[]{:S(2)}) collective-permute-start(bf16[4,256,128]{2,1,0:T(8,128)(2,1)S(1)} %get-tuple-element.53), channel_id=1, source_target_pairs={{0,2},{1,3},{2,0},{3,1},{4,6},{5,7},{6,4},{7,5},{8,10},{9,11},{10,... | collective-permute-start | bytes 786440 | tf_op jit(solution)/shard_map/ppermute | solution.py:230
  18.0 12.3 %collective-permute-start.2 = (bf16[4,256,128]{2,1,0:T(8,128)(2,1)S(1)}, bf16[4,256,128]{2,1,0:T(8,128)(2,1)S(1)}, u32[]{:S(2)}, u32[]{:S(2)}) collective-permute-start(bf16[4,256,128]{2,1,0:T(8,128)(2,1)S(1)} %get-tuple-element.54), channel_id=1, source_target_pairs={{0,3},{1,2},{2,1},{3,0},{4,7},{5,6},{6,5},{7,4},{8,11},{9,10},{10,... | collective-permute-start | bytes 786440 | tf_op jit(solution)/shard_map/ppermute | solution.py:230
  18.3 18.5 %collective-permute-start.4 = (bf16[4,256,128]{2,1,0:T(8,128)(2,1)S(1)}, bf16[4,256,128]{2,1,0:T(8,128)(2,1)S(1)}, u32[]{:S(2)}, u32[]{:S(2)}) collective-permute-start(bf16[4,256,128]{2,1,0:T(8,128)(2,1)S(1)} %get-tuple-element.59), channel_id=1, source_target_pairs={{0,2},{1,3},{2,0},{3,1},{4,6},{5,7},{6,4},{7,5},{8,10},{9,11},{10,... | collective-permute-start | bytes 786440 | tf_op jit(solution)/shard_map/ppermute | solution.py:230
  31.7 71.6 %copy-start.1 = (s32[128]{0:T(128)S(1)}, s32[128]{0:T(128)}, u32[]{:S(2)}) copy-start(s32[128]{0:T(128)} %mirror_ref.1) | copy-start | bytes 1540
  31.7 9.9 %collective-permute-start.5 = (bf16[4,256,128]{2,1,0:T(8,128)(2,1)S(1)}, bf16[4,256,128]{2,1,0:T(8,128)(2,1)S(1)}, u32[]{:S(2)}, u32[]{:S(2)}) collective-permute-start(bf16[4,256,128]{2,1,0:T(8,128)(2,1)S(1)} %get-tuple-element.60), channel_id=1, source_target_pairs={{0,3},{1,2},{2,1},{3,0},{4,7},{5,6},{6,5},{7,4},{8,11},{9,10},{10,... | collective-permute-start | bytes 786440 | tf_op jit(solution)/shard_map/ppermute | solution.py:230
  33.6 12.0 %collective-permute-start.3 = (bf16[4,4,64,128]{3,2,1,0:T(8,128)(2,1)S(1)}, bf16[4,4,64,128]{3,2,1,0:T(8,128)(2,1)S(1)}, u32[]{:S(2)}, u32[]{:S(2)}) collective-permute-start(bf16[4,4,64,128]{3,2,1,0:T(8,128)(2,1)S(1)} %get-tuple-element.58), channel_id=1, source_target_pairs={{0,16},{4,20},{8,24},{12,28},{16,0},{20,4},{24,8},{28,12},{1,17},{... | collective-permute-start | bytes 786440 | tf_op jit(solution)/shard_map/ppermute | solution.py:230
  34.0 14.1 %collective-permute-start.7 = (bf16[4,256,128]{2,1,0:T(8,128)(2,1)S(1)}, bf16[4,256,128]{2,1,0:T(8,128)(2,1)S(1)}, u32[]{:S(2)}, u32[]{:S(2)}) collective-permute-start(bf16[4,256,128]{2,1,0:T(8,128)(2,1)S(1)} %get-tuple-element.65), channel_id=1, source_target_pairs={{0,2},{1,3},{2,0},{3,1},{4,6},{5,7},{6,4},{7,5},{8,10},{9,11},{10,... | collective-permute-start | bytes 786440 | tf_op jit(solution)/shard_map/ppermute | solution.py:230
  42.9 9.9 %collective-permute-start.8 = (bf16[4,256,128]{2,1,0:T(8,128)(2,1)S(1)}, bf16[4,256,128]{2,1,0:T(8,128)(2,1)S(1)}, u32[]{:S(2)}, u32[]{:S(2)}) collective-permute-start(bf16[4,256,128]{2,1,0:T(8,128)(2,1)S(1)} %get-tuple-element.66), channel_id=1, source_target_pairs={{0,3},{1,2},{2,1},{3,0},{4,7},{5,6},{6,5},{7,4},{8,11},{9,10},{10,... | collective-permute-start | bytes 786440 | tf_op jit(solution)/shard_map/ppermute | solution.py:230
  44.8 11.9 %collective-permute-start.6 = (bf16[4,4,64,128]{3,2,1,0:T(8,128)(2,1)S(1)}, bf16[4,4,64,128]{3,2,1,0:T(8,128)(2,1)S(1)}, u32[]{:S(2)}, u32[]{:S(2)}) collective-permute-start(bf16[4,4,64,128]{3,2,1,0:T(8,128)(2,1)S(1)} %get-tuple-element.64), channel_id=1, source_target_pairs={{0,16},{4,20},{8,24},{12,28},{16,0},{20,4},{24,8},{28,12},{1,17},{... | collective-permute-start | bytes 786440 | tf_op jit(solution)/shard_map/ppermute | solution.py:230
  45.5 17.0 %collective-permute-start.10 = (bf16[4,256,128]{2,1,0:T(8,128)(2,1)S(1)}, bf16[4,256,128]{2,1,0:T(8,128)(2,1)S(1)}, u32[]{:S(2)}, u32[]{:S(2)}) collective-permute-start(bf16[4,256,128]{2,1,0:T(8,128)(2,1)S(1)} %get-tuple-element.70), channel_id=1, source_target_pairs={{0,2},{1,3},{2,0},{3,1},{4,6},{5,7},{6,4},{7,5},{8,10},{9,11},{10,... | collective-permute-start | bytes 786440 | tf_op jit(solution)/shard_map/ppermute | solution.py:230
  54.1 9.9 %collective-permute-start.11 = (bf16[4,256,128]{2,1,0:T(8,128)(2,1)S(1)}, bf16[4,256,128]{2,1,0:T(8,128)(2,1)S(1)}, u32[]{:S(2)}, u32[]{:S(2)}) collective-permute-start(bf16[4,256,128]{2,1,0:T(8,128)(2,1)S(1)} %get-tuple-element.71), channel_id=1, source_target_pairs={{0,3},{1,2},{2,1},{3,0},{4,7},{5,6},{6,5},{7,4},{8,11},{9,10},{10,... | collective-permute-start | bytes 786440 | tf_op jit(solution)/shard_map/ppermute | solution.py:230
  56.1 12.7 %collective-permute-start.9 = (bf16[4,4,64,128]{3,2,1,0:T(8,128)(2,1)S(1)}, bf16[4,4,64,128]{3,2,1,0:T(8,128)(2,1)S(1)}, u32[]{:S(2)}, u32[]{:S(2)}) collective-permute-start(bf16[4,4,64,128]{3,2,1,0:T(8,128)(2,1)S(1)} %get-tuple-element.69), channel_id=1, source_target_pairs={{0,16},{4,20},{8,24},{12,28},{16,0},{20,4},{24,8},{28,12},{1,17},{... | collective-permute-start | bytes 786440 | tf_op jit(solution)/shard_map/ppermute | solution.py:230
  56.7 12.0 %collective-permute-start.13 = (bf16[16,64,128]{2,1,0:T(8,128)(2,1)S(1)}, bf16[16,64,128]{2,1,0:T(8,128)(2,1)S(1)}, u32[]{:S(2)}, u32[]{:S(2)}) collective-permute-start(bf16[16,64,128]{2,1,0:T(8,128)(2,1)S(1)} %get-tuple-element.80), channel_id=1, source_target_pairs={{0,4},{4,0},{8,12},{12,8},{16,20},{20,16},{24,28},{28,24},{1,5},{5... | collective-permute-start | bytes 786440 | tf_op jit(solution)/shard_map/ppermute | solution.py:230
  58.3 21.7 %collective-permute-start.14 = (bf16[16,64,128]{2,1,0:T(8,128)(2,1)S(1)}, bf16[16,64,128]{2,1,0:T(8,128)(2,1)S(1)}, u32[]{:S(2)}, u32[]{:S(2)}) collective-permute-start(bf16[16,64,128]{2,1,0:T(8,128)(2,1)S(1)} %get-tuple-element.81), channel_id=1, source_target_pairs={{0,8},{4,12},{8,0},{12,4},{16,24},{20,28},{24,16},{28,20},{1,9},{5... | collective-permute-start | bytes 786440 | tf_op jit(solution)/shard_map/ppermute | solution.py:230
  62.5 22.2 %collective-permute-start.15 = (bf16[16,64,128]{2,1,0:T(8,128)(2,1)S(1)}, bf16[16,64,128]{2,1,0:T(8,128)(2,1)S(1)}, u32[]{:S(2)}, u32[]{:S(2)}) collective-permute-start(bf16[16,64,128]{2,1,0:T(8,128)(2,1)S(1)} %get-tuple-element.82), channel_id=1, source_target_pairs={{0,12},{4,8},{8,4},{12,0},{16,28},{20,24},{24,20},{28,16},{1,13},{... | collective-permute-start | bytes 786440 | tf_op jit(solution)/shard_map/ppermute | solution.py:230
  65.4 29.2 %collective-permute-start.12 = (bf16[4,4,64,128]{3,2,1,0:T(8,128)(2,1)S(1)}, bf16[4,4,64,128]{3,2,1,0:T(8,128)(2,1)S(1)}, u32[]{:S(2)}, u32[]{:S(2)}) collective-permute-start(bf16[4,4,64,128]{3,2,1,0:T(8,128)(2,1)S(1)} %get-tuple-element.73), channel_id=1, source_target_pairs={{0,16},{4,20},{8,24},{12,28},{16,0},{20,4},{24,8},{28,12},{1,17},{... | collective-permute-start | bytes 786440 | tf_op jit(solution)/shard_map/ppermute | solution.py:230
  84.7 5.0 %collective-permute-start.16 = (bf16[8,64,128]{2,1,0:T(8,128)(2,1)S(1)}, bf16[8,64,128]{2,1,0:T(8,128)(2,1)S(1)}, u32[]{:S(2)}, u32[]{:S(2)}) collective-permute-start(bf16[8,64,128]{2,1,0:T(8,128)(2,1)S(1)} %get-tuple-element.86), channel_id=1, source_target_pairs={{0,4},{4,0},{8,12},{12,8},{16,20},{20,16},{24,28},{28,24},{1,5},{5... | collective-permute-start | bytes 393224 | tf_op jit(solution)/shard_map/ppermute | solution.py:230
  85.3 7.4 %collective-permute-start.17 = (bf16[8,64,128]{2,1,0:T(8,128)(2,1)S(1)}, bf16[8,64,128]{2,1,0:T(8,128)(2,1)S(1)}, u32[]{:S(2)}, u32[]{:S(2)}) collective-permute-start(bf16[8,64,128]{2,1,0:T(8,128)(2,1)S(1)} %get-tuple-element.87), channel_id=1, source_target_pairs={{0,8},{4,12},{8,0},{12,4},{16,24},{20,28},{24,16},{28,20},{1,9},{5... | collective-permute-start | bytes 393224 | tf_op jit(solution)/shard_map/ppermute | solution.py:230
  88.7 5.9 %collective-permute-start.18 = (bf16[8,64,128]{2,1,0:T(8,128)(2,1)S(1)}, bf16[8,64,128]{2,1,0:T(8,128)(2,1)S(1)}, u32[]{:S(2)}, u32[]{:S(2)}) collective-permute-start(bf16[8,64,128]{2,1,0:T(8,128)(2,1)S(1)} %get-tuple-element.88), channel_id=1, source_target_pairs={{0,12},{4,8},{8,4},{12,0},{16,28},{20,24},{24,20},{28,16},{1,13},{... | collective-permute-start | bytes 393224 | tf_op jit(solution)/shard_map/ppermute | solution.py:230
  94.6 6.3 %collective-permute-start.19 = (bf16[8,64,128]{2,1,0:T(8,128)(2,1)S(1)}, bf16[8,64,128]{2,1,0:T(8,128)(2,1)S(1)}, u32[]{:S(2)}, u32[]{:S(2)}) collective-permute-start(bf16[8,64,128]{2,1,0:T(8,128)(2,1)S(1)} %get-tuple-element.92), channel_id=1, source_target_pairs={{0,4},{4,0},{8,12},{12,8},{16,20},{20,16},{24,28},{28,24},{1,5},{5... | collective-permute-start | bytes 393224 | tf_op jit(solution)/shard_map/ppermute | solution.py:230
  95.7 5.3 %collective-permute-start.20 = (bf16[8,64,128]{2,1,0:T(8,128)(2,1)S(1)}, bf16[8,64,128]{2,1,0:T(8,128)(2,1)S(1)}, u32[]{:S(2)}, u32[]{:S(2)}) collective-permute-start(bf16[8,64,128]{2,1,0:T(8,128)(2,1)S(1)} %get-tuple-element.93), channel_id=1, source_target_pairs={{0,8},{4,12},{8,0},{12,4},{16,24},{20,28},{24,16},{28,20},{1,9},{5... | collective-permute-start | bytes 393224 | tf_op jit(solution)/shard_map/ppermute | solution.py:230
  97.4 5.9 %collective-permute-start.21 = (bf16[8,64,128]{2,1,0:T(8,128)(2,1)S(1)}, bf16[8,64,128]{2,1,0:T(8,128)(2,1)S(1)}, u32[]{:S(2)}, u32[]{:S(2)}) collective-permute-start(bf16[8,64,128]{2,1,0:T(8,128)(2,1)S(1)} %get-tuple-element.94), channel_id=1, source_target_pairs={{0,12},{4,8},{8,4},{12,0},{16,28},{20,24},{24,20},{28,16},{1,13},{... | collective-permute-start | bytes 393224 | tf_op jit(solution)/shard_map/ppermute | solution.py:230

commit v5 on v4

v5 whole, which is shorter than its diff:
```python
import functools

import jax
import jax.numpy as jnp
from jax import lax
from jax.experimental import pallas as pl
from jax.experimental.pallas import tpu as pltpu
from jax.sharding import PartitionSpec as P

LANES = 128
STEP = 64
CHUNKS = (4, 4, 4, 4)
PART = 256
ROWS_IN_TILE = 8
ALONG = 3
MIB = 1024 * 1024
COST = pl.CostEstimate(flops=1024, bytes_accessed=1024, transcendentals=0)
IN_VMEM = pl.BlockSpec(memory_space=pltpu.VMEM)
IN_SMEM = pl.BlockSpec(memory_space=pltpu.SMEM)
ANYWHERE = pl.BlockSpec(memory_space=pl.ANY)
IN_HBM = pl.BlockSpec(memory_space=pltpu.MemorySpace.HBM)


def quarter_kernel(rows, far, n_after, place_ref, x_ref, c_hbm, *refs):
    refs = refs[n_after:]
    outs, (acc, c_ref, held, c_sem, sems) = refs[:-5], refs[-5:]
    at = pl.program_id(0)
    step, k_all, depth = x_ref.shape
    padded = held.shape[2]
    across = ALONG * step + 1

    @pl.when(at == 0)
    def _():
        first = pl.multiple_of(((place_ref[0] >> 1) ^ far) * 2 * LANES, 2 * LANES)
        copy = pltpu.make_async_copy(c_hbm.at[:, pl.ds(first, 2 * LANES)], c_ref, c_sem)
        copy.start()
        copy.wait()

    many = PART // k_all
    for r in range(0, step, many):
        x = x_ref[r : r + many].reshape(PART, depth)
        product = jnp.dot(x, c_ref[...], preferred_element_type=jnp.float32)
        for n in range(many):
            for k in range(0, k_all, ROWS_IN_TILE):
                line = n * k_all + k
                rows_at = pl.ds(k * across + (r + n) * ALONG, ROWS_IN_TILE, stride=across)
                for d in range(2):
                    acc[d, rows_at, :] = product[line : line + ROWS_IN_TILE, d * LANES : (d + 1) * LANES]
    here = pl.ds(pl.multiple_of(at * step, step), step)
    keep = lax.broadcasted_iota(jnp.int32, (step, LANES), 0) < rows - at * step
    first = 0
    for n, out in enumerate(outs):
        d = (place_ref[0] & 1) ^ (n & 1)
        kc = out.shape[0]
        for k in range(first, first + kc):
            block = acc[d, pl.ds(k * across, step, stride=ALONG), :]
            held[n & 1, k, here] = jnp.where(keep, block, 0.0).astype(jnp.bfloat16)
        mine = held.at[n & 1, pl.ds(first, kc)]
        pltpu.make_async_copy(mine.at[:, here], out.at[:, here], sems.at[n]).start()
        if n & 1:
            first += kc

    @pl.when(at == padded // step - 1)
    def _():
        first = 0
        for n, out in enumerate(outs):
            kc = out.shape[0]
            pltpu.make_async_copy(held.at[n & 1, pl.ds(first, kc)], out, sems.at[n]).wait()
            if n & 1:
                first += kc


def quarter_of(place, by_r, coeffs, far, padded, chunks, after=()):
    rows, k_all, depth = by_r.shape
    outs = [jax.ShapeDtypeStruct((kc, padded, LANES), jnp.bfloat16) for kc in chunks for _ in range(2)]
    out = pl.pallas_call(
        functools.partial(quarter_kernel, rows, far, len(after)),
        grid_spec=pltpu.PrefetchScalarGridSpec(
            num_scalar_prefetch=1,
            grid=(padded // STEP,),
            in_specs=[pl.BlockSpec((STEP, k_all, depth), lambda r, place: (r, 0, 0))]
            + [IN_HBM]
            + [ANYWHERE] * len(after),
            out_specs=[IN_HBM] * len(outs),
            scratch_shapes=[
                pltpu.VMEM((2, (ALONG * STEP + 1) * k_all, LANES), jnp.float32),
                pltpu.VMEM((depth, 2 * LANES), jnp.bfloat16),
                pltpu.VMEM((2, k_all, padded, LANES), jnp.bfloat16),
                pltpu.SemaphoreType.DMA,
                pltpu.SemaphoreType.DMA((len(outs),)),
            ],
        ),
        out_shape=outs,
        compiler_params=pltpu.CompilerParams(vmem_limit_bytes=50 * MIB),
        cost_estimate=COST,
        name=f"quarter{far}",
    )(place, by_r, coeffs, *after)
    return list(out)


def turn_kernel(rows, c_ref, out_ref):
    n_mo, orbitals, padded = out_ref.shape
    none = jnp.zeros((padded - rows, orbitals), jnp.float32)
    for n in range(n_mo):
        part = c_ref[n * rows : (n + 1) * rows, :].astype(jnp.float32)
        out_ref[n] = jnp.concatenate([part, none], axis=0).T.astype(jnp.bfloat16)


def turn(coeffs, n_mo, padded):
    depth, orbitals = coeffs.shape
    return pl.pallas_call(
        functools.partial(turn_kernel, depth // n_mo),
        in_specs=[IN_VMEM],
        out_specs=IN_VMEM,
        out_shape=jax.ShapeDtypeStruct((n_mo, orbitals, padded), jnp.bfloat16),
        compiler_params=pltpu.CompilerParams(vmem_limit_bytes=24 * MIB),
        cost_estimate=COST,
        name="turn",
    )(coeffs)


def half_kernel(n_mo, place_ref, *refs):
    blocks, t_ref, (keep, send, held) = refs[:n_mo], refs[n_mo], refs[-3:]
    _, near, kc, block, lanes = keep.shape
    for k in range(0, kc, 2):
        half = None
        for o, a_ref in enumerate(blocks):
            columns = jnp.concatenate([a_ref[k], a_ref[k + 1]], axis=1)
            part = jnp.dot(t_ref[place_ref[0] ^ o], columns, preferred_element_type=jnp.float32)
            half = part if half is None else half + part
        held[...] = half
        for o in range(2 * near):
            start = pl.multiple_of((place_ref[1] ^ o) * block, block)
            for n in range(2):
                piece = held[pl.ds(start, block), n * lanes : (n + 1) * lanes].astype(jnp.bfloat16)
                if o < near:
                    keep[0, o, k + n] = piece
                else:
                    send[0, o - near, k + n] = piece


def half_of(place, blocks, turned, n_pair, after):
    n_mo, orbitals, _ = turned.shape
    kc, _, lanes = blocks[0].shape
    block, near = orbitals // n_pair, n_pair // 2
    return pl.pallas_call(
        functools.partial(half_kernel, n_mo),
        in_specs=[IN_SMEM] + [IN_VMEM] * (n_mo + 1) + [ANYWHERE] * len(after),
        out_specs=[IN_VMEM] * 2,
        out_shape=[jax.ShapeDtypeStruct((1, near, kc, block, lanes), jnp.bfloat16)] * 2,
        scratch_shapes=[pltpu.VMEM((orbitals, 2 * lanes), jnp.float32)],
        compiler_params=pltpu.CompilerParams(vmem_limit_bytes=24 * MIB),
        cost_estimate=COST,
        name="half",
    )(place, *blocks, turned, *after)


def merge_kernel(n, flip, *refs):
    at = 0
    for x in refs[:n]:
        for i in range(x.shape[0]):
            refs[-1][at] = x[i, flip : 2 * flip]
            at += 1


def merge(parts, flip, after):
    shape = (sum(x.shape[0] for x in parts), flip, *parts[0].shape[2:])
    return pl.pallas_call(
        functools.partial(merge_kernel, len(parts), flip),
        in_specs=[IN_VMEM] * len(parts) + [ANYWHERE] * len(after),
        out_specs=IN_VMEM,
        out_shape=jax.ShapeDtypeStruct(shape, jnp.bfloat16),
        compiler_params=pltpu.CompilerParams(vmem_limit_bytes=24 * MIB),
        cost_estimate=COST,
        name=f"merge{flip}",
    )(*parts, *after)


def combine_kernel(sources, per_step, mirror_ref, place_ref, *refs):
    pieces, out_ref, held = refs[:-2], refs[-2], refs[-1]
    step = pl.program_id(0)

    @pl.when(step == 0)
    def _():
        for piece, (offsets, first) in zip(pieces, sources):
            for n, offset in enumerate(offsets):
                held[place_ref[1] ^ offset, first : first + piece.shape[2]] = piece[n, 0]

    k_all = held.shape[1]
    for n in range(per_step):
        k = step * per_step + n
        m = mirror_ref[k]
        own = held[k // k_all, lax.rem(k, k_all)].astype(jnp.float32)
        partner = held[m // k_all, lax.rem(m, k_all)].astype(jnp.float32)
        out_ref[n] = 0.5 * (own + partner)


def combine(pieces, sources, mirror, place, n_pair):
    block, lanes = pieces[0].shape[-2:]
    k_all = sum(CHUNKS)
    rows = n_pair * k_all
    per_step = max(1, 32 * 64 // block)
    return pl.pallas_call(
        functools.partial(combine_kernel, sources, per_step),
        grid_spec=pltpu.PrefetchScalarGridSpec(
            num_scalar_prefetch=2,
            grid=(rows // per_step,),
            in_specs=[IN_VMEM] * len(pieces),
            out_specs=pl.BlockSpec((per_step, block, lanes), lambda k, m, place: (k, 0, 0)),
            scratch_shapes=[pltpu.VMEM((n_pair, k_all, block, lanes), jnp.bfloat16)],
        ),
        out_shape=jax.ShapeDtypeStruct((rows, block, lanes), jnp.float32),
        compiler_params=pltpu.CompilerParams(vmem_limit_bytes=24 * MIB),
        cost_estimate=COST,
        name="combine",
    )(mirror, place, *pieces)


def flipped(x, axis, size, offset, name):
    with jax.named_scope(name):
        return lax.ppermute(x, axis, [(i, i ^ offset) for i in range(size)])


def on_device(n_pair, n_mo, integrals, coeffs, mirror):
    rows = integrals.shape[1]
    padded = -(-rows // STEP) * STEP
    n_near = n_pair // 2
    by_r = jnp.transpose(integrals, (1, 0, 2))
    place = jnp.stack([lax.axis_index("mo"), lax.axis_index("pair")]).astype(jnp.int32)
    turned = turn(coeffs, n_mo, padded)
    queue = quarter_of(place, by_r, coeffs, 1, padded, CHUNKS)
    arrived = [flipped(x, "mo", n_mo, 2 + (m & 1), f"y{m}") for m, x in enumerate(queue)]
    near = quarter_of(place, by_r, coeffs, 0, padded, CHUNKS, queue[:1])
    beside = [flipped(x, "mo", n_mo, 1, f"beside{c}") for c, x in enumerate(near[1::2])]

    n_chunks = len(CHUNKS)
    firsts = [sum(CHUNKS[:c]) for c in range(n_chunks)]
    flips = [1 << n for n in reversed(range(n_pair.bit_length() - 1))]
    parts, offsets, halves, messages = [], [], [], [[] for _ in flips]
    for t in range(n_chunks + len(flips)):
        for level, flip in enumerate(flips):
            c = t - level
            if not 0 <= c < n_chunks:
                continue
            if level == 0:
                blocks = [near[2 * c], beside[c], *arrived[2 * c : 2 * c + 2]]
                after = [m[-1] for m in messages[1:] if m]
                keep, message = half_of(place, blocks, turned, n_pair, after)
                parts.append([keep])
                offsets.append([[0]])
            else:
                after = [messages[level - 1][-1]] if c + 1 < n_chunks else []
                if flip == 1 and c:
                    after.append(parts[c - 1][-1])
                message = merge(parts[c], flip, after)
            messages[level].append(message)
            offsets[c].append([o ^ flip for group in offsets[c] for o in group])
            parts[c].append(flipped(message, "pair", n_pair, flip, f"z{flip}c{c}"))
    pieces = [x for chunk in parts for x in chunk]
    sources = [(tuple(group), first) for chunk, first in zip(offsets, firsts) for group in chunk]
    return combine(pieces, sources, mirror, place, n_pair)


def solution(mesh):
    return jax.shard_map(
        functools.partial(on_device, mesh.shape["pair"], mesh.shape["mo"]),
        mesh=mesh,
        in_specs=(P("pair", "mo", None), P(), P()),
        out_specs=P(None, "pair", "mo"),
        check_vma=False,
    )
```

time: 107 us -> 100 us (0.935)
  the two profiles are of different devices: /device:TPU:16 before, /device:TPU:0 now
where the time goes in v5:
time: 100 us; the launch traced here: 99.8 us
  waiting for transfers between devices  41.9 us (42%)
  starting transfers between devices  32.5 us (32%)
  Pallas kernels  23.9 us (24%)
  local copies, waits for them, and re-layouts  1.22 us (1%)
    ppermute x24, waiting for transfers between devices, flipped(): return lax.ppermute(x, axis, [(i, i ^ offset) for i in range(size)])  41.9 us
    ppermute x24, starting transfers between devices, flipped(): return lax.ppermute(x, axis, [(i, i ^ offset) for i in range(size)])  32.5 us
    pallas_call x2, Pallas kernels, quarter_of(): pl.pallas_call(functools.partial(quarter_kernel, rows, far, len(after)),...  14.2 us
    pallas_call x4, Pallas kernels, half_of(): pl.pallas_call(functools.partial(half_kernel, n_mo), in_specs=[IN_SMEM] +...  5.37 us
    pallas_call x1, Pallas kernels, combine(): pl.pallas_call(functools.partial(combine_kernel, sources, per_step), grid...  3.79 us
  transfers between devices with their start and end apart: 24, of which 12 were waited for; matrix products, arithmetic and copies ran while one was open for 0% of the time, Pallas kernels for 13%

profile of v5, /device:TPU:0, one launch (start us, length us, event | category | flops | bytes accessed | tf_op | source)
XLA Modules:
  0.0 99.8 jit_solution(7371885102346785984)
XLA Ops:
  0.0 0.1 pad_add_fusion.place_ref
  0.1 1.2 %copy-done = bf16[1000,512]{1,0:T(8,128)(2,1)S(1)} copy-done((bf16[1000,512]{1,0:T(8,128)(2,1)S(1)}, bf16[1000,512]{1,0:T(8,128)(2,1)}, u32[]{:S(2)}) %copy-start) | copy-done | bytes 1024024
  1.3 7.1 %quarter1.1 = (bf16[4,256,128]{2,1,0:T(8,128)(2,1)S(1)}, bf16[4,256,128]{2,1,0:T(8,128)(2,1)S(1)}, bf16[4,256,128]{2,1,0:T(8,128)(2,1)S(1)}, bf16[4,256,128]{2,1...) custom-call(s32[2]{0:T(128)S(1)} %pad_add_fusion.place_ref, ...), custom_call_target="tpu_custom_call" | custom-call | flops 1024 | bytes 1024 | tf_op jit(solution)/shard_map/quarter1/pallas_call | solution.py:76
  8.4 2.5 %collective-permute-start.2 = (bf16[4,256,128]{2,1,0:T(8,128)(2,1)S(1)}, bf16[4,256,128]{2,1,0:T(8,128)(2,1)S(1)}, u32[]{:S(2)}, u32[]{:S(2)}) collective-permute-start(bf16[4,256,128]{2,1,0:T(8,128)(2,1)S(1)} %get-tuple-element.32), channel_id=1, source_target_pairs={{0,3},{1,2},{2,1},{3,0},{4,7},{5,6},{6,5},{7,4},{8,11},{9,10},{10,... | collective-permute-start | bytes 786440 | tf_op jit(solution)/shard_map/y1/ppermute | solution.py:221
  10.9 0.6 collective-permute-start.1
  11.5 7.1 %quarter0.1 = (bf16[4,256,128]{2,1,0:T(8,128)(2,1)S(1)}, bf16[4,256,128]{2,1,0:T(8,128)(2,1)S(1)}, bf16[4,256,128]{2,1,0:T(8,128)(2,1)S(1)}, bf16[4,256,128]{2,1...) custom-call(s32[2]{0:T(128)S(1)} %pad_add_fusion.place_ref, ...), custom_call_target="tpu_custom_call" | custom-call | flops 1024 | bytes 1024 | tf_op jit(solution)/shard_map/quarter0/pallas_call | solution.py:76
  18.6 0.1 collective-permute-start
  18.7 1.7 %collective-permute-start.5 = (bf16[4,256,128]{2,1,0:T(8,128)(2,1)S(1)}, bf16[4,256,128]{2,1,0:T(8,128)(2,1)S(1)}, u32[]{:S(2)}, u32[]{:S(2)}) collective-permute-start(bf16[4,256,128]{2,1,0:T(8,128)(2,1)S(1)} %get-tuple-element.37), channel_id=1, source_target_pairs={{0,2},{1,3},{2,0},{3,1},{4,6},{5,7},{6,4},{7,5},{8,10},{9,11},{10,... | collective-permute-start | bytes 786440 | tf_op jit(solution)/shard_map/y2/ppermute | solution.py:221
  20.5 0.1 collective-permute-start.6
  20.5 0.4 turn.1.refs_4_
  20.9 0.0 collective-permute-done.2.refs_3_
  21.0 0.4 collective-permute-start.4
  21.4 2.8 %collective-permute-done.1.refs_2_ = bf16[4,256,128]{2,1,0:T(8,128)(2,1)S(1)} collective-permute-done((bf16[4,256,128]{2,1,0:T(8,128)(2,1)S(1)}, bf16[4,256,128]{2,1,0:T(8,128)(2,1)S(1)}, u32[]{:S(2)}, u32[]{:S(2)}) %collective-permute-start.1) | collective-permute-done | bytes 262176 | tf_op jit(solution)/shard_map/y0/ppermute | solution.py:221
  24.2 0.0 collective-permute-done.refs_1_
  24.2 1.4 %half.4 = (bf16[1,4,4,64,128]{4,3,2,1,0:T(8,128)(2,1)S(1)}, bf16[1,4,4,64,128]{4,3,2,1,0:T(8,128)(2,1)S(1)}) custom-call(s32[2]{0:T(128)S(1)} %pad_add_fusion.place_ref, bf16[4,256,128]{2,1,0:T(8,128)(2,1)S(1)} %get-tuple-element.30.refs_0_, bf16[4,256,128]{2,1,0:T(8,128)(2,1)S(1)} %collective-permute-done.refs_1_, ...), custom_call_target="tpu_custom_call" | custom-call | flops 1024 | bytes 1024 | tf_op jit(solution)/shard_map/half/pallas_call | solution.py:146
  25.5 2.7 %collective-permute-start.3 = (bf16[1,4,4,64,128]{4,3,2,1,0:T(8,128)(2,1)S(1)}, bf16[1,4,4,64,128]{4,3,2,1,0:T(8,128)(2,1)S(1)}, u32[]{:S(2)}, u32[]{:S(2)}) collective-permute-start(bf16[1,4,4,64,128]{4,3,2,1,0:T(8,128)(2,1)S(1)} %get-tuple-element.34), channel_id=1, source_target_pairs={{0,16},{4,20},{8,24},{12,28},{16,0},{20,4},{24,8},{28,12},{1,17},{... | collective-permute-start | bytes 786440 | tf_op jit(solution)/shard_map/z4c0/ppermute | solution.py:221
  28.2 1.5 %collective-permute-start.10 = (bf16[4,256,128]{2,1,0:T(8,128)(2,1)S(1)}, bf16[4,256,128]{2,1,0:T(8,128)(2,1)S(1)}, u32[]{:S(2)}, u32[]{:S(2)}) collective-permute-start(bf16[4,256,128]{2,1,0:T(8,128)(2,1)S(1)} %get-tuple-element.43), channel_id=1, source_target_pairs={{0,2},{1,3},{2,0},{3,1},{4,6},{5,7},{6,4},{7,5},{8,10},{9,11},{10,... | collective-permute-start | bytes 786440 | tf_op jit(solution)/shard_map/y4/ppermute | solution.py:221
  29.7 0.1 collective-permute-done.5.refs_2_
  29.8 1.2 %collective-permute-start.11 = (bf16[4,256,128]{2,1,0:T(8,128)(2,1)S(1)}, bf16[4,256,128]{2,1,0:T(8,128)(2,1)S(1)}, u32[]{:S(2)}, u32[]{:S(2)}) collective-permute-start(bf16[4,256,128]{2,1,0:T(8,128)(2,1)S(1)} %get-tuple-element.44), channel_id=1, source_target_pairs={{0,3},{1,2},{2,1},{3,0},{4,7},{5,6},{6,5},{7,4},{8,11},{9,10},{10,... | collective-permute-start | bytes 786440 | tf_op jit(solution)/shard_map/y5/ppermute | solution.py:221
  31.0 3.4 %collective-permute-done.6.refs_3_ = bf16[4,256,128]{2,1,0:T(8,128)(2,1)S(1)} collective-permute-done((bf16[4,256,128]{2,1,0:T(8,128)(2,1)S(1)}, bf16[4,256,128]{2,1,0:T(8,128)(2,1)S(1)}, u32[]{:S(2)}, u32[]{:S(2)}) %collective-permute-start.6) | collective-permute-done | bytes 262176 | tf_op jit(solution)/shard_map/y3/ppermute | solution.py:221
  34.4 1.1 %collective-permute-start.9 = (bf16[4,256,128]{2,1,0:T(8,128)(2,1)S(1)}, bf16[4,256,128]{2,1,0:T(8,128)(2,1)S(1)}, u32[]{:S(2)}, u32[]{:S(2)}) collective-permute-start(bf16[4,256,128]{2,1,0:T(8,128)(2,1)S(1)} %get-tuple-element.42), channel_id=1, source_target_pairs={{0,1},{1,0},{2,3},{3,2},{4,5},{5,4},{6,7},{7,6},{8,9},{9,8},{10,11... | collective-permute-start | bytes 786440 | tf_op jit(solution)/shard_map/beside2/ppermute | solution.py:221
  35.5 1.3 %half.5 = (bf16[1,4,4,64,128]{4,3,2,1,0:T(8,128)(2,1)S(1)}, bf16[1,4,4,64,128]{4,3,2,1,0:T(8,128)(2,1)S(1)}) custom-call(s32[2]{0:T(128)S(1)} %pad_add_fusion.place_ref, bf16[4,256,128]{2,1,0:T(8,128)(2,1)S(1)} %get-tuple-element.35.refs_0_, bf16[4,256,128]{2,1,0:T(8,128)(2,1)S(1)} %collective-permute-done.4.refs_1_, ...), custom_call_target="tpu_custom_call" | custom-call | flops 1024 | bytes 1024 | tf_op jit(solution)/shard_map/half/pallas_call | solution.py:146
  36.9 2.6 %collective-permute-start.8 = (bf16[1,4,4,64,128]{4,3,2,1,0:T(8,128)(2,1)S(1)}, bf16[1,4,4,64,128]{4,3,2,1,0:T(8,128)(2,1)S(1)}, u32[]{:S(2)}, u32[]{:S(2)}) collective-permute-start(bf16[1,4,4,64,128]{4,3,2,1,0:T(8,128)(2,1)S(1)} %get-tuple-element.39.refs_2_), channel_id=1, source_target_pairs={{0,16},{4,20},{8,24},{12,28},{16,0},{20,4},{24,8},{28,12},{1,17},{... | collective-permute-start | bytes 786440 | tf_op jit(solution)/shard_map/z4c1/ppermute | solution.py:221
  39.4 0.8 collective-permute-done.3.refs_1_
  40.3 0.9 collective-permute-start.7
  41.2 1.5 %collective-permute-start.16 = (bf16[4,256,128]{2,1,0:T(8,128)(2,1)S(1)}, bf16[4,256,128]{2,1,0:T(8,128)(2,1)S(1)}, u32[]{:S(2)}, u32[]{:S(2)}) collective-permute-start(bf16[4,256,128]{2,1,0:T(8,128)(2,1)S(1)} %get-tuple-element.49), channel_id=1, source_target_pairs={{0,2},{1,3},{2,0},{3,1},{4,6},{5,7},{6,4},{7,5},{8,10},{9,11},{10,... | collective-permute-start | bytes 786440 | tf_op jit(solution)/shard_map/y6/ppermute | solution.py:221
  42.7 3.0 %collective-permute-done.11.refs_3_ = bf16[4,256,128]{2,1,0:T(8,128)(2,1)S(1)} collective-permute-done((bf16[4,256,128]{2,1,0:T(8,128)(2,1)S(1)}, bf16[4,256,128]{2,1,0:T(8,128)(2,1)S(1)}, u32[]{:S(2)}, u32[]{:S(2)}) %collective-permute-start.11) | collective-permute-done | bytes 262176 | tf_op jit(solution)/shard_map/y5/ppermute | solution.py:221
  45.7 2.2 %collective-permute-start.17 = (bf16[4,256,128]{2,1,0:T(8,128)(2,1)S(1)}, bf16[4,256,128]{2,1,0:T(8,128)(2,1)S(1)}, u32[]{:S(2)}, u32[]{:S(2)}) collective-permute-start(bf16[4,256,128]{2,1,0:T(8,128)(2,1)S(1)} %get-tuple-element.50), channel_id=1, source_target_pairs={{0,3},{1,2},{2,1},{3,0},{4,7},{5,6},{6,5},{7,4},{8,11},{9,10},{10,... | collective-permute-start | bytes 786440 | tf_op jit(solution)/shard_map/y7/ppermute | solution.py:221
  47.9 0.4 collective-permute-start.15
  48.2 1.3 %half.6 = (bf16[1,4,4,64,128]{4,3,2,1,0:T(8,128)(2,1)S(1)}, bf16[1,4,4,64,128]{4,3,2,1,0:T(8,128)(2,1)S(1)}) custom-call(s32[2]{0:T(128)S(1)} %pad_add_fusion.place_ref, bf16[4,256,128]{2,1,0:T(8,128)(2,1)S(1)} %get-tuple-element.41.refs_0_, bf16[4,256,128]{2,1,0:T(8,128)(2,1)S(1)} %collective-permute-done.9.refs_1_, ...), custom_call_target="tpu_custom_call" | custom-call | flops 1024 | bytes 1024 | tf_op jit(solution)/shard_map/half/pallas_call | solution.py:146
  49.6 2.4 %collective-permute-done.8.refs_1_.refs_5_ = bf16[1,4,4,64,128]{4,3,2,1,0:T(8,128)(2,1)S(1)} collective-permute-done((bf16[1,4,4,64,128]{4,3,2,1,0:T(8,128)(2,1)S(1)}, bf16[1,4,4,64,128]{4,3,2,1,0:T(8,128)(2,1)S(1)}, u32[]{:S(2)}, u32[]{:S(2)}) %collective-permute-start.8) | collective-permute-done | bytes 262176 | tf_op jit(solution)/shard_map/z4c1/ppermute | solution.py:221
  52.0 0.2 collective-permute-start.14
  52.3 3.9 %collective-permute-start.13 = (bf16[2,2,4,64,128]{4,3,2,1,0:T(8,128)(2,1)S(1)}, bf16[2,2,4,64,128]{4,3,2,1,0:T(8,128)(2,1)S(1)}, u32[]{:S(2)}, u32[]{:S(2)}) collective-permute-start(bf16[2,2,4,64,128]{4,3,2,1,0:T(8,128)(2,1)S(1)} %merge2.5.refs_3_.refs_5_), channel_id=1, source_target_pairs={{0,8},{4,12},{8,0},{12,4},{16,24},{20,28},{24,16},{28,20},{1,9},{5... | collective-permute-start | bytes 786440 | tf_op jit(solution)/shard_map/z2c1/ppermute | solution.py:221
  56.2 1.6 %collective-permute-start.12 = (bf16[4,1,4,64,128]{4,3,2,1,0:T(8,128)(2,1)S(1)}, bf16[4,1,4,64,128]{4,3,2,1,0:T(8,128)(2,1)S(1)}, u32[]{:S(2)}, u32[]{:S(2)}) collective-permute-start(bf16[4,1,4,64,128]{4,3,2,1,0:T(8,128)(2,1)S(1)} %merge1.4.refs_6_), channel_id=1, source_target_pairs={{0,4},{4,0},{8,12},{12,8},{16,20},{20,16},{24,28},{28,24},{1,5},{5... | collective-permute-start | bytes 786440 | tf_op jit(solution)/shard_map/z1c0/ppermute | solution.py:221
  57.8 1.3 %half.7 = (bf16[1,4,4,64,128]{4,3,2,1,0:T(8,128)(2,1)S(1)}, bf16[1,4,4,64,128]{4,3,2,1,0:T(8,128)(2,1)S(1)}) custom-call(s32[2]{0:T(128)S(1)} %pad_add_fusion.place_ref, bf16[4,256,128]{2,1,0:T(8,128)(2,1)S(1)} %get-tuple-element.47.refs_0_, bf16[4,256,128]{2,1,0:T(8,128)(2,1)S(1)} %collective-permute-done.15.refs_1_, ...), custom_call_target="tpu_custom_call" | custom-call | flops 1024 | bytes 1024 | tf_op jit(solution)/shard_map/half/pallas_call | solution.py:146
  59.1 2.6 %collective-permute-start.20 = (bf16[1,4,4,64,128]{4,3,2,1,0:T(8,128)(2,1)S(1)}, bf16[1,4,4,64,128]{4,3,2,1,0:T(8,128)(2,1)S(1)}, u32[]{:S(2)}, u32[]{:S(2)}) collective-permute-start(bf16[1,4,4,64,128]{4,3,2,1,0:T(8,128)(2,1)S(1)} %get-tuple-element.51.refs_2_), channel_id=1, source_target_pairs={{0,16},{4,20},{8,24},{12,28},{16,0},{20,4},{24,8},{28,12},{1,17},{... | collective-permute-start | bytes 786440 | tf_op jit(solution)/shard_map/z4c3/ppermute | solution.py:221
  61.8 11.1 %collective-permute-done.14.refs_1_.refs_9_ = bf16[1,4,4,64,128]{4,3,2,1,0:T(8,128)(2,1)S(1)} collective-permute-done((bf16[1,4,4,64,128]{4,3,2,1,0:T(8,128)(2,1)S(1)}, bf16[1,4,4,64,128]{4,3,2,1,0:T(8,128)(2,1)S(1)}, u32[]{:S(2)}, u32[]{:S(2)}) %collective-permute-start.14) | collective-permute-done | bytes 262176 | tf_op jit(solution)/shard_map/z4c2/ppermute | solution.py:221
  72.9 0.1 collective-permute-start.19
  73.0 1.6 %collective-permute-start.18 = (bf16[4,1,4,64,128]{4,3,2,1,0:T(8,128)(2,1)S(1)}, bf16[4,1,4,64,128]{4,3,2,1,0:T(8,128)(2,1)S(1)}, u32[]{:S(2)}, u32[]{:S(2)}) collective-permute-start(bf16[4,1,4,64,128]{4,3,2,1,0:T(8,128)(2,1)S(1)} %merge1.5), channel_id=1, source_target_pairs={{0,4},{4,0},{8,12},{12,8},{16,20},{20,16},{24,28},{28,24},{1,5},{5... | collective-permute-start | bytes 786440 | tf_op jit(solution)/shard_map/z1c1/ppermute | solution.py:221
  74.6 2.8 %collective-permute-done.20.refs_1_.refs_13_ = bf16[1,4,4,64,128]{4,3,2,1,0:T(8,128)(2,1)S(1)} collective-permute-done((bf16[1,4,4,64,128]{4,3,2,1,0:T(8,128)(2,1)S(1)}, bf16[1,4,4,64,128]{4,3,2,1,0:T(8,128)(2,1)S(1)}, u32[]{:S(2)}, u32[]{:S(2)}) %collective-permute-start.20) | collective-permute-done | bytes 262176 | tf_op jit(solution)/shard_map/z4c3/ppermute | solution.py:221
  77.4 0.1 collective-permute-start.22
  77.5 4.3 %collective-permute-done.19.refs_2_.refs_10_ = bf16[2,2,4,64,128]{4,3,2,1,0:T(8,128)(2,1)S(1)} collective-permute-done((bf16[2,2,4,64,128]{4,3,2,1,0:T(8,128)(2,1)S(1)}, bf16[2,2,4,64,128]{4,3,2,1,0:T(8,128)(2,1)S(1)}, u32[]{:S(2)}, u32[]{:S(2)}) %collective-permute-start.19) | collective-permute-done | bytes 262176 | tf_op jit(solution)/shard_map/z2c2/ppermute | solution.py:221
  81.8 1.6 %collective-permute-start.21 = (bf16[4,1,4,64,128]{4,3,2,1,0:T(8,128)(2,1)S(1)}, bf16[4,1,4,64,128]{4,3,2,1,0:T(8,128)(2,1)S(1)}, u32[]{:S(2)}, u32[]{:S(2)}) collective-permute-start(bf16[4,1,4,64,128]{4,3,2,1,0:T(8,128)(2,1)S(1)} %merge1.6), channel_id=1, source_target_pairs={{0,4},{4,0},{8,12},{12,8},{16,20},{20,16},{24,28},{28,24},{1,5},{5... | collective-permute-start | bytes 786440 | tf_op jit(solution)/shard_map/z1c2/ppermute | solution.py:221
  83.4 2.4 %collective-permute-done.22.refs_2_.refs_14_ = bf16[2,2,4,64,128]{4,3,2,1,0:T(8,128)(2,1)S(1)} collective-permute-done((bf16[2,2,4,64,128]{4,3,2,1,0:T(8,128)(2,1)S(1)}, bf16[2,2,4,64,128]{4,3,2,1,0:T(8,128)(2,1)S(1)}, u32[]{:S(2)}, u32[]{:S(2)}) %collective-permute-start.22) | collective-permute-done | bytes 262176 | tf_op jit(solution)/shard_map/z2c3/ppermute | solution.py:221
  85.8 3.7 %collective-permute-done.21.refs_3_.refs_11_ = bf16[4,1,4,64,128]{4,3,2,1,0:T(8,128)(2,1)S(1)} collective-permute-done((bf16[4,1,4,64,128]{4,3,2,1,0:T(8,128)(2,1)S(1)}, bf16[4,1,4,64,128]{4,3,2,1,0:T(8,128)(2,1)S(1)}, u32[]{:S(2)}, u32[]{:S(2)}) %collective-permute-start.21) | collective-permute-done | bytes 262176 | tf_op jit(solution)/shard_map/z1c2/ppermute | solution.py:221
  89.5 1.5 %collective-permute-start.23 = (bf16[4,1,4,64,128]{4,3,2,1,0:T(8,128)(2,1)S(1)}, bf16[4,1,4,64,128]{4,3,2,1,0:T(8,128)(2,1)S(1)}, u32[]{:S(2)}, u32[]{:S(2)}) collective-permute-start(bf16[4,1,4,64,128]{4,3,2,1,0:T(8,128)(2,1)S(1)} %merge1.7), channel_id=1, source_target_pairs={{0,4},{4,0},{8,12},{12,8},{16,20},{20,16},{24,28},{28,24},{1,5},{5... | collective-permute-start | bytes 786440 | tf_op jit(solution)/shard_map/z1c3/ppermute | solution.py:221
  91.0 5.0 %collective-permute-done.23.refs_15_ = bf16[4,1,4,64,128]{4,3,2,1,0:T(8,128)(2,1)S(1)} collective-permute-done((bf16[4,1,4,64,128]{4,3,2,1,0:T(8,128)(2,1)S(1)}, bf16[4,1,4,64,128]{4,3,2,1,0:T(8,128)(2,1)S(1)}, u32[]{:S(2)}, u32[]{:S(2)}) %collective-permute-start.23) | collective-permute-done | bytes 262176 | tf_op jit(solution)/shard_map/z1c3/ppermute | solution.py:221
  96.0 3.8 %combine.1 = f32[128,64,128]{2,1,0:T(8,128)} custom-call(s32[128]{0:T(128)S(1)} %copy-done.1, s32[2]{0:T(128)S(1)} %pad_add_fusion.place_ref, bf16[1,4,4,64,128]{4,3,2,1,0:T(8,128)(2,1)S(1)} %get-tuple-element.33.refs_0_, bf16[1,4,4,64,128]{4,3,2,1,0:T(8,128)(2,1)S(1)} %collective-permute-done.3.refs_1_, ...), custom_call_target="tpu_custom_call" | custom-call | flops 1024 | bytes 1024 | tf_op jit(solution)/shard_map/combine/pallas_call | solution.py:203
  (21 shorter events, 0.2 us)
Async XLA Ops:
  0.1 1.2 %copy-start = (bf16[1000,512]{1,0:T(8,128)(2,1)S(1)}, bf16[1000,512]{1,0:T(8,128)(2,1)}, u32[]{:S(2)}) copy-start(bf16[1000,512]{1,0:T(8,128)(2,1)} %c_ref.1) | copy-start | bytes 3072004
  8.4 12.6 %collective-permute-start.2 = (bf16[4,256,128]{2,1,0:T(8,128)(2,1)S(1)}, bf16[4,256,128]{2,1,0:T(8,128)(2,1)S(1)}, u32[]{:S(2)}, u32[]{:S(2)}) collective-permute-start(bf16[4,256,128]{2,1,0:T(8,128)(2,1)S(1)} %get-tuple-element.32), channel_id=1, source_target_pairs={{0,3},{1,2},{2,1},{3,0},{4,7},{5,6},{6,5},{7,4},{8,11},{9,10},{10,... | collective-permute-start | bytes 786440 | tf_op jit(solution)/shard_map/y1/ppermute | solution.py:221
  10.9 13.3 %collective-permute-start.1 = (bf16[4,256,128]{2,1,0:T(8,128)(2,1)S(1)}, bf16[4,256,128]{2,1,0:T(8,128)(2,1)S(1)}, u32[]{:S(2)}, u32[]{:S(2)}) collective-permute-start(bf16[4,256,128]{2,1,0:T(8,128)(2,1)S(1)} %get-tuple-element.29.refs_0_), channel_id=1, source_target_pairs={{0,2},{1,3},{2,0},{3,1},{4,6},{5,7},{6,4},{7,5},{8,10},{9,11},{10,... | collective-permute-start | bytes 786440 | tf_op jit(solution)/shard_map/y0/ppermute | solution.py:221
  18.6 5.6 %collective-permute-start = (bf16[4,256,128]{2,1,0:T(8,128)(2,1)S(1)}, bf16[4,256,128]{2,1,0:T(8,128)(2,1)S(1)}, u32[]{:S(2)}, u32[]{:S(2)}) collective-permute-start(bf16[4,256,128]{2,1,0:T(8,128)(2,1)S(1)} %get-tuple-element.31), channel_id=1, source_target_pairs={{0,1},{1,0},{2,3},{3,2},{4,5},{5,4},{6,7},{7,6},{8,9},{9,8},{10,11... | collective-permute-start | bytes 786440 | tf_op jit(solution)/shard_map/beside0/ppermute | solution.py:221
  18.7 11.1 %collective-permute-start.5 = (bf16[4,256,128]{2,1,0:T(8,128)(2,1)S(1)}, bf16[4,256,128]{2,1,0:T(8,128)(2,1)S(1)}, u32[]{:S(2)}, u32[]{:S(2)}) collective-permute-start(bf16[4,256,128]{2,1,0:T(8,128)(2,1)S(1)} %get-tuple-element.37), channel_id=1, source_target_pairs={{0,2},{1,3},{2,0},{3,1},{4,6},{5,7},{6,4},{7,5},{8,10},{9,11},{10,... | collective-permute-start | bytes 786440 | tf_op jit(solution)/shard_map/y2/ppermute | solution.py:221
  20.5 14.0 %collective-permute-start.6 = (bf16[4,256,128]{2,1,0:T(8,128)(2,1)S(1)}, bf16[4,256,128]{2,1,0:T(8,128)(2,1)S(1)}, u32[]{:S(2)}, u32[]{:S(2)}) collective-permute-start(bf16[4,256,128]{2,1,0:T(8,128)(2,1)S(1)} %get-tuple-element.38), channel_id=1, source_target_pairs={{0,3},{1,2},{2,1},{3,0},{4,7},{5,6},{6,5},{7,4},{8,11},{9,10},{10,... | collective-permute-start | bytes 786440 | tf_op jit(solution)/shard_map/y3/ppermute | solution.py:221
  21.0 14.6 %collective-permute-start.4 = (bf16[4,256,128]{2,1,0:T(8,128)(2,1)S(1)}, bf16[4,256,128]{2,1,0:T(8,128)(2,1)S(1)}, u32[]{:S(2)}, u32[]{:S(2)}) collective-permute-start(bf16[4,256,128]{2,1,0:T(8,128)(2,1)S(1)} %get-tuple-element.36), channel_id=1, source_target_pairs={{0,1},{1,0},{2,3},{3,2},{4,5},{5,4},{6,7},{7,6},{8,9},{9,8},{10,11... | collective-permute-start | bytes 786440 | tf_op jit(solution)/shard_map/beside1/ppermute | solution.py:221
  25.5 14.7 %collective-permute-start.3 = (bf16[1,4,4,64,128]{4,3,2,1,0:T(8,128)(2,1)S(1)}, bf16[1,4,4,64,128]{4,3,2,1,0:T(8,128)(2,1)S(1)}, u32[]{:S(2)}, u32[]{:S(2)}) collective-permute-start(bf16[1,4,4,64,128]{4,3,2,1,0:T(8,128)(2,1)S(1)} %get-tuple-element.34), channel_id=1, source_target_pairs={{0,16},{4,20},{8,24},{12,28},{16,0},{20,4},{24,8},{28,12},{1,17},{... | collective-permute-start | bytes 786440 | tf_op jit(solution)/shard_map/z4c0/ppermute | solution.py:221
  28.2 13.0 %collective-permute-start.10 = (bf16[4,256,128]{2,1,0:T(8,128)(2,1)S(1)}, bf16[4,256,128]{2,1,0:T(8,128)(2,1)S(1)}, u32[]{:S(2)}, u32[]{:S(2)}) collective-permute-start(bf16[4,256,128]{2,1,0:T(8,128)(2,1)S(1)} %get-tuple-element.43), channel_id=1, source_target_pairs={{0,2},{1,3},{2,0},{3,1},{4,6},{5,7},{6,4},{7,5},{8,10},{9,11},{10,... | collective-permute-start | bytes 786440 | tf_op jit(solution)/shard_map/y4/ppermute | solution.py:221
  29.8 15.9 %collective-permute-start.11 = (bf16[4,256,128]{2,1,0:T(8,128)(2,1)S(1)}, bf16[4,256,128]{2,1,0:T(8,128)(2,1)S(1)}, u32[]{:S(2)}, u32[]{:S(2)}) collective-permute-start(bf16[4,256,128]{2,1,0:T(8,128)(2,1)S(1)} %get-tuple-element.44), channel_id=1, source_target_pairs={{0,3},{1,2},{2,1},{3,0},{4,7},{5,6},{6,5},{7,4},{8,11},{9,10},{10,... | collective-permute-start | bytes 786440 | tf_op jit(solution)/shard_map/y5/ppermute | solution.py:221
  34.4 13.4 %collective-permute-start.9 = (bf16[4,256,128]{2,1,0:T(8,128)(2,1)S(1)}, bf16[4,256,128]{2,1,0:T(8,128)(2,1)S(1)}, u32[]{:S(2)}, u32[]{:S(2)}) collective-permute-start(bf16[4,256,128]{2,1,0:T(8,128)(2,1)S(1)} %get-tuple-element.42), channel_id=1, source_target_pairs={{0,1},{1,0},{2,3},{3,2},{4,5},{5,4},{6,7},{7,6},{8,9},{9,8},{10,11... | collective-permute-start | bytes 786440 | tf_op jit(solution)/shard_map/beside2/ppermute | solution.py:221
  35.5 60.4 %copy-start.1 = (s32[128]{0:T(128)S(1)}, s32[128]{0:T(128)}, u32[]{:S(2)}) copy-start(s32[128]{0:T(128)} %mirror_ref.1) | copy-start | bytes 1540
  36.9 15.1 %collective-permute-start.8 = (bf16[1,4,4,64,128]{4,3,2,1,0:T(8,128)(2,1)S(1)}, bf16[1,4,4,64,128]{4,3,2,1,0:T(8,128)(2,1)S(1)}, u32[]{:S(2)}, u32[]{:S(2)}) collective-permute-start(bf16[1,4,4,64,128]{4,3,2,1,0:T(8,128)(2,1)S(1)} %get-tuple-element.39.refs_2_), channel_id=1, source_target_pairs={{0,16},{4,20},{8,24},{12,28},{16,0},{20,4},{24,8},{28,12},{1,17},{... | collective-permute-start | bytes 786440 | tf_op jit(solution)/shard_map/z4c1/ppermute | solution.py:221
  40.3 12.0 %collective-permute-start.7 = (bf16[2,2,4,64,128]{4,3,2,1,0:T(8,128)(2,1)S(1)}, bf16[2,2,4,64,128]{4,3,2,1,0:T(8,128)(2,1)S(1)}, u32[]{:S(2)}, u32[]{:S(2)}) collective-permute-start(bf16[2,2,4,64,128]{4,3,2,1,0:T(8,128)(2,1)S(1)} %merge2.4.refs_5_), channel_id=1, source_target_pairs={{0,8},{4,12},{8,0},{12,4},{16,24},{20,28},{24,16},{28,20},{1,9},{5... | collective-permute-start | bytes 786440 | tf_op jit(solution)/shard_map/z2c0/ppermute | solution.py:221
  41.2 15.0 %collective-permute-start.16 = (bf16[4,256,128]{2,1,0:T(8,128)(2,1)S(1)}, bf16[4,256,128]{2,1,0:T(8,128)(2,1)S(1)}, u32[]{:S(2)}, u32[]{:S(2)}) collective-permute-start(bf16[4,256,128]{2,1,0:T(8,128)(2,1)S(1)} %get-tuple-element.49), channel_id=1, source_target_pairs={{0,2},{1,3},{2,0},{3,1},{4,6},{5,7},{6,4},{7,5},{8,10},{9,11},{10,... | collective-permute-start | bytes 786440 | tf_op jit(solution)/shard_map/y6/ppermute | solution.py:221
  45.7 12.1 %collective-permute-start.17 = (bf16[4,256,128]{2,1,0:T(8,128)(2,1)S(1)}, bf16[4,256,128]{2,1,0:T(8,128)(2,1)S(1)}, u32[]{:S(2)}, u32[]{:S(2)}) collective-permute-start(bf16[4,256,128]{2,1,0:T(8,128)(2,1)S(1)} %get-tuple-element.50), channel_id=1, source_target_pairs={{0,3},{1,2},{2,1},{3,0},{4,7},{5,6},{6,5},{7,4},{8,11},{9,10},{10,... | collective-permute-start | bytes 786440 | tf_op jit(solution)/shard_map/y7/ppermute | solution.py:221
  47.9 9.9 %collective-permute-start.15 = (bf16[4,256,128]{2,1,0:T(8,128)(2,1)S(1)}, bf16[4,256,128]{2,1,0:T(8,128)(2,1)S(1)}, u32[]{:S(2)}, u32[]{:S(2)}) collective-permute-start(bf16[4,256,128]{2,1,0:T(8,128)(2,1)S(1)} %get-tuple-element.48), channel_id=1, source_target_pairs={{0,1},{1,0},{2,3},{3,2},{4,5},{5,4},{6,7},{7,6},{8,9},{9,8},{10,11... | collective-permute-start | bytes 786440 | tf_op jit(solution)/shard_map/beside3/ppermute | solution.py:221
  52.0 20.8 %collective-permute-start.14 = (bf16[1,4,4,64,128]{4,3,2,1,0:T(8,128)(2,1)S(1)}, bf16[1,4,4,64,128]{4,3,2,1,0:T(8,128)(2,1)S(1)}, u32[]{:S(2)}, u32[]{:S(2)}) collective-permute-start(bf16[1,4,4,64,128]{4,3,2,1,0:T(8,128)(2,1)S(1)} %get-tuple-element.45.refs_2_), channel_id=1, source_target_pairs={{0,16},{4,20},{8,24},{12,28},{16,0},{20,4},{24,8},{28,12},{1,17},{... | collective-permute-start | bytes 786440 | tf_op jit(solution)/shard_map/z4c2/ppermute | solution.py:221
  52.3 20.7 %collective-permute-start.13 = (bf16[2,2,4,64,128]{4,3,2,1,0:T(8,128)(2,1)S(1)}, bf16[2,2,4,64,128]{4,3,2,1,0:T(8,128)(2,1)S(1)}, u32[]{:S(2)}, u32[]{:S(2)}) collective-permute-start(bf16[2,2,4,64,128]{4,3,2,1,0:T(8,128)(2,1)S(1)} %merge2.5.refs_3_.refs_5_), channel_id=1, source_target_pairs={{0,8},{4,12},{8,0},{12,4},{16,24},{20,28},{24,16},{28,20},{1,9},{5... | collective-permute-start | bytes 786440 | tf_op jit(solution)/shard_map/z2c1/ppermute | solution.py:221
  56.2 16.7 %collective-permute-start.12 = (bf16[4,1,4,64,128]{4,3,2,1,0:T(8,128)(2,1)S(1)}, bf16[4,1,4,64,128]{4,3,2,1,0:T(8,128)(2,1)S(1)}, u32[]{:S(2)}, u32[]{:S(2)}) collective-permute-start(bf16[4,1,4,64,128]{4,3,2,1,0:T(8,128)(2,1)S(1)} %merge1.4.refs_6_), channel_id=1, source_target_pairs={{0,4},{4,0},{8,12},{12,8},{16,20},{20,16},{24,28},{28,24},{1,5},{5... | collective-permute-start | bytes 786440 | tf_op jit(solution)/shard_map/z1c0/ppermute | solution.py:221
  59.1 18.3 %collective-permute-start.20 = (bf16[1,4,4,64,128]{4,3,2,1,0:T(8,128)(2,1)S(1)}, bf16[1,4,4,64,128]{4,3,2,1,0:T(8,128)(2,1)S(1)}, u32[]{:S(2)}, u32[]{:S(2)}) collective-permute-start(bf16[1,4,4,64,128]{4,3,2,1,0:T(8,128)(2,1)S(1)} %get-tuple-element.51.refs_2_), channel_id=1, source_target_pairs={{0,16},{4,20},{8,24},{12,28},{16,0},{20,4},{24,8},{28,12},{1,17},{... | collective-permute-start | bytes 786440 | tf_op jit(solution)/shard_map/z4c3/ppermute | solution.py:221
  72.9 8.9 %collective-permute-start.19 = (bf16[2,2,4,64,128]{4,3,2,1,0:T(8,128)(2,1)S(1)}, bf16[2,2,4,64,128]{4,3,2,1,0:T(8,128)(2,1)S(1)}, u32[]{:S(2)}, u32[]{:S(2)}) collective-permute-start(bf16[2,2,4,64,128]{4,3,2,1,0:T(8,128)(2,1)S(1)} %merge2.6.refs_3_), channel_id=1, source_target_pairs={{0,8},{4,12},{8,0},{12,4},{16,24},{20,28},{24,16},{28,20},{1,9},{5... | collective-permute-start | bytes 786440 | tf_op jit(solution)/shard_map/z2c2/ppermute | solution.py:221
  73.0 8.8 %collective-permute-start.18 = (bf16[4,1,4,64,128]{4,3,2,1,0:T(8,128)(2,1)S(1)}, bf16[4,1,4,64,128]{4,3,2,1,0:T(8,128)(2,1)S(1)}, u32[]{:S(2)}, u32[]{:S(2)}) collective-permute-start(bf16[4,1,4,64,128]{4,3,2,1,0:T(8,128)(2,1)S(1)} %merge1.5), channel_id=1, source_target_pairs={{0,4},{4,0},{8,12},{12,8},{16,20},{20,16},{24,28},{28,24},{1,5},{5... | collective-permute-start | bytes 786440 | tf_op jit(solution)/shard_map/z1c1/ppermute | solution.py:221
  77.4 8.3 %collective-permute-start.22 = (bf16[2,2,4,64,128]{4,3,2,1,0:T(8,128)(2,1)S(1)}, bf16[2,2,4,64,128]{4,3,2,1,0:T(8,128)(2,1)S(1)}, u32[]{:S(2)}, u32[]{:S(2)}) collective-permute-start(bf16[2,2,4,64,128]{4,3,2,1,0:T(8,128)(2,1)S(1)} %merge2.7.refs_3_), channel_id=1, source_target_pairs={{0,8},{4,12},{8,0},{12,4},{16,24},{20,28},{24,16},{28,20},{1,9},{5... | collective-permute-start | bytes 786440 | tf_op jit(solution)/shard_map/z2c3/ppermute | solution.py:221
  81.8 7.7 %collective-permute-start.21 = (bf16[4,1,4,64,128]{4,3,2,1,0:T(8,128)(2,1)S(1)}, bf16[4,1,4,64,128]{4,3,2,1,0:T(8,128)(2,1)S(1)}, u32[]{:S(2)}, u32[]{:S(2)}) collective-permute-start(bf16[4,1,4,64,128]{4,3,2,1,0:T(8,128)(2,1)S(1)} %merge1.6), channel_id=1, source_target_pairs={{0,4},{4,0},{8,12},{12,8},{16,20},{20,16},{24,28},{28,24},{1,5},{5... | collective-permute-start | bytes 786440 | tf_op jit(solution)/shard_map/z1c2/ppermute | solution.py:221
  89.5 6.4 %collective-permute-start.23 = (bf16[4,1,4,64,128]{4,3,2,1,0:T(8,128)(2,1)S(1)}, bf16[4,1,4,64,128]{4,3,2,1,0:T(8,128)(2,1)S(1)}, u32[]{:S(2)}, u32[]{:S(2)}) collective-permute-start(bf16[4,1,4,64,128]{4,3,2,1,0:T(8,128)(2,1)S(1)} %merge1.7), channel_id=1, source_target_pairs={{0,4},{4,0},{8,12},{12,8},{16,20},{20,16},{24,28},{28,24},{1,5},{5... | collective-permute-start | bytes 786440 | tf_op jit(solution)/shard_map/z1c3/ppermute | solution.py:221

commit v6 on v5

v6 whole, which is shorter than its diff:
```python
import functools

import jax
import jax.numpy as jnp
from jax import lax
from jax.experimental import pallas as pl
from jax.experimental.pallas import tpu as pltpu
from jax.sharding import PartitionSpec as P

LANES = 128
STEP = 64
CHUNKS = (4, 4, 4, 4)
LATE = 2
PART = 256
MIB = 1024 * 1024
COST = pl.CostEstimate(flops=1024, bytes_accessed=1024, transcendentals=0)
IN_VMEM = pl.BlockSpec(memory_space=pltpu.VMEM)
IN_SMEM = pl.BlockSpec(memory_space=pltpu.SMEM)
ANYWHERE = pl.BlockSpec(memory_space=pl.ANY)
IN_HBM = pl.BlockSpec(memory_space=pltpu.MemorySpace.HBM)


def quarter_kernel(rows, far, n_after, place_ref, x_ref, c_hbm, *refs):
    refs = refs[n_after:]
    outs, (c_ref, turn_ref, held, c_sem, sems) = refs[:-5], refs[-5:]
    at = pl.program_id(0)
    step, k_all, depth = x_ref.shape
    padded = held.shape[2]
    many = PART // k_all

    @pl.when(at == 0)
    def _():
        first = pl.multiple_of(((place_ref[0] >> 1) ^ far) * 2 * LANES, 2 * LANES)
        copy = pltpu.make_async_copy(c_hbm.at[:, pl.ds(first, 2 * LANES)], c_ref, c_sem)
        copy.start()
        to = lax.broadcasted_iota(jnp.int32, (PART, PART), 0)
        source = lax.broadcasted_iota(jnp.int32, (PART, PART), 1)
        turn_ref[...] = (source == to % many * k_all + to // many).astype(jnp.float32).astype(jnp.bfloat16)
        copy.wait()

    x = x_ref[...].reshape(step * k_all, depth)
    product = jnp.dot(x, c_ref[...], preferred_element_type=jnp.float32)
    line = lax.broadcasted_iota(jnp.int32, product.shape, 0)
    product = jnp.where(line < (rows - at * step) * k_all, product, 0.0).astype(jnp.bfloat16)
    for part in range(step // many):
        lines = jnp.dot(
            turn_ref[...], product[part * PART : (part + 1) * PART], preferred_element_type=jnp.float32
        ).astype(jnp.bfloat16)
        here = pl.ds(pl.multiple_of(at * step + part * many, many), many)
        for k in range(k_all):
            for d in range(2):
                held[d, k, here] = lines[k * many : (k + 1) * many, d * LANES : (d + 1) * LANES]
    here = pl.ds(pl.multiple_of(at * step, step), step)
    first = 0
    for n, out in enumerate(outs):
        d = (place_ref[0] & 1) ^ (n & 1)
        kc = out.shape[0]
        pltpu.make_async_copy(held.at[d, pl.ds(first, kc), here], out.at[:, here], sems.at[n]).start()
        if n & 1:
            first += kc

    @pl.when(at == padded // step - 1)
    def _():
        first = 0
        for n, out in enumerate(outs):
            d = (place_ref[0] & 1) ^ (n & 1)
            kc = out.shape[0]
            pltpu.make_async_copy(held.at[d, pl.ds(first, kc)], out, sems.at[n]).wait()
            if n & 1:
                first += kc


def quarter_of(place, by_r, coeffs, far, padded, chunks, after=()):
    rows, k_all, depth = by_r.shape
    outs = [jax.ShapeDtypeStruct((kc, padded, LANES), jnp.bfloat16) for kc in chunks for _ in range(2)]
    out = pl.pallas_call(
        functools.partial(quarter_kernel, rows, far, len(after)),
        grid_spec=pltpu.PrefetchScalarGridSpec(
            num_scalar_prefetch=1,
            grid=(padded // STEP,),
            in_specs=[pl.BlockSpec((STEP, k_all, depth), lambda r, place: (r, 0, 0))]
            + [IN_HBM]
            + [ANYWHERE] * len(after),
            out_specs=[IN_HBM] * len(outs),
            scratch_shapes=[
                pltpu.VMEM((depth, 2 * LANES), jnp.bfloat16),
                pltpu.VMEM((PART, PART), jnp.bfloat16),
                pltpu.VMEM((2, k_all, padded, LANES), jnp.bfloat16),
                pltpu.SemaphoreType.DMA,
                pltpu.SemaphoreType.DMA((len(outs),)),
            ],
        ),
        out_shape=outs,
        compiler_params=pltpu.CompilerParams(vmem_limit_bytes=50 * MIB),
        cost_estimate=COST,
        name=f"quarter{far}",
    )(place, by_r, coeffs, *after)
    return list(out)


def turn_kernel(rows, c_ref, out_ref):
    n_mo, orbitals, padded = out_ref.shape
    none = jnp.zeros((padded - rows, orbitals), jnp.float32)
    for n in range(n_mo):
        part = c_ref[n * rows : (n + 1) * rows, :].astype(jnp.float32)
        out_ref[n] = jnp.concatenate([part, none], axis=0).T.astype(jnp.bfloat16)


def turn(coeffs, n_mo, padded):
    depth, orbitals = coeffs.shape
    return pl.pallas_call(
        functools.partial(turn_kernel, depth // n_mo),
        in_specs=[IN_VMEM],
        out_specs=IN_VMEM,
        out_shape=jax.ShapeDtypeStruct((n_mo, orbitals, padded), jnp.bfloat16),
        compiler_params=pltpu.CompilerParams(vmem_limit_bytes=24 * MIB),
        cost_estimate=COST,
        name="turn",
    )(coeffs)


def half_kernel(n_mo, plans, place_ref, *refs):
    blocks, t_ref, held = refs[:n_mo], refs[n_mo], refs[-1]
    outs = refs[-1 - 2 * len(plans) : -1]
    lanes = held.shape[1] // 2
    for p, (first, kc, owners) in enumerate(plans):
        for k in range(0, kc, 2):
            half = None
            for o, a_ref in enumerate(blocks):
                columns = jnp.concatenate([a_ref[first + k], a_ref[first + k + 1]], axis=1)
                part = jnp.dot(t_ref[place_ref[0] ^ o], columns, preferred_element_type=jnp.float32)
                half = part if half is None else half + part
            held[...] = half
            for out, its in zip(outs[2 * p : 2 * p + 2], owners):
                block = out.shape[3]
                for at, o in enumerate(its):
                    start = pl.multiple_of((place_ref[1] ^ o) * block, block)
                    for n in range(2):
                        piece = held[pl.ds(start, block), n * lanes : (n + 1) * lanes]
                        out[0, at, k + n] = piece.astype(jnp.bfloat16)


def half_of(place, blocks, turned, plans, after):
    n_mo, orbitals, _ = turned.shape
    lanes = blocks[0].shape[-1]
    shapes = [
        (1, len(its), kc, orbitals // sum(len(x) for x in owners), lanes)
        for _, kc, owners in plans
        for its in owners
    ]
    return pl.pallas_call(
        functools.partial(half_kernel, n_mo, plans),
        in_specs=[IN_SMEM] + [IN_VMEM] * (n_mo + 1) + [ANYWHERE] * len(after),
        out_specs=[IN_VMEM] * len(shapes),
        out_shape=[jax.ShapeDtypeStruct(shape, jnp.bfloat16) for shape in shapes],
        scratch_shapes=[pltpu.VMEM((orbitals, 2 * lanes), jnp.float32)],
        compiler_params=pltpu.CompilerParams(vmem_limit_bytes=24 * MIB),
        cost_estimate=COST,
        name="half",
    )(place, *blocks, turned, *after)


def merge_kernel(picks, *refs):
    at = 0
    for x, pick in zip(refs, picks):
        for i in range(x.shape[0]):
            for n, o in enumerate(pick):
                refs[-1][at, n] = x[i, o]
            at += 1


def merge(parts, picks, after):
    shape = (sum(x.shape[0] for x in parts), len(picks[0]), *parts[0].shape[2:])
    return pl.pallas_call(
        functools.partial(merge_kernel, picks),
        in_specs=[IN_VMEM] * len(parts) + [ANYWHERE] * len(after),
        out_specs=IN_VMEM,
        out_shape=jax.ShapeDtypeStruct(shape, jnp.bfloat16),
        compiler_params=pltpu.CompilerParams(vmem_limit_bytes=24 * MIB),
        cost_estimate=COST,
        name="merge",
    )(*parts, *after)


def combine_kernel(sources, k_all, per_step, mirror_ref, place_ref, *refs):
    pieces, out_ref, held = refs[:-2], refs[-2], refs[-1]
    step = pl.program_id(0)

    @pl.when(step == 0)
    def _():
        for piece, (offsets, first) in zip(pieces, sources):
            for n, offset in enumerate(offsets):
                row = (place_ref[1] ^ offset) * k_all + first
                held[pl.ds(row, piece.shape[2])] = piece[n, 0]

    for n in range(per_step):
        k = step * per_step + n
        out_ref[n] = 0.5 * (held[k].astype(jnp.float32) + held[mirror_ref[k]].astype(jnp.float32))


def combine(pieces, sources, mirror, place, n_pair):
    block, lanes = pieces[0].shape[-2:]
    k_all = sum(CHUNKS)
    rows = n_pair * k_all
    per_step = max(1, 32 * 64 // block)
    return pl.pallas_call(
        functools.partial(combine_kernel, sources, k_all, per_step),
        grid_spec=pltpu.PrefetchScalarGridSpec(
            num_scalar_prefetch=2,
            grid=(rows // per_step,),
            in_specs=[IN_VMEM] * len(pieces),
            out_specs=pl.BlockSpec((per_step, block, lanes), lambda k, m, place: (k, 0, 0)),
            scratch_shapes=[pltpu.VMEM((rows, block, lanes), jnp.bfloat16)],
        ),
        out_shape=jax.ShapeDtypeStruct((rows, block, lanes), jnp.float32),
        compiler_params=pltpu.CompilerParams(vmem_limit_bytes=24 * MIB),
        cost_estimate=COST,
        name="combine",
    )(mirror, place, *pieces)


def flipped(x, axis, size, offset, name):
    with jax.named_scope(name):
        return lax.ppermute(x, axis, [(i, i ^ offset) for i in range(size)])


def on_device(n_pair, n_mo, integrals, coeffs, mirror):
    rows = integrals.shape[1]
    padded = -(-rows // STEP) * STEP
    n_near = n_pair // 2
    by_r = jnp.transpose(integrals, (1, 0, 2))
    place = jnp.stack([lax.axis_index("mo"), lax.axis_index("pair")]).astype(jnp.int32)
    turned = turn(coeffs, n_mo, padded)
    queue = quarter_of(place, by_r, coeffs, 1, padded, CHUNKS)
    arrived = [flipped(x, "mo", n_mo, 2 + (m & 1), f"y{m}") for m, x in enumerate(queue)]
    near = quarter_of(place, by_r, coeffs, 0, padded, CHUNKS, queue[:1])
    beside = [flipped(x, "mo", n_mo, 1, f"beside{c}") for c, x in enumerate(near[1::2])]

    down = tuple(1 << n for n in reversed(range(n_pair.bit_length() - 1)))
    last = len(CHUNKS) - 1
    units = [(c, 0, kc - LATE * (c == last), down) for c, kc in enumerate(CHUNKS)]
    units.append((last, CHUNKS[-1] - LATE, LATE, down[::-1]))
    firsts = [sum(CHUNKS[:c]) + at for c, at, _, _ in units]
    steps = [(c, c, 0) for c in range(len(CHUNKS))]
    for level in range(1, len(down)):
        steps += [(c + level + level / 10, c, level) for c in range(len(CHUNKS))]
        steps.append((last + level - 0.85, last + 1, level))
    parts, owners, offsets = [[] for _ in units], [[] for _ in units], [[[0]] for _ in units]
    token = []

    def send(unit, level, message, sent):
        flip = units[unit][3][level]
        offsets[unit].append([o ^ flip for group in offsets[unit] for o in group])
        owners[unit].append([o ^ flip for o in sent])
        parts[unit].append(flipped(message, "pair", n_pair, flip, f"z{flip}c{unit}"))

    def split(unit, level):
        flips = units[unit][3]
        left = [o for o in range(n_pair) if not o & sum(flips[:level])]
        return [o for o in left if not o & flips[level]], [o for o in left if o & flips[level]]

    for _, n, level in sorted(steps):
        if level == 0:
            mine = [unit for unit, plan in enumerate(units) if plan[0] == n]
            plans = [(units[unit][1], units[unit][2], split(unit, 0)) for unit in mine]
            blocks = [near[2 * n], beside[n], *arrived[2 * n : 2 * n + 2]]
            out = half_of(place, blocks, turned, plans, token)
            for m, unit in enumerate(mine):
                parts[unit].append(out[2 * m])
                owners[unit].append(plans[m][2][0])
                send(unit, 0, out[2 * m + 1], plans[m][2][1])
            token = list(out[:1])
        else:
            sent = split(n, level)[1]
            after = token + ([parts[n - 2][-1]] if level == len(down) - 1 and 1 < n <= last else [])
            message = merge(parts[n], [[its.index(o) for o in sent] for its in owners[n]], after)
            send(n, level, message, sent)
            token = [message]
    pieces = [x for chunk in parts for x in chunk]
    sources = [(tuple(group), first) for chunk, first in zip(offsets, firsts) for group in chunk]
    return combine(pieces, sources, mirror, place, n_pair)


def solution(mesh):
    return jax.shard_map(
        functools.partial(on_device, mesh.shape["pair"], mesh.shape["mo"]),
        mesh=mesh,
        in_specs=(P("pair", "mo", None), P(), P()),
        out_specs=P(None, "pair", "mo"),
        check_vma=False,
    )
```

time: 100 us -> 92.5 us (0.925)
  waiting for transfers between devices: 41.9 us -> 27 us
  starting transfers between devices: 32.5 us -> 39.2 us
    ppermute x24 -> x27, waiting for transfers between devices: 41.9 us -> 27 us  [flipped(): return lax.ppermute(x, axis, [(i, i ^ offset) for i in range(size)])]
    ppermute x24 -> x27, starting transfers between devices: 32.5 us -> 39.2 us  [flipped(): return lax.ppermute(x, axis, [(i, i ^ offset) for i in range(size)])]
    pallas_call x2, Pallas kernels: 14.2 us -> 15.4 us  [quarter_of(): pl.pallas_call(functools.partial(quarter_kernel, rows, far, len(after)),...]
    pallas_call x13 -> x15, Pallas kernels: 9.31 us -> 8.8 us  [the longest x4 5.37 us: half_of(): pl.pallas_call(functools.partial(half_kernel, n_mo, plans), in_specs=[IN_...]
  transfers between devices with their start and end apart: 24 -> 27, of which waited for: 12 -> 11; matrix products, arithmetic and copies ran while one was open for 0% -> 0% of each run, Pallas kernels for 13% -> 15%
where the time goes in v6:
time: 92.5 us; the launch traced here: 92.3 us
  starting transfers between devices  39.2 us (42%)
  waiting for transfers between devices  27 us (29%)
  Pallas kernels  24.6 us (27%)
  local copies, waits for them, and re-layouts  1.22 us (1%)
    ppermute x27, starting transfers between devices, flipped(): return lax.ppermute(x, axis, [(i, i ^ offset) for i in range(size)])  39.2 us
    ppermute x27, waiting for transfers between devices, flipped(): return lax.ppermute(x, axis, [(i, i ^ offset) for i in range(size)])  27 us
    pallas_call x2, Pallas kernels, quarter_of(): pl.pallas_call(functools.partial(quarter_kernel, rows, far, len(after)),...  15.4 us
    pallas_call x4, Pallas kernels, half_of(): pl.pallas_call(functools.partial(half_kernel, n_mo, plans), in_specs=[IN_...  5.37 us
    pallas_call x1, Pallas kernels, combine(): pl.pallas_call(functools.partial(combine_kernel, sources, k_all, per_step...  3.28 us
  transfers between devices with their start and end apart: 27, of which 11 were waited for; matrix products, arithmetic and copies ran while one was open for 0% of the time, Pallas kernels for 15%

profile of v6, /device:TPU:0, one launch (start us, length us, event | category | flops | bytes accessed | tf_op | source)
XLA Modules:
  0.0 92.3 jit_solution(18298514856601233853)
XLA Ops:
  0.0 0.1 pad_add_fusion.place_ref
  0.1 1.2 %copy-done = bf16[1000,512]{1,0:T(8,128)(2,1)S(1)} copy-done((bf16[1000,512]{1,0:T(8,128)(2,1)S(1)}, bf16[1000,512]{1,0:T(8,128)(2,1)}, u32[]{:S(2)}) %copy-start) | copy-done | bytes 1024024
  1.3 7.7 %quarter1.1 = (bf16[4,256,128]{2,1,0:T(8,128)(2,1)S(1)}, bf16[4,256,128]{2,1,0:T(8,128)(2,1)S(1)}, bf16[4,256,128]{2,1,0:T(8,128)(2,1)S(1)}, bf16[4,256,128]{2,1...) custom-call(s32[2]{0:T(128)S(1)} %pad_add_fusion.place_ref, ...), custom_call_target="tpu_custom_call" | custom-call | flops 1024 | bytes 1024 | tf_op jit(solution)/shard_map/quarter1/pallas_call | solution.py:76
  9.0 2.5 %collective-permute-start.2 = (bf16[4,256,128]{2,1,0:T(8,128)(2,1)S(1)}, bf16[4,256,128]{2,1,0:T(8,128)(2,1)S(1)}, u32[]{:S(2)}, u32[]{:S(2)}) collective-permute-start(bf16[4,256,128]{2,1,0:T(8,128)(2,1)S(1)} %get-tuple-element.34), channel_id=1, source_target_pairs={{0,3},{1,2},{2,1},{3,0},{4,7},{5,6},{6,5},{7,4},{8,11},{9,10},{10,... | collective-permute-start | bytes 786440 | tf_op jit(solution)/shard_map/y1/ppermute | solution.py:224
  11.5 0.6 collective-permute-start.1
  12.1 7.7 %quarter0.1 = (bf16[4,256,128]{2,1,0:T(8,128)(2,1)S(1)}, bf16[4,256,128]{2,1,0:T(8,128)(2,1)S(1)}, bf16[4,256,128]{2,1,0:T(8,128)(2,1)S(1)}, bf16[4,256,128]{2,1...) custom-call(s32[2]{0:T(128)S(1)} %pad_add_fusion.place_ref, ...), custom_call_target="tpu_custom_call" | custom-call | flops 1024 | bytes 1024 | tf_op jit(solution)/shard_map/quarter0/pallas_call | solution.py:76
  19.8 0.1 collective-permute-start
  19.9 1.7 %collective-permute-start.5 = (bf16[4,256,128]{2,1,0:T(8,128)(2,1)S(1)}, bf16[4,256,128]{2,1,0:T(8,128)(2,1)S(1)}, u32[]{:S(2)}, u32[]{:S(2)}) collective-permute-start(bf16[4,256,128]{2,1,0:T(8,128)(2,1)S(1)} %get-tuple-element.39), channel_id=1, source_target_pairs={{0,2},{1,3},{2,0},{3,1},{4,6},{5,7},{6,4},{7,5},{8,10},{9,11},{10,... | collective-permute-start | bytes 786440 | tf_op jit(solution)/shard_map/y2/ppermute | solution.py:224
  21.7 0.1 collective-permute-start.6
  21.8 0.3 collective-permute-start.4
  22.1 0.4 turn.1.refs_4_
  22.5 2.3 %collective-permute-done.1.refs_2_ = bf16[4,256,128]{2,1,0:T(8,128)(2,1)S(1)} collective-permute-done((bf16[4,256,128]{2,1,0:T(8,128)(2,1)S(1)}, bf16[4,256,128]{2,1,0:T(8,128)(2,1)S(1)}, u32[]{:S(2)}, u32[]{:S(2)}) %collective-permute-start.1) | collective-permute-done | bytes 262176 | tf_op jit(solution)/shard_map/y0/ppermute | solution.py:224
  24.8 1.3 %half.4 = (bf16[1,4,4,64,128]{4,3,2,1,0:T(8,128)(2,1)S(1)}, bf16[1,4,4,64,128]{4,3,2,1,0:T(8,128)(2,1)S(1)}) custom-call(s32[2]{0:T(128)S(1)} %pad_add_fusion.place_ref, bf16[4,256,128]{2,1,0:T(8,128)(2,1)S(1)} %get-tuple-element.32.refs_0_, bf16[4,256,128]{2,1,0:T(8,128)(2,1)S(1)} %collective-permute-done.refs_1_, ...), custom_call_target="tpu_custom_call" | custom-call | flops 1024 | bytes 1024 | tf_op jit(solution)/shard_map/half/pallas_call | solution.py:151
  26.2 2.7 %collective-permute-start.3 = (bf16[1,4,4,64,128]{4,3,2,1,0:T(8,128)(2,1)S(1)}, bf16[1,4,4,64,128]{4,3,2,1,0:T(8,128)(2,1)S(1)}, u32[]{:S(2)}, u32[]{:S(2)}) collective-permute-start(bf16[1,4,4,64,128]{4,3,2,1,0:T(8,128)(2,1)S(1)} %get-tuple-element.36), channel_id=1, source_target_pairs={{0,16},{4,20},{8,24},{12,28},{16,0},{20,4},{24,8},{28,12},{1,17},{... | collective-permute-start | bytes 786440 | tf_op jit(solution)/shard_map/z4c0/ppermute | solution.py:224
  28.8 1.5 %collective-permute-start.10 = (bf16[4,256,128]{2,1,0:T(8,128)(2,1)S(1)}, bf16[4,256,128]{2,1,0:T(8,128)(2,1)S(1)}, u32[]{:S(2)}, u32[]{:S(2)}) collective-permute-start(bf16[4,256,128]{2,1,0:T(8,128)(2,1)S(1)} %get-tuple-element.45), channel_id=1, source_target_pairs={{0,2},{1,3},{2,0},{3,1},{4,6},{5,7},{6,4},{7,5},{8,10},{9,11},{10,... | collective-permute-start | bytes 786440 | tf_op jit(solution)/shard_map/y4/ppermute | solution.py:224
  30.3 0.1 collective-permute-done.5.refs_2_
  30.4 1.2 %collective-permute-start.11 = (bf16[4,256,128]{2,1,0:T(8,128)(2,1)S(1)}, bf16[4,256,128]{2,1,0:T(8,128)(2,1)S(1)}, u32[]{:S(2)}, u32[]{:S(2)}) collective-permute-start(bf16[4,256,128]{2,1,0:T(8,128)(2,1)S(1)} %get-tuple-element.46), channel_id=1, source_target_pairs={{0,3},{1,2},{2,1},{3,0},{4,7},{5,6},{6,5},{7,4},{8,11},{9,10},{10,... | collective-permute-start | bytes 786440 | tf_op jit(solution)/shard_map/y5/ppermute | solution.py:224
  31.6 3.4 %collective-permute-done.6.refs_3_ = bf16[4,256,128]{2,1,0:T(8,128)(2,1)S(1)} collective-permute-done((bf16[4,256,128]{2,1,0:T(8,128)(2,1)S(1)}, bf16[4,256,128]{2,1,0:T(8,128)(2,1)S(1)}, u32[]{:S(2)}, u32[]{:S(2)}) %collective-permute-start.6) | collective-permute-done | bytes 262176 | tf_op jit(solution)/shard_map/y3/ppermute | solution.py:224
  35.0 1.1 %collective-permute-start.9 = (bf16[4,256,128]{2,1,0:T(8,128)(2,1)S(1)}, bf16[4,256,128]{2,1,0:T(8,128)(2,1)S(1)}, u32[]{:S(2)}, u32[]{:S(2)}) collective-permute-start(bf16[4,256,128]{2,1,0:T(8,128)(2,1)S(1)} %get-tuple-element.44), channel_id=1, source_target_pairs={{0,1},{1,0},{2,3},{3,2},{4,5},{5,4},{6,7},{7,6},{8,9},{9,8},{10,11... | collective-permute-start | bytes 786440 | tf_op jit(solution)/shard_map/beside2/ppermute | solution.py:224
  36.1 1.3 %half.5 = (bf16[1,4,4,64,128]{4,3,2,1,0:T(8,128)(2,1)S(1)}, bf16[1,4,4,64,128]{4,3,2,1,0:T(8,128)(2,1)S(1)}) custom-call(s32[2]{0:T(128)S(1)} %pad_add_fusion.place_ref, bf16[4,256,128]{2,1,0:T(8,128)(2,1)S(1)} %get-tuple-element.37.refs_0_, bf16[4,256,128]{2,1,0:T(8,128)(2,1)S(1)} %collective-permute-done.4.refs_1_, ...), custom_call_target="tpu_custom_call" | custom-call | flops 1024 | bytes 1024 | tf_op jit(solution)/shard_map/half/pallas_call | solution.py:151
  37.5 2.5 %collective-permute-start.8 = (bf16[1,4,4,64,128]{4,3,2,1,0:T(8,128)(2,1)S(1)}, bf16[1,4,4,64,128]{4,3,2,1,0:T(8,128)(2,1)S(1)}, u32[]{:S(2)}, u32[]{:S(2)}) collective-permute-start(bf16[1,4,4,64,128]{4,3,2,1,0:T(8,128)(2,1)S(1)} %get-tuple-element.42), channel_id=1, source_target_pairs={{0,16},{4,20},{8,24},{12,28},{16,0},{20,4},{24,8},{28,12},{1,17},{... | collective-permute-start | bytes 786440 | tf_op jit(solution)/shard_map/z4c1/ppermute | solution.py:224
  40.0 0.9 collective-permute-done.3.refs_1_
  40.9 0.9 %collective-permute-start.7 = (bf16[2,2,4,64,128]{4,3,2,1,0:T(8,128)(2,1)S(1)}, bf16[2,2,4,64,128]{4,3,2,1,0:T(8,128)(2,1)S(1)}, u32[]{:S(2)}, u32[]{:S(2)}) collective-permute-start(bf16[2,2,4,64,128]{4,3,2,1,0:T(8,128)(2,1)S(1)} %merge.10.refs_5_), channel_id=1, source_target_pairs={{0,8},{4,12},{8,0},{12,4},{16,24},{20,28},{24,16},{28,20},{1,9},{5... | collective-permute-start | bytes 786440 | tf_op jit(solution)/shard_map/z2c0/ppermute | solution.py:224
  41.8 1.5 %collective-permute-start.15 = (bf16[4,256,128]{2,1,0:T(8,128)(2,1)S(1)}, bf16[4,256,128]{2,1,0:T(8,128)(2,1)S(1)}, u32[]{:S(2)}, u32[]{:S(2)}) collective-permute-start(bf16[4,256,128]{2,1,0:T(8,128)(2,1)S(1)} %get-tuple-element.50), channel_id=1, source_target_pairs={{0,2},{1,3},{2,0},{3,1},{4,6},{5,7},{6,4},{7,5},{8,10},{9,11},{10,... | collective-permute-start | bytes 786440 | tf_op jit(solution)/shard_map/y6/ppermute | solution.py:224
  43.3 2.9 %collective-permute-done.11.refs_3_ = bf16[4,256,128]{2,1,0:T(8,128)(2,1)S(1)} collective-permute-done((bf16[4,256,128]{2,1,0:T(8,128)(2,1)S(1)}, bf16[4,256,128]{2,1,0:T(8,128)(2,1)S(1)}, u32[]{:S(2)}, u32[]{:S(2)}) %collective-permute-start.11) | collective-permute-done | bytes 262176 | tf_op jit(solution)/shard_map/y5/ppermute | solution.py:224
  46.3 2.2 %collective-permute-start.16 = (bf16[4,256,128]{2,1,0:T(8,128)(2,1)S(1)}, bf16[4,256,128]{2,1,0:T(8,128)(2,1)S(1)}, u32[]{:S(2)}, u32[]{:S(2)}) collective-permute-start(bf16[4,256,128]{2,1,0:T(8,128)(2,1)S(1)} %get-tuple-element.51), channel_id=1, source_target_pairs={{0,3},{1,2},{2,1},{3,0},{4,7},{5,6},{6,5},{7,4},{8,11},{9,10},{10,... | collective-permute-start | bytes 786440 | tf_op jit(solution)/shard_map/y7/ppermute | solution.py:224
  48.5 0.4 collective-permute-start.14
  48.8 1.3 %half.6 = (bf16[1,4,4,64,128]{4,3,2,1,0:T(8,128)(2,1)S(1)}, bf16[1,4,4,64,128]{4,3,2,1,0:T(8,128)(2,1)S(1)}) custom-call(s32[2]{0:T(128)S(1)} %pad_add_fusion.place_ref, bf16[4,256,128]{2,1,0:T(8,128)(2,1)S(1)} %get-tuple-element.43.refs_0_, bf16[4,256,128]{2,1,0:T(8,128)(2,1)S(1)} %collective-permute-done.9.refs_1_, ...), custom_call_target="tpu_custom_call" | custom-call | flops 1024 | bytes 1024 | tf_op jit(solution)/shard_map/half/pallas_call | solution.py:151
  50.2 2.4 %collective-permute-done.8.refs_1_.refs_5_ = bf16[1,4,4,64,128]{4,3,2,1,0:T(8,128)(2,1)S(1)} collective-permute-done((bf16[1,4,4,64,128]{4,3,2,1,0:T(8,128)(2,1)S(1)}, bf16[1,4,4,64,128]{4,3,2,1,0:T(8,128)(2,1)S(1)}, u32[]{:S(2)}, u32[]{:S(2)}) %collective-permute-start.8) | collective-permute-done | bytes 262176 | tf_op jit(solution)/shard_map/z4c1/ppermute | solution.py:224
  52.6 0.2 collective-permute-start.18
  52.9 3.9 %collective-permute-start.13 = (bf16[2,2,4,64,128]{4,3,2,1,0:T(8,128)(2,1)S(1)}, bf16[2,2,4,64,128]{4,3,2,1,0:T(8,128)(2,1)S(1)}, u32[]{:S(2)}, u32[]{:S(2)}) collective-permute-start(bf16[2,2,4,64,128]{4,3,2,1,0:T(8,128)(2,1)S(1)} %merge.11.refs_3_), channel_id=1, source_target_pairs={{0,8},{4,12},{8,0},{12,4},{16,24},{20,28},{24,16},{28,20},{1,9},{5... | collective-permute-start | bytes 786440 | tf_op jit(solution)/shard_map/z2c1/ppermute | solution.py:224
  56.9 0.6 collective-permute-done.16.refs_3_
  57.5 1.3 %half.7 = (bf16[1,4,2,64,128]{4,3,2,1,0:T(8,128)(2,1)S(1)}, bf16[1,4,2,64,128]{4,3,2,1,0:T(8,128)(2,1)S(1)}, bf16[1,4,2,64,128]{4,3,2,1,0:T(8,128)(2,1)S(1)}, bf16[1,4,2,64,128]{4,3,2,1,0:T(8,128)(2,1)S(1)}) custom-call(s32[2]{0:T(128)S(1)} %pad_add_fusion.place_ref, bf16[4,256,128]{2,1,0:T(8,128)(2,1)S(1)} %get-tuple-element.48.refs_0_, ...), custom_call_target="tpu_custom_call" | custom-call | flops 1024 | bytes 1024 | tf_op jit(solution)/shard_map/half/pallas_call | solution.py:151
  58.8 2.4 %collective-permute-start.17 = (bf16[1,4,2,64,128]{4,3,2,1,0:T(8,128)(2,1)S(1)}, bf16[1,4,2,64,128]{4,3,2,1,0:T(8,128)(2,1)S(1)}, u32[]{:S(2)}, u32[]{:S(2)}) collective-permute-start(bf16[1,4,2,64,128]{4,3,2,1,0:T(8,128)(2,1)S(1)} %get-tuple-element.53), channel_id=1, source_target_pairs={{0,4},{4,0},{8,12},{12,8},{16,20},{20,16},{24,28},{28,24},{1,5},{5... | collective-permute-start | bytes 393224 | tf_op jit(solution)/shard_map/z1c4/ppermute | solution.py:224
  61.3 0.1 collective-permute-start.12
  61.4 5.4 %collective-permute-done.18.refs_1_.refs_9_ = bf16[1,4,4,64,128]{4,3,2,1,0:T(8,128)(2,1)S(1)} collective-permute-done((bf16[1,4,4,64,128]{4,3,2,1,0:T(8,128)(2,1)S(1)}, bf16[1,4,4,64,128]{4,3,2,1,0:T(8,128)(2,1)S(1)}, u32[]{:S(2)}, u32[]{:S(2)}) %collective-permute-start.18) | collective-permute-done | bytes 262176 | tf_op jit(solution)/shard_map/z4c2/ppermute | solution.py:224
  66.8 0.1 collective-permute-start.20
  66.9 2.5 %collective-permute-start.22 = (bf16[1,4,2,64,128]{4,3,2,1,0:T(8,128)(2,1)S(1)}, bf16[1,4,2,64,128]{4,3,2,1,0:T(8,128)(2,1)S(1)}, u32[]{:S(2)}, u32[]{:S(2)}) collective-permute-start(bf16[1,4,2,64,128]{4,3,2,1,0:T(8,128)(2,1)S(1)} %get-tuple-element.56), channel_id=1, source_target_pairs={{0,16},{4,20},{8,24},{12,28},{16,0},{20,4},{24,8},{28,12},{1,17},{... | collective-permute-start | bytes 393224 | tf_op jit(solution)/shard_map/z4c3/ppermute | solution.py:224
  69.4 0.1 collective-permute-start.21
  69.6 1.6 %collective-permute-start.19 = (bf16[4,1,4,64,128]{4,3,2,1,0:T(8,128)(2,1)S(1)}, bf16[4,1,4,64,128]{4,3,2,1,0:T(8,128)(2,1)S(1)}, u32[]{:S(2)}, u32[]{:S(2)}) collective-permute-start(bf16[4,1,4,64,128]{4,3,2,1,0:T(8,128)(2,1)S(1)} %merge.15.refs_2_), channel_id=1, source_target_pairs={{0,4},{4,0},{8,12},{12,8},{16,20},{20,16},{24,28},{28,24},{1,5},{5... | collective-permute-start | bytes 786440 | tf_op jit(solution)/shard_map/z1c1/ppermute | solution.py:224
  71.1 4.8 %collective-permute-done.22.refs_1_.refs_13_ = bf16[1,4,2,64,128]{4,3,2,1,0:T(8,128)(2,1)S(1)} collective-permute-done((bf16[1,4,2,64,128]{4,3,2,1,0:T(8,128)(2,1)S(1)}, bf16[1,4,2,64,128]{4,3,2,1,0:T(8,128)(2,1)S(1)}, u32[]{:S(2)}, u32[]{:S(2)}) %collective-permute-start.22) | collective-permute-done | bytes 131104 | tf_op jit(solution)/shard_map/z4c3/ppermute | solution.py:224
  75.9 3.5 %collective-permute-start.24 = (bf16[2,2,2,64,128]{4,3,2,1,0:T(8,128)(2,1)S(1)}, bf16[2,2,2,64,128]{4,3,2,1,0:T(8,128)(2,1)S(1)}, u32[]{:S(2)}, u32[]{:S(2)}) collective-permute-start(bf16[2,2,2,64,128]{4,3,2,1,0:T(8,128)(2,1)S(1)} %merge.16.refs_3_), channel_id=1, source_target_pairs={{0,8},{4,12},{8,0},{12,4},{16,24},{20,28},{24,16},{28,20},{1,9},{5... | collective-permute-start | bytes 393224 | tf_op jit(solution)/shard_map/z2c3/ppermute | solution.py:224
  79.4 1.6 %collective-permute-start.23 = (bf16[4,1,4,64,128]{4,3,2,1,0:T(8,128)(2,1)S(1)}, bf16[4,1,4,64,128]{4,3,2,1,0:T(8,128)(2,1)S(1)}, u32[]{:S(2)}, u32[]{:S(2)}) collective-permute-start(bf16[4,1,4,64,128]{4,3,2,1,0:T(8,128)(2,1)S(1)} %merge.18.refs_3_), channel_id=1, source_target_pairs={{0,4},{4,0},{8,12},{12,8},{16,20},{20,16},{24,28},{28,24},{1,5},{5... | collective-permute-start | bytes 786440 | tf_op jit(solution)/shard_map/z1c2/ppermute | solution.py:224
  81.0 2.7 %collective-permute-start.26 = (bf16[4,1,2,64,128]{4,3,2,1,0:T(8,128)(2,1)S(1)}, bf16[4,1,2,64,128]{4,3,2,1,0:T(8,128)(2,1)S(1)}, u32[]{:S(2)}, u32[]{:S(2)}) collective-permute-start(bf16[4,1,2,64,128]{4,3,2,1,0:T(8,128)(2,1)S(1)} %merge.17.refs_3_), channel_id=1, source_target_pairs={{0,16},{4,20},{8,24},{12,28},{16,0},{20,4},{24,8},{28,12},{1,17},{... | collective-permute-start | bytes 393224 | tf_op jit(solution)/shard_map/z4c4/ppermute | solution.py:224
  83.8 1.2 %collective-permute-start.25 = (bf16[4,1,2,64,128]{4,3,2,1,0:T(8,128)(2,1)S(1)}, bf16[4,1,2,64,128]{4,3,2,1,0:T(8,128)(2,1)S(1)}, u32[]{:S(2)}, u32[]{:S(2)}) collective-permute-start(bf16[4,1,2,64,128]{4,3,2,1,0:T(8,128)(2,1)S(1)} %merge.19), channel_id=1, source_target_pairs={{0,4},{4,0},{8,12},{12,8},{16,20},{20,16},{24,28},{28,24},{1,5},{5... | collective-permute-start | bytes 393224 | tf_op jit(solution)/shard_map/z1c3/ppermute | solution.py:224
  85.0 3.7 %collective-permute-done.26.refs_19_ = bf16[4,1,2,64,128]{4,3,2,1,0:T(8,128)(2,1)S(1)} collective-permute-done((bf16[4,1,2,64,128]{4,3,2,1,0:T(8,128)(2,1)S(1)}, bf16[4,1,2,64,128]{4,3,2,1,0:T(8,128)(2,1)S(1)}, u32[]{:S(2)}, u32[]{:S(2)}) %collective-permute-start.26) | collective-permute-done | bytes 131104 | tf_op jit(solution)/shard_map/z4c4/ppermute | solution.py:224
  88.7 0.3 collective-permute-done.25.refs_15_
  89.0 3.3 %combine.1 = f32[128,64,128]{2,1,0:T(8,128)} custom-call(s32[128]{0:T(128)S(1)} %copy-done.1, s32[2]{0:T(128)S(1)} %pad_add_fusion.place_ref, bf16[1,4,4,64,128]{4,3,2,1,0:T(8,128)(2,1)S(1)} %get-tuple-element.35.refs_5_.refs_0_, bf16[1,4,4,64,128]{4,3,2,1,0:T(8,128)(2,1)S(1)} %collective-permute-done.3.refs_1_, ...), custom_call_target="tpu_custom_call" | custom-call | flops 1024 | bytes 1024 | tf_op jit(solution)/shard_map/combine/pallas_call | solution.py:206
  (29 shorter events, 0.2 us)
Async XLA Ops:
  0.1 1.2 %copy-start = (bf16[1000,512]{1,0:T(8,128)(2,1)S(1)}, bf16[1000,512]{1,0:T(8,128)(2,1)}, u32[]{:S(2)}) copy-start(bf16[1000,512]{1,0:T(8,128)(2,1)} %c_ref.1) | copy-start | bytes 3072004
  9.0 12.8 %collective-permute-start.2 = (bf16[4,256,128]{2,1,0:T(8,128)(2,1)S(1)}, bf16[4,256,128]{2,1,0:T(8,128)(2,1)S(1)}, u32[]{:S(2)}, u32[]{:S(2)}) collective-permute-start(bf16[4,256,128]{2,1,0:T(8,128)(2,1)S(1)} %get-tuple-element.34), channel_id=1, source_target_pairs={{0,3},{1,2},{2,1},{3,0},{4,7},{5,6},{6,5},{7,4},{8,11},{9,10},{10,... | collective-permute-start | bytes 786440 | tf_op jit(solution)/shard_map/y1/ppermute | solution.py:224
  11.5 13.3 %collective-permute-start.1 = (bf16[4,256,128]{2,1,0:T(8,128)(2,1)S(1)}, bf16[4,256,128]{2,1,0:T(8,128)(2,1)S(1)}, u32[]{:S(2)}, u32[]{:S(2)}) collective-permute-start(bf16[4,256,128]{2,1,0:T(8,128)(2,1)S(1)} %get-tuple-element.31.refs_0_), channel_id=1, source_target_pairs={{0,2},{1,3},{2,0},{3,1},{4,6},{5,7},{6,4},{7,5},{8,10},{9,11},{10,... | collective-permute-start | bytes 786440 | tf_op jit(solution)/shard_map/y0/ppermute | solution.py:224
  19.8 5.0 %collective-permute-start = (bf16[4,256,128]{2,1,0:T(8,128)(2,1)S(1)}, bf16[4,256,128]{2,1,0:T(8,128)(2,1)S(1)}, u32[]{:S(2)}, u32[]{:S(2)}) collective-permute-start(bf16[4,256,128]{2,1,0:T(8,128)(2,1)S(1)} %get-tuple-element.33), channel_id=1, source_target_pairs={{0,1},{1,0},{2,3},{3,2},{4,5},{5,4},{6,7},{7,6},{8,9},{9,8},{10,11... | collective-permute-start | bytes 786440 | tf_op jit(solution)/shard_map/beside0/ppermute | solution.py:224
  19.9 10.5 %collective-permute-start.5 = (bf16[4,256,128]{2,1,0:T(8,128)(2,1)S(1)}, bf16[4,256,128]{2,1,0:T(8,128)(2,1)S(1)}, u32[]{:S(2)}, u32[]{:S(2)}) collective-permute-start(bf16[4,256,128]{2,1,0:T(8,128)(2,1)S(1)} %get-tuple-element.39), channel_id=1, source_target_pairs={{0,2},{1,3},{2,0},{3,1},{4,6},{5,7},{6,4},{7,5},{8,10},{9,11},{10,... | collective-permute-start | bytes 786440 | tf_op jit(solution)/shard_map/y2/ppermute | solution.py:224
  21.7 13.3 %collective-permute-start.6 = (bf16[4,256,128]{2,1,0:T(8,128)(2,1)S(1)}, bf16[4,256,128]{2,1,0:T(8,128)(2,1)S(1)}, u32[]{:S(2)}, u32[]{:S(2)}) collective-permute-start(bf16[4,256,128]{2,1,0:T(8,128)(2,1)S(1)} %get-tuple-element.40), channel_id=1, source_target_pairs={{0,3},{1,2},{2,1},{3,0},{4,7},{5,6},{6,5},{7,4},{8,11},{9,10},{10,... | collective-permute-start | bytes 786440 | tf_op jit(solution)/shard_map/y3/ppermute | solution.py:224
  21.8 14.4 %collective-permute-start.4 = (bf16[4,256,128]{2,1,0:T(8,128)(2,1)S(1)}, bf16[4,256,128]{2,1,0:T(8,128)(2,1)S(1)}, u32[]{:S(2)}, u32[]{:S(2)}) collective-permute-start(bf16[4,256,128]{2,1,0:T(8,128)(2,1)S(1)} %get-tuple-element.38), channel_id=1, source_target_pairs={{0,1},{1,0},{2,3},{3,2},{4,5},{5,4},{6,7},{7,6},{8,9},{9,8},{10,11... | collective-permute-start | bytes 786440 | tf_op jit(solution)/shard_map/beside1/ppermute | solution.py:224
  26.2 14.7 %collective-permute-start.3 = (bf16[1,4,4,64,128]{4,3,2,1,0:T(8,128)(2,1)S(1)}, bf16[1,4,4,64,128]{4,3,2,1,0:T(8,128)(2,1)S(1)}, u32[]{:S(2)}, u32[]{:S(2)}) collective-permute-start(bf16[1,4,4,64,128]{4,3,2,1,0:T(8,128)(2,1)S(1)} %get-tuple-element.36), channel_id=1, source_target_pairs={{0,16},{4,20},{8,24},{12,28},{16,0},{20,4},{24,8},{28,12},{1,17},{... | collective-permute-start | bytes 786440 | tf_op jit(solution)/shard_map/z4c0/ppermute | solution.py:224
  28.8 13.0 %collective-permute-start.10 = (bf16[4,256,128]{2,1,0:T(8,128)(2,1)S(1)}, bf16[4,256,128]{2,1,0:T(8,128)(2,1)S(1)}, u32[]{:S(2)}, u32[]{:S(2)}) collective-permute-start(bf16[4,256,128]{2,1,0:T(8,128)(2,1)S(1)} %get-tuple-element.45), channel_id=1, source_target_pairs={{0,2},{1,3},{2,0},{3,1},{4,6},{5,7},{6,4},{7,5},{8,10},{9,11},{10,... | collective-permute-start | bytes 786440 | tf_op jit(solution)/shard_map/y4/ppermute | solution.py:224
  30.4 15.9 %collective-permute-start.11 = (bf16[4,256,128]{2,1,0:T(8,128)(2,1)S(1)}, bf16[4,256,128]{2,1,0:T(8,128)(2,1)S(1)}, u32[]{:S(2)}, u32[]{:S(2)}) collective-permute-start(bf16[4,256,128]{2,1,0:T(8,128)(2,1)S(1)} %get-tuple-element.46), channel_id=1, source_target_pairs={{0,3},{1,2},{2,1},{3,0},{4,7},{5,6},{6,5},{7,4},{8,11},{9,10},{10,... | collective-permute-start | bytes 786440 | tf_op jit(solution)/shard_map/y5/ppermute | solution.py:224
  35.0 13.4 %collective-permute-start.9 = (bf16[4,256,128]{2,1,0:T(8,128)(2,1)S(1)}, bf16[4,256,128]{2,1,0:T(8,128)(2,1)S(1)}, u32[]{:S(2)}, u32[]{:S(2)}) collective-permute-start(bf16[4,256,128]{2,1,0:T(8,128)(2,1)S(1)} %get-tuple-element.44), channel_id=1, source_target_pairs={{0,1},{1,0},{2,3},{3,2},{4,5},{5,4},{6,7},{7,6},{8,9},{9,8},{10,11... | collective-permute-start | bytes 786440 | tf_op jit(solution)/shard_map/beside2/ppermute | solution.py:224
  36.1 52.9 %copy-start.1 = (s32[128]{0:T(128)S(1)}, s32[128]{0:T(128)}, u32[]{:S(2)}) copy-start(s32[128]{0:T(128)} %mirror_ref.1) | copy-start | bytes 1540
  37.5 15.1 %collective-permute-start.8 = (bf16[1,4,4,64,128]{4,3,2,1,0:T(8,128)(2,1)S(1)}, bf16[1,4,4,64,128]{4,3,2,1,0:T(8,128)(2,1)S(1)}, u32[]{:S(2)}, u32[]{:S(2)}) collective-permute-start(bf16[1,4,4,64,128]{4,3,2,1,0:T(8,128)(2,1)S(1)} %get-tuple-element.42), channel_id=1, source_target_pairs={{0,16},{4,20},{8,24},{12,28},{16,0},{20,4},{24,8},{28,12},{1,17},{... | collective-permute-start | bytes 786440 | tf_op jit(solution)/shard_map/z4c1/ppermute | solution.py:224
  40.9 12.0 %collective-permute-start.7 = (bf16[2,2,4,64,128]{4,3,2,1,0:T(8,128)(2,1)S(1)}, bf16[2,2,4,64,128]{4,3,2,1,0:T(8,128)(2,1)S(1)}, u32[]{:S(2)}, u32[]{:S(2)}) collective-permute-start(bf16[2,2,4,64,128]{4,3,2,1,0:T(8,128)(2,1)S(1)} %merge.10.refs_5_), channel_id=1, source_target_pairs={{0,8},{4,12},{8,0},{12,4},{16,24},{20,28},{24,16},{28,20},{1,9},{5... | collective-permute-start | bytes 786440 | tf_op jit(solution)/shard_map/z2c0/ppermute | solution.py:224
  41.8 15.0 %collective-permute-start.15 = (bf16[4,256,128]{2,1,0:T(8,128)(2,1)S(1)}, bf16[4,256,128]{2,1,0:T(8,128)(2,1)S(1)}, u32[]{:S(2)}, u32[]{:S(2)}) collective-permute-start(bf16[4,256,128]{2,1,0:T(8,128)(2,1)S(1)} %get-tuple-element.50), channel_id=1, source_target_pairs={{0,2},{1,3},{2,0},{3,1},{4,6},{5,7},{6,4},{7,5},{8,10},{9,11},{10,... | collective-permute-start | bytes 786440 | tf_op jit(solution)/shard_map/y6/ppermute | solution.py:224
  46.3 11.2 %collective-permute-start.16 = (bf16[4,256,128]{2,1,0:T(8,128)(2,1)S(1)}, bf16[4,256,128]{2,1,0:T(8,128)(2,1)S(1)}, u32[]{:S(2)}, u32[]{:S(2)}) collective-permute-start(bf16[4,256,128]{2,1,0:T(8,128)(2,1)S(1)} %get-tuple-element.51), channel_id=1, source_target_pairs={{0,3},{1,2},{2,1},{3,0},{4,7},{5,6},{6,5},{7,4},{8,11},{9,10},{10,... | collective-permute-start | bytes 786440 | tf_op jit(solution)/shard_map/y7/ppermute | solution.py:224
  48.5 9.0 %collective-permute-start.14 = (bf16[4,256,128]{2,1,0:T(8,128)(2,1)S(1)}, bf16[4,256,128]{2,1,0:T(8,128)(2,1)S(1)}, u32[]{:S(2)}, u32[]{:S(2)}) collective-permute-start(bf16[4,256,128]{2,1,0:T(8,128)(2,1)S(1)} %get-tuple-element.49), channel_id=1, source_target_pairs={{0,1},{1,0},{2,3},{3,2},{4,5},{5,4},{6,7},{7,6},{8,9},{9,8},{10,11... | collective-permute-start | bytes 786440 | tf_op jit(solution)/shard_map/beside3/ppermute | solution.py:224
  52.6 14.2 %collective-permute-start.18 = (bf16[1,4,4,64,128]{4,3,2,1,0:T(8,128)(2,1)S(1)}, bf16[1,4,4,64,128]{4,3,2,1,0:T(8,128)(2,1)S(1)}, u32[]{:S(2)}, u32[]{:S(2)}) collective-permute-start(bf16[1,4,4,64,128]{4,3,2,1,0:T(8,128)(2,1)S(1)} %get-tuple-element.54), channel_id=1, source_target_pairs={{0,16},{4,20},{8,24},{12,28},{16,0},{20,4},{24,8},{28,12},{1,17},{... | collective-permute-start | bytes 786440 | tf_op jit(solution)/shard_map/z4c2/ppermute | solution.py:224
  52.9 16.6 %collective-permute-start.13 = (bf16[2,2,4,64,128]{4,3,2,1,0:T(8,128)(2,1)S(1)}, bf16[2,2,4,64,128]{4,3,2,1,0:T(8,128)(2,1)S(1)}, u32[]{:S(2)}, u32[]{:S(2)}) collective-permute-start(bf16[2,2,4,64,128]{4,3,2,1,0:T(8,128)(2,1)S(1)} %merge.11.refs_3_), channel_id=1, source_target_pairs={{0,8},{4,12},{8,0},{12,4},{16,24},{20,28},{24,16},{28,20},{1,9},{5... | collective-permute-start | bytes 786440 | tf_op jit(solution)/shard_map/z2c1/ppermute | solution.py:224
  58.8 10.5 %collective-permute-start.17 = (bf16[1,4,2,64,128]{4,3,2,1,0:T(8,128)(2,1)S(1)}, bf16[1,4,2,64,128]{4,3,2,1,0:T(8,128)(2,1)S(1)}, u32[]{:S(2)}, u32[]{:S(2)}) collective-permute-start(bf16[1,4,2,64,128]{4,3,2,1,0:T(8,128)(2,1)S(1)} %get-tuple-element.53), channel_id=1, source_target_pairs={{0,4},{4,0},{8,12},{12,8},{16,20},{20,16},{24,28},{28,24},{1,5},{5... | collective-permute-start | bytes 393224 | tf_op jit(solution)/shard_map/z1c4/ppermute | solution.py:224
  61.3 18.1 %collective-permute-start.12 = (bf16[4,1,4,64,128]{4,3,2,1,0:T(8,128)(2,1)S(1)}, bf16[4,1,4,64,128]{4,3,2,1,0:T(8,128)(2,1)S(1)}, u32[]{:S(2)}, u32[]{:S(2)}) collective-permute-start(bf16[4,1,4,64,128]{4,3,2,1,0:T(8,128)(2,1)S(1)} %merge.12.refs_5_), channel_id=1, source_target_pairs={{0,4},{4,0},{8,12},{12,8},{16,20},{20,16},{24,28},{28,24},{1,5},{5... | collective-permute-start | bytes 786440 | tf_op jit(solution)/shard_map/z1c0/ppermute | solution.py:224
  66.8 12.6 %collective-permute-start.20 = (bf16[2,2,4,64,128]{4,3,2,1,0:T(8,128)(2,1)S(1)}, bf16[2,2,4,64,128]{4,3,2,1,0:T(8,128)(2,1)S(1)}, u32[]{:S(2)}, u32[]{:S(2)}) collective-permute-start(bf16[2,2,4,64,128]{4,3,2,1,0:T(8,128)(2,1)S(1)} %merge.13.refs_2_), channel_id=1, source_target_pairs={{0,8},{4,12},{8,0},{12,4},{16,24},{20,28},{24,16},{28,20},{1,9},{5... | collective-permute-start | bytes 786440 | tf_op jit(solution)/shard_map/z2c2/ppermute | solution.py:224
  66.9 9.0 %collective-permute-start.22 = (bf16[1,4,2,64,128]{4,3,2,1,0:T(8,128)(2,1)S(1)}, bf16[1,4,2,64,128]{4,3,2,1,0:T(8,128)(2,1)S(1)}, u32[]{:S(2)}, u32[]{:S(2)}) collective-permute-start(bf16[1,4,2,64,128]{4,3,2,1,0:T(8,128)(2,1)S(1)} %get-tuple-element.56), channel_id=1, source_target_pairs={{0,16},{4,20},{8,24},{12,28},{16,0},{20,4},{24,8},{28,12},{1,17},{... | collective-permute-start | bytes 393224 | tf_op jit(solution)/shard_map/z4c3/ppermute | solution.py:224
  69.4 10.0 %collective-permute-start.21 = (bf16[2,2,2,64,128]{4,3,2,1,0:T(8,128)(2,1)S(1)}, bf16[2,2,2,64,128]{4,3,2,1,0:T(8,128)(2,1)S(1)}, u32[]{:S(2)}, u32[]{:S(2)}) collective-permute-start(bf16[2,2,2,64,128]{4,3,2,1,0:T(8,128)(2,1)S(1)} %merge.14.refs_3_), channel_id=1, source_target_pairs={{0,8},{4,12},{8,0},{12,4},{16,24},{20,28},{24,16},{28,20},{1,9},{5... | collective-permute-start | bytes 393224 | tf_op jit(solution)/shard_map/z2c4/ppermute | solution.py:224
  69.6 14.2 %collective-permute-start.19 = (bf16[4,1,4,64,128]{4,3,2,1,0:T(8,128)(2,1)S(1)}, bf16[4,1,4,64,128]{4,3,2,1,0:T(8,128)(2,1)S(1)}, u32[]{:S(2)}, u32[]{:S(2)}) collective-permute-start(bf16[4,1,4,64,128]{4,3,2,1,0:T(8,128)(2,1)S(1)} %merge.15.refs_2_), channel_id=1, source_target_pairs={{0,4},{4,0},{8,12},{12,8},{16,20},{20,16},{24,28},{28,24},{1,5},{5... | collective-permute-start | bytes 786440 | tf_op jit(solution)/shard_map/z1c1/ppermute | solution.py:224
  75.9 7.8 %collective-permute-start.24 = (bf16[2,2,2,64,128]{4,3,2,1,0:T(8,128)(2,1)S(1)}, bf16[2,2,2,64,128]{4,3,2,1,0:T(8,128)(2,1)S(1)}, u32[]{:S(2)}, u32[]{:S(2)}) collective-permute-start(bf16[2,2,2,64,128]{4,3,2,1,0:T(8,128)(2,1)S(1)} %merge.16.refs_3_), channel_id=1, source_target_pairs={{0,8},{4,12},{8,0},{12,4},{16,24},{20,28},{24,16},{28,20},{1,9},{5... | collective-permute-start | bytes 393224 | tf_op jit(solution)/shard_map/z2c3/ppermute | solution.py:224
  79.4 9.5 %collective-permute-start.23 = (bf16[4,1,4,64,128]{4,3,2,1,0:T(8,128)(2,1)S(1)}, bf16[4,1,4,64,128]{4,3,2,1,0:T(8,128)(2,1)S(1)}, u32[]{:S(2)}, u32[]{:S(2)}) collective-permute-start(bf16[4,1,4,64,128]{4,3,2,1,0:T(8,128)(2,1)S(1)} %merge.18.refs_3_), channel_id=1, source_target_pairs={{0,4},{4,0},{8,12},{12,8},{16,20},{20,16},{24,28},{28,24},{1,5},{5... | collective-permute-start | bytes 786440 | tf_op jit(solution)/shard_map/z1c2/ppermute | solution.py:224
  81.0 7.6 %collective-permute-start.26 = (bf16[4,1,2,64,128]{4,3,2,1,0:T(8,128)(2,1)S(1)}, bf16[4,1,2,64,128]{4,3,2,1,0:T(8,128)(2,1)S(1)}, u32[]{:S(2)}, u32[]{:S(2)}) collective-permute-start(bf16[4,1,2,64,128]{4,3,2,1,0:T(8,128)(2,1)S(1)} %merge.17.refs_3_), channel_id=1, source_target_pairs={{0,16},{4,20},{8,24},{12,28},{16,0},{20,4},{24,8},{28,12},{1,17},{... | collective-permute-start | bytes 393224 | tf_op jit(solution)/shard_map/z4c4/ppermute | solution.py:224
  83.8 5.2 %collective-permute-start.25 = (bf16[4,1,2,64,128]{4,3,2,1,0:T(8,128)(2,1)S(1)}, bf16[4,1,2,64,128]{4,3,2,1,0:T(8,128)(2,1)S(1)}, u32[]{:S(2)}, u32[]{:S(2)}) collective-permute-start(bf16[4,1,2,64,128]{4,3,2,1,0:T(8,128)(2,1)S(1)} %merge.19), channel_id=1, source_target_pairs={{0,4},{4,0},{8,12},{12,8},{16,20},{20,16},{24,28},{28,24},{1,5},{5... | collective-permute-start | bytes 393224 | tf_op jit(solution)/shard_map/z1c3/ppermute | solution.py:224

commit v7 on v6

v7 whole, which is shorter than its diff:
```python
import functools

import jax
import jax.numpy as jnp
from jax import lax
from jax.experimental import pallas as pl
from jax.experimental.pallas import tpu as pltpu
from jax.sharding import PartitionSpec as P

LANES = 128
STEP = 64
CHUNKS = (4, 4, 4, 4)
PART = 256
MIB = 1024 * 1024
COST = pl.CostEstimate(flops=1024, bytes_accessed=1024, transcendentals=0)
IN_VMEM = pl.BlockSpec(memory_space=pltpu.VMEM)
IN_SMEM = pl.BlockSpec(memory_space=pltpu.SMEM)
ANYWHERE = pl.BlockSpec(memory_space=pl.ANY)
IN_HBM = pl.BlockSpec(memory_space=pltpu.MemorySpace.HBM)


def quarter_kernel(rows, n_mo, blocks, place_ref, x_ref, c_hbm, *refs):
    outs, (c_ref, turn_ref, held, c_sem, sems) = refs[:-5], refs[-5:]
    at = pl.program_id(0)
    step, k_all, depth = x_ref.shape
    padded = held.shape[2]
    many = PART // k_all

    @pl.when(at == 0)
    def _():
        copy = pltpu.make_async_copy(c_hbm, c_ref, c_sem)
        copy.start()
        to = lax.broadcasted_iota(jnp.int32, (PART, PART), 0)
        source = lax.broadcasted_iota(jnp.int32, (PART, PART), 1)
        turn_ref[...] = (source == to % many * k_all + to // many).astype(jnp.float32).astype(jnp.bfloat16)
        copy.wait()

    x = x_ref[...].reshape(step * k_all, depth)
    product = jnp.dot(x, c_ref[...], preferred_element_type=jnp.float32)
    line = lax.broadcasted_iota(jnp.int32, product.shape, 0)
    product = jnp.where(line < (rows - at * step) * k_all, product, 0.0).astype(jnp.bfloat16)
    for part in range(step // many):
        lines = jnp.dot(
            turn_ref[...], product[part * PART : (part + 1) * PART], preferred_element_type=jnp.float32
        ).astype(jnp.bfloat16)
        here = pl.ds(pl.multiple_of(at * step + part * many, many), many)
        for k in range(k_all):
            for d in range(n_mo):
                held[d, k, here] = lines[k * many : (k + 1) * many, d * LANES : (d + 1) * LANES]
    here = pl.ds(pl.multiple_of(at * step, step), step)
    for n, (out, (o, first)) in enumerate(zip(outs, blocks)):
        mine = held.at[place_ref[0] ^ o, pl.ds(first, out.shape[0])]
        pltpu.make_async_copy(mine.at[:, here], out.at[:, here], sems.at[n]).start()

    @pl.when(at == padded // step - 1)
    def _():
        for n, (out, (o, first)) in enumerate(zip(outs, blocks)):
            mine = held.at[place_ref[0] ^ o, pl.ds(first, out.shape[0])]
            pltpu.make_async_copy(mine, out, sems.at[n]).wait()


def quarter_of(place, by_r, coeffs, n_mo, padded):
    rows, k_all, depth = by_r.shape
    orbitals = coeffs.shape[1]
    blocks = [(0, 0), (1, 0)] + [(o, sum(CHUNKS[:c])) for c in range(len(CHUNKS)) for o in range(2, n_mo)]
    sizes = [k_all] * 2 + [kc for kc in CHUNKS for _ in range(2, n_mo)]
    outs = [jax.ShapeDtypeStruct((kc, padded, LANES), jnp.bfloat16) for kc in sizes]
    out = pl.pallas_call(
        functools.partial(quarter_kernel, rows, n_mo, blocks),
        grid_spec=pltpu.PrefetchScalarGridSpec(
            num_scalar_prefetch=1,
            grid=(padded // STEP,),
            in_specs=[pl.BlockSpec((STEP, k_all, depth), lambda r, place: (r, 0, 0)), IN_HBM],
            out_specs=[IN_HBM] * len(outs),
            scratch_shapes=[
                pltpu.VMEM((depth, orbitals), jnp.bfloat16),
                pltpu.VMEM((PART, PART), jnp.bfloat16),
                pltpu.VMEM((n_mo, k_all, padded, LANES), jnp.bfloat16),
                pltpu.SemaphoreType.DMA,
                pltpu.SemaphoreType.DMA((len(outs),)),
            ],
        ),
        out_shape=outs,
        compiler_params=pltpu.CompilerParams(vmem_limit_bytes=50 * MIB),
        cost_estimate=COST,
        name="quarter",
    )(place, by_r, coeffs)
    far = n_mo - 2
    return out[:2], [out[2 + far * c : 2 + far * (c + 1)] for c in range(len(CHUNKS))]


def turn_kernel(rows, c_ref, *refs):
    out_ref = refs[-1]
    n_mo, orbitals, padded = out_ref.shape
    none = jnp.zeros((padded - rows, orbitals), jnp.float32)
    for n in range(n_mo):
        part = c_ref[n * rows : (n + 1) * rows, :].astype(jnp.float32)
        out_ref[n] = jnp.concatenate([part, none], axis=0).T.astype(jnp.bfloat16)


def turn(coeffs, n_mo, padded, later, after):
    depth, orbitals = coeffs.shape
    out = pl.pallas_call(
        functools.partial(turn_kernel, depth // n_mo),
        in_specs=[IN_VMEM] + [IN_HBM] * len(later) + [ANYWHERE] * len(after),
        out_specs=[IN_HBM] * len(later) + [IN_VMEM],
        out_shape=[jax.ShapeDtypeStruct(x.shape, x.dtype) for x in later]
        + [jax.ShapeDtypeStruct((n_mo, orbitals, padded), jnp.bfloat16)],
        input_output_aliases={1 + n: n for n in range(len(later))},
        compiler_params=pltpu.CompilerParams(vmem_limit_bytes=24 * MIB),
        cost_estimate=COST,
        name="turn",
    )(coeffs, *later, *after)
    return out[-1], list(out[:-1])


def half_kernel(n_mo, first, owners, place_ref, *refs):
    blocks, t_ref, held = refs[:n_mo], refs[n_mo], refs[-1]
    outs = refs[-1 - len(owners) : -1]
    kc, block, lanes = outs[0].shape[2:]
    firsts = [first if x.shape[0] > kc else 0 for x in blocks]
    columns = [jnp.concatenate([x[at + k] for k in range(kc)], axis=1) for x, at in zip(blocks, firsts)]
    turned = [t_ref[place_ref[0] ^ o] for o in range(n_mo)]
    held[...] = jnp.dot(
        jnp.concatenate(turned, axis=1), jnp.concatenate(columns, axis=0), preferred_element_type=jnp.float32
    )
    for out, its in zip(outs, owners):
        for at, o in enumerate(its):
            start = pl.multiple_of((place_ref[1] ^ o) * block, block)
            for k in range(kc):
                out[0, at, k] = held[pl.ds(start, block), k * lanes : (k + 1) * lanes].astype(jnp.bfloat16)


def half_of(place, blocks, turned, first, owners, after):
    n_mo, orbitals, _ = turned.shape
    kc, _, lanes = blocks[-1].shape
    block = orbitals // sum(len(its) for its in owners)
    return pl.pallas_call(
        functools.partial(half_kernel, n_mo, first, owners),
        in_specs=[IN_SMEM] + [IN_VMEM] * (n_mo + 1) + [ANYWHERE] * len(after),
        out_specs=[IN_VMEM] * len(owners),
        out_shape=[jax.ShapeDtypeStruct((1, len(its), kc, block, lanes), jnp.bfloat16) for its in owners],
        scratch_shapes=[pltpu.VMEM((orbitals, kc * lanes), jnp.float32)],
        compiler_params=pltpu.CompilerParams(vmem_limit_bytes=24 * MIB),
        cost_estimate=COST,
        name="half",
    )(place, *blocks, turned, *after)


def merge_kernel(picks, *refs):
    at = 0
    for x, pick in zip(refs, picks):
        for i in range(x.shape[0]):
            for n, o in enumerate(pick):
                refs[-1][at, n] = x[i, o]
            at += 1


def merge(parts, picks, after):
    shape = (sum(x.shape[0] for x in parts), len(picks[0]), *parts[0].shape[2:])
    return pl.pallas_call(
        functools.partial(merge_kernel, picks),
        in_specs=[IN_VMEM] * len(parts) + [ANYWHERE] * len(after),
        out_specs=IN_VMEM,
        out_shape=jax.ShapeDtypeStruct(shape, jnp.bfloat16),
        compiler_params=pltpu.CompilerParams(vmem_limit_bytes=24 * MIB),
        cost_estimate=COST,
        name="merge",
    )(*parts, *after)


def combine_kernel(sources, k_all, per_step, mirror_ref, place_ref, *refs):
    pieces, out_ref, held = refs[:-2], refs[-2], refs[-1]
    step = pl.program_id(0)

    @pl.when(step == 0)
    def _():
        for piece, (offsets, first) in zip(pieces, sources):
            for n, offset in enumerate(offsets):
                row = (place_ref[1] ^ offset) * k_all + first
                held[pl.ds(row, piece.shape[2])] = piece[n, 0]

    for n in range(per_step):
        k = step * per_step + n
        out_ref[n] = 0.5 * (held[k].astype(jnp.float32) + held[mirror_ref[k]].astype(jnp.float32))


def combine(pieces, sources, mirror, place, n_pair):
    block, lanes = pieces[0].shape[-2:]
    k_all = sum(CHUNKS)
    rows = n_pair * k_all
    per_step = max(1, 32 * 64 // block)
    return pl.pallas_call(
        functools.partial(combine_kernel, sources, k_all, per_step),
        grid_spec=pltpu.PrefetchScalarGridSpec(
            num_scalar_prefetch=2,
            grid=(rows // per_step,),
            in_specs=[IN_VMEM] * len(pieces),
            out_specs=pl.BlockSpec((per_step, block, lanes), lambda k, m, place: (k, 0, 0)),
            scratch_shapes=[pltpu.VMEM((rows, block, lanes), jnp.bfloat16)],
        ),
        out_shape=jax.ShapeDtypeStruct((rows, block, lanes), jnp.float32),
        compiler_params=pltpu.CompilerParams(vmem_limit_bytes=24 * MIB),
        cost_estimate=COST,
        name="combine",
    )(mirror, place, *pieces)


def flipped(x, axis, size, offset, name):
    with jax.named_scope(name):
        return lax.ppermute(x, axis, [(i, i ^ offset) for i in range(size)])


def on_device(n_pair, n_mo, integrals, coeffs, mirror):
    rows = integrals.shape[1]
    padded = -(-rows // STEP) * STEP
    n_near = n_pair // 2
    by_r = jnp.transpose(integrals, (1, 0, 2))
    place = jnp.stack([lax.axis_index("mo"), lax.axis_index("pair")]).astype(jnp.int32)
    (own, beside), queue = quarter_of(place, by_r, coeffs, n_mo, padded)
    beside = flipped(beside, "mo", n_mo, 1, "beside")
    last = len(CHUNKS) - 1
    firsts = [sum(CHUNKS[:c]) for c in range(last + 1)]
    down = [1 << n for n in reversed(range(n_pair.bit_length() - 1))]
    orders = [down] * last + [down[::-1]]
    turned, parts, owners, offsets, token = None, [[] for _ in CHUNKS], [[] for _ in CHUNKS], [[] for _ in CHUNKS], []

    def arrive(c):
        return [flipped(x, "mo", n_mo, o, f"y{2 * c + o - 2}") for o, x in enumerate(queue[c], 2)]

    arrived = [arrive(0)]
    turned, queue[1] = turn(coeffs, n_mo, padded, queue[1], arrived[0][:1])
    arrived += [arrive(c) for c in range(1, last + 1)]

    steps = [(c, c, 0) for c in range(last + 1)]
    for n in range(1, len(down)):
        steps += [(c + n + (0.5 - n / 10 if c + n == last else n / 10), c, n) for c in range(last)]
        steps.append((last + n - (0.55 if n == 1 else 0.95), last, n))
    for _, c, level in sorted(steps):
        flips = orders[c]
        flip, gone = flips[level], sum(flips[:level])
        left = [o for o in range(n_pair) if not o & gone]
        kept, sent = [o for o in left if not o & flip], [o for o in left if o & flip]
        if level == 0:
            keep, message = half_of(place, [own, beside, *arrived[c]], turned, firsts[c], [kept, sent], token)
            parts[c], owners[c], offsets[c] = [keep], [kept], [[0]]
        else:
            after = token + (parts[c - 1][-1:] if level == len(flips) - 1 and 0 < c < last else [])
            message = merge(parts[c], [[its.index(o) for o in sent] for its in owners[c]], after)
        token = [message]
        offsets[c].append([o ^ flip for group in offsets[c] for o in group])
        owners[c].append([o ^ flip for o in sent])
        parts[c].append(flipped(message, "pair", n_pair, flip, f"z{flip}c{c}"))
    pieces = [x for chunk in parts for x in chunk]
    sources = [(tuple(group), first) for chunk, first in zip(offsets, firsts) for group in chunk]
    return combine(pieces, sources, mirror, place, n_pair)


def solution(mesh):
    return jax.shard_map(
        functools.partial(on_device, mesh.shape["pair"], mesh.shape["mo"]),
        mesh=mesh,
        in_specs=(P("pair", "mo", None), P(), P()),
        out_specs=P(None, "pair", "mo"),
        check_vma=False,
    )
```

time: 92.5 us -> 104 us (1.12)
  waiting for transfers between devices: 27 us -> 56.3 us
  starting transfers between devices: 39.2 us -> 25.5 us
  Pallas kernels: 24.6 us -> 19.2 us
  local copies, waits for them, and re-layouts: 1.22 us -> 2.45 us
    ppermute x27 -> x21, waiting for transfers between devices: 27 us -> 56.3 us  [flipped(): return lax.ppermute(x, axis, [(i, i ^ offset) for i in range(size)])]
    ppermute x27 -> x21, starting transfers between devices: 39.2 us -> 25.5 us  [flipped(): return lax.ppermute(x, axis, [(i, i ^ offset) for i in range(size)])]
    pallas_call x6 -> x5, Pallas kernels: 20.8 us -> 15.4 us  [the longest x1 10.2 us: quarter_of(): pl.pallas_call(functools.partial(quarter_kernel, rows, n_mo, blocks), gri...]
    unnamed x4 -> x8, local copies, waits for them, and re-layouts: 1.22 us -> 2.45 us
  transfers between devices with their start and end apart: 27 -> 21, of which waited for: 11 -> 10; matrix products, arithmetic and copies ran while one was open for 0% -> 0% of each run, Pallas kernels for 15% -> 6%
where the time goes in v7:
time: 104 us
  waiting for transfers between devices  56.3 us (54%)
  starting transfers between devices  25.5 us (25%)
  Pallas kernels  19.2 us (18%)
  local copies, waits for them, and re-layouts  2.45 us (2%)
    ppermute x21, waiting for transfers between devices, flipped(): return lax.ppermute(x, axis, [(i, i ^ offset) for i in range(size)])  56.3 us
    ppermute x21, starting transfers between devices, flipped(): return lax.ppermute(x, axis, [(i, i ^ offset) for i in range(size)])  25.5 us
    pallas_call x1, Pallas kernels, quarter_of(): pl.pallas_call(functools.partial(quarter_kernel, rows, n_mo, blocks), gri...  10.2 us
    pallas_call x4, Pallas kernels, half_of(): pl.pallas_call(functools.partial(half_kernel, n_mo, first, owners), in_sp...  5.2 us
    pallas_call x1, Pallas kernels, combine(): pl.pallas_call(functools.partial(combine_kernel, sources, k_all, per_step...  3.28 us
    unnamed x8, local copies, waits for them, and re-layouts  2.45 us
  transfers between devices with their start and end apart: 21, of which 10 were waited for; matrix products, arithmetic and copies ran while one was open for 0% of the time, Pallas kernels for 6%

profile of v7, /device:TPU:0, one launch (start us, length us, event | category | flops | bytes accessed | tf_op | source)
XLA Modules:
  0.0 103.7 jit_solution(7754990197925404585)
XLA Ops:
  0.0 0.1 pad_add_fusion.place_ref
  0.1 1.2 %copy-done.2 = bf16[1000,512]{1,0:T(8,128)(2,1)S(1)} copy-done((bf16[1000,512]{1,0:T(8,128)(2,1)S(1)}, bf16[1000,512]{1,0:T(8,128)(2,1)}, u32[]{:S(2)}) %copy-start.2) | copy-done | bytes 1024024
  1.3 10.2 %quarter.1 = (bf16[16,256,128]{2,1,0:T(8,128)(2,1)}, bf16[16,256,128]{2,1,0:T(8,128)(2,1)}, bf16[4,256,128]{2,1,0:T(8,128)(2,1)S(1)}, bf16[4,256,128]{2,1,0:T(8,...) custom-call(s32[2]{0:T(128)S(1)} %pad_add_fusion.place_ref, ...), custom_call_target="tpu_custom_call" | custom-call | flops 1024 | bytes 1024 | tf_op jit(solution)/shard_map/quarter/pallas_call | solution.py:68
  11.5 0.0 copy-start.1
  11.6 0.5 collective-permute-start
  12.1 2.6 %collective-permute-start.1 = (bf16[4,256,128]{2,1,0:T(8,128)(2,1)S(1)}, bf16[4,256,128]{2,1,0:T(8,128)(2,1)S(1)}, u32[]{:S(2)}, u32[]{:S(2)}) collective-permute-start(bf16[4,256,128]{2,1,0:T(8,128)(2,1)S(1)} %get-tuple-element.28), channel_id=1, source_target_pairs={{0,2},{1,3},{2,0},{3,1},{4,6},{5,7},{6,4},{7,5},{8,10},{9,11},{10,... | collective-permute-start | bytes 786440 | tf_op jit(solution)/shard_map/y0/ppermute | solution.py:211
  14.7 0.1 collective-permute-start.2
  14.7 7.1 %collective-permute-done.1.refs_2_ = bf16[4,256,128]{2,1,0:T(8,128)(2,1)S(1)} collective-permute-done((bf16[4,256,128]{2,1,0:T(8,128)(2,1)S(1)}, bf16[4,256,128]{2,1,0:T(8,128)(2,1)S(1)}, u32[]{:S(2)}, u32[]{:S(2)}) %collective-permute-start.1) | collective-permute-done | bytes 262176 | tf_op jit(solution)/shard_map/y0/ppermute | solution.py:211
  21.8 0.4 turn.1
  22.2 2.0 %collective-permute-start.4 = (bf16[4,256,128]{2,1,0:T(8,128)(2,1)S(1)}, bf16[4,256,128]{2,1,0:T(8,128)(2,1)S(1)}, u32[]{:S(2)}, u32[]{:S(2)}) collective-permute-start(bf16[4,256,128]{2,1,0:T(8,128)(2,1)S(1)} %get-tuple-element.35), channel_id=1, source_target_pairs={{0,2},{1,3},{2,0},{3,1},{4,6},{5,7},{6,4},{7,5},{8,10},{9,11},{10,... | collective-permute-start | bytes 786440 | tf_op jit(solution)/shard_map/y2/ppermute | solution.py:211
  24.2 2.7 %collective-permute-done.2.refs_3_ = bf16[4,256,128]{2,1,0:T(8,128)(2,1)S(1)} collective-permute-done((bf16[4,256,128]{2,1,0:T(8,128)(2,1)S(1)}, bf16[4,256,128]{2,1,0:T(8,128)(2,1)S(1)}, u32[]{:S(2)}, u32[]{:S(2)}) %collective-permute-start.2) | collective-permute-done | bytes 262176 | tf_op jit(solution)/shard_map/y1/ppermute | solution.py:211
  26.9 0.0 collective-permute-done.refs_1_
  26.9 1.2 %copy-done = bf16[16,256,128]{2,1,0:T(8,128)(2,1)S(1)} copy-done((bf16[16,256,128]{2,1,0:T(8,128)(2,1)S(1)}, bf16[16,256,128]{2,1,0:T(8,128)(2,1)}, u32[]{:S(2)}) %copy-start) | copy-done | bytes 1048600
  28.2 1.3 %half.4 = (bf16[1,4,4,64,128]{4,3,2,1,0:T(8,128)(2,1)S(1)}, bf16[1,4,4,64,128]{4,3,2,1,0:T(8,128)(2,1)S(1)}) custom-call(s32[2]{0:T(128)S(1)} %pad_add_fusion.place_ref, bf16[16,256,128]{2,1,0:T(8,128)(2,1)S(1)} %copy-done, bf16[16,256,128]{2,1,0:T(8,128)(2,1)S(1)} %collective-permute-done.refs_1_, bf16[4,256,128]{2,1,0:T(8,128)(2,1)S(1)} %collective-permute-done.1.refs_2_, ...), custom_call_target="tpu_custom_call" | custom-call | flops 1024 | bytes 1024 | tf_op jit(solution)/shard_map/half/pallas_call | solution.py:138
  29.5 2.7 %collective-permute-start.3 = (bf16[1,4,4,64,128]{4,3,2,1,0:T(8,128)(2,1)S(1)}, bf16[1,4,4,64,128]{4,3,2,1,0:T(8,128)(2,1)S(1)}, u32[]{:S(2)}, u32[]{:S(2)}) collective-permute-start(bf16[1,4,4,64,128]{4,3,2,1,0:T(8,128)(2,1)S(1)} %get-tuple-element.34.refs_5_), channel_id=1, source_target_pairs={{0,16},{4,20},{8,24},{12,28},{16,0},{20,4},{24,8},{28,12},{1,17},{... | collective-permute-start | bytes 786440 | tf_op jit(solution)/shard_map/z4c0/ppermute | solution.py:211
  32.2 1.5 %collective-permute-start.8 = (bf16[4,256,128]{2,1,0:T(8,128)(2,1)S(1)}, bf16[4,256,128]{2,1,0:T(8,128)(2,1)S(1)}, u32[]{:S(2)}, u32[]{:S(2)}) collective-permute-start(bf16[4,256,128]{2,1,0:T(8,128)(2,1)S(1)} %get-tuple-element.39), channel_id=1, source_target_pairs={{0,2},{1,3},{2,0},{3,1},{4,6},{5,7},{6,4},{7,5},{8,10},{9,11},{10,... | collective-permute-start | bytes 786440 | tf_op jit(solution)/shard_map/y4/ppermute | solution.py:211
  33.7 0.3 collective-permute-start.9
  34.0 0.0 collective-permute-done.4.refs_2_
  34.0 4.2 %collective-permute-done.5.refs_3_ = bf16[4,256,128]{2,1,0:T(8,128)(2,1)S(1)} collective-permute-done((bf16[4,256,128]{2,1,0:T(8,128)(2,1)S(1)}, bf16[4,256,128]{2,1,0:T(8,128)(2,1)S(1)}, u32[]{:S(2)}, u32[]{:S(2)}) %collective-permute-start.5) | collective-permute-done | bytes 262176 | tf_op jit(solution)/shard_map/y3/ppermute | solution.py:211
  38.2 1.3 %half.5 = (bf16[1,4,4,64,128]{4,3,2,1,0:T(8,128)(2,1)S(1)}, bf16[1,4,4,64,128]{4,3,2,1,0:T(8,128)(2,1)S(1)}) custom-call(s32[2]{0:T(128)S(1)} %pad_add_fusion.place_ref, bf16[16,256,128]{2,1,0:T(8,128)(2,1)S(1)} %copy-done, bf16[16,256,128]{2,1,0:T(8,128)(2,1)S(1)} %collective-permute-done.refs_1_, bf16[4,256,128]{2,1,0:T(8,128)(2,1)S(1)} %collective-permute-done.4.refs_2_, ...), custom_call_target="tpu_custom_call" | custom-call | flops 1024 | bytes 1024 | tf_op jit(solution)/shard_map/half/pallas_call | solution.py:138
  39.5 2.7 %collective-permute-start.7 = (bf16[1,4,4,64,128]{4,3,2,1,0:T(8,128)(2,1)S(1)}, bf16[1,4,4,64,128]{4,3,2,1,0:T(8,128)(2,1)S(1)}, u32[]{:S(2)}, u32[]{:S(2)}) collective-permute-start(bf16[1,4,4,64,128]{4,3,2,1,0:T(8,128)(2,1)S(1)} %get-tuple-element.37.refs_2_), channel_id=1, source_target_pairs={{0,16},{4,20},{8,24},{12,28},{16,0},{20,4},{24,8},{28,12},{1,17},{... | collective-permute-start | bytes 786440 | tf_op jit(solution)/shard_map/z4c1/ppermute | solution.py:211
  42.2 8.7 %collective-permute-done.3.refs_1_ = bf16[1,4,4,64,128]{4,3,2,1,0:T(8,128)(2,1)S(1)} collective-permute-done((bf16[1,4,4,64,128]{4,3,2,1,0:T(8,128)(2,1)S(1)}, bf16[1,4,4,64,128]{4,3,2,1,0:T(8,128)(2,1)S(1)}, u32[]{:S(2)}, u32[]{:S(2)}) %collective-permute-start.3) | collective-permute-done | bytes 262176 | tf_op jit(solution)/shard_map/z4c0/ppermute | solution.py:211
  50.9 0.6 collective-permute-start.6
  51.4 1.5 %collective-permute-start.12 = (bf16[4,256,128]{2,1,0:T(8,128)(2,1)S(1)}, bf16[4,256,128]{2,1,0:T(8,128)(2,1)S(1)}, u32[]{:S(2)}, u32[]{:S(2)}) collective-permute-start(bf16[4,256,128]{2,1,0:T(8,128)(2,1)S(1)} %get-tuple-element.42), channel_id=1, source_target_pairs={{0,2},{1,3},{2,0},{3,1},{4,6},{5,7},{6,4},{7,5},{8,10},{9,11},{10,... | collective-permute-start | bytes 786440 | tf_op jit(solution)/shard_map/y6/ppermute | solution.py:211
  52.9 0.0 collective-permute-done.9.refs_3_
  53.0 1.3 %half.6 = (bf16[1,4,4,64,128]{4,3,2,1,0:T(8,128)(2,1)S(1)}, bf16[1,4,4,64,128]{4,3,2,1,0:T(8,128)(2,1)S(1)}) custom-call(s32[2]{0:T(128)S(1)} %pad_add_fusion.place_ref, bf16[16,256,128]{2,1,0:T(8,128)(2,1)S(1)} %copy-done.1, bf16[16,256,128]{2,1,0:T(8,128)(2,1)S(1)} %collective-permute-done.refs_1_, ...), custom_call_target="tpu_custom_call" | custom-call | flops 1024 | bytes 1024 | tf_op jit(solution)/shard_map/half/pallas_call | solution.py:138
  54.3 3.4 %collective-permute-start.15 = (bf16[1,4,4,64,128]{4,3,2,1,0:T(8,128)(2,1)S(1)}, bf16[1,4,4,64,128]{4,3,2,1,0:T(8,128)(2,1)S(1)}, u32[]{:S(2)}, u32[]{:S(2)}) collective-permute-start(bf16[1,4,4,64,128]{4,3,2,1,0:T(8,128)(2,1)S(1)} %get-tuple-element.41.refs_2_), channel_id=1, source_target_pairs={{0,16},{4,20},{8,24},{12,28},{16,0},{20,4},{24,8},{28,12},{1,17},{... | collective-permute-start | bytes 786440 | tf_op jit(solution)/shard_map/z4c2/ppermute | solution.py:211
  57.7 0.0 collective-permute-done.7.refs_1_.refs_5_
  57.8 0.1 collective-permute-start.11
  57.9 5.7 %collective-permute-done.6.refs_2_ = bf16[2,2,4,64,128]{4,3,2,1,0:T(8,128)(2,1)S(1)} collective-permute-done((bf16[2,2,4,64,128]{4,3,2,1,0:T(8,128)(2,1)S(1)}, bf16[2,2,4,64,128]{4,3,2,1,0:T(8,128)(2,1)S(1)}, u32[]{:S(2)}, u32[]{:S(2)}) %collective-permute-start.6) | collective-permute-done | bytes 262176 | tf_op jit(solution)/shard_map/z2c0/ppermute | solution.py:211
  63.6 1.6 %collective-permute-start.10 = (bf16[4,1,4,64,128]{4,3,2,1,0:T(8,128)(2,1)S(1)}, bf16[4,1,4,64,128]{4,3,2,1,0:T(8,128)(2,1)S(1)}, u32[]{:S(2)}, u32[]{:S(2)}) collective-permute-start(bf16[4,1,4,64,128]{4,3,2,1,0:T(8,128)(2,1)S(1)} %merge.10.refs_5_), channel_id=1, source_target_pairs={{0,4},{4,0},{8,12},{12,8},{16,20},{20,16},{24,28},{28,24},{1,5},{5... | collective-permute-start | bytes 786440 | tf_op jit(solution)/shard_map/z1c0/ppermute | solution.py:211
  65.2 0.0 collective-permute-done.12.refs_2_
  65.2 0.0 collective-permute-done.13.refs_3_
  65.2 1.3 %half.7 = (bf16[1,4,4,64,128]{4,3,2,1,0:T(8,128)(2,1)S(1)}, bf16[1,4,4,64,128]{4,3,2,1,0:T(8,128)(2,1)S(1)}) custom-call(s32[2]{0:T(128)S(1)} %pad_add_fusion.place_ref, bf16[16,256,128]{2,1,0:T(8,128)(2,1)S(1)} %copy-done.1, bf16[16,256,128]{2,1,0:T(8,128)(2,1)S(1)} %collective-permute-done.refs_1_, ...), custom_call_target="tpu_custom_call" | custom-call | flops 1024 | bytes 1024 | tf_op jit(solution)/shard_map/half/pallas_call | solution.py:138
  66.5 0.6 collective-permute-start.17
  67.1 6.0 %collective-permute-done.11.refs_2_.refs_6_ = bf16[2,2,4,64,128]{4,3,2,1,0:T(8,128)(2,1)S(1)} collective-permute-done((bf16[2,2,4,64,128]{4,3,2,1,0:T(8,128)(2,1)S(1)}, bf16[2,2,4,64,128]{4,3,2,1,0:T(8,128)(2,1)S(1)}, u32[]{:S(2)}, u32[]{:S(2)}) %collective-permute-start.11) | collective-permute-done | bytes 262176 | tf_op jit(solution)/shard_map/z2c1/ppermute | solution.py:211
  73.1 0.0 collective-permute-done.15.refs_1_.refs_9_
  73.1 4.3 %collective-permute-done.17.refs_1_.refs_13_ = bf16[1,4,4,64,128]{4,3,2,1,0:T(8,128)(2,1)S(1)} collective-permute-done((bf16[1,4,4,64,128]{4,3,2,1,0:T(8,128)(2,1)S(1)}, bf16[1,4,4,64,128]{4,3,2,1,0:T(8,128)(2,1)S(1)}, u32[]{:S(2)}, u32[]{:S(2)}) %collective-permute-start.17) | collective-permute-done | bytes 262176 | tf_op jit(solution)/shard_map/z1c3/ppermute | solution.py:211
  77.4 0.1 collective-permute-start.18
  77.5 2.0 %collective-permute-start.16 = (bf16[2,2,4,64,128]{4,3,2,1,0:T(8,128)(2,1)S(1)}, bf16[2,2,4,64,128]{4,3,2,1,0:T(8,128)(2,1)S(1)}, u32[]{:S(2)}, u32[]{:S(2)}) collective-permute-start(bf16[2,2,4,64,128]{4,3,2,1,0:T(8,128)(2,1)S(1)} %merge.12.refs_2_), channel_id=1, source_target_pairs={{0,8},{4,12},{8,0},{12,4},{16,24},{20,28},{24,16},{28,20},{1,9},{5... | collective-permute-start | bytes 786440 | tf_op jit(solution)/shard_map/z2c2/ppermute | solution.py:211
  79.5 1.5 %collective-permute-start.14 = (bf16[4,1,4,64,128]{4,3,2,1,0:T(8,128)(2,1)S(1)}, bf16[4,1,4,64,128]{4,3,2,1,0:T(8,128)(2,1)S(1)}, u32[]{:S(2)}, u32[]{:S(2)}) collective-permute-start(bf16[4,1,4,64,128]{4,3,2,1,0:T(8,128)(2,1)S(1)} %merge.11.refs_2_), channel_id=1, source_target_pairs={{0,4},{4,0},{8,12},{12,8},{16,20},{20,16},{24,28},{28,24},{1,5},{5... | collective-permute-start | bytes 786440 | tf_op jit(solution)/shard_map/z1c1/ppermute | solution.py:211
  81.1 8.5 %collective-permute-done.18.refs_2_.refs_14_ = bf16[2,2,4,64,128]{4,3,2,1,0:T(8,128)(2,1)S(1)} collective-permute-done((bf16[2,2,4,64,128]{4,3,2,1,0:T(8,128)(2,1)S(1)}, bf16[2,2,4,64,128]{4,3,2,1,0:T(8,128)(2,1)S(1)}, u32[]{:S(2)}, u32[]{:S(2)}) %collective-permute-start.18) | collective-permute-done | bytes 262176 | tf_op jit(solution)/shard_map/z2c3/ppermute | solution.py:211
  89.6 0.1 collective-permute-start.20
  89.7 3.5 %collective-permute-done.16.refs_2_.refs_10_ = bf16[2,2,4,64,128]{4,3,2,1,0:T(8,128)(2,1)S(1)} collective-permute-done((bf16[2,2,4,64,128]{4,3,2,1,0:T(8,128)(2,1)S(1)}, bf16[2,2,4,64,128]{4,3,2,1,0:T(8,128)(2,1)S(1)}, u32[]{:S(2)}, u32[]{:S(2)}) %collective-permute-start.16) | collective-permute-done | bytes 262176 | tf_op jit(solution)/shard_map/z2c2/ppermute | solution.py:211
  93.2 0.0 collective-permute-done.14.refs_4_.refs_7_
  93.2 1.6 %collective-permute-start.19 = (bf16[4,1,4,64,128]{4,3,2,1,0:T(8,128)(2,1)S(1)}, bf16[4,1,4,64,128]{4,3,2,1,0:T(8,128)(2,1)S(1)}, u32[]{:S(2)}, u32[]{:S(2)}) collective-permute-start(bf16[4,1,4,64,128]{4,3,2,1,0:T(8,128)(2,1)S(1)} %merge.15), channel_id=1, source_target_pairs={{0,4},{4,0},{8,12},{12,8},{16,20},{20,16},{24,28},{28,24},{1,5},{5... | collective-permute-start | bytes 786440 | tf_op jit(solution)/shard_map/z1c2/ppermute | solution.py:211
  94.8 5.6 %collective-permute-done.20.refs_15_ = bf16[4,1,4,64,128]{4,3,2,1,0:T(8,128)(2,1)S(1)} collective-permute-done((bf16[4,1,4,64,128]{4,3,2,1,0:T(8,128)(2,1)S(1)}, bf16[4,1,4,64,128]{4,3,2,1,0:T(8,128)(2,1)S(1)}, u32[]{:S(2)}, u32[]{:S(2)}) %collective-permute-start.20) | collective-permute-done | bytes 262176 | tf_op jit(solution)/shard_map/z4c3/ppermute | solution.py:211
  100.5 3.3 %combine.1 = f32[128,64,128]{2,1,0:T(8,128)} custom-call(s32[128]{0:T(128)S(1)} %copy-done.3, s32[2]{0:T(128)S(1)} %pad_add_fusion.place_ref, bf16[1,4,4,64,128]{4,3,2,1,0:T(8,128)(2,1)S(1)} %get-tuple-element.33.refs_0_, bf16[1,4,4,64,128]{4,3,2,1,0:T(8,128)(2,1)S(1)} %collective-permute-done.3.refs_1_, ...), custom_call_target="tpu_custom_call" | custom-call | flops 1024 | bytes 1024 | tf_op jit(solution)/shard_map/combine/pallas_call | solution.py:193
  (18 shorter events, 0.2 us)
Async XLA Ops:
  0.1 1.2 %copy-start.2 = (bf16[1000,512]{1,0:T(8,128)(2,1)S(1)}, bf16[1000,512]{1,0:T(8,128)(2,1)}, u32[]{:S(2)}) copy-start(bf16[1000,512]{1,0:T(8,128)(2,1)} %c_ref.1) | copy-start | bytes 3072004
  11.5 41.4 %copy-start.1 = (bf16[16,256,128]{2,1,0:T(8,128)(2,1)S(1)}, bf16[16,256,128]{2,1,0:T(8,128)(2,1)}, u32[]{:S(2)}) copy-start(bf16[16,256,128]{2,1,0:T(8,128)(2,1)} %get-tuple-element.26.refs_0_) | copy-start | bytes 3145732
  11.6 15.4 %collective-permute-start = (bf16[16,256,128]{2,1,0:T(8,128)(2,1)}, bf16[16,256,128]{2,1,0:T(8,128)(2,1)S(1)}, u32[]{:S(2)}, u32[]{:S(2)}) collective-permute-start(bf16[16,256,128]{2,1,0:T(8,128)(2,1)} %get-tuple-element.27), channel_id=1, source_target_pairs={{0,1},{1,0},{2,3},{3,2},{4,5},{5,4},{6,7},{7,6},{8,9},{9,8},{10,11... | collective-permute-start | bytes 3145736 | tf_op jit(solution)/shard_map/beside/ppermute | solution.py:211
  12.1 9.8 %collective-permute-start.1 = (bf16[4,256,128]{2,1,0:T(8,128)(2,1)S(1)}, bf16[4,256,128]{2,1,0:T(8,128)(2,1)S(1)}, u32[]{:S(2)}, u32[]{:S(2)}) collective-permute-start(bf16[4,256,128]{2,1,0:T(8,128)(2,1)S(1)} %get-tuple-element.28), channel_id=1, source_target_pairs={{0,2},{1,3},{2,0},{3,1},{4,6},{5,7},{6,4},{7,5},{8,10},{9,11},{10,... | collective-permute-start | bytes 786440 | tf_op jit(solution)/shard_map/y0/ppermute | solution.py:211
  14.7 12.3 %collective-permute-start.2 = (bf16[4,256,128]{2,1,0:T(8,128)(2,1)S(1)}, bf16[4,256,128]{2,1,0:T(8,128)(2,1)S(1)}, u32[]{:S(2)}, u32[]{:S(2)}) collective-permute-start(bf16[4,256,128]{2,1,0:T(8,128)(2,1)S(1)} %get-tuple-element.29), channel_id=1, source_target_pairs={{0,3},{1,2},{2,1},{3,0},{4,7},{5,6},{6,5},{7,4},{8,11},{9,10},{10,... | collective-permute-start | bytes 786440 | tf_op jit(solution)/shard_map/y1/ppermute | solution.py:211
  22.2 11.7 %collective-permute-start.4 = (bf16[4,256,128]{2,1,0:T(8,128)(2,1)S(1)}, bf16[4,256,128]{2,1,0:T(8,128)(2,1)S(1)}, u32[]{:S(2)}, u32[]{:S(2)}) collective-permute-start(bf16[4,256,128]{2,1,0:T(8,128)(2,1)S(1)} %get-tuple-element.35), channel_id=1, source_target_pairs={{0,2},{1,3},{2,0},{3,1},{4,6},{5,7},{6,4},{7,5},{8,10},{9,11},{10,... | collective-permute-start | bytes 786440 | tf_op jit(solution)/shard_map/y2/ppermute | solution.py:211
  24.2 13.9 %collective-permute-start.5 = (bf16[4,256,128]{2,1,0:T(8,128)(2,1)S(1)}, bf16[4,256,128]{2,1,0:T(8,128)(2,1)S(1)}, u32[]{:S(2)}, u32[]{:S(2)}) collective-permute-start(bf16[4,256,128]{2,1,0:T(8,128)(2,1)S(1)} %get-tuple-element.36), channel_id=1, source_target_pairs={{0,3},{1,2},{2,1},{3,0},{4,7},{5,6},{6,5},{7,4},{8,11},{9,10},{10,... | collective-permute-start | bytes 786440 | tf_op jit(solution)/shard_map/y3/ppermute | solution.py:211
  26.9 1.2 %copy-start = (bf16[16,256,128]{2,1,0:T(8,128)(2,1)S(1)}, bf16[16,256,128]{2,1,0:T(8,128)(2,1)}, u32[]{:S(2)}) copy-start(bf16[16,256,128]{2,1,0:T(8,128)(2,1)} %get-tuple-element.26.refs_0_) | copy-start | bytes 3145732
  29.5 21.4 %collective-permute-start.3 = (bf16[1,4,4,64,128]{4,3,2,1,0:T(8,128)(2,1)S(1)}, bf16[1,4,4,64,128]{4,3,2,1,0:T(8,128)(2,1)S(1)}, u32[]{:S(2)}, u32[]{:S(2)}) collective-permute-start(bf16[1,4,4,64,128]{4,3,2,1,0:T(8,128)(2,1)S(1)} %get-tuple-element.34.refs_5_), channel_id=1, source_target_pairs={{0,16},{4,20},{8,24},{12,28},{16,0},{20,4},{24,8},{28,12},{1,17},{... | collective-permute-start | bytes 786440 | tf_op jit(solution)/shard_map/z4c0/ppermute | solution.py:211
  32.2 20.8 %collective-permute-start.8 = (bf16[4,256,128]{2,1,0:T(8,128)(2,1)S(1)}, bf16[4,256,128]{2,1,0:T(8,128)(2,1)S(1)}, u32[]{:S(2)}, u32[]{:S(2)}) collective-permute-start(bf16[4,256,128]{2,1,0:T(8,128)(2,1)S(1)} %get-tuple-element.39), channel_id=1, source_target_pairs={{0,2},{1,3},{2,0},{3,1},{4,6},{5,7},{6,4},{7,5},{8,10},{9,11},{10,... | collective-permute-start | bytes 786440 | tf_op jit(solution)/shard_map/y4/ppermute | solution.py:211
  33.7 19.3 %collective-permute-start.9 = (bf16[4,256,128]{2,1,0:T(8,128)(2,1)S(1)}, bf16[4,256,128]{2,1,0:T(8,128)(2,1)S(1)}, u32[]{:S(2)}, u32[]{:S(2)}) collective-permute-start(bf16[4,256,128]{2,1,0:T(8,128)(2,1)S(1)} %get-tuple-element.40), channel_id=1, source_target_pairs={{0,3},{1,2},{2,1},{3,0},{4,7},{5,6},{6,5},{7,4},{8,11},{9,10},{10,... | collective-permute-start | bytes 786440 | tf_op jit(solution)/shard_map/y5/ppermute | solution.py:211
  39.5 18.3 %collective-permute-start.7 = (bf16[1,4,4,64,128]{4,3,2,1,0:T(8,128)(2,1)S(1)}, bf16[1,4,4,64,128]{4,3,2,1,0:T(8,128)(2,1)S(1)}, u32[]{:S(2)}, u32[]{:S(2)}) collective-permute-start(bf16[1,4,4,64,128]{4,3,2,1,0:T(8,128)(2,1)S(1)} %get-tuple-element.37.refs_2_), channel_id=1, source_target_pairs={{0,16},{4,20},{8,24},{12,28},{16,0},{20,4},{24,8},{28,12},{1,17},{... | collective-permute-start | bytes 786440 | tf_op jit(solution)/shard_map/z4c1/ppermute | solution.py:211
  50.9 12.7 %collective-permute-start.6 = (bf16[2,2,4,64,128]{4,3,2,1,0:T(8,128)(2,1)S(1)}, bf16[2,2,4,64,128]{4,3,2,1,0:T(8,128)(2,1)S(1)}, u32[]{:S(2)}, u32[]{:S(2)}) collective-permute-start(bf16[2,2,4,64,128]{4,3,2,1,0:T(8,128)(2,1)S(1)} %merge.8.refs_5_), channel_id=1, source_target_pairs={{0,8},{4,12},{8,0},{12,4},{16,24},{20,28},{24,16},{28,20},{1,9},{5... | collective-permute-start | bytes 786440 | tf_op jit(solution)/shard_map/z2c0/ppermute | solution.py:211
  51.4 13.8 %collective-permute-start.12 = (bf16[4,256,128]{2,1,0:T(8,128)(2,1)S(1)}, bf16[4,256,128]{2,1,0:T(8,128)(2,1)S(1)}, u32[]{:S(2)}, u32[]{:S(2)}) collective-permute-start(bf16[4,256,128]{2,1,0:T(8,128)(2,1)S(1)} %get-tuple-element.42), channel_id=1, source_target_pairs={{0,2},{1,3},{2,0},{3,1},{4,6},{5,7},{6,4},{7,5},{8,10},{9,11},{10,... | collective-permute-start | bytes 786440 | tf_op jit(solution)/shard_map/y6/ppermute | solution.py:211
  52.9 47.5 %copy-start.3 = (s32[128]{0:T(128)S(1)}, s32[128]{0:T(128)}, u32[]{:S(2)}) copy-start(s32[128]{0:T(128)} %mirror_ref.1) | copy-start | bytes 1540
  52.9 12.3 %collective-permute-start.13 = (bf16[4,256,128]{2,1,0:T(8,128)(2,1)S(1)}, bf16[4,256,128]{2,1,0:T(8,128)(2,1)S(1)}, u32[]{:S(2)}, u32[]{:S(2)}) collective-permute-start(bf16[4,256,128]{2,1,0:T(8,128)(2,1)S(1)} %get-tuple-element.43), channel_id=1, source_target_pairs={{0,3},{1,2},{2,1},{3,0},{4,7},{5,6},{6,5},{7,4},{8,11},{9,10},{10,... | collective-permute-start | bytes 786440 | tf_op jit(solution)/shard_map/y7/ppermute | solution.py:211
  54.3 18.8 %collective-permute-start.15 = (bf16[1,4,4,64,128]{4,3,2,1,0:T(8,128)(2,1)S(1)}, bf16[1,4,4,64,128]{4,3,2,1,0:T(8,128)(2,1)S(1)}, u32[]{:S(2)}, u32[]{:S(2)}) collective-permute-start(bf16[1,4,4,64,128]{4,3,2,1,0:T(8,128)(2,1)S(1)} %get-tuple-element.41.refs_2_), channel_id=1, source_target_pairs={{0,16},{4,20},{8,24},{12,28},{16,0},{20,4},{24,8},{28,12},{1,17},{... | collective-permute-start | bytes 786440 | tf_op jit(solution)/shard_map/z4c2/ppermute | solution.py:211
  57.8 15.3 %collective-permute-start.11 = (bf16[2,2,4,64,128]{4,3,2,1,0:T(8,128)(2,1)S(1)}, bf16[2,2,4,64,128]{4,3,2,1,0:T(8,128)(2,1)S(1)}, u32[]{:S(2)}, u32[]{:S(2)}) collective-permute-start(bf16[2,2,4,64,128]{4,3,2,1,0:T(8,128)(2,1)S(1)} %merge.9.refs_3_), channel_id=1, source_target_pairs={{0,8},{4,12},{8,0},{12,4},{16,24},{20,28},{24,16},{28,20},{1,9},{5... | collective-permute-start | bytes 786440 | tf_op jit(solution)/shard_map/z2c1/ppermute | solution.py:211
  63.6 9.5 %collective-permute-start.10 = (bf16[4,1,4,64,128]{4,3,2,1,0:T(8,128)(2,1)S(1)}, bf16[4,1,4,64,128]{4,3,2,1,0:T(8,128)(2,1)S(1)}, u32[]{:S(2)}, u32[]{:S(2)}) collective-permute-start(bf16[4,1,4,64,128]{4,3,2,1,0:T(8,128)(2,1)S(1)} %merge.10.refs_5_), channel_id=1, source_target_pairs={{0,4},{4,0},{8,12},{12,8},{16,20},{20,16},{24,28},{28,24},{1,5},{5... | collective-permute-start | bytes 786440 | tf_op jit(solution)/shard_map/z1c0/ppermute | solution.py:211
  66.5 10.9 %collective-permute-start.17 = (bf16[1,4,4,64,128]{4,3,2,1,0:T(8,128)(2,1)S(1)}, bf16[1,4,4,64,128]{4,3,2,1,0:T(8,128)(2,1)S(1)}, u32[]{:S(2)}, u32[]{:S(2)}) collective-permute-start(bf16[1,4,4,64,128]{4,3,2,1,0:T(8,128)(2,1)S(1)} %get-tuple-element.44.refs_3_), channel_id=1, source_target_pairs={{0,4},{4,0},{8,12},{12,8},{16,20},{20,16},{24,28},{28,24},{1,5},{5... | collective-permute-start | bytes 786440 | tf_op jit(solution)/shard_map/z1c3/ppermute | solution.py:211
  77.4 12.1 %collective-permute-start.18 = (bf16[2,2,4,64,128]{4,3,2,1,0:T(8,128)(2,1)S(1)}, bf16[2,2,4,64,128]{4,3,2,1,0:T(8,128)(2,1)S(1)}, u32[]{:S(2)}, u32[]{:S(2)}) collective-permute-start(bf16[2,2,4,64,128]{4,3,2,1,0:T(8,128)(2,1)S(1)} %merge.13.refs_3_), channel_id=1, source_target_pairs={{0,8},{4,12},{8,0},{12,4},{16,24},{20,28},{24,16},{28,20},{1,9},{5... | collective-permute-start | bytes 786440 | tf_op jit(solution)/shard_map/z2c3/ppermute | solution.py:211
  77.5 15.7 %collective-permute-start.16 = (bf16[2,2,4,64,128]{4,3,2,1,0:T(8,128)(2,1)S(1)}, bf16[2,2,4,64,128]{4,3,2,1,0:T(8,128)(2,1)S(1)}, u32[]{:S(2)}, u32[]{:S(2)}) collective-permute-start(bf16[2,2,4,64,128]{4,3,2,1,0:T(8,128)(2,1)S(1)} %merge.12.refs_2_), channel_id=1, source_target_pairs={{0,8},{4,12},{8,0},{12,4},{16,24},{20,28},{24,16},{28,20},{1,9},{5... | collective-permute-start | bytes 786440 | tf_op jit(solution)/shard_map/z2c2/ppermute | solution.py:211
  79.5 13.7 %collective-permute-start.14 = (bf16[4,1,4,64,128]{4,3,2,1,0:T(8,128)(2,1)S(1)}, bf16[4,1,4,64,128]{4,3,2,1,0:T(8,128)(2,1)S(1)}, u32[]{:S(2)}, u32[]{:S(2)}) collective-permute-start(bf16[4,1,4,64,128]{4,3,2,1,0:T(8,128)(2,1)S(1)} %merge.11.refs_2_), channel_id=1, source_target_pairs={{0,4},{4,0},{8,12},{12,8},{16,20},{20,16},{24,28},{28,24},{1,5},{5... | collective-permute-start | bytes 786440 | tf_op jit(solution)/shard_map/z1c1/ppermute | solution.py:211
  89.6 10.9 %collective-permute-start.20 = (bf16[4,1,4,64,128]{4,3,2,1,0:T(8,128)(2,1)S(1)}, bf16[4,1,4,64,128]{4,3,2,1,0:T(8,128)(2,1)S(1)}, u32[]{:S(2)}, u32[]{:S(2)}) collective-permute-start(bf16[4,1,4,64,128]{4,3,2,1,0:T(8,128)(2,1)S(1)} %merge.14.refs_3_), channel_id=1, source_target_pairs={{0,16},{4,20},{8,24},{12,28},{16,0},{20,4},{24,8},{28,12},{1,17},{... | collective-permute-start | bytes 786440 | tf_op jit(solution)/shard_map/z4c3/ppermute | solution.py:211
  93.2 7.2 %collective-permute-start.19 = (bf16[4,1,4,64,128]{4,3,2,1,0:T(8,128)(2,1)S(1)}, bf16[4,1,4,64,128]{4,3,2,1,0:T(8,128)(2,1)S(1)}, u32[]{:S(2)}, u32[]{:S(2)}) collective-permute-start(bf16[4,1,4,64,128]{4,3,2,1,0:T(8,128)(2,1)S(1)} %merge.15), channel_id=1, source_target_pairs={{0,4},{4,0},{8,12},{12,8},{16,20},{20,16},{24,28},{28,24},{1,5},{5... | collective-permute-start | bytes 786440 | tf_op jit(solution)/shard_map/z1c2/ppermute | solution.py:211

commit v8 on v7

--- a/solution.py
+++ b/solution.py
@@ -9,7 +9,9 @@
 
 LANES = 128
 STEP = 64
-CHUNKS = (4, 4, 4, 4)
+BATCHES = ((4, 4), (4, 4))
+CHUNKS = sum(BATCHES, ())
+LATE = 2
 PART = 256
 MIB = 1024 * 1024
 COST = pl.CostEstimate(flops=1024, bytes_accessed=1024, transcendentals=0)
@@ -19,12 +21,13 @@
 IN_HBM = pl.BlockSpec(memory_space=pltpu.MemorySpace.HBM)
 
 
-def quarter_kernel(rows, n_mo, blocks, place_ref, x_ref, c_hbm, *refs):
+def quarter_kernel(rows, n_mo, blocks, n_after, place_ref, x_ref, c_hbm, *refs):
+    refs = refs[n_after:]
     outs, (c_ref, turn_ref, held, c_sem, sems) = refs[:-5], refs[-5:]
     at = pl.program_id(0)
-    step, k_all, depth = x_ref.shape
+    step, some, depth = x_ref.shape
     padded = held.shape[2]
-    many = PART // k_all
+    many = PART // some
 
     @pl.when(at == 0)
     def _():
@@ -32,19 +35,19 @@
         copy.start()
         to = lax.broadcasted_iota(jnp.int32, (PART, PART), 0)
         source = lax.broadcasted_iota(jnp.int32, (PART, PART), 1)
-        turn_ref[...] = (source == to % many * k_all + to // many).astype(jnp.float32).astype(jnp.bfloat16)
+        turn_ref[...] = (source == to % many * some + to // many).astype(jnp.float32).astype(jnp.bfloat16)
         copy.wait()
 
-    x = x_ref[...].reshape(step * k_all, depth)
+    x = x_ref[...].reshape(step * some, depth)
     product = jnp.dot(x, c_ref[...], preferred_element_type=jnp.float32)
     line = lax.broadcasted_iota(jnp.int32, product.shape, 0)
-    product = jnp.where(line < (rows - at * step) * k_all, product, 0.0).astype(jnp.bfloat16)
+    product = jnp.where(line < (rows - at * step) * some, product, 0.0).astype(jnp.bfloat16)
     for part in range(step // many):
         lines = jnp.dot(
             turn_ref[...], product[part * PART : (part + 1) * PART], preferred_element_type=jnp.float32
         ).astype(jnp.bfloat16)
         here = pl.ds(pl.multiple_of(at * step + part * many, many), many)
-        for k in range(k_all):
+        for k in range(some):
             for d in range(n_mo):
                 held[d, k, here] = lines[k * many : (k + 1) * many, d * LANES : (d + 1) * LANES]
     here = pl.ds(pl.multiple_of(at * step, step), step)
@@ -59,23 +62,26 @@
             pltpu.make_async_copy(mine, out, sems.at[n]).wait()
 
 
-def quarter_of(place, by_r, coeffs, n_mo, padded):
-    rows, k_all, depth = by_r.shape
+def quarter_of(place, by_r, coeffs, n_mo, padded, batch, after):
+    rows, _, depth = by_r.shape
     orbitals = coeffs.shape[1]
-    blocks = [(0, 0), (1, 0)] + [(o, sum(CHUNKS[:c])) for c in range(len(CHUNKS)) for o in range(2, n_mo)]
-    sizes = [k_all] * 2 + [kc for kc in CHUNKS for _ in range(2, n_mo)]
+    chunks = BATCHES[batch]
+    some = sum(chunks)
+    blocks = [(0, 0), (1, 0)] + [(o, sum(chunks[:c])) for c in range(len(chunks)) for o in range(2, n_mo)]
+    sizes = [some] * 2 + [kc for kc in chunks for _ in range(2, n_mo)]
     outs = [jax.ShapeDtypeStruct((kc, padded, LANES), jnp.bfloat16) for kc in sizes]
     out = pl.pallas_call(
-        functools.partial(quarter_kernel, rows, n_mo, blocks),
+        functools.partial(quarter_kernel, rows, n_mo, blocks, len(after)),
         grid_spec=pltpu.PrefetchScalarGridSpec(
             num_scalar_prefetch=1,
             grid=(padded // STEP,),
-            in_specs=[pl.BlockSpec((STEP, k_all, depth), lambda r, place: (r, 0, 0)), IN_HBM],
+            in_specs=[pl.BlockSpec((STEP, some, depth), lambda r, place: (r, batch, 0)), IN_HBM]
+            + [ANYWHERE] * len(after),
             out_specs=[IN_HBM] * len(outs),
             scratch_shapes=[
                 pltpu.VMEM((depth, orbitals), jnp.bfloat16),
                 pltpu.VMEM((PART, PART), jnp.bfloat16),
-                pltpu.VMEM((n_mo, k_all, padded, LANES), jnp.bfloat16),
+                pltpu.VMEM((n_mo, some, padded, LANES), jnp.bfloat16),
                 pltpu.SemaphoreType.DMA,
                 pltpu.SemaphoreType.DMA((len(outs),)),
             ],
@@ -84,9 +90,9 @@
         compiler_params=pltpu.CompilerParams(vmem_limit_bytes=50 * MIB),
         cost_estimate=COST,
         name="quarter",
-    )(place, by_r, coeffs)
+    )(place, by_r, coeffs, *after)
     far = n_mo - 2
-    return out[:2], [out[2 + far * c : 2 + far * (c + 1)] for c in range(len(CHUNKS))]
+    return out[:2], [out[2 + far * c : 2 + far * (c + 1)] for c in range(len(chunks))]
 
 
 def turn_kernel(rows, c_ref, *refs):
@@ -114,32 +120,36 @@
     return out[-1], list(out[:-1])
 
 
-def half_kernel(n_mo, first, owners, place_ref, *refs):
+def half_kernel(n_mo, first, plans, place_ref, *refs):
     blocks, t_ref, held = refs[:n_mo], refs[n_mo], refs[-1]
-    outs = refs[-1 - len(owners) : -1]
-    kc, block, lanes = outs[0].shape[2:]
+    outs = refs[-1 - len(plans) : -1]
+    block, lanes = outs[0].shape[-2:]
+    kc = blocks[-1].shape[0]
     firsts = [first if x.shape[0] > kc else 0 for x in blocks]
     columns = [jnp.concatenate([x[at + k] for k in range(kc)], axis=1) for x, at in zip(blocks, firsts)]
     turned = [t_ref[place_ref[0] ^ o] for o in range(n_mo)]
     held[...] = jnp.dot(
         jnp.concatenate(turned, axis=1), jnp.concatenate(columns, axis=0), preferred_element_type=jnp.float32
     )
-    for out, its in zip(outs, owners):
-        for at, o in enumerate(its):
+    for out, (at, rows, owners) in zip(outs, plans):
+        for n, o in enumerate(owners):
             start = pl.multiple_of((place_ref[1] ^ o) * block, block)
-            for k in range(kc):
-                out[0, at, k] = held[pl.ds(start, block), k * lanes : (k + 1) * lanes].astype(jnp.bfloat16)
-
-
-def half_of(place, blocks, turned, first, owners, after):
+            for k in range(rows):
+                piece = held[pl.ds(start, block), (at + k) * lanes : (at + k + 1) * lanes]
+                out[0, n, k] = piece.astype(jnp.bfloat16)
+
+
+def half_of(place, blocks, turned, n_pair, first, plans, after):
     n_mo, orbitals, _ = turned.shape
     kc, _, lanes = blocks[-1].shape
-    block = orbitals // sum(len(its) for its in owners)
+    block = orbitals // n_pair
     return pl.pallas_call(
-        functools.partial(half_kernel, n_mo, first, owners),
+        functools.partial(half_kernel, n_mo, first, plans),
         in_specs=[IN_SMEM] + [IN_VMEM] * (n_mo + 1) + [ANYWHERE] * len(after),
-        out_specs=[IN_VMEM] * len(owners),
-        out_shape=[jax.ShapeDtypeStruct((1, len(its), kc, block, lanes), jnp.bfloat16) for its in owners],
+        out_specs=[IN_VMEM] * len(plans),
+        out_shape=[
+            jax.ShapeDtypeStruct((1, len(owners), rows, block, lanes), jnp.bfloat16) for _, rows, owners in plans
+        ],
         scratch_shapes=[pltpu.VMEM((orbitals, kc * lanes), jnp.float32)],
         compiler_params=pltpu.CompilerParams(vmem_limit_bytes=24 * MIB),
         cost_estimate=COST,
@@ -156,17 +166,21 @@
             at += 1
 
 
-def merge(parts, picks, after):
+def merge(parts, picks, later, after):
     shape = (sum(x.shape[0] for x in parts), len(picks[0]), *parts[0].shape[2:])
-    return pl.pallas_call(
+    n = len(parts)
+    out = pl.pallas_call(
         functools.partial(merge_kernel, picks),
-        in_specs=[IN_VMEM] * len(parts) + [ANYWHERE] * len(after),
-        out_specs=IN_VMEM,
-        out_shape=jax.ShapeDtypeStruct(shape, jnp.bfloat16),
+        in_specs=[IN_VMEM] * n + [IN_HBM] * len(later) + [ANYWHERE] * len(after),
+        out_specs=[IN_HBM] * len(later) + [IN_VMEM],
+        out_shape=[jax.ShapeDtypeStruct(x.shape, x.dtype) for x in later]
+        + [jax.ShapeDtypeStruct(shape, jnp.bfloat16)],
+        input_output_aliases={n + m: m for m in range(len(later))},
         compiler_params=pltpu.CompilerParams(vmem_limit_bytes=24 * MIB),
         cost_estimate=COST,
         name="merge",
-    )(*parts, *after)
+    )(*parts, *later, *after)
+    return out[-1], out[:-1]
 
 
 def combine_kernel(sources, k_all, per_step, mirror_ref, place_ref, *refs):
@@ -217,40 +231,71 @@
     n_near = n_pair // 2
     by_r = jnp.transpose(integrals, (1, 0, 2))
     place = jnp.stack([lax.axis_index("mo"), lax.axis_index("pair")]).astype(jnp.int32)
-    (own, beside), queue = quarter_of(place, by_r, coeffs, n_mo, padded)
-    beside = flipped(beside, "mo", n_mo, 1, "beside")
     last = len(CHUNKS) - 1
     firsts = [sum(CHUNKS[:c]) for c in range(last + 1)]
-    down = [1 << n for n in reversed(range(n_pair.bit_length() - 1))]
-    orders = [down] * last + [down[::-1]]
-    turned, parts, owners, offsets, token = None, [[] for _ in CHUNKS], [[] for _ in CHUNKS], [[] for _ in CHUNKS], []
+
+    near, queue, token = [], [], []
+    for batch, chunks in enumerate(BATCHES):
+        (own, beside), far = quarter_of(place, by_r, coeffs, n_mo, padded, batch, token)
+        beside = flipped(beside, "mo", n_mo, 1, f"beside{batch}")
+        near += [(own, beside, sum(chunks[:c])) for c in range(len(chunks))]
+        queue += far
+        token = [own]
 
     def arrive(c):
         return [flipped(x, "mo", n_mo, o, f"y{2 * c + o - 2}") for o, x in enumerate(queue[c], 2)]
 
     arrived = [arrive(0)]
-    turned, queue[1] = turn(coeffs, n_mo, padded, queue[1], arrived[0][:1])
+    turned, queue[1] = turn(coeffs, n_mo, padded, queue[1], arrived[0][:1] + token)
     arrived += [arrive(c) for c in range(1, last + 1)]
 
+    down = [1 << n for n in reversed(range(n_pair.bit_length() - 1))]
+    units = [(c, 0, kc - LATE * (c == last), down) for c, kc in enumerate(CHUNKS)]
+    units.append((last, CHUNKS[-1] - LATE, LATE, down[::-1]))
     steps = [(c, c, 0) for c in range(last + 1)]
     for n in range(1, len(down)):
-        steps += [(c + n + (0.5 - n / 10 if c + n == last else n / 10), c, n) for c in range(last)]
-        steps.append((last + n - (0.55 if n == 1 else 0.95), last, n))
-    for _, c, level in sorted(steps):
-        flips = orders[c]
-        flip, gone = flips[level], sum(flips[:level])
-        left = [o for o in range(n_pair) if not o & gone]
-        kept, sent = [o for o in left if not o & flip], [o for o in left if o & flip]
+        steps += [(c + n + n / 10 + 0.3 * (c + n >= last), c, n) for c in range(last + 1)]
+        steps.append((last + n - 0.55 + 0.1 * (n == 1), last + 1, n))
+    parts, owners, offsets = [[] for _ in units], [[] for _ in units], [[[0]] for _ in units]
+    waiting, token = {}, []
+
+    def split(u, level):
+        flips = units[u][3]
+        left = [o for o in range(n_pair) if not o & sum(flips[:level])]
+        return [o for o in left if not o & flips[level]], [o for o in left if o & flips[level]]
+
+    def send(u, level, message):
+        flip, sent = units[u][3][level], split(u, level)[1]
+        offsets[u].append([o ^ flip for group in offsets[u] for o in group])
+        owners[u].append([o ^ flip for o in sent])
+        parts[u].append(flipped(message, "pair", n_pair, flip, f"z{flip}c{u}"))
+
+    for _, u, level in sorted(steps):
         if level == 0:
-            keep, message = half_of(place, [own, beside, *arrived[c]], turned, firsts[c], [kept, sent], token)
-            parts[c], owners[c], offsets[c] = [keep], [kept], [[0]]
+            mine = [n for n, unit in enumerate(units) if unit[0] == u]
+            plans = [(units[n][1], units[n][2], some) for n in mine for some in split(n, 0)]
+            blocks = [*near[u][:2], *arrived[u]]
+            out = half_of(place, blocks, turned, n_pair, near[u][2], plans, token)
+            for m, n in enumerate(mine):
+                parts[n].append(out[2 * m])
+                owners[n].append(split(n, 0)[0])
+                if 0 < n <= last:
+                    waiting[n] = out[2 * m + 1]
+                else:
+                    send(n, 0, out[2 * m + 1])
+            token = [out[0]]
         else:
-            after = token + (parts[c - 1][-1:] if level == len(flips) - 1 and 0 < c < last else [])
-            message = merge(parts[c], [[its.index(o) for o in sent] for its in owners[c]], after)
-        token = [message]
-        offsets[c].append([o ^ flip for group in offsets[c] for o in group])
-        owners[c].append([o ^ flip for o in sent])
-        parts[c].append(flipped(message, "pair", n_pair, flip, f"z{flip}c{c}"))
+            picks = [[its.index(o) for o in split(u, level)[1]] for its in owners[u]]
+            later = [waiting.pop(u + 1)] if level == 1 and u + 1 in waiting else []
+            done = parts[u - 2][-1:] if level == len(down) - 1 and 1 < u <= last else []
+            if u > last and level == len(down) - 1:
+                done = parts[last][1:2]
+            message, later = merge(parts[u], picks, later, token + done)
+            send(u, level, message)
+            for x in later:
+                send(u + 1, 0, x)
+            token = [message]
+    firsts = [firsts[c] + at for c, at, _, _ in units]
     pieces = [x for chunk in parts for x in chunk]
     sources = [(tuple(group), first) for chunk, first in zip(offsets, firsts) for group in chunk]
     return combine(pieces, sources, mirror, place, n_pair)

time: 104 us -> 96.2 us (0.925)
  waiting for transfers between devices: 56.3 us -> 44.1 us
  Pallas kernels: 19.2 us -> 22.5 us
  starting transfers between devices: 25.5 us -> 27.8 us
  local copies, waits for them, and re-layouts: 2.45 us -> 1.22 us
    ppermute x21 -> x25, waiting for transfers between devices: 56.3 us -> 44.1 us  [flipped(): return lax.ppermute(x, axis, [(i, i ^ offset) for i in range(size)])]
    pallas_call x5 -> x6, Pallas kernels: 15.4 us -> 18.7 us  [the longest x2 13.5 us: quarter_of(): pl.pallas_call(functools.partial(quarter_kernel, rows, n_mo, blocks, len(...]
    ppermute x21 -> x25, starting transfers between devices: 25.5 us -> 27.8 us  [flipped(): return lax.ppermute(x, axis, [(i, i ^ offset) for i in range(size)])]
    unnamed x8 -> x4, local copies, waits for them, and re-layouts: 2.45 us -> 1.22 us
  transfers between devices with their start and end apart: 21 -> 25, of which waited for: 10 -> 14; matrix products, arithmetic and copies ran while one was open for 0% -> 0% of each run, Pallas kernels for 6% -> 13%
where the time goes in v8:
time: 96.2 us; the launch traced here: 95.9 us
  waiting for transfers between devices  44.1 us (46%)
  starting transfers between devices  27.8 us (29%)
  Pallas kernels  22.5 us (23%)
  local copies, waits for them, and re-layouts  1.22 us (1%)
    ppermute x25, waiting for transfers between devices, flipped(): return lax.ppermute(x, axis, [(i, i ^ offset) for i in range(size)])  44.1 us
    ppermute x25, starting transfers between devices, flipped(): return lax.ppermute(x, axis, [(i, i ^ offset) for i in range(size)])  27.8 us
    pallas_call x2, Pallas kernels, quarter_of(): pl.pallas_call(functools.partial(quarter_kernel, rows, n_mo, blocks, len(...  13.5 us
    pallas_call x4, Pallas kernels, half_of(): pl.pallas_call(functools.partial(half_kernel, n_mo, first, plans), in_spe...  5.22 us
    pallas_call x1, Pallas kernels, combine(): pl.pallas_call(functools.partial(combine_kernel, sources, k_all, per_step...  3.28 us
  transfers between devices with their start and end apart: 25, of which 14 were waited for; matrix products, arithmetic and copies ran while one was open for 0% of the time, Pallas kernels for 13%

profile of v8, /device:TPU:0, one launch (start us, length us, event | category | flops | bytes accessed | tf_op | source)
XLA Modules:
  0.0 95.9 jit_solution(18204736860179507496)
XLA Ops:
  0.0 0.1 pad_add_fusion.place_ref
  0.1 1.2 %copy-done = bf16[1000,512]{1,0:T(8,128)(2,1)S(1)} copy-done((bf16[1000,512]{1,0:T(8,128)(2,1)S(1)}, bf16[1000,512]{1,0:T(8,128)(2,1)}, u32[]{:S(2)}) %copy-start) | copy-done | bytes 1024024
  1.3 6.7 %quarter.2 = (bf16[8,256,128]{2,1,0:T(8,128)(2,1)S(1)}, bf16[8,256,128]{2,1,0:T(8,128)(2,1)S(1)}, bf16[4,256,128]{2,1,0:T(8,128)(2,1)S(1)}, bf16[4,256,128]{2,1,...) custom-call(s32[2]{0:T(128)S(1)} %pad_add_fusion.place_ref, ...), custom_call_target="tpu_custom_call" | custom-call | flops 1024 | bytes 1024 | tf_op jit(solution)/shard_map/quarter/pallas_call | solution.py:73
  8.0 0.5 collective-permute-start
  8.6 2.6 %collective-permute-start.1 = (bf16[4,256,128]{2,1,0:T(8,128)(2,1)S(1)}, bf16[4,256,128]{2,1,0:T(8,128)(2,1)S(1)}, u32[]{:S(2)}, u32[]{:S(2)}) collective-permute-start(bf16[4,256,128]{2,1,0:T(8,128)(2,1)S(1)} %get-tuple-element.38), channel_id=1, source_target_pairs={{0,2},{1,3},{2,0},{3,1},{4,6},{5,7},{6,4},{7,5},{8,10},{9,11},{10,... | collective-permute-start | bytes 786440 | tf_op jit(solution)/shard_map/y0/ppermute | solution.py:225
  11.1 0.1 collective-permute-start.2
  11.2 6.7 %quarter.3 = (bf16[8,256,128]{2,1,0:T(8,128)(2,1)S(1)}, bf16[8,256,128]{2,1,0:T(8,128)(2,1)S(1)}, bf16[4,256,128]{2,1,0:T(8,128)(2,1)S(1)}, bf16[4,256,128]{2,1,...) custom-call(s32[2]{0:T(128)S(1)} %pad_add_fusion.place_ref, ...), custom_call_target="tpu_custom_call" | custom-call | flops 1024 | bytes 1024 | tf_op jit(solution)/shard_map/quarter/pallas_call | solution.py:73
  18.0 0.3 collective-permute-done.1.refs_2_
  18.3 0.4 turn.1
  18.7 2.0 %collective-permute-start.4 = (bf16[4,256,128]{2,1,0:T(8,128)(2,1)S(1)}, bf16[4,256,128]{2,1,0:T(8,128)(2,1)S(1)}, u32[]{:S(2)}, u32[]{:S(2)}) collective-permute-start(bf16[4,256,128]{2,1,0:T(8,128)(2,1)S(1)} %get-tuple-element.46), channel_id=1, source_target_pairs={{0,2},{1,3},{2,0},{3,1},{4,6},{5,7},{6,4},{7,5},{8,10},{9,11},{10,... | collective-permute-start | bytes 786440 | tf_op jit(solution)/shard_map/y2/ppermute | solution.py:225
  20.7 0.0 collective-permute-start.5
  20.7 2.7 %collective-permute-done.2.refs_3_ = bf16[4,256,128]{2,1,0:T(8,128)(2,1)S(1)} collective-permute-done((bf16[4,256,128]{2,1,0:T(8,128)(2,1)S(1)}, bf16[4,256,128]{2,1,0:T(8,128)(2,1)S(1)}, u32[]{:S(2)}, u32[]{:S(2)}) %collective-permute-start.2) | collective-permute-done | bytes 262176 | tf_op jit(solution)/shard_map/y1/ppermute | solution.py:225
  23.4 1.3 %half.4 = (bf16[1,4,4,64,128]{4,3,2,1,0:T(8,128)(2,1)S(1)}, bf16[1,4,4,64,128]{4,3,2,1,0:T(8,128)(2,1)S(1)}) custom-call(s32[2]{0:T(128)S(1)} %pad_add_fusion.place_ref, bf16[8,256,128]{2,1,0:T(8,128)(2,1)S(1)} %get-tuple-element.36.refs_0_, bf16[8,256,128]{2,1,0:T(8,128)(2,1)S(1)} %collective-permute-done.refs_1_, ...), custom_call_target="tpu_custom_call" | custom-call | flops 1024 | bytes 1024 | tf_op jit(solution)/shard_map/half/pallas_call | solution.py:146
  24.7 2.7 %collective-permute-start.3 = (bf16[1,4,4,64,128]{4,3,2,1,0:T(8,128)(2,1)S(1)}, bf16[1,4,4,64,128]{4,3,2,1,0:T(8,128)(2,1)S(1)}, u32[]{:S(2)}, u32[]{:S(2)}) collective-permute-start(bf16[1,4,4,64,128]{4,3,2,1,0:T(8,128)(2,1)S(1)} %get-tuple-element.45), channel_id=1, source_target_pairs={{0,16},{4,20},{8,24},{12,28},{16,0},{20,4},{24,8},{28,12},{1,17},{... | collective-permute-start | bytes 786440 | tf_op jit(solution)/shard_map/z4c0/ppermute | solution.py:225
  27.4 0.4 collective-permute-start.8
  27.9 1.5 %collective-permute-start.9 = (bf16[4,256,128]{2,1,0:T(8,128)(2,1)S(1)}, bf16[4,256,128]{2,1,0:T(8,128)(2,1)S(1)}, u32[]{:S(2)}, u32[]{:S(2)}) collective-permute-start(bf16[4,256,128]{2,1,0:T(8,128)(2,1)S(1)} %get-tuple-element.53), channel_id=1, source_target_pairs={{0,2},{1,3},{2,0},{3,1},{4,6},{5,7},{6,4},{7,5},{8,10},{9,11},{10,... | collective-permute-start | bytes 786440 | tf_op jit(solution)/shard_map/y4/ppermute | solution.py:225
  29.4 0.2 collective-permute-done.4.refs_2_
  29.5 0.8 collective-permute-start.10
  30.3 4.3 %collective-permute-done.5.refs_3_ = bf16[4,256,128]{2,1,0:T(8,128)(2,1)S(1)} collective-permute-done((bf16[4,256,128]{2,1,0:T(8,128)(2,1)S(1)}, bf16[4,256,128]{2,1,0:T(8,128)(2,1)S(1)}, u32[]{:S(2)}, u32[]{:S(2)}) %collective-permute-start.5) | collective-permute-done | bytes 262176 | tf_op jit(solution)/shard_map/y3/ppermute | solution.py:225
  34.6 1.3 %half.5 = (bf16[1,4,4,64,128]{4,3,2,1,0:T(8,128)(2,1)S(1)}, bf16[1,4,4,64,128]{4,3,2,1,0:T(8,128)(2,1)S(1)}) custom-call(s32[2]{0:T(128)S(1)} %pad_add_fusion.place_ref, bf16[8,256,128]{2,1,0:T(8,128)(2,1)S(1)} %get-tuple-element.36.refs_0_, bf16[8,256,128]{2,1,0:T(8,128)(2,1)S(1)} %collective-permute-done.refs_1_, ...), custom_call_target="tpu_custom_call" | custom-call | flops 1024 | bytes 1024 | tf_op jit(solution)/shard_map/half/pallas_call | solution.py:146
  35.9 0.0 copy-start.1
  36.0 4.3 %collective-permute-done.3.refs_1_ = bf16[1,4,4,64,128]{4,3,2,1,0:T(8,128)(2,1)S(1)} collective-permute-done((bf16[1,4,4,64,128]{4,3,2,1,0:T(8,128)(2,1)S(1)}, bf16[1,4,4,64,128]{4,3,2,1,0:T(8,128)(2,1)S(1)}, u32[]{:S(2)}, u32[]{:S(2)}) %collective-permute-start.3) | collective-permute-done | bytes 262176 | tf_op jit(solution)/shard_map/z4c0/ppermute | solution.py:225
  40.3 0.1 collective-permute-start.7
  40.3 1.6 %collective-permute-start.14 = (bf16[4,256,128]{2,1,0:T(8,128)(2,1)S(1)}, bf16[4,256,128]{2,1,0:T(8,128)(2,1)S(1)}, u32[]{:S(2)}, u32[]{:S(2)}) collective-permute-start(bf16[4,256,128]{2,1,0:T(8,128)(2,1)S(1)} %get-tuple-element.59), channel_id=1, source_target_pairs={{0,2},{1,3},{2,0},{3,1},{4,6},{5,7},{6,4},{7,5},{8,10},{9,11},{10,... | collective-permute-start | bytes 786440 | tf_op jit(solution)/shard_map/y6/ppermute | solution.py:225
  42.0 3.9 %collective-permute-done.10.refs_3_ = bf16[4,256,128]{2,1,0:T(8,128)(2,1)S(1)} collective-permute-done((bf16[4,256,128]{2,1,0:T(8,128)(2,1)S(1)}, bf16[4,256,128]{2,1,0:T(8,128)(2,1)S(1)}, u32[]{:S(2)}, u32[]{:S(2)}) %collective-permute-start.10) | collective-permute-done | bytes 262176 | tf_op jit(solution)/shard_map/y5/ppermute | solution.py:225
  45.9 1.6 %collective-permute-start.6 = (bf16[2,2,4,64,128]{4,3,2,1,0:T(8,128)(2,1)S(1)}, bf16[2,2,4,64,128]{4,3,2,1,0:T(8,128)(2,1)S(1)}, u32[]{:S(2)}, u32[]{:S(2)}) collective-permute-start(bf16[2,2,4,64,128]{4,3,2,1,0:T(8,128)(2,1)S(1)} %get-tuple-element.50.refs_5_), channel_id=1, source_target_pairs={{0,8},{4,12},{8,0},{12,4},{16,24},{20,28},{24,16},{28,20},{1,9},{5... | collective-permute-start | bytes 786440 | tf_op jit(solution)/shard_map/z2c0/ppermute | solution.py:225
  47.5 1.3 %half.6 = (bf16[1,4,4,64,128]{4,3,2,1,0:T(8,128)(2,1)S(1)}, bf16[1,4,4,64,128]{4,3,2,1,0:T(8,128)(2,1)S(1)}) custom-call(s32[2]{0:T(128)S(1)} %pad_add_fusion.place_ref, bf16[8,256,128]{2,1,0:T(8,128)(2,1)S(1)} %get-tuple-element.42.refs_3_.refs_0_, bf16[8,256,128]{2,1,0:T(8,128)(2,1)S(1)} %collective-permute-done.8.refs_1_, ...), custom_call_target="tpu_custom_call" | custom-call | flops 1024 | bytes 1024 | tf_op jit(solution)/shard_map/half/pallas_call | solution.py:146
  48.8 6.2 %collective-permute-done.7.refs_1_.refs_5_ = bf16[1,4,4,64,128]{4,3,2,1,0:T(8,128)(2,1)S(1)} collective-permute-done((bf16[1,4,4,64,128]{4,3,2,1,0:T(8,128)(2,1)S(1)}, bf16[1,4,4,64,128]{4,3,2,1,0:T(8,128)(2,1)S(1)}, u32[]{:S(2)}, u32[]{:S(2)}) %collective-permute-start.7) | collective-permute-done | bytes 262176 | tf_op jit(solution)/shard_map/z4c1/ppermute | solution.py:225
  55.0 0.1 collective-permute-start.13
  55.1 1.7 %collective-permute-start.12 = (bf16[2,2,4,64,128]{4,3,2,1,0:T(8,128)(2,1)S(1)}, bf16[2,2,4,64,128]{4,3,2,1,0:T(8,128)(2,1)S(1)}, u32[]{:S(2)}, u32[]{:S(2)}) collective-permute-start(bf16[2,2,4,64,128]{4,3,2,1,0:T(8,128)(2,1)S(1)} %get-tuple-element.57.refs_3_), channel_id=1, source_target_pairs={{0,8},{4,12},{8,0},{12,4},{16,24},{20,28},{24,16},{28,20},{1,9},{5... | collective-permute-start | bytes 786440 | tf_op jit(solution)/shard_map/z2c1/ppermute | solution.py:225
  56.9 2.7 %collective-permute-done.6.refs_2_ = bf16[2,2,4,64,128]{4,3,2,1,0:T(8,128)(2,1)S(1)} collective-permute-done((bf16[2,2,4,64,128]{4,3,2,1,0:T(8,128)(2,1)S(1)}, bf16[2,2,4,64,128]{4,3,2,1,0:T(8,128)(2,1)S(1)}, u32[]{:S(2)}, u32[]{:S(2)}) %collective-permute-start.6) | collective-permute-done | bytes 262176 | tf_op jit(solution)/shard_map/z2c0/ppermute | solution.py:225
  59.6 1.6 %collective-permute-start.11 = (bf16[4,1,4,64,128]{4,3,2,1,0:T(8,128)(2,1)S(1)}, bf16[4,1,4,64,128]{4,3,2,1,0:T(8,128)(2,1)S(1)}, u32[]{:S(2)}, u32[]{:S(2)}) collective-permute-start(bf16[4,1,4,64,128]{4,3,2,1,0:T(8,128)(2,1)S(1)} %merge.12.refs_5_), channel_id=1, source_target_pairs={{0,4},{4,0},{8,12},{12,8},{16,20},{20,16},{24,28},{28,24},{1,5},{5... | collective-permute-start | bytes 786440 | tf_op jit(solution)/shard_map/z1c0/ppermute | solution.py:225
  61.2 1.3 %half.7 = (bf16[1,4,2,64,128]{4,3,2,1,0:T(8,128)(2,1)S(1)}, bf16[1,4,2,64,128]{4,3,2,1,0:T(8,128)(2,1)S(1)}, bf16[1,4,2,64,128]{4,3,2,1,0:T(8,128)(2,1)S(1)}, bf16[1,4,2,64,128]{4,3,2,1,0:T(8,128)(2,1)S(1)}) custom-call(s32[2]{0:T(128)S(1)} %pad_add_fusion.place_ref, bf16[8,256,128]{2,1,0:T(8,128)(2,1)S(1)} %get-tuple-element.42.refs_3_.refs_0_, ...), custom_call_target="tpu_custom_call" | custom-call | flops 1024 | bytes 1024 | tf_op jit(solution)/shard_map/half/pallas_call | solution.py:146
  62.5 0.6 collective-permute-start.18
  63.1 5.4 %collective-permute-done.13.refs_1_.refs_9_ = bf16[1,4,4,64,128]{4,3,2,1,0:T(8,128)(2,1)S(1)} collective-permute-done((bf16[1,4,4,64,128]{4,3,2,1,0:T(8,128)(2,1)S(1)}, bf16[1,4,4,64,128]{4,3,2,1,0:T(8,128)(2,1)S(1)}, u32[]{:S(2)}, u32[]{:S(2)}) %collective-permute-start.13) | collective-permute-done | bytes 262176 | tf_op jit(solution)/shard_map/z4c2/ppermute | solution.py:225
  68.5 0.1 collective-permute-start.17
  68.6 2.1 %collective-permute-start.20 = (bf16[1,4,2,64,128]{4,3,2,1,0:T(8,128)(2,1)S(1)}, bf16[1,4,2,64,128]{4,3,2,1,0:T(8,128)(2,1)S(1)}, u32[]{:S(2)}, u32[]{:S(2)}) collective-permute-start(bf16[1,4,2,64,128]{4,3,2,1,0:T(8,128)(2,1)S(1)} %get-tuple-element.66), channel_id=1, source_target_pairs={{0,16},{4,20},{8,24},{12,28},{16,0},{20,4},{24,8},{28,12},{1,17},{... | collective-permute-start | bytes 393224 | tf_op jit(solution)/shard_map/z4c3/ppermute | solution.py:225
  70.8 0.1 collective-permute-start.19
  70.9 1.7 %collective-permute-start.16 = (bf16[4,1,4,64,128]{4,3,2,1,0:T(8,128)(2,1)S(1)}, bf16[4,1,4,64,128]{4,3,2,1,0:T(8,128)(2,1)S(1)}, u32[]{:S(2)}, u32[]{:S(2)}) collective-permute-start(bf16[4,1,4,64,128]{4,3,2,1,0:T(8,128)(2,1)S(1)} %merge.14.refs_2_), channel_id=1, source_target_pairs={{0,4},{4,0},{8,12},{12,8},{16,20},{20,16},{24,28},{28,24},{1,5},{5... | collective-permute-start | bytes 786440 | tf_op jit(solution)/shard_map/z1c1/ppermute | solution.py:225
  72.6 5.5 %collective-permute-done.20.refs_1_.refs_4_.refs_13_ = bf16[1,4,2,64,128]{4,3,2,1,0:T(8,128)(2,1)S(1)} collective-permute-done((bf16[1,4,2,64,128]{4,3,2,1,0:T(8,128)(2,1)S(1)}, bf16[1,4,2,64,128]{4,3,2,1,0:T(8,128)(2,1)S(1)}, u32[]{:S(2)}, u32[]{:S(2)}) %collective-permute-start.20) | collective-permute-done | bytes 131104 | tf_op jit(solution)/shard_map/z4c3/ppermute | solution.py:225
  78.0 2.7 %collective-permute-start.22 = (bf16[2,2,2,64,128]{4,3,2,1,0:T(8,128)(2,1)S(1)}, bf16[2,2,2,64,128]{4,3,2,1,0:T(8,128)(2,1)S(1)}, u32[]{:S(2)}, u32[]{:S(2)}) collective-permute-start(bf16[2,2,2,64,128]{4,3,2,1,0:T(8,128)(2,1)S(1)} %merge.16.refs_3_), channel_id=1, source_target_pairs={{0,8},{4,12},{8,0},{12,4},{16,24},{20,28},{24,16},{28,20},{1,9},{5... | collective-permute-start | bytes 393224 | tf_op jit(solution)/shard_map/z2c3/ppermute | solution.py:225
  80.7 2.6 %collective-permute-done.19.refs_2_.refs_18_ = bf16[2,2,2,64,128]{4,3,2,1,0:T(8,128)(2,1)S(1)} collective-permute-done((bf16[2,2,2,64,128]{4,3,2,1,0:T(8,128)(2,1)S(1)}, bf16[2,2,2,64,128]{4,3,2,1,0:T(8,128)(2,1)S(1)}, u32[]{:S(2)}, u32[]{:S(2)}) %collective-permute-start.19) | collective-permute-done | bytes 131104 | tf_op jit(solution)/shard_map/z2c4/ppermute | solution.py:225
  83.4 1.6 %collective-permute-start.21 = (bf16[4,1,4,64,128]{4,3,2,1,0:T(8,128)(2,1)S(1)}, bf16[4,1,4,64,128]{4,3,2,1,0:T(8,128)(2,1)S(1)}, u32[]{:S(2)}, u32[]{:S(2)}) collective-permute-start(bf16[4,1,4,64,128]{4,3,2,1,0:T(8,128)(2,1)S(1)} %merge.18.refs_3_), channel_id=1, source_target_pairs={{0,4},{4,0},{8,12},{12,8},{16,20},{20,16},{24,28},{28,24},{1,5},{5... | collective-permute-start | bytes 786440 | tf_op jit(solution)/shard_map/z1c2/ppermute | solution.py:225
  85.0 0.1 collective-permute-done.22.refs_2_.refs_14_
  85.2 1.6 %collective-permute-start.23 = (bf16[4,1,2,64,128]{4,3,2,1,0:T(8,128)(2,1)S(1)}, bf16[4,1,2,64,128]{4,3,2,1,0:T(8,128)(2,1)S(1)}, u32[]{:S(2)}, u32[]{:S(2)}) collective-permute-start(bf16[4,1,2,64,128]{4,3,2,1,0:T(8,128)(2,1)S(1)} %merge.19), channel_id=1, source_target_pairs={{0,4},{4,0},{8,12},{12,8},{16,20},{20,16},{24,28},{28,24},{1,5},{5... | collective-permute-start | bytes 393224 | tf_op jit(solution)/shard_map/z1c3/ppermute | solution.py:225
  86.8 5.2 %collective-permute-done.24.refs_19_ = bf16[4,1,2,64,128]{4,3,2,1,0:T(8,128)(2,1)S(1)} collective-permute-done((bf16[4,1,2,64,128]{4,3,2,1,0:T(8,128)(2,1)S(1)}, bf16[4,1,2,64,128]{4,3,2,1,0:T(8,128)(2,1)S(1)}, u32[]{:S(2)}, u32[]{:S(2)}) %collective-permute-start.24) | collective-permute-done | bytes 131104 | tf_op jit(solution)/shard_map/z4c4/ppermute | solution.py:225
  91.9 0.7 collective-permute-done.23.refs_15_
  92.6 3.3 %combine.1 = f32[128,64,128]{2,1,0:T(8,128)} custom-call(s32[128]{0:T(128)S(1)} %copy-done.1, s32[2]{0:T(128)S(1)} %pad_add_fusion.place_ref, bf16[1,4,4,64,128]{4,3,2,1,0:T(8,128)(2,1)S(1)} %get-tuple-element.44.refs_5_.refs_0_, bf16[1,4,4,64,128]{4,3,2,1,0:T(8,128)(2,1)S(1)} %collective-permute-done.3.refs_1_, ...), custom_call_target="tpu_custom_call" | custom-call | flops 1024 | bytes 1024 | tf_op jit(solution)/shard_map/combine/pallas_call | solution.py:207
  (25 shorter events, 0.2 us)
Async XLA Ops:
  0.1 1.2 %copy-start = (bf16[1000,512]{1,0:T(8,128)(2,1)S(1)}, bf16[1000,512]{1,0:T(8,128)(2,1)}, u32[]{:S(2)}) copy-start(bf16[1000,512]{1,0:T(8,128)(2,1)} %c_ref.1) | copy-start | bytes 3072004
  8.0 15.4 %collective-permute-start = (bf16[8,256,128]{2,1,0:T(8,128)(2,1)S(1)}, bf16[8,256,128]{2,1,0:T(8,128)(2,1)S(1)}, u32[]{:S(2)}, u32[]{:S(2)}) collective-permute-start(bf16[8,256,128]{2,1,0:T(8,128)(2,1)S(1)} %get-tuple-element.37), channel_id=1, source_target_pairs={{0,1},{1,0},{2,3},{3,2},{4,5},{5,4},{6,7},{7,6},{8,9},{9,8},{10,11... | collective-permute-start | bytes 1572872 | tf_op jit(solution)/shard_map/beside0/ppermute | solution.py:225
  8.6 9.8 %collective-permute-start.1 = (bf16[4,256,128]{2,1,0:T(8,128)(2,1)S(1)}, bf16[4,256,128]{2,1,0:T(8,128)(2,1)S(1)}, u32[]{:S(2)}, u32[]{:S(2)}) collective-permute-start(bf16[4,256,128]{2,1,0:T(8,128)(2,1)S(1)} %get-tuple-element.38), channel_id=1, source_target_pairs={{0,2},{1,3},{2,0},{3,1},{4,6},{5,7},{6,4},{7,5},{8,10},{9,11},{10,... | collective-permute-start | bytes 786440 | tf_op jit(solution)/shard_map/y0/ppermute | solution.py:225
  11.1 12.3 %collective-permute-start.2 = (bf16[4,256,128]{2,1,0:T(8,128)(2,1)S(1)}, bf16[4,256,128]{2,1,0:T(8,128)(2,1)S(1)}, u32[]{:S(2)}, u32[]{:S(2)}) collective-permute-start(bf16[4,256,128]{2,1,0:T(8,128)(2,1)S(1)} %get-tuple-element.39), channel_id=1, source_target_pairs={{0,3},{1,2},{2,1},{3,0},{4,7},{5,6},{6,5},{7,4},{8,11},{9,10},{10,... | collective-permute-start | bytes 786440 | tf_op jit(solution)/shard_map/y1/ppermute | solution.py:225
  18.7 10.8 %collective-permute-start.4 = (bf16[4,256,128]{2,1,0:T(8,128)(2,1)S(1)}, bf16[4,256,128]{2,1,0:T(8,128)(2,1)S(1)}, u32[]{:S(2)}, u32[]{:S(2)}) collective-permute-start(bf16[4,256,128]{2,1,0:T(8,128)(2,1)S(1)} %get-tuple-element.46), channel_id=1, source_target_pairs={{0,2},{1,3},{2,0},{3,1},{4,6},{5,7},{6,4},{7,5},{8,10},{9,11},{10,... | collective-permute-start | bytes 786440 | tf_op jit(solution)/shard_map/y2/ppermute | solution.py:225
  20.7 13.9 %collective-permute-start.5 = (bf16[4,256,128]{2,1,0:T(8,128)(2,1)S(1)}, bf16[4,256,128]{2,1,0:T(8,128)(2,1)S(1)}, u32[]{:S(2)}, u32[]{:S(2)}) collective-permute-start(bf16[4,256,128]{2,1,0:T(8,128)(2,1)S(1)} %get-tuple-element.47), channel_id=1, source_target_pairs={{0,3},{1,2},{2,1},{3,0},{4,7},{5,6},{6,5},{7,4},{8,11},{9,10},{10,... | collective-permute-start | bytes 786440 | tf_op jit(solution)/shard_map/y3/ppermute | solution.py:225
  24.7 15.5 %collective-permute-start.3 = (bf16[1,4,4,64,128]{4,3,2,1,0:T(8,128)(2,1)S(1)}, bf16[1,4,4,64,128]{4,3,2,1,0:T(8,128)(2,1)S(1)}, u32[]{:S(2)}, u32[]{:S(2)}) collective-permute-start(bf16[1,4,4,64,128]{4,3,2,1,0:T(8,128)(2,1)S(1)} %get-tuple-element.45), channel_id=1, source_target_pairs={{0,16},{4,20},{8,24},{12,28},{16,0},{20,4},{24,8},{28,12},{1,17},{... | collective-permute-start | bytes 786440 | tf_op jit(solution)/shard_map/z4c0/ppermute | solution.py:225
  27.4 20.1 %collective-permute-start.8 = (bf16[8,256,128]{2,1,0:T(8,128)(2,1)S(1)}, bf16[8,256,128]{2,1,0:T(8,128)(2,1)S(1)}, u32[]{:S(2)}, u32[]{:S(2)}) collective-permute-start(bf16[8,256,128]{2,1,0:T(8,128)(2,1)S(1)} %get-tuple-element.52), channel_id=1, source_target_pairs={{0,1},{1,0},{2,3},{3,2},{4,5},{5,4},{6,7},{7,6},{8,9},{9,8},{10,11... | collective-permute-start | bytes 1572872 | tf_op jit(solution)/shard_map/beside1/ppermute | solution.py:225
  27.9 14.1 %collective-permute-start.9 = (bf16[4,256,128]{2,1,0:T(8,128)(2,1)S(1)}, bf16[4,256,128]{2,1,0:T(8,128)(2,1)S(1)}, u32[]{:S(2)}, u32[]{:S(2)}) collective-permute-start(bf16[4,256,128]{2,1,0:T(8,128)(2,1)S(1)} %get-tuple-element.53), channel_id=1, source_target_pairs={{0,2},{1,3},{2,0},{3,1},{4,6},{5,7},{6,4},{7,5},{8,10},{9,11},{10,... | collective-permute-start | bytes 786440 | tf_op jit(solution)/shard_map/y4/ppermute | solution.py:225
  29.5 16.3 %collective-permute-start.10 = (bf16[4,256,128]{2,1,0:T(8,128)(2,1)S(1)}, bf16[4,256,128]{2,1,0:T(8,128)(2,1)S(1)}, u32[]{:S(2)}, u32[]{:S(2)}) collective-permute-start(bf16[4,256,128]{2,1,0:T(8,128)(2,1)S(1)} %get-tuple-element.54), channel_id=1, source_target_pairs={{0,3},{1,2},{2,1},{3,0},{4,7},{5,6},{6,5},{7,4},{8,11},{9,10},{10,... | collective-permute-start | bytes 786440 | tf_op jit(solution)/shard_map/y5/ppermute | solution.py:225
  35.9 56.7 %copy-start.1 = (s32[128]{0:T(128)S(1)}, s32[128]{0:T(128)}, u32[]{:S(2)}) copy-start(s32[128]{0:T(128)} %mirror_ref.1) | copy-start | bytes 1540
  40.3 14.8 %collective-permute-start.7 = (bf16[1,4,4,64,128]{4,3,2,1,0:T(8,128)(2,1)S(1)}, bf16[1,4,4,64,128]{4,3,2,1,0:T(8,128)(2,1)S(1)}, u32[]{:S(2)}, u32[]{:S(2)}) collective-permute-start(bf16[1,4,4,64,128]{4,3,2,1,0:T(8,128)(2,1)S(1)} %get-tuple-element.51), channel_id=1, source_target_pairs={{0,16},{4,20},{8,24},{12,28},{16,0},{20,4},{24,8},{28,12},{1,17},{... | collective-permute-start | bytes 786440 | tf_op jit(solution)/shard_map/z4c1/ppermute | solution.py:225
  40.3 20.8 %collective-permute-start.14 = (bf16[4,256,128]{2,1,0:T(8,128)(2,1)S(1)}, bf16[4,256,128]{2,1,0:T(8,128)(2,1)S(1)}, u32[]{:S(2)}, u32[]{:S(2)}) collective-permute-start(bf16[4,256,128]{2,1,0:T(8,128)(2,1)S(1)} %get-tuple-element.59), channel_id=1, source_target_pairs={{0,2},{1,3},{2,0},{3,1},{4,6},{5,7},{6,4},{7,5},{8,10},{9,11},{10,... | collective-permute-start | bytes 786440 | tf_op jit(solution)/shard_map/y6/ppermute | solution.py:225
  42.0 19.2 %collective-permute-start.15 = (bf16[4,256,128]{2,1,0:T(8,128)(2,1)S(1)}, bf16[4,256,128]{2,1,0:T(8,128)(2,1)S(1)}, u32[]{:S(2)}, u32[]{:S(2)}) collective-permute-start(bf16[4,256,128]{2,1,0:T(8,128)(2,1)S(1)} %get-tuple-element.60), channel_id=1, source_target_pairs={{0,3},{1,2},{2,1},{3,0},{4,7},{5,6},{6,5},{7,4},{8,11},{9,10},{10,... | collective-permute-start | bytes 786440 | tf_op jit(solution)/shard_map/y7/ppermute | solution.py:225
  45.9 13.7 %collective-permute-start.6 = (bf16[2,2,4,64,128]{4,3,2,1,0:T(8,128)(2,1)S(1)}, bf16[2,2,4,64,128]{4,3,2,1,0:T(8,128)(2,1)S(1)}, u32[]{:S(2)}, u32[]{:S(2)}) collective-permute-start(bf16[2,2,4,64,128]{4,3,2,1,0:T(8,128)(2,1)S(1)} %get-tuple-element.50.refs_5_), channel_id=1, source_target_pairs={{0,8},{4,12},{8,0},{12,4},{16,24},{20,28},{24,16},{28,20},{1,9},{5... | collective-permute-start | bytes 786440 | tf_op jit(solution)/shard_map/z2c0/ppermute | solution.py:225
  55.0 13.4 %collective-permute-start.13 = (bf16[1,4,4,64,128]{4,3,2,1,0:T(8,128)(2,1)S(1)}, bf16[1,4,4,64,128]{4,3,2,1,0:T(8,128)(2,1)S(1)}, u32[]{:S(2)}, u32[]{:S(2)}) collective-permute-start(bf16[1,4,4,64,128]{4,3,2,1,0:T(8,128)(2,1)S(1)} %get-tuple-element.58), channel_id=1, source_target_pairs={{0,16},{4,20},{8,24},{12,28},{16,0},{20,4},{24,8},{28,12},{1,17},{... | collective-permute-start | bytes 786440 | tf_op jit(solution)/shard_map/z4c2/ppermute | solution.py:225
  55.1 15.6 %collective-permute-start.12 = (bf16[2,2,4,64,128]{4,3,2,1,0:T(8,128)(2,1)S(1)}, bf16[2,2,4,64,128]{4,3,2,1,0:T(8,128)(2,1)S(1)}, u32[]{:S(2)}, u32[]{:S(2)}) collective-permute-start(bf16[2,2,4,64,128]{4,3,2,1,0:T(8,128)(2,1)S(1)} %get-tuple-element.57.refs_3_), channel_id=1, source_target_pairs={{0,8},{4,12},{8,0},{12,4},{16,24},{20,28},{24,16},{28,20},{1,9},{5... | collective-permute-start | bytes 786440 | tf_op jit(solution)/shard_map/z2c1/ppermute | solution.py:225
  59.6 23.8 %collective-permute-start.11 = (bf16[4,1,4,64,128]{4,3,2,1,0:T(8,128)(2,1)S(1)}, bf16[4,1,4,64,128]{4,3,2,1,0:T(8,128)(2,1)S(1)}, u32[]{:S(2)}, u32[]{:S(2)}) collective-permute-start(bf16[4,1,4,64,128]{4,3,2,1,0:T(8,128)(2,1)S(1)} %merge.12.refs_5_), channel_id=1, source_target_pairs={{0,4},{4,0},{8,12},{12,8},{16,20},{20,16},{24,28},{28,24},{1,5},{5... | collective-permute-start | bytes 786440 | tf_op jit(solution)/shard_map/z1c0/ppermute | solution.py:225
  62.5 8.2 %collective-permute-start.18 = (bf16[1,4,2,64,128]{4,3,2,1,0:T(8,128)(2,1)S(1)}, bf16[1,4,2,64,128]{4,3,2,1,0:T(8,128)(2,1)S(1)}, u32[]{:S(2)}, u32[]{:S(2)}) collective-permute-start(bf16[1,4,2,64,128]{4,3,2,1,0:T(8,128)(2,1)S(1)} %get-tuple-element.65), channel_id=1, source_target_pairs={{0,4},{4,0},{8,12},{12,8},{16,20},{20,16},{24,28},{28,24},{1,5},{5... | collective-permute-start | bytes 393224 | tf_op jit(solution)/shard_map/z1c4/ppermute | solution.py:225
  68.5 14.9 %collective-permute-start.17 = (bf16[2,2,4,64,128]{4,3,2,1,0:T(8,128)(2,1)S(1)}, bf16[2,2,4,64,128]{4,3,2,1,0:T(8,128)(2,1)S(1)}, u32[]{:S(2)}, u32[]{:S(2)}) collective-permute-start(bf16[2,2,4,64,128]{4,3,2,1,0:T(8,128)(2,1)S(1)} %get-tuple-element.63.refs_3_), channel_id=1, source_target_pairs={{0,8},{4,12},{8,0},{12,4},{16,24},{20,28},{24,16},{28,20},{1,9},{5... | collective-permute-start | bytes 786440 | tf_op jit(solution)/shard_map/z2c2/ppermute | solution.py:225
  68.6 9.5 %collective-permute-start.20 = (bf16[1,4,2,64,128]{4,3,2,1,0:T(8,128)(2,1)S(1)}, bf16[1,4,2,64,128]{4,3,2,1,0:T(8,128)(2,1)S(1)}, u32[]{:S(2)}, u32[]{:S(2)}) collective-permute-start(bf16[1,4,2,64,128]{4,3,2,1,0:T(8,128)(2,1)S(1)} %get-tuple-element.66), channel_id=1, source_target_pairs={{0,16},{4,20},{8,24},{12,28},{16,0},{20,4},{24,8},{28,12},{1,17},{... | collective-permute-start | bytes 393224 | tf_op jit(solution)/shard_map/z4c3/ppermute | solution.py:225
  70.8 12.6 %collective-permute-start.19 = (bf16[2,2,2,64,128]{4,3,2,1,0:T(8,128)(2,1)S(1)}, bf16[2,2,2,64,128]{4,3,2,1,0:T(8,128)(2,1)S(1)}, u32[]{:S(2)}, u32[]{:S(2)}) collective-permute-start(bf16[2,2,2,64,128]{4,3,2,1,0:T(8,128)(2,1)S(1)} %merge.15.refs_2_), channel_id=1, source_target_pairs={{0,8},{4,12},{8,0},{12,4},{16,24},{20,28},{24,16},{28,20},{1,9},{5... | collective-permute-start | bytes 393224 | tf_op jit(solution)/shard_map/z2c4/ppermute | solution.py:225
  70.9 14.2 %collective-permute-start.16 = (bf16[4,1,4,64,128]{4,3,2,1,0:T(8,128)(2,1)S(1)}, bf16[4,1,4,64,128]{4,3,2,1,0:T(8,128)(2,1)S(1)}, u32[]{:S(2)}, u32[]{:S(2)}) collective-permute-start(bf16[4,1,4,64,128]{4,3,2,1,0:T(8,128)(2,1)S(1)} %merge.14.refs_2_), channel_id=1, source_target_pairs={{0,4},{4,0},{8,12},{12,8},{16,20},{20,16},{24,28},{28,24},{1,5},{5... | collective-permute-start | bytes 786440 | tf_op jit(solution)/shard_map/z1c1/ppermute | solution.py:225
  78.0 7.1 %collective-permute-start.22 = (bf16[2,2,2,64,128]{4,3,2,1,0:T(8,128)(2,1)S(1)}, bf16[2,2,2,64,128]{4,3,2,1,0:T(8,128)(2,1)S(1)}, u32[]{:S(2)}, u32[]{:S(2)}) collective-permute-start(bf16[2,2,2,64,128]{4,3,2,1,0:T(8,128)(2,1)S(1)} %merge.16.refs_3_), channel_id=1, source_target_pairs={{0,8},{4,12},{8,0},{12,4},{16,24},{20,28},{24,16},{28,20},{1,9},{5... | collective-permute-start | bytes 393224 | tf_op jit(solution)/shard_map/z2c3/ppermute | solution.py:225
  83.4 9.2 %collective-permute-start.21 = (bf16[4,1,4,64,128]{4,3,2,1,0:T(8,128)(2,1)S(1)}, bf16[4,1,4,64,128]{4,3,2,1,0:T(8,128)(2,1)S(1)}, u32[]{:S(2)}, u32[]{:S(2)}) collective-permute-start(bf16[4,1,4,64,128]{4,3,2,1,0:T(8,128)(2,1)S(1)} %merge.18.refs_3_), channel_id=1, source_target_pairs={{0,4},{4,0},{8,12},{12,8},{16,20},{20,16},{24,28},{28,24},{1,5},{5... | collective-permute-start | bytes 786440 | tf_op jit(solution)/shard_map/z1c2/ppermute | solution.py:225
  85.0 6.9 %collective-permute-start.24 = (bf16[4,1,2,64,128]{4,3,2,1,0:T(8,128)(2,1)S(1)}, bf16[4,1,2,64,128]{4,3,2,1,0:T(8,128)(2,1)S(1)}, u32[]{:S(2)}, u32[]{:S(2)}) collective-permute-start(bf16[4,1,2,64,128]{4,3,2,1,0:T(8,128)(2,1)S(1)} %merge.17.refs_3_), channel_id=1, source_target_pairs={{0,16},{4,20},{8,24},{12,28},{16,0},{20,4},{24,8},{28,12},{1,17},{... | collective-permute-start | bytes 393224 | tf_op jit(solution)/shard_map/z4c4/ppermute | solution.py:225
  85.2 7.4 %collective-permute-start.23 = (bf16[4,1,2,64,128]{4,3,2,1,0:T(8,128)(2,1)S(1)}, bf16[4,1,2,64,128]{4,3,2,1,0:T(8,128)(2,1)S(1)}, u32[]{:S(2)}, u32[]{:S(2)}) collective-permute-start(bf16[4,1,2,64,128]{4,3,2,1,0:T(8,128)(2,1)S(1)} %merge.19), channel_id=1, source_target_pairs={{0,4},{4,0},{8,12},{12,8},{16,20},{20,16},{24,28},{28,24},{1,5},{5... | collective-permute-start | bytes 393224 | tf_op jit(solution)/shard_map/z1c3/ppermute | solution.py:225

commit v9 on v7

--- a/solution.py
+++ b/solution.py
@@ -9,7 +9,9 @@
 
 LANES = 128
 STEP = 64
-CHUNKS = (4, 4, 4, 4)
+BATCHES = ((4, 4), (4, 4))
+CHUNKS = sum(BATCHES, ())
+SIZES = ((1,), (1,), (1, 2), (-1, 2))
 PART = 256
 MIB = 1024 * 1024
 COST = pl.CostEstimate(flops=1024, bytes_accessed=1024, transcendentals=0)
@@ -19,32 +21,32 @@
 IN_HBM = pl.BlockSpec(memory_space=pltpu.MemorySpace.HBM)
 
 
-def quarter_kernel(rows, n_mo, blocks, place_ref, x_ref, c_hbm, *refs):
-    outs, (c_ref, turn_ref, held, c_sem, sems) = refs[:-5], refs[-5:]
+def quarter_kernel(rows, n_mo, blocks, n_after, place_ref, x_ref, c_ref, *refs):
+    refs = refs[n_after:]
+    outs, (turn_ref, held, sems) = refs[:-3], refs[-3:]
     at = pl.program_id(0)
-    step, k_all, depth = x_ref.shape
+    step, some, depth = x_ref.shape
     padded = held.shape[2]
-    many = PART // k_all
+    many = PART // some
 
     @pl.when(at == 0)
     def _():
-        copy = pltpu.make_async_copy(c_hbm, c_ref, c_sem)
-        copy.start()
         to = lax.broadcasted_iota(jnp.int32, (PART, PART), 0)
         source = lax.broadcasted_iota(jnp.int32, (PART, PART), 1)
-        turn_ref[...] = (source == to % many * k_all + to // many).astype(jnp.float32).astype(jnp.bfloat16)
-        copy.wait()
-
-    x = x_ref[...].reshape(step * k_all, depth)
+        bits = many.bit_length() - 1
+        is_source = source == (to & (many - 1)) * some + (to >> bits)
+        turn_ref[...] = jnp.where(is_source, 1.0, 0.0).astype(jnp.bfloat16)
+
+    x = x_ref[...].reshape(step * some, depth)
     product = jnp.dot(x, c_ref[...], preferred_element_type=jnp.float32)
     line = lax.broadcasted_iota(jnp.int32, product.shape, 0)
-    product = jnp.where(line < (rows - at * step) * k_all, product, 0.0).astype(jnp.bfloat16)
+    product = jnp.where(line < (rows - at * step) * some, product, 0.0).astype(jnp.bfloat16)
     for part in range(step // many):
         lines = jnp.dot(
             turn_ref[...], product[part * PART : (part + 1) * PART], preferred_element_type=jnp.float32
         ).astype(jnp.bfloat16)
         here = pl.ds(pl.multiple_of(at * step + part * many, many), many)
-        for k in range(k_all):
+        for k in range(some):
             for d in range(n_mo):
                 held[d, k, here] = lines[k * many : (k + 1) * many, d * LANES : (d + 1) * LANES]
     here = pl.ds(pl.multiple_of(at * step, step), step)
@@ -59,24 +61,25 @@
             pltpu.make_async_copy(mine, out, sems.at[n]).wait()
 
 
-def quarter_of(place, by_r, coeffs, n_mo, padded):
-    rows, k_all, depth = by_r.shape
+def quarter_of(place, by_r, coeffs, n_mo, padded, batch, after):
+    rows, _, depth = by_r.shape
     orbitals = coeffs.shape[1]
-    blocks = [(0, 0), (1, 0)] + [(o, sum(CHUNKS[:c])) for c in range(len(CHUNKS)) for o in range(2, n_mo)]
-    sizes = [k_all] * 2 + [kc for kc in CHUNKS for _ in range(2, n_mo)]
+    chunks = BATCHES[batch]
+    some = sum(chunks)
+    blocks = [(0, 0), (1, 0)] + [(o, sum(chunks[:c])) for c in range(len(chunks)) for o in range(2, n_mo)]
+    sizes = [some] * 2 + [kc for kc in chunks for _ in range(2, n_mo)]
     outs = [jax.ShapeDtypeStruct((kc, padded, LANES), jnp.bfloat16) for kc in sizes]
     out = pl.pallas_call(
-        functools.partial(quarter_kernel, rows, n_mo, blocks),
+        functools.partial(quarter_kernel, rows, n_mo, blocks, len(after)),
         grid_spec=pltpu.PrefetchScalarGridSpec(
             num_scalar_prefetch=1,
             grid=(padded // STEP,),
-            in_specs=[pl.BlockSpec((STEP, k_all, depth), lambda r, place: (r, 0, 0)), IN_HBM],
+            in_specs=[pl.BlockSpec((STEP, some, depth), lambda r, place: (r, batch, 0)), IN_VMEM]
+            + [ANYWHERE] * len(after),
             out_specs=[IN_HBM] * len(outs),
             scratch_shapes=[
-                pltpu.VMEM((depth, orbitals), jnp.bfloat16),
                 pltpu.VMEM((PART, PART), jnp.bfloat16),
-                pltpu.VMEM((n_mo, k_all, padded, LANES), jnp.bfloat16),
-                pltpu.SemaphoreType.DMA,
+                pltpu.VMEM((n_mo, some, padded, LANES), jnp.bfloat16),
                 pltpu.SemaphoreType.DMA((len(outs),)),
             ],
         ),
@@ -84,9 +87,9 @@
         compiler_params=pltpu.CompilerParams(vmem_limit_bytes=50 * MIB),
         cost_estimate=COST,
         name="quarter",
-    )(place, by_r, coeffs)
+    )(place, by_r, coeffs, *after)
     far = n_mo - 2
-    return out[:2], [out[2 + far * c : 2 + far * (c + 1)] for c in range(len(CHUNKS))]
+    return out[:2], [out[2 + far * c : 2 + far * (c + 1)] for c in range(len(chunks))]
 
 
 def turn_kernel(rows, c_ref, *refs):
@@ -147,30 +150,51 @@
     )(place, *blocks, turned, *after)
 
 
-def merge_kernel(picks, *refs):
-    at = 0
-    for x, pick in zip(refs, picks):
-        for i in range(x.shape[0]):
-            for n, o in enumerate(pick):
-                refs[-1][at, n] = x[i, o]
-            at += 1
-
-
-def merge(parts, picks, after):
-    shape = (sum(x.shape[0] for x in parts), len(picks[0]), *parts[0].shape[2:])
+def merge_kernel(n_parts, picks, *refs):
+    outs = refs[len(refs) - len(picks) :]
+    for out, its in zip(outs, picks):
+        at = 0
+        for x, pick in zip(refs[:n_parts], its):
+            for i in range(x.shape[0]):
+                for n, o in enumerate(pick):
+                    out[at, n] = x[i, o]
+                at += 1
+
+
+def merge(parts, picks, later, after):
+    lines, n = sum(x.shape[0] for x in parts), len(parts)
+    out = pl.pallas_call(
+        functools.partial(merge_kernel, n, picks),
+        in_specs=[IN_VMEM] * n + [IN_HBM] * len(later) + [ANYWHERE] * len(after),
+        out_specs=[IN_HBM] * len(later) + [IN_VMEM] * len(picks),
+        out_shape=[jax.ShapeDtypeStruct(x.shape, x.dtype) for x in later]
+        + [jax.ShapeDtypeStruct((lines, len(its[0]), *parts[0].shape[2:]), jnp.bfloat16) for its in picks],
+        input_output_aliases={n + m: m for m in range(len(later))},
+        compiler_params=pltpu.CompilerParams(vmem_limit_bytes=24 * MIB),
+        cost_estimate=COST,
+        name="merge",
+    )(*parts, *later, *after)
+    return list(out[len(later) :]), list(out[: len(later)])
+
+
+def wait_kernel(*refs):
+    refs[-1][...] = jnp.zeros_like(refs[-1])
+
+
+def wait_for(after):
     return pl.pallas_call(
-        functools.partial(merge_kernel, picks),
-        in_specs=[IN_VMEM] * len(parts) + [ANYWHERE] * len(after),
+        wait_kernel,
+        in_specs=[ANYWHERE] * len(after),
         out_specs=IN_VMEM,
-        out_shape=jax.ShapeDtypeStruct(shape, jnp.bfloat16),
-        compiler_params=pltpu.CompilerParams(vmem_limit_bytes=24 * MIB),
-        cost_estimate=COST,
-        name="merge",
-    )(*parts, *after)
+        out_shape=jax.ShapeDtypeStruct((8, LANES), jnp.float32),
+        compiler_params=pltpu.CompilerParams(vmem_limit_bytes=24 * MIB),
+        cost_estimate=COST,
+        name="wait",
+    )(*after)
 
 
 def combine_kernel(sources, k_all, per_step, mirror_ref, place_ref, *refs):
-    pieces, out_ref, held = refs[:-2], refs[-2], refs[-1]
+    pieces, out_ref, held = refs[: len(sources)], refs[-2], refs[-1]
     step = pl.program_id(0)
 
     @pl.when(step == 0)
@@ -185,7 +209,7 @@
         out_ref[n] = 0.5 * (held[k].astype(jnp.float32) + held[mirror_ref[k]].astype(jnp.float32))
 
 
-def combine(pieces, sources, mirror, place, n_pair):
+def combine(pieces, sources, mirror, place, n_pair, after):
     block, lanes = pieces[0].shape[-2:]
     k_all = sum(CHUNKS)
     rows = n_pair * k_all
@@ -195,7 +219,7 @@
         grid_spec=pltpu.PrefetchScalarGridSpec(
             num_scalar_prefetch=2,
             grid=(rows // per_step,),
-            in_specs=[IN_VMEM] * len(pieces),
+            in_specs=[IN_VMEM] * len(pieces) + [ANYWHERE] * len(after),
             out_specs=pl.BlockSpec((per_step, block, lanes), lambda k, m, place: (k, 0, 0)),
             scratch_shapes=[pltpu.VMEM((rows, block, lanes), jnp.bfloat16)],
         ),
@@ -203,12 +227,23 @@
         compiler_params=pltpu.CompilerParams(vmem_limit_bytes=24 * MIB),
         cost_estimate=COST,
         name="combine",
-    )(mirror, place, *pieces)
+    )(mirror, place, *pieces, *after)
 
 
 def flipped(x, axis, size, offset, name):
     with jax.named_scope(name):
         return lax.ppermute(x, axis, [(i, i ^ offset) for i in range(size)])
+
+
+def digits(n_pair, sizes):
+    bits = [1 << n for n in reversed(range(n_pair.bit_length() - 1))]
+    masks = []
+    while bits:
+        size = sizes[min(len(masks), len(sizes) - 1)]
+        some = bits[:size] if size > 0 else bits[size:]
+        masks.append(sum(some))
+        bits = [bit for bit in bits if bit not in some]
+    return masks
 
 
 def on_device(n_pair, n_mo, integrals, coeffs, mirror):
@@ -217,43 +252,67 @@
     n_near = n_pair // 2
     by_r = jnp.transpose(integrals, (1, 0, 2))
     place = jnp.stack([lax.axis_index("mo"), lax.axis_index("pair")]).astype(jnp.int32)
-    (own, beside), queue = quarter_of(place, by_r, coeffs, n_mo, padded)
-    beside = flipped(beside, "mo", n_mo, 1, "beside")
     last = len(CHUNKS) - 1
     firsts = [sum(CHUNKS[:c]) for c in range(last + 1)]
-    down = [1 << n for n in reversed(range(n_pair.bit_length() - 1))]
-    orders = [down] * last + [down[::-1]]
-    turned, parts, owners, offsets, token = None, [[] for _ in CHUNKS], [[] for _ in CHUNKS], [[] for _ in CHUNKS], []
+
+    near, queue, token = [], [], []
+    for batch, chunks in enumerate(BATCHES):
+        (own, beside), far = quarter_of(place, by_r, coeffs, n_mo, padded, batch, token)
+        beside = flipped(beside, "mo", n_mo, 1, f"beside{batch}")
+        near += [(own, beside, sum(chunks[:c])) for c in range(len(chunks))]
+        queue += far
+        token = [own]
 
     def arrive(c):
         return [flipped(x, "mo", n_mo, o, f"y{2 * c + o - 2}") for o, x in enumerate(queue[c], 2)]
 
     arrived = [arrive(0)]
-    turned, queue[1] = turn(coeffs, n_mo, padded, queue[1], arrived[0][:1])
+    turned, queue[1] = turn(coeffs, n_mo, padded, queue[1], arrived[0][:1] + token)
     arrived += [arrive(c) for c in range(1, last + 1)]
 
     steps = [(c, c, 0) for c in range(last + 1)]
-    for n in range(1, len(down)):
-        steps += [(c + n + (0.5 - n / 10 if c + n == last else n / 10), c, n) for c in range(last)]
-        steps.append((last + n - (0.55 if n == 1 else 0.95), last, n))
+    levels = [digits(n_pair, sizes) for sizes in SIZES]
+    for c, masks in enumerate(levels):
+        steps += [(c + n + n / 10 - 0.95 * (c == last), c, n) for n in range(1, len(masks))]
+    parts, owners, offsets, token = [[] for _ in CHUNKS], [[] for _ in CHUNKS], [[] for _ in CHUNKS], []
+    waiting = []
+
+    def plan(c, level):
+        mask, gone = levels[c][level], sum(levels[c][:level])
+        flips = [o for o in range(1, n_pair) if not o & ~mask][::-1]
+        left = [o for o in range(n_pair) if not o & gone]
+        return [o for o in left if not o & mask], flips, [[o for o in left if o & mask == flip] for flip in flips]
+
+    def send(c, level, messages):
+        _, flips, sent = plan(c, level)
+        before = [o for group in offsets[c] for o in group]
+        for flip, some, message in zip(flips, sent, messages):
+            offsets[c].append([o ^ flip for o in before])
+            owners[c].append([o ^ flip for o in some])
+            parts[c].append(flipped(message, "pair", n_pair, flip, f"z{flip}c{c}"))
+
     for _, c, level in sorted(steps):
-        flips = orders[c]
-        flip, gone = flips[level], sum(flips[:level])
-        left = [o for o in range(n_pair) if not o & gone]
-        kept, sent = [o for o in left if not o & flip], [o for o in left if o & flip]
+        kept, _, sent = plan(c, level)
         if level == 0:
-            keep, message = half_of(place, [own, beside, *arrived[c]], turned, firsts[c], [kept, sent], token)
+            blocks = [*near[c][:2], *arrived[c]]
+            keep, *messages = half_of(place, blocks, turned, near[c][2], [kept, *sent], token)
             parts[c], owners[c], offsets[c] = [keep], [kept], [[0]]
         else:
-            after = token + (parts[c - 1][-1:] if level == len(flips) - 1 and 0 < c < last else [])
-            message = merge(parts[c], [[its.index(o) for o in sent] for its in owners[c]], after)
-        token = [message]
-        offsets[c].append([o ^ flip for group in offsets[c] for o in group])
-        owners[c].append([o ^ flip for o in sent])
-        parts[c].append(flipped(message, "pair", n_pair, flip, f"z{flip}c{c}"))
+            picks = [[[its.index(o) for o in some] for its in owners[c]] for some in sent]
+            done = parts[c - 1][-1:] if level == 2 and c else []
+            later = waiting if c == last and level == 1 else []
+            messages, later = merge(parts[c], picks, later, token + done)
+            if later:
+                send(last - 1, 1, later)
+        token = messages[:1]
+        if c == last - 1 and level == 1:
+            waiting = messages
+        else:
+            send(c, level, messages)
+    token = [wait_for([x for x in parts[last][-3:]] + token)]
     pieces = [x for chunk in parts for x in chunk]
     sources = [(tuple(group), first) for chunk, first in zip(offsets, firsts) for group in chunk]
-    return combine(pieces, sources, mirror, place, n_pair)
+    return combine(pieces, sources, mirror, place, n_pair, token)
 
 
 def solution(mesh):

time: 104 us -> 90.4 us (0.87)
  waiting for transfers between devices: 56.3 us -> 30.1 us
  starting transfers between devices: 25.5 us -> 36.8 us
  Pallas kernels: 19.2 us -> 21.8 us
  local copies, waits for them, and re-layouts: 2.45 us -> 1.23 us
    ppermute x21 -> x24, waiting for transfers between devices: 56.3 us -> 30.1 us  [flipped(): return lax.ppermute(x, axis, [(i, i ^ offset) for i in range(size)])]
    ppermute x21 -> x24, starting transfers between devices: 25.5 us -> 36.8 us  [flipped(): return lax.ppermute(x, axis, [(i, i ^ offset) for i in range(size)])]
    pallas_call x9, Pallas kernels: 10.4 us -> 12.9 us  [the longest x2 12.8 us: quarter_of(): pl.pallas_call(functools.partial(quarter_kernel, rows, n_mo, blocks, len(...]
    unnamed x8 -> x5, local copies, waits for them, and re-layouts: 2.45 us -> 1.23 us
  transfers between devices with their start and end apart: 21 -> 24, of which waited for: 10 -> 15; matrix products, arithmetic and copies ran while one was open for 0% -> 0% of each run, Pallas kernels for 6% -> 13%
where the time goes in v9:
time: 90.4 us; the launch traced here: 90.1 us
  starting transfers between devices  36.8 us (41%)
  waiting for transfers between devices  30.1 us (33%)
  Pallas kernels  21.8 us (24%)
  local copies, waits for them, and re-layouts  1.23 us (1%)
    ppermute x24, starting transfers between devices, flipped(): return lax.ppermute(x, axis, [(i, i ^ offset) for i in range(size)])  36.8 us
    ppermute x24, waiting for transfers between devices, flipped(): return lax.ppermute(x, axis, [(i, i ^ offset) for i in range(size)])  30.1 us
    pallas_call x2, Pallas kernels, quarter_of(): pl.pallas_call(functools.partial(quarter_kernel, rows, n_mo, blocks, len(...  12.8 us
    pallas_call x4, Pallas kernels, half_of(): pl.pallas_call(functools.partial(half_kernel, n_mo, first, owners), in_sp...  5.21 us
    pallas_call x1, Pallas kernels, combine(): pl.pallas_call(functools.partial(combine_kernel, sources, k_all, per_step...  3.29 us
  transfers between devices with their start and end apart: 24, of which 15 were waited for; matrix products, arithmetic and copies ran while one was open for 0% of the time, Pallas kernels for 13%

profile of v9, /device:TPU:0, one launch (start us, length us, event | category | flops | bytes accessed | tf_op | source)
XLA Modules:
  0.0 90.1 jit_solution(548424825959014286)
XLA Ops:
  0.0 0.1 pad_add_fusion.place_ref
  0.1 1.2 %copy-done = bf16[1000,512]{1,0:T(8,128)(2,1)S(1)} copy-done((bf16[1000,512]{1,0:T(8,128)(2,1)S(1)}, bf16[1000,512]{1,0:T(8,128)(2,1)}, u32[]{:S(2)}) %copy-start) | copy-done | bytes 1024024
  1.3 6.4 %quarter.2 = (bf16[8,256,128]{2,1,0:T(8,128)(2,1)S(1)}, bf16[8,256,128]{2,1,0:T(8,128)(2,1)S(1)}, bf16[4,256,128]{2,1,0:T(8,128)(2,1)S(1)}, bf16[4,256,128]{2,1,...) custom-call(s32[2]{0:T(128)S(1)} %pad_add_fusion.place_ref, ...), custom_call_target="tpu_custom_call" | custom-call | flops 1024 | bytes 1024 | tf_op jit(solution)/shard_map/quarter/pallas_call | solution.py:72
  7.7 0.5 collective-permute-start
  8.2 2.6 %collective-permute-start.1 = (bf16[4,256,128]{2,1,0:T(8,128)(2,1)S(1)}, bf16[4,256,128]{2,1,0:T(8,128)(2,1)S(1)}, u32[]{:S(2)}, u32[]{:S(2)}) collective-permute-start(bf16[4,256,128]{2,1,0:T(8,128)(2,1)S(1)} %get-tuple-element.39), channel_id=1, source_target_pairs={{0,2},{1,3},{2,0},{3,1},{4,6},{5,7},{6,4},{7,5},{8,10},{9,11},{10,... | collective-permute-start | bytes 786440 | tf_op jit(solution)/shard_map/y0/ppermute | solution.py:235
  10.8 0.1 collective-permute-start.2
  10.9 6.4 %quarter.3 = (bf16[8,256,128]{2,1,0:T(8,128)(2,1)S(1)}, bf16[8,256,128]{2,1,0:T(8,128)(2,1)S(1)}, bf16[4,256,128]{2,1,0:T(8,128)(2,1)S(1)}, bf16[4,256,128]{2,1,...) custom-call(s32[2]{0:T(128)S(1)} %pad_add_fusion.place_ref, ...), custom_call_target="tpu_custom_call" | custom-call | flops 1024 | bytes 1024 | tf_op jit(solution)/shard_map/quarter/pallas_call | solution.py:72
  17.3 0.7 collective-permute-done.1.refs_2_
  18.0 0.4 turn.1
  18.3 2.0 %collective-permute-start.4 = (bf16[4,256,128]{2,1,0:T(8,128)(2,1)S(1)}, bf16[4,256,128]{2,1,0:T(8,128)(2,1)S(1)}, u32[]{:S(2)}, u32[]{:S(2)}) collective-permute-start(bf16[4,256,128]{2,1,0:T(8,128)(2,1)S(1)} %get-tuple-element.47), channel_id=1, source_target_pairs={{0,2},{1,3},{2,0},{3,1},{4,6},{5,7},{6,4},{7,5},{8,10},{9,11},{10,... | collective-permute-start | bytes 786440 | tf_op jit(solution)/shard_map/y2/ppermute | solution.py:235
  20.4 0.2 collective-permute-start.5
  20.6 2.5 %collective-permute-done.2.refs_3_ = bf16[4,256,128]{2,1,0:T(8,128)(2,1)S(1)} collective-permute-done((bf16[4,256,128]{2,1,0:T(8,128)(2,1)S(1)}, bf16[4,256,128]{2,1,0:T(8,128)(2,1)S(1)}, u32[]{:S(2)}, u32[]{:S(2)}) %collective-permute-start.2) | collective-permute-done | bytes 262176 | tf_op jit(solution)/shard_map/y1/ppermute | solution.py:235
  23.1 0.0 collective-permute-done.refs_1_
  23.1 1.3 %half.4 = (bf16[1,4,4,64,128]{4,3,2,1,0:T(8,128)(2,1)S(1)}, bf16[1,4,4,64,128]{4,3,2,1,0:T(8,128)(2,1)S(1)}) custom-call(s32[2]{0:T(128)S(1)} %pad_add_fusion.place_ref, bf16[8,256,128]{2,1,0:T(8,128)(2,1)S(1)} %get-tuple-element.37.refs_0_, bf16[8,256,128]{2,1,0:T(8,128)(2,1)S(1)} %collective-permute-done.refs_1_, ...), custom_call_target="tpu_custom_call" | custom-call | flops 1024 | bytes 1024 | tf_op jit(solution)/shard_map/half/pallas_call | solution.py:141
  24.4 0.0 copy-start.1
  24.4 2.7 %collective-permute-start.3 = (bf16[1,4,4,64,128]{4,3,2,1,0:T(8,128)(2,1)S(1)}, bf16[1,4,4,64,128]{4,3,2,1,0:T(8,128)(2,1)S(1)}, u32[]{:S(2)}, u32[]{:S(2)}) collective-permute-start(bf16[1,4,4,64,128]{4,3,2,1,0:T(8,128)(2,1)S(1)} %get-tuple-element.46.refs_5_), channel_id=1, source_target_pairs={{0,16},{4,20},{8,24},{12,28},{16,0},{20,4},{24,8},{28,12},{1,17},{... | collective-permute-start | bytes 786440 | tf_op jit(solution)/shard_map/z4c0/ppermute | solution.py:235
  27.1 1.5 %collective-permute-start.9 = (bf16[4,256,128]{2,1,0:T(8,128)(2,1)S(1)}, bf16[4,256,128]{2,1,0:T(8,128)(2,1)S(1)}, u32[]{:S(2)}, u32[]{:S(2)}) collective-permute-start(bf16[4,256,128]{2,1,0:T(8,128)(2,1)S(1)} %get-tuple-element.52), channel_id=1, source_target_pairs={{0,2},{1,3},{2,0},{3,1},{4,6},{5,7},{6,4},{7,5},{8,10},{9,11},{10,... | collective-permute-start | bytes 786440 | tf_op jit(solution)/shard_map/y4/ppermute | solution.py:235
  28.6 0.6 collective-permute-done.4.refs_2_
  29.2 0.8 collective-permute-start.10
  30.0 4.3 %collective-permute-done.5.refs_3_ = bf16[4,256,128]{2,1,0:T(8,128)(2,1)S(1)} collective-permute-done((bf16[4,256,128]{2,1,0:T(8,128)(2,1)S(1)}, bf16[4,256,128]{2,1,0:T(8,128)(2,1)S(1)}, u32[]{:S(2)}, u32[]{:S(2)}) %collective-permute-start.5) | collective-permute-done | bytes 262176 | tf_op jit(solution)/shard_map/y3/ppermute | solution.py:235
  34.3 1.6 %collective-permute-start.13 = (bf16[4,256,128]{2,1,0:T(8,128)(2,1)S(1)}, bf16[4,256,128]{2,1,0:T(8,128)(2,1)S(1)}, u32[]{:S(2)}, u32[]{:S(2)}) collective-permute-start(bf16[4,256,128]{2,1,0:T(8,128)(2,1)S(1)} %get-tuple-element.55), channel_id=1, source_target_pairs={{0,2},{1,3},{2,0},{3,1},{4,6},{5,7},{6,4},{7,5},{8,10},{9,11},{10,... | collective-permute-start | bytes 786440 | tf_op jit(solution)/shard_map/y6/ppermute | solution.py:235
  35.9 1.3 %half.5 = (bf16[1,4,4,64,128]{4,3,2,1,0:T(8,128)(2,1)S(1)}, bf16[1,4,4,64,128]{4,3,2,1,0:T(8,128)(2,1)S(1)}) custom-call(s32[2]{0:T(128)S(1)} %pad_add_fusion.place_ref, bf16[8,256,128]{2,1,0:T(8,128)(2,1)S(1)} %get-tuple-element.37.refs_0_, bf16[8,256,128]{2,1,0:T(8,128)(2,1)S(1)} %collective-permute-done.refs_1_, ...), custom_call_target="tpu_custom_call" | custom-call | flops 1024 | bytes 1024 | tf_op jit(solution)/shard_map/half/pallas_call | solution.py:141
  37.2 2.7 %collective-permute-done.3.refs_1_ = bf16[1,4,4,64,128]{4,3,2,1,0:T(8,128)(2,1)S(1)} collective-permute-done((bf16[1,4,4,64,128]{4,3,2,1,0:T(8,128)(2,1)S(1)}, bf16[1,4,4,64,128]{4,3,2,1,0:T(8,128)(2,1)S(1)}, u32[]{:S(2)}, u32[]{:S(2)}) %collective-permute-start.3) | collective-permute-done | bytes 262176 | tf_op jit(solution)/shard_map/z4c0/ppermute | solution.py:235
  39.9 0.5 collective-permute-done.9.refs_2_
  40.4 3.7 %collective-permute-start.6 = (bf16[2,2,4,64,128]{4,3,2,1,0:T(8,128)(2,1)S(1)}, bf16[2,2,4,64,128]{4,3,2,1,0:T(8,128)(2,1)S(1)}, u32[]{:S(2)}, u32[]{:S(2)}) collective-permute-start(bf16[2,2,4,64,128]{4,3,2,1,0:T(8,128)(2,1)S(1)} %merge.6.refs_5_), channel_id=1, source_target_pairs={{0,8},{4,12},{8,0},{12,4},{16,24},{20,28},{24,16},{28,20},{1,9},{5... | collective-permute-start | bytes 786440 | tf_op jit(solution)/shard_map/z2c0/ppermute | solution.py:235
  44.1 1.4 %collective-permute-done.10.refs_3_ = bf16[4,256,128]{2,1,0:T(8,128)(2,1)S(1)} collective-permute-done((bf16[4,256,128]{2,1,0:T(8,128)(2,1)S(1)}, bf16[4,256,128]{2,1,0:T(8,128)(2,1)S(1)}, u32[]{:S(2)}, u32[]{:S(2)}) %collective-permute-start.10) | collective-permute-done | bytes 262176 | tf_op jit(solution)/shard_map/y5/ppermute | solution.py:235
  45.5 2.2 %collective-permute-start.14 = (bf16[4,256,128]{2,1,0:T(8,128)(2,1)S(1)}, bf16[4,256,128]{2,1,0:T(8,128)(2,1)S(1)}, u32[]{:S(2)}, u32[]{:S(2)}) collective-permute-start(bf16[4,256,128]{2,1,0:T(8,128)(2,1)S(1)} %get-tuple-element.56), channel_id=1, source_target_pairs={{0,3},{1,2},{2,1},{3,0},{4,7},{5,6},{6,5},{7,4},{8,11},{9,10},{10,... | collective-permute-start | bytes 786440 | tf_op jit(solution)/shard_map/y7/ppermute | solution.py:235
  47.7 1.3 %half.6 = (bf16[1,4,4,64,128]{4,3,2,1,0:T(8,128)(2,1)S(1)}, bf16[1,4,4,64,128]{4,3,2,1,0:T(8,128)(2,1)S(1)}) custom-call(s32[2]{0:T(128)S(1)} %pad_add_fusion.place_ref, bf16[8,256,128]{2,1,0:T(8,128)(2,1)S(1)} %get-tuple-element.43.refs_3_.refs_0_, bf16[8,256,128]{2,1,0:T(8,128)(2,1)S(1)} %collective-permute-done.8.refs_1_, ...), custom_call_target="tpu_custom_call" | custom-call | flops 1024 | bytes 1024 | tf_op jit(solution)/shard_map/half/pallas_call | solution.py:141
  49.0 2.7 %collective-permute-start.16 = (bf16[1,4,4,64,128]{4,3,2,1,0:T(8,128)(2,1)S(1)}, bf16[1,4,4,64,128]{4,3,2,1,0:T(8,128)(2,1)S(1)}, u32[]{:S(2)}, u32[]{:S(2)}) collective-permute-start(bf16[1,4,4,64,128]{4,3,2,1,0:T(8,128)(2,1)S(1)} %get-tuple-element.54.refs_2_), channel_id=1, source_target_pairs={{0,16},{4,20},{8,24},{12,28},{16,0},{20,4},{24,8},{28,12},{1,17},{... | collective-permute-start | bytes 786440 | tf_op jit(solution)/shard_map/z4c2/ppermute | solution.py:235
  51.7 4.5 %collective-permute-done.7.refs_1_.refs_5_ = bf16[1,4,4,64,128]{4,3,2,1,0:T(8,128)(2,1)S(1)} collective-permute-done((bf16[1,4,4,64,128]{4,3,2,1,0:T(8,128)(2,1)S(1)}, bf16[1,4,4,64,128]{4,3,2,1,0:T(8,128)(2,1)S(1)}, u32[]{:S(2)}, u32[]{:S(2)}) %collective-permute-start.7) | collective-permute-done | bytes 262176 | tf_op jit(solution)/shard_map/z4c1/ppermute | solution.py:235
  56.2 0.5 collective-permute-done.14.refs_3_
  56.8 1.3 %half.7 = (bf16[1,4,4,64,128]{4,3,2,1,0:T(8,128)(2,1)S(1)}, bf16[1,4,4,64,128]{4,3,2,1,0:T(8,128)(2,1)S(1)}) custom-call(s32[2]{0:T(128)S(1)} %pad_add_fusion.place_ref, bf16[8,256,128]{2,1,0:T(8,128)(2,1)S(1)} %get-tuple-element.43.refs_3_.refs_0_, bf16[8,256,128]{2,1,0:T(8,128)(2,1)S(1)} %collective-permute-done.8.refs_1_, ...), custom_call_target="tpu_custom_call" | custom-call | flops 1024 | bytes 1024 | tf_op jit(solution)/shard_map/half/pallas_call | solution.py:141
  58.1 1.6 %collective-permute-start.15 = (bf16[1,4,4,64,128]{4,3,2,1,0:T(8,128)(2,1)S(1)}, bf16[1,4,4,64,128]{4,3,2,1,0:T(8,128)(2,1)S(1)}, u32[]{:S(2)}, u32[]{:S(2)}) collective-permute-start(bf16[1,4,4,64,128]{4,3,2,1,0:T(8,128)(2,1)S(1)} %get-tuple-element.58.refs_2_), channel_id=1, source_target_pairs={{0,4},{4,0},{8,12},{12,8},{16,20},{20,16},{24,28},{28,24},{1,5},{5... | collective-permute-start | bytes 786440 | tf_op jit(solution)/shard_map/z1c3/ppermute | solution.py:235
  59.7 1.6 %collective-permute-start.12 = (bf16[2,2,4,64,128]{4,3,2,1,0:T(8,128)(2,1)S(1)}, bf16[2,2,4,64,128]{4,3,2,1,0:T(8,128)(2,1)S(1)}, u32[]{:S(2)}, u32[]{:S(2)}) collective-permute-start(bf16[2,2,4,64,128]{4,3,2,1,0:T(8,128)(2,1)S(1)} %merge.7.refs_3_), channel_id=1, source_target_pairs={{0,8},{4,12},{8,0},{12,4},{16,24},{20,28},{24,16},{28,20},{1,9},{5... | collective-permute-start | bytes 786440 | tf_op jit(solution)/shard_map/z2c1/ppermute | solution.py:235
  61.2 0.5 collective-permute-start.11
  61.8 4.1 %collective-permute-done.16.refs_1_.refs_9_ = bf16[1,4,4,64,128]{4,3,2,1,0:T(8,128)(2,1)S(1)} collective-permute-done((bf16[1,4,4,64,128]{4,3,2,1,0:T(8,128)(2,1)S(1)}, bf16[1,4,4,64,128]{4,3,2,1,0:T(8,128)(2,1)S(1)}, u32[]{:S(2)}, u32[]{:S(2)}) %collective-permute-start.16) | collective-permute-done | bytes 262176 | tf_op jit(solution)/shard_map/z4c2/ppermute | solution.py:235
  65.9 1.4 %collective-permute-done.15.refs_1_.refs_14_ = bf16[1,4,4,64,128]{4,3,2,1,0:T(8,128)(2,1)S(1)} collective-permute-done((bf16[1,4,4,64,128]{4,3,2,1,0:T(8,128)(2,1)S(1)}, bf16[1,4,4,64,128]{4,3,2,1,0:T(8,128)(2,1)S(1)}, u32[]{:S(2)}, u32[]{:S(2)}) %collective-permute-start.15) | collective-permute-done | bytes 262176 | tf_op jit(solution)/shard_map/z1c3/ppermute | solution.py:235
  67.3 2.6 %collective-permute-start.22 = (bf16[2,1,4,64,128]{4,3,2,1,0:T(8,128)(2,1)S(1)}, bf16[2,1,4,64,128]{4,3,2,1,0:T(8,128)(2,1)S(1)}, u32[]{:S(2)}, u32[]{:S(2)}) collective-permute-start(bf16[2,1,4,64,128]{4,3,2,1,0:T(8,128)(2,1)S(1)} %get-tuple-element.67), channel_id=1, source_target_pairs={{0,16},{4,20},{8,24},{12,28},{16,0},{20,4},{24,8},{28,12},{1,17},{... | collective-permute-start | bytes 393224 | tf_op jit(solution)/shard_map/z4c3/ppermute | solution.py:235
  70.0 1.6 %collective-permute-start.23 = (bf16[2,1,4,64,128]{4,3,2,1,0:T(8,128)(2,1)S(1)}, bf16[2,1,4,64,128]{4,3,2,1,0:T(8,128)(2,1)S(1)}, u32[]{:S(2)}, u32[]{:S(2)}) collective-permute-start(bf16[2,1,4,64,128]{4,3,2,1,0:T(8,128)(2,1)S(1)} %get-tuple-element.68), channel_id=1, source_target_pairs={{0,8},{4,12},{8,0},{12,4},{16,24},{20,28},{24,16},{28,20},{1,9},{5... | collective-permute-start | bytes 393224 | tf_op jit(solution)/shard_map/z2c3/ppermute | solution.py:235
  71.6 1.0 %collective-permute-done.12.refs_2_.refs_6_ = bf16[2,2,4,64,128]{4,3,2,1,0:T(8,128)(2,1)S(1)} collective-permute-done((bf16[2,2,4,64,128]{4,3,2,1,0:T(8,128)(2,1)S(1)}, bf16[2,2,4,64,128]{4,3,2,1,0:T(8,128)(2,1)S(1)}, u32[]{:S(2)}, u32[]{:S(2)}) %collective-permute-start.12) | collective-permute-done | bytes 262176 | tf_op jit(solution)/shard_map/z2c1/ppermute | solution.py:235
  72.6 1.6 %collective-permute-start.17 = (bf16[4,1,4,64,128]{4,3,2,1,0:T(8,128)(2,1)S(1)}, bf16[4,1,4,64,128]{4,3,2,1,0:T(8,128)(2,1)S(1)}, u32[]{:S(2)}, u32[]{:S(2)}) collective-permute-start(bf16[4,1,4,64,128]{4,3,2,1,0:T(8,128)(2,1)S(1)} %merge.11.refs_3_), channel_id=1, source_target_pairs={{0,4},{4,0},{8,12},{12,8},{16,20},{20,16},{24,28},{28,24},{1,5},{5... | collective-permute-start | bytes 786440 | tf_op jit(solution)/shard_map/z1c1/ppermute | solution.py:235
  74.2 3.3 %collective-permute-start.21 = (bf16[2,1,4,64,128]{4,3,2,1,0:T(8,128)(2,1)S(1)}, bf16[2,1,4,64,128]{4,3,2,1,0:T(8,128)(2,1)S(1)}, u32[]{:S(2)}, u32[]{:S(2)}) collective-permute-start(bf16[2,1,4,64,128]{4,3,2,1,0:T(8,128)(2,1)S(1)} %get-tuple-element.63.refs_3_), channel_id=1, source_target_pairs={{0,24},{4,28},{8,16},{12,20},{16,8},{20,12},{24,0},{28,4},{1,25},{... | collective-permute-start | bytes 393224 | tf_op jit(solution)/shard_map/z6c3/ppermute | solution.py:235
  77.5 2.0 %collective-permute-start.19 = (bf16[2,1,4,64,128]{4,3,2,1,0:T(8,128)(2,1)S(1)}, bf16[2,1,4,64,128]{4,3,2,1,0:T(8,128)(2,1)S(1)}, u32[]{:S(2)}, u32[]{:S(2)}) collective-permute-start(bf16[2,1,4,64,128]{4,3,2,1,0:T(8,128)(2,1)S(1)} %get-tuple-element.65), channel_id=1, source_target_pairs={{0,8},{4,12},{8,0},{12,4},{16,24},{20,28},{24,16},{28,20},{1,9},{5... | collective-permute-start | bytes 393224 | tf_op jit(solution)/shard_map/z2c2/ppermute | solution.py:235
  79.5 1.5 %collective-permute-start.20 = (bf16[2,1,4,64,128]{4,3,2,1,0:T(8,128)(2,1)S(1)}, bf16[2,1,4,64,128]{4,3,2,1,0:T(8,128)(2,1)S(1)}, u32[]{:S(2)}, u32[]{:S(2)}) collective-permute-start(bf16[2,1,4,64,128]{4,3,2,1,0:T(8,128)(2,1)S(1)} %get-tuple-element.66), channel_id=1, source_target_pairs={{0,4},{4,0},{8,12},{12,8},{16,20},{20,16},{24,28},{28,24},{1,5},{5... | collective-permute-start | bytes 393224 | tf_op jit(solution)/shard_map/z1c2/ppermute | solution.py:235
  81.0 1.4 %collective-permute-done.21.refs_0_.refs_15_ = bf16[2,1,4,64,128]{4,3,2,1,0:T(8,128)(2,1)S(1)} collective-permute-done((bf16[2,1,4,64,128]{4,3,2,1,0:T(8,128)(2,1)S(1)}, bf16[2,1,4,64,128]{4,3,2,1,0:T(8,128)(2,1)S(1)}, u32[]{:S(2)}, u32[]{:S(2)}) %collective-permute-start.21) | collective-permute-done | bytes 131104 | tf_op jit(solution)/shard_map/z6c3/ppermute | solution.py:235
  82.4 2.6 %collective-permute-done.18.refs_10_ = bf16[2,1,4,64,128]{4,3,2,1,0:T(8,128)(2,1)S(1)} collective-permute-done((bf16[2,1,4,64,128]{4,3,2,1,0:T(8,128)(2,1)S(1)}, bf16[2,1,4,64,128]{4,3,2,1,0:T(8,128)(2,1)S(1)}, u32[]{:S(2)}, u32[]{:S(2)}) %collective-permute-start.18) | collective-permute-done | bytes 131104 | tf_op jit(solution)/shard_map/z3c2/ppermute | solution.py:235
  85.0 1.8 %collective-permute-done.19.refs_11_ = bf16[2,1,4,64,128]{4,3,2,1,0:T(8,128)(2,1)S(1)} collective-permute-done((bf16[2,1,4,64,128]{4,3,2,1,0:T(8,128)(2,1)S(1)}, bf16[2,1,4,64,128]{4,3,2,1,0:T(8,128)(2,1)S(1)}, u32[]{:S(2)}, u32[]{:S(2)}) %collective-permute-start.19) | collective-permute-done | bytes 131104 | tf_op jit(solution)/shard_map/z2c2/ppermute | solution.py:235
  86.8 3.3 %combine.1 = f32[128,64,128]{2,1,0:T(8,128)} custom-call(s32[128]{0:T(128)S(1)} %copy-done.1, s32[2]{0:T(128)S(1)} %pad_add_fusion.place_ref, bf16[1,4,4,64,128]{4,3,2,1,0:T(8,128)(2,1)S(1)} %get-tuple-element.45.refs_0_, bf16[1,4,4,64,128]{4,3,2,1,0:T(8,128)(2,1)S(1)} %collective-permute-done.3.refs_1_, ...), custom_call_target="tpu_custom_call" | custom-call | flops 1024 | bytes 1024 | tf_op jit(solution)/shard_map/combine/pallas_call | solution.py:217
  (21 shorter events, 0.2 us)
Async XLA Ops:
  0.1 1.2 %copy-start = (bf16[1000,512]{1,0:T(8,128)(2,1)S(1)}, bf16[1000,512]{1,0:T(8,128)(2,1)}, u32[]{:S(2)}) copy-start(bf16[1000,512]{1,0:T(8,128)(2,1)} %c_ref.5) | copy-start | bytes 3072004
  7.7 15.4 %collective-permute-start = (bf16[8,256,128]{2,1,0:T(8,128)(2,1)S(1)}, bf16[8,256,128]{2,1,0:T(8,128)(2,1)S(1)}, u32[]{:S(2)}, u32[]{:S(2)}) collective-permute-start(bf16[8,256,128]{2,1,0:T(8,128)(2,1)S(1)} %get-tuple-element.38), channel_id=1, source_target_pairs={{0,1},{1,0},{2,3},{3,2},{4,5},{5,4},{6,7},{7,6},{8,9},{9,8},{10,11... | collective-permute-start | bytes 1572872 | tf_op jit(solution)/shard_map/beside0/ppermute | solution.py:235
  8.2 9.8 %collective-permute-start.1 = (bf16[4,256,128]{2,1,0:T(8,128)(2,1)S(1)}, bf16[4,256,128]{2,1,0:T(8,128)(2,1)S(1)}, u32[]{:S(2)}, u32[]{:S(2)}) collective-permute-start(bf16[4,256,128]{2,1,0:T(8,128)(2,1)S(1)} %get-tuple-element.39), channel_id=1, source_target_pairs={{0,2},{1,3},{2,0},{3,1},{4,6},{5,7},{6,4},{7,5},{8,10},{9,11},{10,... | collective-permute-start | bytes 786440 | tf_op jit(solution)/shard_map/y0/ppermute | solution.py:235
  10.8 12.3 %collective-permute-start.2 = (bf16[4,256,128]{2,1,0:T(8,128)(2,1)S(1)}, bf16[4,256,128]{2,1,0:T(8,128)(2,1)S(1)}, u32[]{:S(2)}, u32[]{:S(2)}) collective-permute-start(bf16[4,256,128]{2,1,0:T(8,128)(2,1)S(1)} %get-tuple-element.40), channel_id=1, source_target_pairs={{0,3},{1,2},{2,1},{3,0},{4,7},{5,6},{6,5},{7,4},{8,11},{9,10},{10,... | collective-permute-start | bytes 786440 | tf_op jit(solution)/shard_map/y1/ppermute | solution.py:235
  18.3 10.8 %collective-permute-start.4 = (bf16[4,256,128]{2,1,0:T(8,128)(2,1)S(1)}, bf16[4,256,128]{2,1,0:T(8,128)(2,1)S(1)}, u32[]{:S(2)}, u32[]{:S(2)}) collective-permute-start(bf16[4,256,128]{2,1,0:T(8,128)(2,1)S(1)} %get-tuple-element.47), channel_id=1, source_target_pairs={{0,2},{1,3},{2,0},{3,1},{4,6},{5,7},{6,4},{7,5},{8,10},{9,11},{10,... | collective-permute-start | bytes 786440 | tf_op jit(solution)/shard_map/y2/ppermute | solution.py:235
  20.4 27.4 %collective-permute-start.8 = (bf16[8,256,128]{2,1,0:T(8,128)(2,1)S(1)}, bf16[8,256,128]{2,1,0:T(8,128)(2,1)S(1)}, u32[]{:S(2)}, u32[]{:S(2)}) collective-permute-start(bf16[8,256,128]{2,1,0:T(8,128)(2,1)S(1)} %get-tuple-element.51), channel_id=1, source_target_pairs={{0,1},{1,0},{2,3},{3,2},{4,5},{5,4},{6,7},{7,6},{8,9},{9,8},{10,11... | collective-permute-start | bytes 1572872 | tf_op jit(solution)/shard_map/beside1/ppermute | solution.py:235
  20.4 13.9 %collective-permute-start.5 = (bf16[4,256,128]{2,1,0:T(8,128)(2,1)S(1)}, bf16[4,256,128]{2,1,0:T(8,128)(2,1)S(1)}, u32[]{:S(2)}, u32[]{:S(2)}) collective-permute-start(bf16[4,256,128]{2,1,0:T(8,128)(2,1)S(1)} %get-tuple-element.48), channel_id=1, source_target_pairs={{0,3},{1,2},{2,1},{3,0},{4,7},{5,6},{6,5},{7,4},{8,11},{9,10},{10,... | collective-permute-start | bytes 786440 | tf_op jit(solution)/shard_map/y3/ppermute | solution.py:235
  24.4 62.5 %copy-start.1 = (s32[128]{0:T(128)S(1)}, s32[128]{0:T(128)}, u32[]{:S(2)}) copy-start(s32[128]{0:T(128)} %mirror_ref.1) | copy-start | bytes 1540
  24.4 15.5 %collective-permute-start.3 = (bf16[1,4,4,64,128]{4,3,2,1,0:T(8,128)(2,1)S(1)}, bf16[1,4,4,64,128]{4,3,2,1,0:T(8,128)(2,1)S(1)}, u32[]{:S(2)}, u32[]{:S(2)}) collective-permute-start(bf16[1,4,4,64,128]{4,3,2,1,0:T(8,128)(2,1)S(1)} %get-tuple-element.46.refs_5_), channel_id=1, source_target_pairs={{0,16},{4,20},{8,24},{12,28},{16,0},{20,4},{24,8},{28,12},{1,17},{... | collective-permute-start | bytes 786440 | tf_op jit(solution)/shard_map/z4c0/ppermute | solution.py:235
  27.1 13.3 %collective-permute-start.9 = (bf16[4,256,128]{2,1,0:T(8,128)(2,1)S(1)}, bf16[4,256,128]{2,1,0:T(8,128)(2,1)S(1)}, u32[]{:S(2)}, u32[]{:S(2)}) collective-permute-start(bf16[4,256,128]{2,1,0:T(8,128)(2,1)S(1)} %get-tuple-element.52), channel_id=1, source_target_pairs={{0,2},{1,3},{2,0},{3,1},{4,6},{5,7},{6,4},{7,5},{8,10},{9,11},{10,... | collective-permute-start | bytes 786440 | tf_op jit(solution)/shard_map/y4/ppermute | solution.py:235
  29.2 16.3 %collective-permute-start.10 = (bf16[4,256,128]{2,1,0:T(8,128)(2,1)S(1)}, bf16[4,256,128]{2,1,0:T(8,128)(2,1)S(1)}, u32[]{:S(2)}, u32[]{:S(2)}) collective-permute-start(bf16[4,256,128]{2,1,0:T(8,128)(2,1)S(1)} %get-tuple-element.53), channel_id=1, source_target_pairs={{0,3},{1,2},{2,1},{3,0},{4,7},{5,6},{6,5},{7,4},{8,11},{9,10},{10,... | collective-permute-start | bytes 786440 | tf_op jit(solution)/shard_map/y5/ppermute | solution.py:235
  34.3 21.9 %collective-permute-start.13 = (bf16[4,256,128]{2,1,0:T(8,128)(2,1)S(1)}, bf16[4,256,128]{2,1,0:T(8,128)(2,1)S(1)}, u32[]{:S(2)}, u32[]{:S(2)}) collective-permute-start(bf16[4,256,128]{2,1,0:T(8,128)(2,1)S(1)} %get-tuple-element.55), channel_id=1, source_target_pairs={{0,2},{1,3},{2,0},{3,1},{4,6},{5,7},{6,4},{7,5},{8,10},{9,11},{10,... | collective-permute-start | bytes 786440 | tf_op jit(solution)/shard_map/y6/ppermute | solution.py:235
  39.9 16.3 %collective-permute-start.7 = (bf16[1,4,4,64,128]{4,3,2,1,0:T(8,128)(2,1)S(1)}, bf16[1,4,4,64,128]{4,3,2,1,0:T(8,128)(2,1)S(1)}, u32[]{:S(2)}, u32[]{:S(2)}) collective-permute-start(bf16[1,4,4,64,128]{4,3,2,1,0:T(8,128)(2,1)S(1)} %get-tuple-element.49.refs_2_), channel_id=1, source_target_pairs={{0,16},{4,20},{8,24},{12,28},{16,0},{20,4},{24,8},{28,12},{1,17},{... | collective-permute-start | bytes 786440 | tf_op jit(solution)/shard_map/z4c1/ppermute | solution.py:235
  40.4 15.8 %collective-permute-start.6 = (bf16[2,2,4,64,128]{4,3,2,1,0:T(8,128)(2,1)S(1)}, bf16[2,2,4,64,128]{4,3,2,1,0:T(8,128)(2,1)S(1)}, u32[]{:S(2)}, u32[]{:S(2)}) collective-permute-start(bf16[2,2,4,64,128]{4,3,2,1,0:T(8,128)(2,1)S(1)} %merge.6.refs_5_), channel_id=1, source_target_pairs={{0,8},{4,12},{8,0},{12,4},{16,24},{20,28},{24,16},{28,20},{1,9},{5... | collective-permute-start | bytes 786440 | tf_op jit(solution)/shard_map/z2c0/ppermute | solution.py:235
  45.5 11.2 %collective-permute-start.14 = (bf16[4,256,128]{2,1,0:T(8,128)(2,1)S(1)}, bf16[4,256,128]{2,1,0:T(8,128)(2,1)S(1)}, u32[]{:S(2)}, u32[]{:S(2)}) collective-permute-start(bf16[4,256,128]{2,1,0:T(8,128)(2,1)S(1)} %get-tuple-element.56), channel_id=1, source_target_pairs={{0,3},{1,2},{2,1},{3,0},{4,7},{5,6},{6,5},{7,4},{8,11},{9,10},{10,... | collective-permute-start | bytes 786440 | tf_op jit(solution)/shard_map/y7/ppermute | solution.py:235
  49.0 16.8 %collective-permute-start.16 = (bf16[1,4,4,64,128]{4,3,2,1,0:T(8,128)(2,1)S(1)}, bf16[1,4,4,64,128]{4,3,2,1,0:T(8,128)(2,1)S(1)}, u32[]{:S(2)}, u32[]{:S(2)}) collective-permute-start(bf16[1,4,4,64,128]{4,3,2,1,0:T(8,128)(2,1)S(1)} %get-tuple-element.54.refs_2_), channel_id=1, source_target_pairs={{0,16},{4,20},{8,24},{12,28},{16,0},{20,4},{24,8},{28,12},{1,17},{... | collective-permute-start | bytes 786440 | tf_op jit(solution)/shard_map/z4c2/ppermute | solution.py:235
  58.1 9.2 %collective-permute-start.15 = (bf16[1,4,4,64,128]{4,3,2,1,0:T(8,128)(2,1)S(1)}, bf16[1,4,4,64,128]{4,3,2,1,0:T(8,128)(2,1)S(1)}, u32[]{:S(2)}, u32[]{:S(2)}) collective-permute-start(bf16[1,4,4,64,128]{4,3,2,1,0:T(8,128)(2,1)S(1)} %get-tuple-element.58.refs_2_), channel_id=1, source_target_pairs={{0,4},{4,0},{8,12},{12,8},{16,20},{20,16},{24,28},{28,24},{1,5},{5... | collective-permute-start | bytes 786440 | tf_op jit(solution)/shard_map/z1c3/ppermute | solution.py:235
  59.7 12.9 %collective-permute-start.12 = (bf16[2,2,4,64,128]{4,3,2,1,0:T(8,128)(2,1)S(1)}, bf16[2,2,4,64,128]{4,3,2,1,0:T(8,128)(2,1)S(1)}, u32[]{:S(2)}, u32[]{:S(2)}) collective-permute-start(bf16[2,2,4,64,128]{4,3,2,1,0:T(8,128)(2,1)S(1)} %merge.7.refs_3_), channel_id=1, source_target_pairs={{0,8},{4,12},{8,0},{12,4},{16,24},{20,28},{24,16},{28,20},{1,9},{5... | collective-permute-start | bytes 786440 | tf_op jit(solution)/shard_map/z2c1/ppermute | solution.py:235
  61.2 11.3 %collective-permute-start.11 = (bf16[4,1,4,64,128]{4,3,2,1,0:T(8,128)(2,1)S(1)}, bf16[4,1,4,64,128]{4,3,2,1,0:T(8,128)(2,1)S(1)}, u32[]{:S(2)}, u32[]{:S(2)}) collective-permute-start(bf16[4,1,4,64,128]{4,3,2,1,0:T(8,128)(2,1)S(1)} %merge.8.refs_5_), channel_id=1, source_target_pairs={{0,4},{4,0},{8,12},{12,8},{16,20},{20,16},{24,28},{28,24},{1,5},{5... | collective-permute-start | bytes 786440 | tf_op jit(solution)/shard_map/z1c0/ppermute | solution.py:235
  67.3 10.2 %collective-permute-start.22 = (bf16[2,1,4,64,128]{4,3,2,1,0:T(8,128)(2,1)S(1)}, bf16[2,1,4,64,128]{4,3,2,1,0:T(8,128)(2,1)S(1)}, u32[]{:S(2)}, u32[]{:S(2)}) collective-permute-start(bf16[2,1,4,64,128]{4,3,2,1,0:T(8,128)(2,1)S(1)} %get-tuple-element.67), channel_id=1, source_target_pairs={{0,16},{4,20},{8,24},{12,28},{16,0},{20,4},{24,8},{28,12},{1,17},{... | collective-permute-start | bytes 393224 | tf_op jit(solution)/shard_map/z4c3/ppermute | solution.py:235
  70.0 9.5 %collective-permute-start.23 = (bf16[2,1,4,64,128]{4,3,2,1,0:T(8,128)(2,1)S(1)}, bf16[2,1,4,64,128]{4,3,2,1,0:T(8,128)(2,1)S(1)}, u32[]{:S(2)}, u32[]{:S(2)}) collective-permute-start(bf16[2,1,4,64,128]{4,3,2,1,0:T(8,128)(2,1)S(1)} %get-tuple-element.68), channel_id=1, source_target_pairs={{0,8},{4,12},{8,0},{12,4},{16,24},{20,28},{24,16},{28,20},{1,9},{5... | collective-permute-start | bytes 393224 | tf_op jit(solution)/shard_map/z2c3/ppermute | solution.py:235
  72.6 14.2 %collective-permute-start.17 = (bf16[4,1,4,64,128]{4,3,2,1,0:T(8,128)(2,1)S(1)}, bf16[4,1,4,64,128]{4,3,2,1,0:T(8,128)(2,1)S(1)}, u32[]{:S(2)}, u32[]{:S(2)}) collective-permute-start(bf16[4,1,4,64,128]{4,3,2,1,0:T(8,128)(2,1)S(1)} %merge.11.refs_3_), channel_id=1, source_target_pairs={{0,4},{4,0},{8,12},{12,8},{16,20},{20,16},{24,28},{28,24},{1,5},{5... | collective-permute-start | bytes 786440 | tf_op jit(solution)/shard_map/z1c1/ppermute | solution.py:235
  74.2 8.2 %collective-permute-start.21 = (bf16[2,1,4,64,128]{4,3,2,1,0:T(8,128)(2,1)S(1)}, bf16[2,1,4,64,128]{4,3,2,1,0:T(8,128)(2,1)S(1)}, u32[]{:S(2)}, u32[]{:S(2)}) collective-permute-start(bf16[2,1,4,64,128]{4,3,2,1,0:T(8,128)(2,1)S(1)} %get-tuple-element.63.refs_3_), channel_id=1, source_target_pairs={{0,24},{4,28},{8,16},{12,20},{16,8},{20,12},{24,0},{28,4},{1,25},{... | collective-permute-start | bytes 393224 | tf_op jit(solution)/shard_map/z6c3/ppermute | solution.py:235
  77.5 7.5 %collective-permute-start.18 = (bf16[2,1,4,64,128]{4,3,2,1,0:T(8,128)(2,1)S(1)}, bf16[2,1,4,64,128]{4,3,2,1,0:T(8,128)(2,1)S(1)}, u32[]{:S(2)}, u32[]{:S(2)}) collective-permute-start(bf16[2,1,4,64,128]{4,3,2,1,0:T(8,128)(2,1)S(1)} %get-tuple-element.64), channel_id=1, source_target_pairs={{0,12},{4,8},{8,4},{12,0},{16,28},{20,24},{24,20},{28,16},{1,13},{... | collective-permute-start | bytes 393224 | tf_op jit(solution)/shard_map/z3c2/ppermute | solution.py:235
  77.5 9.4 %collective-permute-start.19 = (bf16[2,1,4,64,128]{4,3,2,1,0:T(8,128)(2,1)S(1)}, bf16[2,1,4,64,128]{4,3,2,1,0:T(8,128)(2,1)S(1)}, u32[]{:S(2)}, u32[]{:S(2)}) collective-permute-start(bf16[2,1,4,64,128]{4,3,2,1,0:T(8,128)(2,1)S(1)} %get-tuple-element.65), channel_id=1, source_target_pairs={{0,8},{4,12},{8,0},{12,4},{16,24},{20,28},{24,16},{28,20},{1,9},{5... | collective-permute-start | bytes 393224 | tf_op jit(solution)/shard_map/z2c2/ppermute | solution.py:235
  79.5 7.3 %collective-permute-start.20 = (bf16[2,1,4,64,128]{4,3,2,1,0:T(8,128)(2,1)S(1)}, bf16[2,1,4,64,128]{4,3,2,1,0:T(8,128)(2,1)S(1)}, u32[]{:S(2)}, u32[]{:S(2)}) collective-permute-start(bf16[2,1,4,64,128]{4,3,2,1,0:T(8,128)(2,1)S(1)} %get-tuple-element.66), channel_id=1, source_target_pairs={{0,4},{4,0},{8,12},{12,8},{16,20},{20,16},{24,28},{28,24},{1,5},{5... | collective-permute-start | bytes 393224 | tf_op jit(solution)/shard_map/z1c2/ppermute | solution.py:235

commit v10 on v9

--- a/solution.py
+++ b/solution.py
@@ -9,7 +9,7 @@
 
 LANES = 128
 STEP = 64
-BATCHES = ((4, 4), (4, 4))
+BATCHES = ((4, 4), (5, 3))
 CHUNKS = sum(BATCHES, ())
 SIZES = ((1,), (1,), (1, 2), (-1, 2))
 PART = 256
@@ -37,18 +37,25 @@
         is_source = source == (to & (many - 1)) * some + (to >> bits)
         turn_ref[...] = jnp.where(is_source, 1.0, 0.0).astype(jnp.bfloat16)
 
-    x = x_ref[...].reshape(step * some, depth)
-    product = jnp.dot(x, c_ref[...], preferred_element_type=jnp.float32)
-    line = lax.broadcasted_iota(jnp.int32, product.shape, 0)
-    product = jnp.where(line < (rows - at * step) * some, product, 0.0).astype(jnp.bfloat16)
-    for part in range(step // many):
-        lines = jnp.dot(
-            turn_ref[...], product[part * PART : (part + 1) * PART], preferred_element_type=jnp.float32
-        ).astype(jnp.bfloat16)
-        here = pl.ds(pl.multiple_of(at * step + part * many, many), many)
-        for k in range(some):
-            for d in range(n_mo):
-                held[d, k, here] = lines[k * many : (k + 1) * many, d * LANES : (d + 1) * LANES]
+    def fill(limit):
+        x = x_ref[...].reshape(step * some, depth)
+        product = jnp.dot(x, c_ref[...], preferred_element_type=jnp.float32)
+        if limit is not None:
+            line = lax.broadcasted_iota(jnp.int32, product.shape, 0)
+            product = jnp.where(line < limit * some, product, 0.0)
+        product = product.astype(jnp.bfloat16)
+        for part in range(step // many):
+            lines = jnp.dot(
+                turn_ref[...], product[part * PART : (part + 1) * PART], preferred_element_type=jnp.float32
+            ).astype(jnp.bfloat16)
+            here = pl.ds(pl.multiple_of(at * step + part * many, many), many)
+            for k in range(some):
+                for d in range(n_mo):
+                    held[d, k, here] = lines[k * many : (k + 1) * many, d * LANES : (d + 1) * LANES]
+
+    steps = padded // step
+    pl.when(at < steps - 1)(lambda: fill(None))
+    pl.when(at == steps - 1)(lambda: fill(rows - (steps - 1) * step))
     here = pl.ds(pl.multiple_of(at * step, step), step)
     for n, (out, (o, first)) in enumerate(zip(outs, blocks)):
         mine = held.at[place_ref[0] ^ o, pl.ds(first, out.shape[0])]
@@ -309,7 +316,8 @@
             waiting = messages
         else:
             send(c, level, messages)
-    token = [wait_for([x for x in parts[last][-3:]] + token)]
+    for x in parts[last][-3:]:
+        token = [wait_for([x, *token])]
     pieces = [x for chunk in parts for x in chunk]
     sources = [(tuple(group), first) for chunk, first in zip(offsets, firsts) for group in chunk]
     return combine(pieces, sources, mirror, place, n_pair, token)

time: 90.4 us -> 91.8 us (1.015)
  waiting for transfers between devices: 30.1 us -> 34.6 us
  starting transfers between devices: 36.8 us -> 33.3 us
    ppermute x24, waiting for transfers between devices: 30.1 us -> 34.6 us  [flipped(): return lax.ppermute(x, axis, [(i, i ^ offset) for i in range(size)])]
    ppermute x24, starting transfers between devices: 36.8 us -> 33.3 us  [flipped(): return lax.ppermute(x, axis, [(i, i ^ offset) for i in range(size)])]
  transfers between devices with their start and end apart: 24 -> 24, of which waited for: 15 -> 10; matrix products, arithmetic and copies ran while one was open for 0% -> 0% of each run, Pallas kernels for 13% -> 14%
where the time goes in v10:
time: 91.8 us; the launch traced here: 91.5 us
  waiting for transfers between devices  34.6 us (38%)
  starting transfers between devices  33.3 us (36%)
  Pallas kernels  22.1 us (24%)
  local copies, waits for them, and re-layouts  1.23 us (1%)
    ppermute x24, waiting for transfers between devices, flipped(): return lax.ppermute(x, axis, [(i, i ^ offset) for i in range(size)])  34.6 us
    ppermute x24, starting transfers between devices, flipped(): return lax.ppermute(x, axis, [(i, i ^ offset) for i in range(size)])  33.3 us
    pallas_call x2, Pallas kernels, quarter_of(): pl.pallas_call(functools.partial(quarter_kernel, rows, n_mo, blocks, len(...  12.8 us
    pallas_call x4, Pallas kernels, half_of(): pl.pallas_call(functools.partial(half_kernel, n_mo, first, owners), in_sp...  5.48 us
    pallas_call x1, Pallas kernels, combine(): pl.pallas_call(functools.partial(combine_kernel, sources, k_all, per_step...  3.29 us
  transfers between devices with their start and end apart: 24, of which 10 were waited for; matrix products, arithmetic and copies ran while one was open for 0% of the time, Pallas kernels for 14%

profile of v10, /device:TPU:0, one launch (start us, length us, event | category | flops | bytes accessed | tf_op | source)
XLA Modules:
  0.0 91.5 jit_solution(6182408723913749898)
XLA Ops:
  0.0 0.1 pad_add_fusion.place_ref
  0.1 1.2 %copy-done = bf16[1000,512]{1,0:T(8,128)(2,1)S(1)} copy-done((bf16[1000,512]{1,0:T(8,128)(2,1)S(1)}, bf16[1000,512]{1,0:T(8,128)(2,1)}, u32[]{:S(2)}) %copy-start) | copy-done | bytes 1024024
  1.3 6.4 %quarter.2 = (bf16[8,256,128]{2,1,0:T(8,128)(2,1)S(1)}, bf16[8,256,128]{2,1,0:T(8,128)(2,1)S(1)}, bf16[4,256,128]{2,1,0:T(8,128)(2,1)S(1)}, bf16[4,256,128]{2,1,...) custom-call(s32[2]{0:T(128)S(1)} %pad_add_fusion.place_ref, ...), custom_call_target="tpu_custom_call" | custom-call | flops 1024 | bytes 1024 | tf_op jit(solution)/shard_map/quarter/pallas_call | solution.py:79
  7.7 0.5 collective-permute-start
  8.2 2.6 %collective-permute-start.1 = (bf16[4,256,128]{2,1,0:T(8,128)(2,1)S(1)}, bf16[4,256,128]{2,1,0:T(8,128)(2,1)S(1)}, u32[]{:S(2)}, u32[]{:S(2)}) collective-permute-start(bf16[4,256,128]{2,1,0:T(8,128)(2,1)S(1)} %get-tuple-element.39), channel_id=1, source_target_pairs={{0,2},{1,3},{2,0},{3,1},{4,6},{5,7},{6,4},{7,5},{8,10},{9,11},{10,... | collective-permute-start | bytes 786440 | tf_op jit(solution)/shard_map/y0/ppermute | solution.py:242
  10.8 0.1 collective-permute-start.2
  10.9 6.4 %quarter.3 = (bf16[8,256,128]{2,1,0:T(8,128)(2,1)S(1)}, bf16[8,256,128]{2,1,0:T(8,128)(2,1)S(1)}, bf16[5,256,128]{2,1,0:T(8,128)(2,1)S(1)}, bf16[5,256,128]{2,1,...) custom-call(s32[2]{0:T(128)S(1)} %pad_add_fusion.place_ref, ...), custom_call_target="tpu_custom_call" | custom-call | flops 1024 | bytes 1024 | tf_op jit(solution)/shard_map/quarter/pallas_call | solution.py:79
  17.3 0.7 collective-permute-done.1.refs_2_
  18.0 0.4 turn.1
  18.4 2.0 %collective-permute-start.4 = (bf16[4,256,128]{2,1,0:T(8,128)(2,1)S(1)}, bf16[4,256,128]{2,1,0:T(8,128)(2,1)S(1)}, u32[]{:S(2)}, u32[]{:S(2)}) collective-permute-start(bf16[4,256,128]{2,1,0:T(8,128)(2,1)S(1)} %get-tuple-element.47), channel_id=1, source_target_pairs={{0,2},{1,3},{2,0},{3,1},{4,6},{5,7},{6,4},{7,5},{8,10},{9,11},{10,... | collective-permute-start | bytes 786440 | tf_op jit(solution)/shard_map/y2/ppermute | solution.py:242
  20.4 0.2 collective-permute-start.5
  20.6 2.5 %collective-permute-done.2.refs_3_ = bf16[4,256,128]{2,1,0:T(8,128)(2,1)S(1)} collective-permute-done((bf16[4,256,128]{2,1,0:T(8,128)(2,1)S(1)}, bf16[4,256,128]{2,1,0:T(8,128)(2,1)S(1)}, u32[]{:S(2)}, u32[]{:S(2)}) %collective-permute-start.2) | collective-permute-done | bytes 262176 | tf_op jit(solution)/shard_map/y1/ppermute | solution.py:242
  23.1 0.0 collective-permute-done.refs_1_
  23.1 1.3 %half.4 = (bf16[1,4,4,64,128]{4,3,2,1,0:T(8,128)(2,1)S(1)}, bf16[1,4,4,64,128]{4,3,2,1,0:T(8,128)(2,1)S(1)}) custom-call(s32[2]{0:T(128)S(1)} %pad_add_fusion.place_ref, bf16[8,256,128]{2,1,0:T(8,128)(2,1)S(1)} %get-tuple-element.37.refs_0_, bf16[8,256,128]{2,1,0:T(8,128)(2,1)S(1)} %collective-permute-done.refs_1_, ...), custom_call_target="tpu_custom_call" | custom-call | flops 1024 | bytes 1024 | tf_op jit(solution)/shard_map/half/pallas_call | solution.py:148
  24.4 0.0 copy-start.1
  24.4 2.7 %collective-permute-start.3 = (bf16[1,4,4,64,128]{4,3,2,1,0:T(8,128)(2,1)S(1)}, bf16[1,4,4,64,128]{4,3,2,1,0:T(8,128)(2,1)S(1)}, u32[]{:S(2)}, u32[]{:S(2)}) collective-permute-start(bf16[1,4,4,64,128]{4,3,2,1,0:T(8,128)(2,1)S(1)} %get-tuple-element.46.refs_5_), channel_id=1, source_target_pairs={{0,16},{4,20},{8,24},{12,28},{16,0},{20,4},{24,8},{28,12},{1,17},{... | collective-permute-start | bytes 786440 | tf_op jit(solution)/shard_map/z4c0/ppermute | solution.py:242
  27.1 1.5 %collective-permute-start.9 = (bf16[5,256,128]{2,1,0:T(8,128)(2,1)S(1)}, bf16[5,256,128]{2,1,0:T(8,128)(2,1)S(1)}, u32[]{:S(2)}, u32[]{:S(2)}) collective-permute-start(bf16[5,256,128]{2,1,0:T(8,128)(2,1)S(1)} %get-tuple-element.52), channel_id=1, source_target_pairs={{0,2},{1,3},{2,0},{3,1},{4,6},{5,7},{6,4},{7,5},{8,10},{9,11},{10,... | collective-permute-start | bytes 983048 | tf_op jit(solution)/shard_map/y4/ppermute | solution.py:242
  28.6 0.6 collective-permute-done.4.refs_2_
  29.2 0.8 collective-permute-start.10
  30.0 4.3 %collective-permute-done.5.refs_3_ = bf16[4,256,128]{2,1,0:T(8,128)(2,1)S(1)} collective-permute-done((bf16[4,256,128]{2,1,0:T(8,128)(2,1)S(1)}, bf16[4,256,128]{2,1,0:T(8,128)(2,1)S(1)}, u32[]{:S(2)}, u32[]{:S(2)}) %collective-permute-start.5) | collective-permute-done | bytes 262176 | tf_op jit(solution)/shard_map/y3/ppermute | solution.py:242
  34.3 1.3 %half.5 = (bf16[1,4,4,64,128]{4,3,2,1,0:T(8,128)(2,1)S(1)}, bf16[1,4,4,64,128]{4,3,2,1,0:T(8,128)(2,1)S(1)}) custom-call(s32[2]{0:T(128)S(1)} %pad_add_fusion.place_ref, bf16[8,256,128]{2,1,0:T(8,128)(2,1)S(1)} %get-tuple-element.37.refs_0_, bf16[8,256,128]{2,1,0:T(8,128)(2,1)S(1)} %collective-permute-done.refs_1_, ...), custom_call_target="tpu_custom_call" | custom-call | flops 1024 | bytes 1024 | tf_op jit(solution)/shard_map/half/pallas_call | solution.py:148
  35.6 2.7 %collective-permute-start.7 = (bf16[1,4,4,64,128]{4,3,2,1,0:T(8,128)(2,1)S(1)}, bf16[1,4,4,64,128]{4,3,2,1,0:T(8,128)(2,1)S(1)}, u32[]{:S(2)}, u32[]{:S(2)}) collective-permute-start(bf16[1,4,4,64,128]{4,3,2,1,0:T(8,128)(2,1)S(1)} %get-tuple-element.49.refs_2_), channel_id=1, source_target_pairs={{0,16},{4,20},{8,24},{12,28},{16,0},{20,4},{24,8},{28,12},{1,17},{... | collective-permute-start | bytes 786440 | tf_op jit(solution)/shard_map/z4c1/ppermute | solution.py:242
  38.3 1.6 %collective-permute-done.3.refs_1_ = bf16[1,4,4,64,128]{4,3,2,1,0:T(8,128)(2,1)S(1)} collective-permute-done((bf16[1,4,4,64,128]{4,3,2,1,0:T(8,128)(2,1)S(1)}, bf16[1,4,4,64,128]{4,3,2,1,0:T(8,128)(2,1)S(1)}, u32[]{:S(2)}, u32[]{:S(2)}) %collective-permute-start.3) | collective-permute-done | bytes 262176 | tf_op jit(solution)/shard_map/z4c0/ppermute | solution.py:242
  39.9 0.8 collective-permute-start.6
  40.7 1.1 %collective-permute-done.9.refs_2_ = bf16[5,256,128]{2,1,0:T(8,128)(2,1)S(1)} collective-permute-done((bf16[5,256,128]{2,1,0:T(8,128)(2,1)S(1)}, bf16[5,256,128]{2,1,0:T(8,128)(2,1)S(1)}, u32[]{:S(2)}, u32[]{:S(2)}) %collective-permute-start.9) | collective-permute-done | bytes 327712 | tf_op jit(solution)/shard_map/y4/ppermute | solution.py:242
  41.8 1.9 %collective-permute-start.13 = (bf16[3,256,128]{2,1,0:T(8,128)(2,1)S(1)}, bf16[3,256,128]{2,1,0:T(8,128)(2,1)S(1)}, u32[]{:S(2)}, u32[]{:S(2)}) collective-permute-start(bf16[3,256,128]{2,1,0:T(8,128)(2,1)S(1)} %get-tuple-element.55), channel_id=1, source_target_pairs={{0,2},{1,3},{2,0},{3,1},{4,6},{5,7},{6,4},{7,5},{8,10},{9,11},{10,... | collective-permute-start | bytes 589832 | tf_op jit(solution)/shard_map/y6/ppermute | solution.py:242
  43.8 4.6 %collective-permute-done.10.refs_3_ = bf16[5,256,128]{2,1,0:T(8,128)(2,1)S(1)} collective-permute-done((bf16[5,256,128]{2,1,0:T(8,128)(2,1)S(1)}, bf16[5,256,128]{2,1,0:T(8,128)(2,1)S(1)}, u32[]{:S(2)}, u32[]{:S(2)}) %collective-permute-start.10) | collective-permute-done | bytes 327712 | tf_op jit(solution)/shard_map/y5/ppermute | solution.py:242
  48.3 2.2 %collective-permute-start.14 = (bf16[3,256,128]{2,1,0:T(8,128)(2,1)S(1)}, bf16[3,256,128]{2,1,0:T(8,128)(2,1)S(1)}, u32[]{:S(2)}, u32[]{:S(2)}) collective-permute-start(bf16[3,256,128]{2,1,0:T(8,128)(2,1)S(1)} %get-tuple-element.56), channel_id=1, source_target_pairs={{0,3},{1,2},{2,1},{3,0},{4,7},{5,6},{6,5},{7,4},{8,11},{9,10},{10,... | collective-permute-start | bytes 589832 | tf_op jit(solution)/shard_map/y7/ppermute | solution.py:242
  50.5 1.6 %half.6 = (bf16[1,4,5,64,128]{4,3,2,1,0:T(8,128)(2,1)S(1)}, bf16[1,4,5,64,128]{4,3,2,1,0:T(8,128)(2,1)S(1)}) custom-call(s32[2]{0:T(128)S(1)} %pad_add_fusion.place_ref, bf16[8,256,128]{2,1,0:T(8,128)(2,1)S(1)} %get-tuple-element.43.refs_3_.refs_0_, bf16[8,256,128]{2,1,0:T(8,128)(2,1)S(1)} %collective-permute-done.8.refs_1_, ...), custom_call_target="tpu_custom_call" | custom-call | flops 1024 | bytes 1024 | tf_op jit(solution)/shard_map/half/pallas_call | solution.py:148
  52.1 2.7 %collective-permute-start.16 = (bf16[1,4,5,64,128]{4,3,2,1,0:T(8,128)(2,1)S(1)}, bf16[1,4,5,64,128]{4,3,2,1,0:T(8,128)(2,1)S(1)}, u32[]{:S(2)}, u32[]{:S(2)}) collective-permute-start(bf16[1,4,5,64,128]{4,3,2,1,0:T(8,128)(2,1)S(1)} %get-tuple-element.54.refs_2_), channel_id=1, source_target_pairs={{0,16},{4,20},{8,24},{12,28},{16,0},{20,4},{24,8},{28,12},{1,17},{... | collective-permute-start | bytes 983048 | tf_op jit(solution)/shard_map/z4c2/ppermute | solution.py:242
  54.8 0.0 collective-permute-done.7.refs_1_.refs_5_
  54.8 1.6 %collective-permute-start.12 = (bf16[2,2,4,64,128]{4,3,2,1,0:T(8,128)(2,1)S(1)}, bf16[2,2,4,64,128]{4,3,2,1,0:T(8,128)(2,1)S(1)}, u32[]{:S(2)}, u32[]{:S(2)}) collective-permute-start(bf16[2,2,4,64,128]{4,3,2,1,0:T(8,128)(2,1)S(1)} %merge.7.refs_3_), channel_id=1, source_target_pairs={{0,8},{4,12},{8,0},{12,4},{16,24},{20,28},{24,16},{28,20},{1,9},{5... | collective-permute-start | bytes 786440 | tf_op jit(solution)/shard_map/z2c1/ppermute | solution.py:242
  56.4 0.0 collective-permute-done.6.refs_2_
  56.5 1.6 %collective-permute-start.11 = (bf16[4,1,4,64,128]{4,3,2,1,0:T(8,128)(2,1)S(1)}, bf16[4,1,4,64,128]{4,3,2,1,0:T(8,128)(2,1)S(1)}, u32[]{:S(2)}, u32[]{:S(2)}) collective-permute-start(bf16[4,1,4,64,128]{4,3,2,1,0:T(8,128)(2,1)S(1)} %merge.8.refs_5_), channel_id=1, source_target_pairs={{0,4},{4,0},{8,12},{12,8},{16,20},{20,16},{24,28},{28,24},{1,5},{5... | collective-permute-start | bytes 786440 | tf_op jit(solution)/shard_map/z1c0/ppermute | solution.py:242
  58.0 1.3 %half.7 = (bf16[1,4,3,64,128]{4,3,2,1,0:T(8,128)(2,1)S(1)}, bf16[1,4,3,64,128]{4,3,2,1,0:T(8,128)(2,1)S(1)}) custom-call(s32[2]{0:T(128)S(1)} %pad_add_fusion.place_ref, bf16[8,256,128]{2,1,0:T(8,128)(2,1)S(1)} %get-tuple-element.43.refs_3_.refs_0_, bf16[8,256,128]{2,1,0:T(8,128)(2,1)S(1)} %collective-permute-done.8.refs_1_, ...), custom_call_target="tpu_custom_call" | custom-call | flops 1024 | bytes 1024 | tf_op jit(solution)/shard_map/half/pallas_call | solution.py:148
  59.3 0.6 collective-permute-start.15
  59.9 9.3 %collective-permute-done.16.refs_1_.refs_9_ = bf16[1,4,5,64,128]{4,3,2,1,0:T(8,128)(2,1)S(1)} collective-permute-done((bf16[1,4,5,64,128]{4,3,2,1,0:T(8,128)(2,1)S(1)}, bf16[1,4,5,64,128]{4,3,2,1,0:T(8,128)(2,1)S(1)}, u32[]{:S(2)}, u32[]{:S(2)}) %collective-permute-start.16) | collective-permute-done | bytes 327712 | tf_op jit(solution)/shard_map/z4c2/ppermute | solution.py:242
  69.3 0.1 collective-permute-start.22
  69.4 0.0 collective-permute-done.12.refs_2_.refs_6_
  69.4 1.6 %collective-permute-start.17 = (bf16[4,1,4,64,128]{4,3,2,1,0:T(8,128)(2,1)S(1)}, bf16[4,1,4,64,128]{4,3,2,1,0:T(8,128)(2,1)S(1)}, u32[]{:S(2)}, u32[]{:S(2)}) collective-permute-start(bf16[4,1,4,64,128]{4,3,2,1,0:T(8,128)(2,1)S(1)} %merge.11.refs_1_), channel_id=1, source_target_pairs={{0,4},{4,0},{8,12},{12,8},{16,20},{20,16},{24,28},{28,24},{1,5},{5... | collective-permute-start | bytes 786440 | tf_op jit(solution)/shard_map/z1c1/ppermute | solution.py:242
  71.0 3.5 %collective-permute-start.21 = (bf16[2,1,3,64,128]{4,3,2,1,0:T(8,128)(2,1)S(1)}, bf16[2,1,3,64,128]{4,3,2,1,0:T(8,128)(2,1)S(1)}, u32[]{:S(2)}, u32[]{:S(2)}) collective-permute-start(bf16[2,1,3,64,128]{4,3,2,1,0:T(8,128)(2,1)S(1)} %get-tuple-element.63.refs_3_), channel_id=1, source_target_pairs={{0,24},{4,28},{8,16},{12,20},{16,8},{20,12},{24,0},{28,4},{1,25},{... | collective-permute-start | bytes 294920 | tf_op jit(solution)/shard_map/z6c3/ppermute | solution.py:242
  74.5 0.5 collective-permute-start.18
  75.0 1.5 %collective-permute-start.19 = (bf16[2,1,5,64,128]{4,3,2,1,0:T(8,128)(2,1)S(1)}, bf16[2,1,5,64,128]{4,3,2,1,0:T(8,128)(2,1)S(1)}, u32[]{:S(2)}, u32[]{:S(2)}) collective-permute-start(bf16[2,1,5,64,128]{4,3,2,1,0:T(8,128)(2,1)S(1)} %get-tuple-element.65), channel_id=1, source_target_pairs={{0,8},{4,12},{8,0},{12,4},{16,24},{20,28},{24,16},{28,20},{1,9},{5... | collective-permute-start | bytes 491528 | tf_op jit(solution)/shard_map/z2c2/ppermute | solution.py:242
  76.5 3.5 %collective-permute-done.22.refs_0_.refs_16_ = bf16[2,1,3,64,128]{4,3,2,1,0:T(8,128)(2,1)S(1)} collective-permute-done((bf16[2,1,3,64,128]{4,3,2,1,0:T(8,128)(2,1)S(1)}, bf16[2,1,3,64,128]{4,3,2,1,0:T(8,128)(2,1)S(1)}, u32[]{:S(2)}, u32[]{:S(2)}) %collective-permute-start.22) | collective-permute-done | bytes 98336 | tf_op jit(solution)/shard_map/z4c3/ppermute | solution.py:242
  80.0 1.5 %collective-permute-start.20 = (bf16[2,1,5,64,128]{4,3,2,1,0:T(8,128)(2,1)S(1)}, bf16[2,1,5,64,128]{4,3,2,1,0:T(8,128)(2,1)S(1)}, u32[]{:S(2)}, u32[]{:S(2)}) collective-permute-start(bf16[2,1,5,64,128]{4,3,2,1,0:T(8,128)(2,1)S(1)} %get-tuple-element.66), channel_id=1, source_target_pairs={{0,4},{4,0},{8,12},{12,8},{16,20},{20,16},{24,28},{28,24},{1,5},{5... | collective-permute-start | bytes 491528 | tf_op jit(solution)/shard_map/z1c2/ppermute | solution.py:242
  81.5 0.2 collective-permute-start.23
  81.7 6.4 %collective-permute-done.23.refs_0_.refs_17_ = bf16[2,1,3,64,128]{4,3,2,1,0:T(8,128)(2,1)S(1)} collective-permute-done((bf16[2,1,3,64,128]{4,3,2,1,0:T(8,128)(2,1)S(1)}, bf16[2,1,3,64,128]{4,3,2,1,0:T(8,128)(2,1)S(1)}, u32[]{:S(2)}, u32[]{:S(2)}) %collective-permute-start.23) | collective-permute-done | bytes 98336 | tf_op jit(solution)/shard_map/z2c3/ppermute | solution.py:242
  88.2 3.3 %combine.1 = f32[128,64,128]{2,1,0:T(8,128)} custom-call(s32[128]{0:T(128)S(1)} %copy-done.1, s32[2]{0:T(128)S(1)} %pad_add_fusion.place_ref, bf16[1,4,4,64,128]{4,3,2,1,0:T(8,128)(2,1)S(1)} %get-tuple-element.45.refs_0_, bf16[1,4,4,64,128]{4,3,2,1,0:T(8,128)(2,1)S(1)} %collective-permute-done.3.refs_1_, ...), custom_call_target="tpu_custom_call" | custom-call | flops 1024 | bytes 1024 | tf_op jit(solution)/shard_map/combine/pallas_call | solution.py:224
  (23 shorter events, 0.2 us)
Async XLA Ops:
  0.1 1.2 %copy-start = (bf16[1000,512]{1,0:T(8,128)(2,1)S(1)}, bf16[1000,512]{1,0:T(8,128)(2,1)}, u32[]{:S(2)}) copy-start(bf16[1000,512]{1,0:T(8,128)(2,1)} %c_ref.5) | copy-start | bytes 3072004
  7.7 15.4 %collective-permute-start = (bf16[8,256,128]{2,1,0:T(8,128)(2,1)S(1)}, bf16[8,256,128]{2,1,0:T(8,128)(2,1)S(1)}, u32[]{:S(2)}, u32[]{:S(2)}) collective-permute-start(bf16[8,256,128]{2,1,0:T(8,128)(2,1)S(1)} %get-tuple-element.38), channel_id=1, source_target_pairs={{0,1},{1,0},{2,3},{3,2},{4,5},{5,4},{6,7},{7,6},{8,9},{9,8},{10,11... | collective-permute-start | bytes 1572872 | tf_op jit(solution)/shard_map/beside0/ppermute | solution.py:242
  8.2 9.7 %collective-permute-start.1 = (bf16[4,256,128]{2,1,0:T(8,128)(2,1)S(1)}, bf16[4,256,128]{2,1,0:T(8,128)(2,1)S(1)}, u32[]{:S(2)}, u32[]{:S(2)}) collective-permute-start(bf16[4,256,128]{2,1,0:T(8,128)(2,1)S(1)} %get-tuple-element.39), channel_id=1, source_target_pairs={{0,2},{1,3},{2,0},{3,1},{4,6},{5,7},{6,4},{7,5},{8,10},{9,11},{10,... | collective-permute-start | bytes 786440 | tf_op jit(solution)/shard_map/y0/ppermute | solution.py:242
  10.8 12.3 %collective-permute-start.2 = (bf16[4,256,128]{2,1,0:T(8,128)(2,1)S(1)}, bf16[4,256,128]{2,1,0:T(8,128)(2,1)S(1)}, u32[]{:S(2)}, u32[]{:S(2)}) collective-permute-start(bf16[4,256,128]{2,1,0:T(8,128)(2,1)S(1)} %get-tuple-element.40), channel_id=1, source_target_pairs={{0,3},{1,2},{2,1},{3,0},{4,7},{5,6},{6,5},{7,4},{8,11},{9,10},{10,... | collective-permute-start | bytes 786440 | tf_op jit(solution)/shard_map/y1/ppermute | solution.py:242
  18.4 10.8 %collective-permute-start.4 = (bf16[4,256,128]{2,1,0:T(8,128)(2,1)S(1)}, bf16[4,256,128]{2,1,0:T(8,128)(2,1)S(1)}, u32[]{:S(2)}, u32[]{:S(2)}) collective-permute-start(bf16[4,256,128]{2,1,0:T(8,128)(2,1)S(1)} %get-tuple-element.47), channel_id=1, source_target_pairs={{0,2},{1,3},{2,0},{3,1},{4,6},{5,7},{6,4},{7,5},{8,10},{9,11},{10,... | collective-permute-start | bytes 786440 | tf_op jit(solution)/shard_map/y2/ppermute | solution.py:242
  20.4 30.2 %collective-permute-start.8 = (bf16[8,256,128]{2,1,0:T(8,128)(2,1)S(1)}, bf16[8,256,128]{2,1,0:T(8,128)(2,1)S(1)}, u32[]{:S(2)}, u32[]{:S(2)}) collective-permute-start(bf16[8,256,128]{2,1,0:T(8,128)(2,1)S(1)} %get-tuple-element.51), channel_id=1, source_target_pairs={{0,1},{1,0},{2,3},{3,2},{4,5},{5,4},{6,7},{7,6},{8,9},{9,8},{10,11... | collective-permute-start | bytes 1572872 | tf_op jit(solution)/shard_map/beside1/ppermute | solution.py:242
  20.4 13.9 %collective-permute-start.5 = (bf16[4,256,128]{2,1,0:T(8,128)(2,1)S(1)}, bf16[4,256,128]{2,1,0:T(8,128)(2,1)S(1)}, u32[]{:S(2)}, u32[]{:S(2)}) collective-permute-start(bf16[4,256,128]{2,1,0:T(8,128)(2,1)S(1)} %get-tuple-element.48), channel_id=1, source_target_pairs={{0,3},{1,2},{2,1},{3,0},{4,7},{5,6},{6,5},{7,4},{8,11},{9,10},{10,... | collective-permute-start | bytes 786440 | tf_op jit(solution)/shard_map/y3/ppermute | solution.py:242
  24.4 63.8 %copy-start.1 = (s32[128]{0:T(128)S(1)}, s32[128]{0:T(128)}, u32[]{:S(2)}) copy-start(s32[128]{0:T(128)} %mirror_ref.1) | copy-start | bytes 1540
  24.4 15.5 %collective-permute-start.3 = (bf16[1,4,4,64,128]{4,3,2,1,0:T(8,128)(2,1)S(1)}, bf16[1,4,4,64,128]{4,3,2,1,0:T(8,128)(2,1)S(1)}, u32[]{:S(2)}, u32[]{:S(2)}) collective-permute-start(bf16[1,4,4,64,128]{4,3,2,1,0:T(8,128)(2,1)S(1)} %get-tuple-element.46.refs_5_), channel_id=1, source_target_pairs={{0,16},{4,20},{8,24},{12,28},{16,0},{20,4},{24,8},{28,12},{1,17},{... | collective-permute-start | bytes 786440 | tf_op jit(solution)/shard_map/z4c0/ppermute | solution.py:242
  27.1 14.7 %collective-permute-start.9 = (bf16[5,256,128]{2,1,0:T(8,128)(2,1)S(1)}, bf16[5,256,128]{2,1,0:T(8,128)(2,1)S(1)}, u32[]{:S(2)}, u32[]{:S(2)}) collective-permute-start(bf16[5,256,128]{2,1,0:T(8,128)(2,1)S(1)} %get-tuple-element.52), channel_id=1, source_target_pairs={{0,2},{1,3},{2,0},{3,1},{4,6},{5,7},{6,4},{7,5},{8,10},{9,11},{10,... | collective-permute-start | bytes 983048 | tf_op jit(solution)/shard_map/y4/ppermute | solution.py:242
  29.2 19.1 %collective-permute-start.10 = (bf16[5,256,128]{2,1,0:T(8,128)(2,1)S(1)}, bf16[5,256,128]{2,1,0:T(8,128)(2,1)S(1)}, u32[]{:S(2)}, u32[]{:S(2)}) collective-permute-start(bf16[5,256,128]{2,1,0:T(8,128)(2,1)S(1)} %get-tuple-element.53), channel_id=1, source_target_pairs={{0,3},{1,2},{2,1},{3,0},{4,7},{5,6},{6,5},{7,4},{8,11},{9,10},{10,... | collective-permute-start | bytes 983048 | tf_op jit(solution)/shard_map/y5/ppermute | solution.py:242
  35.6 19.2 %collective-permute-start.7 = (bf16[1,4,4,64,128]{4,3,2,1,0:T(8,128)(2,1)S(1)}, bf16[1,4,4,64,128]{4,3,2,1,0:T(8,128)(2,1)S(1)}, u32[]{:S(2)}, u32[]{:S(2)}) collective-permute-start(bf16[1,4,4,64,128]{4,3,2,1,0:T(8,128)(2,1)S(1)} %get-tuple-element.49.refs_2_), channel_id=1, source_target_pairs={{0,16},{4,20},{8,24},{12,28},{16,0},{20,4},{24,8},{28,12},{1,17},{... | collective-permute-start | bytes 786440 | tf_op jit(solution)/shard_map/z4c1/ppermute | solution.py:242
  39.9 16.5 %collective-permute-start.6 = (bf16[2,2,4,64,128]{4,3,2,1,0:T(8,128)(2,1)S(1)}, bf16[2,2,4,64,128]{4,3,2,1,0:T(8,128)(2,1)S(1)}, u32[]{:S(2)}, u32[]{:S(2)}) collective-permute-start(bf16[2,2,4,64,128]{4,3,2,1,0:T(8,128)(2,1)S(1)} %merge.6.refs_5_), channel_id=1, source_target_pairs={{0,8},{4,12},{8,0},{12,4},{16,24},{20,28},{24,16},{28,20},{1,9},{5... | collective-permute-start | bytes 786440 | tf_op jit(solution)/shard_map/z2c0/ppermute | solution.py:242
  41.8 16.2 %collective-permute-start.13 = (bf16[3,256,128]{2,1,0:T(8,128)(2,1)S(1)}, bf16[3,256,128]{2,1,0:T(8,128)(2,1)S(1)}, u32[]{:S(2)}, u32[]{:S(2)}) collective-permute-start(bf16[3,256,128]{2,1,0:T(8,128)(2,1)S(1)} %get-tuple-element.55), channel_id=1, source_target_pairs={{0,2},{1,3},{2,0},{3,1},{4,6},{5,7},{6,4},{7,5},{8,10},{9,11},{10,... | collective-permute-start | bytes 589832 | tf_op jit(solution)/shard_map/y6/ppermute | solution.py:242
  48.3 9.7 %collective-permute-start.14 = (bf16[3,256,128]{2,1,0:T(8,128)(2,1)S(1)}, bf16[3,256,128]{2,1,0:T(8,128)(2,1)S(1)}, u32[]{:S(2)}, u32[]{:S(2)}) collective-permute-start(bf16[3,256,128]{2,1,0:T(8,128)(2,1)S(1)} %get-tuple-element.56), channel_id=1, source_target_pairs={{0,3},{1,2},{2,1},{3,0},{4,7},{5,6},{6,5},{7,4},{8,11},{9,10},{10,... | collective-permute-start | bytes 589832 | tf_op jit(solution)/shard_map/y7/ppermute | solution.py:242
  52.1 17.1 %collective-permute-start.16 = (bf16[1,4,5,64,128]{4,3,2,1,0:T(8,128)(2,1)S(1)}, bf16[1,4,5,64,128]{4,3,2,1,0:T(8,128)(2,1)S(1)}, u32[]{:S(2)}, u32[]{:S(2)}) collective-permute-start(bf16[1,4,5,64,128]{4,3,2,1,0:T(8,128)(2,1)S(1)} %get-tuple-element.54.refs_2_), channel_id=1, source_target_pairs={{0,16},{4,20},{8,24},{12,28},{16,0},{20,4},{24,8},{28,12},{1,17},{... | collective-permute-start | bytes 983048 | tf_op jit(solution)/shard_map/z4c2/ppermute | solution.py:242
  54.8 14.6 %collective-permute-start.12 = (bf16[2,2,4,64,128]{4,3,2,1,0:T(8,128)(2,1)S(1)}, bf16[2,2,4,64,128]{4,3,2,1,0:T(8,128)(2,1)S(1)}, u32[]{:S(2)}, u32[]{:S(2)}) collective-permute-start(bf16[2,2,4,64,128]{4,3,2,1,0:T(8,128)(2,1)S(1)} %merge.7.refs_3_), channel_id=1, source_target_pairs={{0,8},{4,12},{8,0},{12,4},{16,24},{20,28},{24,16},{28,20},{1,9},{5... | collective-permute-start | bytes 786440 | tf_op jit(solution)/shard_map/z2c1/ppermute | solution.py:242
  56.5 12.9 %collective-permute-start.11 = (bf16[4,1,4,64,128]{4,3,2,1,0:T(8,128)(2,1)S(1)}, bf16[4,1,4,64,128]{4,3,2,1,0:T(8,128)(2,1)S(1)}, u32[]{:S(2)}, u32[]{:S(2)}) collective-permute-start(bf16[4,1,4,64,128]{4,3,2,1,0:T(8,128)(2,1)S(1)} %merge.8.refs_5_), channel_id=1, source_target_pairs={{0,4},{4,0},{8,12},{12,8},{16,20},{20,16},{24,28},{28,24},{1,5},{5... | collective-permute-start | bytes 786440 | tf_op jit(solution)/shard_map/z1c0/ppermute | solution.py:242
  59.3 9.9 %collective-permute-start.15 = (bf16[1,4,3,64,128]{4,3,2,1,0:T(8,128)(2,1)S(1)}, bf16[1,4,3,64,128]{4,3,2,1,0:T(8,128)(2,1)S(1)}, u32[]{:S(2)}, u32[]{:S(2)}) collective-permute-start(bf16[1,4,3,64,128]{4,3,2,1,0:T(8,128)(2,1)S(1)} %get-tuple-element.58.refs_2_), channel_id=1, source_target_pairs={{0,4},{4,0},{8,12},{12,8},{16,20},{20,16},{24,28},{28,24},{1,5},{5... | collective-permute-start | bytes 589832 | tf_op jit(solution)/shard_map/z1c3/ppermute | solution.py:242
  69.3 10.7 %collective-permute-start.22 = (bf16[2,1,3,64,128]{4,3,2,1,0:T(8,128)(2,1)S(1)}, bf16[2,1,3,64,128]{4,3,2,1,0:T(8,128)(2,1)S(1)}, u32[]{:S(2)}, u32[]{:S(2)}) collective-permute-start(bf16[2,1,3,64,128]{4,3,2,1,0:T(8,128)(2,1)S(1)} %get-tuple-element.67), channel_id=1, source_target_pairs={{0,16},{4,20},{8,24},{12,28},{16,0},{20,4},{24,8},{28,12},{1,17},{... | collective-permute-start | bytes 294920 | tf_op jit(solution)/shard_map/z4c3/ppermute | solution.py:242
  69.4 18.7 %collective-permute-start.17 = (bf16[4,1,4,64,128]{4,3,2,1,0:T(8,128)(2,1)S(1)}, bf16[4,1,4,64,128]{4,3,2,1,0:T(8,128)(2,1)S(1)}, u32[]{:S(2)}, u32[]{:S(2)}) collective-permute-start(bf16[4,1,4,64,128]{4,3,2,1,0:T(8,128)(2,1)S(1)} %merge.11.refs_1_), channel_id=1, source_target_pairs={{0,4},{4,0},{8,12},{12,8},{16,20},{20,16},{24,28},{28,24},{1,5},{5... | collective-permute-start | bytes 786440 | tf_op jit(solution)/shard_map/z1c1/ppermute | solution.py:242
  71.0 10.5 %collective-permute-start.21 = (bf16[2,1,3,64,128]{4,3,2,1,0:T(8,128)(2,1)S(1)}, bf16[2,1,3,64,128]{4,3,2,1,0:T(8,128)(2,1)S(1)}, u32[]{:S(2)}, u32[]{:S(2)}) collective-permute-start(bf16[2,1,3,64,128]{4,3,2,1,0:T(8,128)(2,1)S(1)} %get-tuple-element.63.refs_3_), channel_id=1, source_target_pairs={{0,24},{4,28},{8,16},{12,20},{16,8},{20,12},{24,0},{28,4},{1,25},{... | collective-permute-start | bytes 294920 | tf_op jit(solution)/shard_map/z6c3/ppermute | solution.py:242
  74.5 13.7 %collective-permute-start.18 = (bf16[2,1,5,64,128]{4,3,2,1,0:T(8,128)(2,1)S(1)}, bf16[2,1,5,64,128]{4,3,2,1,0:T(8,128)(2,1)S(1)}, u32[]{:S(2)}, u32[]{:S(2)}) collective-permute-start(bf16[2,1,5,64,128]{4,3,2,1,0:T(8,128)(2,1)S(1)} %get-tuple-element.64), channel_id=1, source_target_pairs={{0,12},{4,8},{8,4},{12,0},{16,28},{20,24},{24,20},{28,16},{1,13},{... | collective-permute-start | bytes 491528 | tf_op jit(solution)/shard_map/z3c2/ppermute | solution.py:242
  75.0 13.2 %collective-permute-start.19 = (bf16[2,1,5,64,128]{4,3,2,1,0:T(8,128)(2,1)S(1)}, bf16[2,1,5,64,128]{4,3,2,1,0:T(8,128)(2,1)S(1)}, u32[]{:S(2)}, u32[]{:S(2)}) collective-permute-start(bf16[2,1,5,64,128]{4,3,2,1,0:T(8,128)(2,1)S(1)} %get-tuple-element.65), channel_id=1, source_target_pairs={{0,8},{4,12},{8,0},{12,4},{16,24},{20,28},{24,16},{28,20},{1,9},{5... | collective-permute-start | bytes 491528 | tf_op jit(solution)/shard_map/z2c2/ppermute | solution.py:242
  80.0 8.2 %collective-permute-start.20 = (bf16[2,1,5,64,128]{4,3,2,1,0:T(8,128)(2,1)S(1)}, bf16[2,1,5,64,128]{4,3,2,1,0:T(8,128)(2,1)S(1)}, u32[]{:S(2)}, u32[]{:S(2)}) collective-permute-start(bf16[2,1,5,64,128]{4,3,2,1,0:T(8,128)(2,1)S(1)} %get-tuple-element.66), channel_id=1, source_target_pairs={{0,4},{4,0},{8,12},{12,8},{16,20},{20,16},{24,28},{28,24},{1,5},{5... | collective-permute-start | bytes 491528 | tf_op jit(solution)/shard_map/z1c2/ppermute | solution.py:242
  81.5 6.7 %collective-permute-start.23 = (bf16[2,1,3,64,128]{4,3,2,1,0:T(8,128)(2,1)S(1)}, bf16[2,1,3,64,128]{4,3,2,1,0:T(8,128)(2,1)S(1)}, u32[]{:S(2)}, u32[]{:S(2)}) collective-permute-start(bf16[2,1,3,64,128]{4,3,2,1,0:T(8,128)(2,1)S(1)} %get-tuple-element.68), channel_id=1, source_target_pairs={{0,8},{4,12},{8,0},{12,4},{16,24},{20,28},{24,16},{28,20},{1,9},{5... | collective-permute-start | bytes 294920 | tf_op jit(solution)/shard_map/z2c3/ppermute | solution.py:242

commit v11 on v10

--- a/solution.py
+++ b/solution.py
@@ -9,7 +9,7 @@
 
 LANES = 128
 STEP = 64
-BATCHES = ((4, 4), (5, 3))
+BATCHES = ((4, 4), (4, 4))
 CHUNKS = sum(BATCHES, ())
 SIZES = ((1,), (1,), (1, 2), (-1, 2))
 PART = 256
@@ -21,12 +21,11 @@
 IN_HBM = pl.BlockSpec(memory_space=pltpu.MemorySpace.HBM)
 
 
-def quarter_kernel(rows, n_mo, blocks, n_after, place_ref, x_ref, c_ref, *refs):
-    refs = refs[n_after:]
-    outs, (turn_ref, held, sems) = refs[:-3], refs[-3:]
+def quarter_kernel(rows, far, n_after, place_ref, x_ref, c_ref, *refs):
+    outs, turn_ref = refs[n_after:-1], refs[-1]
     at = pl.program_id(0)
     step, some, depth = x_ref.shape
-    padded = held.shape[2]
+    padded = outs[0].shape[1]
     many = PART // some
 
     @pl.when(at == 0)
@@ -39,64 +38,58 @@
 
     def fill(limit):
         x = x_ref[...].reshape(step * some, depth)
-        product = jnp.dot(x, c_ref[...], preferred_element_type=jnp.float32)
-        if limit is not None:
-            line = lax.broadcasted_iota(jnp.int32, product.shape, 0)
-            product = jnp.where(line < limit * some, product, 0.0)
-        product = product.astype(jnp.bfloat16)
-        for part in range(step // many):
-            lines = jnp.dot(
-                turn_ref[...], product[part * PART : (part + 1) * PART], preferred_element_type=jnp.float32
-            ).astype(jnp.bfloat16)
-            here = pl.ds(pl.multiple_of(at * step + part * many, many), many)
-            for k in range(some):
-                for d in range(n_mo):
-                    held[d, k, here] = lines[k * many : (k + 1) * many, d * LANES : (d + 1) * LANES]
+        odd = (place_ref[0] & 1) == 1
+        for n, which in enumerate(far):
+            columns = pl.ds(pl.multiple_of(((place_ref[0] >> 1) ^ which) * 2 * LANES, 2 * LANES), 2 * LANES)
+            product = jnp.dot(x, c_ref[:, columns], preferred_element_type=jnp.float32)
+            if limit is not None:
+                line = lax.broadcasted_iota(jnp.int32, product.shape, 0)
+                product = jnp.where(line < limit * some, product, 0.0)
+            low, high = product[:, :LANES], product[:, LANES:]
+            product = [jnp.where(odd, high, low).astype(jnp.bfloat16), jnp.where(odd, low, high).astype(jnp.bfloat16)]
+            product = jnp.concatenate(product, axis=1)
+            for part in range(step // many):
+                lines = jnp.dot(
+                    turn_ref[...], product[part * PART : (part + 1) * PART], preferred_element_type=jnp.float32
+                ).astype(jnp.bfloat16)
+                here = pl.ds(pl.multiple_of(at * step + part * many, many), many)
+                mine = outs[n * len(outs) // len(far) : (n + 1) * len(outs) // len(far)]
+                for o in range(2):
+                    k = 0
+                    for out in mine[o::2]:
+                        for row in range(out.shape[0]):
+                            out[row, here] = lines[k * many : (k + 1) * many, o * LANES : (o + 1) * LANES]
+                            k += 1
 
     steps = padded // step
     pl.when(at < steps - 1)(lambda: fill(None))
     pl.when(at == steps - 1)(lambda: fill(rows - (steps - 1) * step))
-    here = pl.ds(pl.multiple_of(at * step, step), step)
-    for n, (out, (o, first)) in enumerate(zip(outs, blocks)):
-        mine = held.at[place_ref[0] ^ o, pl.ds(first, out.shape[0])]
-        pltpu.make_async_copy(mine.at[:, here], out.at[:, here], sems.at[n]).start()
-
-    @pl.when(at == padded // step - 1)
-    def _():
-        for n, (out, (o, first)) in enumerate(zip(outs, blocks)):
-            mine = held.at[place_ref[0] ^ o, pl.ds(first, out.shape[0])]
-            pltpu.make_async_copy(mine, out, sems.at[n]).wait()
-
-
-def quarter_of(place, by_r, coeffs, n_mo, padded, batch, after):
+
+
+def quarter_of(place, by_r, coeffs, padded, batch, far, after):
     rows, _, depth = by_r.shape
-    orbitals = coeffs.shape[1]
     chunks = BATCHES[batch]
     some = sum(chunks)
-    blocks = [(0, 0), (1, 0)] + [(o, sum(chunks[:c])) for c in range(len(chunks)) for o in range(2, n_mo)]
-    sizes = [some] * 2 + [kc for kc in chunks for _ in range(2, n_mo)]
-    outs = [jax.ShapeDtypeStruct((kc, padded, LANES), jnp.bfloat16) for kc in sizes]
+    outs = [
+        jax.ShapeDtypeStruct((kc, padded, LANES), jnp.bfloat16) for _ in far for kc in chunks for _ in range(2)
+    ]
     out = pl.pallas_call(
-        functools.partial(quarter_kernel, rows, n_mo, blocks, len(after)),
+        functools.partial(quarter_kernel, rows, far, len(after)),
         grid_spec=pltpu.PrefetchScalarGridSpec(
             num_scalar_prefetch=1,
             grid=(padded // STEP,),
             in_specs=[pl.BlockSpec((STEP, some, depth), lambda r, place: (r, batch, 0)), IN_VMEM]
             + [ANYWHERE] * len(after),
-            out_specs=[IN_HBM] * len(outs),
-            scratch_shapes=[
-                pltpu.VMEM((PART, PART), jnp.bfloat16),
-                pltpu.VMEM((n_mo, some, padded, LANES), jnp.bfloat16),
-                pltpu.SemaphoreType.DMA((len(outs),)),
-            ],
+            out_specs=[IN_VMEM] * len(outs),
+            scratch_shapes=[pltpu.VMEM((PART, PART), jnp.bfloat16)],
         ),
         out_shape=outs,
-        compiler_params=pltpu.CompilerParams(vmem_limit_bytes=50 * MIB),
+        compiler_params=pltpu.CompilerParams(vmem_limit_bytes=52 * MIB),
         cost_estimate=COST,
         name="quarter",
     )(place, by_r, coeffs, *after)
-    far = n_mo - 2
-    return out[:2], [out[2 + far * c : 2 + far * (c + 1)] for c in range(len(chunks))]
+    pairs = [list(out[n : n + 2]) for n in range(0, len(out), 2)]
+    return [pairs[n * len(chunks) : (n + 1) * len(chunks)] for n in range(len(far))]
 
 
 def turn_kernel(rows, c_ref, *refs):
@@ -124,12 +117,11 @@
     return out[-1], list(out[:-1])
 
 
-def half_kernel(n_mo, first, owners, place_ref, *refs):
+def half_kernel(n_mo, owners, place_ref, *refs):
     blocks, t_ref, held = refs[:n_mo], refs[n_mo], refs[-1]
     outs = refs[-1 - len(owners) : -1]
     kc, block, lanes = outs[0].shape[2:]
-    firsts = [first if x.shape[0] > kc else 0 for x in blocks]
-    columns = [jnp.concatenate([x[at + k] for k in range(kc)], axis=1) for x, at in zip(blocks, firsts)]
+    columns = [jnp.concatenate([x[k] for k in range(kc)], axis=1) for x in blocks]
     turned = [t_ref[place_ref[0] ^ o] for o in range(n_mo)]
     held[...] = jnp.dot(
         jnp.concatenate(turned, axis=1), jnp.concatenate(columns, axis=0), preferred_element_type=jnp.float32
@@ -141,12 +133,12 @@
                 out[0, at, k] = held[pl.ds(start, block), k * lanes : (k + 1) * lanes].astype(jnp.bfloat16)
 
 
-def half_of(place, blocks, turned, first, owners, after):
+def half_of(place, blocks, turned, owners, after):
     n_mo, orbitals, _ = turned.shape
     kc, _, lanes = blocks[-1].shape
     block = orbitals // sum(len(its) for its in owners)
     return pl.pallas_call(
-        functools.partial(half_kernel, n_mo, first, owners),
+        functools.partial(half_kernel, n_mo, owners),
         in_specs=[IN_SMEM] + [IN_VMEM] * (n_mo + 1) + [ANYWHERE] * len(after),
         out_specs=[IN_VMEM] * len(owners),
         out_shape=[jax.ShapeDtypeStruct((1, len(its), kc, block, lanes), jnp.bfloat16) for its in owners],
@@ -262,13 +254,17 @@
     last = len(CHUNKS) - 1
     firsts = [sum(CHUNKS[:c]) for c in range(last + 1)]
 
-    near, queue, token = [], [], []
-    for batch, chunks in enumerate(BATCHES):
-        (own, beside), far = quarter_of(place, by_r, coeffs, n_mo, padded, batch, token)
-        beside = flipped(beside, "mo", n_mo, 1, f"beside{batch}")
-        near += [(own, beside, sum(chunks[:c])) for c in range(len(chunks))]
-        queue += far
-        token = [own]
+    others = list(range(1, n_mo // 2))
+    blocks = quarter_of(place, by_r, coeffs, padded, 0, others, [])
+    queue = [sum(some, []) for some in zip(*blocks)]
+    (near,) = quarter_of(place, by_r, coeffs, padded, 0, [0], queue[0][:1])
+    token = near[0][:1]
+    for batch in range(1, len(BATCHES)):
+        blocks = quarter_of(place, by_r, coeffs, padded, batch, [0, *others], token)
+        near += blocks[0]
+        queue += [sum(some, []) for some in zip(*blocks[1:])]
+        token = blocks[0][0][:1]
+    near = [(own, flipped(beside, "mo", n_mo, 1, f"beside{c}")) for c, (own, beside) in enumerate(near)]
 
     def arrive(c):
         return [flipped(x, "mo", n_mo, o, f"y{2 * c + o - 2}") for o, x in enumerate(queue[c], 2)]
@@ -301,8 +297,8 @@
     for _, c, level in sorted(steps):
         kept, _, sent = plan(c, level)
         if level == 0:
-            blocks = [*near[c][:2], *arrived[c]]
-            keep, *messages = half_of(place, blocks, turned, near[c][2], [kept, *sent], token)
+            blocks = [*near[c], *arrived[c]]
+            keep, *messages = half_of(place, blocks, turned, [kept, *sent], token)
             parts[c], owners[c], offsets[c] = [keep], [kept], [[0]]
         else:
             picks = [[[its.index(o) for o in some] for its in owners[c]] for some in sent]

time: 91.8 us -> 95.9 us (1.045)
  Pallas kernels: 22.1 us -> 29.7 us
  waiting for transfers between devices: 34.6 us -> 32.5 us
    pallas_call x6 -> x7, Pallas kernels: 18.3 us -> 25.9 us  [the longest x3 20.7 us: quarter_of(): pl.pallas_call(functools.partial(quarter_kernel, rows, far, len(after)),...]
    ppermute x24 -> x26, waiting for transfers between devices: 34.6 us -> 32.5 us  [flipped(): return lax.ppermute(x, axis, [(i, i ^ offset) for i in range(size)])]
    ppermute x24 -> x26, starting transfers between devices: 33.3 us -> 32.5 us  [flipped(): return lax.ppermute(x, axis, [(i, i ^ offset) for i in range(size)])]
  transfers between devices with their start and end apart: 24 -> 26, of which waited for: 10 -> 12; matrix products, arithmetic and copies ran while one was open for 0% -> 0% of each run, Pallas kernels for 14% -> 22%
where the time goes in v11:
time: 95.9 us; the launch traced here: 95.7 us
  starting transfers between devices  32.5 us (34%)
  waiting for transfers between devices  32.5 us (34%)
  Pallas kernels  29.7 us (31%)
    ppermute x26, starting transfers between devices, flipped(): return lax.ppermute(x, axis, [(i, i ^ offset) for i in range(size)])  32.5 us
    ppermute x26, waiting for transfers between devices, flipped(): return lax.ppermute(x, axis, [(i, i ^ offset) for i in range(size)])  32.5 us
    pallas_call x3, Pallas kernels, quarter_of(): pl.pallas_call(functools.partial(quarter_kernel, rows, far, len(after)),...  20.7 us
    pallas_call x4, Pallas kernels, half_of(): pl.pallas_call(functools.partial(half_kernel, n_mo, owners), in_specs=[IN...  5.21 us
    pallas_call x1, Pallas kernels, combine(): pl.pallas_call(functools.partial(combine_kernel, sources, k_all, per_step...  3.29 us
  transfers between devices with their start and end apart: 26, of which 12 were waited for; matrix products, arithmetic and copies ran while one was open for 0% of the time, Pallas kernels for 22%

profile of v11, /device:TPU:0, one launch (start us, length us, event | category | flops | bytes accessed | tf_op | source)
XLA Modules:
  0.0 95.7 jit_solution(4219715791807156257)
XLA Ops:
  0.0 0.1 pad_add_fusion.place_ref
  0.1 5.6 %quarter.3 = (bf16[4,256,128]{2,1,0:T(8,128)(2,1)S(1)}, bf16[4,256,128]{2,1,0:T(8,128)(2,1)S(1)}, bf16[4,256,128]{2,1,0:T(8,128)(2,1)S(1)}, bf16[4,256,128]{2,1,0:T(8,128)(2,1)S(1)}) custom-call(s32[2]{0:T(128)S(1)} %pad_add_fusion.place_ref, bf16[250,16,1000]{2,1,0:T(8,128)(2,1)} %bitcast.3, bf16[1000,512]{1,0:T(8,128)(2,1)} %c_ref.7), custom_call_target="tpu_custom_call" | custom-call | flops 1024 | bytes 1024 | tf_op jit(solution)/shard_map/quarter/pallas_call | solution.py:76
  5.7 3.0 %collective-permute-start.1 = (bf16[4,256,128]{2,1,0:T(8,128)(2,1)S(1)}, bf16[4,256,128]{2,1,0:T(8,128)(2,1)S(1)}, u32[]{:S(2)}, u32[]{:S(2)}) collective-permute-start(bf16[4,256,128]{2,1,0:T(8,128)(2,1)S(1)} %get-tuple-element.41.refs_0_), channel_id=1, source_target_pairs={{0,2},{1,3},{2,0},{3,1},{4,6},{5,7},{6,4},{7,5},{8,10},{9,11},{10,... | collective-permute-start | bytes 786440 | tf_op jit(solution)/shard_map/y0/ppermute | solution.py:234
  8.7 5.7 %quarter.4 = (bf16[4,256,128]{2,1,0:T(8,128)(2,1)S(1)}, bf16[4,256,128]{2,1,0:T(8,128)(2,1)S(1)}, bf16[4,256,128]{2,1,0:T(8,128)(2,1)S(1)}, bf16[4,256,128]{2,1,0:T(8,128)(2,1)S(1)}) custom-call(s32[2]{0:T(128)S(1)} %pad_add_fusion.place_ref, bf16[250,16,1000]{2,1,0:T(8,128)(2,1)} %bitcast.4, bf16[1000,512]{1,0:T(8,128)(2,1)} %c_ref.7, ...), custom_call_target="tpu_custom_call" | custom-call | flops 1024 | bytes 1024 | tf_op jit(solution)/shard_map/quarter/pallas_call | solution.py:76
  14.4 0.0 copy-start.1
  14.4 0.7 copy-done.1
  15.1 0.0 collective-permute-start
  15.2 0.5 collective-permute-start.4
  15.6 9.4 %quarter.5 = (bf16[4,256,128]{2,1,0:T(8,128)(2,1)S(1)}, bf16[4,256,128]{2,1,0:T(8,128)(2,1)S(1)}, bf16[4,256,128]{2,1,0:T(8,128)(2,1)S(1)}, bf16[4,256,128]{2,1,...) custom-call(s32[2]{0:T(128)S(1)} %pad_add_fusion.place_ref, ...), custom_call_target="tpu_custom_call" | custom-call | flops 1024 | bytes 1024 | tf_op jit(solution)/shard_map/quarter/pallas_call | solution.py:76
  25.0 0.4 turn.1
  25.4 1.5 %collective-permute-start.5 = (bf16[4,256,128]{2,1,0:T(8,128)(2,1)S(1)}, bf16[4,256,128]{2,1,0:T(8,128)(2,1)S(1)}, u32[]{:S(2)}, u32[]{:S(2)}) collective-permute-start(bf16[4,256,128]{2,1,0:T(8,128)(2,1)S(1)} %get-tuple-element.53), channel_id=1, source_target_pairs={{0,2},{1,3},{2,0},{3,1},{4,6},{5,7},{6,4},{7,5},{8,10},{9,11},{10,... | collective-permute-start | bytes 786440 | tf_op jit(solution)/shard_map/y2/ppermute | solution.py:234
  27.0 0.2 collective-permute-start.6
  27.2 0.0 copy-start.3
  27.2 1.3 %half.4 = (bf16[1,4,4,64,128]{4,3,2,1,0:T(8,128)(2,1)S(1)}, bf16[1,4,4,64,128]{4,3,2,1,0:T(8,128)(2,1)S(1)}) custom-call(s32[2]{0:T(128)S(1)} %pad_add_fusion.place_ref, bf16[4,256,128]{2,1,0:T(8,128)(2,1)S(1)} %copy-done.2, bf16[4,256,128]{2,1,0:T(8,128)(2,1)S(1)} %collective-permute-done.refs_1_, bf16[4,256,128]{2,1,0:T(8,128)(2,1)S(1)} %collective-permute-done.1.refs_2_, ...), custom_call_target="tpu_custom_call" | custom-call | flops 1024 | bytes 1024 | tf_op jit(solution)/shard_map/half/pallas_call | solution.py:140
  28.5 2.8 %collective-permute-start.3 = (bf16[1,4,4,64,128]{4,3,2,1,0:T(8,128)(2,1)S(1)}, bf16[1,4,4,64,128]{4,3,2,1,0:T(8,128)(2,1)S(1)}, u32[]{:S(2)}, u32[]{:S(2)}) collective-permute-start(bf16[1,4,4,64,128]{4,3,2,1,0:T(8,128)(2,1)S(1)} %get-tuple-element.50.refs_5_), channel_id=1, source_target_pairs={{0,16},{4,20},{8,24},{12,28},{16,0},{20,4},{24,8},{28,12},{1,17},{... | collective-permute-start | bytes 786440 | tf_op jit(solution)/shard_map/z4c0/ppermute | solution.py:234
  31.3 0.0 collective-permute-start.9
  31.3 1.5 %collective-permute-start.10 = (bf16[4,256,128]{2,1,0:T(8,128)(2,1)S(1)}, bf16[4,256,128]{2,1,0:T(8,128)(2,1)S(1)}, u32[]{:S(2)}, u32[]{:S(2)}) collective-permute-start(bf16[4,256,128]{2,1,0:T(8,128)(2,1)S(1)} %get-tuple-element.58), channel_id=1, source_target_pairs={{0,2},{1,3},{2,0},{3,1},{4,6},{5,7},{6,4},{7,5},{8,10},{9,11},{10,... | collective-permute-start | bytes 786440 | tf_op jit(solution)/shard_map/y4/ppermute | solution.py:234
  32.8 1.8 %collective-permute-done.5.refs_2_ = bf16[4,256,128]{2,1,0:T(8,128)(2,1)S(1)} collective-permute-done((bf16[4,256,128]{2,1,0:T(8,128)(2,1)S(1)}, bf16[4,256,128]{2,1,0:T(8,128)(2,1)S(1)}, u32[]{:S(2)}, u32[]{:S(2)}) %collective-permute-start.5) | collective-permute-done | bytes 262176 | tf_op jit(solution)/shard_map/y2/ppermute | solution.py:234
  34.6 0.4 collective-permute-start.11
  35.0 4.2 %collective-permute-done.6.refs_3_ = bf16[4,256,128]{2,1,0:T(8,128)(2,1)S(1)} collective-permute-done((bf16[4,256,128]{2,1,0:T(8,128)(2,1)S(1)}, bf16[4,256,128]{2,1,0:T(8,128)(2,1)S(1)}, u32[]{:S(2)}, u32[]{:S(2)}) %collective-permute-start.6) | collective-permute-done | bytes 262176 | tf_op jit(solution)/shard_map/y3/ppermute | solution.py:234
  39.2 1.2 %collective-permute-start.14 = (bf16[4,256,128]{2,1,0:T(8,128)(2,1)S(1)}, bf16[4,256,128]{2,1,0:T(8,128)(2,1)S(1)}, u32[]{:S(2)}, u32[]{:S(2)}) collective-permute-start(bf16[4,256,128]{2,1,0:T(8,128)(2,1)S(1)} %get-tuple-element.62), channel_id=1, source_target_pairs={{0,1},{1,0},{2,3},{3,2},{4,5},{5,4},{6,7},{7,6},{8,9},{9,8},{10,11... | collective-permute-start | bytes 786440 | tf_op jit(solution)/shard_map/beside3/ppermute | solution.py:234
  40.4 1.3 %half.5 = (bf16[1,4,4,64,128]{4,3,2,1,0:T(8,128)(2,1)S(1)}, bf16[1,4,4,64,128]{4,3,2,1,0:T(8,128)(2,1)S(1)}) custom-call(s32[2]{0:T(128)S(1)} %pad_add_fusion.place_ref, bf16[4,256,128]{2,1,0:T(8,128)(2,1)S(1)} %get-tuple-element.51.refs_0_, bf16[4,256,128]{2,1,0:T(8,128)(2,1)S(1)} %collective-permute-done.4.refs_1_, ...), custom_call_target="tpu_custom_call" | custom-call | flops 1024 | bytes 1024 | tf_op jit(solution)/shard_map/half/pallas_call | solution.py:140
  41.7 2.1 %collective-permute-done.3.refs_1_ = bf16[1,4,4,64,128]{4,3,2,1,0:T(8,128)(2,1)S(1)} collective-permute-done((bf16[1,4,4,64,128]{4,3,2,1,0:T(8,128)(2,1)S(1)}, bf16[1,4,4,64,128]{4,3,2,1,0:T(8,128)(2,1)S(1)}, u32[]{:S(2)}, u32[]{:S(2)}) %collective-permute-start.3) | collective-permute-done | bytes 262176 | tf_op jit(solution)/shard_map/z4c0/ppermute | solution.py:234
  43.8 0.2 collective-permute-start.8
  44.0 3.9 %collective-permute-start.7 = (bf16[2,2,4,64,128]{4,3,2,1,0:T(8,128)(2,1)S(1)}, bf16[2,2,4,64,128]{4,3,2,1,0:T(8,128)(2,1)S(1)}, u32[]{:S(2)}, u32[]{:S(2)}) collective-permute-start(bf16[2,2,4,64,128]{4,3,2,1,0:T(8,128)(2,1)S(1)} %merge.6.refs_5_), channel_id=1, source_target_pairs={{0,8},{4,12},{8,0},{12,4},{16,24},{20,28},{24,16},{28,20},{1,9},{5... | collective-permute-start | bytes 786440 | tf_op jit(solution)/shard_map/z2c0/ppermute | solution.py:234
  47.9 1.5 %collective-permute-start.15 = (bf16[4,256,128]{2,1,0:T(8,128)(2,1)S(1)}, bf16[4,256,128]{2,1,0:T(8,128)(2,1)S(1)}, u32[]{:S(2)}, u32[]{:S(2)}) collective-permute-start(bf16[4,256,128]{2,1,0:T(8,128)(2,1)S(1)} %get-tuple-element.63), channel_id=1, source_target_pairs={{0,2},{1,3},{2,0},{3,1},{4,6},{5,7},{6,4},{7,5},{8,10},{9,11},{10,... | collective-permute-start | bytes 786440 | tf_op jit(solution)/shard_map/y6/ppermute | solution.py:234
  49.4 1.1 %collective-permute-done.11.refs_3_ = bf16[4,256,128]{2,1,0:T(8,128)(2,1)S(1)} collective-permute-done((bf16[4,256,128]{2,1,0:T(8,128)(2,1)S(1)}, bf16[4,256,128]{2,1,0:T(8,128)(2,1)S(1)}, u32[]{:S(2)}, u32[]{:S(2)}) %collective-permute-start.11) | collective-permute-done | bytes 262176 | tf_op jit(solution)/shard_map/y5/ppermute | solution.py:234
  50.4 2.2 %collective-permute-start.16 = (bf16[4,256,128]{2,1,0:T(8,128)(2,1)}, bf16[4,256,128]{2,1,0:T(8,128)(2,1)S(1)}, u32[]{:S(2)}, u32[]{:S(2)}) collective-permute-start(bf16[4,256,128]{2,1,0:T(8,128)(2,1)} %get-tuple-element.64), channel_id=1, source_target_pairs={{0,3},{1,2},{2,1},{3,0},{4,7},{5,6},{6,5},{7,4},{8,11},{9,10},{10,... | collective-permute-start | bytes 786440 | tf_op jit(solution)/shard_map/y7/ppermute | solution.py:234
  52.6 1.3 %half.6 = (bf16[1,4,4,64,128]{4,3,2,1,0:T(8,128)(2,1)S(1)}, bf16[1,4,4,64,128]{4,3,2,1,0:T(8,128)(2,1)S(1)}) custom-call(s32[2]{0:T(128)S(1)} %pad_add_fusion.place_ref, bf16[4,256,128]{2,1,0:T(8,128)(2,1)S(1)} %get-tuple-element.47.refs_3_.refs_0_, bf16[4,256,128]{2,1,0:T(8,128)(2,1)S(1)} %collective-permute-done.9.refs_1_, ...), custom_call_target="tpu_custom_call" | custom-call | flops 1024 | bytes 1024 | tf_op jit(solution)/shard_map/half/pallas_call | solution.py:140
  54.0 4.3 %collective-permute-done.8.refs_1_.refs_5_ = bf16[1,4,4,64,128]{4,3,2,1,0:T(8,128)(2,1)S(1)} collective-permute-done((bf16[1,4,4,64,128]{4,3,2,1,0:T(8,128)(2,1)S(1)}, bf16[1,4,4,64,128]{4,3,2,1,0:T(8,128)(2,1)S(1)}, u32[]{:S(2)}, u32[]{:S(2)}) %collective-permute-start.8) | collective-permute-done | bytes 262176 | tf_op jit(solution)/shard_map/z4c1/ppermute | solution.py:234
  58.3 0.1 collective-permute-done.7.refs_2_
  58.5 2.9 %collective-permute-done.16.refs_3_ = bf16[4,256,128]{2,1,0:T(8,128)(2,1)S(1)} collective-permute-done((bf16[4,256,128]{2,1,0:T(8,128)(2,1)}, bf16[4,256,128]{2,1,0:T(8,128)(2,1)S(1)}, u32[]{:S(2)}, u32[]{:S(2)}) %collective-permute-start.16) | collective-permute-done | bytes 262176 | tf_op jit(solution)/shard_map/y7/ppermute | solution.py:234
  61.4 1.3 %half.7 = (bf16[1,4,4,64,128]{4,3,2,1,0:T(8,128)(2,1)S(1)}, bf16[1,4,4,64,128]{4,3,2,1,0:T(8,128)(2,1)S(1)}) custom-call(s32[2]{0:T(128)S(1)} %pad_add_fusion.place_ref, bf16[4,256,128]{2,1,0:T(8,128)(2,1)S(1)} %get-tuple-element.61.refs_0_, bf16[4,256,128]{2,1,0:T(8,128)(2,1)S(1)} %collective-permute-done.14.refs_1_, ...), custom_call_target="tpu_custom_call" | custom-call | flops 1024 | bytes 1024 | tf_op jit(solution)/shard_map/half/pallas_call | solution.py:140
  62.7 1.9 %collective-permute-start.17 = (bf16[1,4,4,64,128]{4,3,2,1,0:T(8,128)(2,1)S(1)}, bf16[1,4,4,64,128]{4,3,2,1,0:T(8,128)(2,1)S(1)}, u32[]{:S(2)}, u32[]{:S(2)}) collective-permute-start(bf16[1,4,4,64,128]{4,3,2,1,0:T(8,128)(2,1)S(1)} %get-tuple-element.66.refs_2_), channel_id=1, source_target_pairs={{0,4},{4,0},{8,12},{12,8},{16,20},{20,16},{24,28},{28,24},{1,5},{5... | collective-permute-start | bytes 786440 | tf_op jit(solution)/shard_map/z1c3/ppermute | solution.py:234
  64.6 1.7 %collective-permute-start.13 = (bf16[2,2,4,64,128]{4,3,2,1,0:T(8,128)(2,1)S(1)}, bf16[2,2,4,64,128]{4,3,2,1,0:T(8,128)(2,1)S(1)}, u32[]{:S(2)}, u32[]{:S(2)}) collective-permute-start(bf16[2,2,4,64,128]{4,3,2,1,0:T(8,128)(2,1)S(1)} %merge.7.refs_3_), channel_id=1, source_target_pairs={{0,8},{4,12},{8,0},{12,4},{16,24},{20,28},{24,16},{28,20},{1,9},{5... | collective-permute-start | bytes 786440 | tf_op jit(solution)/shard_map/z2c1/ppermute | solution.py:234
  66.3 0.5 collective-permute-start.12
  66.8 5.0 %collective-permute-done.18.refs_1_.refs_9_ = bf16[1,4,4,64,128]{4,3,2,1,0:T(8,128)(2,1)S(1)} collective-permute-done((bf16[1,4,4,64,128]{4,3,2,1,0:T(8,128)(2,1)S(1)}, bf16[1,4,4,64,128]{4,3,2,1,0:T(8,128)(2,1)S(1)}, u32[]{:S(2)}, u32[]{:S(2)}) %collective-permute-start.18) | collective-permute-done | bytes 262176 | tf_op jit(solution)/shard_map/z4c2/ppermute | solution.py:234
  72.0 3.0 %collective-permute-start.24 = (bf16[2,1,4,64,128]{4,3,2,1,0:T(8,128)(2,1)S(1)}, bf16[2,1,4,64,128]{4,3,2,1,0:T(8,128)(2,1)S(1)}, u32[]{:S(2)}, u32[]{:S(2)}) collective-permute-start(bf16[2,1,4,64,128]{4,3,2,1,0:T(8,128)(2,1)S(1)} %get-tuple-element.75), channel_id=1, source_target_pairs={{0,16},{4,20},{8,24},{12,28},{16,0},{20,4},{24,8},{28,12},{1,17},{... | collective-permute-start | bytes 393224 | tf_op jit(solution)/shard_map/z4c3/ppermute | solution.py:234
  75.0 1.3 %collective-permute-start.23 = (bf16[2,1,4,64,128]{4,3,2,1,0:T(8,128)(2,1)S(1)}, bf16[2,1,4,64,128]{4,3,2,1,0:T(8,128)(2,1)S(1)}, u32[]{:S(2)}, u32[]{:S(2)}) collective-permute-start(bf16[2,1,4,64,128]{4,3,2,1,0:T(8,128)(2,1)S(1)} %get-tuple-element.71.refs_3_), channel_id=1, source_target_pairs={{0,24},{4,28},{8,16},{12,20},{16,8},{20,12},{24,0},{28,4},{1,25},{... | collective-permute-start | bytes 393224 | tf_op jit(solution)/shard_map/z6c3/ppermute | solution.py:234
  76.4 2.0 %collective-permute-done.13.refs_2_.refs_6_ = bf16[2,2,4,64,128]{4,3,2,1,0:T(8,128)(2,1)S(1)} collective-permute-done((bf16[2,2,4,64,128]{4,3,2,1,0:T(8,128)(2,1)S(1)}, bf16[2,2,4,64,128]{4,3,2,1,0:T(8,128)(2,1)S(1)}, u32[]{:S(2)}, u32[]{:S(2)}) %collective-permute-start.13) | collective-permute-done | bytes 262176 | tf_op jit(solution)/shard_map/z2c1/ppermute | solution.py:234
  78.4 1.3 %collective-permute-start.19 = (bf16[4,1,4,64,128]{4,3,2,1,0:T(8,128)(2,1)S(1)}, bf16[4,1,4,64,128]{4,3,2,1,0:T(8,128)(2,1)S(1)}, u32[]{:S(2)}, u32[]{:S(2)}) collective-permute-start(bf16[4,1,4,64,128]{4,3,2,1,0:T(8,128)(2,1)S(1)} %merge.11.refs_1_), channel_id=1, source_target_pairs={{0,4},{4,0},{8,12},{12,8},{16,20},{20,16},{24,28},{28,24},{1,5},{5... | collective-permute-start | bytes 786440 | tf_op jit(solution)/shard_map/z1c1/ppermute | solution.py:234
  79.7 1.0 %collective-permute-start.20 = (bf16[2,1,4,64,128]{4,3,2,1,0:T(8,128)(2,1)S(1)}, bf16[2,1,4,64,128]{4,3,2,1,0:T(8,128)(2,1)S(1)}, u32[]{:S(2)}, u32[]{:S(2)}) collective-permute-start(bf16[2,1,4,64,128]{4,3,2,1,0:T(8,128)(2,1)S(1)} %get-tuple-element.72), channel_id=1, source_target_pairs={{0,12},{4,8},{8,4},{12,0},{16,28},{20,24},{24,20},{28,16},{1,13},{... | collective-permute-start | bytes 393224 | tf_op jit(solution)/shard_map/z3c2/ppermute | solution.py:234
  80.7 1.3 %collective-permute-start.25 = (bf16[2,1,4,64,128]{4,3,2,1,0:T(8,128)(2,1)S(1)}, bf16[2,1,4,64,128]{4,3,2,1,0:T(8,128)(2,1)S(1)}, u32[]{:S(2)}, u32[]{:S(2)}) collective-permute-start(bf16[2,1,4,64,128]{4,3,2,1,0:T(8,128)(2,1)S(1)} %get-tuple-element.76), channel_id=1, source_target_pairs={{0,8},{4,12},{8,0},{12,4},{16,24},{20,28},{24,16},{28,20},{1,9},{5... | collective-permute-start | bytes 393224 | tf_op jit(solution)/shard_map/z2c3/ppermute | solution.py:234
  82.0 2.9 %collective-permute-done.24.refs_0_.refs_16_ = bf16[2,1,4,64,128]{4,3,2,1,0:T(8,128)(2,1)S(1)} collective-permute-done((bf16[2,1,4,64,128]{4,3,2,1,0:T(8,128)(2,1)S(1)}, bf16[2,1,4,64,128]{4,3,2,1,0:T(8,128)(2,1)S(1)}, u32[]{:S(2)}, u32[]{:S(2)}) %collective-permute-start.24) | collective-permute-done | bytes 131104 | tf_op jit(solution)/shard_map/z4c3/ppermute | solution.py:234
  84.9 1.5 %collective-permute-start.22 = (bf16[2,1,4,64,128]{4,3,2,1,0:T(8,128)(2,1)S(1)}, bf16[2,1,4,64,128]{4,3,2,1,0:T(8,128)(2,1)S(1)}, u32[]{:S(2)}, u32[]{:S(2)}) collective-permute-start(bf16[2,1,4,64,128]{4,3,2,1,0:T(8,128)(2,1)S(1)} %get-tuple-element.74), channel_id=1, source_target_pairs={{0,4},{4,0},{8,12},{12,8},{16,20},{20,16},{24,28},{28,24},{1,5},{5... | collective-permute-start | bytes 393224 | tf_op jit(solution)/shard_map/z1c2/ppermute | solution.py:234
  86.4 3.4 %collective-permute-done.25.refs_0_.refs_17_ = bf16[2,1,4,64,128]{4,3,2,1,0:T(8,128)(2,1)S(1)} collective-permute-done((bf16[2,1,4,64,128]{4,3,2,1,0:T(8,128)(2,1)S(1)}, bf16[2,1,4,64,128]{4,3,2,1,0:T(8,128)(2,1)S(1)}, u32[]{:S(2)}, u32[]{:S(2)}) %collective-permute-start.25) | collective-permute-done | bytes 131104 | tf_op jit(solution)/shard_map/z2c3/ppermute | solution.py:234
  89.9 2.5 %collective-permute-done.21.refs_11_ = bf16[2,1,4,64,128]{4,3,2,1,0:T(8,128)(2,1)S(1)} collective-permute-done((bf16[2,1,4,64,128]{4,3,2,1,0:T(8,128)(2,1)S(1)}, bf16[2,1,4,64,128]{4,3,2,1,0:T(8,128)(2,1)S(1)}, u32[]{:S(2)}, u32[]{:S(2)}) %collective-permute-start.21) | collective-permute-done | bytes 131104 | tf_op jit(solution)/shard_map/z2c2/ppermute | solution.py:234
  92.4 3.3 %combine.1 = f32[128,64,128]{2,1,0:T(8,128)} custom-call(s32[128]{0:T(128)S(1)} %copy-done.3, s32[2]{0:T(128)S(1)} %pad_add_fusion.place_ref, bf16[1,4,4,64,128]{4,3,2,1,0:T(8,128)(2,1)S(1)} %get-tuple-element.49.refs_0_, bf16[1,4,4,64,128]{4,3,2,1,0:T(8,128)(2,1)S(1)} %collective-permute-done.3.refs_1_, ...), custom_call_target="tpu_custom_call" | custom-call | flops 1024 | bytes 1024 | tf_op jit(solution)/shard_map/combine/pallas_call | solution.py:216
  (32 shorter events, 0.2 us)
Async XLA Ops:
  5.7 19.4 %collective-permute-start.1 = (bf16[4,256,128]{2,1,0:T(8,128)(2,1)S(1)}, bf16[4,256,128]{2,1,0:T(8,128)(2,1)S(1)}, u32[]{:S(2)}, u32[]{:S(2)}) collective-permute-start(bf16[4,256,128]{2,1,0:T(8,128)(2,1)S(1)} %get-tuple-element.41.refs_0_), channel_id=1, source_target_pairs={{0,2},{1,3},{2,0},{3,1},{4,6},{5,7},{6,4},{7,5},{8,10},{9,11},{10,... | collective-permute-start | bytes 786440 | tf_op jit(solution)/shard_map/y0/ppermute | solution.py:234
  8.7 16.3 %copy-start = (bf16[1000,512]{1,0:T(8,128)(2,1)S(1)}, bf16[1000,512]{1,0:T(8,128)(2,1)}, u32[]{:S(2)}) copy-start(bf16[1000,512]{1,0:T(8,128)(2,1)} %c_ref.7) | copy-start | bytes 3072004
  8.7 18.5 %collective-permute-start.2 = (bf16[4,256,128]{2,1,0:T(8,128)(2,1)S(1)}, bf16[4,256,128]{2,1,0:T(8,128)(2,1)S(1)}, u32[]{:S(2)}, u32[]{:S(2)}) collective-permute-start(bf16[4,256,128]{2,1,0:T(8,128)(2,1)S(1)} %get-tuple-element.44), channel_id=1, source_target_pairs={{0,3},{1,2},{2,1},{3,0},{4,7},{5,6},{6,5},{7,4},{8,11},{9,10},{10,... | collective-permute-start | bytes 786440 | tf_op jit(solution)/shard_map/y1/ppermute | solution.py:234
  14.4 0.7 copy-start.1
  15.1 12.0 %copy-start.2 = (bf16[4,256,128]{2,1,0:T(8,128)(2,1)S(1)}, bf16[4,256,128]{2,1,0:T(8,128)(2,1)}, u32[]{:S(2)}) copy-start(bf16[4,256,128]{2,1,0:T(8,128)(2,1)} %copy-done.1) | copy-start | bytes 786436
  15.1 12.0 %collective-permute-start = (bf16[4,256,128]{2,1,0:T(8,128)(2,1)S(1)}, bf16[4,256,128]{2,1,0:T(8,128)(2,1)S(1)}, u32[]{:S(2)}, u32[]{:S(2)}) collective-permute-start(bf16[4,256,128]{2,1,0:T(8,128)(2,1)S(1)} %get-tuple-element.43), channel_id=1, source_target_pairs={{0,1},{1,0},{2,3},{3,2},{4,5},{5,4},{6,7},{7,6},{8,9},{9,8},{10,11... | collective-permute-start | bytes 786440 | tf_op jit(solution)/shard_map/beside0/ppermute | solution.py:234
  15.2 16.2 %collective-permute-start.4 = (bf16[4,256,128]{2,1,0:T(8,128)(2,1)S(1)}, bf16[4,256,128]{2,1,0:T(8,128)(2,1)S(1)}, u32[]{:S(2)}, u32[]{:S(2)}) collective-permute-start(bf16[4,256,128]{2,1,0:T(8,128)(2,1)S(1)} %get-tuple-element.52), channel_id=1, source_target_pairs={{0,1},{1,0},{2,3},{3,2},{4,5},{5,4},{6,7},{7,6},{8,9},{9,8},{10,11... | collective-permute-start | bytes 786440 | tf_op jit(solution)/shard_map/beside1/ppermute | solution.py:234
  25.4 9.2 %collective-permute-start.5 = (bf16[4,256,128]{2,1,0:T(8,128)(2,1)S(1)}, bf16[4,256,128]{2,1,0:T(8,128)(2,1)S(1)}, u32[]{:S(2)}, u32[]{:S(2)}) collective-permute-start(bf16[4,256,128]{2,1,0:T(8,128)(2,1)S(1)} %get-tuple-element.53), channel_id=1, source_target_pairs={{0,2},{1,3},{2,0},{3,1},{4,6},{5,7},{6,4},{7,5},{8,10},{9,11},{10,... | collective-permute-start | bytes 786440 | tf_op jit(solution)/shard_map/y2/ppermute | solution.py:234
  27.0 12.2 %collective-permute-start.6 = (bf16[4,256,128]{2,1,0:T(8,128)(2,1)S(1)}, bf16[4,256,128]{2,1,0:T(8,128)(2,1)S(1)}, u32[]{:S(2)}, u32[]{:S(2)}) collective-permute-start(bf16[4,256,128]{2,1,0:T(8,128)(2,1)S(1)} %get-tuple-element.54), channel_id=1, source_target_pairs={{0,3},{1,2},{2,1},{3,0},{4,7},{5,6},{6,5},{7,4},{8,11},{9,10},{10,... | collective-permute-start | bytes 786440 | tf_op jit(solution)/shard_map/y3/ppermute | solution.py:234
  27.2 65.2 %copy-start.3 = (s32[128]{0:T(128)S(1)}, s32[128]{0:T(128)}, u32[]{:S(2)}) copy-start(s32[128]{0:T(128)} %mirror_ref.1) | copy-start | bytes 1540
  28.5 15.3 %collective-permute-start.3 = (bf16[1,4,4,64,128]{4,3,2,1,0:T(8,128)(2,1)S(1)}, bf16[1,4,4,64,128]{4,3,2,1,0:T(8,128)(2,1)S(1)}, u32[]{:S(2)}, u32[]{:S(2)}) collective-permute-start(bf16[1,4,4,64,128]{4,3,2,1,0:T(8,128)(2,1)S(1)} %get-tuple-element.50.refs_5_), channel_id=1, source_target_pairs={{0,16},{4,20},{8,24},{12,28},{16,0},{20,4},{24,8},{28,12},{1,17},{... | collective-permute-start | bytes 786440 | tf_op jit(solution)/shard_map/z4c0/ppermute | solution.py:234
  31.3 12.7 %collective-permute-start.9 = (bf16[4,256,128]{2,1,0:T(8,128)(2,1)S(1)}, bf16[4,256,128]{2,1,0:T(8,128)(2,1)S(1)}, u32[]{:S(2)}, u32[]{:S(2)}) collective-permute-start(bf16[4,256,128]{2,1,0:T(8,128)(2,1)S(1)} %get-tuple-element.57), channel_id=1, source_target_pairs={{0,1},{1,0},{2,3},{3,2},{4,5},{5,4},{6,7},{7,6},{8,9},{9,8},{10,11... | collective-permute-start | bytes 786440 | tf_op jit(solution)/shard_map/beside2/ppermute | solution.py:234
  31.3 16.6 %collective-permute-start.10 = (bf16[4,256,128]{2,1,0:T(8,128)(2,1)S(1)}, bf16[4,256,128]{2,1,0:T(8,128)(2,1)S(1)}, u32[]{:S(2)}, u32[]{:S(2)}) collective-permute-start(bf16[4,256,128]{2,1,0:T(8,128)(2,1)S(1)} %get-tuple-element.58), channel_id=1, source_target_pairs={{0,2},{1,3},{2,0},{3,1},{4,6},{5,7},{6,4},{7,5},{8,10},{9,11},{10,... | collective-permute-start | bytes 786440 | tf_op jit(solution)/shard_map/y4/ppermute | solution.py:234
  34.6 15.8 %collective-permute-start.11 = (bf16[4,256,128]{2,1,0:T(8,128)(2,1)S(1)}, bf16[4,256,128]{2,1,0:T(8,128)(2,1)S(1)}, u32[]{:S(2)}, u32[]{:S(2)}) collective-permute-start(bf16[4,256,128]{2,1,0:T(8,128)(2,1)S(1)} %get-tuple-element.59), channel_id=1, source_target_pairs={{0,3},{1,2},{2,1},{3,0},{4,7},{5,6},{6,5},{7,4},{8,11},{9,10},{10,... | collective-permute-start | bytes 786440 | tf_op jit(solution)/shard_map/y5/ppermute | solution.py:234
  39.2 19.3 %collective-permute-start.14 = (bf16[4,256,128]{2,1,0:T(8,128)(2,1)S(1)}, bf16[4,256,128]{2,1,0:T(8,128)(2,1)S(1)}, u32[]{:S(2)}, u32[]{:S(2)}) collective-permute-start(bf16[4,256,128]{2,1,0:T(8,128)(2,1)S(1)} %get-tuple-element.62), channel_id=1, source_target_pairs={{0,1},{1,0},{2,3},{3,2},{4,5},{5,4},{6,7},{7,6},{8,9},{9,8},{10,11... | collective-permute-start | bytes 786440 | tf_op jit(solution)/shard_map/beside3/ppermute | solution.py:234
  43.8 14.5 %collective-permute-start.8 = (bf16[1,4,4,64,128]{4,3,2,1,0:T(8,128)(2,1)S(1)}, bf16[1,4,4,64,128]{4,3,2,1,0:T(8,128)(2,1)S(1)}, u32[]{:S(2)}, u32[]{:S(2)}) collective-permute-start(bf16[1,4,4,64,128]{4,3,2,1,0:T(8,128)(2,1)S(1)} %get-tuple-element.55.refs_2_), channel_id=1, source_target_pairs={{0,16},{4,20},{8,24},{12,28},{16,0},{20,4},{24,8},{28,12},{1,17},{... | collective-permute-start | bytes 786440 | tf_op jit(solution)/shard_map/z4c1/ppermute | solution.py:234
  44.0 14.4 %collective-permute-start.7 = (bf16[2,2,4,64,128]{4,3,2,1,0:T(8,128)(2,1)S(1)}, bf16[2,2,4,64,128]{4,3,2,1,0:T(8,128)(2,1)S(1)}, u32[]{:S(2)}, u32[]{:S(2)}) collective-permute-start(bf16[2,2,4,64,128]{4,3,2,1,0:T(8,128)(2,1)S(1)} %merge.6.refs_5_), channel_id=1, source_target_pairs={{0,8},{4,12},{8,0},{12,4},{16,24},{20,28},{24,16},{28,20},{1,9},{5... | collective-permute-start | bytes 786440 | tf_op jit(solution)/shard_map/z2c0/ppermute | solution.py:234
  47.9 10.6 %collective-permute-start.15 = (bf16[4,256,128]{2,1,0:T(8,128)(2,1)S(1)}, bf16[4,256,128]{2,1,0:T(8,128)(2,1)S(1)}, u32[]{:S(2)}, u32[]{:S(2)}) collective-permute-start(bf16[4,256,128]{2,1,0:T(8,128)(2,1)S(1)} %get-tuple-element.63), channel_id=1, source_target_pairs={{0,2},{1,3},{2,0},{3,1},{4,6},{5,7},{6,4},{7,5},{8,10},{9,11},{10,... | collective-permute-start | bytes 786440 | tf_op jit(solution)/shard_map/y6/ppermute | solution.py:234
  50.4 11.0 %collective-permute-start.16 = (bf16[4,256,128]{2,1,0:T(8,128)(2,1)}, bf16[4,256,128]{2,1,0:T(8,128)(2,1)S(1)}, u32[]{:S(2)}, u32[]{:S(2)}) collective-permute-start(bf16[4,256,128]{2,1,0:T(8,128)(2,1)} %get-tuple-element.64), channel_id=1, source_target_pairs={{0,3},{1,2},{2,1},{3,0},{4,7},{5,6},{6,5},{7,4},{8,11},{9,10},{10,... | collective-permute-start | bytes 786440 | tf_op jit(solution)/shard_map/y7/ppermute | solution.py:234
  58.3 13.6 %collective-permute-start.18 = (bf16[1,4,4,64,128]{4,3,2,1,0:T(8,128)(2,1)S(1)}, bf16[1,4,4,64,128]{4,3,2,1,0:T(8,128)(2,1)S(1)}, u32[]{:S(2)}, u32[]{:S(2)}) collective-permute-start(bf16[1,4,4,64,128]{4,3,2,1,0:T(8,128)(2,1)S(1)} %get-tuple-element.60.refs_2_), channel_id=1, source_target_pairs={{0,16},{4,20},{8,24},{12,28},{16,0},{20,4},{24,8},{28,12},{1,17},{... | collective-permute-start | bytes 786440 | tf_op jit(solution)/shard_map/z4c2/ppermute | solution.py:234
  62.7 9.2 %collective-permute-start.17 = (bf16[1,4,4,64,128]{4,3,2,1,0:T(8,128)(2,1)S(1)}, bf16[1,4,4,64,128]{4,3,2,1,0:T(8,128)(2,1)S(1)}, u32[]{:S(2)}, u32[]{:S(2)}) collective-permute-start(bf16[1,4,4,64,128]{4,3,2,1,0:T(8,128)(2,1)S(1)} %get-tuple-element.66.refs_2_), channel_id=1, source_target_pairs={{0,4},{4,0},{8,12},{12,8},{16,20},{20,16},{24,28},{28,24},{1,5},{5... | collective-permute-start | bytes 786440 | tf_op jit(solution)/shard_map/z1c3/ppermute | solution.py:234
  64.6 13.8 %collective-permute-start.13 = (bf16[2,2,4,64,128]{4,3,2,1,0:T(8,128)(2,1)S(1)}, bf16[2,2,4,64,128]{4,3,2,1,0:T(8,128)(2,1)S(1)}, u32[]{:S(2)}, u32[]{:S(2)}) collective-permute-start(bf16[2,2,4,64,128]{4,3,2,1,0:T(8,128)(2,1)S(1)} %merge.7.refs_3_), channel_id=1, source_target_pairs={{0,8},{4,12},{8,0},{12,4},{16,24},{20,28},{24,16},{28,20},{1,9},{5... | collective-permute-start | bytes 786440 | tf_op jit(solution)/shard_map/z2c1/ppermute | solution.py:234
  66.3 12.1 %collective-permute-start.12 = (bf16[4,1,4,64,128]{4,3,2,1,0:T(8,128)(2,1)S(1)}, bf16[4,1,4,64,128]{4,3,2,1,0:T(8,128)(2,1)S(1)}, u32[]{:S(2)}, u32[]{:S(2)}) collective-permute-start(bf16[4,1,4,64,128]{4,3,2,1,0:T(8,128)(2,1)S(1)} %merge.8.refs_5_), channel_id=1, source_target_pairs={{0,4},{4,0},{8,12},{12,8},{16,20},{20,16},{24,28},{28,24},{1,5},{5... | collective-permute-start | bytes 786440 | tf_op jit(solution)/shard_map/z1c0/ppermute | solution.py:234
  72.0 12.9 %collective-permute-start.24 = (bf16[2,1,4,64,128]{4,3,2,1,0:T(8,128)(2,1)S(1)}, bf16[2,1,4,64,128]{4,3,2,1,0:T(8,128)(2,1)S(1)}, u32[]{:S(2)}, u32[]{:S(2)}) collective-permute-start(bf16[2,1,4,64,128]{4,3,2,1,0:T(8,128)(2,1)S(1)} %get-tuple-element.75), channel_id=1, source_target_pairs={{0,16},{4,20},{8,24},{12,28},{16,0},{20,4},{24,8},{28,12},{1,17},{... | collective-permute-start | bytes 393224 | tf_op jit(solution)/shard_map/z4c3/ppermute | solution.py:234
  75.0 9.8 %collective-permute-start.23 = (bf16[2,1,4,64,128]{4,3,2,1,0:T(8,128)(2,1)S(1)}, bf16[2,1,4,64,128]{4,3,2,1,0:T(8,128)(2,1)S(1)}, u32[]{:S(2)}, u32[]{:S(2)}) collective-permute-start(bf16[2,1,4,64,128]{4,3,2,1,0:T(8,128)(2,1)S(1)} %get-tuple-element.71.refs_3_), channel_id=1, source_target_pairs={{0,24},{4,28},{8,16},{12,20},{16,8},{20,12},{24,0},{28,4},{1,25},{... | collective-permute-start | bytes 393224 | tf_op jit(solution)/shard_map/z6c3/ppermute | solution.py:234
  78.4 13.9 %collective-permute-start.19 = (bf16[4,1,4,64,128]{4,3,2,1,0:T(8,128)(2,1)S(1)}, bf16[4,1,4,64,128]{4,3,2,1,0:T(8,128)(2,1)S(1)}, u32[]{:S(2)}, u32[]{:S(2)}) collective-permute-start(bf16[4,1,4,64,128]{4,3,2,1,0:T(8,128)(2,1)S(1)} %merge.11.refs_1_), channel_id=1, source_target_pairs={{0,4},{4,0},{8,12},{12,8},{16,20},{20,16},{24,28},{28,24},{1,5},{5... | collective-permute-start | bytes 786440 | tf_op jit(solution)/shard_map/z1c1/ppermute | solution.py:234
  79.7 10.2 %collective-permute-start.20 = (bf16[2,1,4,64,128]{4,3,2,1,0:T(8,128)(2,1)S(1)}, bf16[2,1,4,64,128]{4,3,2,1,0:T(8,128)(2,1)S(1)}, u32[]{:S(2)}, u32[]{:S(2)}) collective-permute-start(bf16[2,1,4,64,128]{4,3,2,1,0:T(8,128)(2,1)S(1)} %get-tuple-element.72), channel_id=1, source_target_pairs={{0,12},{4,8},{8,4},{12,0},{16,28},{20,24},{24,20},{28,16},{1,13},{... | collective-permute-start | bytes 393224 | tf_op jit(solution)/shard_map/z3c2/ppermute | solution.py:234
  80.7 9.1 %collective-permute-start.25 = (bf16[2,1,4,64,128]{4,3,2,1,0:T(8,128)(2,1)S(1)}, bf16[2,1,4,64,128]{4,3,2,1,0:T(8,128)(2,1)S(1)}, u32[]{:S(2)}, u32[]{:S(2)}) collective-permute-start(bf16[2,1,4,64,128]{4,3,2,1,0:T(8,128)(2,1)S(1)} %get-tuple-element.76), channel_id=1, source_target_pairs={{0,8},{4,12},{8,0},{12,4},{16,24},{20,28},{24,16},{28,20},{1,9},{5... | collective-permute-start | bytes 393224 | tf_op jit(solution)/shard_map/z2c3/ppermute | solution.py:234
  84.9 7.5 %collective-permute-start.21 = (bf16[2,1,4,64,128]{4,3,2,1,0:T(8,128)(2,1)S(1)}, bf16[2,1,4,64,128]{4,3,2,1,0:T(8,128)(2,1)S(1)}, u32[]{:S(2)}, u32[]{:S(2)}) collective-permute-start(bf16[2,1,4,64,128]{4,3,2,1,0:T(8,128)(2,1)S(1)} %get-tuple-element.73), channel_id=1, source_target_pairs={{0,8},{4,12},{8,0},{12,4},{16,24},{20,28},{24,16},{28,20},{1,9},{5... | collective-permute-start | bytes 393224 | tf_op jit(solution)/shard_map/z2c2/ppermute | solution.py:234
  84.9 7.5 %collective-permute-start.22 = (bf16[2,1,4,64,128]{4,3,2,1,0:T(8,128)(2,1)S(1)}, bf16[2,1,4,64,128]{4,3,2,1,0:T(8,128)(2,1)S(1)}, u32[]{:S(2)}, u32[]{:S(2)}) collective-permute-start(bf16[2,1,4,64,128]{4,3,2,1,0:T(8,128)(2,1)S(1)} %get-tuple-element.74), channel_id=1, source_target_pairs={{0,4},{4,0},{8,12},{12,8},{16,20},{20,16},{24,28},{28,24},{1,5},{5... | collective-permute-start | bytes 393224 | tf_op jit(solution)/shard_map/z1c2/ppermute | solution.py:234

commit v12 on v9

--- a/solution.py
+++ b/solution.py
@@ -8,7 +8,7 @@
 from jax.sharding import PartitionSpec as P
 
 LANES = 128
-STEP = 64
+STEP = 32
 BATCHES = ((4, 4), (4, 4))
 CHUNKS = sum(BATCHES, ())
 SIZES = ((1,), (1,), (1, 2), (-1, 2))
@@ -84,7 +84,7 @@
             ],
         ),
         out_shape=outs,
-        compiler_params=pltpu.CompilerParams(vmem_limit_bytes=50 * MIB),
+        compiler_params=pltpu.CompilerParams(vmem_limit_bytes=51 * MIB),
         cost_estimate=COST,
         name="quarter",
     )(place, by_r, coeffs, *after)
@@ -121,17 +121,23 @@
     blocks, t_ref, held = refs[:n_mo], refs[n_mo], refs[-1]
     outs = refs[-1 - len(owners) : -1]
     kc, block, lanes = outs[0].shape[2:]
-    firsts = [first if x.shape[0] > kc else 0 for x in blocks]
-    columns = [jnp.concatenate([x[at + k] for k in range(kc)], axis=1) for x, at in zip(blocks, firsts)]
-    turned = [t_ref[place_ref[0] ^ o] for o in range(n_mo)]
-    held[...] = jnp.dot(
-        jnp.concatenate(turned, axis=1), jnp.concatenate(columns, axis=0), preferred_element_type=jnp.float32
-    )
-    for out, its in zip(outs, owners):
-        for at, o in enumerate(its):
-            start = pl.multiple_of((place_ref[1] ^ o) * block, block)
-            for k in range(kc):
-                out[0, at, k] = held[pl.ds(start, block), k * lanes : (k + 1) * lanes].astype(jnp.bfloat16)
+
+    @pl.loop(0, kc // 2)
+    def _(pair):
+        columns = []
+        for x in blocks:
+            at = 2 * pair + (first if x.shape[0] > kc else 0)
+            columns.append(jnp.concatenate([x[at], x[at + 1]], axis=1))
+        turned = [t_ref[place_ref[0] ^ o] for o in range(n_mo)]
+        held[...] = jnp.dot(
+            jnp.concatenate(turned, axis=1), jnp.concatenate(columns, axis=0), preferred_element_type=jnp.float32
+        )
+        for out, its in zip(outs, owners):
+            for at, o in enumerate(its):
+                start = pl.multiple_of((place_ref[1] ^ o) * block, block)
+                for n in range(2):
+                    piece = held[pl.ds(start, block), n * lanes : (n + 1) * lanes]
+                    out[0, at, 2 * pair + n] = piece.astype(jnp.bfloat16)
 
 
 def half_of(place, blocks, turned, first, owners, after):
@@ -143,7 +149,7 @@
         in_specs=[IN_SMEM] + [IN_VMEM] * (n_mo + 1) + [ANYWHERE] * len(after),
         out_specs=[IN_VMEM] * len(owners),
         out_shape=[jax.ShapeDtypeStruct((1, len(its), kc, block, lanes), jnp.bfloat16) for its in owners],
-        scratch_shapes=[pltpu.VMEM((orbitals, kc * lanes), jnp.float32)],
+        scratch_shapes=[pltpu.VMEM((orbitals, 2 * lanes), jnp.float32)],
         compiler_params=pltpu.CompilerParams(vmem_limit_bytes=24 * MIB),
         cost_estimate=COST,
         name="half",
@@ -309,7 +315,8 @@
             waiting = messages
         else:
             send(c, level, messages)
-    token = [wait_for([x for x in parts[last][-3:]] + token)]
+    for x in parts[last][-3:]:
+        token = [wait_for([x, *token])]
     pieces = [x for chunk in parts for x in chunk]
     sources = [(tuple(group), first) for chunk, first in zip(offsets, firsts) for group in chunk]
     return combine(pieces, sources, mirror, place, n_pair, token)

time: 90.4 us -> 92.5 us (1.023)
  Pallas kernels: 21.8 us -> 27.6 us
  starting transfers between devices: 36.8 us -> 33.2 us
  local copies, waits for them, and re-layouts: 1.23 us -> 0.02 us
  waiting for transfers between devices: 30.1 us -> 31.1 us
    pallas_call x2, Pallas kernels: 12.8 us -> 17.9 us  [quarter_of(): pl.pallas_call(functools.partial(quarter_kernel, rows, n_mo, blocks, len(...]
    ppermute x24, starting transfers between devices: 36.8 us -> 33.2 us  [flipped(): return lax.ppermute(x, axis, [(i, i ^ offset) for i in range(size)])]
    unnamed x5, local copies, waits for them, and re-layouts: 1.23 us -> 0.02 us
    ppermute x24, waiting for transfers between devices: 30.1 us -> 31.1 us  [flipped(): return lax.ppermute(x, axis, [(i, i ^ offset) for i in range(size)])]
  transfers between devices with their start and end apart: 24 -> 24, of which waited for: 15 -> 15; matrix products, arithmetic and copies ran while one was open for 0% -> 0% of each run, Pallas kernels for 13% -> 17%
where the time goes in v12:
time: 92.5 us; the launch traced here: 92.1 us
  starting transfers between devices  33.2 us (36%)
  waiting for transfers between devices  31.1 us (34%)
  Pallas kernels  27.6 us (30%)
    ppermute x24, starting transfers between devices, flipped(): return lax.ppermute(x, axis, [(i, i ^ offset) for i in range(size)])  33.2 us
    ppermute x24, waiting for transfers between devices, flipped(): return lax.ppermute(x, axis, [(i, i ^ offset) for i in range(size)])  31.1 us
    pallas_call x2, Pallas kernels, quarter_of(): pl.pallas_call(functools.partial(quarter_kernel, rows, n_mo, blocks, len(...  17.9 us
    pallas_call x4, Pallas kernels, half_of(): pl.pallas_call(functools.partial(half_kernel, n_mo, first, owners), in_sp...  5.89 us
    pallas_call x1, Pallas kernels, combine(): pl.pallas_call(functools.partial(combine_kernel, sources, k_all, per_step...  3.29 us
  transfers between devices with their start and end apart: 24, of which 15 were waited for; matrix products, arithmetic and copies ran while one was open for 0% of the time, Pallas kernels for 17%

profile of v12, /device:TPU:0, one launch (start us, length us, event | category | flops | bytes accessed | tf_op | source)
XLA Modules:
  0.0 92.1 jit_solution(3079022661700251755)
XLA Ops:
  0.0 0.1 pad_add_fusion.place_ref
  0.1 9.0 %quarter.2 = (bf16[8,256,128]{2,1,0:T(8,128)(2,1)S(1)}, bf16[8,256,128]{2,1,0:T(8,128)(2,1)S(1)}, bf16[4,256,128]{2,1,0:T(8,128)(2,1)S(1)}, bf16[4,256,128]{2,1,...) custom-call(s32[2]{0:T(128)S(1)} %pad_add_fusion.place_ref, ...), custom_call_target="tpu_custom_call" | custom-call | flops 1024 | bytes 1024 | tf_op jit(solution)/shard_map/quarter/pallas_call | solution.py:72
  9.0 0.5 collective-permute-start
  9.6 2.6 %collective-permute-start.1 = (bf16[4,256,128]{2,1,0:T(8,128)(2,1)S(1)}, bf16[4,256,128]{2,1,0:T(8,128)(2,1)S(1)}, u32[]{:S(2)}, u32[]{:S(2)}) collective-permute-start(bf16[4,256,128]{2,1,0:T(8,128)(2,1)S(1)} %get-tuple-element.39), channel_id=1, source_target_pairs={{0,2},{1,3},{2,0},{3,1},{4,6},{5,7},{6,4},{7,5},{8,10},{9,11},{10,... | collective-permute-start | bytes 786440 | tf_op jit(solution)/shard_map/y0/ppermute | solution.py:241
  12.2 0.1 collective-permute-start.2
  12.2 9.0 %quarter.3 = (bf16[8,256,128]{2,1,0:T(8,128)(2,1)S(1)}, bf16[8,256,128]{2,1,0:T(8,128)(2,1)S(1)}, bf16[4,256,128]{2,1,0:T(8,128)(2,1)S(1)}, bf16[4,256,128]{2,1,...) custom-call(s32[2]{0:T(128)S(1)} %pad_add_fusion.place_ref, ...), custom_call_target="tpu_custom_call" | custom-call | flops 1024 | bytes 1024 | tf_op jit(solution)/shard_map/quarter/pallas_call | solution.py:72
  21.2 0.4 turn.1
  21.6 1.8 %collective-permute-start.4 = (bf16[4,256,128]{2,1,0:T(8,128)(2,1)S(1)}, bf16[4,256,128]{2,1,0:T(8,128)(2,1)S(1)}, u32[]{:S(2)}, u32[]{:S(2)}) collective-permute-start(bf16[4,256,128]{2,1,0:T(8,128)(2,1)S(1)} %get-tuple-element.47), channel_id=1, source_target_pairs={{0,2},{1,3},{2,0},{3,1},{4,6},{5,7},{6,4},{7,5},{8,10},{9,11},{10,... | collective-permute-start | bytes 786440 | tf_op jit(solution)/shard_map/y2/ppermute | solution.py:241
  23.4 0.1 collective-permute-start.8
  23.5 0.3 collective-permute-start.5
  23.8 0.6 collective-permute-done.2.refs_3_
  24.4 1.5 %half.4 = (bf16[1,4,4,64,128]{4,3,2,1,0:T(8,128)(2,1)S(1)}, bf16[1,4,4,64,128]{4,3,2,1,0:T(8,128)(2,1)S(1)}) custom-call(s32[2]{0:T(128)S(1)} %pad_add_fusion.place_ref, bf16[8,256,128]{2,1,0:T(8,128)(2,1)S(1)} %get-tuple-element.37.refs_0_, bf16[8,256,128]{2,1,0:T(8,128)(2,1)S(1)} %collective-permute-done.refs_1_, ...), custom_call_target="tpu_custom_call" | custom-call | flops 1024 | bytes 1024 | tf_op jit(solution)/shard_map/half/pallas_call | solution.py:147
  25.9 0.0 copy-start.1
  25.9 2.7 %collective-permute-start.3 = (bf16[1,4,4,64,128]{4,3,2,1,0:T(8,128)(2,1)S(1)}, bf16[1,4,4,64,128]{4,3,2,1,0:T(8,128)(2,1)S(1)}, u32[]{:S(2)}, u32[]{:S(2)}) collective-permute-start(bf16[1,4,4,64,128]{4,3,2,1,0:T(8,128)(2,1)S(1)} %get-tuple-element.46.refs_5_), channel_id=1, source_target_pairs={{0,16},{4,20},{8,24},{12,28},{16,0},{20,4},{24,8},{28,12},{1,17},{... | collective-permute-start | bytes 786440 | tf_op jit(solution)/shard_map/z4c0/ppermute | solution.py:241
  28.6 1.5 %collective-permute-start.9 = (bf16[4,256,128]{2,1,0:T(8,128)(2,1)S(1)}, bf16[4,256,128]{2,1,0:T(8,128)(2,1)S(1)}, u32[]{:S(2)}, u32[]{:S(2)}) collective-permute-start(bf16[4,256,128]{2,1,0:T(8,128)(2,1)S(1)} %get-tuple-element.52), channel_id=1, source_target_pairs={{0,2},{1,3},{2,0},{3,1},{4,6},{5,7},{6,4},{7,5},{8,10},{9,11},{10,... | collective-permute-start | bytes 786440 | tf_op jit(solution)/shard_map/y4/ppermute | solution.py:241
  30.1 0.7 collective-permute-done.4.refs_2_
  30.8 0.5 collective-permute-start.10
  31.3 4.4 %collective-permute-done.5.refs_3_ = bf16[4,256,128]{2,1,0:T(8,128)(2,1)S(1)} collective-permute-done((bf16[4,256,128]{2,1,0:T(8,128)(2,1)S(1)}, bf16[4,256,128]{2,1,0:T(8,128)(2,1)S(1)}, u32[]{:S(2)}, u32[]{:S(2)}) %collective-permute-start.5) | collective-permute-done | bytes 262176 | tf_op jit(solution)/shard_map/y3/ppermute | solution.py:241
  35.7 1.5 %collective-permute-start.13 = (bf16[4,256,128]{2,1,0:T(8,128)(2,1)S(1)}, bf16[4,256,128]{2,1,0:T(8,128)(2,1)S(1)}, u32[]{:S(2)}, u32[]{:S(2)}) collective-permute-start(bf16[4,256,128]{2,1,0:T(8,128)(2,1)S(1)} %get-tuple-element.55), channel_id=1, source_target_pairs={{0,2},{1,3},{2,0},{3,1},{4,6},{5,7},{6,4},{7,5},{8,10},{9,11},{10,... | collective-permute-start | bytes 786440 | tf_op jit(solution)/shard_map/y6/ppermute | solution.py:241
  37.2 1.5 %half.5 = (bf16[1,4,4,64,128]{4,3,2,1,0:T(8,128)(2,1)S(1)}, bf16[1,4,4,64,128]{4,3,2,1,0:T(8,128)(2,1)S(1)}) custom-call(s32[2]{0:T(128)S(1)} %pad_add_fusion.place_ref, bf16[8,256,128]{2,1,0:T(8,128)(2,1)S(1)} %get-tuple-element.37.refs_0_, bf16[8,256,128]{2,1,0:T(8,128)(2,1)S(1)} %collective-permute-done.refs_1_, ...), custom_call_target="tpu_custom_call" | custom-call | flops 1024 | bytes 1024 | tf_op jit(solution)/shard_map/half/pallas_call | solution.py:147
  38.7 2.3 %collective-permute-done.3.refs_1_ = bf16[1,4,4,64,128]{4,3,2,1,0:T(8,128)(2,1)S(1)} collective-permute-done((bf16[1,4,4,64,128]{4,3,2,1,0:T(8,128)(2,1)S(1)}, bf16[1,4,4,64,128]{4,3,2,1,0:T(8,128)(2,1)S(1)}, u32[]{:S(2)}, u32[]{:S(2)}) %collective-permute-start.3) | collective-permute-done | bytes 262176 | tf_op jit(solution)/shard_map/z4c0/ppermute | solution.py:241
  41.0 0.3 collective-permute-start.7
  41.3 0.7 collective-permute-done.9.refs_2_
  42.0 3.2 %collective-permute-start.6 = (bf16[2,2,4,64,128]{4,3,2,1,0:T(8,128)(2,1)S(1)}, bf16[2,2,4,64,128]{4,3,2,1,0:T(8,128)(2,1)S(1)}, u32[]{:S(2)}, u32[]{:S(2)}) collective-permute-start(bf16[2,2,4,64,128]{4,3,2,1,0:T(8,128)(2,1)S(1)} %merge.6.refs_5_), channel_id=1, source_target_pairs={{0,8},{4,12},{8,0},{12,4},{16,24},{20,28},{24,16},{28,20},{1,9},{5... | collective-permute-start | bytes 786440 | tf_op jit(solution)/shard_map/z2c0/ppermute | solution.py:241
  45.2 1.7 %collective-permute-done.10.refs_3_ = bf16[4,256,128]{2,1,0:T(8,128)(2,1)S(1)} collective-permute-done((bf16[4,256,128]{2,1,0:T(8,128)(2,1)S(1)}, bf16[4,256,128]{2,1,0:T(8,128)(2,1)S(1)}, u32[]{:S(2)}, u32[]{:S(2)}) %collective-permute-start.10) | collective-permute-done | bytes 262176 | tf_op jit(solution)/shard_map/y5/ppermute | solution.py:241
  46.9 2.2 %collective-permute-start.14 = (bf16[4,256,128]{2,1,0:T(8,128)(2,1)S(1)}, bf16[4,256,128]{2,1,0:T(8,128)(2,1)S(1)}, u32[]{:S(2)}, u32[]{:S(2)}) collective-permute-start(bf16[4,256,128]{2,1,0:T(8,128)(2,1)S(1)} %get-tuple-element.56), channel_id=1, source_target_pairs={{0,3},{1,2},{2,1},{3,0},{4,7},{5,6},{6,5},{7,4},{8,11},{9,10},{10,... | collective-permute-start | bytes 786440 | tf_op jit(solution)/shard_map/y7/ppermute | solution.py:241
  49.1 1.5 %half.6 = (bf16[1,4,4,64,128]{4,3,2,1,0:T(8,128)(2,1)S(1)}, bf16[1,4,4,64,128]{4,3,2,1,0:T(8,128)(2,1)S(1)}) custom-call(s32[2]{0:T(128)S(1)} %pad_add_fusion.place_ref, bf16[8,256,128]{2,1,0:T(8,128)(2,1)S(1)} %get-tuple-element.43.refs_3_.refs_0_, bf16[8,256,128]{2,1,0:T(8,128)(2,1)S(1)} %collective-permute-done.8.refs_1_, ...), custom_call_target="tpu_custom_call" | custom-call | flops 1024 | bytes 1024 | tf_op jit(solution)/shard_map/half/pallas_call | solution.py:147
  50.6 2.7 %collective-permute-start.16 = (bf16[1,4,4,64,128]{4,3,2,1,0:T(8,128)(2,1)S(1)}, bf16[1,4,4,64,128]{4,3,2,1,0:T(8,128)(2,1)S(1)}, u32[]{:S(2)}, u32[]{:S(2)}) collective-permute-start(bf16[1,4,4,64,128]{4,3,2,1,0:T(8,128)(2,1)S(1)} %get-tuple-element.54.refs_2_), channel_id=1, source_target_pairs={{0,16},{4,20},{8,24},{12,28},{16,0},{20,4},{24,8},{28,12},{1,17},{... | collective-permute-start | bytes 786440 | tf_op jit(solution)/shard_map/z4c2/ppermute | solution.py:241
  53.2 4.2 %collective-permute-done.7.refs_1_.refs_5_ = bf16[1,4,4,64,128]{4,3,2,1,0:T(8,128)(2,1)S(1)} collective-permute-done((bf16[1,4,4,64,128]{4,3,2,1,0:T(8,128)(2,1)S(1)}, bf16[1,4,4,64,128]{4,3,2,1,0:T(8,128)(2,1)S(1)}, u32[]{:S(2)}, u32[]{:S(2)}) %collective-permute-start.7) | collective-permute-done | bytes 262176 | tf_op jit(solution)/shard_map/z4c1/ppermute | solution.py:241
  57.5 0.4 collective-permute-done.14.refs_3_
  57.9 1.5 %half.7 = (bf16[1,4,4,64,128]{4,3,2,1,0:T(8,128)(2,1)S(1)}, bf16[1,4,4,64,128]{4,3,2,1,0:T(8,128)(2,1)S(1)}) custom-call(s32[2]{0:T(128)S(1)} %pad_add_fusion.place_ref, bf16[8,256,128]{2,1,0:T(8,128)(2,1)S(1)} %get-tuple-element.43.refs_3_.refs_0_, bf16[8,256,128]{2,1,0:T(8,128)(2,1)S(1)} %collective-permute-done.8.refs_1_, ...), custom_call_target="tpu_custom_call" | custom-call | flops 1024 | bytes 1024 | tf_op jit(solution)/shard_map/half/pallas_call | solution.py:147
  59.3 1.8 %collective-permute-start.15 = (bf16[1,4,4,64,128]{4,3,2,1,0:T(8,128)(2,1)S(1)}, bf16[1,4,4,64,128]{4,3,2,1,0:T(8,128)(2,1)S(1)}, u32[]{:S(2)}, u32[]{:S(2)}) collective-permute-start(bf16[1,4,4,64,128]{4,3,2,1,0:T(8,128)(2,1)S(1)} %get-tuple-element.58.refs_2_), channel_id=1, source_target_pairs={{0,4},{4,0},{8,12},{12,8},{16,20},{20,16},{24,28},{28,24},{1,5},{5... | collective-permute-start | bytes 786440 | tf_op jit(solution)/shard_map/z1c3/ppermute | solution.py:241
  61.2 1.6 %collective-permute-start.12 = (bf16[2,2,4,64,128]{4,3,2,1,0:T(8,128)(2,1)S(1)}, bf16[2,2,4,64,128]{4,3,2,1,0:T(8,128)(2,1)S(1)}, u32[]{:S(2)}, u32[]{:S(2)}) collective-permute-start(bf16[2,2,4,64,128]{4,3,2,1,0:T(8,128)(2,1)S(1)} %merge.7.refs_3_), channel_id=1, source_target_pairs={{0,8},{4,12},{8,0},{12,4},{16,24},{20,28},{24,16},{28,20},{1,9},{5... | collective-permute-start | bytes 786440 | tf_op jit(solution)/shard_map/z2c1/ppermute | solution.py:241
  62.7 0.5 collective-permute-start.11
  63.3 3.4 %collective-permute-done.16.refs_1_.refs_9_ = bf16[1,4,4,64,128]{4,3,2,1,0:T(8,128)(2,1)S(1)} collective-permute-done((bf16[1,4,4,64,128]{4,3,2,1,0:T(8,128)(2,1)S(1)}, bf16[1,4,4,64,128]{4,3,2,1,0:T(8,128)(2,1)S(1)}, u32[]{:S(2)}, u32[]{:S(2)}) %collective-permute-start.16) | collective-permute-done | bytes 262176 | tf_op jit(solution)/shard_map/z4c2/ppermute | solution.py:241
  66.7 1.9 %collective-permute-done.15.refs_1_.refs_14_ = bf16[1,4,4,64,128]{4,3,2,1,0:T(8,128)(2,1)S(1)} collective-permute-done((bf16[1,4,4,64,128]{4,3,2,1,0:T(8,128)(2,1)S(1)}, bf16[1,4,4,64,128]{4,3,2,1,0:T(8,128)(2,1)S(1)}, u32[]{:S(2)}, u32[]{:S(2)}) %collective-permute-start.15) | collective-permute-done | bytes 262176 | tf_op jit(solution)/shard_map/z1c3/ppermute | solution.py:241
  68.6 2.8 %collective-permute-start.22 = (bf16[2,1,4,64,128]{4,3,2,1,0:T(8,128)(2,1)S(1)}, bf16[2,1,4,64,128]{4,3,2,1,0:T(8,128)(2,1)S(1)}, u32[]{:S(2)}, u32[]{:S(2)}) collective-permute-start(bf16[2,1,4,64,128]{4,3,2,1,0:T(8,128)(2,1)S(1)} %get-tuple-element.67), channel_id=1, source_target_pairs={{0,16},{4,20},{8,24},{12,28},{16,0},{20,4},{24,8},{28,12},{1,17},{... | collective-permute-start | bytes 393224 | tf_op jit(solution)/shard_map/z4c3/ppermute | solution.py:241
  71.4 1.3 %collective-permute-start.21 = (bf16[2,1,4,64,128]{4,3,2,1,0:T(8,128)(2,1)S(1)}, bf16[2,1,4,64,128]{4,3,2,1,0:T(8,128)(2,1)S(1)}, u32[]{:S(2)}, u32[]{:S(2)}) collective-permute-start(bf16[2,1,4,64,128]{4,3,2,1,0:T(8,128)(2,1)S(1)} %get-tuple-element.63.refs_3_), channel_id=1, source_target_pairs={{0,24},{4,28},{8,16},{12,20},{16,8},{20,12},{24,0},{28,4},{1,25},{... | collective-permute-start | bytes 393224 | tf_op jit(solution)/shard_map/z6c3/ppermute | solution.py:241
  72.8 0.5 collective-permute-done.12.refs_2_.refs_6_
  73.2 0.6 collective-permute-done.11.refs_4_.refs_3_
  73.9 1.5 %collective-permute-start.17 = (bf16[4,1,4,64,128]{4,3,2,1,0:T(8,128)(2,1)S(1)}, bf16[4,1,4,64,128]{4,3,2,1,0:T(8,128)(2,1)S(1)}, u32[]{:S(2)}, u32[]{:S(2)}) collective-permute-start(bf16[4,1,4,64,128]{4,3,2,1,0:T(8,128)(2,1)S(1)} %merge.11.refs_1_), channel_id=1, source_target_pairs={{0,4},{4,0},{8,12},{12,8},{16,20},{20,16},{24,28},{28,24},{1,5},{5... | collective-permute-start | bytes 786440 | tf_op jit(solution)/shard_map/z1c1/ppermute | solution.py:241
  75.4 1.8 %collective-permute-start.18 = (bf16[2,1,4,64,128]{4,3,2,1,0:T(8,128)(2,1)S(1)}, bf16[2,1,4,64,128]{4,3,2,1,0:T(8,128)(2,1)S(1)}, u32[]{:S(2)}, u32[]{:S(2)}) collective-permute-start(bf16[2,1,4,64,128]{4,3,2,1,0:T(8,128)(2,1)S(1)} %get-tuple-element.64), channel_id=1, source_target_pairs={{0,12},{4,8},{8,4},{12,0},{16,28},{20,24},{24,20},{28,16},{1,13},{... | collective-permute-start | bytes 393224 | tf_op jit(solution)/shard_map/z3c2/ppermute | solution.py:241
  77.2 0.2 collective-permute-start.23
  77.4 4.0 %collective-permute-done.22.refs_0_.refs_16_ = bf16[2,1,4,64,128]{4,3,2,1,0:T(8,128)(2,1)S(1)} collective-permute-done((bf16[2,1,4,64,128]{4,3,2,1,0:T(8,128)(2,1)S(1)}, bf16[2,1,4,64,128]{4,3,2,1,0:T(8,128)(2,1)S(1)}, u32[]{:S(2)}, u32[]{:S(2)}) %collective-permute-start.22) | collective-permute-done | bytes 131104 | tf_op jit(solution)/shard_map/z4c3/ppermute | solution.py:241
  81.5 1.5 %collective-permute-start.20 = (bf16[2,1,4,64,128]{4,3,2,1,0:T(8,128)(2,1)S(1)}, bf16[2,1,4,64,128]{4,3,2,1,0:T(8,128)(2,1)S(1)}, u32[]{:S(2)}, u32[]{:S(2)}) collective-permute-start(bf16[2,1,4,64,128]{4,3,2,1,0:T(8,128)(2,1)S(1)} %get-tuple-element.66), channel_id=1, source_target_pairs={{0,4},{4,0},{8,12},{12,8},{16,20},{20,16},{24,28},{28,24},{1,5},{5... | collective-permute-start | bytes 393224 | tf_op jit(solution)/shard_map/z1c2/ppermute | solution.py:241
  83.0 3.1 %collective-permute-done.23.refs_0_.refs_17_ = bf16[2,1,4,64,128]{4,3,2,1,0:T(8,128)(2,1)S(1)} collective-permute-done((bf16[2,1,4,64,128]{4,3,2,1,0:T(8,128)(2,1)S(1)}, bf16[2,1,4,64,128]{4,3,2,1,0:T(8,128)(2,1)S(1)}, u32[]{:S(2)}, u32[]{:S(2)}) %collective-permute-start.23) | collective-permute-done | bytes 131104 | tf_op jit(solution)/shard_map/z2c3/ppermute | solution.py:241
  86.1 2.7 %collective-permute-done.19.refs_11_ = bf16[2,1,4,64,128]{4,3,2,1,0:T(8,128)(2,1)S(1)} collective-permute-done((bf16[2,1,4,64,128]{4,3,2,1,0:T(8,128)(2,1)S(1)}, bf16[2,1,4,64,128]{4,3,2,1,0:T(8,128)(2,1)S(1)}, u32[]{:S(2)}, u32[]{:S(2)}) %collective-permute-start.19) | collective-permute-done | bytes 131104 | tf_op jit(solution)/shard_map/z2c2/ppermute | solution.py:241
  88.8 3.3 %combine.1 = f32[128,64,128]{2,1,0:T(8,128)} custom-call(s32[128]{0:T(128)S(1)} %copy-done.1, s32[2]{0:T(128)S(1)} %pad_add_fusion.place_ref, bf16[1,4,4,64,128]{4,3,2,1,0:T(8,128)(2,1)S(1)} %get-tuple-element.45.refs_0_, bf16[1,4,4,64,128]{4,3,2,1,0:T(8,128)(2,1)S(1)} %collective-permute-done.3.refs_1_, ...), custom_call_target="tpu_custom_call" | custom-call | flops 1024 | bytes 1024 | tf_op jit(solution)/shard_map/combine/pallas_call | solution.py:223
  (23 shorter events, 0.2 us)
Async XLA Ops:
  0.1 21.1 %copy-start = (bf16[1000,512]{1,0:T(8,128)(2,1)S(1)}, bf16[1000,512]{1,0:T(8,128)(2,1)}, u32[]{:S(2)}) copy-start(bf16[1000,512]{1,0:T(8,128)(2,1)} %c_ref.5) | copy-start | bytes 3072004
  9.0 15.4 %collective-permute-start = (bf16[8,256,128]{2,1,0:T(8,128)(2,1)S(1)}, bf16[8,256,128]{2,1,0:T(8,128)(2,1)S(1)}, u32[]{:S(2)}, u32[]{:S(2)}) collective-permute-start(bf16[8,256,128]{2,1,0:T(8,128)(2,1)S(1)} %get-tuple-element.38), channel_id=1, source_target_pairs={{0,1},{1,0},{2,3},{3,2},{4,5},{5,4},{6,7},{7,6},{8,9},{9,8},{10,11... | collective-permute-start | bytes 1572872 | tf_op jit(solution)/shard_map/beside0/ppermute | solution.py:241
  9.6 11.6 %collective-permute-start.1 = (bf16[4,256,128]{2,1,0:T(8,128)(2,1)S(1)}, bf16[4,256,128]{2,1,0:T(8,128)(2,1)S(1)}, u32[]{:S(2)}, u32[]{:S(2)}) collective-permute-start(bf16[4,256,128]{2,1,0:T(8,128)(2,1)S(1)} %get-tuple-element.39), channel_id=1, source_target_pairs={{0,2},{1,3},{2,0},{3,1},{4,6},{5,7},{6,4},{7,5},{8,10},{9,11},{10,... | collective-permute-start | bytes 786440 | tf_op jit(solution)/shard_map/y0/ppermute | solution.py:241
  12.2 12.3 %collective-permute-start.2 = (bf16[4,256,128]{2,1,0:T(8,128)(2,1)S(1)}, bf16[4,256,128]{2,1,0:T(8,128)(2,1)S(1)}, u32[]{:S(2)}, u32[]{:S(2)}) collective-permute-start(bf16[4,256,128]{2,1,0:T(8,128)(2,1)S(1)} %get-tuple-element.40), channel_id=1, source_target_pairs={{0,3},{1,2},{2,1},{3,0},{4,7},{5,6},{6,5},{7,4},{8,11},{9,10},{10,... | collective-permute-start | bytes 786440 | tf_op jit(solution)/shard_map/y1/ppermute | solution.py:241
  21.6 9.2 %collective-permute-start.4 = (bf16[4,256,128]{2,1,0:T(8,128)(2,1)S(1)}, bf16[4,256,128]{2,1,0:T(8,128)(2,1)S(1)}, u32[]{:S(2)}, u32[]{:S(2)}) collective-permute-start(bf16[4,256,128]{2,1,0:T(8,128)(2,1)S(1)} %get-tuple-element.47), channel_id=1, source_target_pairs={{0,2},{1,3},{2,0},{3,1},{4,6},{5,7},{6,4},{7,5},{8,10},{9,11},{10,... | collective-permute-start | bytes 786440 | tf_op jit(solution)/shard_map/y2/ppermute | solution.py:241
  23.4 25.7 %collective-permute-start.8 = (bf16[8,256,128]{2,1,0:T(8,128)(2,1)S(1)}, bf16[8,256,128]{2,1,0:T(8,128)(2,1)S(1)}, u32[]{:S(2)}, u32[]{:S(2)}) collective-permute-start(bf16[8,256,128]{2,1,0:T(8,128)(2,1)S(1)} %get-tuple-element.51), channel_id=1, source_target_pairs={{0,1},{1,0},{2,3},{3,2},{4,5},{5,4},{6,7},{7,6},{8,9},{9,8},{10,11... | collective-permute-start | bytes 1572872 | tf_op jit(solution)/shard_map/beside1/ppermute | solution.py:241
  23.5 12.2 %collective-permute-start.5 = (bf16[4,256,128]{2,1,0:T(8,128)(2,1)S(1)}, bf16[4,256,128]{2,1,0:T(8,128)(2,1)S(1)}, u32[]{:S(2)}, u32[]{:S(2)}) collective-permute-start(bf16[4,256,128]{2,1,0:T(8,128)(2,1)S(1)} %get-tuple-element.48), channel_id=1, source_target_pairs={{0,3},{1,2},{2,1},{3,0},{4,7},{5,6},{6,5},{7,4},{8,11},{9,10},{10,... | collective-permute-start | bytes 786440 | tf_op jit(solution)/shard_map/y3/ppermute | solution.py:241
  25.9 62.9 %copy-start.1 = (s32[128]{0:T(128)S(1)}, s32[128]{0:T(128)}, u32[]{:S(2)}) copy-start(s32[128]{0:T(128)} %mirror_ref.1) | copy-start | bytes 1540
  25.9 15.1 %collective-permute-start.3 = (bf16[1,4,4,64,128]{4,3,2,1,0:T(8,128)(2,1)S(1)}, bf16[1,4,4,64,128]{4,3,2,1,0:T(8,128)(2,1)S(1)}, u32[]{:S(2)}, u32[]{:S(2)}) collective-permute-start(bf16[1,4,4,64,128]{4,3,2,1,0:T(8,128)(2,1)S(1)} %get-tuple-element.46.refs_5_), channel_id=1, source_target_pairs={{0,16},{4,20},{8,24},{12,28},{16,0},{20,4},{24,8},{28,12},{1,17},{... | collective-permute-start | bytes 786440 | tf_op jit(solution)/shard_map/z4c0/ppermute | solution.py:241
  28.6 13.4 %collective-permute-start.9 = (bf16[4,256,128]{2,1,0:T(8,128)(2,1)S(1)}, bf16[4,256,128]{2,1,0:T(8,128)(2,1)S(1)}, u32[]{:S(2)}, u32[]{:S(2)}) collective-permute-start(bf16[4,256,128]{2,1,0:T(8,128)(2,1)S(1)} %get-tuple-element.52), channel_id=1, source_target_pairs={{0,2},{1,3},{2,0},{3,1},{4,6},{5,7},{6,4},{7,5},{8,10},{9,11},{10,... | collective-permute-start | bytes 786440 | tf_op jit(solution)/shard_map/y4/ppermute | solution.py:241
  30.8 16.1 %collective-permute-start.10 = (bf16[4,256,128]{2,1,0:T(8,128)(2,1)S(1)}, bf16[4,256,128]{2,1,0:T(8,128)(2,1)S(1)}, u32[]{:S(2)}, u32[]{:S(2)}) collective-permute-start(bf16[4,256,128]{2,1,0:T(8,128)(2,1)S(1)} %get-tuple-element.53), channel_id=1, source_target_pairs={{0,3},{1,2},{2,1},{3,0},{4,7},{5,6},{6,5},{7,4},{8,11},{9,10},{10,... | collective-permute-start | bytes 786440 | tf_op jit(solution)/shard_map/y5/ppermute | solution.py:241
  35.7 21.8 %collective-permute-start.13 = (bf16[4,256,128]{2,1,0:T(8,128)(2,1)S(1)}, bf16[4,256,128]{2,1,0:T(8,128)(2,1)S(1)}, u32[]{:S(2)}, u32[]{:S(2)}) collective-permute-start(bf16[4,256,128]{2,1,0:T(8,128)(2,1)S(1)} %get-tuple-element.55), channel_id=1, source_target_pairs={{0,2},{1,3},{2,0},{3,1},{4,6},{5,7},{6,4},{7,5},{8,10},{9,11},{10,... | collective-permute-start | bytes 786440 | tf_op jit(solution)/shard_map/y6/ppermute | solution.py:241
  41.0 16.4 %collective-permute-start.7 = (bf16[1,4,4,64,128]{4,3,2,1,0:T(8,128)(2,1)S(1)}, bf16[1,4,4,64,128]{4,3,2,1,0:T(8,128)(2,1)S(1)}, u32[]{:S(2)}, u32[]{:S(2)}) collective-permute-start(bf16[1,4,4,64,128]{4,3,2,1,0:T(8,128)(2,1)S(1)} %get-tuple-element.49.refs_2_), channel_id=1, source_target_pairs={{0,16},{4,20},{8,24},{12,28},{16,0},{20,4},{24,8},{28,12},{1,17},{... | collective-permute-start | bytes 786440 | tf_op jit(solution)/shard_map/z4c1/ppermute | solution.py:241
  42.0 15.4 %collective-permute-start.6 = (bf16[2,2,4,64,128]{4,3,2,1,0:T(8,128)(2,1)S(1)}, bf16[2,2,4,64,128]{4,3,2,1,0:T(8,128)(2,1)S(1)}, u32[]{:S(2)}, u32[]{:S(2)}) collective-permute-start(bf16[2,2,4,64,128]{4,3,2,1,0:T(8,128)(2,1)S(1)} %merge.6.refs_5_), channel_id=1, source_target_pairs={{0,8},{4,12},{8,0},{12,4},{16,24},{20,28},{24,16},{28,20},{1,9},{5... | collective-permute-start | bytes 786440 | tf_op jit(solution)/shard_map/z2c0/ppermute | solution.py:241
  46.9 11.0 %collective-permute-start.14 = (bf16[4,256,128]{2,1,0:T(8,128)(2,1)S(1)}, bf16[4,256,128]{2,1,0:T(8,128)(2,1)S(1)}, u32[]{:S(2)}, u32[]{:S(2)}) collective-permute-start(bf16[4,256,128]{2,1,0:T(8,128)(2,1)S(1)} %get-tuple-element.56), channel_id=1, source_target_pairs={{0,3},{1,2},{2,1},{3,0},{4,7},{5,6},{6,5},{7,4},{8,11},{9,10},{10,... | collective-permute-start | bytes 786440 | tf_op jit(solution)/shard_map/y7/ppermute | solution.py:241
  50.6 16.0 %collective-permute-start.16 = (bf16[1,4,4,64,128]{4,3,2,1,0:T(8,128)(2,1)S(1)}, bf16[1,4,4,64,128]{4,3,2,1,0:T(8,128)(2,1)S(1)}, u32[]{:S(2)}, u32[]{:S(2)}) collective-permute-start(bf16[1,4,4,64,128]{4,3,2,1,0:T(8,128)(2,1)S(1)} %get-tuple-element.54.refs_2_), channel_id=1, source_target_pairs={{0,16},{4,20},{8,24},{12,28},{16,0},{20,4},{24,8},{28,12},{1,17},{... | collective-permute-start | bytes 786440 | tf_op jit(solution)/shard_map/z4c2/ppermute | solution.py:241
  59.3 9.2 %collective-permute-start.15 = (bf16[1,4,4,64,128]{4,3,2,1,0:T(8,128)(2,1)S(1)}, bf16[1,4,4,64,128]{4,3,2,1,0:T(8,128)(2,1)S(1)}, u32[]{:S(2)}, u32[]{:S(2)}) collective-permute-start(bf16[1,4,4,64,128]{4,3,2,1,0:T(8,128)(2,1)S(1)} %get-tuple-element.58.refs_2_), channel_id=1, source_target_pairs={{0,4},{4,0},{8,12},{12,8},{16,20},{20,16},{24,28},{28,24},{1,5},{5... | collective-permute-start | bytes 786440 | tf_op jit(solution)/shard_map/z1c3/ppermute | solution.py:241
  61.2 12.1 %collective-permute-start.12 = (bf16[2,2,4,64,128]{4,3,2,1,0:T(8,128)(2,1)S(1)}, bf16[2,2,4,64,128]{4,3,2,1,0:T(8,128)(2,1)S(1)}, u32[]{:S(2)}, u32[]{:S(2)}) collective-permute-start(bf16[2,2,4,64,128]{4,3,2,1,0:T(8,128)(2,1)S(1)} %merge.7.refs_3_), channel_id=1, source_target_pairs={{0,8},{4,12},{8,0},{12,4},{16,24},{20,28},{24,16},{28,20},{1,9},{5... | collective-permute-start | bytes 786440 | tf_op jit(solution)/shard_map/z2c1/ppermute | solution.py:241
  62.7 11.1 %collective-permute-start.11 = (bf16[4,1,4,64,128]{4,3,2,1,0:T(8,128)(2,1)S(1)}, bf16[4,1,4,64,128]{4,3,2,1,0:T(8,128)(2,1)S(1)}, u32[]{:S(2)}, u32[]{:S(2)}) collective-permute-start(bf16[4,1,4,64,128]{4,3,2,1,0:T(8,128)(2,1)S(1)} %merge.8.refs_5_), channel_id=1, source_target_pairs={{0,4},{4,0},{8,12},{12,8},{16,20},{20,16},{24,28},{28,24},{1,5},{5... | collective-permute-start | bytes 786440 | tf_op jit(solution)/shard_map/z1c0/ppermute | solution.py:241
  68.6 12.9 %collective-permute-start.22 = (bf16[2,1,4,64,128]{4,3,2,1,0:T(8,128)(2,1)S(1)}, bf16[2,1,4,64,128]{4,3,2,1,0:T(8,128)(2,1)S(1)}, u32[]{:S(2)}, u32[]{:S(2)}) collective-permute-start(bf16[2,1,4,64,128]{4,3,2,1,0:T(8,128)(2,1)S(1)} %get-tuple-element.67), channel_id=1, source_target_pairs={{0,16},{4,20},{8,24},{12,28},{16,0},{20,4},{24,8},{28,12},{1,17},{... | collective-permute-start | bytes 393224 | tf_op jit(solution)/shard_map/z4c3/ppermute | solution.py:241
  71.4 10.0 %collective-permute-start.21 = (bf16[2,1,4,64,128]{4,3,2,1,0:T(8,128)(2,1)S(1)}, bf16[2,1,4,64,128]{4,3,2,1,0:T(8,128)(2,1)S(1)}, u32[]{:S(2)}, u32[]{:S(2)}) collective-permute-start(bf16[2,1,4,64,128]{4,3,2,1,0:T(8,128)(2,1)S(1)} %get-tuple-element.63.refs_3_), channel_id=1, source_target_pairs={{0,24},{4,28},{8,16},{12,20},{16,8},{20,12},{24,0},{28,4},{1,25},{... | collective-permute-start | bytes 393224 | tf_op jit(solution)/shard_map/z6c3/ppermute | solution.py:241
  73.9 14.9 %collective-permute-start.17 = (bf16[4,1,4,64,128]{4,3,2,1,0:T(8,128)(2,1)S(1)}, bf16[4,1,4,64,128]{4,3,2,1,0:T(8,128)(2,1)S(1)}, u32[]{:S(2)}, u32[]{:S(2)}) collective-permute-start(bf16[4,1,4,64,128]{4,3,2,1,0:T(8,128)(2,1)S(1)} %merge.11.refs_1_), channel_id=1, source_target_pairs={{0,4},{4,0},{8,12},{12,8},{16,20},{20,16},{24,28},{28,24},{1,5},{5... | collective-permute-start | bytes 786440 | tf_op jit(solution)/shard_map/z1c1/ppermute | solution.py:241
  75.4 10.7 %collective-permute-start.18 = (bf16[2,1,4,64,128]{4,3,2,1,0:T(8,128)(2,1)S(1)}, bf16[2,1,4,64,128]{4,3,2,1,0:T(8,128)(2,1)S(1)}, u32[]{:S(2)}, u32[]{:S(2)}) collective-permute-start(bf16[2,1,4,64,128]{4,3,2,1,0:T(8,128)(2,1)S(1)} %get-tuple-element.64), channel_id=1, source_target_pairs={{0,12},{4,8},{8,4},{12,0},{16,28},{20,24},{24,20},{28,16},{1,13},{... | collective-permute-start | bytes 393224 | tf_op jit(solution)/shard_map/z3c2/ppermute | solution.py:241
  77.2 8.9 %collective-permute-start.23 = (bf16[2,1,4,64,128]{4,3,2,1,0:T(8,128)(2,1)S(1)}, bf16[2,1,4,64,128]{4,3,2,1,0:T(8,128)(2,1)S(1)}, u32[]{:S(2)}, u32[]{:S(2)}) collective-permute-start(bf16[2,1,4,64,128]{4,3,2,1,0:T(8,128)(2,1)S(1)} %get-tuple-element.68), channel_id=1, source_target_pairs={{0,8},{4,12},{8,0},{12,4},{16,24},{20,28},{24,16},{28,20},{1,9},{5... | collective-permute-start | bytes 393224 | tf_op jit(solution)/shard_map/z2c3/ppermute | solution.py:241
  81.5 7.3 %collective-permute-start.19 = (bf16[2,1,4,64,128]{4,3,2,1,0:T(8,128)(2,1)S(1)}, bf16[2,1,4,64,128]{4,3,2,1,0:T(8,128)(2,1)S(1)}, u32[]{:S(2)}, u32[]{:S(2)}) collective-permute-start(bf16[2,1,4,64,128]{4,3,2,1,0:T(8,128)(2,1)S(1)} %get-tuple-element.65), channel_id=1, source_target_pairs={{0,8},{4,12},{8,0},{12,4},{16,24},{20,28},{24,16},{28,20},{1,9},{5... | collective-permute-start | bytes 393224 | tf_op jit(solution)/shard_map/z2c2/ppermute | solution.py:241
  81.5 7.3 %collective-permute-start.20 = (bf16[2,1,4,64,128]{4,3,2,1,0:T(8,128)(2,1)S(1)}, bf16[2,1,4,64,128]{4,3,2,1,0:T(8,128)(2,1)S(1)}, u32[]{:S(2)}, u32[]{:S(2)}) collective-permute-start(bf16[2,1,4,64,128]{4,3,2,1,0:T(8,128)(2,1)S(1)} %get-tuple-element.66), channel_id=1, source_target_pairs={{0,4},{4,0},{8,12},{12,8},{16,20},{20,16},{24,28},{28,24},{1,5},{5... | collective-permute-start | bytes 393224 | tf_op jit(solution)/shard_map/z1c2/ppermute | solution.py:241

commit v13 on v10

--- a/solution.py
+++ b/solution.py
@@ -9,7 +9,7 @@
 
 LANES = 128
 STEP = 64
-BATCHES = ((4, 4), (5, 3))
+BATCHES = ((4, 4), (4, 4))
 CHUNKS = sum(BATCHES, ())
 SIZES = ((1,), (1,), (1, 2), (-1, 2))
 PART = 256
@@ -21,82 +21,70 @@
 IN_HBM = pl.BlockSpec(memory_space=pltpu.MemorySpace.HBM)
 
 
-def quarter_kernel(rows, n_mo, blocks, n_after, place_ref, x_ref, c_ref, *refs):
-    refs = refs[n_after:]
-    outs, (turn_ref, held, sems) = refs[:-3], refs[-3:]
-    at = pl.program_id(0)
-    step, some, depth = x_ref.shape
-    padded = held.shape[2]
+def quarter_kernel(batch, n_mo, blocks, n_after, place_ref, x_hbm, c_hbm, *refs):
+    outs, (x_ref, c_ref, turn_ref, x_sems, c_sem) = refs[n_after:-5], refs[-5:]
+    rows, depth = x_hbm.shape[0], x_hbm.shape[2]
+    padded, some, _ = x_ref.shape
     many = PART // some
 
-    @pl.when(at == 0)
-    def _():
-        to = lax.broadcasted_iota(jnp.int32, (PART, PART), 0)
-        source = lax.broadcasted_iota(jnp.int32, (PART, PART), 1)
-        bits = many.bit_length() - 1
-        is_source = source == (to & (many - 1)) * some + (to >> bits)
-        turn_ref[...] = jnp.where(is_source, 1.0, 0.0).astype(jnp.bfloat16)
-
-    def fill(limit):
-        x = x_ref[...].reshape(step * some, depth)
-        product = jnp.dot(x, c_ref[...], preferred_element_type=jnp.float32)
-        if limit is not None:
-            line = lax.broadcasted_iota(jnp.int32, product.shape, 0)
-            product = jnp.where(line < limit * some, product, 0.0)
-        product = product.astype(jnp.bfloat16)
-        for part in range(step // many):
+    columns = []
+    for o in range(n_mo):
+        mine = pl.ds(pl.multiple_of((place_ref[0] ^ o) * LANES, LANES), LANES)
+        columns.append(pltpu.make_async_copy(c_hbm.at[:, mine], c_ref.at[:, o * LANES : (o + 1) * LANES], c_sem.at[o]))
+    parts = []
+    for n, first in enumerate(range(0, padded, STEP)):
+        lines = pl.ds(first, min(STEP, rows - first))
+        source = x_hbm.at[lines, pl.ds(batch * some, some)]
+        parts.append(pltpu.make_async_copy(source, x_ref.at[lines], x_sems.at[n]))
+    for copy in parts[:1] + columns + parts[1:]:
+        copy.start()
+    x_ref[rows:] = jnp.zeros((padded - rows, some, depth), jnp.bfloat16)
+    to = lax.broadcasted_iota(jnp.int32, (PART, PART), 0)
+    source = lax.broadcasted_iota(jnp.int32, (PART, PART), 1)
+    is_source = source == (to & (many - 1)) * some + (to >> (many.bit_length() - 1))
+    turn_ref[...] = jnp.where(is_source, 1.0, 0.0).astype(jnp.bfloat16)
+    for copy in columns:
+        copy.wait()
+    for n, first in enumerate(range(0, padded, STEP)):
+        parts[n].wait()
+        x = x_ref[first : first + STEP].reshape(STEP * some, depth)
+        product = jnp.dot(x, c_ref[...], preferred_element_type=jnp.float32).astype(jnp.bfloat16)
+        for part in range(STEP // many):
             lines = jnp.dot(
                 turn_ref[...], product[part * PART : (part + 1) * PART], preferred_element_type=jnp.float32
             ).astype(jnp.bfloat16)
-            here = pl.ds(pl.multiple_of(at * step + part * many, many), many)
-            for k in range(some):
-                for d in range(n_mo):
-                    held[d, k, here] = lines[k * many : (k + 1) * many, d * LANES : (d + 1) * LANES]
-
-    steps = padded // step
-    pl.when(at < steps - 1)(lambda: fill(None))
-    pl.when(at == steps - 1)(lambda: fill(rows - (steps - 1) * step))
-    here = pl.ds(pl.multiple_of(at * step, step), step)
-    for n, (out, (o, first)) in enumerate(zip(outs, blocks)):
-        mine = held.at[place_ref[0] ^ o, pl.ds(first, out.shape[0])]
-        pltpu.make_async_copy(mine.at[:, here], out.at[:, here], sems.at[n]).start()
-
-    @pl.when(at == padded // step - 1)
-    def _():
-        for n, (out, (o, first)) in enumerate(zip(outs, blocks)):
-            mine = held.at[place_ref[0] ^ o, pl.ds(first, out.shape[0])]
-            pltpu.make_async_copy(mine, out, sems.at[n]).wait()
+            at = first + part * many
+            for out, (o, k) in zip(outs, blocks):
+                for row in range(out.shape[0]):
+                    line = (k + row) * many
+                    out[row, at : at + many] = lines[line : line + many, o * LANES : (o + 1) * LANES]
 
 
 def quarter_of(place, by_r, coeffs, n_mo, padded, batch, after):
-    rows, _, depth = by_r.shape
-    orbitals = coeffs.shape[1]
+    depth, orbitals = coeffs.shape
     chunks = BATCHES[batch]
     some = sum(chunks)
     blocks = [(0, 0), (1, 0)] + [(o, sum(chunks[:c])) for c in range(len(chunks)) for o in range(2, n_mo)]
     sizes = [some] * 2 + [kc for kc in chunks for _ in range(2, n_mo)]
     outs = [jax.ShapeDtypeStruct((kc, padded, LANES), jnp.bfloat16) for kc in sizes]
     out = pl.pallas_call(
-        functools.partial(quarter_kernel, rows, n_mo, blocks, len(after)),
-        grid_spec=pltpu.PrefetchScalarGridSpec(
-            num_scalar_prefetch=1,
-            grid=(padded // STEP,),
-            in_specs=[pl.BlockSpec((STEP, some, depth), lambda r, place: (r, batch, 0)), IN_VMEM]
-            + [ANYWHERE] * len(after),
-            out_specs=[IN_HBM] * len(outs),
-            scratch_shapes=[
-                pltpu.VMEM((PART, PART), jnp.bfloat16),
-                pltpu.VMEM((n_mo, some, padded, LANES), jnp.bfloat16),
-                pltpu.SemaphoreType.DMA((len(outs),)),
-            ],
-        ),
+        functools.partial(quarter_kernel, batch, n_mo, blocks, len(after)),
+        in_specs=[IN_SMEM] + [IN_HBM] * 2 + [ANYWHERE] * len(after),
+        out_specs=[IN_VMEM] * len(outs),
         out_shape=outs,
-        compiler_params=pltpu.CompilerParams(vmem_limit_bytes=50 * MIB),
+        scratch_shapes=[
+            pltpu.VMEM((padded, some, depth), jnp.bfloat16),
+            pltpu.VMEM((depth, orbitals), jnp.bfloat16),
+            pltpu.VMEM((PART, PART), jnp.bfloat16),
+            pltpu.SemaphoreType.DMA((padded // STEP,)),
+            pltpu.SemaphoreType.DMA((n_mo,)),
+        ],
+        compiler_params=pltpu.CompilerParams(vmem_limit_bytes=51 * MIB),
         cost_estimate=COST,
         name="quarter",
     )(place, by_r, coeffs, *after)
     far = n_mo - 2
-    return out[:2], [out[2 + far * c : 2 + far * (c + 1)] for c in range(len(chunks))]
+    return out[:2], [list(out[2 + far * c : 2 + far * (c + 1)]) for c in range(len(chunks))]
 
 
 def turn_kernel(rows, c_ref, *refs):

time: 91.8 us -> 89.8 us (0.978)
  local copies, waits for them, and re-layouts: 1.23 us -> 0.02 us
    unnamed x5, local copies, waits for them, and re-layouts: 1.23 us -> 0.02 us
  transfers between devices with their start and end apart: 24 -> 24, of which waited for: 10 -> 15; matrix products, arithmetic and copies ran while one was open for 0% -> 0% of each run, Pallas kernels for 14% -> 14%
where the time goes in v13:
time: 89.8 us; the launch traced here: 89.7 us
  waiting for transfers between devices  33.7 us (38%)
  starting transfers between devices  33.2 us (37%)
  Pallas kernels  22.5 us (25%)
    ppermute x24, waiting for transfers between devices, flipped(): return lax.ppermute(x, axis, [(i, i ^ offset) for i in range(size)])  33.7 us
    ppermute x24, starting transfers between devices, flipped(): return lax.ppermute(x, axis, [(i, i ^ offset) for i in range(size)])  33.2 us
    pallas_call x2, Pallas kernels, quarter_of(): pl.pallas_call(functools.partial(quarter_kernel, batch, n_mo, blocks, len...  13.5 us
    pallas_call x4, Pallas kernels, half_of(): pl.pallas_call(functools.partial(half_kernel, n_mo, first, owners), in_sp...  5.21 us
    pallas_call x1, Pallas kernels, combine(): pl.pallas_call(functools.partial(combine_kernel, sources, k_all, per_step...  3.29 us
  transfers between devices with their start and end apart: 24, of which 15 were waited for; matrix products, arithmetic and copies ran while one was open for 0% of the time, Pallas kernels for 14%

profile of v13, /device:TPU:0, one launch (start us, length us, event | category | flops | bytes accessed | tf_op | source)
XLA Modules:
  0.0 89.7 jit_solution(8111054889482856008)
XLA Ops:
  0.0 0.1 pad_add_fusion.place_ref
  0.1 6.7 %quarter.2 = (bf16[8,256,128]{2,1,0:T(8,128)(2,1)S(1)}, bf16[8,256,128]{2,1,0:T(8,128)(2,1)S(1)}, bf16[4,256,128]{2,1,0:T(8,128)(2,1)S(1)}, bf16[4,256,128]{2,1,...) custom-call(s32[2]{0:T(128)S(1)} %pad_add_fusion.place_ref, ...), custom_call_target="tpu_custom_call" | custom-call | flops 1024 | bytes 1024 | tf_op jit(solution)/shard_map/quarter/pallas_call | solution.py:70
  6.8 0.5 collective-permute-start
  7.3 2.6 %collective-permute-start.1 = (bf16[4,256,128]{2,1,0:T(8,128)(2,1)S(1)}, bf16[4,256,128]{2,1,0:T(8,128)(2,1)S(1)}, u32[]{:S(2)}, u32[]{:S(2)}) collective-permute-start(bf16[4,256,128]{2,1,0:T(8,128)(2,1)S(1)} %get-tuple-element.39), channel_id=1, source_target_pairs={{0,2},{1,3},{2,0},{3,1},{4,6},{5,7},{6,4},{7,5},{8,10},{9,11},{10,... | collective-permute-start | bytes 786440 | tf_op jit(solution)/shard_map/y0/ppermute | solution.py:230
  9.9 0.1 collective-permute-start.2
  10.0 6.7 %quarter.3 = (bf16[8,256,128]{2,1,0:T(8,128)(2,1)S(1)}, bf16[8,256,128]{2,1,0:T(8,128)(2,1)S(1)}, bf16[4,256,128]{2,1,0:T(8,128)(2,1)S(1)}, bf16[4,256,128]{2,1,...) custom-call(s32[2]{0:T(128)S(1)} %pad_add_fusion.place_ref, ...), custom_call_target="tpu_custom_call" | custom-call | flops 1024 | bytes 1024 | tf_op jit(solution)/shard_map/quarter/pallas_call | solution.py:70
  16.7 0.3 collective-permute-done.1.refs_2_
  17.1 0.4 turn.1
  17.5 2.0 %collective-permute-start.4 = (bf16[4,256,128]{2,1,0:T(8,128)(2,1)S(1)}, bf16[4,256,128]{2,1,0:T(8,128)(2,1)S(1)}, u32[]{:S(2)}, u32[]{:S(2)}) collective-permute-start(bf16[4,256,128]{2,1,0:T(8,128)(2,1)S(1)} %get-tuple-element.47), channel_id=1, source_target_pairs={{0,2},{1,3},{2,0},{3,1},{4,6},{5,7},{6,4},{7,5},{8,10},{9,11},{10,... | collective-permute-start | bytes 786440 | tf_op jit(solution)/shard_map/y2/ppermute | solution.py:230
  19.5 0.2 collective-permute-start.5
  19.7 2.5 %collective-permute-done.2.refs_3_ = bf16[4,256,128]{2,1,0:T(8,128)(2,1)S(1)} collective-permute-done((bf16[4,256,128]{2,1,0:T(8,128)(2,1)S(1)}, bf16[4,256,128]{2,1,0:T(8,128)(2,1)S(1)}, u32[]{:S(2)}, u32[]{:S(2)}) %collective-permute-start.2) | collective-permute-done | bytes 262176 | tf_op jit(solution)/shard_map/y1/ppermute | solution.py:230
  22.2 0.0 collective-permute-done.refs_1_
  22.2 1.3 %half.4 = (bf16[1,4,4,64,128]{4,3,2,1,0:T(8,128)(2,1)S(1)}, bf16[1,4,4,64,128]{4,3,2,1,0:T(8,128)(2,1)S(1)}) custom-call(s32[2]{0:T(128)S(1)} %pad_add_fusion.place_ref, bf16[8,256,128]{2,1,0:T(8,128)(2,1)S(1)} %get-tuple-element.37.refs_0_, bf16[8,256,128]{2,1,0:T(8,128)(2,1)S(1)} %collective-permute-done.refs_1_, ...), custom_call_target="tpu_custom_call" | custom-call | flops 1024 | bytes 1024 | tf_op jit(solution)/shard_map/half/pallas_call | solution.py:136
  23.5 0.0 copy-start.1
  23.5 2.7 %collective-permute-start.3 = (bf16[1,4,4,64,128]{4,3,2,1,0:T(8,128)(2,1)S(1)}, bf16[1,4,4,64,128]{4,3,2,1,0:T(8,128)(2,1)S(1)}, u32[]{:S(2)}, u32[]{:S(2)}) collective-permute-start(bf16[1,4,4,64,128]{4,3,2,1,0:T(8,128)(2,1)S(1)} %get-tuple-element.46.refs_5_), channel_id=1, source_target_pairs={{0,16},{4,20},{8,24},{12,28},{16,0},{20,4},{24,8},{28,12},{1,17},{... | collective-permute-start | bytes 786440 | tf_op jit(solution)/shard_map/z4c0/ppermute | solution.py:230
  26.2 1.5 %collective-permute-start.9 = (bf16[4,256,128]{2,1,0:T(8,128)(2,1)S(1)}, bf16[4,256,128]{2,1,0:T(8,128)(2,1)S(1)}, u32[]{:S(2)}, u32[]{:S(2)}) collective-permute-start(bf16[4,256,128]{2,1,0:T(8,128)(2,1)S(1)} %get-tuple-element.52), channel_id=1, source_target_pairs={{0,2},{1,3},{2,0},{3,1},{4,6},{5,7},{6,4},{7,5},{8,10},{9,11},{10,... | collective-permute-start | bytes 786440 | tf_op jit(solution)/shard_map/y4/ppermute | solution.py:230
  27.7 0.6 collective-permute-done.4.refs_2_
  28.3 0.8 collective-permute-start.10
  29.1 4.3 %collective-permute-done.5.refs_3_ = bf16[4,256,128]{2,1,0:T(8,128)(2,1)S(1)} collective-permute-done((bf16[4,256,128]{2,1,0:T(8,128)(2,1)S(1)}, bf16[4,256,128]{2,1,0:T(8,128)(2,1)S(1)}, u32[]{:S(2)}, u32[]{:S(2)}) %collective-permute-start.5) | collective-permute-done | bytes 262176 | tf_op jit(solution)/shard_map/y3/ppermute | solution.py:230
  33.4 1.6 %collective-permute-start.13 = (bf16[4,256,128]{2,1,0:T(8,128)(2,1)S(1)}, bf16[4,256,128]{2,1,0:T(8,128)(2,1)S(1)}, u32[]{:S(2)}, u32[]{:S(2)}) collective-permute-start(bf16[4,256,128]{2,1,0:T(8,128)(2,1)S(1)} %get-tuple-element.55), channel_id=1, source_target_pairs={{0,2},{1,3},{2,0},{3,1},{4,6},{5,7},{6,4},{7,5},{8,10},{9,11},{10,... | collective-permute-start | bytes 786440 | tf_op jit(solution)/shard_map/y6/ppermute | solution.py:230
  35.0 1.3 %half.5 = (bf16[1,4,4,64,128]{4,3,2,1,0:T(8,128)(2,1)S(1)}, bf16[1,4,4,64,128]{4,3,2,1,0:T(8,128)(2,1)S(1)}) custom-call(s32[2]{0:T(128)S(1)} %pad_add_fusion.place_ref, bf16[8,256,128]{2,1,0:T(8,128)(2,1)S(1)} %get-tuple-element.37.refs_0_, bf16[8,256,128]{2,1,0:T(8,128)(2,1)S(1)} %collective-permute-done.refs_1_, ...), custom_call_target="tpu_custom_call" | custom-call | flops 1024 | bytes 1024 | tf_op jit(solution)/shard_map/half/pallas_call | solution.py:136
  36.3 2.7 %collective-permute-done.3.refs_1_ = bf16[1,4,4,64,128]{4,3,2,1,0:T(8,128)(2,1)S(1)} collective-permute-done((bf16[1,4,4,64,128]{4,3,2,1,0:T(8,128)(2,1)S(1)}, bf16[1,4,4,64,128]{4,3,2,1,0:T(8,128)(2,1)S(1)}, u32[]{:S(2)}, u32[]{:S(2)}) %collective-permute-start.3) | collective-permute-done | bytes 262176 | tf_op jit(solution)/shard_map/z4c0/ppermute | solution.py:230
  39.0 0.5 collective-permute-done.9.refs_2_
  39.6 3.7 %collective-permute-start.6 = (bf16[2,2,4,64,128]{4,3,2,1,0:T(8,128)(2,1)S(1)}, bf16[2,2,4,64,128]{4,3,2,1,0:T(8,128)(2,1)S(1)}, u32[]{:S(2)}, u32[]{:S(2)}) collective-permute-start(bf16[2,2,4,64,128]{4,3,2,1,0:T(8,128)(2,1)S(1)} %merge.6.refs_5_), channel_id=1, source_target_pairs={{0,8},{4,12},{8,0},{12,4},{16,24},{20,28},{24,16},{28,20},{1,9},{5... | collective-permute-start | bytes 786440 | tf_op jit(solution)/shard_map/z2c0/ppermute | solution.py:230
  43.2 1.4 %collective-permute-done.10.refs_3_ = bf16[4,256,128]{2,1,0:T(8,128)(2,1)S(1)} collective-permute-done((bf16[4,256,128]{2,1,0:T(8,128)(2,1)S(1)}, bf16[4,256,128]{2,1,0:T(8,128)(2,1)S(1)}, u32[]{:S(2)}, u32[]{:S(2)}) %collective-permute-start.10) | collective-permute-done | bytes 262176 | tf_op jit(solution)/shard_map/y5/ppermute | solution.py:230
  44.6 2.2 %collective-permute-start.14 = (bf16[4,256,128]{2,1,0:T(8,128)(2,1)S(1)}, bf16[4,256,128]{2,1,0:T(8,128)(2,1)S(1)}, u32[]{:S(2)}, u32[]{:S(2)}) collective-permute-start(bf16[4,256,128]{2,1,0:T(8,128)(2,1)S(1)} %get-tuple-element.56), channel_id=1, source_target_pairs={{0,3},{1,2},{2,1},{3,0},{4,7},{5,6},{6,5},{7,4},{8,11},{9,10},{10,... | collective-permute-start | bytes 786440 | tf_op jit(solution)/shard_map/y7/ppermute | solution.py:230
  46.8 0.0 collective-permute-done.8.refs_1_
  46.8 1.3 %half.6 = (bf16[1,4,4,64,128]{4,3,2,1,0:T(8,128)(2,1)S(1)}, bf16[1,4,4,64,128]{4,3,2,1,0:T(8,128)(2,1)S(1)}) custom-call(s32[2]{0:T(128)S(1)} %pad_add_fusion.place_ref, bf16[8,256,128]{2,1,0:T(8,128)(2,1)S(1)} %get-tuple-element.43.refs_3_.refs_0_, bf16[8,256,128]{2,1,0:T(8,128)(2,1)S(1)} %collective-permute-done.8.refs_1_, ...), custom_call_target="tpu_custom_call" | custom-call | flops 1024 | bytes 1024 | tf_op jit(solution)/shard_map/half/pallas_call | solution.py:136
  48.2 2.7 %collective-permute-start.16 = (bf16[1,4,4,64,128]{4,3,2,1,0:T(8,128)(2,1)S(1)}, bf16[1,4,4,64,128]{4,3,2,1,0:T(8,128)(2,1)S(1)}, u32[]{:S(2)}, u32[]{:S(2)}) collective-permute-start(bf16[1,4,4,64,128]{4,3,2,1,0:T(8,128)(2,1)S(1)} %get-tuple-element.54.refs_2_), channel_id=1, source_target_pairs={{0,16},{4,20},{8,24},{12,28},{16,0},{20,4},{24,8},{28,12},{1,17},{... | collective-permute-start | bytes 786440 | tf_op jit(solution)/shard_map/z4c2/ppermute | solution.py:230
  50.8 4.5 %collective-permute-done.7.refs_1_.refs_5_ = bf16[1,4,4,64,128]{4,3,2,1,0:T(8,128)(2,1)S(1)} collective-permute-done((bf16[1,4,4,64,128]{4,3,2,1,0:T(8,128)(2,1)S(1)}, bf16[1,4,4,64,128]{4,3,2,1,0:T(8,128)(2,1)S(1)}, u32[]{:S(2)}, u32[]{:S(2)}) %collective-permute-start.7) | collective-permute-done | bytes 262176 | tf_op jit(solution)/shard_map/z4c1/ppermute | solution.py:230
  55.4 0.5 collective-permute-done.14.refs_3_
  55.9 1.3 %half.7 = (bf16[1,4,4,64,128]{4,3,2,1,0:T(8,128)(2,1)S(1)}, bf16[1,4,4,64,128]{4,3,2,1,0:T(8,128)(2,1)S(1)}) custom-call(s32[2]{0:T(128)S(1)} %pad_add_fusion.place_ref, bf16[8,256,128]{2,1,0:T(8,128)(2,1)S(1)} %get-tuple-element.43.refs_3_.refs_0_, bf16[8,256,128]{2,1,0:T(8,128)(2,1)S(1)} %collective-permute-done.8.refs_1_, ...), custom_call_target="tpu_custom_call" | custom-call | flops 1024 | bytes 1024 | tf_op jit(solution)/shard_map/half/pallas_call | solution.py:136
  57.2 1.6 %collective-permute-start.15 = (bf16[1,4,4,64,128]{4,3,2,1,0:T(8,128)(2,1)S(1)}, bf16[1,4,4,64,128]{4,3,2,1,0:T(8,128)(2,1)S(1)}, u32[]{:S(2)}, u32[]{:S(2)}) collective-permute-start(bf16[1,4,4,64,128]{4,3,2,1,0:T(8,128)(2,1)S(1)} %get-tuple-element.58.refs_2_), channel_id=1, source_target_pairs={{0,4},{4,0},{8,12},{12,8},{16,20},{20,16},{24,28},{28,24},{1,5},{5... | collective-permute-start | bytes 786440 | tf_op jit(solution)/shard_map/z1c3/ppermute | solution.py:230
  58.8 1.6 %collective-permute-start.12 = (bf16[2,2,4,64,128]{4,3,2,1,0:T(8,128)(2,1)S(1)}, bf16[2,2,4,64,128]{4,3,2,1,0:T(8,128)(2,1)S(1)}, u32[]{:S(2)}, u32[]{:S(2)}) collective-permute-start(bf16[2,2,4,64,128]{4,3,2,1,0:T(8,128)(2,1)S(1)} %merge.7.refs_3_), channel_id=1, source_target_pairs={{0,8},{4,12},{8,0},{12,4},{16,24},{20,28},{24,16},{28,20},{1,9},{5... | collective-permute-start | bytes 786440 | tf_op jit(solution)/shard_map/z2c1/ppermute | solution.py:230
  60.4 0.5 collective-permute-start.11
  60.9 4.1 %collective-permute-done.16.refs_1_.refs_9_ = bf16[1,4,4,64,128]{4,3,2,1,0:T(8,128)(2,1)S(1)} collective-permute-done((bf16[1,4,4,64,128]{4,3,2,1,0:T(8,128)(2,1)S(1)}, bf16[1,4,4,64,128]{4,3,2,1,0:T(8,128)(2,1)S(1)}, u32[]{:S(2)}, u32[]{:S(2)}) %collective-permute-start.16) | collective-permute-done | bytes 262176 | tf_op jit(solution)/shard_map/z4c2/ppermute | solution.py:230
  65.0 1.4 %collective-permute-done.15.refs_1_.refs_14_ = bf16[1,4,4,64,128]{4,3,2,1,0:T(8,128)(2,1)S(1)} collective-permute-done((bf16[1,4,4,64,128]{4,3,2,1,0:T(8,128)(2,1)S(1)}, bf16[1,4,4,64,128]{4,3,2,1,0:T(8,128)(2,1)S(1)}, u32[]{:S(2)}, u32[]{:S(2)}) %collective-permute-start.15) | collective-permute-done | bytes 262176 | tf_op jit(solution)/shard_map/z1c3/ppermute | solution.py:230
  66.4 2.6 %collective-permute-start.22 = (bf16[2,1,4,64,128]{4,3,2,1,0:T(8,128)(2,1)S(1)}, bf16[2,1,4,64,128]{4,3,2,1,0:T(8,128)(2,1)S(1)}, u32[]{:S(2)}, u32[]{:S(2)}) collective-permute-start(bf16[2,1,4,64,128]{4,3,2,1,0:T(8,128)(2,1)S(1)} %get-tuple-element.67), channel_id=1, source_target_pairs={{0,16},{4,20},{8,24},{12,28},{16,0},{20,4},{24,8},{28,12},{1,17},{... | collective-permute-start | bytes 393224 | tf_op jit(solution)/shard_map/z4c3/ppermute | solution.py:230
  69.1 1.4 %collective-permute-start.21 = (bf16[2,1,4,64,128]{4,3,2,1,0:T(8,128)(2,1)S(1)}, bf16[2,1,4,64,128]{4,3,2,1,0:T(8,128)(2,1)S(1)}, u32[]{:S(2)}, u32[]{:S(2)}) collective-permute-start(bf16[2,1,4,64,128]{4,3,2,1,0:T(8,128)(2,1)S(1)} %get-tuple-element.63.refs_3_), channel_id=1, source_target_pairs={{0,24},{4,28},{8,16},{12,20},{16,8},{20,12},{24,0},{28,4},{1,25},{... | collective-permute-start | bytes 393224 | tf_op jit(solution)/shard_map/z6c3/ppermute | solution.py:230
  70.4 1.2 %collective-permute-done.12.refs_2_.refs_6_ = bf16[2,2,4,64,128]{4,3,2,1,0:T(8,128)(2,1)S(1)} collective-permute-done((bf16[2,2,4,64,128]{4,3,2,1,0:T(8,128)(2,1)S(1)}, bf16[2,2,4,64,128]{4,3,2,1,0:T(8,128)(2,1)S(1)}, u32[]{:S(2)}, u32[]{:S(2)}) %collective-permute-start.12) | collective-permute-done | bytes 262176 | tf_op jit(solution)/shard_map/z2c1/ppermute | solution.py:230
  71.7 1.6 %collective-permute-start.17 = (bf16[4,1,4,64,128]{4,3,2,1,0:T(8,128)(2,1)S(1)}, bf16[4,1,4,64,128]{4,3,2,1,0:T(8,128)(2,1)S(1)}, u32[]{:S(2)}, u32[]{:S(2)}) collective-permute-start(bf16[4,1,4,64,128]{4,3,2,1,0:T(8,128)(2,1)S(1)} %merge.11.refs_1_), channel_id=1, source_target_pairs={{0,4},{4,0},{8,12},{12,8},{16,20},{20,16},{24,28},{28,24},{1,5},{5... | collective-permute-start | bytes 786440 | tf_op jit(solution)/shard_map/z1c1/ppermute | solution.py:230
  73.3 1.5 %collective-permute-start.18 = (bf16[2,1,4,64,128]{4,3,2,1,0:T(8,128)(2,1)S(1)}, bf16[2,1,4,64,128]{4,3,2,1,0:T(8,128)(2,1)S(1)}, u32[]{:S(2)}, u32[]{:S(2)}) collective-permute-start(bf16[2,1,4,64,128]{4,3,2,1,0:T(8,128)(2,1)S(1)} %get-tuple-element.64), channel_id=1, source_target_pairs={{0,12},{4,8},{8,4},{12,0},{16,28},{20,24},{24,20},{28,16},{1,13},{... | collective-permute-start | bytes 393224 | tf_op jit(solution)/shard_map/z3c2/ppermute | solution.py:230
  74.8 0.4 collective-permute-start.23
  75.2 3.9 %collective-permute-done.22.refs_0_.refs_16_ = bf16[2,1,4,64,128]{4,3,2,1,0:T(8,128)(2,1)S(1)} collective-permute-done((bf16[2,1,4,64,128]{4,3,2,1,0:T(8,128)(2,1)S(1)}, bf16[2,1,4,64,128]{4,3,2,1,0:T(8,128)(2,1)S(1)}, u32[]{:S(2)}, u32[]{:S(2)}) %collective-permute-start.22) | collective-permute-done | bytes 131104 | tf_op jit(solution)/shard_map/z4c3/ppermute | solution.py:230
  79.1 1.5 %collective-permute-start.20 = (bf16[2,1,4,64,128]{4,3,2,1,0:T(8,128)(2,1)S(1)}, bf16[2,1,4,64,128]{4,3,2,1,0:T(8,128)(2,1)S(1)}, u32[]{:S(2)}, u32[]{:S(2)}) collective-permute-start(bf16[2,1,4,64,128]{4,3,2,1,0:T(8,128)(2,1)S(1)} %get-tuple-element.66), channel_id=1, source_target_pairs={{0,4},{4,0},{8,12},{12,8},{16,20},{20,16},{24,28},{28,24},{1,5},{5... | collective-permute-start | bytes 393224 | tf_op jit(solution)/shard_map/z1c2/ppermute | solution.py:230
  80.6 3.1 %collective-permute-done.23.refs_0_.refs_17_ = bf16[2,1,4,64,128]{4,3,2,1,0:T(8,128)(2,1)S(1)} collective-permute-done((bf16[2,1,4,64,128]{4,3,2,1,0:T(8,128)(2,1)S(1)}, bf16[2,1,4,64,128]{4,3,2,1,0:T(8,128)(2,1)S(1)}, u32[]{:S(2)}, u32[]{:S(2)}) %collective-permute-start.23) | collective-permute-done | bytes 131104 | tf_op jit(solution)/shard_map/z2c3/ppermute | solution.py:230
  83.7 2.7 %collective-permute-done.19.refs_11_ = bf16[2,1,4,64,128]{4,3,2,1,0:T(8,128)(2,1)S(1)} collective-permute-done((bf16[2,1,4,64,128]{4,3,2,1,0:T(8,128)(2,1)S(1)}, bf16[2,1,4,64,128]{4,3,2,1,0:T(8,128)(2,1)S(1)}, u32[]{:S(2)}, u32[]{:S(2)}) %collective-permute-start.19) | collective-permute-done | bytes 131104 | tf_op jit(solution)/shard_map/z2c2/ppermute | solution.py:230
  86.4 3.3 %combine.1 = f32[128,64,128]{2,1,0:T(8,128)} custom-call(s32[128]{0:T(128)S(1)} %copy-done.1, s32[2]{0:T(128)S(1)} %pad_add_fusion.place_ref, bf16[1,4,4,64,128]{4,3,2,1,0:T(8,128)(2,1)S(1)} %get-tuple-element.45.refs_0_, bf16[1,4,4,64,128]{4,3,2,1,0:T(8,128)(2,1)S(1)} %collective-permute-done.3.refs_1_, ...), custom_call_target="tpu_custom_call" | custom-call | flops 1024 | bytes 1024 | tf_op jit(solution)/shard_map/combine/pallas_call | solution.py:212
  (23 shorter events, 0.2 us)
Async XLA Ops:
  0.1 17.0 %copy-start = (bf16[1000,512]{1,0:T(8,128)(2,1)S(1)}, bf16[1000,512]{1,0:T(8,128)(2,1)}, u32[]{:S(2)}) copy-start(bf16[1000,512]{1,0:T(8,128)(2,1)} %c_ref.1) | copy-start | bytes 3072004
  6.8 15.4 %collective-permute-start = (bf16[8,256,128]{2,1,0:T(8,128)(2,1)S(1)}, bf16[8,256,128]{2,1,0:T(8,128)(2,1)S(1)}, u32[]{:S(2)}, u32[]{:S(2)}) collective-permute-start(bf16[8,256,128]{2,1,0:T(8,128)(2,1)S(1)} %get-tuple-element.38), channel_id=1, source_target_pairs={{0,1},{1,0},{2,3},{3,2},{4,5},{5,4},{6,7},{7,6},{8,9},{9,8},{10,11... | collective-permute-start | bytes 1572872 | tf_op jit(solution)/shard_map/beside0/ppermute | solution.py:230
  7.3 9.8 %collective-permute-start.1 = (bf16[4,256,128]{2,1,0:T(8,128)(2,1)S(1)}, bf16[4,256,128]{2,1,0:T(8,128)(2,1)S(1)}, u32[]{:S(2)}, u32[]{:S(2)}) collective-permute-start(bf16[4,256,128]{2,1,0:T(8,128)(2,1)S(1)} %get-tuple-element.39), channel_id=1, source_target_pairs={{0,2},{1,3},{2,0},{3,1},{4,6},{5,7},{6,4},{7,5},{8,10},{9,11},{10,... | collective-permute-start | bytes 786440 | tf_op jit(solution)/shard_map/y0/ppermute | solution.py:230
  9.9 12.3 %collective-permute-start.2 = (bf16[4,256,128]{2,1,0:T(8,128)(2,1)S(1)}, bf16[4,256,128]{2,1,0:T(8,128)(2,1)S(1)}, u32[]{:S(2)}, u32[]{:S(2)}) collective-permute-start(bf16[4,256,128]{2,1,0:T(8,128)(2,1)S(1)} %get-tuple-element.40), channel_id=1, source_target_pairs={{0,3},{1,2},{2,1},{3,0},{4,7},{5,6},{6,5},{7,4},{8,11},{9,10},{10,... | collective-permute-start | bytes 786440 | tf_op jit(solution)/shard_map/y1/ppermute | solution.py:230
  17.5 10.8 %collective-permute-start.4 = (bf16[4,256,128]{2,1,0:T(8,128)(2,1)S(1)}, bf16[4,256,128]{2,1,0:T(8,128)(2,1)S(1)}, u32[]{:S(2)}, u32[]{:S(2)}) collective-permute-start(bf16[4,256,128]{2,1,0:T(8,128)(2,1)S(1)} %get-tuple-element.47), channel_id=1, source_target_pairs={{0,2},{1,3},{2,0},{3,1},{4,6},{5,7},{6,4},{7,5},{8,10},{9,11},{10,... | collective-permute-start | bytes 786440 | tf_op jit(solution)/shard_map/y2/ppermute | solution.py:230
  19.5 27.4 %collective-permute-start.8 = (bf16[8,256,128]{2,1,0:T(8,128)(2,1)S(1)}, bf16[8,256,128]{2,1,0:T(8,128)(2,1)S(1)}, u32[]{:S(2)}, u32[]{:S(2)}) collective-permute-start(bf16[8,256,128]{2,1,0:T(8,128)(2,1)S(1)} %get-tuple-element.51), channel_id=1, source_target_pairs={{0,1},{1,0},{2,3},{3,2},{4,5},{5,4},{6,7},{7,6},{8,9},{9,8},{10,11... | collective-permute-start | bytes 1572872 | tf_op jit(solution)/shard_map/beside1/ppermute | solution.py:230
  19.5 13.9 %collective-permute-start.5 = (bf16[4,256,128]{2,1,0:T(8,128)(2,1)S(1)}, bf16[4,256,128]{2,1,0:T(8,128)(2,1)S(1)}, u32[]{:S(2)}, u32[]{:S(2)}) collective-permute-start(bf16[4,256,128]{2,1,0:T(8,128)(2,1)S(1)} %get-tuple-element.48), channel_id=1, source_target_pairs={{0,3},{1,2},{2,1},{3,0},{4,7},{5,6},{6,5},{7,4},{8,11},{9,10},{10,... | collective-permute-start | bytes 786440 | tf_op jit(solution)/shard_map/y3/ppermute | solution.py:230
  23.5 62.9 %copy-start.1 = (s32[128]{0:T(128)S(1)}, s32[128]{0:T(128)}, u32[]{:S(2)}) copy-start(s32[128]{0:T(128)} %mirror_ref.1) | copy-start | bytes 1540
  23.5 15.5 %collective-permute-start.3 = (bf16[1,4,4,64,128]{4,3,2,1,0:T(8,128)(2,1)S(1)}, bf16[1,4,4,64,128]{4,3,2,1,0:T(8,128)(2,1)S(1)}, u32[]{:S(2)}, u32[]{:S(2)}) collective-permute-start(bf16[1,4,4,64,128]{4,3,2,1,0:T(8,128)(2,1)S(1)} %get-tuple-element.46.refs_5_), channel_id=1, source_target_pairs={{0,16},{4,20},{8,24},{12,28},{16,0},{20,4},{24,8},{28,12},{1,17},{... | collective-permute-start | bytes 786440 | tf_op jit(solution)/shard_map/z4c0/ppermute | solution.py:230
  26.2 13.3 %collective-permute-start.9 = (bf16[4,256,128]{2,1,0:T(8,128)(2,1)S(1)}, bf16[4,256,128]{2,1,0:T(8,128)(2,1)S(1)}, u32[]{:S(2)}, u32[]{:S(2)}) collective-permute-start(bf16[4,256,128]{2,1,0:T(8,128)(2,1)S(1)} %get-tuple-element.52), channel_id=1, source_target_pairs={{0,2},{1,3},{2,0},{3,1},{4,6},{5,7},{6,4},{7,5},{8,10},{9,11},{10,... | collective-permute-start | bytes 786440 | tf_op jit(solution)/shard_map/y4/ppermute | solution.py:230
  28.3 16.3 %collective-permute-start.10 = (bf16[4,256,128]{2,1,0:T(8,128)(2,1)S(1)}, bf16[4,256,128]{2,1,0:T(8,128)(2,1)S(1)}, u32[]{:S(2)}, u32[]{:S(2)}) collective-permute-start(bf16[4,256,128]{2,1,0:T(8,128)(2,1)S(1)} %get-tuple-element.53), channel_id=1, source_target_pairs={{0,3},{1,2},{2,1},{3,0},{4,7},{5,6},{6,5},{7,4},{8,11},{9,10},{10,... | collective-permute-start | bytes 786440 | tf_op jit(solution)/shard_map/y5/ppermute | solution.py:230
  33.4 21.9 %collective-permute-start.13 = (bf16[4,256,128]{2,1,0:T(8,128)(2,1)S(1)}, bf16[4,256,128]{2,1,0:T(8,128)(2,1)S(1)}, u32[]{:S(2)}, u32[]{:S(2)}) collective-permute-start(bf16[4,256,128]{2,1,0:T(8,128)(2,1)S(1)} %get-tuple-element.55), channel_id=1, source_target_pairs={{0,2},{1,3},{2,0},{3,1},{4,6},{5,7},{6,4},{7,5},{8,10},{9,11},{10,... | collective-permute-start | bytes 786440 | tf_op jit(solution)/shard_map/y6/ppermute | solution.py:230
  39.0 16.3 %collective-permute-start.7 = (bf16[1,4,4,64,128]{4,3,2,1,0:T(8,128)(2,1)S(1)}, bf16[1,4,4,64,128]{4,3,2,1,0:T(8,128)(2,1)S(1)}, u32[]{:S(2)}, u32[]{:S(2)}) collective-permute-start(bf16[1,4,4,64,128]{4,3,2,1,0:T(8,128)(2,1)S(1)} %get-tuple-element.49.refs_2_), channel_id=1, source_target_pairs={{0,16},{4,20},{8,24},{12,28},{16,0},{20,4},{24,8},{28,12},{1,17},{... | collective-permute-start | bytes 786440 | tf_op jit(solution)/shard_map/z4c1/ppermute | solution.py:230
  39.6 15.8 %collective-permute-start.6 = (bf16[2,2,4,64,128]{4,3,2,1,0:T(8,128)(2,1)S(1)}, bf16[2,2,4,64,128]{4,3,2,1,0:T(8,128)(2,1)S(1)}, u32[]{:S(2)}, u32[]{:S(2)}) collective-permute-start(bf16[2,2,4,64,128]{4,3,2,1,0:T(8,128)(2,1)S(1)} %merge.6.refs_5_), channel_id=1, source_target_pairs={{0,8},{4,12},{8,0},{12,4},{16,24},{20,28},{24,16},{28,20},{1,9},{5... | collective-permute-start | bytes 786440 | tf_op jit(solution)/shard_map/z2c0/ppermute | solution.py:230
  44.6 11.2 %collective-permute-start.14 = (bf16[4,256,128]{2,1,0:T(8,128)(2,1)S(1)}, bf16[4,256,128]{2,1,0:T(8,128)(2,1)S(1)}, u32[]{:S(2)}, u32[]{:S(2)}) collective-permute-start(bf16[4,256,128]{2,1,0:T(8,128)(2,1)S(1)} %get-tuple-element.56), channel_id=1, source_target_pairs={{0,3},{1,2},{2,1},{3,0},{4,7},{5,6},{6,5},{7,4},{8,11},{9,10},{10,... | collective-permute-start | bytes 786440 | tf_op jit(solution)/shard_map/y7/ppermute | solution.py:230
  48.2 16.8 %collective-permute-start.16 = (bf16[1,4,4,64,128]{4,3,2,1,0:T(8,128)(2,1)S(1)}, bf16[1,4,4,64,128]{4,3,2,1,0:T(8,128)(2,1)S(1)}, u32[]{:S(2)}, u32[]{:S(2)}) collective-permute-start(bf16[1,4,4,64,128]{4,3,2,1,0:T(8,128)(2,1)S(1)} %get-tuple-element.54.refs_2_), channel_id=1, source_target_pairs={{0,16},{4,20},{8,24},{12,28},{16,0},{20,4},{24,8},{28,12},{1,17},{... | collective-permute-start | bytes 786440 | tf_op jit(solution)/shard_map/z4c2/ppermute | solution.py:230
  57.2 9.2 %collective-permute-start.15 = (bf16[1,4,4,64,128]{4,3,2,1,0:T(8,128)(2,1)S(1)}, bf16[1,4,4,64,128]{4,3,2,1,0:T(8,128)(2,1)S(1)}, u32[]{:S(2)}, u32[]{:S(2)}) collective-permute-start(bf16[1,4,4,64,128]{4,3,2,1,0:T(8,128)(2,1)S(1)} %get-tuple-element.58.refs_2_), channel_id=1, source_target_pairs={{0,4},{4,0},{8,12},{12,8},{16,20},{20,16},{24,28},{28,24},{1,5},{5... | collective-permute-start | bytes 786440 | tf_op jit(solution)/shard_map/z1c3/ppermute | solution.py:230
  58.8 12.8 %collective-permute-start.12 = (bf16[2,2,4,64,128]{4,3,2,1,0:T(8,128)(2,1)S(1)}, bf16[2,2,4,64,128]{4,3,2,1,0:T(8,128)(2,1)S(1)}, u32[]{:S(2)}, u32[]{:S(2)}) collective-permute-start(bf16[2,2,4,64,128]{4,3,2,1,0:T(8,128)(2,1)S(1)} %merge.7.refs_3_), channel_id=1, source_target_pairs={{0,8},{4,12},{8,0},{12,4},{16,24},{20,28},{24,16},{28,20},{1,9},{5... | collective-permute-start | bytes 786440 | tf_op jit(solution)/shard_map/z2c1/ppermute | solution.py:230
  60.4 11.3 %collective-permute-start.11 = (bf16[4,1,4,64,128]{4,3,2,1,0:T(8,128)(2,1)S(1)}, bf16[4,1,4,64,128]{4,3,2,1,0:T(8,128)(2,1)S(1)}, u32[]{:S(2)}, u32[]{:S(2)}) collective-permute-start(bf16[4,1,4,64,128]{4,3,2,1,0:T(8,128)(2,1)S(1)} %merge.8.refs_5_), channel_id=1, source_target_pairs={{0,4},{4,0},{8,12},{12,8},{16,20},{20,16},{24,28},{28,24},{1,5},{5... | collective-permute-start | bytes 786440 | tf_op jit(solution)/shard_map/z1c0/ppermute | solution.py:230
  66.4 12.7 %collective-permute-start.22 = (bf16[2,1,4,64,128]{4,3,2,1,0:T(8,128)(2,1)S(1)}, bf16[2,1,4,64,128]{4,3,2,1,0:T(8,128)(2,1)S(1)}, u32[]{:S(2)}, u32[]{:S(2)}) collective-permute-start(bf16[2,1,4,64,128]{4,3,2,1,0:T(8,128)(2,1)S(1)} %get-tuple-element.67), channel_id=1, source_target_pairs={{0,16},{4,20},{8,24},{12,28},{16,0},{20,4},{24,8},{28,12},{1,17},{... | collective-permute-start | bytes 393224 | tf_op jit(solution)/shard_map/z4c3/ppermute | solution.py:230
  69.1 10.0 %collective-permute-start.21 = (bf16[2,1,4,64,128]{4,3,2,1,0:T(8,128)(2,1)S(1)}, bf16[2,1,4,64,128]{4,3,2,1,0:T(8,128)(2,1)S(1)}, u32[]{:S(2)}, u32[]{:S(2)}) collective-permute-start(bf16[2,1,4,64,128]{4,3,2,1,0:T(8,128)(2,1)S(1)} %get-tuple-element.63.refs_3_), channel_id=1, source_target_pairs={{0,24},{4,28},{8,16},{12,20},{16,8},{20,12},{24,0},{28,4},{1,25},{... | collective-permute-start | bytes 393224 | tf_op jit(solution)/shard_map/z6c3/ppermute | solution.py:230
  71.7 14.7 %collective-permute-start.17 = (bf16[4,1,4,64,128]{4,3,2,1,0:T(8,128)(2,1)S(1)}, bf16[4,1,4,64,128]{4,3,2,1,0:T(8,128)(2,1)S(1)}, u32[]{:S(2)}, u32[]{:S(2)}) collective-permute-start(bf16[4,1,4,64,128]{4,3,2,1,0:T(8,128)(2,1)S(1)} %merge.11.refs_1_), channel_id=1, source_target_pairs={{0,4},{4,0},{8,12},{12,8},{16,20},{20,16},{24,28},{28,24},{1,5},{5... | collective-permute-start | bytes 786440 | tf_op jit(solution)/shard_map/z1c1/ppermute | solution.py:230
  73.3 10.4 %collective-permute-start.18 = (bf16[2,1,4,64,128]{4,3,2,1,0:T(8,128)(2,1)S(1)}, bf16[2,1,4,64,128]{4,3,2,1,0:T(8,128)(2,1)S(1)}, u32[]{:S(2)}, u32[]{:S(2)}) collective-permute-start(bf16[2,1,4,64,128]{4,3,2,1,0:T(8,128)(2,1)S(1)} %get-tuple-element.64), channel_id=1, source_target_pairs={{0,12},{4,8},{8,4},{12,0},{16,28},{20,24},{24,20},{28,16},{1,13},{... | collective-permute-start | bytes 393224 | tf_op jit(solution)/shard_map/z3c2/ppermute | solution.py:230
  74.8 8.8 %collective-permute-start.23 = (bf16[2,1,4,64,128]{4,3,2,1,0:T(8,128)(2,1)S(1)}, bf16[2,1,4,64,128]{4,3,2,1,0:T(8,128)(2,1)S(1)}, u32[]{:S(2)}, u32[]{:S(2)}) collective-permute-start(bf16[2,1,4,64,128]{4,3,2,1,0:T(8,128)(2,1)S(1)} %get-tuple-element.68), channel_id=1, source_target_pairs={{0,8},{4,12},{8,0},{12,4},{16,24},{20,28},{24,16},{28,20},{1,9},{5... | collective-permute-start | bytes 393224 | tf_op jit(solution)/shard_map/z2c3/ppermute | solution.py:230
  79.1 7.3 %collective-permute-start.19 = (bf16[2,1,4,64,128]{4,3,2,1,0:T(8,128)(2,1)S(1)}, bf16[2,1,4,64,128]{4,3,2,1,0:T(8,128)(2,1)S(1)}, u32[]{:S(2)}, u32[]{:S(2)}) collective-permute-start(bf16[2,1,4,64,128]{4,3,2,1,0:T(8,128)(2,1)S(1)} %get-tuple-element.65), channel_id=1, source_target_pairs={{0,8},{4,12},{8,0},{12,4},{16,24},{20,28},{24,16},{28,20},{1,9},{5... | collective-permute-start | bytes 393224 | tf_op jit(solution)/shard_map/z2c2/ppermute | solution.py:230
  79.1 7.3 %collective-permute-start.20 = (bf16[2,1,4,64,128]{4,3,2,1,0:T(8,128)(2,1)S(1)}, bf16[2,1,4,64,128]{4,3,2,1,0:T(8,128)(2,1)S(1)}, u32[]{:S(2)}, u32[]{:S(2)}) collective-permute-start(bf16[2,1,4,64,128]{4,3,2,1,0:T(8,128)(2,1)S(1)} %get-tuple-element.66), channel_id=1, source_target_pairs={{0,4},{4,0},{8,12},{12,8},{16,20},{20,16},{24,28},{28,24},{1,5},{5... | collective-permute-start | bytes 393224 | tf_op jit(solution)/shard_map/z1c2/ppermute | solution.py:230

commit v14 on v13

--- a/solution.py
+++ b/solution.py
@@ -11,7 +11,7 @@
 STEP = 64
 BATCHES = ((4, 4), (4, 4))
 CHUNKS = sum(BATCHES, ())
-SIZES = ((1,), (1,), (1, 2), (-1, 2))
+SIZES = ((1,), (1,), (-1, 2), (-1, 2))
 PART = 256
 MIB = 1024 * 1024
 COST = pl.CostEstimate(flops=1024, bytes_accessed=1024, transcendentals=0)
@@ -156,20 +156,20 @@
                 at += 1
 
 
-def merge(parts, picks, later, after):
-    lines, n = sum(x.shape[0] for x in parts), len(parts)
+def merge(parts, picks, after):
+    lines = sum(x.shape[0] for x in parts)
     out = pl.pallas_call(
-        functools.partial(merge_kernel, n, picks),
-        in_specs=[IN_VMEM] * n + [IN_HBM] * len(later) + [ANYWHERE] * len(after),
-        out_specs=[IN_HBM] * len(later) + [IN_VMEM] * len(picks),
-        out_shape=[jax.ShapeDtypeStruct(x.shape, x.dtype) for x in later]
-        + [jax.ShapeDtypeStruct((lines, len(its[0]), *parts[0].shape[2:]), jnp.bfloat16) for its in picks],
-        input_output_aliases={n + m: m for m in range(len(later))},
+        functools.partial(merge_kernel, len(parts), picks),
+        in_specs=[IN_VMEM] * len(parts) + [ANYWHERE] * len(after),
+        out_specs=[IN_VMEM] * len(picks),
+        out_shape=[
+            jax.ShapeDtypeStruct((lines, len(its[0]), *parts[0].shape[2:]), jnp.bfloat16) for its in picks
+        ],
         compiler_params=pltpu.CompilerParams(vmem_limit_bytes=24 * MIB),
         cost_estimate=COST,
         name="merge",
-    )(*parts, *later, *after)
-    return list(out[len(later) :]), list(out[: len(later)])
+    )(*parts, *after)
+    return list(out)
 
 
 def wait_kernel(*refs):
@@ -265,12 +265,11 @@
     turned, queue[1] = turn(coeffs, n_mo, padded, queue[1], arrived[0][:1] + token)
     arrived += [arrive(c) for c in range(1, last + 1)]
 
+    levels = [digits(n_pair, sizes) for sizes in SIZES]
     steps = [(c, c, 0) for c in range(last + 1)]
-    levels = [digits(n_pair, sizes) for sizes in SIZES]
     for c, masks in enumerate(levels):
-        steps += [(c + n + n / 10 - 0.95 * (c == last), c, n) for n in range(1, len(masks))]
+        steps += [(c + (n + n / 10 if SIZES[c][0] > 0 else n * 3 / 10), c, n) for n in range(1, len(masks))]
     parts, owners, offsets, token = [[] for _ in CHUNKS], [[] for _ in CHUNKS], [[] for _ in CHUNKS], []
-    waiting = []
 
     def plan(c, level):
         mask, gone = levels[c][level], sum(levels[c][:level])
@@ -294,17 +293,12 @@
             parts[c], owners[c], offsets[c] = [keep], [kept], [[0]]
         else:
             picks = [[[its.index(o) for o in some] for its in owners[c]] for some in sent]
-            done = parts[c - 1][-1:] if level == 2 and c else []
-            later = waiting if c == last and level == 1 else []
-            messages, later = merge(parts[c], picks, later, token + done)
-            if later:
-                send(last - 1, 1, later)
+            done = {(0, 2): arrived[last][:1], (last - 1, 1): arrived[last][1:], (last, 1): parts[0][-1:]}
+            done = list(done.get((c, level), []))
+            messages = merge(parts[c], picks, token + done)
         token = messages[:1]
-        if c == last - 1 and level == 1:
-            waiting = messages
-        else:
-            send(c, level, messages)
-    for x in parts[last][-3:]:
+        send(c, level, messages)
+    for x in parts[last - 1][-3:] + parts[last][-3:]:
         token = [wait_for([x, *token])]
     pieces = [x for chunk in parts for x in chunk]
     sources = [(tuple(group), first) for chunk, first in zip(offsets, firsts) for group in chunk]

time: 89.8 us -> 89.6 us (level)
  waiting for transfers between devices: 33.7 us -> 30.5 us
  starting transfers between devices: 33.2 us -> 36.2 us
    ppermute x24, waiting for transfers between devices: 33.7 us -> 30.5 us  [flipped(): return lax.ppermute(x, axis, [(i, i ^ offset) for i in range(size)])]
    ppermute x24, starting transfers between devices: 33.2 us -> 36.2 us  [flipped(): return lax.ppermute(x, axis, [(i, i ^ offset) for i in range(size)])]
  transfers between devices with their start and end apart: 24 -> 24, of which waited for: 15 -> 12; matrix products, arithmetic and copies ran while one was open for 0% -> 0% of each run, Pallas kernels for 14% -> 14%
where the time goes in v14:
time: 89.6 us; the launch traced here: 89.5 us
  starting transfers between devices  36.2 us (40%)
  waiting for transfers between devices  30.5 us (34%)
  Pallas kernels  22.5 us (25%)
    ppermute x24, starting transfers between devices, flipped(): return lax.ppermute(x, axis, [(i, i ^ offset) for i in range(size)])  36.2 us
    ppermute x24, waiting for transfers between devices, flipped(): return lax.ppermute(x, axis, [(i, i ^ offset) for i in range(size)])  30.5 us
    pallas_call x2, Pallas kernels, quarter_of(): pl.pallas_call(functools.partial(quarter_kernel, batch, n_mo, blocks, len...  13.5 us
    pallas_call x4, Pallas kernels, half_of(): pl.pallas_call(functools.partial(half_kernel, n_mo, first, owners), in_sp...  5.21 us
    pallas_call x1, Pallas kernels, combine(): pl.pallas_call(functools.partial(combine_kernel, sources, k_all, per_step...  3.29 us
  transfers between devices with their start and end apart: 24, of which 12 were waited for; matrix products, arithmetic and copies ran while one was open for 0% of the time, Pallas kernels for 14%

profile of v14, /device:TPU:0, one launch (start us, length us, event | category | flops | bytes accessed | tf_op | source)
XLA Modules:
  0.0 89.5 jit_solution(13220201885093758274)
XLA Ops:
  0.0 0.1 pad_add_fusion.place_ref
  0.1 6.7 %quarter.2 = (bf16[8,256,128]{2,1,0:T(8,128)(2,1)S(1)}, bf16[8,256,128]{2,1,0:T(8,128)(2,1)S(1)}, bf16[4,256,128]{2,1,0:T(8,128)(2,1)S(1)}, bf16[4,256,128]{2,1,...) custom-call(s32[2]{0:T(128)S(1)} %pad_add_fusion.place_ref, ...), custom_call_target="tpu_custom_call" | custom-call | flops 1024 | bytes 1024 | tf_op jit(solution)/shard_map/quarter/pallas_call | solution.py:70
  6.8 0.5 collective-permute-start
  7.3 2.6 %collective-permute-start.1 = (bf16[4,256,128]{2,1,0:T(8,128)(2,1)S(1)}, bf16[4,256,128]{2,1,0:T(8,128)(2,1)S(1)}, u32[]{:S(2)}, u32[]{:S(2)}) collective-permute-start(bf16[4,256,128]{2,1,0:T(8,128)(2,1)S(1)} %get-tuple-element.36), channel_id=1, source_target_pairs={{0,2},{1,3},{2,0},{3,1},{4,6},{5,7},{6,4},{7,5},{8,10},{9,11},{10,... | collective-permute-start | bytes 786440 | tf_op jit(solution)/shard_map/y0/ppermute | solution.py:230
  9.9 0.1 collective-permute-start.2
  10.0 6.7 %quarter.3 = (bf16[8,256,128]{2,1,0:T(8,128)(2,1)S(1)}, bf16[8,256,128]{2,1,0:T(8,128)(2,1)S(1)}, bf16[4,256,128]{2,1,0:T(8,128)(2,1)S(1)}, bf16[4,256,128]{2,1,...) custom-call(s32[2]{0:T(128)S(1)} %pad_add_fusion.place_ref, ...), custom_call_target="tpu_custom_call" | custom-call | flops 1024 | bytes 1024 | tf_op jit(solution)/shard_map/quarter/pallas_call | solution.py:70
  16.7 0.3 collective-permute-done.1.refs_2_
  17.1 0.4 turn.1
  17.5 2.0 %collective-permute-start.4 = (bf16[4,256,128]{2,1,0:T(8,128)(2,1)S(1)}, bf16[4,256,128]{2,1,0:T(8,128)(2,1)S(1)}, u32[]{:S(2)}, u32[]{:S(2)}) collective-permute-start(bf16[4,256,128]{2,1,0:T(8,128)(2,1)S(1)} %get-tuple-element.44), channel_id=1, source_target_pairs={{0,2},{1,3},{2,0},{3,1},{4,6},{5,7},{6,4},{7,5},{8,10},{9,11},{10,... | collective-permute-start | bytes 786440 | tf_op jit(solution)/shard_map/y2/ppermute | solution.py:230
  19.5 0.0 collective-permute-start.8
  19.5 0.2 collective-permute-start.5
  19.7 2.5 %collective-permute-done.2.refs_3_ = bf16[4,256,128]{2,1,0:T(8,128)(2,1)S(1)} collective-permute-done((bf16[4,256,128]{2,1,0:T(8,128)(2,1)S(1)}, bf16[4,256,128]{2,1,0:T(8,128)(2,1)S(1)}, u32[]{:S(2)}, u32[]{:S(2)}) %collective-permute-start.2) | collective-permute-done | bytes 262176 | tf_op jit(solution)/shard_map/y1/ppermute | solution.py:230
  22.2 0.0 collective-permute-done.refs_1_
  22.2 1.3 %half.4 = (bf16[1,4,4,64,128]{4,3,2,1,0:T(8,128)(2,1)S(1)}, bf16[1,4,4,64,128]{4,3,2,1,0:T(8,128)(2,1)S(1)}) custom-call(s32[2]{0:T(128)S(1)} %pad_add_fusion.place_ref, bf16[8,256,128]{2,1,0:T(8,128)(2,1)S(1)} %get-tuple-element.34.refs_0_, bf16[8,256,128]{2,1,0:T(8,128)(2,1)S(1)} %collective-permute-done.refs_1_, ...), custom_call_target="tpu_custom_call" | custom-call | flops 1024 | bytes 1024 | tf_op jit(solution)/shard_map/half/pallas_call | solution.py:136
  23.5 2.7 %collective-permute-start.3 = (bf16[1,4,4,64,128]{4,3,2,1,0:T(8,128)(2,1)S(1)}, bf16[1,4,4,64,128]{4,3,2,1,0:T(8,128)(2,1)S(1)}, u32[]{:S(2)}, u32[]{:S(2)}) collective-permute-start(bf16[1,4,4,64,128]{4,3,2,1,0:T(8,128)(2,1)S(1)} %get-tuple-element.43.refs_5_), channel_id=1, source_target_pairs={{0,16},{4,20},{8,24},{12,28},{16,0},{20,4},{24,8},{28,12},{1,17},{... | collective-permute-start | bytes 786440 | tf_op jit(solution)/shard_map/z4c0/ppermute | solution.py:230
  26.2 1.5 %collective-permute-start.9 = (bf16[4,256,128]{2,1,0:T(8,128)(2,1)S(1)}, bf16[4,256,128]{2,1,0:T(8,128)(2,1)S(1)}, u32[]{:S(2)}, u32[]{:S(2)}) collective-permute-start(bf16[4,256,128]{2,1,0:T(8,128)(2,1)S(1)} %get-tuple-element.49), channel_id=1, source_target_pairs={{0,2},{1,3},{2,0},{3,1},{4,6},{5,7},{6,4},{7,5},{8,10},{9,11},{10,... | collective-permute-start | bytes 786440 | tf_op jit(solution)/shard_map/y4/ppermute | solution.py:230
  27.7 0.6 collective-permute-done.4.refs_2_
  28.3 0.8 collective-permute-start.10
  29.1 4.3 %collective-permute-done.5.refs_3_ = bf16[4,256,128]{2,1,0:T(8,128)(2,1)S(1)} collective-permute-done((bf16[4,256,128]{2,1,0:T(8,128)(2,1)S(1)}, bf16[4,256,128]{2,1,0:T(8,128)(2,1)S(1)}, u32[]{:S(2)}, u32[]{:S(2)}) %collective-permute-start.5) | collective-permute-done | bytes 262176 | tf_op jit(solution)/shard_map/y3/ppermute | solution.py:230
  33.4 1.3 %half.5 = (bf16[1,4,4,64,128]{4,3,2,1,0:T(8,128)(2,1)S(1)}, bf16[1,4,4,64,128]{4,3,2,1,0:T(8,128)(2,1)S(1)}) custom-call(s32[2]{0:T(128)S(1)} %pad_add_fusion.place_ref, bf16[8,256,128]{2,1,0:T(8,128)(2,1)S(1)} %get-tuple-element.34.refs_0_, bf16[8,256,128]{2,1,0:T(8,128)(2,1)S(1)} %collective-permute-done.refs_1_, ...), custom_call_target="tpu_custom_call" | custom-call | flops 1024 | bytes 1024 | tf_op jit(solution)/shard_map/half/pallas_call | solution.py:136
  34.7 2.7 %collective-permute-start.7 = (bf16[1,4,4,64,128]{4,3,2,1,0:T(8,128)(2,1)S(1)}, bf16[1,4,4,64,128]{4,3,2,1,0:T(8,128)(2,1)S(1)}, u32[]{:S(2)}, u32[]{:S(2)}) collective-permute-start(bf16[1,4,4,64,128]{4,3,2,1,0:T(8,128)(2,1)S(1)} %get-tuple-element.46.refs_2_), channel_id=1, source_target_pairs={{0,16},{4,20},{8,24},{12,28},{16,0},{20,4},{24,8},{28,12},{1,17},{... | collective-permute-start | bytes 786440 | tf_op jit(solution)/shard_map/z4c1/ppermute | solution.py:230
  37.4 1.6 %collective-permute-done.3.refs_1_ = bf16[1,4,4,64,128]{4,3,2,1,0:T(8,128)(2,1)S(1)} collective-permute-done((bf16[1,4,4,64,128]{4,3,2,1,0:T(8,128)(2,1)S(1)}, bf16[1,4,4,64,128]{4,3,2,1,0:T(8,128)(2,1)S(1)}, u32[]{:S(2)}, u32[]{:S(2)}) %collective-permute-start.3) | collective-permute-done | bytes 262176 | tf_op jit(solution)/shard_map/z4c0/ppermute | solution.py:230
  39.0 1.6 %collective-permute-start.11 = (bf16[4,256,128]{2,1,0:T(8,128)(2,1)S(1)}, bf16[4,256,128]{2,1,0:T(8,128)(2,1)S(1)}, u32[]{:S(2)}, u32[]{:S(2)}) collective-permute-start(bf16[4,256,128]{2,1,0:T(8,128)(2,1)S(1)} %get-tuple-element.52), channel_id=1, source_target_pairs={{0,2},{1,3},{2,0},{3,1},{4,6},{5,7},{6,4},{7,5},{8,10},{9,11},{10,... | collective-permute-start | bytes 786440 | tf_op jit(solution)/shard_map/y6/ppermute | solution.py:230
  40.6 0.0 collective-permute-done.9.refs_2_
  40.6 0.1 collective-permute-start.14
  40.7 4.0 %collective-permute-done.10.refs_3_ = bf16[4,256,128]{2,1,0:T(8,128)(2,1)S(1)} collective-permute-done((bf16[4,256,128]{2,1,0:T(8,128)(2,1)S(1)}, bf16[4,256,128]{2,1,0:T(8,128)(2,1)S(1)}, u32[]{:S(2)}, u32[]{:S(2)}) %collective-permute-start.10) | collective-permute-done | bytes 262176 | tf_op jit(solution)/shard_map/y5/ppermute | solution.py:230
  44.6 1.6 %collective-permute-start.6 = (bf16[2,2,4,64,128]{4,3,2,1,0:T(8,128)(2,1)S(1)}, bf16[2,2,4,64,128]{4,3,2,1,0:T(8,128)(2,1)S(1)}, u32[]{:S(2)}, u32[]{:S(2)}) collective-permute-start(bf16[2,2,4,64,128]{4,3,2,1,0:T(8,128)(2,1)S(1)} %merge.6.refs_5_), channel_id=1, source_target_pairs={{0,8},{4,12},{8,0},{12,4},{16,24},{20,28},{24,16},{28,20},{1,9},{5... | collective-permute-start | bytes 786440 | tf_op jit(solution)/shard_map/z2c0/ppermute | solution.py:230
  46.3 0.0 collective-permute-done.8.refs_1_
  46.3 1.3 %half.6 = (bf16[1,4,4,64,128]{4,3,2,1,0:T(8,128)(2,1)S(1)}, bf16[1,4,4,64,128]{4,3,2,1,0:T(8,128)(2,1)S(1)}) custom-call(s32[2]{0:T(128)S(1)} %pad_add_fusion.place_ref, bf16[8,256,128]{2,1,0:T(8,128)(2,1)S(1)} %get-tuple-element.40.refs_3_.refs_0_, bf16[8,256,128]{2,1,0:T(8,128)(2,1)S(1)} %collective-permute-done.8.refs_1_, ...), custom_call_target="tpu_custom_call" | custom-call | flops 1024 | bytes 1024 | tf_op jit(solution)/shard_map/half/pallas_call | solution.py:136
  47.6 1.6 %collective-permute-start.15 = (bf16[1,4,4,64,128]{4,3,2,1,0:T(8,128)(2,1)S(1)}, bf16[1,4,4,64,128]{4,3,2,1,0:T(8,128)(2,1)S(1)}, u32[]{:S(2)}, u32[]{:S(2)}) collective-permute-start(bf16[1,4,4,64,128]{4,3,2,1,0:T(8,128)(2,1)S(1)} %get-tuple-element.51.refs_2_), channel_id=1, source_target_pairs={{0,4},{4,0},{8,12},{12,8},{16,20},{20,16},{24,28},{28,24},{1,5},{5... | collective-permute-start | bytes 786440 | tf_op jit(solution)/shard_map/z1c2/ppermute | solution.py:230
  49.1 1.2 %collective-permute-done.7.refs_1_.refs_5_ = bf16[1,4,4,64,128]{4,3,2,1,0:T(8,128)(2,1)S(1)} collective-permute-done((bf16[1,4,4,64,128]{4,3,2,1,0:T(8,128)(2,1)S(1)}, bf16[1,4,4,64,128]{4,3,2,1,0:T(8,128)(2,1)S(1)}, u32[]{:S(2)}, u32[]{:S(2)}) %collective-permute-start.7) | collective-permute-done | bytes 262176 | tf_op jit(solution)/shard_map/z4c1/ppermute | solution.py:230
  50.4 0.7 collective-permute-start.13
  51.1 4.8 %collective-permute-done.6.refs_2_ = bf16[2,2,4,64,128]{4,3,2,1,0:T(8,128)(2,1)S(1)} collective-permute-done((bf16[2,2,4,64,128]{4,3,2,1,0:T(8,128)(2,1)S(1)}, bf16[2,2,4,64,128]{4,3,2,1,0:T(8,128)(2,1)S(1)}, u32[]{:S(2)}, u32[]{:S(2)}) %collective-permute-start.6) | collective-permute-done | bytes 262176 | tf_op jit(solution)/shard_map/z2c0/ppermute | solution.py:230
  55.9 1.8 %collective-permute-start.12 = (bf16[4,1,4,64,128]{4,3,2,1,0:T(8,128)(2,1)S(1)}, bf16[4,1,4,64,128]{4,3,2,1,0:T(8,128)(2,1)S(1)}, u32[]{:S(2)}, u32[]{:S(2)}) collective-permute-start(bf16[4,1,4,64,128]{4,3,2,1,0:T(8,128)(2,1)S(1)} %merge.8.refs_2_), channel_id=1, source_target_pairs={{0,4},{4,0},{8,12},{12,8},{16,20},{20,16},{24,28},{28,24},{1,5},{5... | collective-permute-start | bytes 786440 | tf_op jit(solution)/shard_map/z1c0/ppermute | solution.py:230
  57.7 0.0 collective-permute-done.14.refs_3_
  57.7 0.0 collective-permute-done.15.refs_1_.refs_9_
  57.8 1.3 %half.7 = (bf16[1,4,4,64,128]{4,3,2,1,0:T(8,128)(2,1)S(1)}, bf16[1,4,4,64,128]{4,3,2,1,0:T(8,128)(2,1)S(1)}) custom-call(s32[2]{0:T(128)S(1)} %pad_add_fusion.place_ref, bf16[8,256,128]{2,1,0:T(8,128)(2,1)S(1)} %get-tuple-element.40.refs_3_.refs_0_, bf16[8,256,128]{2,1,0:T(8,128)(2,1)S(1)} %collective-permute-done.8.refs_1_, ...), custom_call_target="tpu_custom_call" | custom-call | flops 1024 | bytes 1024 | tf_op jit(solution)/shard_map/half/pallas_call | solution.py:136
  59.1 0.3 collective-permute-start.20
  59.4 2.7 %collective-permute-start.18 = (bf16[2,1,4,64,128]{4,3,2,1,0:T(8,128)(2,1)S(1)}, bf16[2,1,4,64,128]{4,3,2,1,0:T(8,128)(2,1)S(1)}, u32[]{:S(2)}, u32[]{:S(2)}) collective-permute-start(bf16[2,1,4,64,128]{4,3,2,1,0:T(8,128)(2,1)S(1)} %get-tuple-element.57), channel_id=1, source_target_pairs={{0,16},{4,20},{8,24},{12,28},{16,0},{20,4},{24,8},{28,12},{1,17},{... | collective-permute-start | bytes 393224 | tf_op jit(solution)/shard_map/z4c2/ppermute | solution.py:230
  62.1 0.8 collective-permute-start.17
  62.9 1.6 %collective-permute-start.16 = (bf16[4,1,4,64,128]{4,3,2,1,0:T(8,128)(2,1)S(1)}, bf16[4,1,4,64,128]{4,3,2,1,0:T(8,128)(2,1)S(1)}, u32[]{:S(2)}, u32[]{:S(2)}) collective-permute-start(bf16[4,1,4,64,128]{4,3,2,1,0:T(8,128)(2,1)S(1)} %merge.10.refs_2_), channel_id=1, source_target_pairs={{0,4},{4,0},{8,12},{12,8},{16,20},{20,16},{24,28},{28,24},{1,5},{5... | collective-permute-start | bytes 786440 | tf_op jit(solution)/shard_map/z1c1/ppermute | solution.py:230
  64.5 0.6 collective-permute-done.12.refs_3_
  65.1 5.6 %collective-permute-done.20.refs_1_.refs_14_ = bf16[1,4,4,64,128]{4,3,2,1,0:T(8,128)(2,1)S(1)} collective-permute-done((bf16[1,4,4,64,128]{4,3,2,1,0:T(8,128)(2,1)S(1)}, bf16[1,4,4,64,128]{4,3,2,1,0:T(8,128)(2,1)S(1)}, u32[]{:S(2)}, u32[]{:S(2)}) %collective-permute-start.20) | collective-permute-done | bytes 262176 | tf_op jit(solution)/shard_map/z1c3/ppermute | solution.py:230
  70.8 3.6 %collective-permute-start.21 = (bf16[2,1,4,64,128]{4,3,2,1,0:T(8,128)(2,1)S(1)}, bf16[2,1,4,64,128]{4,3,2,1,0:T(8,128)(2,1)S(1)}, u32[]{:S(2)}, u32[]{:S(2)}) collective-permute-start(bf16[2,1,4,64,128]{4,3,2,1,0:T(8,128)(2,1)S(1)} %get-tuple-element.60.refs_1_), channel_id=1, source_target_pairs={{0,24},{4,28},{8,16},{12,20},{16,8},{20,12},{24,0},{28,4},{1,25},{... | collective-permute-start | bytes 393224 | tf_op jit(solution)/shard_map/z6c3/ppermute | solution.py:230
  74.4 6.8 %collective-permute-start.23 = (bf16[2,1,4,64,128]{4,3,2,1,0:T(8,128)(2,1)S(1)}, bf16[2,1,4,64,128]{4,3,2,1,0:T(8,128)(2,1)S(1)}, u32[]{:S(2)}, u32[]{:S(2)}) collective-permute-start(bf16[2,1,4,64,128]{4,3,2,1,0:T(8,128)(2,1)S(1)} %get-tuple-element.62), channel_id=1, source_target_pairs={{0,8},{4,12},{8,0},{12,4},{16,24},{20,28},{24,16},{28,20},{1,9},{5... | collective-permute-start | bytes 393224 | tf_op jit(solution)/shard_map/z2c3/ppermute | solution.py:230
  81.2 4.0 %collective-permute-done.22.refs_0_.refs_16_ = bf16[2,1,4,64,128]{4,3,2,1,0:T(8,128)(2,1)S(1)} collective-permute-done((bf16[2,1,4,64,128]{4,3,2,1,0:T(8,128)(2,1)S(1)}, bf16[2,1,4,64,128]{4,3,2,1,0:T(8,128)(2,1)S(1)}, u32[]{:S(2)}, u32[]{:S(2)}) %collective-permute-start.22) | collective-permute-done | bytes 131104 | tf_op jit(solution)/shard_map/z4c3/ppermute | solution.py:230
  85.3 0.9 %collective-permute-done.23.refs_0_.refs_17_ = bf16[2,1,4,64,128]{4,3,2,1,0:T(8,128)(2,1)S(1)} collective-permute-done((bf16[2,1,4,64,128]{4,3,2,1,0:T(8,128)(2,1)S(1)}, bf16[2,1,4,64,128]{4,3,2,1,0:T(8,128)(2,1)S(1)}, u32[]{:S(2)}, u32[]{:S(2)}) %collective-permute-start.23) | collective-permute-done | bytes 131104 | tf_op jit(solution)/shard_map/z2c3/ppermute | solution.py:230
  86.2 3.3 %combine.1 = f32[128,64,128]{2,1,0:T(8,128)} custom-call(s32[128]{0:T(128)S(1)} %copy-done.1, s32[2]{0:T(128)S(1)} %pad_add_fusion.place_ref, bf16[1,4,4,64,128]{4,3,2,1,0:T(8,128)(2,1)S(1)} %get-tuple-element.42.refs_0_, bf16[1,4,4,64,128]{4,3,2,1,0:T(8,128)(2,1)S(1)} %collective-permute-done.3.refs_1_, ...), custom_call_target="tpu_custom_call" | custom-call | flops 1024 | bytes 1024 | tf_op jit(solution)/shard_map/combine/pallas_call | solution.py:212
  (25 shorter events, 0.2 us)
Async XLA Ops:
  0.1 17.0 %copy-start = (bf16[1000,512]{1,0:T(8,128)(2,1)S(1)}, bf16[1000,512]{1,0:T(8,128)(2,1)}, u32[]{:S(2)}) copy-start(bf16[1000,512]{1,0:T(8,128)(2,1)} %c_ref.1) | copy-start | bytes 3072004
  6.8 15.4 %collective-permute-start = (bf16[8,256,128]{2,1,0:T(8,128)(2,1)S(1)}, bf16[8,256,128]{2,1,0:T(8,128)(2,1)S(1)}, u32[]{:S(2)}, u32[]{:S(2)}) collective-permute-start(bf16[8,256,128]{2,1,0:T(8,128)(2,1)S(1)} %get-tuple-element.35), channel_id=1, source_target_pairs={{0,1},{1,0},{2,3},{3,2},{4,5},{5,4},{6,7},{7,6},{8,9},{9,8},{10,11... | collective-permute-start | bytes 1572872 | tf_op jit(solution)/shard_map/beside0/ppermute | solution.py:230
  7.3 9.8 %collective-permute-start.1 = (bf16[4,256,128]{2,1,0:T(8,128)(2,1)S(1)}, bf16[4,256,128]{2,1,0:T(8,128)(2,1)S(1)}, u32[]{:S(2)}, u32[]{:S(2)}) collective-permute-start(bf16[4,256,128]{2,1,0:T(8,128)(2,1)S(1)} %get-tuple-element.36), channel_id=1, source_target_pairs={{0,2},{1,3},{2,0},{3,1},{4,6},{5,7},{6,4},{7,5},{8,10},{9,11},{10,... | collective-permute-start | bytes 786440 | tf_op jit(solution)/shard_map/y0/ppermute | solution.py:230
  9.9 12.3 %collective-permute-start.2 = (bf16[4,256,128]{2,1,0:T(8,128)(2,1)S(1)}, bf16[4,256,128]{2,1,0:T(8,128)(2,1)S(1)}, u32[]{:S(2)}, u32[]{:S(2)}) collective-permute-start(bf16[4,256,128]{2,1,0:T(8,128)(2,1)S(1)} %get-tuple-element.37), channel_id=1, source_target_pairs={{0,3},{1,2},{2,1},{3,0},{4,7},{5,6},{6,5},{7,4},{8,11},{9,10},{10,... | collective-permute-start | bytes 786440 | tf_op jit(solution)/shard_map/y1/ppermute | solution.py:230
  17.5 10.8 %collective-permute-start.4 = (bf16[4,256,128]{2,1,0:T(8,128)(2,1)S(1)}, bf16[4,256,128]{2,1,0:T(8,128)(2,1)S(1)}, u32[]{:S(2)}, u32[]{:S(2)}) collective-permute-start(bf16[4,256,128]{2,1,0:T(8,128)(2,1)S(1)} %get-tuple-element.44), channel_id=1, source_target_pairs={{0,2},{1,3},{2,0},{3,1},{4,6},{5,7},{6,4},{7,5},{8,10},{9,11},{10,... | collective-permute-start | bytes 786440 | tf_op jit(solution)/shard_map/y2/ppermute | solution.py:230
  19.5 26.8 %collective-permute-start.8 = (bf16[8,256,128]{2,1,0:T(8,128)(2,1)S(1)}, bf16[8,256,128]{2,1,0:T(8,128)(2,1)S(1)}, u32[]{:S(2)}, u32[]{:S(2)}) collective-permute-start(bf16[8,256,128]{2,1,0:T(8,128)(2,1)S(1)} %get-tuple-element.48), channel_id=1, source_target_pairs={{0,1},{1,0},{2,3},{3,2},{4,5},{5,4},{6,7},{7,6},{8,9},{9,8},{10,11... | collective-permute-start | bytes 1572872 | tf_op jit(solution)/shard_map/beside1/ppermute | solution.py:230
  19.5 13.9 %collective-permute-start.5 = (bf16[4,256,128]{2,1,0:T(8,128)(2,1)S(1)}, bf16[4,256,128]{2,1,0:T(8,128)(2,1)S(1)}, u32[]{:S(2)}, u32[]{:S(2)}) collective-permute-start(bf16[4,256,128]{2,1,0:T(8,128)(2,1)S(1)} %get-tuple-element.45), channel_id=1, source_target_pairs={{0,3},{1,2},{2,1},{3,0},{4,7},{5,6},{6,5},{7,4},{8,11},{9,10},{10,... | collective-permute-start | bytes 786440 | tf_op jit(solution)/shard_map/y3/ppermute | solution.py:230
  23.5 15.5 %collective-permute-start.3 = (bf16[1,4,4,64,128]{4,3,2,1,0:T(8,128)(2,1)S(1)}, bf16[1,4,4,64,128]{4,3,2,1,0:T(8,128)(2,1)S(1)}, u32[]{:S(2)}, u32[]{:S(2)}) collective-permute-start(bf16[1,4,4,64,128]{4,3,2,1,0:T(8,128)(2,1)S(1)} %get-tuple-element.43.refs_5_), channel_id=1, source_target_pairs={{0,16},{4,20},{8,24},{12,28},{16,0},{20,4},{24,8},{28,12},{1,17},{... | collective-permute-start | bytes 786440 | tf_op jit(solution)/shard_map/z4c0/ppermute | solution.py:230
  26.2 14.4 %collective-permute-start.9 = (bf16[4,256,128]{2,1,0:T(8,128)(2,1)S(1)}, bf16[4,256,128]{2,1,0:T(8,128)(2,1)S(1)}, u32[]{:S(2)}, u32[]{:S(2)}) collective-permute-start(bf16[4,256,128]{2,1,0:T(8,128)(2,1)S(1)} %get-tuple-element.49), channel_id=1, source_target_pairs={{0,2},{1,3},{2,0},{3,1},{4,6},{5,7},{6,4},{7,5},{8,10},{9,11},{10,... | collective-permute-start | bytes 786440 | tf_op jit(solution)/shard_map/y4/ppermute | solution.py:230
  28.3 57.9 %copy-start.1 = (s32[128]{0:T(128)S(1)}, s32[128]{0:T(128)}, u32[]{:S(2)}) copy-start(s32[128]{0:T(128)} %mirror_ref.1) | copy-start | bytes 1540
  28.3 16.3 %collective-permute-start.10 = (bf16[4,256,128]{2,1,0:T(8,128)(2,1)S(1)}, bf16[4,256,128]{2,1,0:T(8,128)(2,1)S(1)}, u32[]{:S(2)}, u32[]{:S(2)}) collective-permute-start(bf16[4,256,128]{2,1,0:T(8,128)(2,1)S(1)} %get-tuple-element.50), channel_id=1, source_target_pairs={{0,3},{1,2},{2,1},{3,0},{4,7},{5,6},{6,5},{7,4},{8,11},{9,10},{10,... | collective-permute-start | bytes 786440 | tf_op jit(solution)/shard_map/y5/ppermute | solution.py:230
  34.7 15.6 %collective-permute-start.7 = (bf16[1,4,4,64,128]{4,3,2,1,0:T(8,128)(2,1)S(1)}, bf16[1,4,4,64,128]{4,3,2,1,0:T(8,128)(2,1)S(1)}, u32[]{:S(2)}, u32[]{:S(2)}) collective-permute-start(bf16[1,4,4,64,128]{4,3,2,1,0:T(8,128)(2,1)S(1)} %get-tuple-element.46.refs_2_), channel_id=1, source_target_pairs={{0,16},{4,20},{8,24},{12,28},{16,0},{20,4},{24,8},{28,12},{1,17},{... | collective-permute-start | bytes 786440 | tf_op jit(solution)/shard_map/z4c1/ppermute | solution.py:230
  39.0 12.1 %collective-permute-start.11 = (bf16[4,256,128]{2,1,0:T(8,128)(2,1)S(1)}, bf16[4,256,128]{2,1,0:T(8,128)(2,1)S(1)}, u32[]{:S(2)}, u32[]{:S(2)}) collective-permute-start(bf16[4,256,128]{2,1,0:T(8,128)(2,1)S(1)} %get-tuple-element.52), channel_id=1, source_target_pairs={{0,2},{1,3},{2,0},{3,1},{4,6},{5,7},{6,4},{7,5},{8,10},{9,11},{10,... | collective-permute-start | bytes 786440 | tf_op jit(solution)/shard_map/y6/ppermute | solution.py:230
  40.6 17.1 %collective-permute-start.14 = (bf16[4,256,128]{2,1,0:T(8,128)(2,1)S(1)}, bf16[4,256,128]{2,1,0:T(8,128)(2,1)S(1)}, u32[]{:S(2)}, u32[]{:S(2)}) collective-permute-start(bf16[4,256,128]{2,1,0:T(8,128)(2,1)S(1)} %get-tuple-element.53), channel_id=1, source_target_pairs={{0,3},{1,2},{2,1},{3,0},{4,7},{5,6},{6,5},{7,4},{8,11},{9,10},{10,... | collective-permute-start | bytes 786440 | tf_op jit(solution)/shard_map/y7/ppermute | solution.py:230
  44.6 11.2 %collective-permute-start.6 = (bf16[2,2,4,64,128]{4,3,2,1,0:T(8,128)(2,1)S(1)}, bf16[2,2,4,64,128]{4,3,2,1,0:T(8,128)(2,1)S(1)}, u32[]{:S(2)}, u32[]{:S(2)}) collective-permute-start(bf16[2,2,4,64,128]{4,3,2,1,0:T(8,128)(2,1)S(1)} %merge.6.refs_5_), channel_id=1, source_target_pairs={{0,8},{4,12},{8,0},{12,4},{16,24},{20,28},{24,16},{28,20},{1,9},{5... | collective-permute-start | bytes 786440 | tf_op jit(solution)/shard_map/z2c0/ppermute | solution.py:230
  47.6 10.2 %collective-permute-start.15 = (bf16[1,4,4,64,128]{4,3,2,1,0:T(8,128)(2,1)S(1)}, bf16[1,4,4,64,128]{4,3,2,1,0:T(8,128)(2,1)S(1)}, u32[]{:S(2)}, u32[]{:S(2)}) collective-permute-start(bf16[1,4,4,64,128]{4,3,2,1,0:T(8,128)(2,1)S(1)} %get-tuple-element.51.refs_2_), channel_id=1, source_target_pairs={{0,4},{4,0},{8,12},{12,8},{16,20},{20,16},{24,28},{28,24},{1,5},{5... | collective-permute-start | bytes 786440 | tf_op jit(solution)/shard_map/z1c2/ppermute | solution.py:230
  50.4 12.6 %collective-permute-start.13 = (bf16[2,2,4,64,128]{4,3,2,1,0:T(8,128)(2,1)S(1)}, bf16[2,2,4,64,128]{4,3,2,1,0:T(8,128)(2,1)S(1)}, u32[]{:S(2)}, u32[]{:S(2)}) collective-permute-start(bf16[2,2,4,64,128]{4,3,2,1,0:T(8,128)(2,1)S(1)} %merge.7.refs_3_), channel_id=1, source_target_pairs={{0,8},{4,12},{8,0},{12,4},{16,24},{20,28},{24,16},{28,20},{1,9},{5... | collective-permute-start | bytes 786440 | tf_op jit(solution)/shard_map/z2c1/ppermute | solution.py:230
  55.9 9.2 %collective-permute-start.12 = (bf16[4,1,4,64,128]{4,3,2,1,0:T(8,128)(2,1)S(1)}, bf16[4,1,4,64,128]{4,3,2,1,0:T(8,128)(2,1)S(1)}, u32[]{:S(2)}, u32[]{:S(2)}) collective-permute-start(bf16[4,1,4,64,128]{4,3,2,1,0:T(8,128)(2,1)S(1)} %merge.8.refs_2_), channel_id=1, source_target_pairs={{0,4},{4,0},{8,12},{12,8},{16,20},{20,16},{24,28},{28,24},{1,5},{5... | collective-permute-start | bytes 786440 | tf_op jit(solution)/shard_map/z1c0/ppermute | solution.py:230
  59.1 11.7 %collective-permute-start.20 = (bf16[1,4,4,64,128]{4,3,2,1,0:T(8,128)(2,1)S(1)}, bf16[1,4,4,64,128]{4,3,2,1,0:T(8,128)(2,1)S(1)}, u32[]{:S(2)}, u32[]{:S(2)}) collective-permute-start(bf16[1,4,4,64,128]{4,3,2,1,0:T(8,128)(2,1)S(1)} %get-tuple-element.56.refs_3_), channel_id=1, source_target_pairs={{0,4},{4,0},{8,12},{12,8},{16,20},{20,16},{24,28},{28,24},{1,5},{5... | collective-permute-start | bytes 786440 | tf_op jit(solution)/shard_map/z1c3/ppermute | solution.py:230
  59.4 14.9 %collective-permute-start.18 = (bf16[2,1,4,64,128]{4,3,2,1,0:T(8,128)(2,1)S(1)}, bf16[2,1,4,64,128]{4,3,2,1,0:T(8,128)(2,1)S(1)}, u32[]{:S(2)}, u32[]{:S(2)}) collective-permute-start(bf16[2,1,4,64,128]{4,3,2,1,0:T(8,128)(2,1)S(1)} %get-tuple-element.57), channel_id=1, source_target_pairs={{0,16},{4,20},{8,24},{12,28},{16,0},{20,4},{24,8},{28,12},{1,17},{... | collective-permute-start | bytes 393224 | tf_op jit(solution)/shard_map/z4c2/ppermute | solution.py:230
  62.1 12.3 %collective-permute-start.17 = (bf16[2,1,4,64,128]{4,3,2,1,0:T(8,128)(2,1)S(1)}, bf16[2,1,4,64,128]{4,3,2,1,0:T(8,128)(2,1)S(1)}, u32[]{:S(2)}, u32[]{:S(2)}) collective-permute-start(bf16[2,1,4,64,128]{4,3,2,1,0:T(8,128)(2,1)S(1)} %get-tuple-element.55.refs_5_), channel_id=1, source_target_pairs={{0,24},{4,28},{8,16},{12,20},{16,8},{20,12},{24,0},{28,4},{1,25},{... | collective-permute-start | bytes 393224 | tf_op jit(solution)/shard_map/z6c2/ppermute | solution.py:230
  62.9 23.2 %collective-permute-start.16 = (bf16[4,1,4,64,128]{4,3,2,1,0:T(8,128)(2,1)S(1)}, bf16[4,1,4,64,128]{4,3,2,1,0:T(8,128)(2,1)S(1)}, u32[]{:S(2)}, u32[]{:S(2)}) collective-permute-start(bf16[4,1,4,64,128]{4,3,2,1,0:T(8,128)(2,1)S(1)} %merge.10.refs_2_), channel_id=1, source_target_pairs={{0,4},{4,0},{8,12},{12,8},{16,20},{20,16},{24,28},{28,24},{1,5},{5... | collective-permute-start | bytes 786440 | tf_op jit(solution)/shard_map/z1c1/ppermute | solution.py:230
  65.1 16.1 %collective-permute-start.19 = (bf16[2,1,4,64,128]{4,3,2,1,0:T(8,128)(2,1)S(1)}, bf16[2,1,4,64,128]{4,3,2,1,0:T(8,128)(2,1)S(1)}, u32[]{:S(2)}, u32[]{:S(2)}) collective-permute-start(bf16[2,1,4,64,128]{4,3,2,1,0:T(8,128)(2,1)S(1)} %get-tuple-element.58), channel_id=1, source_target_pairs={{0,8},{4,12},{8,0},{12,4},{16,24},{20,28},{24,16},{28,20},{1,9},{5... | collective-permute-start | bytes 393224 | tf_op jit(solution)/shard_map/z2c2/ppermute | solution.py:230
  70.8 10.4 %collective-permute-start.21 = (bf16[2,1,4,64,128]{4,3,2,1,0:T(8,128)(2,1)S(1)}, bf16[2,1,4,64,128]{4,3,2,1,0:T(8,128)(2,1)S(1)}, u32[]{:S(2)}, u32[]{:S(2)}) collective-permute-start(bf16[2,1,4,64,128]{4,3,2,1,0:T(8,128)(2,1)S(1)} %get-tuple-element.60.refs_1_), channel_id=1, source_target_pairs={{0,24},{4,28},{8,16},{12,20},{16,8},{20,12},{24,0},{28,4},{1,25},{... | collective-permute-start | bytes 393224 | tf_op jit(solution)/shard_map/z6c3/ppermute | solution.py:230
  74.4 10.9 %collective-permute-start.22 = (bf16[2,1,4,64,128]{4,3,2,1,0:T(8,128)(2,1)S(1)}, bf16[2,1,4,64,128]{4,3,2,1,0:T(8,128)(2,1)S(1)}, u32[]{:S(2)}, u32[]{:S(2)}) collective-permute-start(bf16[2,1,4,64,128]{4,3,2,1,0:T(8,128)(2,1)S(1)} %get-tuple-element.61), channel_id=1, source_target_pairs={{0,16},{4,20},{8,24},{12,28},{16,0},{20,4},{24,8},{28,12},{1,17},{... | collective-permute-start | bytes 393224 | tf_op jit(solution)/shard_map/z4c3/ppermute | solution.py:230
  74.4 11.8 %collective-permute-start.23 = (bf16[2,1,4,64,128]{4,3,2,1,0:T(8,128)(2,1)S(1)}, bf16[2,1,4,64,128]{4,3,2,1,0:T(8,128)(2,1)S(1)}, u32[]{:S(2)}, u32[]{:S(2)}) collective-permute-start(bf16[2,1,4,64,128]{4,3,2,1,0:T(8,128)(2,1)S(1)} %get-tuple-element.62), channel_id=1, source_target_pairs={{0,8},{4,12},{8,0},{12,4},{16,24},{20,28},{24,16},{28,20},{1,9},{5... | collective-permute-start | bytes 393224 | tf_op jit(solution)/shard_map/z2c3/ppermute | solution.py:230

commit v15 on v14

--- a/solution.py
+++ b/solution.py
@@ -87,62 +87,66 @@
     return out[:2], [list(out[2 + far * c : 2 + far * (c + 1)]) for c in range(len(chunks))]
 
 
-def turn_kernel(rows, c_ref, *refs):
+def turn_kernel(rows, n_mo, n_pair, place_ref, c_ref, *refs):
     out_ref = refs[-1]
-    n_mo, orbitals, padded = out_ref.shape
+    orbitals, padded = out_ref.shape[0], out_ref.shape[1] // n_mo
+    block = orbitals // n_pair
     none = jnp.zeros((padded - rows, orbitals), jnp.float32)
     for n in range(n_mo):
         part = c_ref[n * rows : (n + 1) * rows, :].astype(jnp.float32)
-        out_ref[n] = jnp.concatenate([part, none], axis=0).T.astype(jnp.bfloat16)
-
-
-def turn(coeffs, n_mo, padded, later, after):
+        part = jnp.concatenate([part, none], axis=0).T
+        columns = pl.ds(pl.multiple_of((place_ref[0] ^ n) * padded, padded), padded)
+        for o in range(n_pair):
+            lines = pl.ds(pl.multiple_of((place_ref[1] ^ o) * block, block), block)
+            out_ref[lines, columns] = part[o * block : (o + 1) * block].astype(jnp.bfloat16)
+
+
+def turn(place, coeffs, n_mo, n_pair, padded, later, after):
     depth, orbitals = coeffs.shape
     out = pl.pallas_call(
-        functools.partial(turn_kernel, depth // n_mo),
-        in_specs=[IN_VMEM] + [IN_HBM] * len(later) + [ANYWHERE] * len(after),
+        functools.partial(turn_kernel, depth // n_mo, n_mo, n_pair),
+        in_specs=[IN_SMEM, IN_VMEM] + [IN_HBM] * len(later) + [ANYWHERE] * len(after),
         out_specs=[IN_HBM] * len(later) + [IN_VMEM],
         out_shape=[jax.ShapeDtypeStruct(x.shape, x.dtype) for x in later]
-        + [jax.ShapeDtypeStruct((n_mo, orbitals, padded), jnp.bfloat16)],
-        input_output_aliases={1 + n: n for n in range(len(later))},
+        + [jax.ShapeDtypeStruct((orbitals, n_mo * padded), jnp.bfloat16)],
+        input_output_aliases={2 + n: n for n in range(len(later))},
         compiler_params=pltpu.CompilerParams(vmem_limit_bytes=24 * MIB),
         cost_estimate=COST,
         name="turn",
-    )(coeffs, *later, *after)
+    )(place, coeffs, *later, *after)
     return out[-1], list(out[:-1])
 
 
-def half_kernel(n_mo, first, owners, place_ref, *refs):
-    blocks, t_ref, held = refs[:n_mo], refs[n_mo], refs[-1]
-    outs = refs[-1 - len(owners) : -1]
+def half_kernel(first, owners, *refs):
+    n_mo = len(refs) - len(owners) - 1
+    blocks, t_ref, outs = refs[:n_mo], refs[n_mo], refs[n_mo + 1 :]
     kc, block, lanes = outs[0].shape[2:]
     firsts = [first if x.shape[0] > kc else 0 for x in blocks]
     columns = [jnp.concatenate([x[at + k] for k in range(kc)], axis=1) for x, at in zip(blocks, firsts)]
-    turned = [t_ref[place_ref[0] ^ o] for o in range(n_mo)]
-    held[...] = jnp.dot(
-        jnp.concatenate(turned, axis=1), jnp.concatenate(columns, axis=0), preferred_element_type=jnp.float32
-    )
+    half = jnp.dot(t_ref[...], jnp.concatenate(columns, axis=0), preferred_element_type=jnp.float32)
     for out, its in zip(outs, owners):
         for at, o in enumerate(its):
-            start = pl.multiple_of((place_ref[1] ^ o) * block, block)
             for k in range(kc):
-                out[0, at, k] = held[pl.ds(start, block), k * lanes : (k + 1) * lanes].astype(jnp.bfloat16)
-
-
-def half_of(place, blocks, turned, first, owners, after):
-    n_mo, orbitals, _ = turned.shape
+                piece = half[o * block : (o + 1) * block, k * lanes : (k + 1) * lanes]
+                out[0, at, k] = piece.astype(jnp.bfloat16)
+
+
+def half_kernel_after(n_blocks, n_after, first, owners, *refs):
+    half_kernel(first, owners, *refs[: n_blocks + 1], *refs[n_blocks + 1 + n_after :])
+
+
+def half_of(blocks, turned, first, owners, after):
     kc, _, lanes = blocks[-1].shape
-    block = orbitals // sum(len(its) for its in owners)
+    block = turned.shape[0] // sum(len(its) for its in owners)
     return pl.pallas_call(
-        functools.partial(half_kernel, n_mo, first, owners),
-        in_specs=[IN_SMEM] + [IN_VMEM] * (n_mo + 1) + [ANYWHERE] * len(after),
+        functools.partial(half_kernel_after, len(blocks), len(after), first, owners),
+        in_specs=[IN_VMEM] * (len(blocks) + 1) + [ANYWHERE] * len(after),
         out_specs=[IN_VMEM] * len(owners),
         out_shape=[jax.ShapeDtypeStruct((1, len(its), kc, block, lanes), jnp.bfloat16) for its in owners],
-        scratch_shapes=[pltpu.VMEM((orbitals, kc * lanes), jnp.float32)],
         compiler_params=pltpu.CompilerParams(vmem_limit_bytes=24 * MIB),
         cost_estimate=COST,
         name="half",
-    )(place, *blocks, turned, *after)
+    )(*blocks, turned, *after)
 
 
 def merge_kernel(n_parts, picks, *refs):
@@ -189,36 +193,43 @@
 
 
 def combine_kernel(sources, k_all, per_step, mirror_ref, place_ref, *refs):
-    pieces, out_ref, held = refs[: len(sources)], refs[-2], refs[-1]
-    step = pl.program_id(0)
-
-    @pl.when(step == 0)
-    def _():
-        for piece, (offsets, first) in zip(pieces, sources):
-            for n, offset in enumerate(offsets):
-                row = (place_ref[1] ^ offset) * k_all + first
-                held[pl.ds(row, piece.shape[2])] = piece[n, 0]
-
-    for n in range(per_step):
-        k = step * per_step + n
-        out_ref[n] = 0.5 * (held[k].astype(jnp.float32) + held[mirror_ref[k]].astype(jnp.float32))
+    pieces, (out_hbm, held, done, sems) = refs[: len(sources)], refs[-4:]
+    for piece, (offsets, first) in zip(pieces, sources):
+        for n, offset in enumerate(offsets):
+            row = (place_ref[1] ^ offset) * k_all + first
+            held[pl.ds(row, piece.shape[2])] = piece[n, 0]
+
+    def copy_of(step):
+        rows = pl.ds(step * per_step, per_step)
+        return pltpu.make_async_copy(done.at[rows], out_hbm.at[rows], sems.at[step])
+
+    @pl.loop(0, held.shape[0] // per_step)
+    def _(step):
+        for n in range(per_step):
+            k = step * per_step + n
+            done[k] = 0.5 * (held[k].astype(jnp.float32) + held[mirror_ref[k]].astype(jnp.float32))
+        copy_of(step).start()
+
+    @pl.loop(0, held.shape[0] // per_step)
+    def _(step):
+        copy_of(step).wait()
 
 
 def combine(pieces, sources, mirror, place, n_pair, after):
     block, lanes = pieces[0].shape[-2:]
     k_all = sum(CHUNKS)
     rows = n_pair * k_all
-    per_step = max(1, 32 * 64 // block)
+    per_step = max(1, 16 * 64 // block)
     return pl.pallas_call(
         functools.partial(combine_kernel, sources, k_all, per_step),
-        grid_spec=pltpu.PrefetchScalarGridSpec(
-            num_scalar_prefetch=2,
-            grid=(rows // per_step,),
-            in_specs=[IN_VMEM] * len(pieces) + [ANYWHERE] * len(after),
-            out_specs=pl.BlockSpec((per_step, block, lanes), lambda k, m, place: (k, 0, 0)),
-            scratch_shapes=[pltpu.VMEM((rows, block, lanes), jnp.bfloat16)],
-        ),
+        in_specs=[IN_SMEM] * 2 + [IN_VMEM] * len(pieces) + [ANYWHERE] * len(after),
+        out_specs=IN_HBM,
         out_shape=jax.ShapeDtypeStruct((rows, block, lanes), jnp.float32),
+        scratch_shapes=[
+            pltpu.VMEM((rows, block, lanes), jnp.bfloat16),
+            pltpu.VMEM((rows, block, lanes), jnp.float32),
+            pltpu.SemaphoreType.DMA((rows // per_step,)),
+        ],
         compiler_params=pltpu.CompilerParams(vmem_limit_bytes=24 * MIB),
         cost_estimate=COST,
         name="combine",
@@ -262,7 +273,7 @@
         return [flipped(x, "mo", n_mo, o, f"y{2 * c + o - 2}") for o, x in enumerate(queue[c], 2)]
 
     arrived = [arrive(0)]
-    turned, queue[1] = turn(coeffs, n_mo, padded, queue[1], arrived[0][:1] + token)
+    turned, queue[1] = turn(place, coeffs, n_mo, n_pair, padded, queue[1], arrived[0][:1] + token)
     arrived += [arrive(c) for c in range(1, last + 1)]
 
     levels = [digits(n_pair, sizes) for sizes in SIZES]
@@ -289,7 +300,7 @@
         kept, _, sent = plan(c, level)
         if level == 0:
             blocks = [*near[c][:2], *arrived[c]]
-            keep, *messages = half_of(place, blocks, turned, near[c][2], [kept, *sent], token)
+            keep, *messages = half_of(blocks, turned, near[c][2], [kept, *sent], token)
             parts[c], owners[c], offsets[c] = [keep], [kept], [[0]]
         else:
             picks = [[[its.index(o) for o in some] for its in owners[c]] for some in sent]

time: 89.6 us -> 88.6 us (0.989)
  Pallas kernels: 22.5 us -> 20.3 us
  waiting for transfers between devices: 30.5 us -> 31.8 us
    pallas_call x5, Pallas kernels: 5.59 us -> 3.83 us  [the longest x4 2.86 us: half_of(): pl.pallas_call(functools.partial(half_kernel_after, len(blocks), len(afte...]
    ppermute x24, waiting for transfers between devices: 30.5 us -> 31.8 us  [flipped(): return lax.ppermute(x, axis, [(i, i ^ offset) for i in range(size)])]
  transfers between devices with their start and end apart: 24 -> 24, of which waited for: 12 -> 13; matrix products, arithmetic and copies ran while one was open for 0% -> 0% of each run, Pallas kernels for 14% -> 12%
where the time goes in v15:
time: 88.6 us; the launch traced here: 88.5 us
  starting transfers between devices  36.2 us (41%)
  waiting for transfers between devices  31.8 us (36%)
  Pallas kernels  20.3 us (23%)
    ppermute x24, starting transfers between devices, flipped(): return lax.ppermute(x, axis, [(i, i ^ offset) for i in range(size)])  36.2 us
    ppermute x24, waiting for transfers between devices, flipped(): return lax.ppermute(x, axis, [(i, i ^ offset) for i in range(size)])  31.8 us
    pallas_call x2, Pallas kernels, quarter_of(): pl.pallas_call(functools.partial(quarter_kernel, batch, n_mo, blocks, len...  13.5 us
    pallas_call x4, Pallas kernels, half_of(): pl.pallas_call(functools.partial(half_kernel_after, len(blocks), len(afte...  2.86 us
    pallas_call x1, Pallas kernels, combine(): pl.pallas_call(functools.partial(combine_kernel, sources, k_all, per_step...  2.84 us
  transfers between devices with their start and end apart: 24, of which 13 were waited for; matrix products, arithmetic and copies ran while one was open for 0% of the time, Pallas kernels for 12%

profile of v15, /device:TPU:0, one launch (start us, length us, event | category | flops | bytes accessed | tf_op | source)
XLA Modules:
  0.0 88.5 jit_solution(8978031159618762548)
XLA Ops:
  0.0 0.1 pad_add_fusion.place_ref
  0.1 6.7 %quarter.2 = (bf16[8,256,128]{2,1,0:T(8,128)(2,1)S(1)}, bf16[8,256,128]{2,1,0:T(8,128)(2,1)S(1)}, bf16[4,256,128]{2,1,0:T(8,128)(2,1)S(1)}, bf16[4,256,128]{2,1,...) custom-call(s32[2]{0:T(128)S(1)} %pad_add_fusion.place_ref, ...), custom_call_target="tpu_custom_call" | custom-call | flops 1024 | bytes 1024 | tf_op jit(solution)/shard_map/quarter/pallas_call | solution.py:70
  6.8 0.5 collective-permute-start
  7.3 2.6 %collective-permute-start.1 = (bf16[4,256,128]{2,1,0:T(8,128)(2,1)S(1)}, bf16[4,256,128]{2,1,0:T(8,128)(2,1)S(1)}, u32[]{:S(2)}, u32[]{:S(2)}) collective-permute-start(bf16[4,256,128]{2,1,0:T(8,128)(2,1)S(1)} %get-tuple-element.36), channel_id=1, source_target_pairs={{0,2},{1,3},{2,0},{3,1},{4,6},{5,7},{6,4},{7,5},{8,10},{9,11},{10,... | collective-permute-start | bytes 786440 | tf_op jit(solution)/shard_map/y0/ppermute | solution.py:241
  9.9 0.1 collective-permute-start.2
  10.0 6.7 %quarter.3 = (bf16[8,256,128]{2,1,0:T(8,128)(2,1)S(1)}, bf16[8,256,128]{2,1,0:T(8,128)(2,1)S(1)}, bf16[4,256,128]{2,1,0:T(8,128)(2,1)S(1)}, bf16[4,256,128]{2,1,...) custom-call(s32[2]{0:T(128)S(1)} %pad_add_fusion.place_ref, ...), custom_call_target="tpu_custom_call" | custom-call | flops 1024 | bytes 1024 | tf_op jit(solution)/shard_map/quarter/pallas_call | solution.py:70
  16.7 0.3 collective-permute-done.1.refs_2_
  17.1 1.0 %turn.1 = (bf16[4,256,128]{2,1,0:T(8,128)(2,1)S(1)}, bf16[4,256,128]{2,1,0:T(8,128)(2,1)S(1)}, bf16[512,1024]{1,0:T(8,128)(2,1)S(1)}) custom-call(s32[2]{0:T(128)S(1)} %pad_add_fusion.place_ref, bf16[1000,512]{1,0:T(8,128)(2,1)S(1)} %copy-done, bf16[4,256,128]{2,1,0:T(8,128)(2,1)S(1)} %get-tuple-element.38.refs_0_, ...), custom_call_target="tpu_custom_call", output_to_operand_aliasing={{0}: (2, {}), {1}: (3, {})} | custom-call | flops 1024 | bytes 1024 | tf_op jit(solution)/shard_map/turn/pallas_call | solution.py:106
  18.1 2.0 %collective-permute-start.4 = (bf16[4,256,128]{2,1,0:T(8,128)(2,1)S(1)}, bf16[4,256,128]{2,1,0:T(8,128)(2,1)S(1)}, u32[]{:S(2)}, u32[]{:S(2)}) collective-permute-start(bf16[4,256,128]{2,1,0:T(8,128)(2,1)S(1)} %get-tuple-element.44), channel_id=1, source_target_pairs={{0,2},{1,3},{2,0},{3,1},{4,6},{5,7},{6,4},{7,5},{8,10},{9,11},{10,... | collective-permute-start | bytes 786440 | tf_op jit(solution)/shard_map/y2/ppermute | solution.py:241
  20.1 0.2 collective-permute-start.5
  20.3 1.9 %collective-permute-done.2.refs_3_ = bf16[4,256,128]{2,1,0:T(8,128)(2,1)S(1)} collective-permute-done((bf16[4,256,128]{2,1,0:T(8,128)(2,1)S(1)}, bf16[4,256,128]{2,1,0:T(8,128)(2,1)S(1)}, u32[]{:S(2)}, u32[]{:S(2)}) %collective-permute-start.2) | collective-permute-done | bytes 262176 | tf_op jit(solution)/shard_map/y1/ppermute | solution.py:241
  22.2 0.0 collective-permute-done.refs_1_
  22.2 0.7 half.4
  22.9 2.7 %collective-permute-start.3 = (bf16[1,4,4,64,128]{4,3,2,1,0:T(8,128)(2,1)S(1)}, bf16[1,4,4,64,128]{4,3,2,1,0:T(8,128)(2,1)S(1)}, u32[]{:S(2)}, u32[]{:S(2)}) collective-permute-start(bf16[1,4,4,64,128]{4,3,2,1,0:T(8,128)(2,1)S(1)} %get-tuple-element.43.refs_5_), channel_id=1, source_target_pairs={{0,16},{4,20},{8,24},{12,28},{16,0},{20,4},{24,8},{28,12},{1,17},{... | collective-permute-start | bytes 786440 | tf_op jit(solution)/shard_map/z4c0/ppermute | solution.py:241
  25.6 1.5 %collective-permute-start.9 = (bf16[4,256,128]{2,1,0:T(8,128)(2,1)S(1)}, bf16[4,256,128]{2,1,0:T(8,128)(2,1)S(1)}, u32[]{:S(2)}, u32[]{:S(2)}) collective-permute-start(bf16[4,256,128]{2,1,0:T(8,128)(2,1)S(1)} %get-tuple-element.49), channel_id=1, source_target_pairs={{0,2},{1,3},{2,0},{3,1},{4,6},{5,7},{6,4},{7,5},{8,10},{9,11},{10,... | collective-permute-start | bytes 786440 | tf_op jit(solution)/shard_map/y4/ppermute | solution.py:241
  27.1 1.2 %collective-permute-done.4.refs_2_ = bf16[4,256,128]{2,1,0:T(8,128)(2,1)S(1)} collective-permute-done((bf16[4,256,128]{2,1,0:T(8,128)(2,1)S(1)}, bf16[4,256,128]{2,1,0:T(8,128)(2,1)S(1)}, u32[]{:S(2)}, u32[]{:S(2)}) %collective-permute-start.4) | collective-permute-done | bytes 262176 | tf_op jit(solution)/shard_map/y2/ppermute | solution.py:241
  28.3 0.8 collective-permute-start.10
  29.1 4.3 %collective-permute-done.5.refs_3_ = bf16[4,256,128]{2,1,0:T(8,128)(2,1)S(1)} collective-permute-done((bf16[4,256,128]{2,1,0:T(8,128)(2,1)S(1)}, bf16[4,256,128]{2,1,0:T(8,128)(2,1)S(1)}, u32[]{:S(2)}, u32[]{:S(2)}) %collective-permute-start.5) | collective-permute-done | bytes 262176 | tf_op jit(solution)/shard_map/y3/ppermute | solution.py:241
  33.4 0.7 half.5
  34.1 2.7 %collective-permute-start.7 = (bf16[1,4,4,64,128]{4,3,2,1,0:T(8,128)(2,1)S(1)}, bf16[1,4,4,64,128]{4,3,2,1,0:T(8,128)(2,1)S(1)}, u32[]{:S(2)}, u32[]{:S(2)}) collective-permute-start(bf16[1,4,4,64,128]{4,3,2,1,0:T(8,128)(2,1)S(1)} %get-tuple-element.46.refs_2_), channel_id=1, source_target_pairs={{0,16},{4,20},{8,24},{12,28},{16,0},{20,4},{24,8},{28,12},{1,17},{... | collective-permute-start | bytes 786440 | tf_op jit(solution)/shard_map/z4c1/ppermute | solution.py:241
  36.8 1.6 %collective-permute-done.3.refs_1_ = bf16[1,4,4,64,128]{4,3,2,1,0:T(8,128)(2,1)S(1)} collective-permute-done((bf16[1,4,4,64,128]{4,3,2,1,0:T(8,128)(2,1)S(1)}, bf16[1,4,4,64,128]{4,3,2,1,0:T(8,128)(2,1)S(1)}, u32[]{:S(2)}, u32[]{:S(2)}) %collective-permute-start.3) | collective-permute-done | bytes 262176 | tf_op jit(solution)/shard_map/z4c0/ppermute | solution.py:241
  38.4 1.6 %collective-permute-start.11 = (bf16[4,256,128]{2,1,0:T(8,128)(2,1)S(1)}, bf16[4,256,128]{2,1,0:T(8,128)(2,1)S(1)}, u32[]{:S(2)}, u32[]{:S(2)}) collective-permute-start(bf16[4,256,128]{2,1,0:T(8,128)(2,1)S(1)} %get-tuple-element.52), channel_id=1, source_target_pairs={{0,2},{1,3},{2,0},{3,1},{4,6},{5,7},{6,4},{7,5},{8,10},{9,11},{10,... | collective-permute-start | bytes 786440 | tf_op jit(solution)/shard_map/y6/ppermute | solution.py:241
  40.0 0.0 collective-permute-done.9.refs_2_
  40.0 0.3 collective-permute-start.14
  40.3 4.3 %collective-permute-done.10.refs_3_ = bf16[4,256,128]{2,1,0:T(8,128)(2,1)S(1)} collective-permute-done((bf16[4,256,128]{2,1,0:T(8,128)(2,1)S(1)}, bf16[4,256,128]{2,1,0:T(8,128)(2,1)S(1)}, u32[]{:S(2)}, u32[]{:S(2)}) %collective-permute-start.10) | collective-permute-done | bytes 262176 | tf_op jit(solution)/shard_map/y5/ppermute | solution.py:241
  44.6 1.6 %collective-permute-start.6 = (bf16[2,2,4,64,128]{4,3,2,1,0:T(8,128)(2,1)S(1)}, bf16[2,2,4,64,128]{4,3,2,1,0:T(8,128)(2,1)S(1)}, u32[]{:S(2)}, u32[]{:S(2)}) collective-permute-start(bf16[2,2,4,64,128]{4,3,2,1,0:T(8,128)(2,1)S(1)} %merge.6.refs_5_), channel_id=1, source_target_pairs={{0,8},{4,12},{8,0},{12,4},{16,24},{20,28},{24,16},{28,20},{1,9},{5... | collective-permute-start | bytes 786440 | tf_op jit(solution)/shard_map/z2c0/ppermute | solution.py:241
  46.3 0.0 collective-permute-done.8.refs_1_
  46.3 0.7 half.6
  47.0 1.6 %collective-permute-start.15 = (bf16[1,4,4,64,128]{4,3,2,1,0:T(8,128)(2,1)S(1)}, bf16[1,4,4,64,128]{4,3,2,1,0:T(8,128)(2,1)S(1)}, u32[]{:S(2)}, u32[]{:S(2)}) collective-permute-start(bf16[1,4,4,64,128]{4,3,2,1,0:T(8,128)(2,1)S(1)} %get-tuple-element.51.refs_2_), channel_id=1, source_target_pairs={{0,4},{4,0},{8,12},{12,8},{16,20},{20,16},{24,28},{28,24},{1,5},{5... | collective-permute-start | bytes 786440 | tf_op jit(solution)/shard_map/z1c2/ppermute | solution.py:241
  48.6 1.2 %collective-permute-done.7.refs_1_.refs_5_ = bf16[1,4,4,64,128]{4,3,2,1,0:T(8,128)(2,1)S(1)} collective-permute-done((bf16[1,4,4,64,128]{4,3,2,1,0:T(8,128)(2,1)S(1)}, bf16[1,4,4,64,128]{4,3,2,1,0:T(8,128)(2,1)S(1)}, u32[]{:S(2)}, u32[]{:S(2)}) %collective-permute-start.7) | collective-permute-done | bytes 262176 | tf_op jit(solution)/shard_map/z4c1/ppermute | solution.py:241
  49.8 0.7 collective-permute-start.13
  50.5 0.3 collective-permute-done.11.refs_4_.refs_2_
  50.8 4.5 %collective-permute-done.6.refs_2_ = bf16[2,2,4,64,128]{4,3,2,1,0:T(8,128)(2,1)S(1)} collective-permute-done((bf16[2,2,4,64,128]{4,3,2,1,0:T(8,128)(2,1)S(1)}, bf16[2,2,4,64,128]{4,3,2,1,0:T(8,128)(2,1)S(1)}, u32[]{:S(2)}, u32[]{:S(2)}) %collective-permute-start.6) | collective-permute-done | bytes 262176 | tf_op jit(solution)/shard_map/z2c0/ppermute | solution.py:241
  55.3 1.8 %collective-permute-start.12 = (bf16[4,1,4,64,128]{4,3,2,1,0:T(8,128)(2,1)S(1)}, bf16[4,1,4,64,128]{4,3,2,1,0:T(8,128)(2,1)S(1)}, u32[]{:S(2)}, u32[]{:S(2)}) collective-permute-start(bf16[4,1,4,64,128]{4,3,2,1,0:T(8,128)(2,1)S(1)} %merge.8.refs_2_), channel_id=1, source_target_pairs={{0,4},{4,0},{8,12},{12,8},{16,20},{20,16},{24,28},{28,24},{1,5},{5... | collective-permute-start | bytes 786440 | tf_op jit(solution)/shard_map/z1c0/ppermute | solution.py:241
  57.2 0.7 half.7
  57.9 0.3 collective-permute-start.20
  58.3 2.7 %collective-permute-start.18 = (bf16[2,1,4,64,128]{4,3,2,1,0:T(8,128)(2,1)S(1)}, bf16[2,1,4,64,128]{4,3,2,1,0:T(8,128)(2,1)S(1)}, u32[]{:S(2)}, u32[]{:S(2)}) collective-permute-start(bf16[2,1,4,64,128]{4,3,2,1,0:T(8,128)(2,1)S(1)} %get-tuple-element.57), channel_id=1, source_target_pairs={{0,16},{4,20},{8,24},{12,28},{16,0},{20,4},{24,8},{28,12},{1,17},{... | collective-permute-start | bytes 393224 | tf_op jit(solution)/shard_map/z4c2/ppermute | solution.py:241
  60.9 1.3 %collective-permute-start.17 = (bf16[2,1,4,64,128]{4,3,2,1,0:T(8,128)(2,1)S(1)}, bf16[2,1,4,64,128]{4,3,2,1,0:T(8,128)(2,1)S(1)}, u32[]{:S(2)}, u32[]{:S(2)}) collective-permute-start(bf16[2,1,4,64,128]{4,3,2,1,0:T(8,128)(2,1)S(1)} %get-tuple-element.55.refs_5_), channel_id=1, source_target_pairs={{0,24},{4,28},{8,16},{12,20},{16,8},{20,12},{24,0},{28,4},{1,25},{... | collective-permute-start | bytes 393224 | tf_op jit(solution)/shard_map/z6c2/ppermute | solution.py:241
  62.2 1.1 %collective-permute-start.16 = (bf16[4,1,4,64,128]{4,3,2,1,0:T(8,128)(2,1)S(1)}, bf16[4,1,4,64,128]{4,3,2,1,0:T(8,128)(2,1)S(1)}, u32[]{:S(2)}, u32[]{:S(2)}) collective-permute-start(bf16[4,1,4,64,128]{4,3,2,1,0:T(8,128)(2,1)S(1)} %merge.10.refs_2_), channel_id=1, source_target_pairs={{0,4},{4,0},{8,12},{12,8},{16,20},{20,16},{24,28},{28,24},{1,5},{5... | collective-permute-start | bytes 786440 | tf_op jit(solution)/shard_map/z1c1/ppermute | solution.py:241
  63.3 1.2 %collective-permute-done.12.refs_3_ = bf16[4,1,4,64,128]{4,3,2,1,0:T(8,128)(2,1)S(1)} collective-permute-done((bf16[4,1,4,64,128]{4,3,2,1,0:T(8,128)(2,1)S(1)}, bf16[4,1,4,64,128]{4,3,2,1,0:T(8,128)(2,1)S(1)}, u32[]{:S(2)}, u32[]{:S(2)}) %collective-permute-start.12) | collective-permute-done | bytes 262176 | tf_op jit(solution)/shard_map/z1c0/ppermute | solution.py:241
  64.5 0.2 collective-permute-start.19
  64.8 5.4 %collective-permute-done.20.refs_1_.refs_14_ = bf16[1,4,4,64,128]{4,3,2,1,0:T(8,128)(2,1)S(1)} collective-permute-done((bf16[1,4,4,64,128]{4,3,2,1,0:T(8,128)(2,1)S(1)}, bf16[1,4,4,64,128]{4,3,2,1,0:T(8,128)(2,1)S(1)}, u32[]{:S(2)}, u32[]{:S(2)}) %collective-permute-start.20) | collective-permute-done | bytes 262176 | tf_op jit(solution)/shard_map/z1c3/ppermute | solution.py:241
  70.2 3.6 %collective-permute-start.21 = (bf16[2,1,4,64,128]{4,3,2,1,0:T(8,128)(2,1)S(1)}, bf16[2,1,4,64,128]{4,3,2,1,0:T(8,128)(2,1)S(1)}, u32[]{:S(2)}, u32[]{:S(2)}) collective-permute-start(bf16[2,1,4,64,128]{4,3,2,1,0:T(8,128)(2,1)S(1)} %get-tuple-element.60.refs_1_), channel_id=1, source_target_pairs={{0,24},{4,28},{8,16},{12,20},{16,8},{20,12},{24,0},{28,4},{1,25},{... | collective-permute-start | bytes 393224 | tf_op jit(solution)/shard_map/z6c3/ppermute | solution.py:241
  73.8 0.0 collective-permute-done.18.refs_0_.refs_11_
  73.8 6.3 %collective-permute-start.23 = (bf16[2,1,4,64,128]{4,3,2,1,0:T(8,128)(2,1)S(1)}, bf16[2,1,4,64,128]{4,3,2,1,0:T(8,128)(2,1)S(1)}, u32[]{:S(2)}, u32[]{:S(2)}) collective-permute-start(bf16[2,1,4,64,128]{4,3,2,1,0:T(8,128)(2,1)S(1)} %get-tuple-element.62), channel_id=1, source_target_pairs={{0,8},{4,12},{8,0},{12,4},{16,24},{20,28},{24,16},{28,20},{1,9},{5... | collective-permute-start | bytes 393224 | tf_op jit(solution)/shard_map/z2c3/ppermute | solution.py:241
  80.2 4.5 %collective-permute-done.22.refs_0_.refs_16_ = bf16[2,1,4,64,128]{4,3,2,1,0:T(8,128)(2,1)S(1)} collective-permute-done((bf16[2,1,4,64,128]{4,3,2,1,0:T(8,128)(2,1)S(1)}, bf16[2,1,4,64,128]{4,3,2,1,0:T(8,128)(2,1)S(1)}, u32[]{:S(2)}, u32[]{:S(2)}) %collective-permute-start.22) | collective-permute-done | bytes 131104 | tf_op jit(solution)/shard_map/z4c3/ppermute | solution.py:241
  84.7 0.9 %collective-permute-done.23.refs_0_.refs_17_ = bf16[2,1,4,64,128]{4,3,2,1,0:T(8,128)(2,1)S(1)} collective-permute-done((bf16[2,1,4,64,128]{4,3,2,1,0:T(8,128)(2,1)S(1)}, bf16[2,1,4,64,128]{4,3,2,1,0:T(8,128)(2,1)S(1)}, u32[]{:S(2)}, u32[]{:S(2)}) %collective-permute-start.23) | collective-permute-done | bytes 131104 | tf_op jit(solution)/shard_map/z2c3/ppermute | solution.py:241
  85.6 2.8 %combine.1 = f32[128,64,128]{2,1,0:T(8,128)} custom-call(s32[128]{0:T(128)S(1)} %copy-done.1, s32[2]{0:T(128)S(1)} %pad_add_fusion.place_ref, bf16[1,4,4,64,128]{4,3,2,1,0:T(8,128)(2,1)S(1)} %get-tuple-element.42.refs_0_, bf16[1,4,4,64,128]{4,3,2,1,0:T(8,128)(2,1)S(1)} %collective-permute-done.3.refs_1_, ...), custom_call_target="tpu_custom_call" | custom-call | flops 1024 | bytes 1024 | tf_op jit(solution)/shard_map/combine/pallas_call | solution.py:223
  (25 shorter events, 0.2 us)
Async XLA Ops:
  0.1 17.0 %copy-start = (bf16[1000,512]{1,0:T(8,128)(2,1)S(1)}, bf16[1000,512]{1,0:T(8,128)(2,1)}, u32[]{:S(2)}) copy-start(bf16[1000,512]{1,0:T(8,128)(2,1)} %c_ref.1) | copy-start | bytes 3072004
  6.8 15.4 %collective-permute-start = (bf16[8,256,128]{2,1,0:T(8,128)(2,1)S(1)}, bf16[8,256,128]{2,1,0:T(8,128)(2,1)S(1)}, u32[]{:S(2)}, u32[]{:S(2)}) collective-permute-start(bf16[8,256,128]{2,1,0:T(8,128)(2,1)S(1)} %get-tuple-element.35), channel_id=1, source_target_pairs={{0,1},{1,0},{2,3},{3,2},{4,5},{5,4},{6,7},{7,6},{8,9},{9,8},{10,11... | collective-permute-start | bytes 1572872 | tf_op jit(solution)/shard_map/beside0/ppermute | solution.py:241
  7.3 9.8 %collective-permute-start.1 = (bf16[4,256,128]{2,1,0:T(8,128)(2,1)S(1)}, bf16[4,256,128]{2,1,0:T(8,128)(2,1)S(1)}, u32[]{:S(2)}, u32[]{:S(2)}) collective-permute-start(bf16[4,256,128]{2,1,0:T(8,128)(2,1)S(1)} %get-tuple-element.36), channel_id=1, source_target_pairs={{0,2},{1,3},{2,0},{3,1},{4,6},{5,7},{6,4},{7,5},{8,10},{9,11},{10,... | collective-permute-start | bytes 786440 | tf_op jit(solution)/shard_map/y0/ppermute | solution.py:241
  9.9 12.3 %collective-permute-start.2 = (bf16[4,256,128]{2,1,0:T(8,128)(2,1)S(1)}, bf16[4,256,128]{2,1,0:T(8,128)(2,1)S(1)}, u32[]{:S(2)}, u32[]{:S(2)}) collective-permute-start(bf16[4,256,128]{2,1,0:T(8,128)(2,1)S(1)} %get-tuple-element.37), channel_id=1, source_target_pairs={{0,3},{1,2},{2,1},{3,0},{4,7},{5,6},{6,5},{7,4},{8,11},{9,10},{10,... | collective-permute-start | bytes 786440 | tf_op jit(solution)/shard_map/y1/ppermute | solution.py:241
  18.1 10.2 %collective-permute-start.4 = (bf16[4,256,128]{2,1,0:T(8,128)(2,1)S(1)}, bf16[4,256,128]{2,1,0:T(8,128)(2,1)S(1)}, u32[]{:S(2)}, u32[]{:S(2)}) collective-permute-start(bf16[4,256,128]{2,1,0:T(8,128)(2,1)S(1)} %get-tuple-element.44), channel_id=1, source_target_pairs={{0,2},{1,3},{2,0},{3,1},{4,6},{5,7},{6,4},{7,5},{8,10},{9,11},{10,... | collective-permute-start | bytes 786440 | tf_op jit(solution)/shard_map/y2/ppermute | solution.py:241
  20.1 26.2 %collective-permute-start.8 = (bf16[8,256,128]{2,1,0:T(8,128)(2,1)S(1)}, bf16[8,256,128]{2,1,0:T(8,128)(2,1)S(1)}, u32[]{:S(2)}, u32[]{:S(2)}) collective-permute-start(bf16[8,256,128]{2,1,0:T(8,128)(2,1)S(1)} %get-tuple-element.48), channel_id=1, source_target_pairs={{0,1},{1,0},{2,3},{3,2},{4,5},{5,4},{6,7},{7,6},{8,9},{9,8},{10,11... | collective-permute-start | bytes 1572872 | tf_op jit(solution)/shard_map/beside1/ppermute | solution.py:241
  20.1 13.3 %collective-permute-start.5 = (bf16[4,256,128]{2,1,0:T(8,128)(2,1)S(1)}, bf16[4,256,128]{2,1,0:T(8,128)(2,1)S(1)}, u32[]{:S(2)}, u32[]{:S(2)}) collective-permute-start(bf16[4,256,128]{2,1,0:T(8,128)(2,1)S(1)} %get-tuple-element.45), channel_id=1, source_target_pairs={{0,3},{1,2},{2,1},{3,0},{4,7},{5,6},{6,5},{7,4},{8,11},{9,10},{10,... | collective-permute-start | bytes 786440 | tf_op jit(solution)/shard_map/y3/ppermute | solution.py:241
  22.9 15.5 %collective-permute-start.3 = (bf16[1,4,4,64,128]{4,3,2,1,0:T(8,128)(2,1)S(1)}, bf16[1,4,4,64,128]{4,3,2,1,0:T(8,128)(2,1)S(1)}, u32[]{:S(2)}, u32[]{:S(2)}) collective-permute-start(bf16[1,4,4,64,128]{4,3,2,1,0:T(8,128)(2,1)S(1)} %get-tuple-element.43.refs_5_), channel_id=1, source_target_pairs={{0,16},{4,20},{8,24},{12,28},{16,0},{20,4},{24,8},{28,12},{1,17},{... | collective-permute-start | bytes 786440 | tf_op jit(solution)/shard_map/z4c0/ppermute | solution.py:241
  25.6 14.4 %collective-permute-start.9 = (bf16[4,256,128]{2,1,0:T(8,128)(2,1)S(1)}, bf16[4,256,128]{2,1,0:T(8,128)(2,1)S(1)}, u32[]{:S(2)}, u32[]{:S(2)}) collective-permute-start(bf16[4,256,128]{2,1,0:T(8,128)(2,1)S(1)} %get-tuple-element.49), channel_id=1, source_target_pairs={{0,2},{1,3},{2,0},{3,1},{4,6},{5,7},{6,4},{7,5},{8,10},{9,11},{10,... | collective-permute-start | bytes 786440 | tf_op jit(solution)/shard_map/y4/ppermute | solution.py:241
  28.3 57.3 %copy-start.1 = (s32[128]{0:T(128)S(1)}, s32[128]{0:T(128)}, u32[]{:S(2)}) copy-start(s32[128]{0:T(128)} %mirror_ref.1) | copy-start | bytes 1540
  28.3 16.3 %collective-permute-start.10 = (bf16[4,256,128]{2,1,0:T(8,128)(2,1)S(1)}, bf16[4,256,128]{2,1,0:T(8,128)(2,1)S(1)}, u32[]{:S(2)}, u32[]{:S(2)}) collective-permute-start(bf16[4,256,128]{2,1,0:T(8,128)(2,1)S(1)} %get-tuple-element.50), channel_id=1, source_target_pairs={{0,3},{1,2},{2,1},{3,0},{4,7},{5,6},{6,5},{7,4},{8,11},{9,10},{10,... | collective-permute-start | bytes 786440 | tf_op jit(solution)/shard_map/y5/ppermute | solution.py:241
  34.1 15.6 %collective-permute-start.7 = (bf16[1,4,4,64,128]{4,3,2,1,0:T(8,128)(2,1)S(1)}, bf16[1,4,4,64,128]{4,3,2,1,0:T(8,128)(2,1)S(1)}, u32[]{:S(2)}, u32[]{:S(2)}) collective-permute-start(bf16[1,4,4,64,128]{4,3,2,1,0:T(8,128)(2,1)S(1)} %get-tuple-element.46.refs_2_), channel_id=1, source_target_pairs={{0,16},{4,20},{8,24},{12,28},{16,0},{20,4},{24,8},{28,12},{1,17},{... | collective-permute-start | bytes 786440 | tf_op jit(solution)/shard_map/z4c1/ppermute | solution.py:241
  38.4 12.4 %collective-permute-start.11 = (bf16[4,256,128]{2,1,0:T(8,128)(2,1)S(1)}, bf16[4,256,128]{2,1,0:T(8,128)(2,1)S(1)}, u32[]{:S(2)}, u32[]{:S(2)}) collective-permute-start(bf16[4,256,128]{2,1,0:T(8,128)(2,1)S(1)} %get-tuple-element.52), channel_id=1, source_target_pairs={{0,2},{1,3},{2,0},{3,1},{4,6},{5,7},{6,4},{7,5},{8,10},{9,11},{10,... | collective-permute-start | bytes 786440 | tf_op jit(solution)/shard_map/y6/ppermute | solution.py:241
  40.0 17.1 %collective-permute-start.14 = (bf16[4,256,128]{2,1,0:T(8,128)(2,1)S(1)}, bf16[4,256,128]{2,1,0:T(8,128)(2,1)S(1)}, u32[]{:S(2)}, u32[]{:S(2)}) collective-permute-start(bf16[4,256,128]{2,1,0:T(8,128)(2,1)S(1)} %get-tuple-element.53), channel_id=1, source_target_pairs={{0,3},{1,2},{2,1},{3,0},{4,7},{5,6},{6,5},{7,4},{8,11},{9,10},{10,... | collective-permute-start | bytes 786440 | tf_op jit(solution)/shard_map/y7/ppermute | solution.py:241
  44.6 10.6 %collective-permute-start.6 = (bf16[2,2,4,64,128]{4,3,2,1,0:T(8,128)(2,1)S(1)}, bf16[2,2,4,64,128]{4,3,2,1,0:T(8,128)(2,1)S(1)}, u32[]{:S(2)}, u32[]{:S(2)}) collective-permute-start(bf16[2,2,4,64,128]{4,3,2,1,0:T(8,128)(2,1)S(1)} %merge.6.refs_5_), channel_id=1, source_target_pairs={{0,8},{4,12},{8,0},{12,4},{16,24},{20,28},{24,16},{28,20},{1,9},{5... | collective-permute-start | bytes 786440 | tf_op jit(solution)/shard_map/z2c0/ppermute | solution.py:241
  47.0 10.2 %collective-permute-start.15 = (bf16[1,4,4,64,128]{4,3,2,1,0:T(8,128)(2,1)S(1)}, bf16[1,4,4,64,128]{4,3,2,1,0:T(8,128)(2,1)S(1)}, u32[]{:S(2)}, u32[]{:S(2)}) collective-permute-start(bf16[1,4,4,64,128]{4,3,2,1,0:T(8,128)(2,1)S(1)} %get-tuple-element.51.refs_2_), channel_id=1, source_target_pairs={{0,4},{4,0},{8,12},{12,8},{16,20},{20,16},{24,28},{28,24},{1,5},{5... | collective-permute-start | bytes 786440 | tf_op jit(solution)/shard_map/z1c2/ppermute | solution.py:241
  49.8 12.4 %collective-permute-start.13 = (bf16[2,2,4,64,128]{4,3,2,1,0:T(8,128)(2,1)S(1)}, bf16[2,2,4,64,128]{4,3,2,1,0:T(8,128)(2,1)S(1)}, u32[]{:S(2)}, u32[]{:S(2)}) collective-permute-start(bf16[2,2,4,64,128]{4,3,2,1,0:T(8,128)(2,1)S(1)} %merge.7.refs_3_), channel_id=1, source_target_pairs={{0,8},{4,12},{8,0},{12,4},{16,24},{20,28},{24,16},{28,20},{1,9},{5... | collective-permute-start | bytes 786440 | tf_op jit(solution)/shard_map/z2c1/ppermute | solution.py:241
  55.3 9.2 %collective-permute-start.12 = (bf16[4,1,4,64,128]{4,3,2,1,0:T(8,128)(2,1)S(1)}, bf16[4,1,4,64,128]{4,3,2,1,0:T(8,128)(2,1)S(1)}, u32[]{:S(2)}, u32[]{:S(2)}) collective-permute-start(bf16[4,1,4,64,128]{4,3,2,1,0:T(8,128)(2,1)S(1)} %merge.8.refs_2_), channel_id=1, source_target_pairs={{0,4},{4,0},{8,12},{12,8},{16,20},{20,16},{24,28},{28,24},{1,5},{5... | collective-permute-start | bytes 786440 | tf_op jit(solution)/shard_map/z1c0/ppermute | solution.py:241
  57.9 12.2 %collective-permute-start.20 = (bf16[1,4,4,64,128]{4,3,2,1,0:T(8,128)(2,1)S(1)}, bf16[1,4,4,64,128]{4,3,2,1,0:T(8,128)(2,1)S(1)}, u32[]{:S(2)}, u32[]{:S(2)}) collective-permute-start(bf16[1,4,4,64,128]{4,3,2,1,0:T(8,128)(2,1)S(1)} %get-tuple-element.56.refs_3_), channel_id=1, source_target_pairs={{0,4},{4,0},{8,12},{12,8},{16,20},{20,16},{24,28},{28,24},{1,5},{5... | collective-permute-start | bytes 786440 | tf_op jit(solution)/shard_map/z1c3/ppermute | solution.py:241
  58.3 15.5 %collective-permute-start.18 = (bf16[2,1,4,64,128]{4,3,2,1,0:T(8,128)(2,1)S(1)}, bf16[2,1,4,64,128]{4,3,2,1,0:T(8,128)(2,1)S(1)}, u32[]{:S(2)}, u32[]{:S(2)}) collective-permute-start(bf16[2,1,4,64,128]{4,3,2,1,0:T(8,128)(2,1)S(1)} %get-tuple-element.57), channel_id=1, source_target_pairs={{0,16},{4,20},{8,24},{12,28},{16,0},{20,4},{24,8},{28,12},{1,17},{... | collective-permute-start | bytes 393224 | tf_op jit(solution)/shard_map/z4c2/ppermute | solution.py:241
  60.9 12.9 %collective-permute-start.17 = (bf16[2,1,4,64,128]{4,3,2,1,0:T(8,128)(2,1)S(1)}, bf16[2,1,4,64,128]{4,3,2,1,0:T(8,128)(2,1)S(1)}, u32[]{:S(2)}, u32[]{:S(2)}) collective-permute-start(bf16[2,1,4,64,128]{4,3,2,1,0:T(8,128)(2,1)S(1)} %get-tuple-element.55.refs_5_), channel_id=1, source_target_pairs={{0,24},{4,28},{8,16},{12,20},{16,8},{20,12},{24,0},{28,4},{1,25},{... | collective-permute-start | bytes 393224 | tf_op jit(solution)/shard_map/z6c2/ppermute | solution.py:241
  62.2 23.4 %collective-permute-start.16 = (bf16[4,1,4,64,128]{4,3,2,1,0:T(8,128)(2,1)S(1)}, bf16[4,1,4,64,128]{4,3,2,1,0:T(8,128)(2,1)S(1)}, u32[]{:S(2)}, u32[]{:S(2)}) collective-permute-start(bf16[4,1,4,64,128]{4,3,2,1,0:T(8,128)(2,1)S(1)} %merge.10.refs_2_), channel_id=1, source_target_pairs={{0,4},{4,0},{8,12},{12,8},{16,20},{20,16},{24,28},{28,24},{1,5},{5... | collective-permute-start | bytes 786440 | tf_op jit(solution)/shard_map/z1c1/ppermute | solution.py:241
  64.5 15.6 %collective-permute-start.19 = (bf16[2,1,4,64,128]{4,3,2,1,0:T(8,128)(2,1)S(1)}, bf16[2,1,4,64,128]{4,3,2,1,0:T(8,128)(2,1)S(1)}, u32[]{:S(2)}, u32[]{:S(2)}) collective-permute-start(bf16[2,1,4,64,128]{4,3,2,1,0:T(8,128)(2,1)S(1)} %get-tuple-element.58), channel_id=1, source_target_pairs={{0,8},{4,12},{8,0},{12,4},{16,24},{20,28},{24,16},{28,20},{1,9},{5... | collective-permute-start | bytes 393224 | tf_op jit(solution)/shard_map/z2c2/ppermute | solution.py:241
  70.2 9.9 %collective-permute-start.21 = (bf16[2,1,4,64,128]{4,3,2,1,0:T(8,128)(2,1)S(1)}, bf16[2,1,4,64,128]{4,3,2,1,0:T(8,128)(2,1)S(1)}, u32[]{:S(2)}, u32[]{:S(2)}) collective-permute-start(bf16[2,1,4,64,128]{4,3,2,1,0:T(8,128)(2,1)S(1)} %get-tuple-element.60.refs_1_), channel_id=1, source_target_pairs={{0,24},{4,28},{8,16},{12,20},{16,8},{20,12},{24,0},{28,4},{1,25},{... | collective-permute-start | bytes 393224 | tf_op jit(solution)/shard_map/z6c3/ppermute | solution.py:241
  73.8 10.9 %collective-permute-start.22 = (bf16[2,1,4,64,128]{4,3,2,1,0:T(8,128)(2,1)S(1)}, bf16[2,1,4,64,128]{4,3,2,1,0:T(8,128)(2,1)S(1)}, u32[]{:S(2)}, u32[]{:S(2)}) collective-permute-start(bf16[2,1,4,64,128]{4,3,2,1,0:T(8,128)(2,1)S(1)} %get-tuple-element.61), channel_id=1, source_target_pairs={{0,16},{4,20},{8,24},{12,28},{16,0},{20,4},{24,8},{28,12},{1,17},{... | collective-permute-start | bytes 393224 | tf_op jit(solution)/shard_map/z4c3/ppermute | solution.py:241
  73.8 11.8 %collective-permute-start.23 = (bf16[2,1,4,64,128]{4,3,2,1,0:T(8,128)(2,1)S(1)}, bf16[2,1,4,64,128]{4,3,2,1,0:T(8,128)(2,1)S(1)}, u32[]{:S(2)}, u32[]{:S(2)}) collective-permute-start(bf16[2,1,4,64,128]{4,3,2,1,0:T(8,128)(2,1)S(1)} %get-tuple-element.62), channel_id=1, source_target_pairs={{0,8},{4,12},{8,0},{12,4},{16,24},{20,28},{24,16},{28,20},{1,9},{5... | collective-permute-start | bytes 393224 | tf_op jit(solution)/shard_map/z2c3/ppermute | solution.py:241

commit v16 on v15

--- a/solution.py
+++ b/solution.py
@@ -9,7 +9,8 @@
 
 LANES = 128
 STEP = 64
-BATCHES = ((4, 4), (4, 4))
+LATER = {0: (2, [2, 3]), 1: (3, [2]), 2: (3, [3])}
+BATCHES = ((4, 4), (5, 3))
 CHUNKS = sum(BATCHES, ())
 SIZES = ((1,), (1,), (-1, 2), (-1, 2))
 PART = 256
@@ -131,22 +132,26 @@
                 out[0, at, k] = piece.astype(jnp.bfloat16)
 
 
-def half_kernel_after(n_blocks, n_after, first, owners, *refs):
-    half_kernel(first, owners, *refs[: n_blocks + 1], *refs[n_blocks + 1 + n_after :])
-
-
-def half_of(blocks, turned, first, owners, after):
+def half_kernel_after(n_blocks, n_outs, first, owners, *refs):
+    half_kernel(first, owners, *refs[: n_blocks + 1], *refs[len(refs) - n_outs :])
+
+
+def half_of(blocks, turned, first, owners, later, after):
     kc, _, lanes = blocks[-1].shape
     block = turned.shape[0] // sum(len(its) for its in owners)
-    return pl.pallas_call(
-        functools.partial(half_kernel_after, len(blocks), len(after), first, owners),
-        in_specs=[IN_VMEM] * (len(blocks) + 1) + [ANYWHERE] * len(after),
-        out_specs=[IN_VMEM] * len(owners),
-        out_shape=[jax.ShapeDtypeStruct((1, len(its), kc, block, lanes), jnp.bfloat16) for its in owners],
+    n = len(blocks) + 1
+    out = pl.pallas_call(
+        functools.partial(half_kernel_after, len(blocks), len(owners), first, owners),
+        in_specs=[IN_VMEM] * n + [IN_HBM] * len(later) + [ANYWHERE] * len(after),
+        out_specs=[IN_HBM] * len(later) + [IN_VMEM] * len(owners),
+        out_shape=[jax.ShapeDtypeStruct(x.shape, x.dtype) for x in later]
+        + [jax.ShapeDtypeStruct((1, len(its), kc, block, lanes), jnp.bfloat16) for its in owners],
+        input_output_aliases={n + m: m for m in range(len(later))},
         compiler_params=pltpu.CompilerParams(vmem_limit_bytes=24 * MIB),
         cost_estimate=COST,
         name="half",
-    )(*blocks, turned, *after)
+    )(*blocks, turned, *later, *after)
+    return list(out[len(later) :]), list(out[: len(later)])
 
 
 def merge_kernel(n_parts, picks, *refs):
@@ -269,12 +274,15 @@
         queue += far
         token = [own]
 
+    def fetch(c, o, x):
+        return flipped(x, "mo", n_mo, o, f"y{2 * c + o - 2}")
+
     def arrive(c):
-        return [flipped(x, "mo", n_mo, o, f"y{2 * c + o - 2}") for o, x in enumerate(queue[c], 2)]
+        return [fetch(c, o, x) for o, x in enumerate(queue[c], 2)]
 
     arrived = [arrive(0)]
     turned, queue[1] = turn(place, coeffs, n_mo, n_pair, padded, queue[1], arrived[0][:1] + token)
-    arrived += [arrive(c) for c in range(1, last + 1)]
+    arrived += [arrive(1)] + [[] for _ in range(2, last + 1)]
 
     levels = [digits(n_pair, sizes) for sizes in SIZES]
     steps = [(c, c, 0) for c in range(last + 1)]
@@ -300,16 +308,19 @@
         kept, _, sent = plan(c, level)
         if level == 0:
             blocks = [*near[c][:2], *arrived[c]]
-            keep, *messages = half_of(blocks, turned, near[c][2], [kept, *sent], token)
+            later, coming = LATER.get(c, (0, []))
+            wait = [queue[later][o - 2] for o in coming]
+            (keep, *messages), wait = half_of(blocks, turned, near[c][2], [kept, *sent], wait, token)
+            arrived[later] += [fetch(later, o, x) for o, x in zip(coming, wait)]
             parts[c], owners[c], offsets[c] = [keep], [kept], [[0]]
         else:
             picks = [[[its.index(o) for o in some] for its in owners[c]] for some in sent]
-            done = {(0, 2): arrived[last][:1], (last - 1, 1): arrived[last][1:], (last, 1): parts[0][-1:]}
+            done = {(1, 1): arrived[last][:1], (last, 1): parts[0][-1:] + parts[last - 1][-2:-1]}
             done = list(done.get((c, level), []))
             messages = merge(parts[c], picks, token + done)
         token = messages[:1]
         send(c, level, messages)
-    for x in parts[last - 1][-3:] + parts[last][-3:]:
+    for x in [parts[last - 1][-3], parts[last - 1][-1]] + parts[last][-3:]:
         token = [wait_for([x, *token])]
     pieces = [x for chunk in parts for x in chunk]
     sources = [(tuple(group), first) for chunk, first in zip(offsets, firsts) for group in chunk]

time: 88.6 us -> 92.1 us (1.040)
  waiting for transfers between devices: 31.8 us -> 38.2 us
  starting transfers between devices: 36.2 us -> 33 us
    ppermute x24, waiting for transfers between devices: 31.8 us -> 38.2 us  [flipped(): return lax.ppermute(x, axis, [(i, i ^ offset) for i in range(size)])]
    ppermute x24, starting transfers between devices: 36.2 us -> 33 us  [flipped(): return lax.ppermute(x, axis, [(i, i ^ offset) for i in range(size)])]
where the time goes in v16:
time: 92.1 us; the launch traced here: 91.9 us
  waiting for transfers between devices  38.2 us (41%)
  starting transfers between devices  33 us (36%)
  Pallas kernels  20.5 us (22%)
    ppermute x24, waiting for transfers between devices, flipped(): return lax.ppermute(x, axis, [(i, i ^ offset) for i in range(size)])  38.2 us
    ppermute x24, starting transfers between devices, flipped(): return lax.ppermute(x, axis, [(i, i ^ offset) for i in range(size)])  33 us
    pallas_call x2, Pallas kernels, quarter_of(): pl.pallas_call(functools.partial(quarter_kernel, batch, n_mo, blocks, len...  13.5 us
    pallas_call x4, Pallas kernels, half_of(): pl.pallas_call(functools.partial(half_kernel_after, len(blocks), len(owne...  3.12 us
    pallas_call x1, Pallas kernels, combine(): pl.pallas_call(functools.partial(combine_kernel, sources, k_all, per_step...  2.84 us
  transfers between devices with their start and end apart: 24, of which 13 were waited for; matrix products, arithmetic and copies ran while one was open for 0% of the time, Pallas kernels for 12%

profile of v16, /device:TPU:0, one launch (start us, length us, event | category | flops | bytes accessed | tf_op | source)
XLA Modules:
  0.0 91.9 jit_solution(31691998269657911)
XLA Ops:
  0.0 0.1 pad_add_fusion.place_ref
  0.1 6.7 %quarter.2 = (bf16[8,256,128]{2,1,0:T(8,128)(2,1)S(1)}, bf16[8,256,128]{2,1,0:T(8,128)(2,1)S(1)}, bf16[4,256,128]{2,1,0:T(8,128)(2,1)S(1)}, bf16[4,256,128]{2,1,...) custom-call(s32[2]{0:T(128)S(1)} %pad_add_fusion.place_ref, ...), custom_call_target="tpu_custom_call" | custom-call | flops 1024 | bytes 1024 | tf_op jit(solution)/shard_map/quarter/pallas_call | solution.py:71
  6.8 0.5 collective-permute-start
  7.3 2.6 %collective-permute-start.1 = (bf16[4,256,128]{2,1,0:T(8,128)(2,1)S(1)}, bf16[4,256,128]{2,1,0:T(8,128)(2,1)S(1)}, u32[]{:S(2)}, u32[]{:S(2)}) collective-permute-start(bf16[4,256,128]{2,1,0:T(8,128)(2,1)S(1)} %get-tuple-element.40), channel_id=1, source_target_pairs={{0,2},{1,3},{2,0},{3,1},{4,6},{5,7},{6,4},{7,5},{8,10},{9,11},{10,... | collective-permute-start | bytes 786440 | tf_op jit(solution)/shard_map/y0/ppermute | solution.py:246
  9.9 0.1 collective-permute-start.2
  10.0 6.7 %quarter.3 = (bf16[8,256,128]{2,1,0:T(8,128)(2,1)S(1)}, bf16[8,256,128]{2,1,0:T(8,128)(2,1)S(1)}, bf16[5,256,128]{2,1,0:T(8,128)(2,1)S(1)}, bf16[5,256,128]{2,1,...) custom-call(s32[2]{0:T(128)S(1)} %pad_add_fusion.place_ref, ...), custom_call_target="tpu_custom_call" | custom-call | flops 1024 | bytes 1024 | tf_op jit(solution)/shard_map/quarter/pallas_call | solution.py:71
  16.7 0.3 collective-permute-done.1.refs_2_
  17.1 1.0 %turn.1 = (bf16[4,256,128]{2,1,0:T(8,128)(2,1)S(1)}, bf16[4,256,128]{2,1,0:T(8,128)(2,1)S(1)}, bf16[512,1024]{1,0:T(8,128)(2,1)S(1)}) custom-call(s32[2]{0:T(128)S(1)} %pad_add_fusion.place_ref, bf16[1000,512]{1,0:T(8,128)(2,1)S(1)} %copy-done, bf16[4,256,128]{2,1,0:T(8,128)(2,1)S(1)} %get-tuple-element.42.refs_0_, ...), custom_call_target="tpu_custom_call", output_to_operand_aliasing={{0}: (2, {}), {1}: (3, {})} | custom-call | flops 1024 | bytes 1024 | tf_op jit(solution)/shard_map/turn/pallas_call | solution.py:107
  18.1 2.0 %collective-permute-start.4 = (bf16[4,256,128]{2,1,0:T(8,128)(2,1)S(1)}, bf16[4,256,128]{2,1,0:T(8,128)(2,1)S(1)}, u32[]{:S(2)}, u32[]{:S(2)}) collective-permute-start(bf16[4,256,128]{2,1,0:T(8,128)(2,1)S(1)} %get-tuple-element.50), channel_id=1, source_target_pairs={{0,2},{1,3},{2,0},{3,1},{4,6},{5,7},{6,4},{7,5},{8,10},{9,11},{10,... | collective-permute-start | bytes 786440 | tf_op jit(solution)/shard_map/y2/ppermute | solution.py:246
  20.1 0.0 collective-permute-start.8
  20.1 0.2 collective-permute-start.5
  20.3 1.9 %collective-permute-done.2.refs_3_ = bf16[4,256,128]{2,1,0:T(8,128)(2,1)S(1)} collective-permute-done((bf16[4,256,128]{2,1,0:T(8,128)(2,1)S(1)}, bf16[4,256,128]{2,1,0:T(8,128)(2,1)S(1)}, u32[]{:S(2)}, u32[]{:S(2)}) %collective-permute-start.2) | collective-permute-done | bytes 262176 | tf_op jit(solution)/shard_map/y1/ppermute | solution.py:246
  22.2 0.0 collective-permute-done.refs_1_
  22.2 0.7 half.4
  22.9 2.7 %collective-permute-start.3 = (bf16[1,4,4,64,128]{4,3,2,1,0:T(8,128)(2,1)S(1)}, bf16[1,4,4,64,128]{4,3,2,1,0:T(8,128)(2,1)S(1)}, u32[]{:S(2)}, u32[]{:S(2)}) collective-permute-start(bf16[1,4,4,64,128]{4,3,2,1,0:T(8,128)(2,1)S(1)} %get-tuple-element.49.refs_6_), channel_id=1, source_target_pairs={{0,16},{4,20},{8,24},{12,28},{16,0},{20,4},{24,8},{28,12},{1,17},{... | collective-permute-start | bytes 786440 | tf_op jit(solution)/shard_map/z4c0/ppermute | solution.py:246
  25.6 1.5 %collective-permute-start.9 = (bf16[5,256,128]{2,1,0:T(8,128)(2,1)S(1)}, bf16[5,256,128]{2,1,0:T(8,128)(2,1)S(1)}, u32[]{:S(2)}, u32[]{:S(2)}) collective-permute-start(bf16[5,256,128]{2,1,0:T(8,128)(2,1)S(1)} %get-tuple-element.56), channel_id=1, source_target_pairs={{0,2},{1,3},{2,0},{3,1},{4,6},{5,7},{6,4},{7,5},{8,10},{9,11},{10,... | collective-permute-start | bytes 983048 | tf_op jit(solution)/shard_map/y4/ppermute | solution.py:246
  27.1 1.2 %collective-permute-done.4.refs_2_ = bf16[4,256,128]{2,1,0:T(8,128)(2,1)S(1)} collective-permute-done((bf16[4,256,128]{2,1,0:T(8,128)(2,1)S(1)}, bf16[4,256,128]{2,1,0:T(8,128)(2,1)S(1)}, u32[]{:S(2)}, u32[]{:S(2)}) %collective-permute-start.4) | collective-permute-done | bytes 262176 | tf_op jit(solution)/shard_map/y2/ppermute | solution.py:246
  28.3 0.8 collective-permute-start.10
  29.1 4.3 %collective-permute-done.5.refs_3_ = bf16[4,256,128]{2,1,0:T(8,128)(2,1)S(1)} collective-permute-done((bf16[4,256,128]{2,1,0:T(8,128)(2,1)S(1)}, bf16[4,256,128]{2,1,0:T(8,128)(2,1)S(1)}, u32[]{:S(2)}, u32[]{:S(2)}) %collective-permute-start.5) | collective-permute-done | bytes 262176 | tf_op jit(solution)/shard_map/y3/ppermute | solution.py:246
  33.4 0.7 half.5
  34.1 2.7 %collective-permute-start.7 = (bf16[1,4,4,64,128]{4,3,2,1,0:T(8,128)(2,1)S(1)}, bf16[1,4,4,64,128]{4,3,2,1,0:T(8,128)(2,1)S(1)}, u32[]{:S(2)}, u32[]{:S(2)}) collective-permute-start(bf16[1,4,4,64,128]{4,3,2,1,0:T(8,128)(2,1)S(1)} %get-tuple-element.53.refs_2_), channel_id=1, source_target_pairs={{0,16},{4,20},{8,24},{12,28},{16,0},{20,4},{24,8},{28,12},{1,17},{... | collective-permute-start | bytes 786440 | tf_op jit(solution)/shard_map/z4c1/ppermute | solution.py:246
  36.8 1.6 %collective-permute-done.3.refs_1_ = bf16[1,4,4,64,128]{4,3,2,1,0:T(8,128)(2,1)S(1)} collective-permute-done((bf16[1,4,4,64,128]{4,3,2,1,0:T(8,128)(2,1)S(1)}, bf16[1,4,4,64,128]{4,3,2,1,0:T(8,128)(2,1)S(1)}, u32[]{:S(2)}, u32[]{:S(2)}) %collective-permute-start.3) | collective-permute-done | bytes 262176 | tf_op jit(solution)/shard_map/z4c0/ppermute | solution.py:246
  38.4 1.6 %collective-permute-start.11 = (bf16[3,256,128]{2,1,0:T(8,128)(2,1)S(1)}, bf16[3,256,128]{2,1,0:T(8,128)(2,1)S(1)}, u32[]{:S(2)}, u32[]{:S(2)}) collective-permute-start(bf16[3,256,128]{2,1,0:T(8,128)(2,1)S(1)} %get-tuple-element.60), channel_id=1, source_target_pairs={{0,2},{1,3},{2,0},{3,1},{4,6},{5,7},{6,4},{7,5},{8,10},{9,11},{10,... | collective-permute-start | bytes 589832 | tf_op jit(solution)/shard_map/y6/ppermute | solution.py:246
  40.0 0.8 collective-permute-start.6
  40.8 0.2 collective-permute-done.9.refs_2_
  41.0 6.5 %collective-permute-done.10.refs_3_ = bf16[5,256,128]{2,1,0:T(8,128)(2,1)S(1)} collective-permute-done((bf16[5,256,128]{2,1,0:T(8,128)(2,1)S(1)}, bf16[5,256,128]{2,1,0:T(8,128)(2,1)S(1)}, u32[]{:S(2)}, u32[]{:S(2)}) %collective-permute-start.10) | collective-permute-done | bytes 327712 | tf_op jit(solution)/shard_map/y5/ppermute | solution.py:246
  47.5 1.0 %half.6 = (bf16[3,256,128]{2,1,0:T(8,128)(2,1)S(1)}, bf16[1,4,5,64,128]{4,3,2,1,0:T(8,128)(2,1)S(1)}, bf16[1,4,5,64,128]{4,3,2,1,0:T(8,128)(2,1)S(1)}) custom-call(bf16[8,256,128]{2,1,0:T(8,128)(2,1)S(1)} %get-tuple-element.44.refs_3_.refs_0_, bf16[8,256,128]{2,1,0:T(8,128)(2,1)S(1)} %collective-permute-done.8.refs_1_, ...), custom_call_target="tpu_custom_call", output_to_operand_aliasing={{0}: (5, {})} | custom-call | flops 1024 | bytes 1024 | tf_op jit(solution)/shard_map/half/pallas_call | solution.py:143
  48.4 1.6 %collective-permute-start.15 = (bf16[1,4,5,64,128]{4,3,2,1,0:T(8,128)(2,1)S(1)}, bf16[1,4,5,64,128]{4,3,2,1,0:T(8,128)(2,1)S(1)}, u32[]{:S(2)}, u32[]{:S(2)}) collective-permute-start(bf16[1,4,5,64,128]{4,3,2,1,0:T(8,128)(2,1)S(1)} %get-tuple-element.59.refs_2_), channel_id=1, source_target_pairs={{0,4},{4,0},{8,12},{12,8},{16,20},{20,16},{24,28},{28,24},{1,5},{5... | collective-permute-start | bytes 983048 | tf_op jit(solution)/shard_map/z1c2/ppermute | solution.py:246
  50.1 1.9 %collective-permute-done.11.refs_3_.refs_2_ = bf16[3,256,128]{2,1,0:T(8,128)(2,1)S(1)} collective-permute-done((bf16[3,256,128]{2,1,0:T(8,128)(2,1)S(1)}, bf16[3,256,128]{2,1,0:T(8,128)(2,1)S(1)}, u32[]{:S(2)}, u32[]{:S(2)}) %collective-permute-start.11) | collective-permute-done | bytes 196640 | tf_op jit(solution)/shard_map/y6/ppermute | solution.py:246
  51.9 0.0 collective-permute-done.7.refs_1_.refs_5_
  52.0 1.9 %collective-permute-start.13 = (bf16[2,2,4,64,128]{4,3,2,1,0:T(8,128)(2,1)S(1)}, bf16[2,2,4,64,128]{4,3,2,1,0:T(8,128)(2,1)S(1)}, u32[]{:S(2)}, u32[]{:S(2)}) collective-permute-start(bf16[2,2,4,64,128]{4,3,2,1,0:T(8,128)(2,1)S(1)} %merge.7.refs_3_), channel_id=1, source_target_pairs={{0,8},{4,12},{8,0},{12,4},{16,24},{20,28},{24,16},{28,20},{1,9},{5... | collective-permute-start | bytes 786440 | tf_op jit(solution)/shard_map/z2c1/ppermute | solution.py:246
  53.8 0.5 collective-permute-start.14
  54.4 0.0 collective-permute-done.6.refs_2_
  54.4 1.6 %collective-permute-start.12 = (bf16[4,1,4,64,128]{4,3,2,1,0:T(8,128)(2,1)S(1)}, bf16[4,1,4,64,128]{4,3,2,1,0:T(8,128)(2,1)S(1)}, u32[]{:S(2)}, u32[]{:S(2)}) collective-permute-start(bf16[4,1,4,64,128]{4,3,2,1,0:T(8,128)(2,1)S(1)} %merge.8.refs_2_), channel_id=1, source_target_pairs={{0,4},{4,0},{8,12},{12,8},{16,20},{20,16},{24,28},{28,24},{1,5},{5... | collective-permute-start | bytes 786440 | tf_op jit(solution)/shard_map/z1c0/ppermute | solution.py:246
  55.9 3.2 %collective-permute-done.15.refs_1_.refs_9_ = bf16[1,4,5,64,128]{4,3,2,1,0:T(8,128)(2,1)S(1)} collective-permute-done((bf16[1,4,5,64,128]{4,3,2,1,0:T(8,128)(2,1)S(1)}, bf16[1,4,5,64,128]{4,3,2,1,0:T(8,128)(2,1)S(1)}, u32[]{:S(2)}, u32[]{:S(2)}) %collective-permute-start.15) | collective-permute-done | bytes 327712 | tf_op jit(solution)/shard_map/z1c2/ppermute | solution.py:246
  59.1 1.8 %collective-permute-done.14.refs_3_ = bf16[3,256,128]{2,1,0:T(8,128)(2,1)S(1)} collective-permute-done((bf16[3,256,128]{2,1,0:T(8,128)(2,1)S(1)}, bf16[3,256,128]{2,1,0:T(8,128)(2,1)S(1)}, u32[]{:S(2)}, u32[]{:S(2)}) %collective-permute-start.14) | collective-permute-done | bytes 196640 | tf_op jit(solution)/shard_map/y7/ppermute | solution.py:246
  61.0 0.7 half.7
  61.7 1.6 %collective-permute-start.20 = (bf16[1,4,3,64,128]{4,3,2,1,0:T(8,128)(2,1)S(1)}, bf16[1,4,3,64,128]{4,3,2,1,0:T(8,128)(2,1)S(1)}, u32[]{:S(2)}, u32[]{:S(2)}) collective-permute-start(bf16[1,4,3,64,128]{4,3,2,1,0:T(8,128)(2,1)S(1)} %get-tuple-element.64.refs_3_), channel_id=1, source_target_pairs={{0,4},{4,0},{8,12},{12,8},{16,20},{20,16},{24,28},{28,24},{1,5},{5... | collective-permute-start | bytes 589832 | tf_op jit(solution)/shard_map/z1c3/ppermute | solution.py:246
  63.2 2.6 %collective-permute-start.18 = (bf16[2,1,5,64,128]{4,3,2,1,0:T(8,128)(2,1)S(1)}, bf16[2,1,5,64,128]{4,3,2,1,0:T(8,128)(2,1)S(1)}, u32[]{:S(2)}, u32[]{:S(2)}) collective-permute-start(bf16[2,1,5,64,128]{4,3,2,1,0:T(8,128)(2,1)S(1)} %get-tuple-element.65), channel_id=1, source_target_pairs={{0,16},{4,20},{8,24},{12,28},{16,0},{20,4},{24,8},{28,12},{1,17},{... | collective-permute-start | bytes 491528 | tf_op jit(solution)/shard_map/z4c2/ppermute | solution.py:246
  65.8 0.2 collective-permute-start.17
  66.1 0.4 collective-permute-start.16
  66.5 0.9 collective-permute-start.19
  67.4 9.9 %collective-permute-done.18.refs_4_.refs_11_ = bf16[2,1,5,64,128]{4,3,2,1,0:T(8,128)(2,1)S(1)} collective-permute-done((bf16[2,1,5,64,128]{4,3,2,1,0:T(8,128)(2,1)S(1)}, bf16[2,1,5,64,128]{4,3,2,1,0:T(8,128)(2,1)S(1)}, u32[]{:S(2)}, u32[]{:S(2)}) %collective-permute-start.18) | collective-permute-done | bytes 163872 | tf_op jit(solution)/shard_map/z4c2/ppermute | solution.py:246
  77.2 3.6 %collective-permute-start.21 = (bf16[2,1,3,64,128]{4,3,2,1,0:T(8,128)(2,1)S(1)}, bf16[2,1,3,64,128]{4,3,2,1,0:T(8,128)(2,1)S(1)}, u32[]{:S(2)}, u32[]{:S(2)}) collective-permute-start(bf16[2,1,3,64,128]{4,3,2,1,0:T(8,128)(2,1)S(1)} %get-tuple-element.68.refs_1_), channel_id=1, source_target_pairs={{0,24},{4,28},{8,16},{12,20},{16,8},{20,12},{24,0},{28,4},{1,25},{... | collective-permute-start | bytes 294920 | tf_op jit(solution)/shard_map/z6c3/ppermute | solution.py:246
  80.9 2.7 %collective-permute-start.23 = (bf16[2,1,3,64,128]{4,3,2,1,0:T(8,128)(2,1)S(1)}, bf16[2,1,3,64,128]{4,3,2,1,0:T(8,128)(2,1)S(1)}, u32[]{:S(2)}, u32[]{:S(2)}) collective-permute-start(bf16[2,1,3,64,128]{4,3,2,1,0:T(8,128)(2,1)S(1)} %get-tuple-element.70), channel_id=1, source_target_pairs={{0,8},{4,12},{8,0},{12,4},{16,24},{20,28},{24,16},{28,20},{1,9},{5... | collective-permute-start | bytes 294920 | tf_op jit(solution)/shard_map/z2c3/ppermute | solution.py:246
  83.6 1.2 %collective-permute-done.21.refs_0_.refs_15_ = bf16[2,1,3,64,128]{4,3,2,1,0:T(8,128)(2,1)S(1)} collective-permute-done((bf16[2,1,3,64,128]{4,3,2,1,0:T(8,128)(2,1)S(1)}, bf16[2,1,3,64,128]{4,3,2,1,0:T(8,128)(2,1)S(1)}, u32[]{:S(2)}, u32[]{:S(2)}) %collective-permute-start.21) | collective-permute-done | bytes 98336 | tf_op jit(solution)/shard_map/z6c3/ppermute | solution.py:246
  84.8 4.2 %collective-permute-done.22.refs_0_.refs_16_ = bf16[2,1,3,64,128]{4,3,2,1,0:T(8,128)(2,1)S(1)} collective-permute-done((bf16[2,1,3,64,128]{4,3,2,1,0:T(8,128)(2,1)S(1)}, bf16[2,1,3,64,128]{4,3,2,1,0:T(8,128)(2,1)S(1)}, u32[]{:S(2)}, u32[]{:S(2)}) %collective-permute-start.22) | collective-permute-done | bytes 98336 | tf_op jit(solution)/shard_map/z4c3/ppermute | solution.py:246
  89.1 2.8 %combine.1 = f32[128,64,128]{2,1,0:T(8,128)} custom-call(s32[128]{0:T(128)S(1)} %copy-done.1, s32[2]{0:T(128)S(1)} %pad_add_fusion.place_ref, bf16[1,4,4,64,128]{4,3,2,1,0:T(8,128)(2,1)S(1)} %get-tuple-element.48.refs_0_, bf16[1,4,4,64,128]{4,3,2,1,0:T(8,128)(2,1)S(1)} %collective-permute-done.3.refs_1_, ...), custom_call_target="tpu_custom_call" | custom-call | flops 1024 | bytes 1024 | tf_op jit(solution)/shard_map/combine/pallas_call | solution.py:228
  (24 shorter events, 0.2 us)
Async XLA Ops:
  0.1 17.0 %copy-start = (bf16[1000,512]{1,0:T(8,128)(2,1)S(1)}, bf16[1000,512]{1,0:T(8,128)(2,1)}, u32[]{:S(2)}) copy-start(bf16[1000,512]{1,0:T(8,128)(2,1)} %c_ref.1) | copy-start | bytes 3072004
  6.8 15.4 %collective-permute-start = (bf16[8,256,128]{2,1,0:T(8,128)(2,1)S(1)}, bf16[8,256,128]{2,1,0:T(8,128)(2,1)S(1)}, u32[]{:S(2)}, u32[]{:S(2)}) collective-permute-start(bf16[8,256,128]{2,1,0:T(8,128)(2,1)S(1)} %get-tuple-element.39), channel_id=1, source_target_pairs={{0,1},{1,0},{2,3},{3,2},{4,5},{5,4},{6,7},{7,6},{8,9},{9,8},{10,11... | collective-permute-start | bytes 1572872 | tf_op jit(solution)/shard_map/beside0/ppermute | solution.py:246
  7.3 9.8 %collective-permute-start.1 = (bf16[4,256,128]{2,1,0:T(8,128)(2,1)S(1)}, bf16[4,256,128]{2,1,0:T(8,128)(2,1)S(1)}, u32[]{:S(2)}, u32[]{:S(2)}) collective-permute-start(bf16[4,256,128]{2,1,0:T(8,128)(2,1)S(1)} %get-tuple-element.40), channel_id=1, source_target_pairs={{0,2},{1,3},{2,0},{3,1},{4,6},{5,7},{6,4},{7,5},{8,10},{9,11},{10,... | collective-permute-start | bytes 786440 | tf_op jit(solution)/shard_map/y0/ppermute | solution.py:246
  9.9 12.3 %collective-permute-start.2 = (bf16[4,256,128]{2,1,0:T(8,128)(2,1)S(1)}, bf16[4,256,128]{2,1,0:T(8,128)(2,1)S(1)}, u32[]{:S(2)}, u32[]{:S(2)}) collective-permute-start(bf16[4,256,128]{2,1,0:T(8,128)(2,1)S(1)} %get-tuple-element.41), channel_id=1, source_target_pairs={{0,3},{1,2},{2,1},{3,0},{4,7},{5,6},{6,5},{7,4},{8,11},{9,10},{10,... | collective-permute-start | bytes 786440 | tf_op jit(solution)/shard_map/y1/ppermute | solution.py:246
  18.1 10.2 %collective-permute-start.4 = (bf16[4,256,128]{2,1,0:T(8,128)(2,1)S(1)}, bf16[4,256,128]{2,1,0:T(8,128)(2,1)S(1)}, u32[]{:S(2)}, u32[]{:S(2)}) collective-permute-start(bf16[4,256,128]{2,1,0:T(8,128)(2,1)S(1)} %get-tuple-element.50), channel_id=1, source_target_pairs={{0,2},{1,3},{2,0},{3,1},{4,6},{5,7},{6,4},{7,5},{8,10},{9,11},{10,... | collective-permute-start | bytes 786440 | tf_op jit(solution)/shard_map/y2/ppermute | solution.py:246
  20.1 19.9 %collective-permute-start.8 = (bf16[8,256,128]{2,1,0:T(8,128)(2,1)S(1)}, bf16[8,256,128]{2,1,0:T(8,128)(2,1)S(1)}, u32[]{:S(2)}, u32[]{:S(2)}) collective-permute-start(bf16[8,256,128]{2,1,0:T(8,128)(2,1)S(1)} %get-tuple-element.55), channel_id=1, source_target_pairs={{0,1},{1,0},{2,3},{3,2},{4,5},{5,4},{6,7},{7,6},{8,9},{9,8},{10,11... | collective-permute-start | bytes 1572872 | tf_op jit(solution)/shard_map/beside1/ppermute | solution.py:246
  20.1 13.3 %collective-permute-start.5 = (bf16[4,256,128]{2,1,0:T(8,128)(2,1)S(1)}, bf16[4,256,128]{2,1,0:T(8,128)(2,1)S(1)}, u32[]{:S(2)}, u32[]{:S(2)}) collective-permute-start(bf16[4,256,128]{2,1,0:T(8,128)(2,1)S(1)} %get-tuple-element.51), channel_id=1, source_target_pairs={{0,3},{1,2},{2,1},{3,0},{4,7},{5,6},{6,5},{7,4},{8,11},{9,10},{10,... | collective-permute-start | bytes 786440 | tf_op jit(solution)/shard_map/y3/ppermute | solution.py:246
  22.9 15.5 %collective-permute-start.3 = (bf16[1,4,4,64,128]{4,3,2,1,0:T(8,128)(2,1)S(1)}, bf16[1,4,4,64,128]{4,3,2,1,0:T(8,128)(2,1)S(1)}, u32[]{:S(2)}, u32[]{:S(2)}) collective-permute-start(bf16[1,4,4,64,128]{4,3,2,1,0:T(8,128)(2,1)S(1)} %get-tuple-element.49.refs_6_), channel_id=1, source_target_pairs={{0,16},{4,20},{8,24},{12,28},{16,0},{20,4},{24,8},{28,12},{1,17},{... | collective-permute-start | bytes 786440 | tf_op jit(solution)/shard_map/z4c0/ppermute | solution.py:246
  25.6 15.4 %collective-permute-start.9 = (bf16[5,256,128]{2,1,0:T(8,128)(2,1)S(1)}, bf16[5,256,128]{2,1,0:T(8,128)(2,1)S(1)}, u32[]{:S(2)}, u32[]{:S(2)}) collective-permute-start(bf16[5,256,128]{2,1,0:T(8,128)(2,1)S(1)} %get-tuple-element.56), channel_id=1, source_target_pairs={{0,2},{1,3},{2,0},{3,1},{4,6},{5,7},{6,4},{7,5},{8,10},{9,11},{10,... | collective-permute-start | bytes 983048 | tf_op jit(solution)/shard_map/y4/ppermute | solution.py:246
  28.3 19.1 %collective-permute-start.10 = (bf16[5,256,128]{2,1,0:T(8,128)(2,1)S(1)}, bf16[5,256,128]{2,1,0:T(8,128)(2,1)S(1)}, u32[]{:S(2)}, u32[]{:S(2)}) collective-permute-start(bf16[5,256,128]{2,1,0:T(8,128)(2,1)S(1)} %get-tuple-element.57), channel_id=1, source_target_pairs={{0,3},{1,2},{2,1},{3,0},{4,7},{5,6},{6,5},{7,4},{8,11},{9,10},{10,... | collective-permute-start | bytes 983048 | tf_op jit(solution)/shard_map/y5/ppermute | solution.py:246
  33.4 55.7 %copy-start.1 = (s32[128]{0:T(128)S(1)}, s32[128]{0:T(128)}, u32[]{:S(2)}) copy-start(s32[128]{0:T(128)} %mirror_ref.1) | copy-start | bytes 1540
  34.1 17.8 %collective-permute-start.7 = (bf16[1,4,4,64,128]{4,3,2,1,0:T(8,128)(2,1)S(1)}, bf16[1,4,4,64,128]{4,3,2,1,0:T(8,128)(2,1)S(1)}, u32[]{:S(2)}, u32[]{:S(2)}) collective-permute-start(bf16[1,4,4,64,128]{4,3,2,1,0:T(8,128)(2,1)S(1)} %get-tuple-element.53.refs_2_), channel_id=1, source_target_pairs={{0,16},{4,20},{8,24},{12,28},{16,0},{20,4},{24,8},{28,12},{1,17},{... | collective-permute-start | bytes 786440 | tf_op jit(solution)/shard_map/z4c1/ppermute | solution.py:246
  38.4 13.5 %collective-permute-start.11 = (bf16[3,256,128]{2,1,0:T(8,128)(2,1)S(1)}, bf16[3,256,128]{2,1,0:T(8,128)(2,1)S(1)}, u32[]{:S(2)}, u32[]{:S(2)}) collective-permute-start(bf16[3,256,128]{2,1,0:T(8,128)(2,1)S(1)} %get-tuple-element.60), channel_id=1, source_target_pairs={{0,2},{1,3},{2,0},{3,1},{4,6},{5,7},{6,4},{7,5},{8,10},{9,11},{10,... | collective-permute-start | bytes 589832 | tf_op jit(solution)/shard_map/y6/ppermute | solution.py:246
  40.0 14.3 %collective-permute-start.6 = (bf16[2,2,4,64,128]{4,3,2,1,0:T(8,128)(2,1)S(1)}, bf16[2,2,4,64,128]{4,3,2,1,0:T(8,128)(2,1)S(1)}, u32[]{:S(2)}, u32[]{:S(2)}) collective-permute-start(bf16[2,2,4,64,128]{4,3,2,1,0:T(8,128)(2,1)S(1)} %merge.6.refs_6_), channel_id=1, source_target_pairs={{0,8},{4,12},{8,0},{12,4},{16,24},{20,28},{24,16},{28,20},{1,9},{5... | collective-permute-start | bytes 786440 | tf_op jit(solution)/shard_map/z2c0/ppermute | solution.py:246
  48.4 10.7 %collective-permute-start.15 = (bf16[1,4,5,64,128]{4,3,2,1,0:T(8,128)(2,1)S(1)}, bf16[1,4,5,64,128]{4,3,2,1,0:T(8,128)(2,1)S(1)}, u32[]{:S(2)}, u32[]{:S(2)}) collective-permute-start(bf16[1,4,5,64,128]{4,3,2,1,0:T(8,128)(2,1)S(1)} %get-tuple-element.59.refs_2_), channel_id=1, source_target_pairs={{0,4},{4,0},{8,12},{12,8},{16,20},{20,16},{24,28},{28,24},{1,5},{5... | collective-permute-start | bytes 983048 | tf_op jit(solution)/shard_map/z1c2/ppermute | solution.py:246
  52.0 14.1 %collective-permute-start.13 = (bf16[2,2,4,64,128]{4,3,2,1,0:T(8,128)(2,1)S(1)}, bf16[2,2,4,64,128]{4,3,2,1,0:T(8,128)(2,1)S(1)}, u32[]{:S(2)}, u32[]{:S(2)}) collective-permute-start(bf16[2,2,4,64,128]{4,3,2,1,0:T(8,128)(2,1)S(1)} %merge.7.refs_3_), channel_id=1, source_target_pairs={{0,8},{4,12},{8,0},{12,4},{16,24},{20,28},{24,16},{28,20},{1,9},{5... | collective-permute-start | bytes 786440 | tf_op jit(solution)/shard_map/z2c1/ppermute | solution.py:246
  53.8 7.1 %collective-permute-start.14 = (bf16[3,256,128]{2,1,0:T(8,128)(2,1)S(1)}, bf16[3,256,128]{2,1,0:T(8,128)(2,1)S(1)}, u32[]{:S(2)}, u32[]{:S(2)}) collective-permute-start(bf16[3,256,128]{2,1,0:T(8,128)(2,1)S(1)} %get-tuple-element.61), channel_id=1, source_target_pairs={{0,3},{1,2},{2,1},{3,0},{4,7},{5,6},{6,5},{7,4},{8,11},{9,10},{10,... | collective-permute-start | bytes 589832 | tf_op jit(solution)/shard_map/y7/ppermute | solution.py:246
  54.4 12.1 %collective-permute-start.12 = (bf16[4,1,4,64,128]{4,3,2,1,0:T(8,128)(2,1)S(1)}, bf16[4,1,4,64,128]{4,3,2,1,0:T(8,128)(2,1)S(1)}, u32[]{:S(2)}, u32[]{:S(2)}) collective-permute-start(bf16[4,1,4,64,128]{4,3,2,1,0:T(8,128)(2,1)S(1)} %merge.8.refs_2_), channel_id=1, source_target_pairs={{0,4},{4,0},{8,12},{12,8},{16,20},{20,16},{24,28},{28,24},{1,5},{5... | collective-permute-start | bytes 786440 | tf_op jit(solution)/shard_map/z1c0/ppermute | solution.py:246
  61.7 15.5 %collective-permute-start.20 = (bf16[1,4,3,64,128]{4,3,2,1,0:T(8,128)(2,1)S(1)}, bf16[1,4,3,64,128]{4,3,2,1,0:T(8,128)(2,1)S(1)}, u32[]{:S(2)}, u32[]{:S(2)}) collective-permute-start(bf16[1,4,3,64,128]{4,3,2,1,0:T(8,128)(2,1)S(1)} %get-tuple-element.64.refs_3_), channel_id=1, source_target_pairs={{0,4},{4,0},{8,12},{12,8},{16,20},{20,16},{24,28},{28,24},{1,5},{5... | collective-permute-start | bytes 589832 | tf_op jit(solution)/shard_map/z1c3/ppermute | solution.py:246
  63.2 14.0 %collective-permute-start.18 = (bf16[2,1,5,64,128]{4,3,2,1,0:T(8,128)(2,1)S(1)}, bf16[2,1,5,64,128]{4,3,2,1,0:T(8,128)(2,1)S(1)}, u32[]{:S(2)}, u32[]{:S(2)}) collective-permute-start(bf16[2,1,5,64,128]{4,3,2,1,0:T(8,128)(2,1)S(1)} %get-tuple-element.65), channel_id=1, source_target_pairs={{0,16},{4,20},{8,24},{12,28},{16,0},{20,4},{24,8},{28,12},{1,17},{... | collective-permute-start | bytes 491528 | tf_op jit(solution)/shard_map/z4c2/ppermute | solution.py:246
  65.8 15.0 %collective-permute-start.17 = (bf16[2,1,5,64,128]{4,3,2,1,0:T(8,128)(2,1)S(1)}, bf16[2,1,5,64,128]{4,3,2,1,0:T(8,128)(2,1)S(1)}, u32[]{:S(2)}, u32[]{:S(2)}) collective-permute-start(bf16[2,1,5,64,128]{4,3,2,1,0:T(8,128)(2,1)S(1)} %get-tuple-element.63.refs_5_), channel_id=1, source_target_pairs={{0,24},{4,28},{8,16},{12,20},{16,8},{20,12},{24,0},{28,4},{1,25},{... | collective-permute-start | bytes 491528 | tf_op jit(solution)/shard_map/z6c2/ppermute | solution.py:246
  66.1 23.0 %collective-permute-start.16 = (bf16[4,1,4,64,128]{4,3,2,1,0:T(8,128)(2,1)S(1)}, bf16[4,1,4,64,128]{4,3,2,1,0:T(8,128)(2,1)S(1)}, u32[]{:S(2)}, u32[]{:S(2)}) collective-permute-start(bf16[4,1,4,64,128]{4,3,2,1,0:T(8,128)(2,1)S(1)} %merge.10.refs_2_), channel_id=1, source_target_pairs={{0,4},{4,0},{8,12},{12,8},{16,20},{20,16},{24,28},{28,24},{1,5},{5... | collective-permute-start | bytes 786440 | tf_op jit(solution)/shard_map/z1c1/ppermute | solution.py:246
  66.5 17.2 %collective-permute-start.19 = (bf16[2,1,5,64,128]{4,3,2,1,0:T(8,128)(2,1)S(1)}, bf16[2,1,5,64,128]{4,3,2,1,0:T(8,128)(2,1)S(1)}, u32[]{:S(2)}, u32[]{:S(2)}) collective-permute-start(bf16[2,1,5,64,128]{4,3,2,1,0:T(8,128)(2,1)S(1)} %get-tuple-element.66), channel_id=1, source_target_pairs={{0,8},{4,12},{8,0},{12,4},{16,24},{20,28},{24,16},{28,20},{1,9},{5... | collective-permute-start | bytes 491528 | tf_op jit(solution)/shard_map/z2c2/ppermute | solution.py:246
  77.2 7.6 %collective-permute-start.21 = (bf16[2,1,3,64,128]{4,3,2,1,0:T(8,128)(2,1)S(1)}, bf16[2,1,3,64,128]{4,3,2,1,0:T(8,128)(2,1)S(1)}, u32[]{:S(2)}, u32[]{:S(2)}) collective-permute-start(bf16[2,1,3,64,128]{4,3,2,1,0:T(8,128)(2,1)S(1)} %get-tuple-element.68.refs_1_), channel_id=1, source_target_pairs={{0,24},{4,28},{8,16},{12,20},{16,8},{20,12},{24,0},{28,4},{1,25},{... | collective-permute-start | bytes 294920 | tf_op jit(solution)/shard_map/z6c3/ppermute | solution.py:246
  80.9 8.2 %collective-permute-start.22 = (bf16[2,1,3,64,128]{4,3,2,1,0:T(8,128)(2,1)S(1)}, bf16[2,1,3,64,128]{4,3,2,1,0:T(8,128)(2,1)S(1)}, u32[]{:S(2)}, u32[]{:S(2)}) collective-permute-start(bf16[2,1,3,64,128]{4,3,2,1,0:T(8,128)(2,1)S(1)} %get-tuple-element.69), channel_id=1, source_target_pairs={{0,16},{4,20},{8,24},{12,28},{16,0},{20,4},{24,8},{28,12},{1,17},{... | collective-permute-start | bytes 294920 | tf_op jit(solution)/shard_map/z4c3/ppermute | solution.py:246
  80.9 8.2 %collective-permute-start.23 = (bf16[2,1,3,64,128]{4,3,2,1,0:T(8,128)(2,1)S(1)}, bf16[2,1,3,64,128]{4,3,2,1,0:T(8,128)(2,1)S(1)}, u32[]{:S(2)}, u32[]{:S(2)}) collective-permute-start(bf16[2,1,3,64,128]{4,3,2,1,0:T(8,128)(2,1)S(1)} %get-tuple-element.70), channel_id=1, source_target_pairs={{0,8},{4,12},{8,0},{12,4},{16,24},{20,28},{24,16},{28,20},{1,9},{5... | collective-permute-start | bytes 294920 | tf_op jit(solution)/shard_map/z2c3/ppermute | solution.py:246

commit v17 on v16

--- a/solution.py
+++ b/solution.py
@@ -10,7 +10,7 @@
 LANES = 128
 STEP = 64
 LATER = {0: (2, [2, 3]), 1: (3, [2]), 2: (3, [3])}
-BATCHES = ((4, 4), (5, 3))
+BATCHES = ((4, 4), (4, 4))
 CHUNKS = sum(BATCHES, ())
 SIZES = ((1,), (1,), (-1, 2), (-1, 2))
 PART = 256
@@ -315,12 +315,12 @@
             parts[c], owners[c], offsets[c] = [keep], [kept], [[0]]
         else:
             picks = [[[its.index(o) for o in some] for its in owners[c]] for some in sent]
-            done = {(1, 1): arrived[last][:1], (last, 1): parts[0][-1:] + parts[last - 1][-2:-1]}
+            done = {(1, 1): arrived[last][:1], (last, 1): parts[0][-1:]}
             done = list(done.get((c, level), []))
             messages = merge(parts[c], picks, token + done)
         token = messages[:1]
         send(c, level, messages)
-    for x in [parts[last - 1][-3], parts[last - 1][-1]] + parts[last][-3:]:
+    for x in parts[last - 1][-3:] + parts[last][-3:]:
         token = [wait_for([x, *token])]
     pieces = [x for chunk in parts for x in chunk]
     sources = [(tuple(group), first) for chunk, first in zip(offsets, firsts) for group in chunk]

time: 92.1 us -> 89.1 us (0.967)
  waiting for transfers between devices: 38.2 us -> 29.1 us
  starting transfers between devices: 33 us -> 39.4 us
    ppermute x24, waiting for transfers between devices: 38.2 us -> 29.1 us  [flipped(): return lax.ppermute(x, axis, [(i, i ^ offset) for i in range(size)])]
    ppermute x24, starting transfers between devices: 33 us -> 39.4 us  [flipped(): return lax.ppermute(x, axis, [(i, i ^ offset) for i in range(size)])]
  transfers between devices with their start and end apart: 24 -> 24, of which waited for: 13 -> 14; matrix products, arithmetic and copies ran while one was open for 0% -> 0% of each run, Pallas kernels for 12% -> 12%
where the time goes in v17:
time: 89.1 us; the launch traced here: 88.9 us
  starting transfers between devices  39.4 us (44%)
  waiting for transfers between devices  29.1 us (33%)
  Pallas kernels  20.3 us (23%)
    ppermute x24, starting transfers between devices, flipped(): return lax.ppermute(x, axis, [(i, i ^ offset) for i in range(size)])  39.4 us
    ppermute x24, waiting for transfers between devices, flipped(): return lax.ppermute(x, axis, [(i, i ^ offset) for i in range(size)])  29.1 us
    pallas_call x2, Pallas kernels, quarter_of(): pl.pallas_call(functools.partial(quarter_kernel, batch, n_mo, blocks, len...  13.5 us
    pallas_call x4, Pallas kernels, half_of(): pl.pallas_call(functools.partial(half_kernel_after, len(blocks), len(owne...  2.86 us
    pallas_call x1, Pallas kernels, combine(): pl.pallas_call(functools.partial(combine_kernel, sources, k_all, per_step...  2.84 us
  transfers between devices with their start and end apart: 24, of which 14 were waited for; matrix products, arithmetic and copies ran while one was open for 0% of the time, Pallas kernels for 12%

profile of v17, /device:TPU:0, one launch (start us, length us, event | category | flops | bytes accessed | tf_op | source)
XLA Modules:
  0.0 88.9 jit_solution(14163902924586537421)
XLA Ops:
  0.0 0.1 pad_add_fusion.place_ref
  0.1 6.7 %quarter.2 = (bf16[8,256,128]{2,1,0:T(8,128)(2,1)S(1)}, bf16[8,256,128]{2,1,0:T(8,128)(2,1)S(1)}, bf16[4,256,128]{2,1,0:T(8,128)(2,1)S(1)}, bf16[4,256,128]{2,1,...) custom-call(s32[2]{0:T(128)S(1)} %pad_add_fusion.place_ref, ...), custom_call_target="tpu_custom_call" | custom-call | flops 1024 | bytes 1024 | tf_op jit(solution)/shard_map/quarter/pallas_call | solution.py:71
  6.8 0.5 collective-permute-start
  7.3 2.6 %collective-permute-start.1 = (bf16[4,256,128]{2,1,0:T(8,128)(2,1)S(1)}, bf16[4,256,128]{2,1,0:T(8,128)(2,1)S(1)}, u32[]{:S(2)}, u32[]{:S(2)}) collective-permute-start(bf16[4,256,128]{2,1,0:T(8,128)(2,1)S(1)} %get-tuple-element.40), channel_id=1, source_target_pairs={{0,2},{1,3},{2,0},{3,1},{4,6},{5,7},{6,4},{7,5},{8,10},{9,11},{10,... | collective-permute-start | bytes 786440 | tf_op jit(solution)/shard_map/y0/ppermute | solution.py:246
  9.9 0.1 collective-permute-start.2
  10.0 6.7 %quarter.3 = (bf16[8,256,128]{2,1,0:T(8,128)(2,1)S(1)}, bf16[8,256,128]{2,1,0:T(8,128)(2,1)S(1)}, bf16[4,256,128]{2,1,0:T(8,128)(2,1)S(1)}, bf16[4,256,128]{2,1,...) custom-call(s32[2]{0:T(128)S(1)} %pad_add_fusion.place_ref, ...), custom_call_target="tpu_custom_call" | custom-call | flops 1024 | bytes 1024 | tf_op jit(solution)/shard_map/quarter/pallas_call | solution.py:71
  16.7 0.2 collective-permute-start.8
  16.9 0.2 collective-permute-done.1.refs_2_
  17.1 1.0 %turn.1 = (bf16[4,256,128]{2,1,0:T(8,128)(2,1)S(1)}, bf16[4,256,128]{2,1,0:T(8,128)(2,1)S(1)}, bf16[512,1024]{1,0:T(8,128)(2,1)S(1)}) custom-call(s32[2]{0:T(128)S(1)} %pad_add_fusion.place_ref, bf16[1000,512]{1,0:T(8,128)(2,1)S(1)} %copy-done, bf16[4,256,128]{2,1,0:T(8,128)(2,1)S(1)} %get-tuple-element.42.refs_0_, ...), custom_call_target="tpu_custom_call", output_to_operand_aliasing={{0}: (2, {}), {1}: (3, {})} | custom-call | flops 1024 | bytes 1024 | tf_op jit(solution)/shard_map/turn/pallas_call | solution.py:107
  18.1 2.0 %collective-permute-start.4 = (bf16[4,256,128]{2,1,0:T(8,128)(2,1)S(1)}, bf16[4,256,128]{2,1,0:T(8,128)(2,1)S(1)}, u32[]{:S(2)}, u32[]{:S(2)}) collective-permute-start(bf16[4,256,128]{2,1,0:T(8,128)(2,1)S(1)} %get-tuple-element.50), channel_id=1, source_target_pairs={{0,2},{1,3},{2,0},{3,1},{4,6},{5,7},{6,4},{7,5},{8,10},{9,11},{10,... | collective-permute-start | bytes 786440 | tf_op jit(solution)/shard_map/y2/ppermute | solution.py:246
  20.1 2.1 %collective-permute-done.2.refs_3_ = bf16[4,256,128]{2,1,0:T(8,128)(2,1)S(1)} collective-permute-done((bf16[4,256,128]{2,1,0:T(8,128)(2,1)S(1)}, bf16[4,256,128]{2,1,0:T(8,128)(2,1)S(1)}, u32[]{:S(2)}, u32[]{:S(2)}) %collective-permute-start.2) | collective-permute-done | bytes 262176 | tf_op jit(solution)/shard_map/y1/ppermute | solution.py:246
  22.2 0.7 half.4
  22.9 2.7 %collective-permute-start.3 = (bf16[1,4,4,64,128]{4,3,2,1,0:T(8,128)(2,1)S(1)}, bf16[1,4,4,64,128]{4,3,2,1,0:T(8,128)(2,1)S(1)}, u32[]{:S(2)}, u32[]{:S(2)}) collective-permute-start(bf16[1,4,4,64,128]{4,3,2,1,0:T(8,128)(2,1)S(1)} %get-tuple-element.49.refs_6_), channel_id=1, source_target_pairs={{0,16},{4,20},{8,24},{12,28},{16,0},{20,4},{24,8},{28,12},{1,17},{... | collective-permute-start | bytes 786440 | tf_op jit(solution)/shard_map/z4c0/ppermute | solution.py:246
  25.6 1.5 %collective-permute-start.9 = (bf16[4,256,128]{2,1,0:T(8,128)(2,1)S(1)}, bf16[4,256,128]{2,1,0:T(8,128)(2,1)S(1)}, u32[]{:S(2)}, u32[]{:S(2)}) collective-permute-start(bf16[4,256,128]{2,1,0:T(8,128)(2,1)S(1)} %get-tuple-element.56), channel_id=1, source_target_pairs={{0,2},{1,3},{2,0},{3,1},{4,6},{5,7},{6,4},{7,5},{8,10},{9,11},{10,... | collective-permute-start | bytes 786440 | tf_op jit(solution)/shard_map/y4/ppermute | solution.py:246
  27.1 1.2 %collective-permute-done.4.refs_2_ = bf16[4,256,128]{2,1,0:T(8,128)(2,1)S(1)} collective-permute-done((bf16[4,256,128]{2,1,0:T(8,128)(2,1)S(1)}, bf16[4,256,128]{2,1,0:T(8,128)(2,1)S(1)}, u32[]{:S(2)}, u32[]{:S(2)}) %collective-permute-start.4) | collective-permute-done | bytes 262176 | tf_op jit(solution)/shard_map/y2/ppermute | solution.py:246
  28.3 0.8 collective-permute-start.10
  29.1 4.3 %collective-permute-done.5.refs_3_ = bf16[4,256,128]{2,1,0:T(8,128)(2,1)S(1)} collective-permute-done((bf16[4,256,128]{2,1,0:T(8,128)(2,1)S(1)}, bf16[4,256,128]{2,1,0:T(8,128)(2,1)S(1)}, u32[]{:S(2)}, u32[]{:S(2)}) %collective-permute-start.5) | collective-permute-done | bytes 262176 | tf_op jit(solution)/shard_map/y3/ppermute | solution.py:246
  33.4 0.7 half.5
  34.1 1.6 %collective-permute-start.11 = (bf16[4,256,128]{2,1,0:T(8,128)(2,1)S(1)}, bf16[4,256,128]{2,1,0:T(8,128)(2,1)S(1)}, u32[]{:S(2)}, u32[]{:S(2)}) collective-permute-start(bf16[4,256,128]{2,1,0:T(8,128)(2,1)S(1)} %get-tuple-element.60), channel_id=1, source_target_pairs={{0,2},{1,3},{2,0},{3,1},{4,6},{5,7},{6,4},{7,5},{8,10},{9,11},{10,... | collective-permute-start | bytes 786440 | tf_op jit(solution)/shard_map/y6/ppermute | solution.py:246
  35.8 2.7 %collective-permute-done.3.refs_1_ = bf16[1,4,4,64,128]{4,3,2,1,0:T(8,128)(2,1)S(1)} collective-permute-done((bf16[1,4,4,64,128]{4,3,2,1,0:T(8,128)(2,1)S(1)}, bf16[1,4,4,64,128]{4,3,2,1,0:T(8,128)(2,1)S(1)}, u32[]{:S(2)}, u32[]{:S(2)}) %collective-permute-start.3) | collective-permute-done | bytes 262176 | tf_op jit(solution)/shard_map/z4c0/ppermute | solution.py:246
  38.4 0.0 collective-permute-start.7
  38.4 0.0 collective-permute-done.8.refs_1_
  38.5 4.2 %collective-permute-start.6 = (bf16[2,2,4,64,128]{4,3,2,1,0:T(8,128)(2,1)S(1)}, bf16[2,2,4,64,128]{4,3,2,1,0:T(8,128)(2,1)S(1)}, u32[]{:S(2)}, u32[]{:S(2)}) collective-permute-start(bf16[2,2,4,64,128]{4,3,2,1,0:T(8,128)(2,1)S(1)} %merge.6.refs_6_), channel_id=1, source_target_pairs={{0,8},{4,12},{8,0},{12,4},{16,24},{20,28},{24,16},{28,20},{1,9},{5... | collective-permute-start | bytes 786440 | tf_op jit(solution)/shard_map/z2c0/ppermute | solution.py:246
  42.6 2.0 %collective-permute-done.10.refs_3_ = bf16[4,256,128]{2,1,0:T(8,128)(2,1)S(1)} collective-permute-done((bf16[4,256,128]{2,1,0:T(8,128)(2,1)S(1)}, bf16[4,256,128]{2,1,0:T(8,128)(2,1)S(1)}, u32[]{:S(2)}, u32[]{:S(2)}) %collective-permute-start.10) | collective-permute-done | bytes 262176 | tf_op jit(solution)/shard_map/y5/ppermute | solution.py:246
  44.6 0.7 half.6
  45.4 1.6 %collective-permute-start.15 = (bf16[1,4,4,64,128]{4,3,2,1,0:T(8,128)(2,1)S(1)}, bf16[1,4,4,64,128]{4,3,2,1,0:T(8,128)(2,1)S(1)}, u32[]{:S(2)}, u32[]{:S(2)}) collective-permute-start(bf16[1,4,4,64,128]{4,3,2,1,0:T(8,128)(2,1)S(1)} %get-tuple-element.59.refs_2_), channel_id=1, source_target_pairs={{0,4},{4,0},{8,12},{12,8},{16,20},{20,16},{24,28},{28,24},{1,5},{5... | collective-permute-start | bytes 786440 | tf_op jit(solution)/shard_map/z1c2/ppermute | solution.py:246
  47.0 1.9 %collective-permute-start.14 = (bf16[4,256,128]{2,1,0:T(8,128)(2,1)S(1)}, bf16[4,256,128]{2,1,0:T(8,128)(2,1)S(1)}, u32[]{:S(2)}, u32[]{:S(2)}) collective-permute-start(bf16[4,256,128]{2,1,0:T(8,128)(2,1)S(1)} %get-tuple-element.61), channel_id=1, source_target_pairs={{0,3},{1,2},{2,1},{3,0},{4,7},{5,6},{6,5},{7,4},{8,11},{9,10},{10,... | collective-permute-start | bytes 786440 | tf_op jit(solution)/shard_map/y7/ppermute | solution.py:246
  48.8 2.0 %collective-permute-done.11.refs_3_.refs_2_ = bf16[4,256,128]{2,1,0:T(8,128)(2,1)S(1)} collective-permute-done((bf16[4,256,128]{2,1,0:T(8,128)(2,1)S(1)}, bf16[4,256,128]{2,1,0:T(8,128)(2,1)S(1)}, u32[]{:S(2)}, u32[]{:S(2)}) %collective-permute-start.11) | collective-permute-done | bytes 262176 | tf_op jit(solution)/shard_map/y6/ppermute | solution.py:246
  50.8 2.3 %collective-permute-done.7.refs_1_.refs_5_ = bf16[1,4,4,64,128]{4,3,2,1,0:T(8,128)(2,1)S(1)} collective-permute-done((bf16[1,4,4,64,128]{4,3,2,1,0:T(8,128)(2,1)S(1)}, bf16[1,4,4,64,128]{4,3,2,1,0:T(8,128)(2,1)S(1)}, u32[]{:S(2)}, u32[]{:S(2)}) %collective-permute-start.7) | collective-permute-done | bytes 262176 | tf_op jit(solution)/shard_map/z4c1/ppermute | solution.py:246
  53.1 0.1 collective-permute-start.13
  53.2 0.1 collective-permute-done.6.refs_2_
  53.3 1.6 %collective-permute-start.12 = (bf16[4,1,4,64,128]{4,3,2,1,0:T(8,128)(2,1)S(1)}, bf16[4,1,4,64,128]{4,3,2,1,0:T(8,128)(2,1)S(1)}, u32[]{:S(2)}, u32[]{:S(2)}) collective-permute-start(bf16[4,1,4,64,128]{4,3,2,1,0:T(8,128)(2,1)S(1)} %merge.8.refs_2_), channel_id=1, source_target_pairs={{0,4},{4,0},{8,12},{12,8},{16,20},{20,16},{24,28},{28,24},{1,5},{5... | collective-permute-start | bytes 786440 | tf_op jit(solution)/shard_map/z1c0/ppermute | solution.py:246
  54.9 0.0 collective-permute-done.15.refs_1_.refs_9_
  55.0 0.7 collective-permute-done.14.refs_3_
  55.7 0.7 half.7
  56.4 1.8 %collective-permute-start.20 = (bf16[1,4,4,64,128]{4,3,2,1,0:T(8,128)(2,1)S(1)}, bf16[1,4,4,64,128]{4,3,2,1,0:T(8,128)(2,1)S(1)}, u32[]{:S(2)}, u32[]{:S(2)}) collective-permute-start(bf16[1,4,4,64,128]{4,3,2,1,0:T(8,128)(2,1)S(1)} %get-tuple-element.64.refs_3_), channel_id=1, source_target_pairs={{0,4},{4,0},{8,12},{12,8},{16,20},{20,16},{24,28},{28,24},{1,5},{5... | collective-permute-start | bytes 786440 | tf_op jit(solution)/shard_map/z1c3/ppermute | solution.py:246
  58.2 2.6 %collective-permute-start.18 = (bf16[2,1,4,64,128]{4,3,2,1,0:T(8,128)(2,1)S(1)}, bf16[2,1,4,64,128]{4,3,2,1,0:T(8,128)(2,1)S(1)}, u32[]{:S(2)}, u32[]{:S(2)}) collective-permute-start(bf16[2,1,4,64,128]{4,3,2,1,0:T(8,128)(2,1)S(1)} %get-tuple-element.65), channel_id=1, source_target_pairs={{0,16},{4,20},{8,24},{12,28},{16,0},{20,4},{24,8},{28,12},{1,17},{... | collective-permute-start | bytes 393224 | tf_op jit(solution)/shard_map/z4c2/ppermute | solution.py:246
  60.8 1.3 %collective-permute-start.17 = (bf16[2,1,4,64,128]{4,3,2,1,0:T(8,128)(2,1)S(1)}, bf16[2,1,4,64,128]{4,3,2,1,0:T(8,128)(2,1)S(1)}, u32[]{:S(2)}, u32[]{:S(2)}) collective-permute-start(bf16[2,1,4,64,128]{4,3,2,1,0:T(8,128)(2,1)S(1)} %get-tuple-element.63.refs_5_), channel_id=1, source_target_pairs={{0,24},{4,28},{8,16},{12,20},{16,8},{20,12},{24,0},{28,4},{1,25},{... | collective-permute-start | bytes 393224 | tf_op jit(solution)/shard_map/z6c2/ppermute | solution.py:246
  62.2 0.6 collective-permute-start.16
  62.8 0.2 collective-permute-start.19
  63.0 4.1 %collective-permute-done.20.refs_1_.refs_14_ = bf16[1,4,4,64,128]{4,3,2,1,0:T(8,128)(2,1)S(1)} collective-permute-done((bf16[1,4,4,64,128]{4,3,2,1,0:T(8,128)(2,1)S(1)}, bf16[1,4,4,64,128]{4,3,2,1,0:T(8,128)(2,1)S(1)}, u32[]{:S(2)}, u32[]{:S(2)}) %collective-permute-start.20) | collective-permute-done | bytes 262176 | tf_op jit(solution)/shard_map/z1c3/ppermute | solution.py:246
  67.2 2.8 %collective-permute-start.21 = (bf16[2,1,4,64,128]{4,3,2,1,0:T(8,128)(2,1)S(1)}, bf16[2,1,4,64,128]{4,3,2,1,0:T(8,128)(2,1)S(1)}, u32[]{:S(2)}, u32[]{:S(2)}) collective-permute-start(bf16[2,1,4,64,128]{4,3,2,1,0:T(8,128)(2,1)S(1)} %get-tuple-element.68.refs_1_), channel_id=1, source_target_pairs={{0,24},{4,28},{8,16},{12,20},{16,8},{20,12},{24,0},{28,4},{1,25},{... | collective-permute-start | bytes 393224 | tf_op jit(solution)/shard_map/z6c3/ppermute | solution.py:246
  69.9 1.4 %collective-permute-done.18.refs_0_.refs_11_ = bf16[2,1,4,64,128]{4,3,2,1,0:T(8,128)(2,1)S(1)} collective-permute-done((bf16[2,1,4,64,128]{4,3,2,1,0:T(8,128)(2,1)S(1)}, bf16[2,1,4,64,128]{4,3,2,1,0:T(8,128)(2,1)S(1)}, u32[]{:S(2)}, u32[]{:S(2)}) %collective-permute-start.18) | collective-permute-done | bytes 131104 | tf_op jit(solution)/shard_map/z4c2/ppermute | solution.py:246
  71.4 0.0 collective-permute-start.22
  71.4 8.7 %collective-permute-start.23 = (bf16[2,1,4,64,128]{4,3,2,1,0:T(8,128)(2,1)S(1)}, bf16[2,1,4,64,128]{4,3,2,1,0:T(8,128)(2,1)S(1)}, u32[]{:S(2)}, u32[]{:S(2)}) collective-permute-start(bf16[2,1,4,64,128]{4,3,2,1,0:T(8,128)(2,1)S(1)} %get-tuple-element.70), channel_id=1, source_target_pairs={{0,8},{4,12},{8,0},{12,4},{16,24},{20,28},{24,16},{28,20},{1,9},{5... | collective-permute-start | bytes 393224 | tf_op jit(solution)/shard_map/z2c3/ppermute | solution.py:246
  80.1 4.4 %collective-permute-done.22.refs_0_.refs_16_ = bf16[2,1,4,64,128]{4,3,2,1,0:T(8,128)(2,1)S(1)} collective-permute-done((bf16[2,1,4,64,128]{4,3,2,1,0:T(8,128)(2,1)S(1)}, bf16[2,1,4,64,128]{4,3,2,1,0:T(8,128)(2,1)S(1)}, u32[]{:S(2)}, u32[]{:S(2)}) %collective-permute-start.22) | collective-permute-done | bytes 131104 | tf_op jit(solution)/shard_map/z4c3/ppermute | solution.py:246
  84.6 1.5 %collective-permute-done.23.refs_0_.refs_17_ = bf16[2,1,4,64,128]{4,3,2,1,0:T(8,128)(2,1)S(1)} collective-permute-done((bf16[2,1,4,64,128]{4,3,2,1,0:T(8,128)(2,1)S(1)}, bf16[2,1,4,64,128]{4,3,2,1,0:T(8,128)(2,1)S(1)}, u32[]{:S(2)}, u32[]{:S(2)}) %collective-permute-start.23) | collective-permute-done | bytes 131104 | tf_op jit(solution)/shard_map/z2c3/ppermute | solution.py:246
  86.1 2.8 %combine.1 = f32[128,64,128]{2,1,0:T(8,128)} custom-call(s32[128]{0:T(128)S(1)} %copy-done.1, s32[2]{0:T(128)S(1)} %pad_add_fusion.place_ref, bf16[1,4,4,64,128]{4,3,2,1,0:T(8,128)(2,1)S(1)} %get-tuple-element.48.refs_0_, bf16[1,4,4,64,128]{4,3,2,1,0:T(8,128)(2,1)S(1)} %collective-permute-done.3.refs_1_, ...), custom_call_target="tpu_custom_call" | custom-call | flops 1024 | bytes 1024 | tf_op jit(solution)/shard_map/combine/pallas_call | solution.py:228
  (25 shorter events, 0.2 us)
Async XLA Ops:
  0.1 17.0 %copy-start = (bf16[1000,512]{1,0:T(8,128)(2,1)S(1)}, bf16[1000,512]{1,0:T(8,128)(2,1)}, u32[]{:S(2)}) copy-start(bf16[1000,512]{1,0:T(8,128)(2,1)} %c_ref.1) | copy-start | bytes 3072004
  6.8 15.4 %collective-permute-start = (bf16[8,256,128]{2,1,0:T(8,128)(2,1)S(1)}, bf16[8,256,128]{2,1,0:T(8,128)(2,1)S(1)}, u32[]{:S(2)}, u32[]{:S(2)}) collective-permute-start(bf16[8,256,128]{2,1,0:T(8,128)(2,1)S(1)} %get-tuple-element.39), channel_id=1, source_target_pairs={{0,1},{1,0},{2,3},{3,2},{4,5},{5,4},{6,7},{7,6},{8,9},{9,8},{10,11... | collective-permute-start | bytes 1572872 | tf_op jit(solution)/shard_map/beside0/ppermute | solution.py:246
  7.3 9.8 %collective-permute-start.1 = (bf16[4,256,128]{2,1,0:T(8,128)(2,1)S(1)}, bf16[4,256,128]{2,1,0:T(8,128)(2,1)S(1)}, u32[]{:S(2)}, u32[]{:S(2)}) collective-permute-start(bf16[4,256,128]{2,1,0:T(8,128)(2,1)S(1)} %get-tuple-element.40), channel_id=1, source_target_pairs={{0,2},{1,3},{2,0},{3,1},{4,6},{5,7},{6,4},{7,5},{8,10},{9,11},{10,... | collective-permute-start | bytes 786440 | tf_op jit(solution)/shard_map/y0/ppermute | solution.py:246
  9.9 12.3 %collective-permute-start.2 = (bf16[4,256,128]{2,1,0:T(8,128)(2,1)S(1)}, bf16[4,256,128]{2,1,0:T(8,128)(2,1)S(1)}, u32[]{:S(2)}, u32[]{:S(2)}) collective-permute-start(bf16[4,256,128]{2,1,0:T(8,128)(2,1)S(1)} %get-tuple-element.41), channel_id=1, source_target_pairs={{0,3},{1,2},{2,1},{3,0},{4,7},{5,6},{6,5},{7,4},{8,11},{9,10},{10,... | collective-permute-start | bytes 786440 | tf_op jit(solution)/shard_map/y1/ppermute | solution.py:246
  16.7 21.7 %collective-permute-start.8 = (bf16[8,256,128]{2,1,0:T(8,128)(2,1)S(1)}, bf16[8,256,128]{2,1,0:T(8,128)(2,1)S(1)}, u32[]{:S(2)}, u32[]{:S(2)}) collective-permute-start(bf16[8,256,128]{2,1,0:T(8,128)(2,1)S(1)} %get-tuple-element.55), channel_id=1, source_target_pairs={{0,1},{1,0},{2,3},{3,2},{4,5},{5,4},{6,7},{7,6},{8,9},{9,8},{10,11... | collective-permute-start | bytes 1572872 | tf_op jit(solution)/shard_map/beside1/ppermute | solution.py:246
  18.1 10.2 %collective-permute-start.4 = (bf16[4,256,128]{2,1,0:T(8,128)(2,1)S(1)}, bf16[4,256,128]{2,1,0:T(8,128)(2,1)S(1)}, u32[]{:S(2)}, u32[]{:S(2)}) collective-permute-start(bf16[4,256,128]{2,1,0:T(8,128)(2,1)S(1)} %get-tuple-element.50), channel_id=1, source_target_pairs={{0,2},{1,3},{2,0},{3,1},{4,6},{5,7},{6,4},{7,5},{8,10},{9,11},{10,... | collective-permute-start | bytes 786440 | tf_op jit(solution)/shard_map/y2/ppermute | solution.py:246
  20.1 13.3 %collective-permute-start.5 = (bf16[4,256,128]{2,1,0:T(8,128)(2,1)S(1)}, bf16[4,256,128]{2,1,0:T(8,128)(2,1)S(1)}, u32[]{:S(2)}, u32[]{:S(2)}) collective-permute-start(bf16[4,256,128]{2,1,0:T(8,128)(2,1)S(1)} %get-tuple-element.51), channel_id=1, source_target_pairs={{0,3},{1,2},{2,1},{3,0},{4,7},{5,6},{6,5},{7,4},{8,11},{9,10},{10,... | collective-permute-start | bytes 786440 | tf_op jit(solution)/shard_map/y3/ppermute | solution.py:246
  22.9 15.5 %collective-permute-start.3 = (bf16[1,4,4,64,128]{4,3,2,1,0:T(8,128)(2,1)S(1)}, bf16[1,4,4,64,128]{4,3,2,1,0:T(8,128)(2,1)S(1)}, u32[]{:S(2)}, u32[]{:S(2)}) collective-permute-start(bf16[1,4,4,64,128]{4,3,2,1,0:T(8,128)(2,1)S(1)} %get-tuple-element.49.refs_6_), channel_id=1, source_target_pairs={{0,16},{4,20},{8,24},{12,28},{16,0},{20,4},{24,8},{28,12},{1,17},{... | collective-permute-start | bytes 786440 | tf_op jit(solution)/shard_map/z4c0/ppermute | solution.py:246
  25.6 17.0 %collective-permute-start.9 = (bf16[4,256,128]{2,1,0:T(8,128)(2,1)S(1)}, bf16[4,256,128]{2,1,0:T(8,128)(2,1)S(1)}, u32[]{:S(2)}, u32[]{:S(2)}) collective-permute-start(bf16[4,256,128]{2,1,0:T(8,128)(2,1)S(1)} %get-tuple-element.56), channel_id=1, source_target_pairs={{0,2},{1,3},{2,0},{3,1},{4,6},{5,7},{6,4},{7,5},{8,10},{9,11},{10,... | collective-permute-start | bytes 786440 | tf_op jit(solution)/shard_map/y4/ppermute | solution.py:246
  28.3 16.3 %collective-permute-start.10 = (bf16[4,256,128]{2,1,0:T(8,128)(2,1)S(1)}, bf16[4,256,128]{2,1,0:T(8,128)(2,1)S(1)}, u32[]{:S(2)}, u32[]{:S(2)}) collective-permute-start(bf16[4,256,128]{2,1,0:T(8,128)(2,1)S(1)} %get-tuple-element.57), channel_id=1, source_target_pairs={{0,3},{1,2},{2,1},{3,0},{4,7},{5,6},{6,5},{7,4},{8,11},{9,10},{10,... | collective-permute-start | bytes 786440 | tf_op jit(solution)/shard_map/y5/ppermute | solution.py:246
  33.4 52.7 %copy-start.1 = (s32[128]{0:T(128)S(1)}, s32[128]{0:T(128)}, u32[]{:S(2)}) copy-start(s32[128]{0:T(128)} %mirror_ref.1) | copy-start | bytes 1540
  34.1 16.7 %collective-permute-start.11 = (bf16[4,256,128]{2,1,0:T(8,128)(2,1)S(1)}, bf16[4,256,128]{2,1,0:T(8,128)(2,1)S(1)}, u32[]{:S(2)}, u32[]{:S(2)}) collective-permute-start(bf16[4,256,128]{2,1,0:T(8,128)(2,1)S(1)} %get-tuple-element.60), channel_id=1, source_target_pairs={{0,2},{1,3},{2,0},{3,1},{4,6},{5,7},{6,4},{7,5},{8,10},{9,11},{10,... | collective-permute-start | bytes 786440 | tf_op jit(solution)/shard_map/y6/ppermute | solution.py:246
  38.4 14.7 %collective-permute-start.7 = (bf16[1,4,4,64,128]{4,3,2,1,0:T(8,128)(2,1)S(1)}, bf16[1,4,4,64,128]{4,3,2,1,0:T(8,128)(2,1)S(1)}, u32[]{:S(2)}, u32[]{:S(2)}) collective-permute-start(bf16[1,4,4,64,128]{4,3,2,1,0:T(8,128)(2,1)S(1)} %get-tuple-element.53.refs_2_), channel_id=1, source_target_pairs={{0,16},{4,20},{8,24},{12,28},{16,0},{20,4},{24,8},{28,12},{1,17},{... | collective-permute-start | bytes 786440 | tf_op jit(solution)/shard_map/z4c1/ppermute | solution.py:246
  38.5 14.8 %collective-permute-start.6 = (bf16[2,2,4,64,128]{4,3,2,1,0:T(8,128)(2,1)S(1)}, bf16[2,2,4,64,128]{4,3,2,1,0:T(8,128)(2,1)S(1)}, u32[]{:S(2)}, u32[]{:S(2)}) collective-permute-start(bf16[2,2,4,64,128]{4,3,2,1,0:T(8,128)(2,1)S(1)} %merge.6.refs_6_), channel_id=1, source_target_pairs={{0,8},{4,12},{8,0},{12,4},{16,24},{20,28},{24,16},{28,20},{1,9},{5... | collective-permute-start | bytes 786440 | tf_op jit(solution)/shard_map/z2c0/ppermute | solution.py:246
  45.4 9.6 %collective-permute-start.15 = (bf16[1,4,4,64,128]{4,3,2,1,0:T(8,128)(2,1)S(1)}, bf16[1,4,4,64,128]{4,3,2,1,0:T(8,128)(2,1)S(1)}, u32[]{:S(2)}, u32[]{:S(2)}) collective-permute-start(bf16[1,4,4,64,128]{4,3,2,1,0:T(8,128)(2,1)S(1)} %get-tuple-element.59.refs_2_), channel_id=1, source_target_pairs={{0,4},{4,0},{8,12},{12,8},{16,20},{20,16},{24,28},{28,24},{1,5},{5... | collective-permute-start | bytes 786440 | tf_op jit(solution)/shard_map/z1c2/ppermute | solution.py:246
  47.0 8.7 %collective-permute-start.14 = (bf16[4,256,128]{2,1,0:T(8,128)(2,1)S(1)}, bf16[4,256,128]{2,1,0:T(8,128)(2,1)S(1)}, u32[]{:S(2)}, u32[]{:S(2)}) collective-permute-start(bf16[4,256,128]{2,1,0:T(8,128)(2,1)S(1)} %get-tuple-element.61), channel_id=1, source_target_pairs={{0,3},{1,2},{2,1},{3,0},{4,7},{5,6},{6,5},{7,4},{8,11},{9,10},{10,... | collective-permute-start | bytes 786440 | tf_op jit(solution)/shard_map/y7/ppermute | solution.py:246
  53.1 9.0 %collective-permute-start.13 = (bf16[2,2,4,64,128]{4,3,2,1,0:T(8,128)(2,1)S(1)}, bf16[2,2,4,64,128]{4,3,2,1,0:T(8,128)(2,1)S(1)}, u32[]{:S(2)}, u32[]{:S(2)}) collective-permute-start(bf16[2,2,4,64,128]{4,3,2,1,0:T(8,128)(2,1)S(1)} %merge.7.refs_3_), channel_id=1, source_target_pairs={{0,8},{4,12},{8,0},{12,4},{16,24},{20,28},{24,16},{28,20},{1,9},{5... | collective-permute-start | bytes 786440 | tf_op jit(solution)/shard_map/z2c1/ppermute | solution.py:246
  53.3 9.5 %collective-permute-start.12 = (bf16[4,1,4,64,128]{4,3,2,1,0:T(8,128)(2,1)S(1)}, bf16[4,1,4,64,128]{4,3,2,1,0:T(8,128)(2,1)S(1)}, u32[]{:S(2)}, u32[]{:S(2)}) collective-permute-start(bf16[4,1,4,64,128]{4,3,2,1,0:T(8,128)(2,1)S(1)} %merge.8.refs_2_), channel_id=1, source_target_pairs={{0,4},{4,0},{8,12},{12,8},{16,20},{20,16},{24,28},{28,24},{1,5},{5... | collective-permute-start | bytes 786440 | tf_op jit(solution)/shard_map/z1c0/ppermute | solution.py:246
  56.4 10.7 %collective-permute-start.20 = (bf16[1,4,4,64,128]{4,3,2,1,0:T(8,128)(2,1)S(1)}, bf16[1,4,4,64,128]{4,3,2,1,0:T(8,128)(2,1)S(1)}, u32[]{:S(2)}, u32[]{:S(2)}) collective-permute-start(bf16[1,4,4,64,128]{4,3,2,1,0:T(8,128)(2,1)S(1)} %get-tuple-element.64.refs_3_), channel_id=1, source_target_pairs={{0,4},{4,0},{8,12},{12,8},{16,20},{20,16},{24,28},{28,24},{1,5},{5... | collective-permute-start | bytes 786440 | tf_op jit(solution)/shard_map/z1c3/ppermute | solution.py:246
  58.2 13.2 %collective-permute-start.18 = (bf16[2,1,4,64,128]{4,3,2,1,0:T(8,128)(2,1)S(1)}, bf16[2,1,4,64,128]{4,3,2,1,0:T(8,128)(2,1)S(1)}, u32[]{:S(2)}, u32[]{:S(2)}) collective-permute-start(bf16[2,1,4,64,128]{4,3,2,1,0:T(8,128)(2,1)S(1)} %get-tuple-element.65), channel_id=1, source_target_pairs={{0,16},{4,20},{8,24},{12,28},{16,0},{20,4},{24,8},{28,12},{1,17},{... | collective-permute-start | bytes 393224 | tf_op jit(solution)/shard_map/z4c2/ppermute | solution.py:246
  60.8 10.6 %collective-permute-start.17 = (bf16[2,1,4,64,128]{4,3,2,1,0:T(8,128)(2,1)S(1)}, bf16[2,1,4,64,128]{4,3,2,1,0:T(8,128)(2,1)S(1)}, u32[]{:S(2)}, u32[]{:S(2)}) collective-permute-start(bf16[2,1,4,64,128]{4,3,2,1,0:T(8,128)(2,1)S(1)} %get-tuple-element.63.refs_5_), channel_id=1, source_target_pairs={{0,24},{4,28},{8,16},{12,20},{16,8},{20,12},{24,0},{28,4},{1,25},{... | collective-permute-start | bytes 393224 | tf_op jit(solution)/shard_map/z6c2/ppermute | solution.py:246
  62.2 23.9 %collective-permute-start.16 = (bf16[4,1,4,64,128]{4,3,2,1,0:T(8,128)(2,1)S(1)}, bf16[4,1,4,64,128]{4,3,2,1,0:T(8,128)(2,1)S(1)}, u32[]{:S(2)}, u32[]{:S(2)}) collective-permute-start(bf16[4,1,4,64,128]{4,3,2,1,0:T(8,128)(2,1)S(1)} %merge.10.refs_2_), channel_id=1, source_target_pairs={{0,4},{4,0},{8,12},{12,8},{16,20},{20,16},{24,28},{28,24},{1,5},{5... | collective-permute-start | bytes 786440 | tf_op jit(solution)/shard_map/z1c1/ppermute | solution.py:246
  62.8 17.3 %collective-permute-start.19 = (bf16[2,1,4,64,128]{4,3,2,1,0:T(8,128)(2,1)S(1)}, bf16[2,1,4,64,128]{4,3,2,1,0:T(8,128)(2,1)S(1)}, u32[]{:S(2)}, u32[]{:S(2)}) collective-permute-start(bf16[2,1,4,64,128]{4,3,2,1,0:T(8,128)(2,1)S(1)} %get-tuple-element.66), channel_id=1, source_target_pairs={{0,8},{4,12},{8,0},{12,4},{16,24},{20,28},{24,16},{28,20},{1,9},{5... | collective-permute-start | bytes 393224 | tf_op jit(solution)/shard_map/z2c2/ppermute | solution.py:246
  67.2 12.9 %collective-permute-start.21 = (bf16[2,1,4,64,128]{4,3,2,1,0:T(8,128)(2,1)S(1)}, bf16[2,1,4,64,128]{4,3,2,1,0:T(8,128)(2,1)S(1)}, u32[]{:S(2)}, u32[]{:S(2)}) collective-permute-start(bf16[2,1,4,64,128]{4,3,2,1,0:T(8,128)(2,1)S(1)} %get-tuple-element.68.refs_1_), channel_id=1, source_target_pairs={{0,24},{4,28},{8,16},{12,20},{16,8},{20,12},{24,0},{28,4},{1,25},{... | collective-permute-start | bytes 393224 | tf_op jit(solution)/shard_map/z6c3/ppermute | solution.py:246
  71.4 13.2 %collective-permute-start.22 = (bf16[2,1,4,64,128]{4,3,2,1,0:T(8,128)(2,1)S(1)}, bf16[2,1,4,64,128]{4,3,2,1,0:T(8,128)(2,1)S(1)}, u32[]{:S(2)}, u32[]{:S(2)}) collective-permute-start(bf16[2,1,4,64,128]{4,3,2,1,0:T(8,128)(2,1)S(1)} %get-tuple-element.69), channel_id=1, source_target_pairs={{0,16},{4,20},{8,24},{12,28},{16,0},{20,4},{24,8},{28,12},{1,17},{... | collective-permute-start | bytes 393224 | tf_op jit(solution)/shard_map/z4c3/ppermute | solution.py:246
  71.4 14.7 %collective-permute-start.23 = (bf16[2,1,4,64,128]{4,3,2,1,0:T(8,128)(2,1)S(1)}, bf16[2,1,4,64,128]{4,3,2,1,0:T(8,128)(2,1)S(1)}, u32[]{:S(2)}, u32[]{:S(2)}) collective-permute-start(bf16[2,1,4,64,128]{4,3,2,1,0:T(8,128)(2,1)S(1)} %get-tuple-element.70), channel_id=1, source_target_pairs={{0,8},{4,12},{8,0},{12,4},{16,24},{20,28},{24,16},{28,20},{1,9},{5... | collective-permute-start | bytes 393224 | tf_op jit(solution)/shard_map/z2c3/ppermute | solution.py:246

commit v18 on v17

--- a/solution.py
+++ b/solution.py
@@ -320,7 +320,7 @@
             messages = merge(parts[c], picks, token + done)
         token = messages[:1]
         send(c, level, messages)
-    for x in parts[last - 1][-3:] + parts[last][-3:]:
+    for x in [parts[last - 1][n] for n in (-2, -1, -3)] + parts[last][-3:]:
         token = [wait_for([x, *token])]
     pieces = [x for chunk in parts for x in chunk]
     sources = [(tuple(group), first) for chunk, first in zip(offsets, firsts) for group in chunk]

time: 89.1 us -> 87.4 us (0.981)
  starting transfers between devices: 39.4 us -> 34.5 us
  waiting for transfers between devices: 29.1 us -> 32.3 us
    ppermute x24, starting transfers between devices: 39.4 us -> 34.5 us  [flipped(): return lax.ppermute(x, axis, [(i, i ^ offset) for i in range(size)])]
    ppermute x24, waiting for transfers between devices: 29.1 us -> 32.3 us  [flipped(): return lax.ppermute(x, axis, [(i, i ^ offset) for i in range(size)])]
  transfers between devices with their start and end apart: 24 -> 24, of which waited for: 14 -> 13; matrix products, arithmetic and copies ran while one was open for 0% -> 0% of each run, Pallas kernels for 12% -> 12%
where the time goes in v18:
time: 87.4 us; the launch traced here: 87.3 us
  starting transfers between devices  34.5 us (39%)
  waiting for transfers between devices  32.3 us (37%)
  Pallas kernels  20.3 us (23%)
    ppermute x24, starting transfers between devices, flipped(): return lax.ppermute(x, axis, [(i, i ^ offset) for i in range(size)])  34.5 us
    ppermute x24, waiting for transfers between devices, flipped(): return lax.ppermute(x, axis, [(i, i ^ offset) for i in range(size)])  32.3 us
    pallas_call x2, Pallas kernels, quarter_of(): pl.pallas_call(functools.partial(quarter_kernel, batch, n_mo, blocks, len...  13.5 us
    pallas_call x4, Pallas kernels, half_of(): pl.pallas_call(functools.partial(half_kernel_after, len(blocks), len(owne...  2.86 us
    pallas_call x1, Pallas kernels, combine(): pl.pallas_call(functools.partial(combine_kernel, sources, k_all, per_step...  2.84 us
  transfers between devices with their start and end apart: 24, of which 13 were waited for; matrix products, arithmetic and copies ran while one was open for 0% of the time, Pallas kernels for 12%

profile of v18, /device:TPU:0, one launch (start us, length us, event | category | flops | bytes accessed | tf_op | source)
XLA Modules:
  0.0 87.3 jit_solution(3630794231535686851)
XLA Ops:
  0.0 0.1 pad_add_fusion.place_ref
  0.1 6.7 %quarter.2 = (bf16[8,256,128]{2,1,0:T(8,128)(2,1)S(1)}, bf16[8,256,128]{2,1,0:T(8,128)(2,1)S(1)}, bf16[4,256,128]{2,1,0:T(8,128)(2,1)S(1)}, bf16[4,256,128]{2,1,...) custom-call(s32[2]{0:T(128)S(1)} %pad_add_fusion.place_ref, ...), custom_call_target="tpu_custom_call" | custom-call | flops 1024 | bytes 1024 | tf_op jit(solution)/shard_map/quarter/pallas_call | solution.py:71
  6.8 0.5 collective-permute-start
  7.3 2.6 %collective-permute-start.1 = (bf16[4,256,128]{2,1,0:T(8,128)(2,1)S(1)}, bf16[4,256,128]{2,1,0:T(8,128)(2,1)S(1)}, u32[]{:S(2)}, u32[]{:S(2)}) collective-permute-start(bf16[4,256,128]{2,1,0:T(8,128)(2,1)S(1)} %get-tuple-element.40), channel_id=1, source_target_pairs={{0,2},{1,3},{2,0},{3,1},{4,6},{5,7},{6,4},{7,5},{8,10},{9,11},{10,... | collective-permute-start | bytes 786440 | tf_op jit(solution)/shard_map/y0/ppermute | solution.py:246
  9.9 0.1 collective-permute-start.2
  10.0 6.7 %quarter.3 = (bf16[8,256,128]{2,1,0:T(8,128)(2,1)S(1)}, bf16[8,256,128]{2,1,0:T(8,128)(2,1)S(1)}, bf16[4,256,128]{2,1,0:T(8,128)(2,1)S(1)}, bf16[4,256,128]{2,1,...) custom-call(s32[2]{0:T(128)S(1)} %pad_add_fusion.place_ref, ...), custom_call_target="tpu_custom_call" | custom-call | flops 1024 | bytes 1024 | tf_op jit(solution)/shard_map/quarter/pallas_call | solution.py:71
  16.7 0.2 collective-permute-start.8
  16.9 0.2 collective-permute-done.1.refs_2_
  17.1 1.0 %turn.1 = (bf16[4,256,128]{2,1,0:T(8,128)(2,1)S(1)}, bf16[4,256,128]{2,1,0:T(8,128)(2,1)S(1)}, bf16[512,1024]{1,0:T(8,128)(2,1)S(1)}) custom-call(s32[2]{0:T(128)S(1)} %pad_add_fusion.place_ref, bf16[1000,512]{1,0:T(8,128)(2,1)S(1)} %copy-done, bf16[4,256,128]{2,1,0:T(8,128)(2,1)S(1)} %get-tuple-element.42.refs_0_, ...), custom_call_target="tpu_custom_call", output_to_operand_aliasing={{0}: (2, {}), {1}: (3, {})} | custom-call | flops 1024 | bytes 1024 | tf_op jit(solution)/shard_map/turn/pallas_call | solution.py:107
  18.1 2.0 %collective-permute-start.4 = (bf16[4,256,128]{2,1,0:T(8,128)(2,1)S(1)}, bf16[4,256,128]{2,1,0:T(8,128)(2,1)S(1)}, u32[]{:S(2)}, u32[]{:S(2)}) collective-permute-start(bf16[4,256,128]{2,1,0:T(8,128)(2,1)S(1)} %get-tuple-element.50), channel_id=1, source_target_pairs={{0,2},{1,3},{2,0},{3,1},{4,6},{5,7},{6,4},{7,5},{8,10},{9,11},{10,... | collective-permute-start | bytes 786440 | tf_op jit(solution)/shard_map/y2/ppermute | solution.py:246
  20.1 2.1 %collective-permute-done.2.refs_3_ = bf16[4,256,128]{2,1,0:T(8,128)(2,1)S(1)} collective-permute-done((bf16[4,256,128]{2,1,0:T(8,128)(2,1)S(1)}, bf16[4,256,128]{2,1,0:T(8,128)(2,1)S(1)}, u32[]{:S(2)}, u32[]{:S(2)}) %collective-permute-start.2) | collective-permute-done | bytes 262176 | tf_op jit(solution)/shard_map/y1/ppermute | solution.py:246
  22.2 0.0 collective-permute-done.refs_1_
  22.2 0.7 half.4
  22.9 2.7 %collective-permute-start.3 = (bf16[1,4,4,64,128]{4,3,2,1,0:T(8,128)(2,1)S(1)}, bf16[1,4,4,64,128]{4,3,2,1,0:T(8,128)(2,1)S(1)}, u32[]{:S(2)}, u32[]{:S(2)}) collective-permute-start(bf16[1,4,4,64,128]{4,3,2,1,0:T(8,128)(2,1)S(1)} %get-tuple-element.49.refs_6_), channel_id=1, source_target_pairs={{0,16},{4,20},{8,24},{12,28},{16,0},{20,4},{24,8},{28,12},{1,17},{... | collective-permute-start | bytes 786440 | tf_op jit(solution)/shard_map/z4c0/ppermute | solution.py:246
  25.6 1.5 %collective-permute-start.9 = (bf16[4,256,128]{2,1,0:T(8,128)(2,1)S(1)}, bf16[4,256,128]{2,1,0:T(8,128)(2,1)S(1)}, u32[]{:S(2)}, u32[]{:S(2)}) collective-permute-start(bf16[4,256,128]{2,1,0:T(8,128)(2,1)S(1)} %get-tuple-element.56), channel_id=1, source_target_pairs={{0,2},{1,3},{2,0},{3,1},{4,6},{5,7},{6,4},{7,5},{8,10},{9,11},{10,... | collective-permute-start | bytes 786440 | tf_op jit(solution)/shard_map/y4/ppermute | solution.py:246
  27.1 1.2 %collective-permute-done.4.refs_2_ = bf16[4,256,128]{2,1,0:T(8,128)(2,1)S(1)} collective-permute-done((bf16[4,256,128]{2,1,0:T(8,128)(2,1)S(1)}, bf16[4,256,128]{2,1,0:T(8,128)(2,1)S(1)}, u32[]{:S(2)}, u32[]{:S(2)}) %collective-permute-start.4) | collective-permute-done | bytes 262176 | tf_op jit(solution)/shard_map/y2/ppermute | solution.py:246
  28.3 0.8 collective-permute-start.10
  29.1 4.3 %collective-permute-done.5.refs_3_ = bf16[4,256,128]{2,1,0:T(8,128)(2,1)S(1)} collective-permute-done((bf16[4,256,128]{2,1,0:T(8,128)(2,1)S(1)}, bf16[4,256,128]{2,1,0:T(8,128)(2,1)S(1)}, u32[]{:S(2)}, u32[]{:S(2)}) %collective-permute-start.5) | collective-permute-done | bytes 262176 | tf_op jit(solution)/shard_map/y3/ppermute | solution.py:246
  33.4 0.7 half.5
  34.1 1.6 %collective-permute-start.11 = (bf16[4,256,128]{2,1,0:T(8,128)(2,1)S(1)}, bf16[4,256,128]{2,1,0:T(8,128)(2,1)S(1)}, u32[]{:S(2)}, u32[]{:S(2)}) collective-permute-start(bf16[4,256,128]{2,1,0:T(8,128)(2,1)S(1)} %get-tuple-element.60), channel_id=1, source_target_pairs={{0,2},{1,3},{2,0},{3,1},{4,6},{5,7},{6,4},{7,5},{8,10},{9,11},{10,... | collective-permute-start | bytes 786440 | tf_op jit(solution)/shard_map/y6/ppermute | solution.py:246
  35.8 2.7 %collective-permute-done.3.refs_1_ = bf16[1,4,4,64,128]{4,3,2,1,0:T(8,128)(2,1)S(1)} collective-permute-done((bf16[1,4,4,64,128]{4,3,2,1,0:T(8,128)(2,1)S(1)}, bf16[1,4,4,64,128]{4,3,2,1,0:T(8,128)(2,1)S(1)}, u32[]{:S(2)}, u32[]{:S(2)}) %collective-permute-start.3) | collective-permute-done | bytes 262176 | tf_op jit(solution)/shard_map/z4c0/ppermute | solution.py:246
  38.4 0.0 collective-permute-start.7
  38.4 0.0 collective-permute-done.8.refs_1_
  38.5 4.2 %collective-permute-start.6 = (bf16[2,2,4,64,128]{4,3,2,1,0:T(8,128)(2,1)S(1)}, bf16[2,2,4,64,128]{4,3,2,1,0:T(8,128)(2,1)S(1)}, u32[]{:S(2)}, u32[]{:S(2)}) collective-permute-start(bf16[2,2,4,64,128]{4,3,2,1,0:T(8,128)(2,1)S(1)} %merge.6.refs_6_), channel_id=1, source_target_pairs={{0,8},{4,12},{8,0},{12,4},{16,24},{20,28},{24,16},{28,20},{1,9},{5... | collective-permute-start | bytes 786440 | tf_op jit(solution)/shard_map/z2c0/ppermute | solution.py:246
  42.6 0.0 collective-permute-done.9.refs_2_
  42.6 2.0 %collective-permute-done.10.refs_3_ = bf16[4,256,128]{2,1,0:T(8,128)(2,1)S(1)} collective-permute-done((bf16[4,256,128]{2,1,0:T(8,128)(2,1)S(1)}, bf16[4,256,128]{2,1,0:T(8,128)(2,1)S(1)}, u32[]{:S(2)}, u32[]{:S(2)}) %collective-permute-start.10) | collective-permute-done | bytes 262176 | tf_op jit(solution)/shard_map/y5/ppermute | solution.py:246
  44.6 0.7 half.6
  45.4 1.6 %collective-permute-start.15 = (bf16[1,4,4,64,128]{4,3,2,1,0:T(8,128)(2,1)S(1)}, bf16[1,4,4,64,128]{4,3,2,1,0:T(8,128)(2,1)S(1)}, u32[]{:S(2)}, u32[]{:S(2)}) collective-permute-start(bf16[1,4,4,64,128]{4,3,2,1,0:T(8,128)(2,1)S(1)} %get-tuple-element.59.refs_2_), channel_id=1, source_target_pairs={{0,4},{4,0},{8,12},{12,8},{16,20},{20,16},{24,28},{28,24},{1,5},{5... | collective-permute-start | bytes 786440 | tf_op jit(solution)/shard_map/z1c2/ppermute | solution.py:246
  47.0 1.9 %collective-permute-start.14 = (bf16[4,256,128]{2,1,0:T(8,128)(2,1)S(1)}, bf16[4,256,128]{2,1,0:T(8,128)(2,1)S(1)}, u32[]{:S(2)}, u32[]{:S(2)}) collective-permute-start(bf16[4,256,128]{2,1,0:T(8,128)(2,1)S(1)} %get-tuple-element.61), channel_id=1, source_target_pairs={{0,3},{1,2},{2,1},{3,0},{4,7},{5,6},{6,5},{7,4},{8,11},{9,10},{10,... | collective-permute-start | bytes 786440 | tf_op jit(solution)/shard_map/y7/ppermute | solution.py:246
  48.8 2.0 %collective-permute-done.11.refs_3_.refs_2_ = bf16[4,256,128]{2,1,0:T(8,128)(2,1)S(1)} collective-permute-done((bf16[4,256,128]{2,1,0:T(8,128)(2,1)S(1)}, bf16[4,256,128]{2,1,0:T(8,128)(2,1)S(1)}, u32[]{:S(2)}, u32[]{:S(2)}) %collective-permute-start.11) | collective-permute-done | bytes 262176 | tf_op jit(solution)/shard_map/y6/ppermute | solution.py:246
  50.8 2.3 %collective-permute-done.7.refs_1_.refs_5_ = bf16[1,4,4,64,128]{4,3,2,1,0:T(8,128)(2,1)S(1)} collective-permute-done((bf16[1,4,4,64,128]{4,3,2,1,0:T(8,128)(2,1)S(1)}, bf16[1,4,4,64,128]{4,3,2,1,0:T(8,128)(2,1)S(1)}, u32[]{:S(2)}, u32[]{:S(2)}) %collective-permute-start.7) | collective-permute-done | bytes 262176 | tf_op jit(solution)/shard_map/z4c1/ppermute | solution.py:246
  53.1 0.1 collective-permute-start.13
  53.2 0.1 collective-permute-done.6.refs_2_
  53.3 1.6 %collective-permute-start.12 = (bf16[4,1,4,64,128]{4,3,2,1,0:T(8,128)(2,1)S(1)}, bf16[4,1,4,64,128]{4,3,2,1,0:T(8,128)(2,1)S(1)}, u32[]{:S(2)}, u32[]{:S(2)}) collective-permute-start(bf16[4,1,4,64,128]{4,3,2,1,0:T(8,128)(2,1)S(1)} %merge.8.refs_2_), channel_id=1, source_target_pairs={{0,4},{4,0},{8,12},{12,8},{16,20},{20,16},{24,28},{28,24},{1,5},{5... | collective-permute-start | bytes 786440 | tf_op jit(solution)/shard_map/z1c0/ppermute | solution.py:246
  55.0 0.7 collective-permute-done.14.refs_3_
  55.7 0.7 half.7
  56.4 1.8 %collective-permute-start.20 = (bf16[1,4,4,64,128]{4,3,2,1,0:T(8,128)(2,1)S(1)}, bf16[1,4,4,64,128]{4,3,2,1,0:T(8,128)(2,1)S(1)}, u32[]{:S(2)}, u32[]{:S(2)}) collective-permute-start(bf16[1,4,4,64,128]{4,3,2,1,0:T(8,128)(2,1)S(1)} %get-tuple-element.64.refs_3_), channel_id=1, source_target_pairs={{0,4},{4,0},{8,12},{12,8},{16,20},{20,16},{24,28},{28,24},{1,5},{5... | collective-permute-start | bytes 786440 | tf_op jit(solution)/shard_map/z1c3/ppermute | solution.py:246
  58.2 2.6 %collective-permute-start.18 = (bf16[2,1,4,64,128]{4,3,2,1,0:T(8,128)(2,1)S(1)}, bf16[2,1,4,64,128]{4,3,2,1,0:T(8,128)(2,1)S(1)}, u32[]{:S(2)}, u32[]{:S(2)}) collective-permute-start(bf16[2,1,4,64,128]{4,3,2,1,0:T(8,128)(2,1)S(1)} %get-tuple-element.65), channel_id=1, source_target_pairs={{0,16},{4,20},{8,24},{12,28},{16,0},{20,4},{24,8},{28,12},{1,17},{... | collective-permute-start | bytes 393224 | tf_op jit(solution)/shard_map/z4c2/ppermute | solution.py:246
  60.8 1.6 %collective-permute-start.19 = (bf16[2,1,4,64,128]{4,3,2,1,0:T(8,128)(2,1)S(1)}, bf16[2,1,4,64,128]{4,3,2,1,0:T(8,128)(2,1)S(1)}, u32[]{:S(2)}, u32[]{:S(2)}) collective-permute-start(bf16[2,1,4,64,128]{4,3,2,1,0:T(8,128)(2,1)S(1)} %get-tuple-element.66), channel_id=1, source_target_pairs={{0,8},{4,12},{8,0},{12,4},{16,24},{20,28},{24,16},{28,20},{1,9},{5... | collective-permute-start | bytes 393224 | tf_op jit(solution)/shard_map/z2c2/ppermute | solution.py:246
  62.4 0.6 collective-permute-start.16
  63.0 1.4 %collective-permute-start.17 = (bf16[2,1,4,64,128]{4,3,2,1,0:T(8,128)(2,1)S(1)}, bf16[2,1,4,64,128]{4,3,2,1,0:T(8,128)(2,1)S(1)}, u32[]{:S(2)}, u32[]{:S(2)}) collective-permute-start(bf16[2,1,4,64,128]{4,3,2,1,0:T(8,128)(2,1)S(1)} %get-tuple-element.63.refs_5_), channel_id=1, source_target_pairs={{0,24},{4,28},{8,16},{12,20},{16,8},{20,12},{24,0},{28,4},{1,25},{... | collective-permute-start | bytes 393224 | tf_op jit(solution)/shard_map/z6c2/ppermute | solution.py:246
  64.4 2.7 %collective-permute-done.20.refs_1_.refs_14_ = bf16[1,4,4,64,128]{4,3,2,1,0:T(8,128)(2,1)S(1)} collective-permute-done((bf16[1,4,4,64,128]{4,3,2,1,0:T(8,128)(2,1)S(1)}, bf16[1,4,4,64,128]{4,3,2,1,0:T(8,128)(2,1)S(1)}, u32[]{:S(2)}, u32[]{:S(2)}) %collective-permute-start.20) | collective-permute-done | bytes 262176 | tf_op jit(solution)/shard_map/z1c3/ppermute | solution.py:246
  67.2 2.8 %collective-permute-start.21 = (bf16[2,1,4,64,128]{4,3,2,1,0:T(8,128)(2,1)S(1)}, bf16[2,1,4,64,128]{4,3,2,1,0:T(8,128)(2,1)S(1)}, u32[]{:S(2)}, u32[]{:S(2)}) collective-permute-start(bf16[2,1,4,64,128]{4,3,2,1,0:T(8,128)(2,1)S(1)} %get-tuple-element.68.refs_1_), channel_id=1, source_target_pairs={{0,24},{4,28},{8,16},{12,20},{16,8},{20,12},{24,0},{28,4},{1,25},{... | collective-permute-start | bytes 393224 | tf_op jit(solution)/shard_map/z6c3/ppermute | solution.py:246
  69.9 0.1 collective-permute-start.22
  70.0 2.3 %collective-permute-start.23 = (bf16[2,1,4,64,128]{4,3,2,1,0:T(8,128)(2,1)S(1)}, bf16[2,1,4,64,128]{4,3,2,1,0:T(8,128)(2,1)S(1)}, u32[]{:S(2)}, u32[]{:S(2)}) collective-permute-start(bf16[2,1,4,64,128]{4,3,2,1,0:T(8,128)(2,1)S(1)} %get-tuple-element.70), channel_id=1, source_target_pairs={{0,8},{4,12},{8,0},{12,4},{16,24},{20,28},{24,16},{28,20},{1,9},{5... | collective-permute-start | bytes 393224 | tf_op jit(solution)/shard_map/z2c3/ppermute | solution.py:246
  72.4 3.1 %collective-permute-done.21.refs_0_.refs_15_ = bf16[2,1,4,64,128]{4,3,2,1,0:T(8,128)(2,1)S(1)} collective-permute-done((bf16[2,1,4,64,128]{4,3,2,1,0:T(8,128)(2,1)S(1)}, bf16[2,1,4,64,128]{4,3,2,1,0:T(8,128)(2,1)S(1)}, u32[]{:S(2)}, u32[]{:S(2)}) %collective-permute-start.21) | collective-permute-done | bytes 131104 | tf_op jit(solution)/shard_map/z6c3/ppermute | solution.py:246
  75.5 8.9 %collective-permute-done.22.refs_0_.refs_16_ = bf16[2,1,4,64,128]{4,3,2,1,0:T(8,128)(2,1)S(1)} collective-permute-done((bf16[2,1,4,64,128]{4,3,2,1,0:T(8,128)(2,1)S(1)}, bf16[2,1,4,64,128]{4,3,2,1,0:T(8,128)(2,1)S(1)}, u32[]{:S(2)}, u32[]{:S(2)}) %collective-permute-start.22) | collective-permute-done | bytes 131104 | tf_op jit(solution)/shard_map/z4c3/ppermute | solution.py:246
  84.4 2.8 %combine.1 = f32[128,64,128]{2,1,0:T(8,128)} custom-call(s32[128]{0:T(128)S(1)} %copy-done.1, s32[2]{0:T(128)S(1)} %pad_add_fusion.place_ref, bf16[1,4,4,64,128]{4,3,2,1,0:T(8,128)(2,1)S(1)} %get-tuple-element.48.refs_0_, bf16[1,4,4,64,128]{4,3,2,1,0:T(8,128)(2,1)S(1)} %collective-permute-done.3.refs_1_, ...), custom_call_target="tpu_custom_call" | custom-call | flops 1024 | bytes 1024 | tf_op jit(solution)/shard_map/combine/pallas_call | solution.py:228
  (25 shorter events, 0.2 us)
Async XLA Ops:
  0.1 17.0 %copy-start = (bf16[1000,512]{1,0:T(8,128)(2,1)S(1)}, bf16[1000,512]{1,0:T(8,128)(2,1)}, u32[]{:S(2)}) copy-start(bf16[1000,512]{1,0:T(8,128)(2,1)} %c_ref.1) | copy-start | bytes 3072004
  6.8 15.4 %collective-permute-start = (bf16[8,256,128]{2,1,0:T(8,128)(2,1)S(1)}, bf16[8,256,128]{2,1,0:T(8,128)(2,1)S(1)}, u32[]{:S(2)}, u32[]{:S(2)}) collective-permute-start(bf16[8,256,128]{2,1,0:T(8,128)(2,1)S(1)} %get-tuple-element.39), channel_id=1, source_target_pairs={{0,1},{1,0},{2,3},{3,2},{4,5},{5,4},{6,7},{7,6},{8,9},{9,8},{10,11... | collective-permute-start | bytes 1572872 | tf_op jit(solution)/shard_map/beside0/ppermute | solution.py:246
  7.3 9.8 %collective-permute-start.1 = (bf16[4,256,128]{2,1,0:T(8,128)(2,1)S(1)}, bf16[4,256,128]{2,1,0:T(8,128)(2,1)S(1)}, u32[]{:S(2)}, u32[]{:S(2)}) collective-permute-start(bf16[4,256,128]{2,1,0:T(8,128)(2,1)S(1)} %get-tuple-element.40), channel_id=1, source_target_pairs={{0,2},{1,3},{2,0},{3,1},{4,6},{5,7},{6,4},{7,5},{8,10},{9,11},{10,... | collective-permute-start | bytes 786440 | tf_op jit(solution)/shard_map/y0/ppermute | solution.py:246
  9.9 12.3 %collective-permute-start.2 = (bf16[4,256,128]{2,1,0:T(8,128)(2,1)S(1)}, bf16[4,256,128]{2,1,0:T(8,128)(2,1)S(1)}, u32[]{:S(2)}, u32[]{:S(2)}) collective-permute-start(bf16[4,256,128]{2,1,0:T(8,128)(2,1)S(1)} %get-tuple-element.41), channel_id=1, source_target_pairs={{0,3},{1,2},{2,1},{3,0},{4,7},{5,6},{6,5},{7,4},{8,11},{9,10},{10,... | collective-permute-start | bytes 786440 | tf_op jit(solution)/shard_map/y1/ppermute | solution.py:246
  16.7 21.7 %collective-permute-start.8 = (bf16[8,256,128]{2,1,0:T(8,128)(2,1)S(1)}, bf16[8,256,128]{2,1,0:T(8,128)(2,1)S(1)}, u32[]{:S(2)}, u32[]{:S(2)}) collective-permute-start(bf16[8,256,128]{2,1,0:T(8,128)(2,1)S(1)} %get-tuple-element.55), channel_id=1, source_target_pairs={{0,1},{1,0},{2,3},{3,2},{4,5},{5,4},{6,7},{7,6},{8,9},{9,8},{10,11... | collective-permute-start | bytes 1572872 | tf_op jit(solution)/shard_map/beside1/ppermute | solution.py:246
  18.1 10.2 %collective-permute-start.4 = (bf16[4,256,128]{2,1,0:T(8,128)(2,1)S(1)}, bf16[4,256,128]{2,1,0:T(8,128)(2,1)S(1)}, u32[]{:S(2)}, u32[]{:S(2)}) collective-permute-start(bf16[4,256,128]{2,1,0:T(8,128)(2,1)S(1)} %get-tuple-element.50), channel_id=1, source_target_pairs={{0,2},{1,3},{2,0},{3,1},{4,6},{5,7},{6,4},{7,5},{8,10},{9,11},{10,... | collective-permute-start | bytes 786440 | tf_op jit(solution)/shard_map/y2/ppermute | solution.py:246
  20.1 13.3 %collective-permute-start.5 = (bf16[4,256,128]{2,1,0:T(8,128)(2,1)S(1)}, bf16[4,256,128]{2,1,0:T(8,128)(2,1)S(1)}, u32[]{:S(2)}, u32[]{:S(2)}) collective-permute-start(bf16[4,256,128]{2,1,0:T(8,128)(2,1)S(1)} %get-tuple-element.51), channel_id=1, source_target_pairs={{0,3},{1,2},{2,1},{3,0},{4,7},{5,6},{6,5},{7,4},{8,11},{9,10},{10,... | collective-permute-start | bytes 786440 | tf_op jit(solution)/shard_map/y3/ppermute | solution.py:246
  22.9 15.5 %collective-permute-start.3 = (bf16[1,4,4,64,128]{4,3,2,1,0:T(8,128)(2,1)S(1)}, bf16[1,4,4,64,128]{4,3,2,1,0:T(8,128)(2,1)S(1)}, u32[]{:S(2)}, u32[]{:S(2)}) collective-permute-start(bf16[1,4,4,64,128]{4,3,2,1,0:T(8,128)(2,1)S(1)} %get-tuple-element.49.refs_6_), channel_id=1, source_target_pairs={{0,16},{4,20},{8,24},{12,28},{16,0},{20,4},{24,8},{28,12},{1,17},{... | collective-permute-start | bytes 786440 | tf_op jit(solution)/shard_map/z4c0/ppermute | solution.py:246
  25.6 17.0 %collective-permute-start.9 = (bf16[4,256,128]{2,1,0:T(8,128)(2,1)S(1)}, bf16[4,256,128]{2,1,0:T(8,128)(2,1)S(1)}, u32[]{:S(2)}, u32[]{:S(2)}) collective-permute-start(bf16[4,256,128]{2,1,0:T(8,128)(2,1)S(1)} %get-tuple-element.56), channel_id=1, source_target_pairs={{0,2},{1,3},{2,0},{3,1},{4,6},{5,7},{6,4},{7,5},{8,10},{9,11},{10,... | collective-permute-start | bytes 786440 | tf_op jit(solution)/shard_map/y4/ppermute | solution.py:246
  28.3 16.3 %collective-permute-start.10 = (bf16[4,256,128]{2,1,0:T(8,128)(2,1)S(1)}, bf16[4,256,128]{2,1,0:T(8,128)(2,1)S(1)}, u32[]{:S(2)}, u32[]{:S(2)}) collective-permute-start(bf16[4,256,128]{2,1,0:T(8,128)(2,1)S(1)} %get-tuple-element.57), channel_id=1, source_target_pairs={{0,3},{1,2},{2,1},{3,0},{4,7},{5,6},{6,5},{7,4},{8,11},{9,10},{10,... | collective-permute-start | bytes 786440 | tf_op jit(solution)/shard_map/y5/ppermute | solution.py:246
  33.4 51.0 %copy-start.1 = (s32[128]{0:T(128)S(1)}, s32[128]{0:T(128)}, u32[]{:S(2)}) copy-start(s32[128]{0:T(128)} %mirror_ref.1) | copy-start | bytes 1540
  34.1 16.7 %collective-permute-start.11 = (bf16[4,256,128]{2,1,0:T(8,128)(2,1)S(1)}, bf16[4,256,128]{2,1,0:T(8,128)(2,1)S(1)}, u32[]{:S(2)}, u32[]{:S(2)}) collective-permute-start(bf16[4,256,128]{2,1,0:T(8,128)(2,1)S(1)} %get-tuple-element.60), channel_id=1, source_target_pairs={{0,2},{1,3},{2,0},{3,1},{4,6},{5,7},{6,4},{7,5},{8,10},{9,11},{10,... | collective-permute-start | bytes 786440 | tf_op jit(solution)/shard_map/y6/ppermute | solution.py:246
  38.4 14.7 %collective-permute-start.7 = (bf16[1,4,4,64,128]{4,3,2,1,0:T(8,128)(2,1)S(1)}, bf16[1,4,4,64,128]{4,3,2,1,0:T(8,128)(2,1)S(1)}, u32[]{:S(2)}, u32[]{:S(2)}) collective-permute-start(bf16[1,4,4,64,128]{4,3,2,1,0:T(8,128)(2,1)S(1)} %get-tuple-element.53.refs_2_), channel_id=1, source_target_pairs={{0,16},{4,20},{8,24},{12,28},{16,0},{20,4},{24,8},{28,12},{1,17},{... | collective-permute-start | bytes 786440 | tf_op jit(solution)/shard_map/z4c1/ppermute | solution.py:246
  38.5 14.8 %collective-permute-start.6 = (bf16[2,2,4,64,128]{4,3,2,1,0:T(8,128)(2,1)S(1)}, bf16[2,2,4,64,128]{4,3,2,1,0:T(8,128)(2,1)S(1)}, u32[]{:S(2)}, u32[]{:S(2)}) collective-permute-start(bf16[2,2,4,64,128]{4,3,2,1,0:T(8,128)(2,1)S(1)} %merge.6.refs_6_), channel_id=1, source_target_pairs={{0,8},{4,12},{8,0},{12,4},{16,24},{20,28},{24,16},{28,20},{1,9},{5... | collective-permute-start | bytes 786440 | tf_op jit(solution)/shard_map/z2c0/ppermute | solution.py:246
  45.4 9.6 %collective-permute-start.15 = (bf16[1,4,4,64,128]{4,3,2,1,0:T(8,128)(2,1)S(1)}, bf16[1,4,4,64,128]{4,3,2,1,0:T(8,128)(2,1)S(1)}, u32[]{:S(2)}, u32[]{:S(2)}) collective-permute-start(bf16[1,4,4,64,128]{4,3,2,1,0:T(8,128)(2,1)S(1)} %get-tuple-element.59.refs_2_), channel_id=1, source_target_pairs={{0,4},{4,0},{8,12},{12,8},{16,20},{20,16},{24,28},{28,24},{1,5},{5... | collective-permute-start | bytes 786440 | tf_op jit(solution)/shard_map/z1c2/ppermute | solution.py:246
  47.0 8.7 %collective-permute-start.14 = (bf16[4,256,128]{2,1,0:T(8,128)(2,1)S(1)}, bf16[4,256,128]{2,1,0:T(8,128)(2,1)S(1)}, u32[]{:S(2)}, u32[]{:S(2)}) collective-permute-start(bf16[4,256,128]{2,1,0:T(8,128)(2,1)S(1)} %get-tuple-element.61), channel_id=1, source_target_pairs={{0,3},{1,2},{2,1},{3,0},{4,7},{5,6},{6,5},{7,4},{8,11},{9,10},{10,... | collective-permute-start | bytes 786440 | tf_op jit(solution)/shard_map/y7/ppermute | solution.py:246
  53.1 9.2 %collective-permute-start.13 = (bf16[2,2,4,64,128]{4,3,2,1,0:T(8,128)(2,1)S(1)}, bf16[2,2,4,64,128]{4,3,2,1,0:T(8,128)(2,1)S(1)}, u32[]{:S(2)}, u32[]{:S(2)}) collective-permute-start(bf16[2,2,4,64,128]{4,3,2,1,0:T(8,128)(2,1)S(1)} %merge.7.refs_3_), channel_id=1, source_target_pairs={{0,8},{4,12},{8,0},{12,4},{16,24},{20,28},{24,16},{28,20},{1,9},{5... | collective-permute-start | bytes 786440 | tf_op jit(solution)/shard_map/z2c1/ppermute | solution.py:246
  53.3 9.7 %collective-permute-start.12 = (bf16[4,1,4,64,128]{4,3,2,1,0:T(8,128)(2,1)S(1)}, bf16[4,1,4,64,128]{4,3,2,1,0:T(8,128)(2,1)S(1)}, u32[]{:S(2)}, u32[]{:S(2)}) collective-permute-start(bf16[4,1,4,64,128]{4,3,2,1,0:T(8,128)(2,1)S(1)} %merge.8.refs_2_), channel_id=1, source_target_pairs={{0,4},{4,0},{8,12},{12,8},{16,20},{20,16},{24,28},{28,24},{1,5},{5... | collective-permute-start | bytes 786440 | tf_op jit(solution)/shard_map/z1c0/ppermute | solution.py:246
  56.4 10.7 %collective-permute-start.20 = (bf16[1,4,4,64,128]{4,3,2,1,0:T(8,128)(2,1)S(1)}, bf16[1,4,4,64,128]{4,3,2,1,0:T(8,128)(2,1)S(1)}, u32[]{:S(2)}, u32[]{:S(2)}) collective-permute-start(bf16[1,4,4,64,128]{4,3,2,1,0:T(8,128)(2,1)S(1)} %get-tuple-element.64.refs_3_), channel_id=1, source_target_pairs={{0,4},{4,0},{8,12},{12,8},{16,20},{20,16},{24,28},{28,24},{1,5},{5... | collective-permute-start | bytes 786440 | tf_op jit(solution)/shard_map/z1c3/ppermute | solution.py:246
  58.2 11.7 %collective-permute-start.18 = (bf16[2,1,4,64,128]{4,3,2,1,0:T(8,128)(2,1)S(1)}, bf16[2,1,4,64,128]{4,3,2,1,0:T(8,128)(2,1)S(1)}, u32[]{:S(2)}, u32[]{:S(2)}) collective-permute-start(bf16[2,1,4,64,128]{4,3,2,1,0:T(8,128)(2,1)S(1)} %get-tuple-element.65), channel_id=1, source_target_pairs={{0,16},{4,20},{8,24},{12,28},{16,0},{20,4},{24,8},{28,12},{1,17},{... | collective-permute-start | bytes 393224 | tf_op jit(solution)/shard_map/z4c2/ppermute | solution.py:246
  60.8 9.2 %collective-permute-start.19 = (bf16[2,1,4,64,128]{4,3,2,1,0:T(8,128)(2,1)S(1)}, bf16[2,1,4,64,128]{4,3,2,1,0:T(8,128)(2,1)S(1)}, u32[]{:S(2)}, u32[]{:S(2)}) collective-permute-start(bf16[2,1,4,64,128]{4,3,2,1,0:T(8,128)(2,1)S(1)} %get-tuple-element.66), channel_id=1, source_target_pairs={{0,8},{4,12},{8,0},{12,4},{16,24},{20,28},{24,16},{28,20},{1,9},{5... | collective-permute-start | bytes 393224 | tf_op jit(solution)/shard_map/z2c2/ppermute | solution.py:246
  62.4 22.0 %collective-permute-start.16 = (bf16[4,1,4,64,128]{4,3,2,1,0:T(8,128)(2,1)S(1)}, bf16[4,1,4,64,128]{4,3,2,1,0:T(8,128)(2,1)S(1)}, u32[]{:S(2)}, u32[]{:S(2)}) collective-permute-start(bf16[4,1,4,64,128]{4,3,2,1,0:T(8,128)(2,1)S(1)} %merge.10.refs_2_), channel_id=1, source_target_pairs={{0,4},{4,0},{8,12},{12,8},{16,20},{20,16},{24,28},{28,24},{1,5},{5... | collective-permute-start | bytes 786440 | tf_op jit(solution)/shard_map/z1c1/ppermute | solution.py:246
  63.0 9.4 %collective-permute-start.17 = (bf16[2,1,4,64,128]{4,3,2,1,0:T(8,128)(2,1)S(1)}, bf16[2,1,4,64,128]{4,3,2,1,0:T(8,128)(2,1)S(1)}, u32[]{:S(2)}, u32[]{:S(2)}) collective-permute-start(bf16[2,1,4,64,128]{4,3,2,1,0:T(8,128)(2,1)S(1)} %get-tuple-element.63.refs_5_), channel_id=1, source_target_pairs={{0,24},{4,28},{8,16},{12,20},{16,8},{20,12},{24,0},{28,4},{1,25},{... | collective-permute-start | bytes 393224 | tf_op jit(solution)/shard_map/z6c2/ppermute | solution.py:246
  67.2 8.4 %collective-permute-start.21 = (bf16[2,1,4,64,128]{4,3,2,1,0:T(8,128)(2,1)S(1)}, bf16[2,1,4,64,128]{4,3,2,1,0:T(8,128)(2,1)S(1)}, u32[]{:S(2)}, u32[]{:S(2)}) collective-permute-start(bf16[2,1,4,64,128]{4,3,2,1,0:T(8,128)(2,1)S(1)} %get-tuple-element.68.refs_1_), channel_id=1, source_target_pairs={{0,24},{4,28},{8,16},{12,20},{16,8},{20,12},{24,0},{28,4},{1,25},{... | collective-permute-start | bytes 393224 | tf_op jit(solution)/shard_map/z6c3/ppermute | solution.py:246
  69.9 14.5 %collective-permute-start.22 = (bf16[2,1,4,64,128]{4,3,2,1,0:T(8,128)(2,1)S(1)}, bf16[2,1,4,64,128]{4,3,2,1,0:T(8,128)(2,1)S(1)}, u32[]{:S(2)}, u32[]{:S(2)}) collective-permute-start(bf16[2,1,4,64,128]{4,3,2,1,0:T(8,128)(2,1)S(1)} %get-tuple-element.69), channel_id=1, source_target_pairs={{0,16},{4,20},{8,24},{12,28},{16,0},{20,4},{24,8},{28,12},{1,17},{... | collective-permute-start | bytes 393224 | tf_op jit(solution)/shard_map/z4c3/ppermute | solution.py:246
  70.0 14.4 %collective-permute-start.23 = (bf16[2,1,4,64,128]{4,3,2,1,0:T(8,128)(2,1)S(1)}, bf16[2,1,4,64,128]{4,3,2,1,0:T(8,128)(2,1)S(1)}, u32[]{:S(2)}, u32[]{:S(2)}) collective-permute-start(bf16[2,1,4,64,128]{4,3,2,1,0:T(8,128)(2,1)S(1)} %get-tuple-element.70), channel_id=1, source_target_pairs={{0,8},{4,12},{8,0},{12,4},{16,24},{20,28},{24,16},{28,20},{1,9},{5... | collective-permute-start | bytes 393224 | tf_op jit(solution)/shard_map/z2c3/ppermute | solution.py:246

commit v19 on v18

--- a/solution.py
+++ b/solution.py
@@ -8,7 +8,7 @@
 from jax.sharding import PartitionSpec as P
 
 LANES = 128
-STEP = 64
+STEP = 128
 LATER = {0: (2, [2, 3]), 1: (3, [2]), 2: (3, [3])}
 BATCHES = ((4, 4), (4, 4))
 CHUNKS = sum(BATCHES, ())
@@ -197,12 +197,34 @@
     )(*after)
 
 
-def combine_kernel(sources, k_all, per_step, mirror_ref, place_ref, *refs):
-    pieces, (out_hbm, held, done, sems) = refs[: len(sources)], refs[-4:]
+def place_rows(pieces, sources, k_all, place_ref, held):
     for piece, (offsets, first) in zip(pieces, sources):
         for n, offset in enumerate(offsets):
             row = (place_ref[1] ^ offset) * k_all + first
             held[pl.ds(row, piece.shape[2])] = piece[n, 0]
+
+
+def collect_kernel(sources, k_all, place_ref, *refs):
+    place_rows(refs, sources, k_all, place_ref, refs[-1])
+
+
+def collect(pieces, sources, place, n_pair, after):
+    block, lanes = pieces[0].shape[-2:]
+    k_all = sum(CHUNKS)
+    return pl.pallas_call(
+        functools.partial(collect_kernel, sources, k_all),
+        in_specs=[IN_SMEM] + [IN_VMEM] * len(pieces) + [ANYWHERE] * len(after),
+        out_specs=IN_VMEM,
+        out_shape=jax.ShapeDtypeStruct((n_pair * k_all, block, lanes), jnp.bfloat16),
+        compiler_params=pltpu.CompilerParams(vmem_limit_bytes=24 * MIB),
+        cost_estimate=COST,
+        name="collect",
+    )(place, *pieces, *after)
+
+
+def combine_kernel(sources, k_all, per_step, mirror_ref, place_ref, *refs):
+    out_hbm, held, done, sems = refs[-4:]
+    place_rows(refs[1:], sources, k_all, place_ref, held)
 
     def copy_of(step):
         rows = pl.ds(step * per_step, per_step)
@@ -220,25 +242,26 @@
         copy_of(step).wait()
 
 
-def combine(pieces, sources, mirror, place, n_pair, after):
-    block, lanes = pieces[0].shape[-2:]
-    k_all = sum(CHUNKS)
-    rows = n_pair * k_all
+def combine(held, pieces, sources, mirror, place, after):
+    rows, block, lanes = held.shape
     per_step = max(1, 16 * 64 // block)
     return pl.pallas_call(
-        functools.partial(combine_kernel, sources, k_all, per_step),
-        in_specs=[IN_SMEM] * 2 + [IN_VMEM] * len(pieces) + [ANYWHERE] * len(after),
-        out_specs=IN_HBM,
-        out_shape=jax.ShapeDtypeStruct((rows, block, lanes), jnp.float32),
+        functools.partial(combine_kernel, sources, sum(CHUNKS), per_step),
+        in_specs=[IN_SMEM] * 2 + [IN_VMEM] * (1 + len(pieces)) + [ANYWHERE] * len(after),
+        out_specs=[IN_HBM, IN_VMEM],
+        out_shape=[
+            jax.ShapeDtypeStruct((rows, block, lanes), jnp.float32),
+            jax.ShapeDtypeStruct((rows, block, lanes), jnp.bfloat16),
+        ],
+        input_output_aliases={2: 1},
         scratch_shapes=[
-            pltpu.VMEM((rows, block, lanes), jnp.bfloat16),
             pltpu.VMEM((rows, block, lanes), jnp.float32),
             pltpu.SemaphoreType.DMA((rows // per_step,)),
         ],
         compiler_params=pltpu.CompilerParams(vmem_limit_bytes=24 * MIB),
         cost_estimate=COST,
         name="combine",
-    )(mirror, place, *pieces, *after)
+    )(mirror, place, held, *pieces, *after)[0]
 
 
 def flipped(x, axis, size, offset, name):
@@ -320,11 +343,21 @@
             messages = merge(parts[c], picks, token + done)
         token = messages[:1]
         send(c, level, messages)
-    for x in [parts[last - 1][n] for n in (-2, -1, -3)] + parts[last][-3:]:
+    for n in (-2, -1, -3):
+        token = [wait_for([parts[last - 1][n], *token])]
+    late = [parts[1][-1], *parts[last][-3:]]
+    both = [
+        (x, (tuple(group), first))
+        for chunk, its, first in zip(parts, offsets, firsts)
+        for x, group in zip(chunk, its)
+    ]
+    early = [entry for entry in both if all(entry[0] is not x for x in late)]
+    held = collect(*zip(*early), place, n_pair, token)
+    token = [held]
+    for x in late[1:]:
         token = [wait_for([x, *token])]
-    pieces = [x for chunk in parts for x in chunk]
-    sources = [(tuple(group), first) for chunk, first in zip(offsets, firsts) for group in chunk]
-    return combine(pieces, sources, mirror, place, n_pair, token)
+    rest = [entry for entry in both if any(entry[0] is x for x in late)]
+    return combine(held, *zip(*rest), mirror, place, token[:1] if token[0] is not held else [])
 
 
 def solution(mesh):

time: 87.4 us -> 86.7 us (level)
    pallas_call x2, Pallas kernels: 13.5 us -> 12.3 us  [quarter_of(): pl.pallas_call(functools.partial(quarter_kernel, batch, n_mo, blocks, len...]
    pallas_call x1 -> x2, Pallas kernels: 2.84 us -> 3.38 us  [the longest x1 2.73 us: combine(): pl.pallas_call(functools.partial(combine_kernel, sources, sum(CHUNKS), pe...]
where the time goes in v19:
time: 86.7 us; the launch traced here: 86.6 us
  starting transfers between devices  34.4 us (40%)
  waiting for transfers between devices  32.3 us (37%)
  Pallas kernels  19.6 us (23%)
    ppermute x24, starting transfers between devices, flipped(): return lax.ppermute(x, axis, [(i, i ^ offset) for i in range(size)])  34.4 us
    ppermute x24, waiting for transfers between devices, flipped(): return lax.ppermute(x, axis, [(i, i ^ offset) for i in range(size)])  32.3 us
    pallas_call x2, Pallas kernels, quarter_of(): pl.pallas_call(functools.partial(quarter_kernel, batch, n_mo, blocks, len...  12.3 us
    pallas_call x4, Pallas kernels, half_of(): pl.pallas_call(functools.partial(half_kernel_after, len(blocks), len(owne...  2.85 us
    pallas_call x1, Pallas kernels, combine(): pl.pallas_call(functools.partial(combine_kernel, sources, sum(CHUNKS), pe...  2.73 us
  transfers between devices with their start and end apart: 24, of which 13 were waited for; matrix products, arithmetic and copies ran while one was open for 0% of the time, Pallas kernels for 12%

profile of v19, /device:TPU:0, one launch (start us, length us, event | category | flops | bytes accessed | tf_op | source)
XLA Modules:
  0.0 86.6 jit_solution(10932716047950302343)
XLA Ops:
  0.0 0.1 pad_add_fusion.place_ref
  0.1 6.1 %quarter.2 = (bf16[8,256,128]{2,1,0:T(8,128)(2,1)S(1)}, bf16[8,256,128]{2,1,0:T(8,128)(2,1)S(1)}, bf16[4,256,128]{2,1,0:T(8,128)(2,1)S(1)}, bf16[4,256,128]{2,1,...) custom-call(s32[2]{0:T(128)S(1)} %pad_add_fusion.place_ref, ...), custom_call_target="tpu_custom_call" | custom-call | flops 1024 | bytes 1024 | tf_op jit(solution)/shard_map/quarter/pallas_call | solution.py:71
  6.2 0.5 collective-permute-start
  6.7 2.6 %collective-permute-start.1 = (bf16[4,256,128]{2,1,0:T(8,128)(2,1)S(1)}, bf16[4,256,128]{2,1,0:T(8,128)(2,1)S(1)}, u32[]{:S(2)}, u32[]{:S(2)}) collective-permute-start(bf16[4,256,128]{2,1,0:T(8,128)(2,1)S(1)} %get-tuple-element.41), channel_id=1, source_target_pairs={{0,2},{1,3},{2,0},{3,1},{4,6},{5,7},{6,4},{7,5},{8,10},{9,11},{10,... | collective-permute-start | bytes 786440 | tf_op jit(solution)/shard_map/y0/ppermute | solution.py:269
  9.3 0.1 collective-permute-start.2
  9.4 6.1 %quarter.3 = (bf16[8,256,128]{2,1,0:T(8,128)(2,1)S(1)}, bf16[8,256,128]{2,1,0:T(8,128)(2,1)S(1)}, bf16[4,256,128]{2,1,0:T(8,128)(2,1)S(1)}, bf16[4,256,128]{2,1,...) custom-call(s32[2]{0:T(128)S(1)} %pad_add_fusion.place_ref, ...), custom_call_target="tpu_custom_call" | custom-call | flops 1024 | bytes 1024 | tf_op jit(solution)/shard_map/quarter/pallas_call | solution.py:71
  15.5 0.2 collective-permute-start.8
  15.7 0.7 collective-permute-done.1.refs_2_
  16.5 1.0 %turn.1 = (bf16[4,256,128]{2,1,0:T(8,128)(2,1)S(1)}, bf16[4,256,128]{2,1,0:T(8,128)(2,1)S(1)}, bf16[512,1024]{1,0:T(8,128)(2,1)S(1)}) custom-call(s32[2]{0:T(128)S(1)} %pad_add_fusion.place_ref, bf16[1000,512]{1,0:T(8,128)(2,1)S(1)} %copy-done, bf16[4,256,128]{2,1,0:T(8,128)(2,1)S(1)} %get-tuple-element.43.refs_0_, ...), custom_call_target="tpu_custom_call", output_to_operand_aliasing={{0}: (2, {}), {1}: (3, {})} | custom-call | flops 1024 | bytes 1024 | tf_op jit(solution)/shard_map/turn/pallas_call | solution.py:107
  17.5 2.0 %collective-permute-start.4 = (bf16[4,256,128]{2,1,0:T(8,128)(2,1)S(1)}, bf16[4,256,128]{2,1,0:T(8,128)(2,1)S(1)}, u32[]{:S(2)}, u32[]{:S(2)}) collective-permute-start(bf16[4,256,128]{2,1,0:T(8,128)(2,1)S(1)} %get-tuple-element.51), channel_id=1, source_target_pairs={{0,2},{1,3},{2,0},{3,1},{4,6},{5,7},{6,4},{7,5},{8,10},{9,11},{10,... | collective-permute-start | bytes 786440 | tf_op jit(solution)/shard_map/y2/ppermute | solution.py:269
  19.5 0.0 collective-permute-start.5
  19.5 2.1 %collective-permute-done.2.refs_3_ = bf16[4,256,128]{2,1,0:T(8,128)(2,1)S(1)} collective-permute-done((bf16[4,256,128]{2,1,0:T(8,128)(2,1)S(1)}, bf16[4,256,128]{2,1,0:T(8,128)(2,1)S(1)}, u32[]{:S(2)}, u32[]{:S(2)}) %collective-permute-start.2) | collective-permute-done | bytes 262176 | tf_op jit(solution)/shard_map/y1/ppermute | solution.py:269
  21.6 0.7 half.4
  22.3 2.7 %collective-permute-start.3 = (bf16[1,4,4,64,128]{4,3,2,1,0:T(8,128)(2,1)S(1)}, bf16[1,4,4,64,128]{4,3,2,1,0:T(8,128)(2,1)S(1)}, u32[]{:S(2)}, u32[]{:S(2)}) collective-permute-start(bf16[1,4,4,64,128]{4,3,2,1,0:T(8,128)(2,1)S(1)} %get-tuple-element.50.refs_6_), channel_id=1, source_target_pairs={{0,16},{4,20},{8,24},{12,28},{16,0},{20,4},{24,8},{28,12},{1,17},{... | collective-permute-start | bytes 786440 | tf_op jit(solution)/shard_map/z4c0/ppermute | solution.py:269
  25.0 1.5 %collective-permute-start.9 = (bf16[4,256,128]{2,1,0:T(8,128)(2,1)S(1)}, bf16[4,256,128]{2,1,0:T(8,128)(2,1)S(1)}, u32[]{:S(2)}, u32[]{:S(2)}) collective-permute-start(bf16[4,256,128]{2,1,0:T(8,128)(2,1)S(1)} %get-tuple-element.57), channel_id=1, source_target_pairs={{0,2},{1,3},{2,0},{3,1},{4,6},{5,7},{6,4},{7,5},{8,10},{9,11},{10,... | collective-permute-start | bytes 786440 | tf_op jit(solution)/shard_map/y4/ppermute | solution.py:269
  26.5 1.2 %collective-permute-done.4.refs_2_ = bf16[4,256,128]{2,1,0:T(8,128)(2,1)S(1)} collective-permute-done((bf16[4,256,128]{2,1,0:T(8,128)(2,1)S(1)}, bf16[4,256,128]{2,1,0:T(8,128)(2,1)S(1)}, u32[]{:S(2)}, u32[]{:S(2)}) %collective-permute-start.4) | collective-permute-done | bytes 262176 | tf_op jit(solution)/shard_map/y2/ppermute | solution.py:269
  27.7 0.8 collective-permute-start.10
  28.5 4.3 %collective-permute-done.5.refs_3_ = bf16[4,256,128]{2,1,0:T(8,128)(2,1)S(1)} collective-permute-done((bf16[4,256,128]{2,1,0:T(8,128)(2,1)S(1)}, bf16[4,256,128]{2,1,0:T(8,128)(2,1)S(1)}, u32[]{:S(2)}, u32[]{:S(2)}) %collective-permute-start.5) | collective-permute-done | bytes 262176 | tf_op jit(solution)/shard_map/y3/ppermute | solution.py:269
  32.8 0.7 half.5
  33.5 1.6 %collective-permute-start.11 = (bf16[4,256,128]{2,1,0:T(8,128)(2,1)S(1)}, bf16[4,256,128]{2,1,0:T(8,128)(2,1)S(1)}, u32[]{:S(2)}, u32[]{:S(2)}) collective-permute-start(bf16[4,256,128]{2,1,0:T(8,128)(2,1)S(1)} %get-tuple-element.61), channel_id=1, source_target_pairs={{0,2},{1,3},{2,0},{3,1},{4,6},{5,7},{6,4},{7,5},{8,10},{9,11},{10,... | collective-permute-start | bytes 786440 | tf_op jit(solution)/shard_map/y6/ppermute | solution.py:269
  35.2 2.7 %collective-permute-done.3.refs_1_ = bf16[1,4,4,64,128]{4,3,2,1,0:T(8,128)(2,1)S(1)} collective-permute-done((bf16[1,4,4,64,128]{4,3,2,1,0:T(8,128)(2,1)S(1)}, bf16[1,4,4,64,128]{4,3,2,1,0:T(8,128)(2,1)S(1)}, u32[]{:S(2)}, u32[]{:S(2)}) %collective-permute-start.3) | collective-permute-done | bytes 262176 | tf_op jit(solution)/shard_map/z4c0/ppermute | solution.py:269
  37.8 0.0 collective-permute-start.7
  37.8 0.0 collective-permute-done.8.refs_1_
  37.9 4.2 %collective-permute-start.6 = (bf16[2,2,4,64,128]{4,3,2,1,0:T(8,128)(2,1)S(1)}, bf16[2,2,4,64,128]{4,3,2,1,0:T(8,128)(2,1)S(1)}, u32[]{:S(2)}, u32[]{:S(2)}) collective-permute-start(bf16[2,2,4,64,128]{4,3,2,1,0:T(8,128)(2,1)S(1)} %merge.6.refs_6_), channel_id=1, source_target_pairs={{0,8},{4,12},{8,0},{12,4},{16,24},{20,28},{24,16},{28,20},{1,9},{5... | collective-permute-start | bytes 786440 | tf_op jit(solution)/shard_map/z2c0/ppermute | solution.py:269
  42.0 2.0 %collective-permute-done.10.refs_3_ = bf16[4,256,128]{2,1,0:T(8,128)(2,1)S(1)} collective-permute-done((bf16[4,256,128]{2,1,0:T(8,128)(2,1)S(1)}, bf16[4,256,128]{2,1,0:T(8,128)(2,1)S(1)}, u32[]{:S(2)}, u32[]{:S(2)}) %collective-permute-start.10) | collective-permute-done | bytes 262176 | tf_op jit(solution)/shard_map/y5/ppermute | solution.py:269
  44.1 0.7 half.6
  44.8 1.6 %collective-permute-start.14 = (bf16[1,4,4,64,128]{4,3,2,1,0:T(8,128)(2,1)S(1)}, bf16[1,4,4,64,128]{4,3,2,1,0:T(8,128)(2,1)S(1)}, u32[]{:S(2)}, u32[]{:S(2)}) collective-permute-start(bf16[1,4,4,64,128]{4,3,2,1,0:T(8,128)(2,1)S(1)} %get-tuple-element.60.refs_2_), channel_id=1, source_target_pairs={{0,4},{4,0},{8,12},{12,8},{16,20},{20,16},{24,28},{28,24},{1,5},{5... | collective-permute-start | bytes 786440 | tf_op jit(solution)/shard_map/z1c2/ppermute | solution.py:269
  46.4 1.9 %collective-permute-start.18 = (bf16[4,256,128]{2,1,0:T(8,128)(2,1)S(1)}, bf16[4,256,128]{2,1,0:T(8,128)(2,1)S(1)}, u32[]{:S(2)}, u32[]{:S(2)}) collective-permute-start(bf16[4,256,128]{2,1,0:T(8,128)(2,1)S(1)} %get-tuple-element.66), channel_id=1, source_target_pairs={{0,3},{1,2},{2,1},{3,0},{4,7},{5,6},{6,5},{7,4},{8,11},{9,10},{10,... | collective-permute-start | bytes 786440 | tf_op jit(solution)/shard_map/y7/ppermute | solution.py:269
  48.2 1.9 %collective-permute-done.11.refs_3_.refs_2_ = bf16[4,256,128]{2,1,0:T(8,128)(2,1)S(1)} collective-permute-done((bf16[4,256,128]{2,1,0:T(8,128)(2,1)S(1)}, bf16[4,256,128]{2,1,0:T(8,128)(2,1)S(1)}, u32[]{:S(2)}, u32[]{:S(2)}) %collective-permute-start.11) | collective-permute-done | bytes 262176 | tf_op jit(solution)/shard_map/y6/ppermute | solution.py:269
  50.2 2.3 %collective-permute-done.7.refs_1_.refs_5_ = bf16[1,4,4,64,128]{4,3,2,1,0:T(8,128)(2,1)S(1)} collective-permute-done((bf16[1,4,4,64,128]{4,3,2,1,0:T(8,128)(2,1)S(1)}, bf16[1,4,4,64,128]{4,3,2,1,0:T(8,128)(2,1)S(1)}, u32[]{:S(2)}, u32[]{:S(2)}) %collective-permute-start.7) | collective-permute-done | bytes 262176 | tf_op jit(solution)/shard_map/z4c1/ppermute | solution.py:269
  52.5 0.1 collective-permute-start.13
  52.6 0.1 collective-permute-done.6.refs_2_
  52.7 1.6 %collective-permute-start.12 = (bf16[4,1,4,64,128]{4,3,2,1,0:T(8,128)(2,1)S(1)}, bf16[4,1,4,64,128]{4,3,2,1,0:T(8,128)(2,1)S(1)}, u32[]{:S(2)}, u32[]{:S(2)}) collective-permute-start(bf16[4,1,4,64,128]{4,3,2,1,0:T(8,128)(2,1)S(1)} %merge.8.refs_2_), channel_id=1, source_target_pairs={{0,4},{4,0},{8,12},{12,8},{16,20},{20,16},{24,28},{28,24},{1,5},{5... | collective-permute-start | bytes 786440 | tf_op jit(solution)/shard_map/z1c0/ppermute | solution.py:269
  54.4 0.8 collective-permute-done.18.refs_3_
  55.1 0.7 half.7
  55.8 1.8 %collective-permute-start.19 = (bf16[1,4,4,64,128]{4,3,2,1,0:T(8,128)(2,1)S(1)}, bf16[1,4,4,64,128]{4,3,2,1,0:T(8,128)(2,1)S(1)}, u32[]{:S(2)}, u32[]{:S(2)}) collective-permute-start(bf16[1,4,4,64,128]{4,3,2,1,0:T(8,128)(2,1)S(1)} %get-tuple-element.68.refs_3_), channel_id=1, source_target_pairs={{0,4},{4,0},{8,12},{12,8},{16,20},{20,16},{24,28},{28,24},{1,5},{5... | collective-permute-start | bytes 786440 | tf_op jit(solution)/shard_map/z1c3/ppermute | solution.py:269
  57.6 2.6 %collective-permute-start.16 = (bf16[2,1,4,64,128]{4,3,2,1,0:T(8,128)(2,1)S(1)}, bf16[2,1,4,64,128]{4,3,2,1,0:T(8,128)(2,1)S(1)}, u32[]{:S(2)}, u32[]{:S(2)}) collective-permute-start(bf16[2,1,4,64,128]{4,3,2,1,0:T(8,128)(2,1)S(1)} %get-tuple-element.64), channel_id=1, source_target_pairs={{0,16},{4,20},{8,24},{12,28},{16,0},{20,4},{24,8},{28,12},{1,17},{... | collective-permute-start | bytes 393224 | tf_op jit(solution)/shard_map/z4c2/ppermute | solution.py:269
  60.2 1.6 %collective-permute-start.17 = (bf16[2,1,4,64,128]{4,3,2,1,0:T(8,128)(2,1)S(1)}, bf16[2,1,4,64,128]{4,3,2,1,0:T(8,128)(2,1)S(1)}, u32[]{:S(2)}, u32[]{:S(2)}) collective-permute-start(bf16[2,1,4,64,128]{4,3,2,1,0:T(8,128)(2,1)S(1)} %get-tuple-element.65), channel_id=1, source_target_pairs={{0,8},{4,12},{8,0},{12,4},{16,24},{20,28},{24,16},{28,20},{1,9},{5... | collective-permute-start | bytes 393224 | tf_op jit(solution)/shard_map/z2c2/ppermute | solution.py:269
  61.8 0.6 collective-permute-start.20
  62.4 1.4 %collective-permute-start.15 = (bf16[2,1,4,64,128]{4,3,2,1,0:T(8,128)(2,1)S(1)}, bf16[2,1,4,64,128]{4,3,2,1,0:T(8,128)(2,1)S(1)}, u32[]{:S(2)}, u32[]{:S(2)}) collective-permute-start(bf16[2,1,4,64,128]{4,3,2,1,0:T(8,128)(2,1)S(1)} %get-tuple-element.63.refs_5_), channel_id=1, source_target_pairs={{0,24},{4,28},{8,16},{12,20},{16,8},{20,12},{24,0},{28,4},{1,25},{... | collective-permute-start | bytes 393224 | tf_op jit(solution)/shard_map/z6c2/ppermute | solution.py:269
  63.8 2.8 %collective-permute-done.19.refs_1_.refs_13_ = bf16[1,4,4,64,128]{4,3,2,1,0:T(8,128)(2,1)S(1)} collective-permute-done((bf16[1,4,4,64,128]{4,3,2,1,0:T(8,128)(2,1)S(1)}, bf16[1,4,4,64,128]{4,3,2,1,0:T(8,128)(2,1)S(1)}, u32[]{:S(2)}, u32[]{:S(2)}) %collective-permute-start.19) | collective-permute-done | bytes 262176 | tf_op jit(solution)/shard_map/z1c3/ppermute | solution.py:269
  66.6 2.7 %collective-permute-start.21 = (bf16[2,1,4,64,128]{4,3,2,1,0:T(8,128)(2,1)S(1)}, bf16[2,1,4,64,128]{4,3,2,1,0:T(8,128)(2,1)S(1)}, u32[]{:S(2)}, u32[]{:S(2)}) collective-permute-start(bf16[2,1,4,64,128]{4,3,2,1,0:T(8,128)(2,1)S(1)} %get-tuple-element.69.refs_1_), channel_id=1, source_target_pairs={{0,24},{4,28},{8,16},{12,20},{16,8},{20,12},{24,0},{28,4},{1,25},{... | collective-permute-start | bytes 393224 | tf_op jit(solution)/shard_map/z6c3/ppermute | solution.py:269
  69.3 0.1 collective-permute-start.22
  69.5 2.3 %collective-permute-start.23 = (bf16[2,1,4,64,128]{4,3,2,1,0:T(8,128)(2,1)S(1)}, bf16[2,1,4,64,128]{4,3,2,1,0:T(8,128)(2,1)S(1)}, u32[]{:S(2)}, u32[]{:S(2)}) collective-permute-start(bf16[2,1,4,64,128]{4,3,2,1,0:T(8,128)(2,1)S(1)} %get-tuple-element.71), channel_id=1, source_target_pairs={{0,8},{4,12},{8,0},{12,4},{16,24},{20,28},{24,16},{28,20},{1,9},{5... | collective-permute-start | bytes 393224 | tf_op jit(solution)/shard_map/z2c3/ppermute | solution.py:269
  71.8 0.6 collect.1.refs_1_.refs_0_
  72.4 2.5 %collective-permute-done.21.refs_0_.refs_2_ = bf16[2,1,4,64,128]{4,3,2,1,0:T(8,128)(2,1)S(1)} collective-permute-done((bf16[2,1,4,64,128]{4,3,2,1,0:T(8,128)(2,1)S(1)}, bf16[2,1,4,64,128]{4,3,2,1,0:T(8,128)(2,1)S(1)}, u32[]{:S(2)}, u32[]{:S(2)}) %collective-permute-start.21) | collective-permute-done | bytes 131104 | tf_op jit(solution)/shard_map/z6c3/ppermute | solution.py:269
  75.0 8.8 %collective-permute-done.22.refs_0_.refs_3_ = bf16[2,1,4,64,128]{4,3,2,1,0:T(8,128)(2,1)S(1)} collective-permute-done((bf16[2,1,4,64,128]{4,3,2,1,0:T(8,128)(2,1)S(1)}, bf16[2,1,4,64,128]{4,3,2,1,0:T(8,128)(2,1)S(1)}, u32[]{:S(2)}, u32[]{:S(2)}) %collective-permute-start.22) | collective-permute-done | bytes 131104 | tf_op jit(solution)/shard_map/z4c3/ppermute | solution.py:269
  83.8 2.7 %combine.1 = (f32[128,64,128]{2,1,0:T(8,128)}, bf16[128,64,128]{2,1,0:T(8,128)(2,1)S(1)}) custom-call(s32[128]{0:T(128)S(1)} %copy-done.1, s32[2]{0:T(128)S(1)} %pad_add_fusion.place_ref, bf16[128,64,128]{2,1,0:T(8,128)(2,1)S(1)} %collect.1.refs_1_.refs_0_, ...), custom_call_target="tpu_custom_call", output_to_operand_aliasing={{1}: (2, {})} | custom-call | flops 1024 | bytes 1024 | tf_op jit(solution)/shard_map/combine/pallas_call | solution.py:248
  (26 shorter events, 0.2 us)
Async XLA Ops:
  6.2 15.4 %collective-permute-start = (bf16[8,256,128]{2,1,0:T(8,128)(2,1)S(1)}, bf16[8,256,128]{2,1,0:T(8,128)(2,1)S(1)}, u32[]{:S(2)}, u32[]{:S(2)}) collective-permute-start(bf16[8,256,128]{2,1,0:T(8,128)(2,1)S(1)} %get-tuple-element.40), channel_id=1, source_target_pairs={{0,1},{1,0},{2,3},{3,2},{4,5},{5,4},{6,7},{7,6},{8,9},{9,8},{10,11... | collective-permute-start | bytes 1572872 | tf_op jit(solution)/shard_map/beside0/ppermute | solution.py:269
  6.7 9.7 %collective-permute-start.1 = (bf16[4,256,128]{2,1,0:T(8,128)(2,1)S(1)}, bf16[4,256,128]{2,1,0:T(8,128)(2,1)S(1)}, u32[]{:S(2)}, u32[]{:S(2)}) collective-permute-start(bf16[4,256,128]{2,1,0:T(8,128)(2,1)S(1)} %get-tuple-element.41), channel_id=1, source_target_pairs={{0,2},{1,3},{2,0},{3,1},{4,6},{5,7},{6,4},{7,5},{8,10},{9,11},{10,... | collective-permute-start | bytes 786440 | tf_op jit(solution)/shard_map/y0/ppermute | solution.py:269
  9.3 12.3 %collective-permute-start.2 = (bf16[4,256,128]{2,1,0:T(8,128)(2,1)S(1)}, bf16[4,256,128]{2,1,0:T(8,128)(2,1)S(1)}, u32[]{:S(2)}, u32[]{:S(2)}) collective-permute-start(bf16[4,256,128]{2,1,0:T(8,128)(2,1)S(1)} %get-tuple-element.42), channel_id=1, source_target_pairs={{0,3},{1,2},{2,1},{3,0},{4,7},{5,6},{6,5},{7,4},{8,11},{9,10},{10,... | collective-permute-start | bytes 786440 | tf_op jit(solution)/shard_map/y1/ppermute | solution.py:269
  9.4 7.1 %copy-start = (bf16[1000,512]{1,0:T(8,128)(2,1)S(1)}, bf16[1000,512]{1,0:T(8,128)(2,1)}, u32[]{:S(2)}) copy-start(bf16[1000,512]{1,0:T(8,128)(2,1)} %c_ref.1) | copy-start | bytes 3072004
  15.5 22.3 %collective-permute-start.8 = (bf16[8,256,128]{2,1,0:T(8,128)(2,1)S(1)}, bf16[8,256,128]{2,1,0:T(8,128)(2,1)S(1)}, u32[]{:S(2)}, u32[]{:S(2)}) collective-permute-start(bf16[8,256,128]{2,1,0:T(8,128)(2,1)S(1)} %get-tuple-element.56), channel_id=1, source_target_pairs={{0,1},{1,0},{2,3},{3,2},{4,5},{5,4},{6,7},{7,6},{8,9},{9,8},{10,11... | collective-permute-start | bytes 1572872 | tf_op jit(solution)/shard_map/beside1/ppermute | solution.py:269
  17.5 10.2 %collective-permute-start.4 = (bf16[4,256,128]{2,1,0:T(8,128)(2,1)S(1)}, bf16[4,256,128]{2,1,0:T(8,128)(2,1)S(1)}, u32[]{:S(2)}, u32[]{:S(2)}) collective-permute-start(bf16[4,256,128]{2,1,0:T(8,128)(2,1)S(1)} %get-tuple-element.51), channel_id=1, source_target_pairs={{0,2},{1,3},{2,0},{3,1},{4,6},{5,7},{6,4},{7,5},{8,10},{9,11},{10,... | collective-permute-start | bytes 786440 | tf_op jit(solution)/shard_map/y2/ppermute | solution.py:269
  19.5 13.3 %collective-permute-start.5 = (bf16[4,256,128]{2,1,0:T(8,128)(2,1)S(1)}, bf16[4,256,128]{2,1,0:T(8,128)(2,1)S(1)}, u32[]{:S(2)}, u32[]{:S(2)}) collective-permute-start(bf16[4,256,128]{2,1,0:T(8,128)(2,1)S(1)} %get-tuple-element.52), channel_id=1, source_target_pairs={{0,3},{1,2},{2,1},{3,0},{4,7},{5,6},{6,5},{7,4},{8,11},{9,10},{10,... | collective-permute-start | bytes 786440 | tf_op jit(solution)/shard_map/y3/ppermute | solution.py:269
  22.3 15.5 %collective-permute-start.3 = (bf16[1,4,4,64,128]{4,3,2,1,0:T(8,128)(2,1)S(1)}, bf16[1,4,4,64,128]{4,3,2,1,0:T(8,128)(2,1)S(1)}, u32[]{:S(2)}, u32[]{:S(2)}) collective-permute-start(bf16[1,4,4,64,128]{4,3,2,1,0:T(8,128)(2,1)S(1)} %get-tuple-element.50.refs_6_), channel_id=1, source_target_pairs={{0,16},{4,20},{8,24},{12,28},{16,0},{20,4},{24,8},{28,12},{1,17},{... | collective-permute-start | bytes 786440 | tf_op jit(solution)/shard_map/z4c0/ppermute | solution.py:269
  25.0 17.0 %collective-permute-start.9 = (bf16[4,256,128]{2,1,0:T(8,128)(2,1)S(1)}, bf16[4,256,128]{2,1,0:T(8,128)(2,1)S(1)}, u32[]{:S(2)}, u32[]{:S(2)}) collective-permute-start(bf16[4,256,128]{2,1,0:T(8,128)(2,1)S(1)} %get-tuple-element.57), channel_id=1, source_target_pairs={{0,2},{1,3},{2,0},{3,1},{4,6},{5,7},{6,4},{7,5},{8,10},{9,11},{10,... | collective-permute-start | bytes 786440 | tf_op jit(solution)/shard_map/y4/ppermute | solution.py:269
  27.7 16.3 %collective-permute-start.10 = (bf16[4,256,128]{2,1,0:T(8,128)(2,1)S(1)}, bf16[4,256,128]{2,1,0:T(8,128)(2,1)S(1)}, u32[]{:S(2)}, u32[]{:S(2)}) collective-permute-start(bf16[4,256,128]{2,1,0:T(8,128)(2,1)S(1)} %get-tuple-element.58), channel_id=1, source_target_pairs={{0,3},{1,2},{2,1},{3,0},{4,7},{5,6},{6,5},{7,4},{8,11},{9,10},{10,... | collective-permute-start | bytes 786440 | tf_op jit(solution)/shard_map/y5/ppermute | solution.py:269
  33.5 16.7 %collective-permute-start.11 = (bf16[4,256,128]{2,1,0:T(8,128)(2,1)S(1)}, bf16[4,256,128]{2,1,0:T(8,128)(2,1)S(1)}, u32[]{:S(2)}, u32[]{:S(2)}) collective-permute-start(bf16[4,256,128]{2,1,0:T(8,128)(2,1)S(1)} %get-tuple-element.61), channel_id=1, source_target_pairs={{0,2},{1,3},{2,0},{3,1},{4,6},{5,7},{6,4},{7,5},{8,10},{9,11},{10,... | collective-permute-start | bytes 786440 | tf_op jit(solution)/shard_map/y6/ppermute | solution.py:269
  37.8 14.7 %collective-permute-start.7 = (bf16[1,4,4,64,128]{4,3,2,1,0:T(8,128)(2,1)S(1)}, bf16[1,4,4,64,128]{4,3,2,1,0:T(8,128)(2,1)S(1)}, u32[]{:S(2)}, u32[]{:S(2)}) collective-permute-start(bf16[1,4,4,64,128]{4,3,2,1,0:T(8,128)(2,1)S(1)} %get-tuple-element.54.refs_2_), channel_id=1, source_target_pairs={{0,16},{4,20},{8,24},{12,28},{16,0},{20,4},{24,8},{28,12},{1,17},{... | collective-permute-start | bytes 786440 | tf_op jit(solution)/shard_map/z4c1/ppermute | solution.py:269
  37.9 14.8 %collective-permute-start.6 = (bf16[2,2,4,64,128]{4,3,2,1,0:T(8,128)(2,1)S(1)}, bf16[2,2,4,64,128]{4,3,2,1,0:T(8,128)(2,1)S(1)}, u32[]{:S(2)}, u32[]{:S(2)}) collective-permute-start(bf16[2,2,4,64,128]{4,3,2,1,0:T(8,128)(2,1)S(1)} %merge.6.refs_6_), channel_id=1, source_target_pairs={{0,8},{4,12},{8,0},{12,4},{16,24},{20,28},{24,16},{28,20},{1,9},{5... | collective-permute-start | bytes 786440 | tf_op jit(solution)/shard_map/z2c0/ppermute | solution.py:269
  44.8 9.6 %collective-permute-start.14 = (bf16[1,4,4,64,128]{4,3,2,1,0:T(8,128)(2,1)S(1)}, bf16[1,4,4,64,128]{4,3,2,1,0:T(8,128)(2,1)S(1)}, u32[]{:S(2)}, u32[]{:S(2)}) collective-permute-start(bf16[1,4,4,64,128]{4,3,2,1,0:T(8,128)(2,1)S(1)} %get-tuple-element.60.refs_2_), channel_id=1, source_target_pairs={{0,4},{4,0},{8,12},{12,8},{16,20},{20,16},{24,28},{28,24},{1,5},{5... | collective-permute-start | bytes 786440 | tf_op jit(solution)/shard_map/z1c2/ppermute | solution.py:269
  46.4 8.8 %collective-permute-start.18 = (bf16[4,256,128]{2,1,0:T(8,128)(2,1)S(1)}, bf16[4,256,128]{2,1,0:T(8,128)(2,1)S(1)}, u32[]{:S(2)}, u32[]{:S(2)}) collective-permute-start(bf16[4,256,128]{2,1,0:T(8,128)(2,1)S(1)} %get-tuple-element.66), channel_id=1, source_target_pairs={{0,3},{1,2},{2,1},{3,0},{4,7},{5,6},{6,5},{7,4},{8,11},{9,10},{10,... | collective-permute-start | bytes 786440 | tf_op jit(solution)/shard_map/y7/ppermute | solution.py:269
  52.5 9.2 %collective-permute-start.13 = (bf16[2,2,4,64,128]{4,3,2,1,0:T(8,128)(2,1)S(1)}, bf16[2,2,4,64,128]{4,3,2,1,0:T(8,128)(2,1)S(1)}, u32[]{:S(2)}, u32[]{:S(2)}) collective-permute-start(bf16[2,2,4,64,128]{4,3,2,1,0:T(8,128)(2,1)S(1)} %merge.7.refs_3_), channel_id=1, source_target_pairs={{0,8},{4,12},{8,0},{12,4},{16,24},{20,28},{24,16},{28,20},{1,9},{5... | collective-permute-start | bytes 786440 | tf_op jit(solution)/shard_map/z2c1/ppermute | solution.py:269
  52.7 9.7 %collective-permute-start.12 = (bf16[4,1,4,64,128]{4,3,2,1,0:T(8,128)(2,1)S(1)}, bf16[4,1,4,64,128]{4,3,2,1,0:T(8,128)(2,1)S(1)}, u32[]{:S(2)}, u32[]{:S(2)}) collective-permute-start(bf16[4,1,4,64,128]{4,3,2,1,0:T(8,128)(2,1)S(1)} %merge.8.refs_2_), channel_id=1, source_target_pairs={{0,4},{4,0},{8,12},{12,8},{16,20},{20,16},{24,28},{28,24},{1,5},{5... | collective-permute-start | bytes 786440 | tf_op jit(solution)/shard_map/z1c0/ppermute | solution.py:269
  55.8 10.7 %collective-permute-start.19 = (bf16[1,4,4,64,128]{4,3,2,1,0:T(8,128)(2,1)S(1)}, bf16[1,4,4,64,128]{4,3,2,1,0:T(8,128)(2,1)S(1)}, u32[]{:S(2)}, u32[]{:S(2)}) collective-permute-start(bf16[1,4,4,64,128]{4,3,2,1,0:T(8,128)(2,1)S(1)} %get-tuple-element.68.refs_3_), channel_id=1, source_target_pairs={{0,4},{4,0},{8,12},{12,8},{16,20},{20,16},{24,28},{28,24},{1,5},{5... | collective-permute-start | bytes 786440 | tf_op jit(solution)/shard_map/z1c3/ppermute | solution.py:269
  57.6 11.7 %collective-permute-start.16 = (bf16[2,1,4,64,128]{4,3,2,1,0:T(8,128)(2,1)S(1)}, bf16[2,1,4,64,128]{4,3,2,1,0:T(8,128)(2,1)S(1)}, u32[]{:S(2)}, u32[]{:S(2)}) collective-permute-start(bf16[2,1,4,64,128]{4,3,2,1,0:T(8,128)(2,1)S(1)} %get-tuple-element.64), channel_id=1, source_target_pairs={{0,16},{4,20},{8,24},{12,28},{16,0},{20,4},{24,8},{28,12},{1,17},{... | collective-permute-start | bytes 393224 | tf_op jit(solution)/shard_map/z4c2/ppermute | solution.py:269
  60.2 9.3 %collective-permute-start.17 = (bf16[2,1,4,64,128]{4,3,2,1,0:T(8,128)(2,1)S(1)}, bf16[2,1,4,64,128]{4,3,2,1,0:T(8,128)(2,1)S(1)}, u32[]{:S(2)}, u32[]{:S(2)}) collective-permute-start(bf16[2,1,4,64,128]{4,3,2,1,0:T(8,128)(2,1)S(1)} %get-tuple-element.65), channel_id=1, source_target_pairs={{0,8},{4,12},{8,0},{12,4},{16,24},{20,28},{24,16},{28,20},{1,9},{5... | collective-permute-start | bytes 393224 | tf_op jit(solution)/shard_map/z2c2/ppermute | solution.py:269
  61.8 22.0 %collective-permute-start.20 = (bf16[4,1,4,64,128]{4,3,2,1,0:T(8,128)(2,1)S(1)}, bf16[4,1,4,64,128]{4,3,2,1,0:T(8,128)(2,1)S(1)}, u32[]{:S(2)}, u32[]{:S(2)}) collective-permute-start(bf16[4,1,4,64,128]{4,3,2,1,0:T(8,128)(2,1)S(1)} %merge.10.refs_2_), channel_id=1, source_target_pairs={{0,4},{4,0},{8,12},{12,8},{16,20},{20,16},{24,28},{28,24},{1,5},{5... | collective-permute-start | bytes 786440 | tf_op jit(solution)/shard_map/z1c1/ppermute | solution.py:269
  62.4 9.4 %collective-permute-start.15 = (bf16[2,1,4,64,128]{4,3,2,1,0:T(8,128)(2,1)S(1)}, bf16[2,1,4,64,128]{4,3,2,1,0:T(8,128)(2,1)S(1)}, u32[]{:S(2)}, u32[]{:S(2)}) collective-permute-start(bf16[2,1,4,64,128]{4,3,2,1,0:T(8,128)(2,1)S(1)} %get-tuple-element.63.refs_5_), channel_id=1, source_target_pairs={{0,24},{4,28},{8,16},{12,20},{16,8},{20,12},{24,0},{28,4},{1,25},{... | collective-permute-start | bytes 393224 | tf_op jit(solution)/shard_map/z6c2/ppermute | solution.py:269
  66.6 8.4 %collective-permute-start.21 = (bf16[2,1,4,64,128]{4,3,2,1,0:T(8,128)(2,1)S(1)}, bf16[2,1,4,64,128]{4,3,2,1,0:T(8,128)(2,1)S(1)}, u32[]{:S(2)}, u32[]{:S(2)}) collective-permute-start(bf16[2,1,4,64,128]{4,3,2,1,0:T(8,128)(2,1)S(1)} %get-tuple-element.69.refs_1_), channel_id=1, source_target_pairs={{0,24},{4,28},{8,16},{12,20},{16,8},{20,12},{24,0},{28,4},{1,25},{... | collective-permute-start | bytes 393224 | tf_op jit(solution)/shard_map/z6c3/ppermute | solution.py:269
  69.3 14.5 %collective-permute-start.22 = (bf16[2,1,4,64,128]{4,3,2,1,0:T(8,128)(2,1)S(1)}, bf16[2,1,4,64,128]{4,3,2,1,0:T(8,128)(2,1)S(1)}, u32[]{:S(2)}, u32[]{:S(2)}) collective-permute-start(bf16[2,1,4,64,128]{4,3,2,1,0:T(8,128)(2,1)S(1)} %get-tuple-element.70), channel_id=1, source_target_pairs={{0,16},{4,20},{8,24},{12,28},{16,0},{20,4},{24,8},{28,12},{1,17},{... | collective-permute-start | bytes 393224 | tf_op jit(solution)/shard_map/z4c3/ppermute | solution.py:269
  69.5 14.4 %copy-start.1 = (s32[128]{0:T(128)S(1)}, s32[128]{0:T(128)}, u32[]{:S(2)}) copy-start(s32[128]{0:T(128)} %mirror_ref.1) | copy-start | bytes 1540
  69.5 14.4 %collective-permute-start.23 = (bf16[2,1,4,64,128]{4,3,2,1,0:T(8,128)(2,1)S(1)}, bf16[2,1,4,64,128]{4,3,2,1,0:T(8,128)(2,1)S(1)}, u32[]{:S(2)}, u32[]{:S(2)}) collective-permute-start(bf16[2,1,4,64,128]{4,3,2,1,0:T(8,128)(2,1)S(1)} %get-tuple-element.71), channel_id=1, source_target_pairs={{0,8},{4,12},{8,0},{12,4},{16,24},{20,28},{24,16},{28,20},{1,9},{5... | collective-permute-start | bytes 393224 | tf_op jit(solution)/shard_map/z2c3/ppermute | solution.py:269

commit v20 on v19

--- a/solution.py
+++ b/solution.py
@@ -8,7 +8,7 @@
 from jax.sharding import PartitionSpec as P
 
 LANES = 128
-STEP = 128
+STEP = 64
 LATER = {0: (2, [2, 3]), 1: (3, [2]), 2: (3, [3])}
 BATCHES = ((4, 4), (4, 4))
 CHUNKS = sum(BATCHES, ())
@@ -33,11 +33,12 @@
         mine = pl.ds(pl.multiple_of((place_ref[0] ^ o) * LANES, LANES), LANES)
         columns.append(pltpu.make_async_copy(c_hbm.at[:, mine], c_ref.at[:, o * LANES : (o + 1) * LANES], c_sem.at[o]))
     parts = []
-    for n, first in enumerate(range(0, padded, STEP)):
-        lines = pl.ds(first, min(STEP, rows - first))
+    steps = [(0, STEP), (STEP, padded - STEP)]
+    for n, (first, step) in enumerate(steps):
+        lines = pl.ds(first, min(step, rows - first))
         source = x_hbm.at[lines, pl.ds(batch * some, some)]
         parts.append(pltpu.make_async_copy(source, x_ref.at[lines], x_sems.at[n]))
-    for copy in parts[:1] + columns + parts[1:]:
+    for copy in columns + parts:
         copy.start()
     x_ref[rows:] = jnp.zeros((padded - rows, some, depth), jnp.bfloat16)
     to = lax.broadcasted_iota(jnp.int32, (PART, PART), 0)
@@ -46,11 +47,11 @@
     turn_ref[...] = jnp.where(is_source, 1.0, 0.0).astype(jnp.bfloat16)
     for copy in columns:
         copy.wait()
-    for n, first in enumerate(range(0, padded, STEP)):
+    for n, (first, step) in enumerate(steps):
         parts[n].wait()
-        x = x_ref[first : first + STEP].reshape(STEP * some, depth)
+        x = x_ref[first : first + step].reshape(step * some, depth)
         product = jnp.dot(x, c_ref[...], preferred_element_type=jnp.float32).astype(jnp.bfloat16)
-        for part in range(STEP // many):
+        for part in range(step // many):
             lines = jnp.dot(
                 turn_ref[...], product[part * PART : (part + 1) * PART], preferred_element_type=jnp.float32
             ).astype(jnp.bfloat16)
@@ -77,7 +78,7 @@
             pltpu.VMEM((padded, some, depth), jnp.bfloat16),
             pltpu.VMEM((depth, orbitals), jnp.bfloat16),
             pltpu.VMEM((PART, PART), jnp.bfloat16),
-            pltpu.SemaphoreType.DMA((padded // STEP,)),
+            pltpu.SemaphoreType.DMA((2,)),
             pltpu.SemaphoreType.DMA((n_mo,)),
         ],
         compiler_params=pltpu.CompilerParams(vmem_limit_bytes=51 * MIB),

time: 86.7 us -> 86.9 us (level)
  transfers between devices with their start and end apart: 24 -> 24, of which waited for: 13 -> 13; matrix products, arithmetic and copies ran while one was open for 0% -> 0% of each run, Pallas kernels for 12% -> 13%
where the time goes in v20:
time: 86.9 us; the launch traced here: 86.7 us
  starting transfers between devices  34.4 us (40%)
  waiting for transfers between devices  32.2 us (37%)
  Pallas kernels  19.9 us (23%)
    ppermute x24, starting transfers between devices, flipped(): return lax.ppermute(x, axis, [(i, i ^ offset) for i in range(size)])  34.4 us
    ppermute x24, waiting for transfers between devices, flipped(): return lax.ppermute(x, axis, [(i, i ^ offset) for i in range(size)])  32.2 us
    pallas_call x2, Pallas kernels, quarter_of(): pl.pallas_call(functools.partial(quarter_kernel, batch, n_mo, blocks, len...  12.5 us
    pallas_call x4, Pallas kernels, half_of(): pl.pallas_call(functools.partial(half_kernel_after, len(blocks), len(owne...  2.85 us
    pallas_call x1, Pallas kernels, combine(): pl.pallas_call(functools.partial(combine_kernel, sources, sum(CHUNKS), pe...  2.73 us
  transfers between devices with their start and end apart: 24, of which 13 were waited for; matrix products, arithmetic and copies ran while one was open for 0% of the time, Pallas kernels for 13%

profile of v20, /device:TPU:0, one launch (start us, length us, event | category | flops | bytes accessed | tf_op | source)
XLA Modules:
  0.0 86.7 jit_solution(2757217494500735885)
XLA Ops:
  0.0 0.1 pad_add_fusion.place_ref
  0.1 6.3 %quarter.2 = (bf16[8,256,128]{2,1,0:T(8,128)(2,1)S(1)}, bf16[8,256,128]{2,1,0:T(8,128)(2,1)S(1)}, bf16[4,256,128]{2,1,0:T(8,128)(2,1)S(1)}, bf16[4,256,128]{2,1,...) custom-call(s32[2]{0:T(128)S(1)} %pad_add_fusion.place_ref, ...), custom_call_target="tpu_custom_call" | custom-call | flops 1024 | bytes 1024 | tf_op jit(solution)/shard_map/quarter/pallas_call | solution.py:72
  6.4 0.5 collective-permute-start
  6.9 2.6 %collective-permute-start.1 = (bf16[4,256,128]{2,1,0:T(8,128)(2,1)S(1)}, bf16[4,256,128]{2,1,0:T(8,128)(2,1)S(1)}, u32[]{:S(2)}, u32[]{:S(2)}) collective-permute-start(bf16[4,256,128]{2,1,0:T(8,128)(2,1)S(1)} %get-tuple-element.41), channel_id=1, source_target_pairs={{0,2},{1,3},{2,0},{3,1},{4,6},{5,7},{6,4},{7,5},{8,10},{9,11},{10,... | collective-permute-start | bytes 786440 | tf_op jit(solution)/shard_map/y0/ppermute | solution.py:270
  9.5 0.1 collective-permute-start.2
  9.5 6.3 %quarter.3 = (bf16[8,256,128]{2,1,0:T(8,128)(2,1)S(1)}, bf16[8,256,128]{2,1,0:T(8,128)(2,1)S(1)}, bf16[4,256,128]{2,1,0:T(8,128)(2,1)S(1)}, bf16[4,256,128]{2,1,...) custom-call(s32[2]{0:T(128)S(1)} %pad_add_fusion.place_ref, ...), custom_call_target="tpu_custom_call" | custom-call | flops 1024 | bytes 1024 | tf_op jit(solution)/shard_map/quarter/pallas_call | solution.py:72
  15.8 0.2 collective-permute-start.8
  16.0 0.6 collective-permute-done.1.refs_2_
  16.6 1.0 %turn.1 = (bf16[4,256,128]{2,1,0:T(8,128)(2,1)S(1)}, bf16[4,256,128]{2,1,0:T(8,128)(2,1)S(1)}, bf16[512,1024]{1,0:T(8,128)(2,1)S(1)}) custom-call(s32[2]{0:T(128)S(1)} %pad_add_fusion.place_ref, bf16[1000,512]{1,0:T(8,128)(2,1)S(1)} %copy-done, bf16[4,256,128]{2,1,0:T(8,128)(2,1)S(1)} %get-tuple-element.43.refs_0_, ...), custom_call_target="tpu_custom_call", output_to_operand_aliasing={{0}: (2, {}), {1}: (3, {})} | custom-call | flops 1024 | bytes 1024 | tf_op jit(solution)/shard_map/turn/pallas_call | solution.py:108
  17.6 2.0 %collective-permute-start.4 = (bf16[4,256,128]{2,1,0:T(8,128)(2,1)S(1)}, bf16[4,256,128]{2,1,0:T(8,128)(2,1)S(1)}, u32[]{:S(2)}, u32[]{:S(2)}) collective-permute-start(bf16[4,256,128]{2,1,0:T(8,128)(2,1)S(1)} %get-tuple-element.51), channel_id=1, source_target_pairs={{0,2},{1,3},{2,0},{3,1},{4,6},{5,7},{6,4},{7,5},{8,10},{9,11},{10,... | collective-permute-start | bytes 786440 | tf_op jit(solution)/shard_map/y2/ppermute | solution.py:270
  19.6 0.0 collective-permute-start.5
  19.6 2.1 %collective-permute-done.2.refs_3_ = bf16[4,256,128]{2,1,0:T(8,128)(2,1)S(1)} collective-permute-done((bf16[4,256,128]{2,1,0:T(8,128)(2,1)S(1)}, bf16[4,256,128]{2,1,0:T(8,128)(2,1)S(1)}, u32[]{:S(2)}, u32[]{:S(2)}) %collective-permute-start.2) | collective-permute-done | bytes 262176 | tf_op jit(solution)/shard_map/y1/ppermute | solution.py:270
  21.7 0.7 half.4
  22.4 2.7 %collective-permute-start.3 = (bf16[1,4,4,64,128]{4,3,2,1,0:T(8,128)(2,1)S(1)}, bf16[1,4,4,64,128]{4,3,2,1,0:T(8,128)(2,1)S(1)}, u32[]{:S(2)}, u32[]{:S(2)}) collective-permute-start(bf16[1,4,4,64,128]{4,3,2,1,0:T(8,128)(2,1)S(1)} %get-tuple-element.50.refs_6_), channel_id=1, source_target_pairs={{0,16},{4,20},{8,24},{12,28},{16,0},{20,4},{24,8},{28,12},{1,17},{... | collective-permute-start | bytes 786440 | tf_op jit(solution)/shard_map/z4c0/ppermute | solution.py:270
  25.1 1.5 %collective-permute-start.9 = (bf16[4,256,128]{2,1,0:T(8,128)(2,1)S(1)}, bf16[4,256,128]{2,1,0:T(8,128)(2,1)S(1)}, u32[]{:S(2)}, u32[]{:S(2)}) collective-permute-start(bf16[4,256,128]{2,1,0:T(8,128)(2,1)S(1)} %get-tuple-element.57), channel_id=1, source_target_pairs={{0,2},{1,3},{2,0},{3,1},{4,6},{5,7},{6,4},{7,5},{8,10},{9,11},{10,... | collective-permute-start | bytes 786440 | tf_op jit(solution)/shard_map/y4/ppermute | solution.py:270
  26.7 1.2 %collective-permute-done.4.refs_2_ = bf16[4,256,128]{2,1,0:T(8,128)(2,1)S(1)} collective-permute-done((bf16[4,256,128]{2,1,0:T(8,128)(2,1)S(1)}, bf16[4,256,128]{2,1,0:T(8,128)(2,1)S(1)}, u32[]{:S(2)}, u32[]{:S(2)}) %collective-permute-start.4) | collective-permute-done | bytes 262176 | tf_op jit(solution)/shard_map/y2/ppermute | solution.py:270
  27.9 0.8 collective-permute-start.10
  28.6 4.3 %collective-permute-done.5.refs_3_ = bf16[4,256,128]{2,1,0:T(8,128)(2,1)S(1)} collective-permute-done((bf16[4,256,128]{2,1,0:T(8,128)(2,1)S(1)}, bf16[4,256,128]{2,1,0:T(8,128)(2,1)S(1)}, u32[]{:S(2)}, u32[]{:S(2)}) %collective-permute-start.5) | collective-permute-done | bytes 262176 | tf_op jit(solution)/shard_map/y3/ppermute | solution.py:270
  33.0 0.7 half.5
  33.7 1.6 %collective-permute-start.11 = (bf16[4,256,128]{2,1,0:T(8,128)(2,1)S(1)}, bf16[4,256,128]{2,1,0:T(8,128)(2,1)S(1)}, u32[]{:S(2)}, u32[]{:S(2)}) collective-permute-start(bf16[4,256,128]{2,1,0:T(8,128)(2,1)S(1)} %get-tuple-element.61), channel_id=1, source_target_pairs={{0,2},{1,3},{2,0},{3,1},{4,6},{5,7},{6,4},{7,5},{8,10},{9,11},{10,... | collective-permute-start | bytes 786440 | tf_op jit(solution)/shard_map/y6/ppermute | solution.py:270
  35.3 2.6 %collective-permute-done.3.refs_1_ = bf16[1,4,4,64,128]{4,3,2,1,0:T(8,128)(2,1)S(1)} collective-permute-done((bf16[1,4,4,64,128]{4,3,2,1,0:T(8,128)(2,1)S(1)}, bf16[1,4,4,64,128]{4,3,2,1,0:T(8,128)(2,1)S(1)}, u32[]{:S(2)}, u32[]{:S(2)}) %collective-permute-start.3) | collective-permute-done | bytes 262176 | tf_op jit(solution)/shard_map/z4c0/ppermute | solution.py:270
  38.0 0.0 collective-permute-done.8.refs_1_
  38.0 4.2 %collective-permute-start.6 = (bf16[2,2,4,64,128]{4,3,2,1,0:T(8,128)(2,1)S(1)}, bf16[2,2,4,64,128]{4,3,2,1,0:T(8,128)(2,1)S(1)}, u32[]{:S(2)}, u32[]{:S(2)}) collective-permute-start(bf16[2,2,4,64,128]{4,3,2,1,0:T(8,128)(2,1)S(1)} %merge.6.refs_6_), channel_id=1, source_target_pairs={{0,8},{4,12},{8,0},{12,4},{16,24},{20,28},{24,16},{28,20},{1,9},{5... | collective-permute-start | bytes 786440 | tf_op jit(solution)/shard_map/z2c0/ppermute | solution.py:270
  42.2 2.0 %collective-permute-done.10.refs_3_ = bf16[4,256,128]{2,1,0:T(8,128)(2,1)S(1)} collective-permute-done((bf16[4,256,128]{2,1,0:T(8,128)(2,1)S(1)}, bf16[4,256,128]{2,1,0:T(8,128)(2,1)S(1)}, u32[]{:S(2)}, u32[]{:S(2)}) %collective-permute-start.10) | collective-permute-done | bytes 262176 | tf_op jit(solution)/shard_map/y5/ppermute | solution.py:270
  44.2 0.7 half.6
  44.9 1.6 %collective-permute-start.14 = (bf16[1,4,4,64,128]{4,3,2,1,0:T(8,128)(2,1)S(1)}, bf16[1,4,4,64,128]{4,3,2,1,0:T(8,128)(2,1)S(1)}, u32[]{:S(2)}, u32[]{:S(2)}) collective-permute-start(bf16[1,4,4,64,128]{4,3,2,1,0:T(8,128)(2,1)S(1)} %get-tuple-element.60.refs_2_), channel_id=1, source_target_pairs={{0,4},{4,0},{8,12},{12,8},{16,20},{20,16},{24,28},{28,24},{1,5},{5... | collective-permute-start | bytes 786440 | tf_op jit(solution)/shard_map/z1c2/ppermute | solution.py:270
  46.5 1.9 %collective-permute-start.18 = (bf16[4,256,128]{2,1,0:T(8,128)(2,1)S(1)}, bf16[4,256,128]{2,1,0:T(8,128)(2,1)S(1)}, u32[]{:S(2)}, u32[]{:S(2)}) collective-permute-start(bf16[4,256,128]{2,1,0:T(8,128)(2,1)S(1)} %get-tuple-element.66), channel_id=1, source_target_pairs={{0,3},{1,2},{2,1},{3,0},{4,7},{5,6},{6,5},{7,4},{8,11},{9,10},{10,... | collective-permute-start | bytes 786440 | tf_op jit(solution)/shard_map/y7/ppermute | solution.py:270
  48.4 2.0 %collective-permute-done.11.refs_3_.refs_2_ = bf16[4,256,128]{2,1,0:T(8,128)(2,1)S(1)} collective-permute-done((bf16[4,256,128]{2,1,0:T(8,128)(2,1)S(1)}, bf16[4,256,128]{2,1,0:T(8,128)(2,1)S(1)}, u32[]{:S(2)}, u32[]{:S(2)}) %collective-permute-start.11) | collective-permute-done | bytes 262176 | tf_op jit(solution)/shard_map/y6/ppermute | solution.py:270
  50.3 2.3 %collective-permute-done.7.refs_1_.refs_5_ = bf16[1,4,4,64,128]{4,3,2,1,0:T(8,128)(2,1)S(1)} collective-permute-done((bf16[1,4,4,64,128]{4,3,2,1,0:T(8,128)(2,1)S(1)}, bf16[1,4,4,64,128]{4,3,2,1,0:T(8,128)(2,1)S(1)}, u32[]{:S(2)}, u32[]{:S(2)}) %collective-permute-start.7) | collective-permute-done | bytes 262176 | tf_op jit(solution)/shard_map/z4c1/ppermute | solution.py:270
  52.7 0.1 collective-permute-start.13
  52.7 0.1 collective-permute-done.6.refs_2_
  52.8 1.6 %collective-permute-start.12 = (bf16[4,1,4,64,128]{4,3,2,1,0:T(8,128)(2,1)S(1)}, bf16[4,1,4,64,128]{4,3,2,1,0:T(8,128)(2,1)S(1)}, u32[]{:S(2)}, u32[]{:S(2)}) collective-permute-start(bf16[4,1,4,64,128]{4,3,2,1,0:T(8,128)(2,1)S(1)} %merge.8.refs_2_), channel_id=1, source_target_pairs={{0,4},{4,0},{8,12},{12,8},{16,20},{20,16},{24,28},{28,24},{1,5},{5... | collective-permute-start | bytes 786440 | tf_op jit(solution)/shard_map/z1c0/ppermute | solution.py:270
  54.5 0.8 collective-permute-done.18.refs_3_
  55.3 0.7 half.7
  56.0 1.7 %collective-permute-start.19 = (bf16[1,4,4,64,128]{4,3,2,1,0:T(8,128)(2,1)S(1)}, bf16[1,4,4,64,128]{4,3,2,1,0:T(8,128)(2,1)S(1)}, u32[]{:S(2)}, u32[]{:S(2)}) collective-permute-start(bf16[1,4,4,64,128]{4,3,2,1,0:T(8,128)(2,1)S(1)} %get-tuple-element.68.refs_3_), channel_id=1, source_target_pairs={{0,4},{4,0},{8,12},{12,8},{16,20},{20,16},{24,28},{28,24},{1,5},{5... | collective-permute-start | bytes 786440 | tf_op jit(solution)/shard_map/z1c3/ppermute | solution.py:270
  57.7 2.6 %collective-permute-start.16 = (bf16[2,1,4,64,128]{4,3,2,1,0:T(8,128)(2,1)S(1)}, bf16[2,1,4,64,128]{4,3,2,1,0:T(8,128)(2,1)S(1)}, u32[]{:S(2)}, u32[]{:S(2)}) collective-permute-start(bf16[2,1,4,64,128]{4,3,2,1,0:T(8,128)(2,1)S(1)} %get-tuple-element.64), channel_id=1, source_target_pairs={{0,16},{4,20},{8,24},{12,28},{16,0},{20,4},{24,8},{28,12},{1,17},{... | collective-permute-start | bytes 393224 | tf_op jit(solution)/shard_map/z4c2/ppermute | solution.py:270
  60.3 1.6 %collective-permute-start.17 = (bf16[2,1,4,64,128]{4,3,2,1,0:T(8,128)(2,1)S(1)}, bf16[2,1,4,64,128]{4,3,2,1,0:T(8,128)(2,1)S(1)}, u32[]{:S(2)}, u32[]{:S(2)}) collective-permute-start(bf16[2,1,4,64,128]{4,3,2,1,0:T(8,128)(2,1)S(1)} %get-tuple-element.65), channel_id=1, source_target_pairs={{0,8},{4,12},{8,0},{12,4},{16,24},{20,28},{24,16},{28,20},{1,9},{5... | collective-permute-start | bytes 393224 | tf_op jit(solution)/shard_map/z2c2/ppermute | solution.py:270
  61.9 0.0 collective-permute-done.13.refs_2_.refs_6_
  61.9 0.6 collective-permute-start.20
  62.5 1.4 %collective-permute-start.15 = (bf16[2,1,4,64,128]{4,3,2,1,0:T(8,128)(2,1)S(1)}, bf16[2,1,4,64,128]{4,3,2,1,0:T(8,128)(2,1)S(1)}, u32[]{:S(2)}, u32[]{:S(2)}) collective-permute-start(bf16[2,1,4,64,128]{4,3,2,1,0:T(8,128)(2,1)S(1)} %get-tuple-element.63.refs_5_), channel_id=1, source_target_pairs={{0,24},{4,28},{8,16},{12,20},{16,8},{20,12},{24,0},{28,4},{1,25},{... | collective-permute-start | bytes 393224 | tf_op jit(solution)/shard_map/z6c2/ppermute | solution.py:270
  63.9 2.7 %collective-permute-done.19.refs_1_.refs_13_ = bf16[1,4,4,64,128]{4,3,2,1,0:T(8,128)(2,1)S(1)} collective-permute-done((bf16[1,4,4,64,128]{4,3,2,1,0:T(8,128)(2,1)S(1)}, bf16[1,4,4,64,128]{4,3,2,1,0:T(8,128)(2,1)S(1)}, u32[]{:S(2)}, u32[]{:S(2)}) %collective-permute-start.19) | collective-permute-done | bytes 262176 | tf_op jit(solution)/shard_map/z1c3/ppermute | solution.py:270
  66.7 2.8 %collective-permute-start.21 = (bf16[2,1,4,64,128]{4,3,2,1,0:T(8,128)(2,1)S(1)}, bf16[2,1,4,64,128]{4,3,2,1,0:T(8,128)(2,1)S(1)}, u32[]{:S(2)}, u32[]{:S(2)}) collective-permute-start(bf16[2,1,4,64,128]{4,3,2,1,0:T(8,128)(2,1)S(1)} %get-tuple-element.69.refs_1_), channel_id=1, source_target_pairs={{0,24},{4,28},{8,16},{12,20},{16,8},{20,12},{24,0},{28,4},{1,25},{... | collective-permute-start | bytes 393224 | tf_op jit(solution)/shard_map/z6c3/ppermute | solution.py:270
  69.5 0.1 collective-permute-start.22
  69.5 2.4 %collective-permute-start.23 = (bf16[2,1,4,64,128]{4,3,2,1,0:T(8,128)(2,1)S(1)}, bf16[2,1,4,64,128]{4,3,2,1,0:T(8,128)(2,1)S(1)}, u32[]{:S(2)}, u32[]{:S(2)}) collective-permute-start(bf16[2,1,4,64,128]{4,3,2,1,0:T(8,128)(2,1)S(1)} %get-tuple-element.71), channel_id=1, source_target_pairs={{0,8},{4,12},{8,0},{12,4},{16,24},{20,28},{24,16},{28,20},{1,9},{5... | collective-permute-start | bytes 393224 | tf_op jit(solution)/shard_map/z2c3/ppermute | solution.py:270
  71.9 0.6 collect.1.refs_1_.refs_0_
  72.6 2.5 %collective-permute-done.21.refs_0_.refs_2_ = bf16[2,1,4,64,128]{4,3,2,1,0:T(8,128)(2,1)S(1)} collective-permute-done((bf16[2,1,4,64,128]{4,3,2,1,0:T(8,128)(2,1)S(1)}, bf16[2,1,4,64,128]{4,3,2,1,0:T(8,128)(2,1)S(1)}, u32[]{:S(2)}, u32[]{:S(2)}) %collective-permute-start.21) | collective-permute-done | bytes 131104 | tf_op jit(solution)/shard_map/z6c3/ppermute | solution.py:270
  75.0 8.9 %collective-permute-done.22.refs_0_.refs_3_ = bf16[2,1,4,64,128]{4,3,2,1,0:T(8,128)(2,1)S(1)} collective-permute-done((bf16[2,1,4,64,128]{4,3,2,1,0:T(8,128)(2,1)S(1)}, bf16[2,1,4,64,128]{4,3,2,1,0:T(8,128)(2,1)S(1)}, u32[]{:S(2)}, u32[]{:S(2)}) %collective-permute-start.22) | collective-permute-done | bytes 131104 | tf_op jit(solution)/shard_map/z4c3/ppermute | solution.py:270
  84.0 2.7 %combine.1 = (f32[128,64,128]{2,1,0:T(8,128)}, bf16[128,64,128]{2,1,0:T(8,128)(2,1)S(1)}) custom-call(s32[128]{0:T(128)S(1)} %copy-done.1, s32[2]{0:T(128)S(1)} %pad_add_fusion.place_ref, bf16[128,64,128]{2,1,0:T(8,128)(2,1)S(1)} %collect.1.refs_1_.refs_0_, ...), custom_call_target="tpu_custom_call", output_to_operand_aliasing={{1}: (2, {})} | custom-call | flops 1024 | bytes 1024 | tf_op jit(solution)/shard_map/combine/pallas_call | solution.py:249
  (26 shorter events, 0.2 us)
Async XLA Ops:
  6.4 15.4 %collective-permute-start = (bf16[8,256,128]{2,1,0:T(8,128)(2,1)S(1)}, bf16[8,256,128]{2,1,0:T(8,128)(2,1)S(1)}, u32[]{:S(2)}, u32[]{:S(2)}) collective-permute-start(bf16[8,256,128]{2,1,0:T(8,128)(2,1)S(1)} %get-tuple-element.40), channel_id=1, source_target_pairs={{0,1},{1,0},{2,3},{3,2},{4,5},{5,4},{6,7},{7,6},{8,9},{9,8},{10,11... | collective-permute-start | bytes 1572872 | tf_op jit(solution)/shard_map/beside0/ppermute | solution.py:270
  6.9 9.8 %collective-permute-start.1 = (bf16[4,256,128]{2,1,0:T(8,128)(2,1)S(1)}, bf16[4,256,128]{2,1,0:T(8,128)(2,1)S(1)}, u32[]{:S(2)}, u32[]{:S(2)}) collective-permute-start(bf16[4,256,128]{2,1,0:T(8,128)(2,1)S(1)} %get-tuple-element.41), channel_id=1, source_target_pairs={{0,2},{1,3},{2,0},{3,1},{4,6},{5,7},{6,4},{7,5},{8,10},{9,11},{10,... | collective-permute-start | bytes 786440 | tf_op jit(solution)/shard_map/y0/ppermute | solution.py:270
  9.5 12.3 %collective-permute-start.2 = (bf16[4,256,128]{2,1,0:T(8,128)(2,1)S(1)}, bf16[4,256,128]{2,1,0:T(8,128)(2,1)S(1)}, u32[]{:S(2)}, u32[]{:S(2)}) collective-permute-start(bf16[4,256,128]{2,1,0:T(8,128)(2,1)S(1)} %get-tuple-element.42), channel_id=1, source_target_pairs={{0,3},{1,2},{2,1},{3,0},{4,7},{5,6},{6,5},{7,4},{8,11},{9,10},{10,... | collective-permute-start | bytes 786440 | tf_op jit(solution)/shard_map/y1/ppermute | solution.py:270
  9.5 7.1 %copy-start = (bf16[1000,512]{1,0:T(8,128)(2,1)S(1)}, bf16[1000,512]{1,0:T(8,128)(2,1)}, u32[]{:S(2)}) copy-start(bf16[1000,512]{1,0:T(8,128)(2,1)} %c_ref.1) | copy-start | bytes 3072004
  15.8 22.2 %collective-permute-start.8 = (bf16[8,256,128]{2,1,0:T(8,128)(2,1)S(1)}, bf16[8,256,128]{2,1,0:T(8,128)(2,1)S(1)}, u32[]{:S(2)}, u32[]{:S(2)}) collective-permute-start(bf16[8,256,128]{2,1,0:T(8,128)(2,1)S(1)} %get-tuple-element.56), channel_id=1, source_target_pairs={{0,1},{1,0},{2,3},{3,2},{4,5},{5,4},{6,7},{7,6},{8,9},{9,8},{10,11... | collective-permute-start | bytes 1572872 | tf_op jit(solution)/shard_map/beside1/ppermute | solution.py:270
  17.6 10.2 %collective-permute-start.4 = (bf16[4,256,128]{2,1,0:T(8,128)(2,1)S(1)}, bf16[4,256,128]{2,1,0:T(8,128)(2,1)S(1)}, u32[]{:S(2)}, u32[]{:S(2)}) collective-permute-start(bf16[4,256,128]{2,1,0:T(8,128)(2,1)S(1)} %get-tuple-element.51), channel_id=1, source_target_pairs={{0,2},{1,3},{2,0},{3,1},{4,6},{5,7},{6,4},{7,5},{8,10},{9,11},{10,... | collective-permute-start | bytes 786440 | tf_op jit(solution)/shard_map/y2/ppermute | solution.py:270
  19.6 13.3 %collective-permute-start.5 = (bf16[4,256,128]{2,1,0:T(8,128)(2,1)S(1)}, bf16[4,256,128]{2,1,0:T(8,128)(2,1)S(1)}, u32[]{:S(2)}, u32[]{:S(2)}) collective-permute-start(bf16[4,256,128]{2,1,0:T(8,128)(2,1)S(1)} %get-tuple-element.52), channel_id=1, source_target_pairs={{0,3},{1,2},{2,1},{3,0},{4,7},{5,6},{6,5},{7,4},{8,11},{9,10},{10,... | collective-permute-start | bytes 786440 | tf_op jit(solution)/shard_map/y3/ppermute | solution.py:270
  22.4 15.5 %collective-permute-start.3 = (bf16[1,4,4,64,128]{4,3,2,1,0:T(8,128)(2,1)S(1)}, bf16[1,4,4,64,128]{4,3,2,1,0:T(8,128)(2,1)S(1)}, u32[]{:S(2)}, u32[]{:S(2)}) collective-permute-start(bf16[1,4,4,64,128]{4,3,2,1,0:T(8,128)(2,1)S(1)} %get-tuple-element.50.refs_6_), channel_id=1, source_target_pairs={{0,16},{4,20},{8,24},{12,28},{16,0},{20,4},{24,8},{28,12},{1,17},{... | collective-permute-start | bytes 786440 | tf_op jit(solution)/shard_map/z4c0/ppermute | solution.py:270
  25.1 17.0 %collective-permute-start.9 = (bf16[4,256,128]{2,1,0:T(8,128)(2,1)S(1)}, bf16[4,256,128]{2,1,0:T(8,128)(2,1)S(1)}, u32[]{:S(2)}, u32[]{:S(2)}) collective-permute-start(bf16[4,256,128]{2,1,0:T(8,128)(2,1)S(1)} %get-tuple-element.57), channel_id=1, source_target_pairs={{0,2},{1,3},{2,0},{3,1},{4,6},{5,7},{6,4},{7,5},{8,10},{9,11},{10,... | collective-permute-start | bytes 786440 | tf_op jit(solution)/shard_map/y4/ppermute | solution.py:270
  27.9 16.3 %collective-permute-start.10 = (bf16[4,256,128]{2,1,0:T(8,128)(2,1)S(1)}, bf16[4,256,128]{2,1,0:T(8,128)(2,1)S(1)}, u32[]{:S(2)}, u32[]{:S(2)}) collective-permute-start(bf16[4,256,128]{2,1,0:T(8,128)(2,1)S(1)} %get-tuple-element.58), channel_id=1, source_target_pairs={{0,3},{1,2},{2,1},{3,0},{4,7},{5,6},{6,5},{7,4},{8,11},{9,10},{10,... | collective-permute-start | bytes 786440 | tf_op jit(solution)/shard_map/y5/ppermute | solution.py:270
  33.7 16.7 %collective-permute-start.11 = (bf16[4,256,128]{2,1,0:T(8,128)(2,1)S(1)}, bf16[4,256,128]{2,1,0:T(8,128)(2,1)S(1)}, u32[]{:S(2)}, u32[]{:S(2)}) collective-permute-start(bf16[4,256,128]{2,1,0:T(8,128)(2,1)S(1)} %get-tuple-element.61), channel_id=1, source_target_pairs={{0,2},{1,3},{2,0},{3,1},{4,6},{5,7},{6,4},{7,5},{8,10},{9,11},{10,... | collective-permute-start | bytes 786440 | tf_op jit(solution)/shard_map/y6/ppermute | solution.py:270
  38.0 14.7 %collective-permute-start.7 = (bf16[1,4,4,64,128]{4,3,2,1,0:T(8,128)(2,1)S(1)}, bf16[1,4,4,64,128]{4,3,2,1,0:T(8,128)(2,1)S(1)}, u32[]{:S(2)}, u32[]{:S(2)}) collective-permute-start(bf16[1,4,4,64,128]{4,3,2,1,0:T(8,128)(2,1)S(1)} %get-tuple-element.54.refs_2_), channel_id=1, source_target_pairs={{0,16},{4,20},{8,24},{12,28},{16,0},{20,4},{24,8},{28,12},{1,17},{... | collective-permute-start | bytes 786440 | tf_op jit(solution)/shard_map/z4c1/ppermute | solution.py:270
  38.0 14.8 %collective-permute-start.6 = (bf16[2,2,4,64,128]{4,3,2,1,0:T(8,128)(2,1)S(1)}, bf16[2,2,4,64,128]{4,3,2,1,0:T(8,128)(2,1)S(1)}, u32[]{:S(2)}, u32[]{:S(2)}) collective-permute-start(bf16[2,2,4,64,128]{4,3,2,1,0:T(8,128)(2,1)S(1)} %merge.6.refs_6_), channel_id=1, source_target_pairs={{0,8},{4,12},{8,0},{12,4},{16,24},{20,28},{24,16},{28,20},{1,9},{5... | collective-permute-start | bytes 786440 | tf_op jit(solution)/shard_map/z2c0/ppermute | solution.py:270
  44.9 9.6 %collective-permute-start.14 = (bf16[1,4,4,64,128]{4,3,2,1,0:T(8,128)(2,1)S(1)}, bf16[1,4,4,64,128]{4,3,2,1,0:T(8,128)(2,1)S(1)}, u32[]{:S(2)}, u32[]{:S(2)}) collective-permute-start(bf16[1,4,4,64,128]{4,3,2,1,0:T(8,128)(2,1)S(1)} %get-tuple-element.60.refs_2_), channel_id=1, source_target_pairs={{0,4},{4,0},{8,12},{12,8},{16,20},{20,16},{24,28},{28,24},{1,5},{5... | collective-permute-start | bytes 786440 | tf_op jit(solution)/shard_map/z1c2/ppermute | solution.py:270
  46.5 8.8 %collective-permute-start.18 = (bf16[4,256,128]{2,1,0:T(8,128)(2,1)S(1)}, bf16[4,256,128]{2,1,0:T(8,128)(2,1)S(1)}, u32[]{:S(2)}, u32[]{:S(2)}) collective-permute-start(bf16[4,256,128]{2,1,0:T(8,128)(2,1)S(1)} %get-tuple-element.66), channel_id=1, source_target_pairs={{0,3},{1,2},{2,1},{3,0},{4,7},{5,6},{6,5},{7,4},{8,11},{9,10},{10,... | collective-permute-start | bytes 786440 | tf_op jit(solution)/shard_map/y7/ppermute | solution.py:270
  52.7 9.2 %collective-permute-start.13 = (bf16[2,2,4,64,128]{4,3,2,1,0:T(8,128)(2,1)S(1)}, bf16[2,2,4,64,128]{4,3,2,1,0:T(8,128)(2,1)S(1)}, u32[]{:S(2)}, u32[]{:S(2)}) collective-permute-start(bf16[2,2,4,64,128]{4,3,2,1,0:T(8,128)(2,1)S(1)} %merge.7.refs_3_), channel_id=1, source_target_pairs={{0,8},{4,12},{8,0},{12,4},{16,24},{20,28},{24,16},{28,20},{1,9},{5... | collective-permute-start | bytes 786440 | tf_op jit(solution)/shard_map/z2c1/ppermute | solution.py:270
  52.8 9.7 %collective-permute-start.12 = (bf16[4,1,4,64,128]{4,3,2,1,0:T(8,128)(2,1)S(1)}, bf16[4,1,4,64,128]{4,3,2,1,0:T(8,128)(2,1)S(1)}, u32[]{:S(2)}, u32[]{:S(2)}) collective-permute-start(bf16[4,1,4,64,128]{4,3,2,1,0:T(8,128)(2,1)S(1)} %merge.8.refs_2_), channel_id=1, source_target_pairs={{0,4},{4,0},{8,12},{12,8},{16,20},{20,16},{24,28},{28,24},{1,5},{5... | collective-permute-start | bytes 786440 | tf_op jit(solution)/shard_map/z1c0/ppermute | solution.py:270
  56.0 10.6 %collective-permute-start.19 = (bf16[1,4,4,64,128]{4,3,2,1,0:T(8,128)(2,1)S(1)}, bf16[1,4,4,64,128]{4,3,2,1,0:T(8,128)(2,1)S(1)}, u32[]{:S(2)}, u32[]{:S(2)}) collective-permute-start(bf16[1,4,4,64,128]{4,3,2,1,0:T(8,128)(2,1)S(1)} %get-tuple-element.68.refs_3_), channel_id=1, source_target_pairs={{0,4},{4,0},{8,12},{12,8},{16,20},{20,16},{24,28},{28,24},{1,5},{5... | collective-permute-start | bytes 786440 | tf_op jit(solution)/shard_map/z1c3/ppermute | solution.py:270
  57.7 11.7 %collective-permute-start.16 = (bf16[2,1,4,64,128]{4,3,2,1,0:T(8,128)(2,1)S(1)}, bf16[2,1,4,64,128]{4,3,2,1,0:T(8,128)(2,1)S(1)}, u32[]{:S(2)}, u32[]{:S(2)}) collective-permute-start(bf16[2,1,4,64,128]{4,3,2,1,0:T(8,128)(2,1)S(1)} %get-tuple-element.64), channel_id=1, source_target_pairs={{0,16},{4,20},{8,24},{12,28},{16,0},{20,4},{24,8},{28,12},{1,17},{... | collective-permute-start | bytes 393224 | tf_op jit(solution)/shard_map/z4c2/ppermute | solution.py:270
  60.3 9.2 %collective-permute-start.17 = (bf16[2,1,4,64,128]{4,3,2,1,0:T(8,128)(2,1)S(1)}, bf16[2,1,4,64,128]{4,3,2,1,0:T(8,128)(2,1)S(1)}, u32[]{:S(2)}, u32[]{:S(2)}) collective-permute-start(bf16[2,1,4,64,128]{4,3,2,1,0:T(8,128)(2,1)S(1)} %get-tuple-element.65), channel_id=1, source_target_pairs={{0,8},{4,12},{8,0},{12,4},{16,24},{20,28},{24,16},{28,20},{1,9},{5... | collective-permute-start | bytes 393224 | tf_op jit(solution)/shard_map/z2c2/ppermute | solution.py:270
  61.9 22.0 %collective-permute-start.20 = (bf16[4,1,4,64,128]{4,3,2,1,0:T(8,128)(2,1)S(1)}, bf16[4,1,4,64,128]{4,3,2,1,0:T(8,128)(2,1)S(1)}, u32[]{:S(2)}, u32[]{:S(2)}) collective-permute-start(bf16[4,1,4,64,128]{4,3,2,1,0:T(8,128)(2,1)S(1)} %merge.10.refs_2_), channel_id=1, source_target_pairs={{0,4},{4,0},{8,12},{12,8},{16,20},{20,16},{24,28},{28,24},{1,5},{5... | collective-permute-start | bytes 786440 | tf_op jit(solution)/shard_map/z1c1/ppermute | solution.py:270
  62.5 9.4 %collective-permute-start.15 = (bf16[2,1,4,64,128]{4,3,2,1,0:T(8,128)(2,1)S(1)}, bf16[2,1,4,64,128]{4,3,2,1,0:T(8,128)(2,1)S(1)}, u32[]{:S(2)}, u32[]{:S(2)}) collective-permute-start(bf16[2,1,4,64,128]{4,3,2,1,0:T(8,128)(2,1)S(1)} %get-tuple-element.63.refs_5_), channel_id=1, source_target_pairs={{0,24},{4,28},{8,16},{12,20},{16,8},{20,12},{24,0},{28,4},{1,25},{... | collective-permute-start | bytes 393224 | tf_op jit(solution)/shard_map/z6c2/ppermute | solution.py:270
  66.7 8.4 %collective-permute-start.21 = (bf16[2,1,4,64,128]{4,3,2,1,0:T(8,128)(2,1)S(1)}, bf16[2,1,4,64,128]{4,3,2,1,0:T(8,128)(2,1)S(1)}, u32[]{:S(2)}, u32[]{:S(2)}) collective-permute-start(bf16[2,1,4,64,128]{4,3,2,1,0:T(8,128)(2,1)S(1)} %get-tuple-element.69.refs_1_), channel_id=1, source_target_pairs={{0,24},{4,28},{8,16},{12,20},{16,8},{20,12},{24,0},{28,4},{1,25},{... | collective-permute-start | bytes 393224 | tf_op jit(solution)/shard_map/z6c3/ppermute | solution.py:270
  69.5 14.5 %collective-permute-start.22 = (bf16[2,1,4,64,128]{4,3,2,1,0:T(8,128)(2,1)S(1)}, bf16[2,1,4,64,128]{4,3,2,1,0:T(8,128)(2,1)S(1)}, u32[]{:S(2)}, u32[]{:S(2)}) collective-permute-start(bf16[2,1,4,64,128]{4,3,2,1,0:T(8,128)(2,1)S(1)} %get-tuple-element.70), channel_id=1, source_target_pairs={{0,16},{4,20},{8,24},{12,28},{16,0},{20,4},{24,8},{28,12},{1,17},{... | collective-permute-start | bytes 393224 | tf_op jit(solution)/shard_map/z4c3/ppermute | solution.py:270
  69.5 14.4 %copy-start.1 = (s32[128]{0:T(128)S(1)}, s32[128]{0:T(128)}, u32[]{:S(2)}) copy-start(s32[128]{0:T(128)} %mirror_ref.1) | copy-start | bytes 1540
  69.5 14.4 %collective-permute-start.23 = (bf16[2,1,4,64,128]{4,3,2,1,0:T(8,128)(2,1)S(1)}, bf16[2,1,4,64,128]{4,3,2,1,0:T(8,128)(2,1)S(1)}, u32[]{:S(2)}, u32[]{:S(2)}) collective-permute-start(bf16[2,1,4,64,128]{4,3,2,1,0:T(8,128)(2,1)S(1)} %get-tuple-element.71), channel_id=1, source_target_pairs={{0,8},{4,12},{8,0},{12,4},{16,24},{20,28},{24,16},{28,20},{1,9},{5... | collective-permute-start | bytes 393224 | tf_op jit(solution)/shard_map/z2c3/ppermute | solution.py:270

commit v21 on v19

--- a/solution.py
+++ b/solution.py
@@ -201,7 +201,7 @@
     for piece, (offsets, first) in zip(pieces, sources):
         for n, offset in enumerate(offsets):
             row = (place_ref[1] ^ offset) * k_all + first
-            held[pl.ds(row, piece.shape[2])] = piece[n, 0]
+            held[pl.ds(row, piece.shape[2])] = 0.5 * piece[n, 0].astype(jnp.float32)
 
 
 def collect_kernel(sources, k_all, place_ref, *refs):
@@ -215,7 +215,7 @@
         functools.partial(collect_kernel, sources, k_all),
         in_specs=[IN_SMEM] + [IN_VMEM] * len(pieces) + [ANYWHERE] * len(after),
         out_specs=IN_VMEM,
-        out_shape=jax.ShapeDtypeStruct((n_pair * k_all, block, lanes), jnp.bfloat16),
+        out_shape=jax.ShapeDtypeStruct((n_pair * k_all, block, lanes), jnp.float32),
         compiler_params=pltpu.CompilerParams(vmem_limit_bytes=24 * MIB),
         cost_estimate=COST,
         name="collect",
@@ -234,7 +234,7 @@
     def _(step):
         for n in range(per_step):
             k = step * per_step + n
-            done[k] = 0.5 * (held[k].astype(jnp.float32) + held[mirror_ref[k]].astype(jnp.float32))
+            done[k] = held[k] + held[mirror_ref[k]]
         copy_of(step).start()
 
     @pl.loop(0, held.shape[0] // per_step)
@@ -251,7 +251,7 @@
         out_specs=[IN_HBM, IN_VMEM],
         out_shape=[
             jax.ShapeDtypeStruct((rows, block, lanes), jnp.float32),
-            jax.ShapeDtypeStruct((rows, block, lanes), jnp.bfloat16),
+            jax.ShapeDtypeStruct((rows, block, lanes), jnp.float32),
         ],
         input_output_aliases={2: 1},
         scratch_shapes=[

time: 86.7 us -> 86.7 us (level)
  transfers between devices with their start and end apart: 24 -> 24, of which waited for: 13 -> 13; matrix products, arithmetic and copies ran while one was open for 0% -> 0% of each run, Pallas kernels for 12% -> 13%
where the time goes in v21:
time: 86.7 us; the launch traced here: 86.6 us
  starting transfers between devices  34.4 us (40%)
  waiting for transfers between devices  32.2 us (37%)
  Pallas kernels  19.7 us (23%)
    ppermute x24, starting transfers between devices, flipped(): return lax.ppermute(x, axis, [(i, i ^ offset) for i in range(size)])  34.4 us
    ppermute x24, waiting for transfers between devices, flipped(): return lax.ppermute(x, axis, [(i, i ^ offset) for i in range(size)])  32.2 us
    pallas_call x2, Pallas kernels, quarter_of(): pl.pallas_call(functools.partial(quarter_kernel, batch, n_mo, blocks, len...  12.3 us
    pallas_call x4, Pallas kernels, half_of(): pl.pallas_call(functools.partial(half_kernel_after, len(blocks), len(owne...  2.85 us
    pallas_call x1, Pallas kernels, combine(): pl.pallas_call(functools.partial(combine_kernel, sources, sum(CHUNKS), pe...  2.76 us
  transfers between devices with their start and end apart: 24, of which 13 were waited for; matrix products, arithmetic and copies ran while one was open for 0% of the time, Pallas kernels for 13%

profile of v21, /device:TPU:0, one launch (start us, length us, event | category | flops | bytes accessed | tf_op | source)
XLA Modules:
  0.0 86.6 jit_solution(4034135762161799277)
XLA Ops:
  0.0 0.1 pad_add_fusion.place_ref
  0.1 6.1 %quarter.2 = (bf16[8,256,128]{2,1,0:T(8,128)(2,1)S(1)}, bf16[8,256,128]{2,1,0:T(8,128)(2,1)S(1)}, bf16[4,256,128]{2,1,0:T(8,128)(2,1)S(1)}, bf16[4,256,128]{2,1,...) custom-call(s32[2]{0:T(128)S(1)} %pad_add_fusion.place_ref, ...), custom_call_target="tpu_custom_call" | custom-call | flops 1024 | bytes 1024 | tf_op jit(solution)/shard_map/quarter/pallas_call | solution.py:71
  6.2 0.5 collective-permute-start
  6.7 2.6 %collective-permute-start.1 = (bf16[4,256,128]{2,1,0:T(8,128)(2,1)S(1)}, bf16[4,256,128]{2,1,0:T(8,128)(2,1)S(1)}, u32[]{:S(2)}, u32[]{:S(2)}) collective-permute-start(bf16[4,256,128]{2,1,0:T(8,128)(2,1)S(1)} %get-tuple-element.41), channel_id=1, source_target_pairs={{0,2},{1,3},{2,0},{3,1},{4,6},{5,7},{6,4},{7,5},{8,10},{9,11},{10,... | collective-permute-start | bytes 786440 | tf_op jit(solution)/shard_map/y0/ppermute | solution.py:269
  9.3 0.1 collective-permute-start.2
  9.4 6.1 %quarter.3 = (bf16[8,256,128]{2,1,0:T(8,128)(2,1)S(1)}, bf16[8,256,128]{2,1,0:T(8,128)(2,1)S(1)}, bf16[4,256,128]{2,1,0:T(8,128)(2,1)S(1)}, bf16[4,256,128]{2,1,...) custom-call(s32[2]{0:T(128)S(1)} %pad_add_fusion.place_ref, ...), custom_call_target="tpu_custom_call" | custom-call | flops 1024 | bytes 1024 | tf_op jit(solution)/shard_map/quarter/pallas_call | solution.py:71
  15.5 0.2 collective-permute-start.8
  15.7 0.7 collective-permute-done.1.refs_2_
  16.5 1.0 %turn.1 = (bf16[4,256,128]{2,1,0:T(8,128)(2,1)S(1)}, bf16[4,256,128]{2,1,0:T(8,128)(2,1)S(1)}, bf16[512,1024]{1,0:T(8,128)(2,1)S(1)}) custom-call(s32[2]{0:T(128)S(1)} %pad_add_fusion.place_ref, bf16[1000,512]{1,0:T(8,128)(2,1)S(1)} %copy-done, bf16[4,256,128]{2,1,0:T(8,128)(2,1)S(1)} %get-tuple-element.43.refs_0_, ...), custom_call_target="tpu_custom_call", output_to_operand_aliasing={{0}: (2, {}), {1}: (3, {})} | custom-call | flops 1024 | bytes 1024 | tf_op jit(solution)/shard_map/turn/pallas_call | solution.py:107
  17.5 2.0 %collective-permute-start.4 = (bf16[4,256,128]{2,1,0:T(8,128)(2,1)S(1)}, bf16[4,256,128]{2,1,0:T(8,128)(2,1)S(1)}, u32[]{:S(2)}, u32[]{:S(2)}) collective-permute-start(bf16[4,256,128]{2,1,0:T(8,128)(2,1)S(1)} %get-tuple-element.51), channel_id=1, source_target_pairs={{0,2},{1,3},{2,0},{3,1},{4,6},{5,7},{6,4},{7,5},{8,10},{9,11},{10,... | collective-permute-start | bytes 786440 | tf_op jit(solution)/shard_map/y2/ppermute | solution.py:269
  19.5 2.1 %collective-permute-done.2.refs_3_ = bf16[4,256,128]{2,1,0:T(8,128)(2,1)S(1)} collective-permute-done((bf16[4,256,128]{2,1,0:T(8,128)(2,1)S(1)}, bf16[4,256,128]{2,1,0:T(8,128)(2,1)S(1)}, u32[]{:S(2)}, u32[]{:S(2)}) %collective-permute-start.2) | collective-permute-done | bytes 262176 | tf_op jit(solution)/shard_map/y1/ppermute | solution.py:269
  21.6 0.0 collective-permute-done.refs_1_
  21.6 0.7 half.4
  22.3 2.7 %collective-permute-start.3 = (bf16[1,4,4,64,128]{4,3,2,1,0:T(8,128)(2,1)S(1)}, bf16[1,4,4,64,128]{4,3,2,1,0:T(8,128)(2,1)S(1)}, u32[]{:S(2)}, u32[]{:S(2)}) collective-permute-start(bf16[1,4,4,64,128]{4,3,2,1,0:T(8,128)(2,1)S(1)} %get-tuple-element.50.refs_6_), channel_id=1, source_target_pairs={{0,16},{4,20},{8,24},{12,28},{16,0},{20,4},{24,8},{28,12},{1,17},{... | collective-permute-start | bytes 786440 | tf_op jit(solution)/shard_map/z4c0/ppermute | solution.py:269
  25.0 1.5 %collective-permute-start.9 = (bf16[4,256,128]{2,1,0:T(8,128)(2,1)S(1)}, bf16[4,256,128]{2,1,0:T(8,128)(2,1)S(1)}, u32[]{:S(2)}, u32[]{:S(2)}) collective-permute-start(bf16[4,256,128]{2,1,0:T(8,128)(2,1)S(1)} %get-tuple-element.57), channel_id=1, source_target_pairs={{0,2},{1,3},{2,0},{3,1},{4,6},{5,7},{6,4},{7,5},{8,10},{9,11},{10,... | collective-permute-start | bytes 786440 | tf_op jit(solution)/shard_map/y4/ppermute | solution.py:269
  26.5 1.2 %collective-permute-done.4.refs_2_ = bf16[4,256,128]{2,1,0:T(8,128)(2,1)S(1)} collective-permute-done((bf16[4,256,128]{2,1,0:T(8,128)(2,1)S(1)}, bf16[4,256,128]{2,1,0:T(8,128)(2,1)S(1)}, u32[]{:S(2)}, u32[]{:S(2)}) %collective-permute-start.4) | collective-permute-done | bytes 262176 | tf_op jit(solution)/shard_map/y2/ppermute | solution.py:269
  27.7 0.8 collective-permute-start.10
  28.5 4.3 %collective-permute-done.5.refs_3_ = bf16[4,256,128]{2,1,0:T(8,128)(2,1)S(1)} collective-permute-done((bf16[4,256,128]{2,1,0:T(8,128)(2,1)S(1)}, bf16[4,256,128]{2,1,0:T(8,128)(2,1)S(1)}, u32[]{:S(2)}, u32[]{:S(2)}) %collective-permute-start.5) | collective-permute-done | bytes 262176 | tf_op jit(solution)/shard_map/y3/ppermute | solution.py:269
  32.8 0.7 half.5
  33.5 1.6 %collective-permute-start.11 = (bf16[4,256,128]{2,1,0:T(8,128)(2,1)S(1)}, bf16[4,256,128]{2,1,0:T(8,128)(2,1)S(1)}, u32[]{:S(2)}, u32[]{:S(2)}) collective-permute-start(bf16[4,256,128]{2,1,0:T(8,128)(2,1)S(1)} %get-tuple-element.61), channel_id=1, source_target_pairs={{0,2},{1,3},{2,0},{3,1},{4,6},{5,7},{6,4},{7,5},{8,10},{9,11},{10,... | collective-permute-start | bytes 786440 | tf_op jit(solution)/shard_map/y6/ppermute | solution.py:269
  35.2 2.7 %collective-permute-done.3.refs_1_ = bf16[1,4,4,64,128]{4,3,2,1,0:T(8,128)(2,1)S(1)} collective-permute-done((bf16[1,4,4,64,128]{4,3,2,1,0:T(8,128)(2,1)S(1)}, bf16[1,4,4,64,128]{4,3,2,1,0:T(8,128)(2,1)S(1)}, u32[]{:S(2)}, u32[]{:S(2)}) %collective-permute-start.3) | collective-permute-done | bytes 262176 | tf_op jit(solution)/shard_map/z4c0/ppermute | solution.py:269
  37.8 0.0 collective-permute-start.7
  37.9 4.2 %collective-permute-start.6 = (bf16[2,2,4,64,128]{4,3,2,1,0:T(8,128)(2,1)S(1)}, bf16[2,2,4,64,128]{4,3,2,1,0:T(8,128)(2,1)S(1)}, u32[]{:S(2)}, u32[]{:S(2)}) collective-permute-start(bf16[2,2,4,64,128]{4,3,2,1,0:T(8,128)(2,1)S(1)} %merge.6.refs_6_), channel_id=1, source_target_pairs={{0,8},{4,12},{8,0},{12,4},{16,24},{20,28},{24,16},{28,20},{1,9},{5... | collective-permute-start | bytes 786440 | tf_op jit(solution)/shard_map/z2c0/ppermute | solution.py:269
  42.0 2.0 %collective-permute-done.10.refs_3_ = bf16[4,256,128]{2,1,0:T(8,128)(2,1)S(1)} collective-permute-done((bf16[4,256,128]{2,1,0:T(8,128)(2,1)S(1)}, bf16[4,256,128]{2,1,0:T(8,128)(2,1)S(1)}, u32[]{:S(2)}, u32[]{:S(2)}) %collective-permute-start.10) | collective-permute-done | bytes 262176 | tf_op jit(solution)/shard_map/y5/ppermute | solution.py:269
  44.1 0.7 half.6
  44.8 1.6 %collective-permute-start.14 = (bf16[1,4,4,64,128]{4,3,2,1,0:T(8,128)(2,1)S(1)}, bf16[1,4,4,64,128]{4,3,2,1,0:T(8,128)(2,1)S(1)}, u32[]{:S(2)}, u32[]{:S(2)}) collective-permute-start(bf16[1,4,4,64,128]{4,3,2,1,0:T(8,128)(2,1)S(1)} %get-tuple-element.60.refs_2_), channel_id=1, source_target_pairs={{0,4},{4,0},{8,12},{12,8},{16,20},{20,16},{24,28},{28,24},{1,5},{5... | collective-permute-start | bytes 786440 | tf_op jit(solution)/shard_map/z1c2/ppermute | solution.py:269
  46.4 1.9 %collective-permute-start.18 = (bf16[4,256,128]{2,1,0:T(8,128)(2,1)S(1)}, bf16[4,256,128]{2,1,0:T(8,128)(2,1)S(1)}, u32[]{:S(2)}, u32[]{:S(2)}) collective-permute-start(bf16[4,256,128]{2,1,0:T(8,128)(2,1)S(1)} %get-tuple-element.66), channel_id=1, source_target_pairs={{0,3},{1,2},{2,1},{3,0},{4,7},{5,6},{6,5},{7,4},{8,11},{9,10},{10,... | collective-permute-start | bytes 786440 | tf_op jit(solution)/shard_map/y7/ppermute | solution.py:269
  48.2 1.9 %collective-permute-done.11.refs_3_.refs_2_ = bf16[4,256,128]{2,1,0:T(8,128)(2,1)S(1)} collective-permute-done((bf16[4,256,128]{2,1,0:T(8,128)(2,1)S(1)}, bf16[4,256,128]{2,1,0:T(8,128)(2,1)S(1)}, u32[]{:S(2)}, u32[]{:S(2)}) %collective-permute-start.11) | collective-permute-done | bytes 262176 | tf_op jit(solution)/shard_map/y6/ppermute | solution.py:269
  50.2 2.3 %collective-permute-done.7.refs_1_.refs_5_ = bf16[1,4,4,64,128]{4,3,2,1,0:T(8,128)(2,1)S(1)} collective-permute-done((bf16[1,4,4,64,128]{4,3,2,1,0:T(8,128)(2,1)S(1)}, bf16[1,4,4,64,128]{4,3,2,1,0:T(8,128)(2,1)S(1)}, u32[]{:S(2)}, u32[]{:S(2)}) %collective-permute-start.7) | collective-permute-done | bytes 262176 | tf_op jit(solution)/shard_map/z4c1/ppermute | solution.py:269
  52.5 0.1 collective-permute-start.13
  52.6 0.1 collective-permute-done.6.refs_2_
  52.7 1.6 %collective-permute-start.12 = (bf16[4,1,4,64,128]{4,3,2,1,0:T(8,128)(2,1)S(1)}, bf16[4,1,4,64,128]{4,3,2,1,0:T(8,128)(2,1)S(1)}, u32[]{:S(2)}, u32[]{:S(2)}) collective-permute-start(bf16[4,1,4,64,128]{4,3,2,1,0:T(8,128)(2,1)S(1)} %merge.8.refs_2_), channel_id=1, source_target_pairs={{0,4},{4,0},{8,12},{12,8},{16,20},{20,16},{24,28},{28,24},{1,5},{5... | collective-permute-start | bytes 786440 | tf_op jit(solution)/shard_map/z1c0/ppermute | solution.py:269
  54.4 0.7 collective-permute-done.18.refs_3_
  55.1 0.7 half.7
  55.8 1.8 %collective-permute-start.19 = (bf16[1,4,4,64,128]{4,3,2,1,0:T(8,128)(2,1)S(1)}, bf16[1,4,4,64,128]{4,3,2,1,0:T(8,128)(2,1)S(1)}, u32[]{:S(2)}, u32[]{:S(2)}) collective-permute-start(bf16[1,4,4,64,128]{4,3,2,1,0:T(8,128)(2,1)S(1)} %get-tuple-element.68.refs_3_), channel_id=1, source_target_pairs={{0,4},{4,0},{8,12},{12,8},{16,20},{20,16},{24,28},{28,24},{1,5},{5... | collective-permute-start | bytes 786440 | tf_op jit(solution)/shard_map/z1c3/ppermute | solution.py:269
  57.6 2.6 %collective-permute-start.16 = (bf16[2,1,4,64,128]{4,3,2,1,0:T(8,128)(2,1)S(1)}, bf16[2,1,4,64,128]{4,3,2,1,0:T(8,128)(2,1)S(1)}, u32[]{:S(2)}, u32[]{:S(2)}) collective-permute-start(bf16[2,1,4,64,128]{4,3,2,1,0:T(8,128)(2,1)S(1)} %get-tuple-element.64), channel_id=1, source_target_pairs={{0,16},{4,20},{8,24},{12,28},{16,0},{20,4},{24,8},{28,12},{1,17},{... | collective-permute-start | bytes 393224 | tf_op jit(solution)/shard_map/z4c2/ppermute | solution.py:269
  60.2 1.6 %collective-permute-start.17 = (bf16[2,1,4,64,128]{4,3,2,1,0:T(8,128)(2,1)S(1)}, bf16[2,1,4,64,128]{4,3,2,1,0:T(8,128)(2,1)S(1)}, u32[]{:S(2)}, u32[]{:S(2)}) collective-permute-start(bf16[2,1,4,64,128]{4,3,2,1,0:T(8,128)(2,1)S(1)} %get-tuple-element.65), channel_id=1, source_target_pairs={{0,8},{4,12},{8,0},{12,4},{16,24},{20,28},{24,16},{28,20},{1,9},{5... | collective-permute-start | bytes 393224 | tf_op jit(solution)/shard_map/z2c2/ppermute | solution.py:269
  61.8 0.6 collective-permute-start.20
  62.4 1.4 %collective-permute-start.15 = (bf16[2,1,4,64,128]{4,3,2,1,0:T(8,128)(2,1)S(1)}, bf16[2,1,4,64,128]{4,3,2,1,0:T(8,128)(2,1)S(1)}, u32[]{:S(2)}, u32[]{:S(2)}) collective-permute-start(bf16[2,1,4,64,128]{4,3,2,1,0:T(8,128)(2,1)S(1)} %get-tuple-element.63.refs_5_), channel_id=1, source_target_pairs={{0,24},{4,28},{8,16},{12,20},{16,8},{20,12},{24,0},{28,4},{1,25},{... | collective-permute-start | bytes 393224 | tf_op jit(solution)/shard_map/z6c2/ppermute | solution.py:269
  63.8 2.8 %collective-permute-done.19.refs_1_.refs_13_ = bf16[1,4,4,64,128]{4,3,2,1,0:T(8,128)(2,1)S(1)} collective-permute-done((bf16[1,4,4,64,128]{4,3,2,1,0:T(8,128)(2,1)S(1)}, bf16[1,4,4,64,128]{4,3,2,1,0:T(8,128)(2,1)S(1)}, u32[]{:S(2)}, u32[]{:S(2)}) %collective-permute-start.19) | collective-permute-done | bytes 262176 | tf_op jit(solution)/shard_map/z1c3/ppermute | solution.py:269
  66.6 2.7 %collective-permute-start.21 = (bf16[2,1,4,64,128]{4,3,2,1,0:T(8,128)(2,1)S(1)}, bf16[2,1,4,64,128]{4,3,2,1,0:T(8,128)(2,1)S(1)}, u32[]{:S(2)}, u32[]{:S(2)}) collective-permute-start(bf16[2,1,4,64,128]{4,3,2,1,0:T(8,128)(2,1)S(1)} %get-tuple-element.69.refs_1_), channel_id=1, source_target_pairs={{0,24},{4,28},{8,16},{12,20},{16,8},{20,12},{24,0},{28,4},{1,25},{... | collective-permute-start | bytes 393224 | tf_op jit(solution)/shard_map/z6c3/ppermute | solution.py:269
  69.3 0.1 collective-permute-start.22
  69.5 2.3 %collective-permute-start.23 = (bf16[2,1,4,64,128]{4,3,2,1,0:T(8,128)(2,1)S(1)}, bf16[2,1,4,64,128]{4,3,2,1,0:T(8,128)(2,1)S(1)}, u32[]{:S(2)}, u32[]{:S(2)}) collective-permute-start(bf16[2,1,4,64,128]{4,3,2,1,0:T(8,128)(2,1)S(1)} %get-tuple-element.71), channel_id=1, source_target_pairs={{0,8},{4,12},{8,0},{12,4},{16,24},{20,28},{24,16},{28,20},{1,9},{5... | collective-permute-start | bytes 393224 | tf_op jit(solution)/shard_map/z2c3/ppermute | solution.py:269
  71.8 0.0 copy-start.1
  71.8 0.7 collect.1.refs_1_.refs_0_
  72.5 2.4 %collective-permute-done.21.refs_0_.refs_2_ = bf16[2,1,4,64,128]{4,3,2,1,0:T(8,128)(2,1)S(1)} collective-permute-done((bf16[2,1,4,64,128]{4,3,2,1,0:T(8,128)(2,1)S(1)}, bf16[2,1,4,64,128]{4,3,2,1,0:T(8,128)(2,1)S(1)}, u32[]{:S(2)}, u32[]{:S(2)}) %collective-permute-start.21) | collective-permute-done | bytes 131104 | tf_op jit(solution)/shard_map/z6c3/ppermute | solution.py:269
  75.0 8.9 %collective-permute-done.22.refs_0_.refs_3_ = bf16[2,1,4,64,128]{4,3,2,1,0:T(8,128)(2,1)S(1)} collective-permute-done((bf16[2,1,4,64,128]{4,3,2,1,0:T(8,128)(2,1)S(1)}, bf16[2,1,4,64,128]{4,3,2,1,0:T(8,128)(2,1)S(1)}, u32[]{:S(2)}, u32[]{:S(2)}) %collective-permute-start.22) | collective-permute-done | bytes 131104 | tf_op jit(solution)/shard_map/z4c3/ppermute | solution.py:269
  83.8 2.8 %combine.1 = (f32[128,64,128]{2,1,0:T(8,128)}, f32[128,64,128]{2,1,0:T(8,128)S(1)}) custom-call(s32[128]{0:T(128)S(1)} %copy-done.1, s32[2]{0:T(128)S(1)} %pad_add_fusion.place_ref, f32[128,64,128]{2,1,0:T(8,128)S(1)} %collect.1.refs_1_.refs_0_, bf16[4,1,4,64,128]{4,3,2,1,0:T(8,128)(2,1)S(1)} %collective-permute-done.20.refs_1_, ...), custom_call_target="tpu_custom_call", output_to_operand_aliasing={{1}: (2, {})} | custom-call | flops 1024 | bytes 1024 | tf_op jit(solution)/shard_map/combine/pallas_call | solution.py:248
  (26 shorter events, 0.2 us)
Async XLA Ops:
  6.2 15.4 %collective-permute-start = (bf16[8,256,128]{2,1,0:T(8,128)(2,1)S(1)}, bf16[8,256,128]{2,1,0:T(8,128)(2,1)S(1)}, u32[]{:S(2)}, u32[]{:S(2)}) collective-permute-start(bf16[8,256,128]{2,1,0:T(8,128)(2,1)S(1)} %get-tuple-element.40), channel_id=1, source_target_pairs={{0,1},{1,0},{2,3},{3,2},{4,5},{5,4},{6,7},{7,6},{8,9},{9,8},{10,11... | collective-permute-start | bytes 1572872 | tf_op jit(solution)/shard_map/beside0/ppermute | solution.py:269
  6.7 9.7 %collective-permute-start.1 = (bf16[4,256,128]{2,1,0:T(8,128)(2,1)S(1)}, bf16[4,256,128]{2,1,0:T(8,128)(2,1)S(1)}, u32[]{:S(2)}, u32[]{:S(2)}) collective-permute-start(bf16[4,256,128]{2,1,0:T(8,128)(2,1)S(1)} %get-tuple-element.41), channel_id=1, source_target_pairs={{0,2},{1,3},{2,0},{3,1},{4,6},{5,7},{6,4},{7,5},{8,10},{9,11},{10,... | collective-permute-start | bytes 786440 | tf_op jit(solution)/shard_map/y0/ppermute | solution.py:269
  9.3 12.3 %collective-permute-start.2 = (bf16[4,256,128]{2,1,0:T(8,128)(2,1)S(1)}, bf16[4,256,128]{2,1,0:T(8,128)(2,1)S(1)}, u32[]{:S(2)}, u32[]{:S(2)}) collective-permute-start(bf16[4,256,128]{2,1,0:T(8,128)(2,1)S(1)} %get-tuple-element.42), channel_id=1, source_target_pairs={{0,3},{1,2},{2,1},{3,0},{4,7},{5,6},{6,5},{7,4},{8,11},{9,10},{10,... | collective-permute-start | bytes 786440 | tf_op jit(solution)/shard_map/y1/ppermute | solution.py:269
  9.4 7.1 %copy-start = (bf16[1000,512]{1,0:T(8,128)(2,1)S(1)}, bf16[1000,512]{1,0:T(8,128)(2,1)}, u32[]{:S(2)}) copy-start(bf16[1000,512]{1,0:T(8,128)(2,1)} %c_ref.1) | copy-start | bytes 3072004
  15.5 22.3 %collective-permute-start.8 = (bf16[8,256,128]{2,1,0:T(8,128)(2,1)S(1)}, bf16[8,256,128]{2,1,0:T(8,128)(2,1)S(1)}, u32[]{:S(2)}, u32[]{:S(2)}) collective-permute-start(bf16[8,256,128]{2,1,0:T(8,128)(2,1)S(1)} %get-tuple-element.56), channel_id=1, source_target_pairs={{0,1},{1,0},{2,3},{3,2},{4,5},{5,4},{6,7},{7,6},{8,9},{9,8},{10,11... | collective-permute-start | bytes 1572872 | tf_op jit(solution)/shard_map/beside1/ppermute | solution.py:269
  17.5 10.2 %collective-permute-start.4 = (bf16[4,256,128]{2,1,0:T(8,128)(2,1)S(1)}, bf16[4,256,128]{2,1,0:T(8,128)(2,1)S(1)}, u32[]{:S(2)}, u32[]{:S(2)}) collective-permute-start(bf16[4,256,128]{2,1,0:T(8,128)(2,1)S(1)} %get-tuple-element.51), channel_id=1, source_target_pairs={{0,2},{1,3},{2,0},{3,1},{4,6},{5,7},{6,4},{7,5},{8,10},{9,11},{10,... | collective-permute-start | bytes 786440 | tf_op jit(solution)/shard_map/y2/ppermute | solution.py:269
  19.5 13.3 %collective-permute-start.5 = (bf16[4,256,128]{2,1,0:T(8,128)(2,1)S(1)}, bf16[4,256,128]{2,1,0:T(8,128)(2,1)S(1)}, u32[]{:S(2)}, u32[]{:S(2)}) collective-permute-start(bf16[4,256,128]{2,1,0:T(8,128)(2,1)S(1)} %get-tuple-element.52), channel_id=1, source_target_pairs={{0,3},{1,2},{2,1},{3,0},{4,7},{5,6},{6,5},{7,4},{8,11},{9,10},{10,... | collective-permute-start | bytes 786440 | tf_op jit(solution)/shard_map/y3/ppermute | solution.py:269
  22.3 15.5 %collective-permute-start.3 = (bf16[1,4,4,64,128]{4,3,2,1,0:T(8,128)(2,1)S(1)}, bf16[1,4,4,64,128]{4,3,2,1,0:T(8,128)(2,1)S(1)}, u32[]{:S(2)}, u32[]{:S(2)}) collective-permute-start(bf16[1,4,4,64,128]{4,3,2,1,0:T(8,128)(2,1)S(1)} %get-tuple-element.50.refs_6_), channel_id=1, source_target_pairs={{0,16},{4,20},{8,24},{12,28},{16,0},{20,4},{24,8},{28,12},{1,17},{... | collective-permute-start | bytes 786440 | tf_op jit(solution)/shard_map/z4c0/ppermute | solution.py:269
  25.0 17.0 %collective-permute-start.9 = (bf16[4,256,128]{2,1,0:T(8,128)(2,1)S(1)}, bf16[4,256,128]{2,1,0:T(8,128)(2,1)S(1)}, u32[]{:S(2)}, u32[]{:S(2)}) collective-permute-start(bf16[4,256,128]{2,1,0:T(8,128)(2,1)S(1)} %get-tuple-element.57), channel_id=1, source_target_pairs={{0,2},{1,3},{2,0},{3,1},{4,6},{5,7},{6,4},{7,5},{8,10},{9,11},{10,... | collective-permute-start | bytes 786440 | tf_op jit(solution)/shard_map/y4/ppermute | solution.py:269
  27.7 16.3 %collective-permute-start.10 = (bf16[4,256,128]{2,1,0:T(8,128)(2,1)S(1)}, bf16[4,256,128]{2,1,0:T(8,128)(2,1)S(1)}, u32[]{:S(2)}, u32[]{:S(2)}) collective-permute-start(bf16[4,256,128]{2,1,0:T(8,128)(2,1)S(1)} %get-tuple-element.58), channel_id=1, source_target_pairs={{0,3},{1,2},{2,1},{3,0},{4,7},{5,6},{6,5},{7,4},{8,11},{9,10},{10,... | collective-permute-start | bytes 786440 | tf_op jit(solution)/shard_map/y5/ppermute | solution.py:269
  33.5 16.7 %collective-permute-start.11 = (bf16[4,256,128]{2,1,0:T(8,128)(2,1)S(1)}, bf16[4,256,128]{2,1,0:T(8,128)(2,1)S(1)}, u32[]{:S(2)}, u32[]{:S(2)}) collective-permute-start(bf16[4,256,128]{2,1,0:T(8,128)(2,1)S(1)} %get-tuple-element.61), channel_id=1, source_target_pairs={{0,2},{1,3},{2,0},{3,1},{4,6},{5,7},{6,4},{7,5},{8,10},{9,11},{10,... | collective-permute-start | bytes 786440 | tf_op jit(solution)/shard_map/y6/ppermute | solution.py:269
  37.8 14.7 %collective-permute-start.7 = (bf16[1,4,4,64,128]{4,3,2,1,0:T(8,128)(2,1)S(1)}, bf16[1,4,4,64,128]{4,3,2,1,0:T(8,128)(2,1)S(1)}, u32[]{:S(2)}, u32[]{:S(2)}) collective-permute-start(bf16[1,4,4,64,128]{4,3,2,1,0:T(8,128)(2,1)S(1)} %get-tuple-element.54.refs_2_), channel_id=1, source_target_pairs={{0,16},{4,20},{8,24},{12,28},{16,0},{20,4},{24,8},{28,12},{1,17},{... | collective-permute-start | bytes 786440 | tf_op jit(solution)/shard_map/z4c1/ppermute | solution.py:269
  37.9 14.8 %collective-permute-start.6 = (bf16[2,2,4,64,128]{4,3,2,1,0:T(8,128)(2,1)S(1)}, bf16[2,2,4,64,128]{4,3,2,1,0:T(8,128)(2,1)S(1)}, u32[]{:S(2)}, u32[]{:S(2)}) collective-permute-start(bf16[2,2,4,64,128]{4,3,2,1,0:T(8,128)(2,1)S(1)} %merge.6.refs_6_), channel_id=1, source_target_pairs={{0,8},{4,12},{8,0},{12,4},{16,24},{20,28},{24,16},{28,20},{1,9},{5... | collective-permute-start | bytes 786440 | tf_op jit(solution)/shard_map/z2c0/ppermute | solution.py:269
  44.8 9.6 %collective-permute-start.14 = (bf16[1,4,4,64,128]{4,3,2,1,0:T(8,128)(2,1)S(1)}, bf16[1,4,4,64,128]{4,3,2,1,0:T(8,128)(2,1)S(1)}, u32[]{:S(2)}, u32[]{:S(2)}) collective-permute-start(bf16[1,4,4,64,128]{4,3,2,1,0:T(8,128)(2,1)S(1)} %get-tuple-element.60.refs_2_), channel_id=1, source_target_pairs={{0,4},{4,0},{8,12},{12,8},{16,20},{20,16},{24,28},{28,24},{1,5},{5... | collective-permute-start | bytes 786440 | tf_op jit(solution)/shard_map/z1c2/ppermute | solution.py:269
  46.4 8.8 %collective-permute-start.18 = (bf16[4,256,128]{2,1,0:T(8,128)(2,1)S(1)}, bf16[4,256,128]{2,1,0:T(8,128)(2,1)S(1)}, u32[]{:S(2)}, u32[]{:S(2)}) collective-permute-start(bf16[4,256,128]{2,1,0:T(8,128)(2,1)S(1)} %get-tuple-element.66), channel_id=1, source_target_pairs={{0,3},{1,2},{2,1},{3,0},{4,7},{5,6},{6,5},{7,4},{8,11},{9,10},{10,... | collective-permute-start | bytes 786440 | tf_op jit(solution)/shard_map/y7/ppermute | solution.py:269
  52.5 9.2 %collective-permute-start.13 = (bf16[2,2,4,64,128]{4,3,2,1,0:T(8,128)(2,1)S(1)}, bf16[2,2,4,64,128]{4,3,2,1,0:T(8,128)(2,1)S(1)}, u32[]{:S(2)}, u32[]{:S(2)}) collective-permute-start(bf16[2,2,4,64,128]{4,3,2,1,0:T(8,128)(2,1)S(1)} %merge.7.refs_3_), channel_id=1, source_target_pairs={{0,8},{4,12},{8,0},{12,4},{16,24},{20,28},{24,16},{28,20},{1,9},{5... | collective-permute-start | bytes 786440 | tf_op jit(solution)/shard_map/z2c1/ppermute | solution.py:269
  52.7 9.7 %collective-permute-start.12 = (bf16[4,1,4,64,128]{4,3,2,1,0:T(8,128)(2,1)S(1)}, bf16[4,1,4,64,128]{4,3,2,1,0:T(8,128)(2,1)S(1)}, u32[]{:S(2)}, u32[]{:S(2)}) collective-permute-start(bf16[4,1,4,64,128]{4,3,2,1,0:T(8,128)(2,1)S(1)} %merge.8.refs_2_), channel_id=1, source_target_pairs={{0,4},{4,0},{8,12},{12,8},{16,20},{20,16},{24,28},{28,24},{1,5},{5... | collective-permute-start | bytes 786440 | tf_op jit(solution)/shard_map/z1c0/ppermute | solution.py:269
  55.8 10.7 %collective-permute-start.19 = (bf16[1,4,4,64,128]{4,3,2,1,0:T(8,128)(2,1)S(1)}, bf16[1,4,4,64,128]{4,3,2,1,0:T(8,128)(2,1)S(1)}, u32[]{:S(2)}, u32[]{:S(2)}) collective-permute-start(bf16[1,4,4,64,128]{4,3,2,1,0:T(8,128)(2,1)S(1)} %get-tuple-element.68.refs_3_), channel_id=1, source_target_pairs={{0,4},{4,0},{8,12},{12,8},{16,20},{20,16},{24,28},{28,24},{1,5},{5... | collective-permute-start | bytes 786440 | tf_op jit(solution)/shard_map/z1c3/ppermute | solution.py:269
  57.6 11.7 %collective-permute-start.16 = (bf16[2,1,4,64,128]{4,3,2,1,0:T(8,128)(2,1)S(1)}, bf16[2,1,4,64,128]{4,3,2,1,0:T(8,128)(2,1)S(1)}, u32[]{:S(2)}, u32[]{:S(2)}) collective-permute-start(bf16[2,1,4,64,128]{4,3,2,1,0:T(8,128)(2,1)S(1)} %get-tuple-element.64), channel_id=1, source_target_pairs={{0,16},{4,20},{8,24},{12,28},{16,0},{20,4},{24,8},{28,12},{1,17},{... | collective-permute-start | bytes 393224 | tf_op jit(solution)/shard_map/z4c2/ppermute | solution.py:269
  60.2 9.3 %collective-permute-start.17 = (bf16[2,1,4,64,128]{4,3,2,1,0:T(8,128)(2,1)S(1)}, bf16[2,1,4,64,128]{4,3,2,1,0:T(8,128)(2,1)S(1)}, u32[]{:S(2)}, u32[]{:S(2)}) collective-permute-start(bf16[2,1,4,64,128]{4,3,2,1,0:T(8,128)(2,1)S(1)} %get-tuple-element.65), channel_id=1, source_target_pairs={{0,8},{4,12},{8,0},{12,4},{16,24},{20,28},{24,16},{28,20},{1,9},{5... | collective-permute-start | bytes 393224 | tf_op jit(solution)/shard_map/z2c2/ppermute | solution.py:269
  61.8 22.0 %collective-permute-start.20 = (bf16[4,1,4,64,128]{4,3,2,1,0:T(8,128)(2,1)S(1)}, bf16[4,1,4,64,128]{4,3,2,1,0:T(8,128)(2,1)S(1)}, u32[]{:S(2)}, u32[]{:S(2)}) collective-permute-start(bf16[4,1,4,64,128]{4,3,2,1,0:T(8,128)(2,1)S(1)} %merge.10.refs_2_), channel_id=1, source_target_pairs={{0,4},{4,0},{8,12},{12,8},{16,20},{20,16},{24,28},{28,24},{1,5},{5... | collective-permute-start | bytes 786440 | tf_op jit(solution)/shard_map/z1c1/ppermute | solution.py:269
  62.4 9.4 %collective-permute-start.15 = (bf16[2,1,4,64,128]{4,3,2,1,0:T(8,128)(2,1)S(1)}, bf16[2,1,4,64,128]{4,3,2,1,0:T(8,128)(2,1)S(1)}, u32[]{:S(2)}, u32[]{:S(2)}) collective-permute-start(bf16[2,1,4,64,128]{4,3,2,1,0:T(8,128)(2,1)S(1)} %get-tuple-element.63.refs_5_), channel_id=1, source_target_pairs={{0,24},{4,28},{8,16},{12,20},{16,8},{20,12},{24,0},{28,4},{1,25},{... | collective-permute-start | bytes 393224 | tf_op jit(solution)/shard_map/z6c2/ppermute | solution.py:269
  66.6 8.4 %collective-permute-start.21 = (bf16[2,1,4,64,128]{4,3,2,1,0:T(8,128)(2,1)S(1)}, bf16[2,1,4,64,128]{4,3,2,1,0:T(8,128)(2,1)S(1)}, u32[]{:S(2)}, u32[]{:S(2)}) collective-permute-start(bf16[2,1,4,64,128]{4,3,2,1,0:T(8,128)(2,1)S(1)} %get-tuple-element.69.refs_1_), channel_id=1, source_target_pairs={{0,24},{4,28},{8,16},{12,20},{16,8},{20,12},{24,0},{28,4},{1,25},{... | collective-permute-start | bytes 393224 | tf_op jit(solution)/shard_map/z6c3/ppermute | solution.py:269
  69.3 14.5 %collective-permute-start.22 = (bf16[2,1,4,64,128]{4,3,2,1,0:T(8,128)(2,1)S(1)}, bf16[2,1,4,64,128]{4,3,2,1,0:T(8,128)(2,1)S(1)}, u32[]{:S(2)}, u32[]{:S(2)}) collective-permute-start(bf16[2,1,4,64,128]{4,3,2,1,0:T(8,128)(2,1)S(1)} %get-tuple-element.70), channel_id=1, source_target_pairs={{0,16},{4,20},{8,24},{12,28},{16,0},{20,4},{24,8},{28,12},{1,17},{... | collective-permute-start | bytes 393224 | tf_op jit(solution)/shard_map/z4c3/ppermute | solution.py:269
  69.5 14.4 %collective-permute-start.23 = (bf16[2,1,4,64,128]{4,3,2,1,0:T(8,128)(2,1)S(1)}, bf16[2,1,4,64,128]{4,3,2,1,0:T(8,128)(2,1)S(1)}, u32[]{:S(2)}, u32[]{:S(2)}) collective-permute-start(bf16[2,1,4,64,128]{4,3,2,1,0:T(8,128)(2,1)S(1)} %get-tuple-element.71), channel_id=1, source_target_pairs={{0,8},{4,12},{8,0},{12,4},{16,24},{20,28},{24,16},{28,20},{1,9},{5... | collective-permute-start | bytes 393224 | tf_op jit(solution)/shard_map/z2c3/ppermute | solution.py:269
  71.8 12.1 %copy-start.1 = (s32[128]{0:T(128)S(1)}, s32[128]{0:T(128)}, u32[]{:S(2)}) copy-start(s32[128]{0:T(128)} %mirror_ref.1) | copy-start | bytes 1540

commit v22 on v21

--- a/solution.py
+++ b/solution.py
@@ -244,7 +244,7 @@
 
 def combine(held, pieces, sources, mirror, place, after):
     rows, block, lanes = held.shape
-    per_step = max(1, 16 * 64 // block)
+    per_step = max(1, 8 * 64 // block)
     return pl.pallas_call(
         functools.partial(combine_kernel, sources, sum(CHUNKS), per_step),
         in_specs=[IN_SMEM] * 2 + [IN_VMEM] * (1 + len(pieces)) + [ANYWHERE] * len(after),

time: 86.7 us -> 86.8 us (level)
  no operation moved by 1% of the time
where the time goes in v22:
time: 86.8 us; the launch traced here: 86.6 us
  starting transfers between devices  34.4 us (40%)
  waiting for transfers between devices  32.2 us (37%)
  Pallas kernels  19.8 us (23%)
    ppermute x24, starting transfers between devices, flipped(): return lax.ppermute(x, axis, [(i, i ^ offset) for i in range(size)])  34.4 us
    ppermute x24, waiting for transfers between devices, flipped(): return lax.ppermute(x, axis, [(i, i ^ offset) for i in range(size)])  32.2 us
    pallas_call x2, Pallas kernels, quarter_of(): pl.pallas_call(functools.partial(quarter_kernel, batch, n_mo, blocks, len...  12.3 us
    pallas_call x4, Pallas kernels, half_of(): pl.pallas_call(functools.partial(half_kernel_after, len(blocks), len(owne...  2.85 us
    pallas_call x1, Pallas kernels, combine(): pl.pallas_call(functools.partial(combine_kernel, sources, sum(CHUNKS), pe...  2.8 us
  transfers between devices with their start and end apart: 24, of which 13 were waited for; matrix products, arithmetic and copies ran while one was open for 0% of the time, Pallas kernels for 13%

profile of v22, /device:TPU:0, one launch (start us, length us, event | category | flops | bytes accessed | tf_op | source)
XLA Modules:
  0.0 86.6 jit_solution(11607968883329766578)
XLA Ops:
  0.0 0.1 pad_add_fusion.place_ref
  0.1 6.1 %quarter.2 = (bf16[8,256,128]{2,1,0:T(8,128)(2,1)S(1)}, bf16[8,256,128]{2,1,0:T(8,128)(2,1)S(1)}, bf16[4,256,128]{2,1,0:T(8,128)(2,1)S(1)}, bf16[4,256,128]{2,1,...) custom-call(s32[2]{0:T(128)S(1)} %pad_add_fusion.place_ref, ...), custom_call_target="tpu_custom_call" | custom-call | flops 1024 | bytes 1024 | tf_op jit(solution)/shard_map/quarter/pallas_call | solution.py:71
  6.2 0.5 collective-permute-start
  6.7 2.6 %collective-permute-start.1 = (bf16[4,256,128]{2,1,0:T(8,128)(2,1)S(1)}, bf16[4,256,128]{2,1,0:T(8,128)(2,1)S(1)}, u32[]{:S(2)}, u32[]{:S(2)}) collective-permute-start(bf16[4,256,128]{2,1,0:T(8,128)(2,1)S(1)} %get-tuple-element.41), channel_id=1, source_target_pairs={{0,2},{1,3},{2,0},{3,1},{4,6},{5,7},{6,4},{7,5},{8,10},{9,11},{10,... | collective-permute-start | bytes 786440 | tf_op jit(solution)/shard_map/y0/ppermute | solution.py:269
  9.3 0.1 collective-permute-start.2
  9.4 6.1 %quarter.3 = (bf16[8,256,128]{2,1,0:T(8,128)(2,1)S(1)}, bf16[8,256,128]{2,1,0:T(8,128)(2,1)S(1)}, bf16[4,256,128]{2,1,0:T(8,128)(2,1)S(1)}, bf16[4,256,128]{2,1,...) custom-call(s32[2]{0:T(128)S(1)} %pad_add_fusion.place_ref, ...), custom_call_target="tpu_custom_call" | custom-call | flops 1024 | bytes 1024 | tf_op jit(solution)/shard_map/quarter/pallas_call | solution.py:71
  15.5 0.2 collective-permute-start.8
  15.7 0.7 collective-permute-done.1.refs_2_
  16.5 1.0 %turn.1 = (bf16[4,256,128]{2,1,0:T(8,128)(2,1)S(1)}, bf16[4,256,128]{2,1,0:T(8,128)(2,1)S(1)}, bf16[512,1024]{1,0:T(8,128)(2,1)S(1)}) custom-call(s32[2]{0:T(128)S(1)} %pad_add_fusion.place_ref, bf16[1000,512]{1,0:T(8,128)(2,1)S(1)} %copy-done, bf16[4,256,128]{2,1,0:T(8,128)(2,1)S(1)} %get-tuple-element.43.refs_0_, ...), custom_call_target="tpu_custom_call", output_to_operand_aliasing={{0}: (2, {}), {1}: (3, {})} | custom-call | flops 1024 | bytes 1024 | tf_op jit(solution)/shard_map/turn/pallas_call | solution.py:107
  17.5 2.0 %collective-permute-start.4 = (bf16[4,256,128]{2,1,0:T(8,128)(2,1)S(1)}, bf16[4,256,128]{2,1,0:T(8,128)(2,1)S(1)}, u32[]{:S(2)}, u32[]{:S(2)}) collective-permute-start(bf16[4,256,128]{2,1,0:T(8,128)(2,1)S(1)} %get-tuple-element.51), channel_id=1, source_target_pairs={{0,2},{1,3},{2,0},{3,1},{4,6},{5,7},{6,4},{7,5},{8,10},{9,11},{10,... | collective-permute-start | bytes 786440 | tf_op jit(solution)/shard_map/y2/ppermute | solution.py:269
  19.5 2.1 %collective-permute-done.2.refs_3_ = bf16[4,256,128]{2,1,0:T(8,128)(2,1)S(1)} collective-permute-done((bf16[4,256,128]{2,1,0:T(8,128)(2,1)S(1)}, bf16[4,256,128]{2,1,0:T(8,128)(2,1)S(1)}, u32[]{:S(2)}, u32[]{:S(2)}) %collective-permute-start.2) | collective-permute-done | bytes 262176 | tf_op jit(solution)/shard_map/y1/ppermute | solution.py:269
  21.6 0.0 collective-permute-done.refs_1_
  21.6 0.7 half.4
  22.3 2.7 %collective-permute-start.3 = (bf16[1,4,4,64,128]{4,3,2,1,0:T(8,128)(2,1)S(1)}, bf16[1,4,4,64,128]{4,3,2,1,0:T(8,128)(2,1)S(1)}, u32[]{:S(2)}, u32[]{:S(2)}) collective-permute-start(bf16[1,4,4,64,128]{4,3,2,1,0:T(8,128)(2,1)S(1)} %get-tuple-element.50.refs_6_), channel_id=1, source_target_pairs={{0,16},{4,20},{8,24},{12,28},{16,0},{20,4},{24,8},{28,12},{1,17},{... | collective-permute-start | bytes 786440 | tf_op jit(solution)/shard_map/z4c0/ppermute | solution.py:269
  25.0 1.5 %collective-permute-start.9 = (bf16[4,256,128]{2,1,0:T(8,128)(2,1)S(1)}, bf16[4,256,128]{2,1,0:T(8,128)(2,1)S(1)}, u32[]{:S(2)}, u32[]{:S(2)}) collective-permute-start(bf16[4,256,128]{2,1,0:T(8,128)(2,1)S(1)} %get-tuple-element.57), channel_id=1, source_target_pairs={{0,2},{1,3},{2,0},{3,1},{4,6},{5,7},{6,4},{7,5},{8,10},{9,11},{10,... | collective-permute-start | bytes 786440 | tf_op jit(solution)/shard_map/y4/ppermute | solution.py:269
  26.5 1.2 %collective-permute-done.4.refs_2_ = bf16[4,256,128]{2,1,0:T(8,128)(2,1)S(1)} collective-permute-done((bf16[4,256,128]{2,1,0:T(8,128)(2,1)S(1)}, bf16[4,256,128]{2,1,0:T(8,128)(2,1)S(1)}, u32[]{:S(2)}, u32[]{:S(2)}) %collective-permute-start.4) | collective-permute-done | bytes 262176 | tf_op jit(solution)/shard_map/y2/ppermute | solution.py:269
  27.7 0.8 collective-permute-start.10
  28.5 4.3 %collective-permute-done.5.refs_3_ = bf16[4,256,128]{2,1,0:T(8,128)(2,1)S(1)} collective-permute-done((bf16[4,256,128]{2,1,0:T(8,128)(2,1)S(1)}, bf16[4,256,128]{2,1,0:T(8,128)(2,1)S(1)}, u32[]{:S(2)}, u32[]{:S(2)}) %collective-permute-start.5) | collective-permute-done | bytes 262176 | tf_op jit(solution)/shard_map/y3/ppermute | solution.py:269
  32.8 0.7 half.5
  33.5 1.6 %collective-permute-start.11 = (bf16[4,256,128]{2,1,0:T(8,128)(2,1)S(1)}, bf16[4,256,128]{2,1,0:T(8,128)(2,1)S(1)}, u32[]{:S(2)}, u32[]{:S(2)}) collective-permute-start(bf16[4,256,128]{2,1,0:T(8,128)(2,1)S(1)} %get-tuple-element.61), channel_id=1, source_target_pairs={{0,2},{1,3},{2,0},{3,1},{4,6},{5,7},{6,4},{7,5},{8,10},{9,11},{10,... | collective-permute-start | bytes 786440 | tf_op jit(solution)/shard_map/y6/ppermute | solution.py:269
  35.2 2.7 %collective-permute-done.3.refs_1_ = bf16[1,4,4,64,128]{4,3,2,1,0:T(8,128)(2,1)S(1)} collective-permute-done((bf16[1,4,4,64,128]{4,3,2,1,0:T(8,128)(2,1)S(1)}, bf16[1,4,4,64,128]{4,3,2,1,0:T(8,128)(2,1)S(1)}, u32[]{:S(2)}, u32[]{:S(2)}) %collective-permute-start.3) | collective-permute-done | bytes 262176 | tf_op jit(solution)/shard_map/z4c0/ppermute | solution.py:269
  37.8 0.0 collective-permute-start.7
  37.9 4.2 %collective-permute-start.6 = (bf16[2,2,4,64,128]{4,3,2,1,0:T(8,128)(2,1)S(1)}, bf16[2,2,4,64,128]{4,3,2,1,0:T(8,128)(2,1)S(1)}, u32[]{:S(2)}, u32[]{:S(2)}) collective-permute-start(bf16[2,2,4,64,128]{4,3,2,1,0:T(8,128)(2,1)S(1)} %merge.6.refs_6_), channel_id=1, source_target_pairs={{0,8},{4,12},{8,0},{12,4},{16,24},{20,28},{24,16},{28,20},{1,9},{5... | collective-permute-start | bytes 786440 | tf_op jit(solution)/shard_map/z2c0/ppermute | solution.py:269
  42.0 2.0 %collective-permute-done.10.refs_3_ = bf16[4,256,128]{2,1,0:T(8,128)(2,1)S(1)} collective-permute-done((bf16[4,256,128]{2,1,0:T(8,128)(2,1)S(1)}, bf16[4,256,128]{2,1,0:T(8,128)(2,1)S(1)}, u32[]{:S(2)}, u32[]{:S(2)}) %collective-permute-start.10) | collective-permute-done | bytes 262176 | tf_op jit(solution)/shard_map/y5/ppermute | solution.py:269
  44.1 0.7 half.6
  44.8 1.6 %collective-permute-start.14 = (bf16[1,4,4,64,128]{4,3,2,1,0:T(8,128)(2,1)S(1)}, bf16[1,4,4,64,128]{4,3,2,1,0:T(8,128)(2,1)S(1)}, u32[]{:S(2)}, u32[]{:S(2)}) collective-permute-start(bf16[1,4,4,64,128]{4,3,2,1,0:T(8,128)(2,1)S(1)} %get-tuple-element.60.refs_2_), channel_id=1, source_target_pairs={{0,4},{4,0},{8,12},{12,8},{16,20},{20,16},{24,28},{28,24},{1,5},{5... | collective-permute-start | bytes 786440 | tf_op jit(solution)/shard_map/z1c2/ppermute | solution.py:269
  46.4 1.9 %collective-permute-start.18 = (bf16[4,256,128]{2,1,0:T(8,128)(2,1)S(1)}, bf16[4,256,128]{2,1,0:T(8,128)(2,1)S(1)}, u32[]{:S(2)}, u32[]{:S(2)}) collective-permute-start(bf16[4,256,128]{2,1,0:T(8,128)(2,1)S(1)} %get-tuple-element.66), channel_id=1, source_target_pairs={{0,3},{1,2},{2,1},{3,0},{4,7},{5,6},{6,5},{7,4},{8,11},{9,10},{10,... | collective-permute-start | bytes 786440 | tf_op jit(solution)/shard_map/y7/ppermute | solution.py:269
  48.2 1.9 %collective-permute-done.11.refs_3_.refs_2_ = bf16[4,256,128]{2,1,0:T(8,128)(2,1)S(1)} collective-permute-done((bf16[4,256,128]{2,1,0:T(8,128)(2,1)S(1)}, bf16[4,256,128]{2,1,0:T(8,128)(2,1)S(1)}, u32[]{:S(2)}, u32[]{:S(2)}) %collective-permute-start.11) | collective-permute-done | bytes 262176 | tf_op jit(solution)/shard_map/y6/ppermute | solution.py:269
  50.2 2.3 %collective-permute-done.7.refs_1_.refs_5_ = bf16[1,4,4,64,128]{4,3,2,1,0:T(8,128)(2,1)S(1)} collective-permute-done((bf16[1,4,4,64,128]{4,3,2,1,0:T(8,128)(2,1)S(1)}, bf16[1,4,4,64,128]{4,3,2,1,0:T(8,128)(2,1)S(1)}, u32[]{:S(2)}, u32[]{:S(2)}) %collective-permute-start.7) | collective-permute-done | bytes 262176 | tf_op jit(solution)/shard_map/z4c1/ppermute | solution.py:269
  52.5 0.1 collective-permute-start.13
  52.6 0.1 collective-permute-done.6.refs_2_
  52.7 1.6 %collective-permute-start.12 = (bf16[4,1,4,64,128]{4,3,2,1,0:T(8,128)(2,1)S(1)}, bf16[4,1,4,64,128]{4,3,2,1,0:T(8,128)(2,1)S(1)}, u32[]{:S(2)}, u32[]{:S(2)}) collective-permute-start(bf16[4,1,4,64,128]{4,3,2,1,0:T(8,128)(2,1)S(1)} %merge.8.refs_2_), channel_id=1, source_target_pairs={{0,4},{4,0},{8,12},{12,8},{16,20},{20,16},{24,28},{28,24},{1,5},{5... | collective-permute-start | bytes 786440 | tf_op jit(solution)/shard_map/z1c0/ppermute | solution.py:269
  54.4 0.7 collective-permute-done.18.refs_3_
  55.1 0.7 half.7
  55.8 1.8 %collective-permute-start.19 = (bf16[1,4,4,64,128]{4,3,2,1,0:T(8,128)(2,1)S(1)}, bf16[1,4,4,64,128]{4,3,2,1,0:T(8,128)(2,1)S(1)}, u32[]{:S(2)}, u32[]{:S(2)}) collective-permute-start(bf16[1,4,4,64,128]{4,3,2,1,0:T(8,128)(2,1)S(1)} %get-tuple-element.68.refs_3_), channel_id=1, source_target_pairs={{0,4},{4,0},{8,12},{12,8},{16,20},{20,16},{24,28},{28,24},{1,5},{5... | collective-permute-start | bytes 786440 | tf_op jit(solution)/shard_map/z1c3/ppermute | solution.py:269
  57.6 2.6 %collective-permute-start.16 = (bf16[2,1,4,64,128]{4,3,2,1,0:T(8,128)(2,1)S(1)}, bf16[2,1,4,64,128]{4,3,2,1,0:T(8,128)(2,1)S(1)}, u32[]{:S(2)}, u32[]{:S(2)}) collective-permute-start(bf16[2,1,4,64,128]{4,3,2,1,0:T(8,128)(2,1)S(1)} %get-tuple-element.64), channel_id=1, source_target_pairs={{0,16},{4,20},{8,24},{12,28},{16,0},{20,4},{24,8},{28,12},{1,17},{... | collective-permute-start | bytes 393224 | tf_op jit(solution)/shard_map/z4c2/ppermute | solution.py:269
  60.2 1.6 %collective-permute-start.17 = (bf16[2,1,4,64,128]{4,3,2,1,0:T(8,128)(2,1)S(1)}, bf16[2,1,4,64,128]{4,3,2,1,0:T(8,128)(2,1)S(1)}, u32[]{:S(2)}, u32[]{:S(2)}) collective-permute-start(bf16[2,1,4,64,128]{4,3,2,1,0:T(8,128)(2,1)S(1)} %get-tuple-element.65), channel_id=1, source_target_pairs={{0,8},{4,12},{8,0},{12,4},{16,24},{20,28},{24,16},{28,20},{1,9},{5... | collective-permute-start | bytes 393224 | tf_op jit(solution)/shard_map/z2c2/ppermute | solution.py:269
  61.8 0.6 collective-permute-start.20
  62.4 1.4 %collective-permute-start.15 = (bf16[2,1,4,64,128]{4,3,2,1,0:T(8,128)(2,1)S(1)}, bf16[2,1,4,64,128]{4,3,2,1,0:T(8,128)(2,1)S(1)}, u32[]{:S(2)}, u32[]{:S(2)}) collective-permute-start(bf16[2,1,4,64,128]{4,3,2,1,0:T(8,128)(2,1)S(1)} %get-tuple-element.63.refs_5_), channel_id=1, source_target_pairs={{0,24},{4,28},{8,16},{12,20},{16,8},{20,12},{24,0},{28,4},{1,25},{... | collective-permute-start | bytes 393224 | tf_op jit(solution)/shard_map/z6c2/ppermute | solution.py:269
  63.8 2.8 %collective-permute-done.19.refs_1_.refs_13_ = bf16[1,4,4,64,128]{4,3,2,1,0:T(8,128)(2,1)S(1)} collective-permute-done((bf16[1,4,4,64,128]{4,3,2,1,0:T(8,128)(2,1)S(1)}, bf16[1,4,4,64,128]{4,3,2,1,0:T(8,128)(2,1)S(1)}, u32[]{:S(2)}, u32[]{:S(2)}) %collective-permute-start.19) | collective-permute-done | bytes 262176 | tf_op jit(solution)/shard_map/z1c3/ppermute | solution.py:269
  66.6 2.7 %collective-permute-start.21 = (bf16[2,1,4,64,128]{4,3,2,1,0:T(8,128)(2,1)S(1)}, bf16[2,1,4,64,128]{4,3,2,1,0:T(8,128)(2,1)S(1)}, u32[]{:S(2)}, u32[]{:S(2)}) collective-permute-start(bf16[2,1,4,64,128]{4,3,2,1,0:T(8,128)(2,1)S(1)} %get-tuple-element.69.refs_1_), channel_id=1, source_target_pairs={{0,24},{4,28},{8,16},{12,20},{16,8},{20,12},{24,0},{28,4},{1,25},{... | collective-permute-start | bytes 393224 | tf_op jit(solution)/shard_map/z6c3/ppermute | solution.py:269
  69.3 0.1 collective-permute-start.22
  69.5 2.3 %collective-permute-start.23 = (bf16[2,1,4,64,128]{4,3,2,1,0:T(8,128)(2,1)S(1)}, bf16[2,1,4,64,128]{4,3,2,1,0:T(8,128)(2,1)S(1)}, u32[]{:S(2)}, u32[]{:S(2)}) collective-permute-start(bf16[2,1,4,64,128]{4,3,2,1,0:T(8,128)(2,1)S(1)} %get-tuple-element.71), channel_id=1, source_target_pairs={{0,8},{4,12},{8,0},{12,4},{16,24},{20,28},{24,16},{28,20},{1,9},{5... | collective-permute-start | bytes 393224 | tf_op jit(solution)/shard_map/z2c3/ppermute | solution.py:269
  71.8 0.0 copy-start.1
  71.8 0.7 collect.1.refs_1_.refs_0_
  72.5 2.4 %collective-permute-done.21.refs_0_.refs_2_ = bf16[2,1,4,64,128]{4,3,2,1,0:T(8,128)(2,1)S(1)} collective-permute-done((bf16[2,1,4,64,128]{4,3,2,1,0:T(8,128)(2,1)S(1)}, bf16[2,1,4,64,128]{4,3,2,1,0:T(8,128)(2,1)S(1)}, u32[]{:S(2)}, u32[]{:S(2)}) %collective-permute-start.21) | collective-permute-done | bytes 131104 | tf_op jit(solution)/shard_map/z6c3/ppermute | solution.py:269
  75.0 8.9 %collective-permute-done.22.refs_0_.refs_3_ = bf16[2,1,4,64,128]{4,3,2,1,0:T(8,128)(2,1)S(1)} collective-permute-done((bf16[2,1,4,64,128]{4,3,2,1,0:T(8,128)(2,1)S(1)}, bf16[2,1,4,64,128]{4,3,2,1,0:T(8,128)(2,1)S(1)}, u32[]{:S(2)}, u32[]{:S(2)}) %collective-permute-start.22) | collective-permute-done | bytes 131104 | tf_op jit(solution)/shard_map/z4c3/ppermute | solution.py:269
  83.8 2.8 %combine.1 = (f32[128,64,128]{2,1,0:T(8,128)}, f32[128,64,128]{2,1,0:T(8,128)S(1)}) custom-call(s32[128]{0:T(128)S(1)} %copy-done.1, s32[2]{0:T(128)S(1)} %pad_add_fusion.place_ref, f32[128,64,128]{2,1,0:T(8,128)S(1)} %collect.1.refs_1_.refs_0_, bf16[4,1,4,64,128]{4,3,2,1,0:T(8,128)(2,1)S(1)} %collective-permute-done.20.refs_1_, ...), custom_call_target="tpu_custom_call", output_to_operand_aliasing={{1}: (2, {})} | custom-call | flops 1024 | bytes 1024 | tf_op jit(solution)/shard_map/combine/pallas_call | solution.py:248
  (26 shorter events, 0.2 us)
Async XLA Ops:
  6.2 15.4 %collective-permute-start = (bf16[8,256,128]{2,1,0:T(8,128)(2,1)S(1)}, bf16[8,256,128]{2,1,0:T(8,128)(2,1)S(1)}, u32[]{:S(2)}, u32[]{:S(2)}) collective-permute-start(bf16[8,256,128]{2,1,0:T(8,128)(2,1)S(1)} %get-tuple-element.40), channel_id=1, source_target_pairs={{0,1},{1,0},{2,3},{3,2},{4,5},{5,4},{6,7},{7,6},{8,9},{9,8},{10,11... | collective-permute-start | bytes 1572872 | tf_op jit(solution)/shard_map/beside0/ppermute | solution.py:269
  6.7 9.7 %collective-permute-start.1 = (bf16[4,256,128]{2,1,0:T(8,128)(2,1)S(1)}, bf16[4,256,128]{2,1,0:T(8,128)(2,1)S(1)}, u32[]{:S(2)}, u32[]{:S(2)}) collective-permute-start(bf16[4,256,128]{2,1,0:T(8,128)(2,1)S(1)} %get-tuple-element.41), channel_id=1, source_target_pairs={{0,2},{1,3},{2,0},{3,1},{4,6},{5,7},{6,4},{7,5},{8,10},{9,11},{10,... | collective-permute-start | bytes 786440 | tf_op jit(solution)/shard_map/y0/ppermute | solution.py:269
  9.3 12.3 %collective-permute-start.2 = (bf16[4,256,128]{2,1,0:T(8,128)(2,1)S(1)}, bf16[4,256,128]{2,1,0:T(8,128)(2,1)S(1)}, u32[]{:S(2)}, u32[]{:S(2)}) collective-permute-start(bf16[4,256,128]{2,1,0:T(8,128)(2,1)S(1)} %get-tuple-element.42), channel_id=1, source_target_pairs={{0,3},{1,2},{2,1},{3,0},{4,7},{5,6},{6,5},{7,4},{8,11},{9,10},{10,... | collective-permute-start | bytes 786440 | tf_op jit(solution)/shard_map/y1/ppermute | solution.py:269
  9.4 7.1 %copy-start = (bf16[1000,512]{1,0:T(8,128)(2,1)S(1)}, bf16[1000,512]{1,0:T(8,128)(2,1)}, u32[]{:S(2)}) copy-start(bf16[1000,512]{1,0:T(8,128)(2,1)} %c_ref.1) | copy-start | bytes 3072004
  15.5 22.3 %collective-permute-start.8 = (bf16[8,256,128]{2,1,0:T(8,128)(2,1)S(1)}, bf16[8,256,128]{2,1,0:T(8,128)(2,1)S(1)}, u32[]{:S(2)}, u32[]{:S(2)}) collective-permute-start(bf16[8,256,128]{2,1,0:T(8,128)(2,1)S(1)} %get-tuple-element.56), channel_id=1, source_target_pairs={{0,1},{1,0},{2,3},{3,2},{4,5},{5,4},{6,7},{7,6},{8,9},{9,8},{10,11... | collective-permute-start | bytes 1572872 | tf_op jit(solution)/shard_map/beside1/ppermute | solution.py:269
  17.5 10.2 %collective-permute-start.4 = (bf16[4,256,128]{2,1,0:T(8,128)(2,1)S(1)}, bf16[4,256,128]{2,1,0:T(8,128)(2,1)S(1)}, u32[]{:S(2)}, u32[]{:S(2)}) collective-permute-start(bf16[4,256,128]{2,1,0:T(8,128)(2,1)S(1)} %get-tuple-element.51), channel_id=1, source_target_pairs={{0,2},{1,3},{2,0},{3,1},{4,6},{5,7},{6,4},{7,5},{8,10},{9,11},{10,... | collective-permute-start | bytes 786440 | tf_op jit(solution)/shard_map/y2/ppermute | solution.py:269
  19.5 13.3 %collective-permute-start.5 = (bf16[4,256,128]{2,1,0:T(8,128)(2,1)S(1)}, bf16[4,256,128]{2,1,0:T(8,128)(2,1)S(1)}, u32[]{:S(2)}, u32[]{:S(2)}) collective-permute-start(bf16[4,256,128]{2,1,0:T(8,128)(2,1)S(1)} %get-tuple-element.52), channel_id=1, source_target_pairs={{0,3},{1,2},{2,1},{3,0},{4,7},{5,6},{6,5},{7,4},{8,11},{9,10},{10,... | collective-permute-start | bytes 786440 | tf_op jit(solution)/shard_map/y3/ppermute | solution.py:269
  22.3 15.5 %collective-permute-start.3 = (bf16[1,4,4,64,128]{4,3,2,1,0:T(8,128)(2,1)S(1)}, bf16[1,4,4,64,128]{4,3,2,1,0:T(8,128)(2,1)S(1)}, u32[]{:S(2)}, u32[]{:S(2)}) collective-permute-start(bf16[1,4,4,64,128]{4,3,2,1,0:T(8,128)(2,1)S(1)} %get-tuple-element.50.refs_6_), channel_id=1, source_target_pairs={{0,16},{4,20},{8,24},{12,28},{16,0},{20,4},{24,8},{28,12},{1,17},{... | collective-permute-start | bytes 786440 | tf_op jit(solution)/shard_map/z4c0/ppermute | solution.py:269
  25.0 17.0 %collective-permute-start.9 = (bf16[4,256,128]{2,1,0:T(8,128)(2,1)S(1)}, bf16[4,256,128]{2,1,0:T(8,128)(2,1)S(1)}, u32[]{:S(2)}, u32[]{:S(2)}) collective-permute-start(bf16[4,256,128]{2,1,0:T(8,128)(2,1)S(1)} %get-tuple-element.57), channel_id=1, source_target_pairs={{0,2},{1,3},{2,0},{3,1},{4,6},{5,7},{6,4},{7,5},{8,10},{9,11},{10,... | collective-permute-start | bytes 786440 | tf_op jit(solution)/shard_map/y4/ppermute | solution.py:269
  27.7 16.3 %collective-permute-start.10 = (bf16[4,256,128]{2,1,0:T(8,128)(2,1)S(1)}, bf16[4,256,128]{2,1,0:T(8,128)(2,1)S(1)}, u32[]{:S(2)}, u32[]{:S(2)}) collective-permute-start(bf16[4,256,128]{2,1,0:T(8,128)(2,1)S(1)} %get-tuple-element.58), channel_id=1, source_target_pairs={{0,3},{1,2},{2,1},{3,0},{4,7},{5,6},{6,5},{7,4},{8,11},{9,10},{10,... | collective-permute-start | bytes 786440 | tf_op jit(solution)/shard_map/y5/ppermute | solution.py:269
  33.5 16.7 %collective-permute-start.11 = (bf16[4,256,128]{2,1,0:T(8,128)(2,1)S(1)}, bf16[4,256,128]{2,1,0:T(8,128)(2,1)S(1)}, u32[]{:S(2)}, u32[]{:S(2)}) collective-permute-start(bf16[4,256,128]{2,1,0:T(8,128)(2,1)S(1)} %get-tuple-element.61), channel_id=1, source_target_pairs={{0,2},{1,3},{2,0},{3,1},{4,6},{5,7},{6,4},{7,5},{8,10},{9,11},{10,... | collective-permute-start | bytes 786440 | tf_op jit(solution)/shard_map/y6/ppermute | solution.py:269
  37.8 14.7 %collective-permute-start.7 = (bf16[1,4,4,64,128]{4,3,2,1,0:T(8,128)(2,1)S(1)}, bf16[1,4,4,64,128]{4,3,2,1,0:T(8,128)(2,1)S(1)}, u32[]{:S(2)}, u32[]{:S(2)}) collective-permute-start(bf16[1,4,4,64,128]{4,3,2,1,0:T(8,128)(2,1)S(1)} %get-tuple-element.54.refs_2_), channel_id=1, source_target_pairs={{0,16},{4,20},{8,24},{12,28},{16,0},{20,4},{24,8},{28,12},{1,17},{... | collective-permute-start | bytes 786440 | tf_op jit(solution)/shard_map/z4c1/ppermute | solution.py:269
  37.9 14.8 %collective-permute-start.6 = (bf16[2,2,4,64,128]{4,3,2,1,0:T(8,128)(2,1)S(1)}, bf16[2,2,4,64,128]{4,3,2,1,0:T(8,128)(2,1)S(1)}, u32[]{:S(2)}, u32[]{:S(2)}) collective-permute-start(bf16[2,2,4,64,128]{4,3,2,1,0:T(8,128)(2,1)S(1)} %merge.6.refs_6_), channel_id=1, source_target_pairs={{0,8},{4,12},{8,0},{12,4},{16,24},{20,28},{24,16},{28,20},{1,9},{5... | collective-permute-start | bytes 786440 | tf_op jit(solution)/shard_map/z2c0/ppermute | solution.py:269
  44.8 9.6 %collective-permute-start.14 = (bf16[1,4,4,64,128]{4,3,2,1,0:T(8,128)(2,1)S(1)}, bf16[1,4,4,64,128]{4,3,2,1,0:T(8,128)(2,1)S(1)}, u32[]{:S(2)}, u32[]{:S(2)}) collective-permute-start(bf16[1,4,4,64,128]{4,3,2,1,0:T(8,128)(2,1)S(1)} %get-tuple-element.60.refs_2_), channel_id=1, source_target_pairs={{0,4},{4,0},{8,12},{12,8},{16,20},{20,16},{24,28},{28,24},{1,5},{5... | collective-permute-start | bytes 786440 | tf_op jit(solution)/shard_map/z1c2/ppermute | solution.py:269
  46.4 8.8 %collective-permute-start.18 = (bf16[4,256,128]{2,1,0:T(8,128)(2,1)S(1)}, bf16[4,256,128]{2,1,0:T(8,128)(2,1)S(1)}, u32[]{:S(2)}, u32[]{:S(2)}) collective-permute-start(bf16[4,256,128]{2,1,0:T(8,128)(2,1)S(1)} %get-tuple-element.66), channel_id=1, source_target_pairs={{0,3},{1,2},{2,1},{3,0},{4,7},{5,6},{6,5},{7,4},{8,11},{9,10},{10,... | collective-permute-start | bytes 786440 | tf_op jit(solution)/shard_map/y7/ppermute | solution.py:269
  52.5 9.2 %collective-permute-start.13 = (bf16[2,2,4,64,128]{4,3,2,1,0:T(8,128)(2,1)S(1)}, bf16[2,2,4,64,128]{4,3,2,1,0:T(8,128)(2,1)S(1)}, u32[]{:S(2)}, u32[]{:S(2)}) collective-permute-start(bf16[2,2,4,64,128]{4,3,2,1,0:T(8,128)(2,1)S(1)} %merge.7.refs_3_), channel_id=1, source_target_pairs={{0,8},{4,12},{8,0},{12,4},{16,24},{20,28},{24,16},{28,20},{1,9},{5... | collective-permute-start | bytes 786440 | tf_op jit(solution)/shard_map/z2c1/ppermute | solution.py:269
  52.7 9.7 %collective-permute-start.12 = (bf16[4,1,4,64,128]{4,3,2,1,0:T(8,128)(2,1)S(1)}, bf16[4,1,4,64,128]{4,3,2,1,0:T(8,128)(2,1)S(1)}, u32[]{:S(2)}, u32[]{:S(2)}) collective-permute-start(bf16[4,1,4,64,128]{4,3,2,1,0:T(8,128)(2,1)S(1)} %merge.8.refs_2_), channel_id=1, source_target_pairs={{0,4},{4,0},{8,12},{12,8},{16,20},{20,16},{24,28},{28,24},{1,5},{5... | collective-permute-start | bytes 786440 | tf_op jit(solution)/shard_map/z1c0/ppermute | solution.py:269
  55.8 10.7 %collective-permute-start.19 = (bf16[1,4,4,64,128]{4,3,2,1,0:T(8,128)(2,1)S(1)}, bf16[1,4,4,64,128]{4,3,2,1,0:T(8,128)(2,1)S(1)}, u32[]{:S(2)}, u32[]{:S(2)}) collective-permute-start(bf16[1,4,4,64,128]{4,3,2,1,0:T(8,128)(2,1)S(1)} %get-tuple-element.68.refs_3_), channel_id=1, source_target_pairs={{0,4},{4,0},{8,12},{12,8},{16,20},{20,16},{24,28},{28,24},{1,5},{5... | collective-permute-start | bytes 786440 | tf_op jit(solution)/shard_map/z1c3/ppermute | solution.py:269
  57.6 11.7 %collective-permute-start.16 = (bf16[2,1,4,64,128]{4,3,2,1,0:T(8,128)(2,1)S(1)}, bf16[2,1,4,64,128]{4,3,2,1,0:T(8,128)(2,1)S(1)}, u32[]{:S(2)}, u32[]{:S(2)}) collective-permute-start(bf16[2,1,4,64,128]{4,3,2,1,0:T(8,128)(2,1)S(1)} %get-tuple-element.64), channel_id=1, source_target_pairs={{0,16},{4,20},{8,24},{12,28},{16,0},{20,4},{24,8},{28,12},{1,17},{... | collective-permute-start | bytes 393224 | tf_op jit(solution)/shard_map/z4c2/ppermute | solution.py:269
  60.2 9.3 %collective-permute-start.17 = (bf16[2,1,4,64,128]{4,3,2,1,0:T(8,128)(2,1)S(1)}, bf16[2,1,4,64,128]{4,3,2,1,0:T(8,128)(2,1)S(1)}, u32[]{:S(2)}, u32[]{:S(2)}) collective-permute-start(bf16[2,1,4,64,128]{4,3,2,1,0:T(8,128)(2,1)S(1)} %get-tuple-element.65), channel_id=1, source_target_pairs={{0,8},{4,12},{8,0},{12,4},{16,24},{20,28},{24,16},{28,20},{1,9},{5... | collective-permute-start | bytes 393224 | tf_op jit(solution)/shard_map/z2c2/ppermute | solution.py:269
  61.8 22.0 %collective-permute-start.20 = (bf16[4,1,4,64,128]{4,3,2,1,0:T(8,128)(2,1)S(1)}, bf16[4,1,4,64,128]{4,3,2,1,0:T(8,128)(2,1)S(1)}, u32[]{:S(2)}, u32[]{:S(2)}) collective-permute-start(bf16[4,1,4,64,128]{4,3,2,1,0:T(8,128)(2,1)S(1)} %merge.10.refs_2_), channel_id=1, source_target_pairs={{0,4},{4,0},{8,12},{12,8},{16,20},{20,16},{24,28},{28,24},{1,5},{5... | collective-permute-start | bytes 786440 | tf_op jit(solution)/shard_map/z1c1/ppermute | solution.py:269
  62.4 9.4 %collective-permute-start.15 = (bf16[2,1,4,64,128]{4,3,2,1,0:T(8,128)(2,1)S(1)}, bf16[2,1,4,64,128]{4,3,2,1,0:T(8,128)(2,1)S(1)}, u32[]{:S(2)}, u32[]{:S(2)}) collective-permute-start(bf16[2,1,4,64,128]{4,3,2,1,0:T(8,128)(2,1)S(1)} %get-tuple-element.63.refs_5_), channel_id=1, source_target_pairs={{0,24},{4,28},{8,16},{12,20},{16,8},{20,12},{24,0},{28,4},{1,25},{... | collective-permute-start | bytes 393224 | tf_op jit(solution)/shard_map/z6c2/ppermute | solution.py:269
  66.6 8.4 %collective-permute-start.21 = (bf16[2,1,4,64,128]{4,3,2,1,0:T(8,128)(2,1)S(1)}, bf16[2,1,4,64,128]{4,3,2,1,0:T(8,128)(2,1)S(1)}, u32[]{:S(2)}, u32[]{:S(2)}) collective-permute-start(bf16[2,1,4,64,128]{4,3,2,1,0:T(8,128)(2,1)S(1)} %get-tuple-element.69.refs_1_), channel_id=1, source_target_pairs={{0,24},{4,28},{8,16},{12,20},{16,8},{20,12},{24,0},{28,4},{1,25},{... | collective-permute-start | bytes 393224 | tf_op jit(solution)/shard_map/z6c3/ppermute | solution.py:269
  69.3 14.5 %collective-permute-start.22 = (bf16[2,1,4,64,128]{4,3,2,1,0:T(8,128)(2,1)S(1)}, bf16[2,1,4,64,128]{4,3,2,1,0:T(8,128)(2,1)S(1)}, u32[]{:S(2)}, u32[]{:S(2)}) collective-permute-start(bf16[2,1,4,64,128]{4,3,2,1,0:T(8,128)(2,1)S(1)} %get-tuple-element.70), channel_id=1, source_target_pairs={{0,16},{4,20},{8,24},{12,28},{16,0},{20,4},{24,8},{28,12},{1,17},{... | collective-permute-start | bytes 393224 | tf_op jit(solution)/shard_map/z4c3/ppermute | solution.py:269
  69.5 14.4 %collective-permute-start.23 = (bf16[2,1,4,64,128]{4,3,2,1,0:T(8,128)(2,1)S(1)}, bf16[2,1,4,64,128]{4,3,2,1,0:T(8,128)(2,1)S(1)}, u32[]{:S(2)}, u32[]{:S(2)}) collective-permute-start(bf16[2,1,4,64,128]{4,3,2,1,0:T(8,128)(2,1)S(1)} %get-tuple-element.71), channel_id=1, source_target_pairs={{0,8},{4,12},{8,0},{12,4},{16,24},{20,28},{24,16},{28,20},{1,9},{5... | collective-permute-start | bytes 393224 | tf_op jit(solution)/shard_map/z2c3/ppermute | solution.py:269
  71.8 12.1 %copy-start.1 = (s32[128]{0:T(128)S(1)}, s32[128]{0:T(128)}, u32[]{:S(2)}) copy-start(s32[128]{0:T(128)} %mirror_ref.1) | copy-start | bytes 1540
